TPU v7x, 32 devices: a whole 2x2x4 slice. The times are simulated.
32 devices in a mesh: grp: 2 (over y), tp: 8 (over z, x), rep: 2 (over core).
Axes of the slice: x: 2, y: 2, z: 4, core: 2. Of those that a mesh axis runs over, the one named last changes fastest.
Arguments:
- stretch: bfloat16 [192, 12, 16384], P(None, ('grp', 'rep'), 'tp'), parts along dimension 1, may hold values from -512 to 512
- norm_gain: float32 [16384], P('tp'), may hold values from 0.1 to 1.9
- kv_codes: int32 [16384, 2048], P('tp'), may hold values from 0 to 15
- scale_codes: int32 [256, 2048], P('tp'), may hold values from 0 to 255
- outer_scales: float32 [256, 8], P('tp'), may hold values from 0.01 to 0.09
- prompt_lengths: int32 [12], P('grp'), parts along dimension 0, may hold values from 194 to 2240, as said below
- target_rows: int32 [12], P('grp'), parts along dimension 0, may hold values from 0 to 7, as said below
- cache_lengths: int32 [16], P(('grp', 'tp')), parts along dimension 0, may hold values from 2 to 2048, as said below
- kv_cache: bfloat16 [16, 2048, 2048], P(('grp', 'tp'), 'rep'), parts along dimension 0, may hold values from -6 to 6
- queries: bfloat16 [16, 2, 16384], P(('grp', 'tp')), parts along dimension 0, may hold values from -96 to 96
- new_kv: bfloat16 [16, 2, 2048], P(('grp', 'tp')), parts along dimension 0, may hold values from -6 to 6
Outputs:
- attended: bfloat16 [16, 2, 16384], P(('grp', 'tp')), parts along dimension 0
There are 2 independent parts, one for each index of `grp`. A program takes and returns all parts, laid end to end along the dimension named above; an argument that names none is the same for every part. Nothing has to cross between parts.
Inputs may be any that keep to these rules, and one draw needn't show every extreme that they name: `target_rows`: distinct rows; the 3 prompts of one index of rep go to distinct owners, the owner of row g being g. `prompt_lengths`: both ends are reached. `cache_lengths`: both ends are reached.
All inputs are finite; a program needn't handle non-finite values.
Results may differ from a plain program's by a relative error of at most 0.013.
Values may be sent and summed in bfloat16 or wider, within the bound.
No kernel may reach another device: no remote copies, remote signals or barrier semaphores. Data moves between devices by JAX's collectives and lax.ppermute only.
A program may use at most 128 MiB of HBM per device.

v0:
```python
import jax
import jax.numpy as jnp
from jax import lax
from jax.sharding import PartitionSpec as P

D = 16384
HEADS = 128
KV_HEADS = 8
HEAD_DIM = 128
STRETCH = 192
SLOTS = 1
STEPS = 2


NORMAL_FLOAT_LEVELS = [
    -1.0,
    -0.6961928009986877,
    -0.5250730514526367,
    -0.39491748809814453,
    -0.28444138169288635,
    -0.18477343022823334,
    -0.09105003625154495,
    0.0,
    0.07958029955625534,
    0.16093020141124725,
    0.24611230194568634,
    0.33791524171829224,
    0.44070982933044434,
    0.5626170039176941,
    0.7229568362236023,
    1.0,
]
ROTARY_BASE = 500000.0
EPSILON = 1e-05
NEGATIVE = -1e30


def joined(value, axis, join):
    gathered = jax.tree.map(
        lambda a, kind: lax.all_gather(a.astype(kind), axis),
        value,
        (jnp.bfloat16, jnp.bfloat16, jnp.bfloat16),
    )

    def take(source):
        return jax.tree.map(
            lambda a, own: lax.dynamic_index_in_dim(a, source, 0, False).astype(own.dtype),
            gathered,
            value,
        )

    return lax.fori_loop(
        1, lax.axis_size(axis), lambda source, state: join(state, take(source)), take(0)
    )


def dequantize(weight_codes, block_codes, group_scales):
    levels = jnp.zeros(weight_codes.shape, jnp.float32)
    for code_value in range(16):
        levels = jnp.where(weight_codes == code_value, NORMAL_FLOAT_LEVELS[code_value], levels)
    inner = (block_codes.astype(jnp.float32) + 1.0) / 256.0
    columns_per = weight_codes.shape[1] // group_scales.shape[1]
    block_scale = inner * jnp.repeat(group_scales, columns_per, axis=1)
    rows_per = weight_codes.shape[0] // block_codes.shape[0]
    return (levels * jnp.repeat(block_scale, rows_per, axis=0)).astype(jnp.bfloat16)


def rotate_keys(keys, positions):
    half_dim = HEAD_DIM // 2
    frequency = ROTARY_BASE ** (-jnp.arange(half_dim, dtype=jnp.float32) / half_dim)
    angles = positions[..., None] * frequency
    cosine = jnp.cos(angles)[..., None, :]
    sine_part = jnp.sin(angles)[..., None, :]
    heads = keys.reshape(keys.shape[:-1] + (KV_HEADS, HEAD_DIM))
    lower = heads[..., :half_dim]
    upper = heads[..., half_dim:]
    turned = jnp.concatenate(
        [lower * cosine - upper * sine_part, upper * cosine + lower * sine_part], axis=-1
    )
    return turned.reshape(keys.shape)


def combine_parts(former, latter):
    highest = jnp.maximum(former[0], latter[0])
    former_factor = jnp.exp(former[0] - highest)
    latter_factor = jnp.exp(latter[0] - highest)
    totals = former[1] * former_factor + latter[1] * latter_factor
    sums = former[2] * former_factor[..., None] + latter[2] * latter_factor[..., None]
    return (highest, totals, sums)


def per_device(
    stretch,
    norm_gain,
    kv_codes,
    scale_codes,
    outer_scales,
    prompt_lengths,
    target_rows,
    cache_lengths,
    kv_cache,
    queries,
    new_kv,
):
    tp_count = lax.axis_size("tp")
    tp_here = lax.axis_index("tp")
    rep_here = lax.axis_index("rep")
    per_rep = stretch.shape[1]
    key_width = KV_HEADS * HEAD_DIM
    column_count = kv_codes.shape[1]
    squares = lax.psum(jnp.sum(jnp.square(stretch.astype(jnp.float32)), axis=2), "tp")
    inverse = lax.rsqrt(squares / D + EPSILON)
    weight = dequantize(kv_codes, scale_codes, outer_scales)
    targets_here = lax.dynamic_slice_in_dim(target_rows, rep_here * per_rep, per_rep)
    lengths_here = lax.dynamic_slice_in_dim(prompt_lengths, rep_here * per_rep, per_rep)
    owners = targets_here // SLOTS
    select = (owners[None, :] == jnp.arange(tp_count, dtype=jnp.int32)[:, None]).astype(
        jnp.bfloat16
    )
    summed = lax.psum_scatter(
        jnp.einsum(
            "cpd,dn->cpn",
            (stretch.astype(jnp.float32) * inverse[..., None] * norm_gain).astype(jnp.bfloat16),
            weight,
            preferred_element_type=jnp.float32,
        ),
        "tp",
        scatter_dimension=0,
        tiled=True,
    )
    outgoing = jnp.einsum(
        "jp,cpn->jcn", select, summed.astype(jnp.bfloat16), preferred_element_type=jnp.float32
    ).astype(jnp.bfloat16)
    incoming = lax.all_to_all(outgoing, "tp", split_axis=0, concat_axis=0, tiled=True)
    received = incoming.reshape(-1, column_count)
    matched_here = owners == tp_here
    arrived = jnp.any(matched_here)
    slot_index = jnp.sum(jnp.where(matched_here, targets_here % SLOTS, 0))
    first_position = jnp.sum(jnp.where(matched_here, lengths_here - STRETCH, 0))
    positions = (first_position + jnp.arange(received.shape[0], dtype=jnp.int32)).astype(
        jnp.float32
    )
    stretch_keys = rotate_keys(received[:, :key_width].astype(jnp.float32), positions).astype(
        jnp.bfloat16
    )
    stretch_keys = stretch_keys.reshape(-1, KV_HEADS, HEAD_DIM)
    stretch_values = received[:, key_width:].reshape(-1, KV_HEADS, HEAD_DIM)
    slot_count = kv_cache.shape[0]
    local_length = kv_cache.shape[1]
    rows_here = tp_here * slot_count + jnp.arange(slot_count, dtype=jnp.int32)
    matches = target_rows[None, :] == rows_here[:, None]
    row_spans = jnp.where(
        jnp.any(matches, axis=1),
        jnp.sum(jnp.where(matches, prompt_lengths[None, :] - STRETCH, 0), axis=1),
        cache_lengths,
    )
    places = rep_here * local_length + jnp.arange(local_length, dtype=jnp.int32)
    cache_allowed = (places[None, :] < row_spans[:, None])[:, None, None, :]
    stretch_allowed = (arrived & (jnp.arange(slot_count, dtype=jnp.int32) == slot_index))[
        :, None, None, None
    ]
    group_size = HEADS // KV_HEADS
    step_of = jnp.arange(STEPS * group_size, dtype=jnp.int32) // group_size
    fresh_allowed = (
        (jnp.arange(STEPS, dtype=jnp.int32)[None, :] <= step_of[:, None]) & (rep_here == 0)
    )[None, None, :, :]
    grouped = queries.reshape(slot_count, STEPS, KV_HEADS, group_size, HEAD_DIM).transpose(
        0, 2, 1, 3, 4
    )
    grouped = grouped.reshape(slot_count, KV_HEADS, STEPS * group_size, HEAD_DIM)
    cache_keys = kv_cache[..., :key_width].reshape(slot_count, local_length, KV_HEADS, HEAD_DIM)
    cache_values = kv_cache[..., key_width:].reshape(slot_count, local_length, KV_HEADS, HEAD_DIM)
    fresh_keys = new_kv[..., :key_width].reshape(slot_count, STEPS, KV_HEADS, HEAD_DIM)
    fresh_values = new_kv[..., key_width:].reshape(slot_count, STEPS, KV_HEADS, HEAD_DIM)
    scaling = HEAD_DIM ** (-0.5)
    score_cache = (
        jnp.einsum("skqd,sjkd->skqj", grouped, cache_keys, preferred_element_type=jnp.float32)
        * scaling
    )
    score_stretch = (
        jnp.einsum("skqd,ckd->skqc", grouped, stretch_keys, preferred_element_type=jnp.float32)
        * scaling
    )
    score_fresh = (
        jnp.einsum("skqd,sukd->skqu", grouped, fresh_keys, preferred_element_type=jnp.float32)
        * scaling
    )
    highest = jnp.maximum(
        jnp.max(jnp.where(cache_allowed, score_cache, NEGATIVE), axis=-1),
        jnp.max(jnp.where(stretch_allowed, score_stretch, NEGATIVE), axis=-1),
    )
    highest = jnp.maximum(
        highest, jnp.max(jnp.where(fresh_allowed, score_fresh, NEGATIVE), axis=-1)
    )
    weight_cache = jnp.where(cache_allowed, jnp.exp(score_cache - highest[..., None]), 0.0)
    weight_stretch = jnp.where(stretch_allowed, jnp.exp(score_stretch - highest[..., None]), 0.0)
    weight_fresh = jnp.where(fresh_allowed, jnp.exp(score_fresh - highest[..., None]), 0.0)
    totals = (
        jnp.sum(weight_cache, axis=-1)
        + jnp.sum(weight_stretch, axis=-1)
        + jnp.sum(weight_fresh, axis=-1)
    )
    sums = jnp.einsum(
        "skqj,sjkd->skqd",
        weight_cache.astype(jnp.bfloat16),
        cache_values,
        preferred_element_type=jnp.float32,
    )
    sums = sums + jnp.einsum(
        "skqc,ckd->skqd",
        weight_stretch.astype(jnp.bfloat16),
        stretch_values,
        preferred_element_type=jnp.float32,
    )
    sums = sums + jnp.einsum(
        "skqu,sukd->skqd",
        weight_fresh.astype(jnp.bfloat16),
        fresh_values,
        preferred_element_type=jnp.float32,
    )
    highest, totals, sums = joined((highest, totals, sums), "rep", combine_parts)
    result = (sums / totals[..., None]).astype(jnp.bfloat16)
    result = result.reshape(slot_count, KV_HEADS, STEPS, group_size, HEAD_DIM).transpose(
        0, 2, 1, 3, 4
    )
    return result.reshape(slot_count, STEPS, HEADS * HEAD_DIM)


def solution(mesh):
    in_specs = (
        P(None, ("grp", "rep"), "tp"),
        P("tp"),
        P("tp", None),
        P("tp", None),
        P("tp", None),
        P("grp"),
        P("grp"),
        P(("grp", "tp")),
        P(("grp", "tp"), "rep", None),
        P(("grp", "tp"), None, None),
        P(("grp", "tp"), None, None),
    )
    out_specs = P(("grp", "tp"), None, None)
    return jax.shard_map(
        per_device, mesh=mesh, in_specs=in_specs, out_specs=out_specs, check_vma=False
    )
```

profile of v0, /device:TPU:0, one launch (start us, length us, event | category | flops | bytes accessed | tf_op | source)
XLA Modules:
  0.0 338.5 jit_solution(11828079073711931449)
XLA Ops:
  0.0 0.8 copy.29
  0.8 0.1 broadcast_in_dim.162
  0.9 0.1 copy.46
  1.0 2.2 fusion.3
  3.2 23.1 %psum.7 = f32[192,3]{0,1:T(4,128)S(1)} all-reduce(f32[192,3]{0,1:T(4,128)S(1)} %fusion.3), channel_id=1, replica_groups=mesh['grp'=2,'tp'=8,'rep'=2] {'tp'}, use_global_device_ids=true, to_apply=%region_5.6 | all-reduce | flops 576 | bytes 4608 | tf_op jit(solution)/shard_map/psum | solution.py:111
  26.3 1.0 multiply_multiply_fusion
  27.3 0.0 copy-start.5
  27.3 20.3 %fusion = bf16[2048,2048]{1,0:T(8,128)(2,1)S(1)} fusion(s32[2048,2048]{1,0:T(8,128)} %param.13, f32[32,2048]{1,0:T(8,128)S(1)} %multiply_multiply_fusion), kind=kLoop, calls=%fused_computation.1 | loop fusion | flops 142606336 | bytes 25427968 | tf_op jit(solution)/shard_map/convert_element_type | solution.py:65
  47.6 5.1 %fusion.1 = f32[192,3,2048]{2,0,1:T(8,128)S(1)} fusion(bf16[2048,2048]{1,0:T(8,128)(2,1)S(1)} %fusion, bf16[192,3,2048]{2,0,1:T(8,128)(2,1)S(1)} %copy-done, f32[2048]{0:T(1024)S(1)} %copy-done.5, f32[192,3]{0,1:T(4,128)S(1)} %add_rsqrt_fusion), kind=kOutput, calls=%fused_computation.2 | convolution fusion | flops 4836556800 | bytes 15476992 | tf_op jit(solution)/shard_map/cpd,dn->cpn/dot_general | solution.py:121
  52.7 0.0 copy-start.6
  52.7 5.9 %copy.30 = f32[192,3,2048]{2,1,0:T(4,128)} copy(f32[192,3,2048]{2,0,1:T(8,128)S(1)} %fusion.1) | data formatting | bytes 9437184 | tf_op jit(solution)/shard_map/cpd,dn->cpn/dot_general | solution.py:121
  58.6 239.6 %all-reduce.2 = bf16[192,3,2048]{2,1,0:T(4,128)(2,1)S(1)} all-reduce(f32[192,3,2048]{2,1,0:T(4,128)} %copy.30), channel_id=5, replica_groups=mesh['grp'=2,'tp'=8,'rep'=2] {'tp'}, use_global_device_ids=true, to_apply=%region_6.7.clone | all-reduce | flops 1179648 | bytes 7077888
  298.2 0.0 copy-start.1
  298.2 0.6 dynamic-slice
  299.5 0.8 compare_reduce_fusion
  300.2 0.5 convolution_convert_fusion
  300.7 1.3 copy.31
  302.1 4.4 %all-to-all-start = ((bf16[8,24,2048]{2,1,0:T(8,128)(2,1)}), bf16[8,24,2048]{2,1,0:T(8,128)(2,1)}, u32[]{:S(2)}, u32[]{:S(2)}) async-start(bf16[8,24,2048]{2,1,0:T(8,128)(2,1)} %copy.31), calls=%async_computation | async-start | bytes 1572864 | tf_op jit(solution)/shard_map/all_to_all | solution.py:134
  306.5 0.6 compare_reduce_fusion.1
  307.1 0.6 fusion.43
  307.8 4.0 %fusion.54 = (bf16[1,1024,1024]{2,1,0:T(8,128)(2,1)}, bf16[1,1024,1024]{2,1,0:T(8,128)(2,1)S(1)}) fusion(bf16[1,1024,2048]{2,1,0:T(8,128)(2,1)} %param.19), kind=kLoop, calls=%fused_computation.99 | loop fusion | bytes 8388608 | tf_op jit(solution)/shard_map/slice | solution.py:172
  312.4 2.6 copy.40
  315.0 2.9 copy.43
  319.1 0.7 fusion.44
  319.8 0.6 add_convert_fusion.2
  320.5 0.2 select_reduce_fusion.2
  320.7 0.4 multiply_cosine_fusion
  321.1 2.1 select_reduce_fusion
  323.2 2.1 all-to-all-done
  325.3 1.2 slice_bitcast_fusion
  326.5 0.1 copy.47
  326.7 0.3 fusion.55
  326.9 0.3 subtract_convert_fusion
  327.3 1.2 select_reduce_fusion.1
  328.5 0.2 convolution_bitcast_fusion.2
  328.7 0.9 bitcast_reduce_fusion
  329.6 1.0 convolution_bitcast_fusion
  330.6 0.3 fusion.13
  330.9 0.9 fusion.12
  331.8 1.9 all-gather
  333.7 1.8 all-gather.2
  335.5 0.1 reshape.448
  335.6 0.1 reshape.447
  335.7 1.8 all-gather.1
  337.4 0.1 reshape.444
  337.5 0.1 reshape.445
  337.6 0.2 fusion.32
  337.8 0.7 reshape.440
  (26 shorter events, 0.2 us)
Async XLA Ops:
  27.3 20.3 %copy-start = (bf16[192,3,2048]{2,0,1:T(8,128)(2,1)S(1)}, bf16[192,3,2048]{2,0,1:T(8,128)(2,1)}, u32[]{:S(2)}) copy-start(bf16[192,3,2048]{2,0,1:T(8,128)(2,1)} %param.11) | copy-start | bytes 7077892
  27.3 20.3 %copy-start.5 = (f32[2048]{0:T(1024)S(1)}, f32[2048]{0:T(1024)}, u32[]{:S(2)}) copy-start(f32[2048]{0:T(1024)} %param.12) | copy-start | bytes 24580
  52.7 245.5 %copy-start.6 = (u32[32]{0:T(128)S(1)}, u32[32]{0:T(128)}, u32[]{:S(2)}) copy-start(u32[32]{0:T(128)} %constant.177) | copy-start | bytes 388
  52.7 246.8 %copy-start.3 = (s32[6]{0:T(128)S(1)}, s32[6]{0:T(128)}, u32[]{:S(2)}) copy-start(s32[6]{0:T(128)} %param.17) | copy-start | bytes 76
  58.6 248.6 %copy-start.4 = (s32[6]{0:T(128)S(1)}, s32[6]{0:T(128)}, u32[]{:S(2)}) copy-start(s32[6]{0:T(128)} %param.16) | copy-start | bytes 76
  298.2 13.6 %copy-start.1 = (bf16[1,2,16384]{2,1,0:T(2,128)(2,1)S(1)}, bf16[1,2,16384]{2,1,0:T(2,128)(2,1)}, u32[]{:S(2)}) copy-start(bf16[1,2,16384]{2,1,0:T(2,128)(2,1)} %param.20) | copy-start | bytes 196612
  302.1 23.2 %all-to-all-start = ((bf16[8,24,2048]{2,1,0:T(8,128)(2,1)}), bf16[8,24,2048]{2,1,0:T(8,128)(2,1)}, u32[]{:S(2)}, u32[]{:S(2)}) async-start(bf16[8,24,2048]{2,1,0:T(8,128)(2,1)} %copy.31), calls=%async_computation | async-start | bytes 1572864 | tf_op jit(solution)/shard_map/all_to_all | solution.py:134
  307.8 12.7 %copy-start.2 = (bf16[1,2,2048]{2,1,0:T(2,128)(2,1)S(1)}, bf16[1,2,2048]{2,1,0:T(2,128)(2,1)}, u32[]{:S(2)}) copy-start(bf16[1,2,2048]{2,1,0:T(2,128)(2,1)} %param.21) | copy-start | bytes 24580
where the time goes:
time: 339 us; the launch traced here: 338 us
  blocking collectives  268 us (79%)
  other arithmetic  30.3 us (9%)
  local copies, waits for them, and re-layouts  19.6 us (6%)
  matrix products  11.1 us (3%)
  starting transfers between devices  4.4 us (1%)
    unnamed x1, blocking collectives  240 us
    psum x1, blocking collectives, per_device(): lax.psum(jnp.sum(jnp.square(stretch.astype(jnp.float32)), axis=2), 'tp')  23.1 us
    convert_element_type x1, other arithmetic, dequantize(): (levels * jnp.repeat(block_scale, rows_per, axis=0)).astype(jnp.bfloat16)  20.3 us
    unnamed x21, local copies, waits for them, and re-layouts  7.06 us
  transfers between devices with their start and end apart: 1, of which 1 were waited for; matrix products, arithmetic and copies ran while one was open for 4% of the time, Pallas kernels for 0%

commit v1 on v0

v1 whole, which is shorter than its diff:
```python
import functools
import math

import jax
import jax.numpy as jnp
from jax import lax
from jax.experimental import pallas as pl
from jax.experimental.pallas import tpu as pltpu
from jax.sharding import PartitionSpec as P

D = 16384
HEADS = 128
KV_HEADS = 8
HEAD_DIM = 128
STRETCH = 192
STEPS = 2
QBLOCK = 64
GROUP = HEADS // KV_HEADS
ROWS = STEPS * GROUP
TAIL = 16
PART = ROWS + TAIL
NORMAL_FLOAT_LEVELS = [
    -1.0,
    -0.6961928009986877,
    -0.5250730514526367,
    -0.39491748809814453,
    -0.28444138169288635,
    -0.18477343022823334,
    -0.09105003625154495,
    0.0,
    0.07958029955625534,
    0.16093020141124725,
    0.24611230194568634,
    0.33791524171829224,
    0.44070982933044434,
    0.5626170039176941,
    0.7229568362236023,
    1.0,
]
ROTARY_BASE = 500000.0
EPSILON = 1e-05
NEGATIVE = -1e30
BF16 = jnp.bfloat16
F32 = jnp.float32


def ring_device(place, count):
    half = count // 2
    if isinstance(place, int):
        return 2 * place if place < half else 2 * (count - 1 - place) + 1
    return jnp.where(place < half, 2 * place, 2 * (count - 1 - place) + 1)


def project_kernel(
    heads, groups, x, key_codes, value_codes, key_scales, value_scales, outer, gain, levels,
    out, table,
):
    item, block = pl.program_id(0), pl.program_id(1)
    depth = key_codes.shape[0]

    @pl.when((item == 0) & (block == 0))
    def _():
        rows = lax.broadcasted_iota(jnp.int32, (128, 128), 0)
        lanes = lax.broadcasted_iota(jnp.int32, (128, 128), 1)
        for at in range(gain.shape[0]):
            column = jnp.sum(
                jnp.where(rows == lanes, gain[at : at + 1, :], 0.0), axis=1, keepdims=True
            )
            table[at * 128 : (at + 1) * 128, :] = column * levels[...]

    begin = pl.multiple_of(block * depth, depth)
    source = table[pl.ds(begin, depth), :]
    scale_rows = depth // QBLOCK
    if scale_rows == key_scales.shape[0]:
        scale_at = slice(None)
    else:
        scale_at = pl.ds(pl.multiple_of(block * scale_rows, scale_rows), scale_rows)
    head = heads[item]
    outer_here = outer[scale_at, :]
    lane = lax.broadcasted_iota(jnp.int32, outer_here.shape, 1)

    def weight(codes, scales, column):
        second = jnp.sum(jnp.where(lane == column, outer_here, 0.0), axis=1, keepdims=True)
        scale = (scales[scale_at, :].astype(F32) + 1.0) / 256.0 * second
        level = jnp.take_along_axis(source, codes[...], axis=1)
        level = level.reshape(scale_rows, QBLOCK, HEAD_DIM) * scale[:, None, :]
        return level.reshape(depth, HEAD_DIM).astype(BF16)

    heads_per = KV_HEADS // (outer.shape[1] // 2)
    both = jnp.concatenate(
        [
            weight(key_codes, key_scales, head // heads_per),
            weight(value_codes, value_scales, outer.shape[1] // 2 + head // heads_per),
        ],
        axis=1,
    )
    product = jnp.dot(x[0, :, pl.ds(begin, depth)], both, preferred_element_type=F32)

    if x.shape[2] == depth:
        out[0, 0] = product[:, :HEAD_DIM].astype(out.dtype)
        out[0, 1] = product[:, HEAD_DIM:].astype(out.dtype)
    else:

        @pl.when(block == 0)
        def _():
            out[0, 0] = product[:, :HEAD_DIM]
            out[0, 1] = product[:, HEAD_DIM:]

        @pl.when(block != 0)
        def _():
            out[0, 0] += product[:, :HEAD_DIM]
            out[0, 1] += product[:, HEAD_DIM:]


def project(owners, x, codes, scales, outer, gain, levels):
    count = owners.shape[0]
    tokens, features = x.shape[1:]
    depth = min(1024, features)
    blocks = features // depth
    heads = owners % KV_HEADS
    groups = owners // KV_HEADS
    return pl.pallas_call(
        project_kernel,
        grid_spec=pltpu.PrefetchScalarGridSpec(
            num_scalar_prefetch=2,
            grid=(count, blocks),
            in_specs=[
                pl.BlockSpec((1, tokens, features), lambda i, k, h, g: (g[i], 0, 0)),
                pl.BlockSpec((depth, HEAD_DIM), lambda i, k, h, g: (k, h[i])),
                pl.BlockSpec((depth, HEAD_DIM), lambda i, k, h, g: (k, KV_HEADS + h[i])),
                pl.BlockSpec((scales.shape[0], HEAD_DIM), lambda i, k, h, g: (0, h[i])),
                pl.BlockSpec((scales.shape[0], HEAD_DIM), lambda i, k, h, g: (0, KV_HEADS + h[i])),
                pl.BlockSpec(outer.shape, lambda i, k, h, g: (0, 0)),
                pl.BlockSpec(gain.shape, lambda i, k, h, g: (0, 0)),
                pl.BlockSpec(levels.shape, lambda i, k, h, g: (0, 0)),
            ],
            out_specs=pl.BlockSpec((1, 2, tokens, HEAD_DIM), lambda i, k, h, g: (i, 0, 0, 0)),
            scratch_shapes=[pltpu.VMEM((features, 128), F32)],
        ),
        out_shape=jax.ShapeDtypeStruct((count, 2, tokens, HEAD_DIM), F32),
        compiler_params=pltpu.CompilerParams(vmem_limit_bytes=24 * 1024 * 1024),
        cost_estimate=pl.CostEstimate(
            flops=count * 4 * tokens * features * HEAD_DIM,
            bytes_accessed=count * features * 2 * HEAD_DIM * 4 + x.shape[1] * features * 2,
            transcendentals=0,
        ),
        name="project",
    )(heads, groups, x, codes, codes, scales, scales, outer, gain, levels)


def pieces_tail(logs):
    rows = lax.broadcasted_iota(jnp.int32, (ROWS, 128), 0)
    lanes = lax.broadcasted_iota(jnp.int32, (ROWS, 128), 1)
    row = jnp.sum(jnp.where(rows == lanes, logs, 0.0), axis=0, keepdims=True)
    high = row.astype(BF16).astype(F32)
    middle = (row - high).astype(BF16).astype(F32)
    low = row - high - middle
    at = lax.broadcasted_iota(jnp.int32, (TAIL, 128), 0)
    tail = jnp.where(at == 0, high, jnp.where(at == 1, middle, jnp.where(at == 2, low, 0.0)))
    return tail.astype(BF16)


def tail_pieces(tail):
    tail = tail.astype(F32)
    row = tail[0:1, :] + tail[1:2, :] + tail[2:3, :]
    rows = lax.broadcasted_iota(jnp.int32, (ROWS, 128), 0)
    lanes = lax.broadcasted_iota(jnp.int32, (ROWS, 128), 1)
    return jnp.sum(jnp.where(rows == lanes, row, 0.0), axis=1, keepdims=True)


def cache_kernel(info, q, keys, values, fresh_keys, fresh_values, out):
    scaling = HEAD_DIM ** (-0.5)
    dims = (((1,), (1,)), ((), ()))
    length = keys.shape[1]
    query = q[0]
    scores = lax.dot_general(query, keys[0], dims, preferred_element_type=F32) * scaling
    fresh = lax.dot_general(query, fresh_keys[...], dims, preferred_element_type=F32) * scaling
    place = lax.broadcasted_iota(jnp.int32, scores.shape, 1) + info[1] * length
    allowed = place < info[0]
    slot = lax.broadcasted_iota(jnp.int32, fresh.shape, 1)
    step = lax.broadcasted_iota(jnp.int32, fresh.shape, 0) // GROUP
    fresh_allowed = (slot <= step) & (slot < STEPS) & (info[1] == 0)
    highest = jnp.maximum(
        jnp.max(jnp.where(allowed, scores, NEGATIVE), axis=1, keepdims=True),
        jnp.max(jnp.where(fresh_allowed, fresh, NEGATIVE), axis=1, keepdims=True),
    )
    weights = jnp.where(allowed, jnp.exp(scores - highest), 0.0)
    fresh_weights = jnp.where(fresh_allowed, jnp.exp(fresh - highest), 0.0)
    totals = jnp.sum(weights, axis=1, keepdims=True) + jnp.sum(
        fresh_weights, axis=1, keepdims=True
    )
    sums = jnp.dot(weights.astype(BF16), values[0], preferred_element_type=F32)
    sums += jnp.dot(fresh_weights.astype(BF16), fresh_values[...], preferred_element_type=F32)
    some = totals > 0.0
    out[0, :ROWS] = jnp.where(some, sums / jnp.where(some, totals, 1.0), 0.0).astype(BF16)
    logs = jnp.where(some, highest + jnp.log(jnp.where(some, totals, 1.0)), NEGATIVE)
    out[0, ROWS:] = pieces_tail(logs)


def cache_attention(info, grouped, kv_cache, fresh):
    length = kv_cache.shape[1]
    return pl.pallas_call(
        cache_kernel,
        grid_spec=pltpu.PrefetchScalarGridSpec(
            num_scalar_prefetch=1,
            grid=(KV_HEADS,),
            in_specs=[
                pl.BlockSpec((1, ROWS, HEAD_DIM), lambda h, s: (h, 0, 0)),
                pl.BlockSpec((1, length, HEAD_DIM), lambda h, s: (0, 0, h)),
                pl.BlockSpec((1, length, HEAD_DIM), lambda h, s: (0, 0, KV_HEADS + h)),
                pl.BlockSpec((fresh.shape[0], HEAD_DIM), lambda h, s: (0, h)),
                pl.BlockSpec((fresh.shape[0], HEAD_DIM), lambda h, s: (0, KV_HEADS + h)),
            ],
            out_specs=pl.BlockSpec((1, PART, HEAD_DIM), lambda h, s: (h, 0, 0)),
        ),
        out_shape=jax.ShapeDtypeStruct((KV_HEADS, PART, HEAD_DIM), BF16),
        compiler_params=pltpu.CompilerParams(vmem_limit_bytes=16 * 1024 * 1024),
        cost_estimate=pl.CostEstimate(
            flops=4 * HEADS * STEPS * length * HEAD_DIM,
            bytes_accessed=length * 2 * KV_HEADS * HEAD_DIM * 2,
            transcendentals=HEADS * STEPS * length,
        ),
        name="cache_attention",
    )(info, grouped, kv_cache, kv_cache, fresh, fresh)


def stretch_kernel(targets, own, right, left, inverse, cosine, sine, q, out):
    scaling = HEAD_DIM ** (-0.5)
    dims = (((1,), (1,)), ((), ()))
    empty = jnp.zeros((ROWS, HEAD_DIM), BF16)
    empty_tail = pieces_tail(jnp.full((ROWS, 1), NEGATIVE, F32))
    for owner in range(out.shape[0]):
        for core in range(2):
            out[owner, core, :ROWS] = empty
            out[owner, core, ROWS:] = empty_tail
    for prompt in range(own.shape[2] // STRETCH):
        at = slice(prompt * STRETCH, (prompt + 1) * STRETCH)
        scale = inverse[at, :]
        keys = own[0, 0, at] + right[0, at].astype(F32) + left[0, at].astype(F32)
        values = own[0, 1, at] + right[1, at].astype(F32) + left[1, at].astype(F32)
        keys = (keys * scale).astype(BF16).astype(F32)
        values = (values * scale).astype(BF16)
        keys = keys * cosine[at, :] + pltpu.roll(keys, HEAD_DIM // 2, 1) * sine[at, :]
        target = targets[prompt]
        query = q[target, :ROWS]
        scores = lax.dot_general(query, keys.astype(BF16), dims, preferred_element_type=F32)
        scores = scores * scaling
        highest = jnp.max(scores, axis=1, keepdims=True)
        weights = jnp.exp(scores - highest)
        totals = jnp.sum(weights, axis=1, keepdims=True)
        sums = jnp.dot(weights.astype(BF16), values, preferred_element_type=F32)
        result = (sums / totals).astype(BF16)
        tail = pieces_tail(highest + jnp.log(totals))
        for core in range(2):
            out[target, core, :ROWS] = result
            out[target, core, ROWS:] = tail


def stretch_attention(targets, own, right, left, inverse, cosine, sine, q):
    vmem = pl.BlockSpec(memory_space=pltpu.VMEM)
    return pl.pallas_call(
        stretch_kernel,
        in_specs=[pl.BlockSpec(memory_space=pltpu.SMEM)] + [vmem] * 7,
        out_specs=vmem,
        out_shape=jax.ShapeDtypeStruct((q.shape[0], 2, PART, HEAD_DIM), BF16),
        compiler_params=pltpu.CompilerParams(vmem_limit_bytes=16 * 1024 * 1024),
        name="stretch_attention",
    )(targets, own, right, left, inverse, cosine, sine, q)


def combine_kernel(cached, handed, out):
    groups = handed.shape[0]
    for head in range(KV_HEADS):
        parts = [cached[0, head], cached[1, head]]
        for group in range(groups):
            parts += [handed[group, head, 0], handed[group, head, 1]]
        logs = [tail_pieces(part[ROWS:]) for part in parts]
        highest = functools.reduce(jnp.maximum, logs)
        shares = [jnp.exp(log - highest) for log in logs]
        total = functools.reduce(jnp.add, shares)
        sums = functools.reduce(
            jnp.add, [share * part[:ROWS].astype(F32) for share, part in zip(shares, parts)]
        )
        result = (sums / total).astype(BF16)
        for step in range(STEPS):
            out[step, head * GROUP : (head + 1) * GROUP] = result[
                step * GROUP : (step + 1) * GROUP
            ]


def combine(cached, handed):
    vmem = pl.BlockSpec(memory_space=pltpu.VMEM)
    return pl.pallas_call(
        combine_kernel,
        in_specs=[vmem] * 2,
        out_specs=vmem,
        out_shape=jax.ShapeDtypeStruct((STEPS, HEADS, HEAD_DIM), BF16),
        compiler_params=pltpu.CompilerParams(vmem_limit_bytes=16 * 1024 * 1024),
        name="combine",
    )(cached, handed)


def split_pieces(value):
    high = lax.reduce_precision(value, 8, 7)
    middle = lax.reduce_precision(value - high, 8, 7)
    low = lax.reduce_precision(value - high - middle, 8, 7)
    return jnp.stack([high, middle, low], axis=1).astype(BF16)


def per_device(
    stretch,
    norm_gain,
    kv_codes,
    scale_codes,
    outer_scales,
    prompt_lengths,
    target_rows,
    cache_lengths,
    kv_cache,
    queries,
    new_kv,
):
    count = lax.axis_size("tp")
    here = lax.axis_index("tp")
    rep_here = lax.axis_index("rep")
    per_rep = stretch.shape[1]
    features = stretch.shape[2]
    groups = count // KV_HEADS
    per_group = per_rep // groups
    tokens = per_group * STRETCH
    group_here = here // KV_HEADS
    place = jnp.where(here % 2 == 0, here // 2, count - 1 - here // 2)

    x = stretch.transpose(1, 0, 2).reshape(groups, tokens, features)
    gain = norm_gain.reshape(features // 128, 128)
    levels = jnp.pad(jnp.array(NORMAL_FLOAT_LEVELS, F32), (0, 128 - 16)).reshape(1, 128)

    def owners_at(distances):
        places = (place + jnp.array(distances, jnp.int32)) % count
        return ring_device(places, count).astype(jnp.int32)

    def project_at(distances):
        return project(
            owners_at(distances), x, kv_codes, scale_codes, outer_scales, gain, levels
        )

    ring = [ring_device(at, count) for at in range(count)]
    to_right = [(ring[at], ring[(at + 1) % count]) for at in range(count)]
    to_left = [(ring[at], ring[at - 1]) for at in range(count)]

    half = count // 2
    far = project_at([half])[0].astype(BF16)
    right = lax.ppermute(far[0], "tp", to_right)
    left = lax.ppermute(far[1], "tp", to_left)

    grouped = queries.reshape(STEPS, KV_HEADS, GROUP, HEAD_DIM).transpose(1, 0, 2, 3)
    grouped = grouped.reshape(KV_HEADS, ROWS, HEAD_DIM)
    squares = jnp.sum(jnp.square(x.astype(F32)), axis=2)
    width = -(-tokens // 128) * 128
    squares = split_pieces(jnp.pad(squares, ((0, 0), (0, width - tokens))))
    squares = squares.reshape(groups, 3 * width // 128, 128)
    squares = jnp.pad(squares, ((0, 0), (0, TAIL - squares.shape[1]), (0, 0)))
    outgoing = jnp.concatenate(
        [
            jnp.broadcast_to(grouped[None], (groups, KV_HEADS, ROWS, HEAD_DIM)),
            jnp.broadcast_to(squares[:, None], (groups, KV_HEADS, TAIL, HEAD_DIM)),
        ],
        axis=2,
    ).reshape(count, PART, HEAD_DIM)
    incoming = lax.all_to_all(outgoing, "tp", split_axis=0, concat_axis=0, tiled=True)
    squares = jnp.sum(incoming[:, ROWS : ROWS + 3 * width // 128].astype(F32), axis=0)
    squares = jnp.sum(squares.reshape(3, width), axis=0)[:tokens]
    inverse = lax.rsqrt(squares / D + EPSILON)[:, None]

    first = rep_here * per_rep + group_here * per_group
    targets = lax.dynamic_slice_in_dim(target_rows, first, per_group)
    lengths = lax.dynamic_slice_in_dim(prompt_lengths, first, per_group)
    half_dim = HEAD_DIM // 2
    frequency = ROTARY_BASE ** (-jnp.arange(half_dim, dtype=F32) / half_dim)
    positions = (lengths[:, None] - STRETCH + jnp.arange(STRETCH, dtype=jnp.int32)[None, :])
    angles = positions.astype(F32).reshape(tokens, 1) * frequency
    cosine, sine = jnp.cos(angles), jnp.sin(angles)
    cosine = jnp.concatenate([cosine, cosine], axis=1)
    sine = jnp.concatenate([-sine, sine], axis=1)

    matches = target_rows == here
    span = jnp.where(
        jnp.any(matches),
        jnp.sum(jnp.where(matches, prompt_lengths - STRETCH, 0)),
        cache_lengths[0],
    )
    info = jnp.stack([span, rep_here]).astype(jnp.int32)
    fresh = jnp.pad(new_kv[0], ((0, 16 - STEPS), (0, 0)))
    cached = cache_attention(info, grouped, kv_cache, fresh)
    cached = lax.all_gather(cached, "rep")

    distances = list(range(half - 1, 0, -1))
    size = max(1, -(-len(distances) // 3))
    own = None
    for begin in range(0, len(distances), size):
        here_distances = distances[begin : begin + size]
        wanted = [sign * d for d in here_distances for sign in (1, -1)]
        if begin + size >= len(distances):
            wanted = wanted + [0]
        terms = project_at(wanted)
        for at, distance in enumerate(here_distances):
            if distance == half - 1:
                right = jnp.stack([terms[2 * at, 0] + right.astype(F32), terms[2 * at, 1]])
                left = jnp.stack([terms[2 * at + 1, 0], terms[2 * at + 1, 1] + left.astype(F32)])
            else:
                right = terms[2 * at] + right.astype(F32)
                left = terms[2 * at + 1] + left.astype(F32)
            right = lax.ppermute(right.astype(BF16), "tp", to_right)
            left = lax.ppermute(left.astype(BF16), "tp", to_left)
        own = terms[-1:]

    handed = stretch_attention(targets, own, right, left, inverse, cosine, sine, incoming)
    handed = handed.reshape(2 * count, PART, HEAD_DIM)
    handed = lax.all_to_all(handed, ("tp", "rep"), split_axis=0, concat_axis=0, tiled=True)
    handed = handed.reshape(groups, KV_HEADS, 2, PART, HEAD_DIM)
    return combine(cached, handed).reshape(1, STEPS, HEADS * HEAD_DIM)


def solution(mesh):
    in_specs = (
        P(None, ("grp", "rep"), "tp"),
        P("tp"),
        P("tp", None),
        P("tp", None),
        P("tp", None),
        P("grp"),
        P("grp"),
        P(("grp", "tp")),
        P(("grp", "tp"), "rep", None),
        P(("grp", "tp"), None, None),
        P(("grp", "tp"), None, None),
    )
    out_specs = P(("grp", "tp"), None, None)
    return jax.shard_map(
        per_device, mesh=mesh, in_specs=in_specs, out_specs=out_specs, check_vma=False
    )
```

time: 339 us -> 111 us (0.33)
  blocking collectives: 268 us -> 2 us
  Pallas kernels: 0 us -> 33 us
  other arithmetic: 30.3 us -> 5.88 us
  local copies, waits for them, and re-layouts: 19.6 us -> 36 us
  starting transfers between devices: 4.4 us -> 19.4 us
  matrix products: 11.1 us -> 0 us
  waiting for transfers between devices: 2.14 us -> 11.4 us
    unnamed x1 -> x0, blocking collectives: 240 us -> none
    pallas_call x0 -> x7, Pallas kernels: none -> 33 us  [the longest x4 25 us: project(): pl.pallas_call(project_kernel, grid_spec=pltpu.PrefetchScalarGridSpec(num...]
    unnamed x21 -> x52, local copies, waits for them, and re-layouts: 7.06 us -> 32.3 us
    psum x1 -> x0, blocking collectives: 23.1 us -> none  [per_device(): lax.psum(jnp.sum(jnp.square(stretch.astype(jnp.float32)), axis=2), 'tp')]
    convert_element_type x6 -> x4, other arithmetic: 20.9 us -> 0.38 us  [the longest x2 0.26 us: per_device(): left = lax.ppermute(left.astype(BF16), 'tp', to_left)]
    ppermute x0 -> x8, waiting for transfers between devices: none -> 11.4 us  [the longest x3 8.45 us: per_device(): right = lax.ppermute(right.astype(BF16), 'tp', to_right)]
    dot_general x8 -> x0, matrix products: 11.1 us -> none  [the longest x1 5.09 us: per_device(): jnp.einsum('cpd,dn->cpn', (stretch.astype(jnp.float32) * inverse[..., Non...]
    ppermute x0 -> x8, starting transfers between devices: none -> 9.38 us  [the longest x3 5.65 us: per_device(): right = lax.ppermute(right.astype(BF16), 'tp', to_right)]
  transfers between devices with their start and end apart: 1 -> 10, of which waited for: 1 -> 4; matrix products, arithmetic and copies ran while one was open for 4% -> 7% of each run, Pallas kernels for 0% -> 25%
where the time goes in v1:
time: 111 us; the launch traced here: 110 us
  local copies, waits for them, and re-layouts  36 us (32%)
  Pallas kernels  33 us (30%)
  starting transfers between devices  19.4 us (17%)
  waiting for transfers between devices  11.4 us (10%)
  other arithmetic  5.88 us (5%)
  between operations  2.39 us (2%)
  blocking collectives  2 us (2%)
    unnamed x52, local copies, waits for them, and re-layouts  32.3 us
    pallas_call x4, Pallas kernels, project(): pl.pallas_call(project_kernel, grid_spec=pltpu.PrefetchScalarGridSpec(num...  25 us
    ppermute x3, waiting for transfers between devices, per_device(): right = lax.ppermute(right.astype(BF16), 'tp', to_right)  8.45 us
    all_to_all x1, starting transfers between devices, per_device(): lax.all_to_all(outgoing, 'tp', split_axis=0, concat_axis=0, tiled=True)  6.25 us
    ppermute x3, starting transfers between devices, per_device(): right = lax.ppermute(right.astype(BF16), 'tp', to_right)  5.65 us
    pallas_call x1, Pallas kernels, cache_attention(): pl.pallas_call(cache_kernel, grid_spec=pltpu.PrefetchScalarGridSpec(num_s...  5.42 us
    all_to_all x1, starting transfers between devices, per_device(): lax.all_to_all(handed, ('tp', 'rep'), split_axis=0, concat_axis=0, tiled=...  3.74 us
    ppermute x1, starting transfers between devices, per_device(): right = lax.ppermute(far[0], 'tp', to_right)  3.03 us
  transfers between devices with their start and end apart: 10, of which 4 were waited for; matrix products, arithmetic and copies ran while one was open for 7% of the time, Pallas kernels for 25%

profile of v1, /device:TPU:0, one launch (start us, length us, event | category | flops | bytes accessed | tf_op | source)
XLA Modules:
  0.0 110.0 jit_solution(3680330079087724880)
XLA Ops:
  0.0 0.8 copy.35.outer
  0.8 5.8 %copy-done = s32[2048,2048]{1,0:T(8,128)S(1)} copy-done((s32[2048,2048]{1,0:T(8,128)S(1)}, s32[2048,2048]{1,0:T(8,128)}, u32[]{:S(2)}) %copy-start) | copy-done | bytes 16777240
  6.5 1.7 %copy-done.4 = bf16[192,3,2048]{2,0,1:T(8,128)(2,1)S(1)} copy-done((bf16[192,3,2048]{2,0,1:T(8,128)(2,1)S(1)}, bf16[192,3,2048]{2,0,1:T(8,128)(2,1)}, u32[]{:S(2)}) %copy-start.4) | copy-done | bytes 2359320
  8.2 0.9 copy-done.6
  9.2 0.7 copy-done.12
  9.8 0.7 copy-done.14
  10.5 3.1 %project.7 = f32[1,2,576,128]{3,2,1,0:T(8,128)S(1)} custom-call(s32[1]{0:T(128)S(6)} %select_n.118.heads, s32[1]{0:T(128)S(6)} %select_n.119.groups, bf16[1,576,2048]{2,1,0:T(8,128)(2,1)S(1)} %bitcast.85, s32[2048,2048]{1,0:T(8,128)S(1)} %copy-done, s32[2048,2048]{1,0:T(8,128)S(1)} %copy-done, s32[32,2048]{1,0:T(8,128)S(1)} %copy-done.6, ...), custom_call_target="tpu_custom_call" | custom-call | flops 603979776 | bytes 4456448 | tf_op jit(solution)/shard_map/project/pallas_call | solution.py:122
  13.7 0.7 slice_bitcast_fusion.6
  14.4 3.0 %collective-permute-start = (bf16[576,128]{1,0:T(8,128)(2,1)}, bf16[576,128]{1,0:T(8,128)(2,1)}, u32[]{:S(2)}, u32[]{:S(2)}) collective-permute-start(bf16[576,128]{1,0:T(8,128)(2,1)} %get-tuple-element.20), channel_id=1, source_target_pairs={{0,4},{4,8},{8,12},{12,14},{14,10},{10,6},{6,2},{2,0},{1,5},{5,9},... | collective-permute-start | bytes 442376 | tf_op jit(solution)/shard_map/ppermute | solution.py:353
  17.5 0.5 multiply_reduce_fusion
  18.0 0.1 reduce_sum.40
  18.2 0.6 maximum_bitcast_fusion
  18.9 6.3 %all-to-all-start = ((bf16[8,48,128]{2,1,0:T(8,128)(2,1)}), bf16[8,48,128]{2,1,0:T(8,128)(2,1)S(1)}, u32[]{:S(2)}, u32[]{:S(2)}) async-start(bf16[8,48,128]{2,1,0:T(8,128)(2,1)} %maximum_bitcast_fusion), calls=%async_computation | async-start | bytes 196608 | tf_op jit(solution)/shard_map/all_to_all | solution.py:370
  25.2 5.8 %copy-done.1 = s32[2048,2048]{1,0:T(8,128)S(1)} copy-done((s32[2048,2048]{1,0:T(8,128)S(1)}, s32[2048,2048]{1,0:T(8,128)}, u32[]{:S(2)}) %copy-start.1) | copy-done | bytes 16777240
  31.0 6.4 %project.6 = f32[2,2,576,128]{3,2,1,0:T(8,128)S(1)} custom-call(s32[2]{0:T(128)S(1)} %and_select_fusion.1.heads, s32[2]{0:T(128)S(1)} %get-tuple-element.5.groups, bf16[1,576,2048]{2,1,0:T(8,128)(2,1)S(1)} %bitcast.86, s32[2048,2048]{1,0:T(8,128)S(1)} %copy-done.1, s32[2048,2048]{1,0:T(8,128)S(1)} %copy-done.1, s32[32,2048]{1,0:T(8,128)S(1)} %copy-done.7, ...), custom_call_target="tpu_custom_call" | custom-call | flops 1207959552 | bytes 6553600 | tf_op jit(solution)/shard_map/project/pallas_call | solution.py:122
  37.4 1.0 copy-done.9
  38.4 0.1 convert.29
  38.5 0.7 slice_bitcast_fusion.7
  39.4 5.8 %copy-done.2 = s32[2048,2048]{1,0:T(8,128)S(1)} copy-done((s32[2048,2048]{1,0:T(8,128)S(1)}, s32[2048,2048]{1,0:T(8,128)}, u32[]{:S(2)}) %copy-start.2) | copy-done | bytes 16777240
  45.2 9.1 %project.4 = f32[3,2,576,128]{3,2,1,0:T(8,128)S(1)} custom-call(s32[3]{0:T(128)S(1)} %and_select_fusion.7.heads, s32[3]{0:T(128)S(1)} %get-tuple-element.9.groups, bf16[1,576,2048]{2,1,0:T(8,128)(2,1)S(1)} %bitcast.87, s32[2048,2048]{1,0:T(8,128)S(1)} %copy-done.2, s32[2048,2048]{1,0:T(8,128)S(1)} %copy-done.2, s32[32,2048]{1,0:T(8,128)S(1)} %copy-done.7, ...), custom_call_target="tpu_custom_call" | custom-call | flops 1811939328 | bytes 8650752 | tf_op jit(solution)/shard_map/project/pallas_call | solution.py:122
  54.4 1.2 %copy-done.10 = f32[3,2,576,128]{3,2,1,0:T(8,128)} copy-done((f32[3,2,576,128]{3,2,1,0:T(8,128)}, f32[3,2,576,128]{3,2,1,0:T(8,128)S(1)}, u32[]{:S(2)}) %copy-start.10) | copy-done | bytes 1769496
  55.7 1.1 %slice.56.own = f32[1,2,576,128]{3,2,1,0:T(8,128)S(1)} slice(f32[3,2,576,128]{3,2,1,0:T(8,128)} %copy-done.10), slice={[2:3], [0:2], [0:576], [0:128]} | slice | bytes 1179648 | tf_op jit(solution)/shard_map/slice | solution.py:415
  57.6 1.2 %fusion.13 = (bf16[1,576,128]{2,1,0:T(8,128)(2,1)S(1)}, bf16[1,576,128]{2,1,0:T(8,128)(2,1)S(1)}) fusion(bf16[576,128]{1,0:T(8,128)(2,1)} %collective-permute-done.4, f32[2,2,576,128]{3,2,1,0:T(8,128)} %copy-done.9, bf16[576,128]{1,0:T(8,128)(2,1)} %collective-permute-done), kind=kLoop, calls=%fused_computation.26 | loop fusion | flops 442368 | bytes 1179648 | tf_op jit(solution)/shard_map/stack | solution.py:409
  58.9 2.1 %collective-permute-start.1 = (bf16[2,576,128]{2,1,0:T(8,128)(2,1)S(1)}, bf16[2,576,128]{2,1,0:T(8,128)(2,1)S(1)}, u32[]{:S(2)}, u32[]{:S(2)}) collective-permute-start(bf16[2,576,128]{2,1,0:T(8,128)(2,1)S(1)} %pad_maximum_fusion), channel_id=1, source_target_pairs={{0,4},{4,8},{8,12},{12,14},{14,10},{10,6},{6,2},{2,0},{1,5},{5,9},... | collective-permute-start | bytes 884744 | tf_op jit(solution)/shard_map/ppermute | solution.py:413
  61.0 0.1 collective-permute-start.5
  61.1 5.8 %copy-done.3 = s32[2048,2048]{1,0:T(8,128)S(1)} copy-done((s32[2048,2048]{1,0:T(8,128)S(1)}, s32[2048,2048]{1,0:T(8,128)}, u32[]{:S(2)}) %copy-start.3) | copy-done | bytes 16777240
  66.9 6.4 %project.5 = f32[2,2,576,128]{3,2,1,0:T(8,128)S(1)} custom-call(s32[2]{0:T(128)S(1)} %and_select_fusion.4.heads, s32[2]{0:T(128)S(1)} %get-tuple-element.27.groups, bf16[1,576,2048]{2,1,0:T(8,128)(2,1)S(1)} %bitcast.88, s32[2048,2048]{1,0:T(8,128)S(1)} %copy-done.3, s32[2048,2048]{1,0:T(8,128)S(1)} %copy-done.3, s32[32,2048]{1,0:T(8,128)S(1)} %copy-done.7, ...), custom_call_target="tpu_custom_call" | custom-call | flops 1207959552 | bytes 6553600 | tf_op jit(solution)/shard_map/project/pallas_call | solution.py:122
  73.3 0.1 fusion.1
  73.4 2.1 %collective-permute-start.2 = (bf16[2,576,128]{2,1,0:T(8,128)(2,1)S(1)}, bf16[2,576,128]{2,1,0:T(8,128)(2,1)S(1)}, u32[]{:S(2)}, u32[]{:S(2)}) collective-permute-start(bf16[2,576,128]{2,1,0:T(8,128)(2,1)S(1)} %get-tuple-element.14), channel_id=1, source_target_pairs={{0,4},{4,8},{8,12},{12,14},{14,10},{10,6},{6,2},{2,0},{1,5},{5,9},... | collective-permute-start | bytes 884744 | tf_op jit(solution)/shard_map/ppermute | solution.py:413
  75.6 1.1 %fusion.14 = (f32[576,64]{1,0:T(8,128)S(1)}, f32[576,64]{1,0:T(8,128)S(1)}, f32[576,64]{1,0:T(8,128)S(1)}) fusion(f32[64]{0:T(128)S(1)} %multiply_power_fusion, f32[576]{0:T(1024)S(1)} %convert_element_type.91), kind=kLoop, calls=%fused_computation.32 | loop fusion | flops 73728 | bytes 444928 | tf_op jit(solution)/shard_map/neg | solution.py:384
  76.7 0.2 pad_maximum_fusion.2
  76.9 4.0 %collective-permute-done.2 = bf16[2,576,128]{2,1,0:T(8,128)(2,1)S(1)} collective-permute-done((bf16[2,576,128]{2,1,0:T(8,128)(2,1)S(1)}, bf16[2,576,128]{2,1,0:T(8,128)(2,1)S(1)}, u32[]{:S(2)}, u32[]{:S(2)}) %collective-permute-start.2) | collective-permute-done | bytes 294944 | tf_op jit(solution)/shard_map/ppermute | solution.py:413
  80.9 1.4 %collective-permute-done.6 = bf16[2,576,128]{2,1,0:T(8,128)(2,1)S(1)} collective-permute-done((bf16[2,576,128]{2,1,0:T(8,128)(2,1)S(1)}, bf16[2,576,128]{2,1,0:T(8,128)(2,1)S(1)}, u32[]{:S(2)}, u32[]{:S(2)}) %collective-permute-start.6) | collective-permute-done | bytes 294944 | tf_op jit(solution)/shard_map/ppermute | solution.py:414
  82.3 0.1 fusion.3
  82.4 1.5 %collective-permute-start.3 = (bf16[2,576,128]{2,1,0:T(8,128)(2,1)S(1)}, bf16[2,576,128]{2,1,0:T(8,128)(2,1)S(1)}, u32[]{:S(2)}, u32[]{:S(2)}) collective-permute-start(bf16[2,576,128]{2,1,0:T(8,128)(2,1)S(1)} %get-tuple-element.12), channel_id=1, source_target_pairs={{0,4},{4,8},{8,12},{12,14},{14,10},{10,6},{6,2},{2,0},{1,5},{5,9},... | collective-permute-start | bytes 884744 | tf_op jit(solution)/shard_map/ppermute | solution.py:413
  83.9 0.5 collective-permute-start.7
  84.6 0.1 broadcast_in_dim.22.inverse
  84.7 4.5 %collective-permute-done.3.right = bf16[2,576,128]{2,1,0:T(8,128)(2,1)S(1)} collective-permute-done((bf16[2,576,128]{2,1,0:T(8,128)(2,1)S(1)}, bf16[2,576,128]{2,1,0:T(8,128)(2,1)S(1)}, u32[]{:S(2)}, u32[]{:S(2)}) %collective-permute-start.3) | collective-permute-done | bytes 294944 | tf_op jit(solution)/shard_map/ppermute | solution.py:413
  89.2 1.5 %collective-permute-done.7.left = bf16[2,576,128]{2,1,0:T(8,128)(2,1)S(1)} collective-permute-done((bf16[2,576,128]{2,1,0:T(8,128)(2,1)S(1)}, bf16[2,576,128]{2,1,0:T(8,128)(2,1)S(1)}, u32[]{:S(2)}, u32[]{:S(2)}) %collective-permute-start.7) | collective-permute-done | bytes 294944 | tf_op jit(solution)/shard_map/ppermute | solution.py:414
  90.7 2.3 %stretch_attention.1 = bf16[8,2,48,128]{3,2,1,0:T(8,128)(2,1)} custom-call(s32[3]{0:T(128)S(1)} %dynamic_slice.6.targets, f32[1,2,576,128]{3,2,1,0:T(8,128)S(1)} %slice.56.own, bf16[2,576,128]{2,1,0:T(8,128)(2,1)S(1)} %collective-permute-done.3.right, bf16[2,576,128]{2,1,0:T(8,128)(2,1)S(1)} %collective-permute-done.7.left, ...), custom_call_target="tpu_custom_call" | custom-call | tf_op jit(solution)/shard_map/stretch_attention/pallas_call | solution.py:261
  93.0 3.7 %all-to-all-start.1 = ((bf16[16,48,128]{2,1,0:T(8,128)(2,1)}), bf16[16,48,128]{2,1,0:T(8,128)(2,1)S(1)}, u32[]{:S(2)}, u32[]{:S(2)}) async-start(bf16[16,48,128]{2,1,0:T(8,128)(2,1)} %bitcast.30), calls=%async_computation.1 | async-start | bytes 393216 | tf_op jit(solution)/shard_map/all_to_all | solution.py:419
  96.7 0.6 compare_reduce_fusion
  97.4 0.7 fusion.23
  99.5 2.2 %copy-done.8 = bf16[1,1024,2048]{2,1,0:T(8,128)(2,1)S(1)} copy-done((bf16[1,1024,2048]{2,1,0:T(8,128)(2,1)S(1)}, bf16[1,1024,2048]{2,1,0:T(8,128)(2,1)}, u32[]{:S(2)}) %copy-start.8) | copy-done | bytes 4194328
  101.6 5.4 %cache_attention.1 = bf16[8,48,128]{2,1,0:T(8,128)(2,1)S(1)} custom-call(s32[2]{0:T(128)S(1)} %pad_add_fusion.info, bf16[8,32,128]{2,1,0:T(8,128)(2,1)S(1)} %bitcast.92, bf16[1,1024,2048]{2,1,0:T(8,128)(2,1)S(1)} %copy-done.8, bf16[1,1024,2048]{2,1,0:T(8,128)(2,1)S(1)} %copy-done.8, bf16[16,2048]{1,0:T(8,128)(2,1)S(1)} %pad.16.fresh_keys.fresh_values, ...), custom_call_target="tpu_custom_call" | custom-call | flops 134217728 | bytes 4194304 | tf_op jit(solution)/shard_map/cache_attention/pallas_call | solution.py:202
  107.1 2.0 %all-gather = bf16[16,48,128]{2,1,0:T(8,128)(2,1)S(1)} all-gather(bf16[8,48,128]{2,1,0:T(8,128)(2,1)S(1)} %cache_attention.1), channel_id=2, replica_groups=mesh['grp'=2,'tp'=8,'rep'=2] {'rep'}, dimensions={0}, use_global_device_ids=true | all-gather | bytes 294912 | tf_op jit(solution)/shard_map/all_gather | solution.py:395
  109.1 0.3 combine.1
  109.3 0.7 reshape.111
  (73 shorter events, 0.9 us)
Async XLA Ops:
  0.8 5.8 %copy-start = (s32[2048,2048]{1,0:T(8,128)S(1)}, s32[2048,2048]{1,0:T(8,128)}, u32[]{:S(2)}) copy-start(s32[2048,2048]{1,0:T(8,128)} %value_codes.7) | copy-start | bytes 50331652
  6.5 1.7 %copy-start.4 = (bf16[192,3,2048]{2,0,1:T(8,128)(2,1)S(1)}, bf16[192,3,2048]{2,0,1:T(8,128)(2,1)}, u32[]{:S(2)}) copy-start(bf16[192,3,2048]{2,0,1:T(8,128)(2,1)} %param.16) | copy-start | bytes 7077892
  8.2 0.9 copy-start.6
  9.1 0.7 copy-start.12
  9.8 0.7 copy-start.14
  13.6 4.6 %copy-start.18 = (bf16[1,2,16384]{2,1,0:T(2,128)(2,1)S(1)}, bf16[1,2,16384]{2,1,0:T(2,128)(2,1)}, u32[]{:S(2)}) copy-start(bf16[1,2,16384]{2,1,0:T(2,128)(2,1)} %param.25) | copy-start | bytes 196612
  13.6 11.5 %copy-start.20 = (s32[2]{0:T(128)S(1)}, s32[2]{0:T(128)}, u32[]{:S(2)}) copy-start(s32[2]{0:T(128)} %constant.200.clone) | copy-start | bytes 28
  13.6 11.5 %copy-start.21 = (s32[2]{0:T(128)S(1)}, s32[2]{0:T(128)}, u32[]{:S(2)}) copy-start(s32[2]{0:T(128)} %constant.201.clone) | copy-start | bytes 28
  13.6 11.6 %copy-start.5 = (bf16[192,3,2048]{2,0,1:T(8,128)(2,1)S(1)}, bf16[192,3,2048]{2,0,1:T(8,128)(2,1)}, u32[]{:S(2)}) copy-start(bf16[192,3,2048]{2,0,1:T(8,128)(2,1)} %param.16) | copy-start | bytes 7077892
  13.6 11.6 %copy-start.7 = (s32[32,2048]{1,0:T(8,128)S(1)}, s32[32,2048]{1,0:T(8,128)}, u32[]{:S(2)}) copy-start(s32[32,2048]{1,0:T(8,128)} %value_scales.7) | copy-start | bytes 786436
  13.7 11.6 %copy-start.13 = (f32[2048]{0:T(1024)S(1)}, f32[2048]{0:T(1024)}, u32[]{:S(2)}) copy-start(f32[2048]{0:T(1024)} %param.17) | copy-start | bytes 24580
  13.7 11.6 %copy-start.15 = (f32[1,128]{1,0:T(1,128)S(1)}, f32[1,128]{1,0:T(1,128)}, u32[]{:S(2)}) copy-start(f32[1,128]{1,0:T(1,128)} %constant.217.levels) | copy-start | bytes 1540
  14.4 43.2 %collective-permute-start = (bf16[576,128]{1,0:T(8,128)(2,1)}, bf16[576,128]{1,0:T(8,128)(2,1)}, u32[]{:S(2)}, u32[]{:S(2)}) collective-permute-start(bf16[576,128]{1,0:T(8,128)(2,1)} %get-tuple-element.20), channel_id=1, source_target_pairs={{0,4},{4,8},{8,12},{12,14},{14,10},{10,6},{6,2},{2,0},{1,5},{5,9},... | collective-permute-start | bytes 442376 | tf_op jit(solution)/shard_map/ppermute | solution.py:353
  17.5 40.1 %collective-permute-start.4 = (bf16[576,128]{1,0:T(8,128)(2,1)}, bf16[576,128]{1,0:T(8,128)(2,1)}, u32[]{:S(2)}, u32[]{:S(2)}) collective-permute-start(bf16[576,128]{1,0:T(8,128)(2,1)} %get-tuple-element.19), channel_id=1, source_target_pairs={{0,2},{4,0},{8,4},{12,8},{14,12},{10,14},{6,10},{2,6},{1,3},{5,1},... | collective-permute-start | bytes 442376 | tf_op jit(solution)/shard_map/ppermute | solution.py:354
  18.9 65.6 %all-to-all-start = ((bf16[8,48,128]{2,1,0:T(8,128)(2,1)}), bf16[8,48,128]{2,1,0:T(8,128)(2,1)S(1)}, u32[]{:S(2)}, u32[]{:S(2)}) async-start(bf16[8,48,128]{2,1,0:T(8,128)(2,1)} %maximum_bitcast_fusion), calls=%async_computation | async-start | bytes 196608 | tf_op jit(solution)/shard_map/all_to_all | solution.py:370
  25.2 5.8 %copy-start.1 = (s32[2048,2048]{1,0:T(8,128)S(1)}, s32[2048,2048]{1,0:T(8,128)}, u32[]{:S(2)}) copy-start(s32[2048,2048]{1,0:T(8,128)} %value_codes.7) | copy-start | bytes 50331652
  37.4 1.0 copy-start.9
  38.4 0.8 copy-start.24
  38.4 0.9 copy-start.23
  39.4 5.8 %copy-start.2 = (s32[2048,2048]{1,0:T(8,128)S(1)}, s32[2048,2048]{1,0:T(8,128)}, u32[]{:S(2)}) copy-start(s32[2048,2048]{1,0:T(8,128)} %value_codes.7) | copy-start | bytes 50331652
  45.2 11.6 %copy-start.22 = (s32[6]{0:T(128)S(1)}, s32[6]{0:T(128)}, u32[]{:S(2)}) copy-start(s32[6]{0:T(128)} %param.22) | copy-start | bytes 76
  45.2 12.3 %copy-start.19 = (bf16[1,2,2048]{2,1,0:T(2,128)(2,1)S(1)}, bf16[1,2,2048]{2,1,0:T(2,128)(2,1)}, u32[]{:S(2)}) copy-start(bf16[1,2,2048]{2,1,0:T(2,128)(2,1)} %param.26) | copy-start | bytes 24580
  54.4 1.2 %copy-start.10 = (f32[3,2,576,128]{3,2,1,0:T(8,128)}, f32[3,2,576,128]{3,2,1,0:T(8,128)S(1)}, u32[]{:S(2)}) copy-start(f32[3,2,576,128]{3,2,1,0:T(8,128)S(1)} %project.4) | copy-start | bytes 5308420
  55.7 3.2 %copy-start.17 = (bf16[1,576,128]{2,1,0:T(8,128)(2,1)S(1)}, bf16[1,576,128]{2,1,0:T(8,128)(2,1)}, u32[]{:S(2)}) copy-start(bf16[1,576,128]{2,1,0:T(8,128)(2,1)} %get-tuple-element.18) | copy-start | bytes 442372
  55.7 5.3 %copy-start.16 = (bf16[1,576,128]{2,1,0:T(8,128)(2,1)S(1)}, bf16[1,576,128]{2,1,0:T(8,128)(2,1)}, u32[]{:S(2)}) copy-start(bf16[1,576,128]{2,1,0:T(8,128)(2,1)} %get-tuple-element.17) | copy-start | bytes 442372
  58.9 14.4 %collective-permute-start.1 = (bf16[2,576,128]{2,1,0:T(8,128)(2,1)S(1)}, bf16[2,576,128]{2,1,0:T(8,128)(2,1)S(1)}, u32[]{:S(2)}, u32[]{:S(2)}) collective-permute-start(bf16[2,576,128]{2,1,0:T(8,128)(2,1)S(1)} %pad_maximum_fusion), channel_id=1, source_target_pairs={{0,4},{4,8},{8,12},{12,14},{14,10},{10,6},{6,2},{2,0},{1,5},{5,9},... | collective-permute-start | bytes 884744 | tf_op jit(solution)/shard_map/ppermute | solution.py:413
  61.0 12.3 %collective-permute-start.5 = (bf16[2,576,128]{2,1,0:T(8,128)(2,1)S(1)}, bf16[2,576,128]{2,1,0:T(8,128)(2,1)S(1)}, u32[]{:S(2)}, u32[]{:S(2)}) collective-permute-start(bf16[2,576,128]{2,1,0:T(8,128)(2,1)S(1)} %pad_maximum_fusion.1), channel_id=1, source_target_pairs={{0,2},{4,0},{8,4},{12,8},{14,12},{10,14},{6,10},{2,6},{1,3},{5,1},... | collective-permute-start | bytes 884744 | tf_op jit(solution)/shard_map/ppermute | solution.py:414
  61.1 5.8 %copy-start.3 = (s32[2048,2048]{1,0:T(8,128)S(1)}, s32[2048,2048]{1,0:T(8,128)}, u32[]{:S(2)}) copy-start(s32[2048,2048]{1,0:T(8,128)} %value_codes.7) | copy-start | bytes 50331652
  73.3 9.0 %copy-start.11 = (f32[3,2,576,128]{3,2,1,0:T(8,128)S(1)}, f32[3,2,576,128]{3,2,1,0:T(8,128)}, u32[]{:S(2)}) copy-start(f32[3,2,576,128]{3,2,1,0:T(8,128)} %copy-done.10) | copy-start | bytes 5308420
  73.4 7.4 %collective-permute-start.2 = (bf16[2,576,128]{2,1,0:T(8,128)(2,1)S(1)}, bf16[2,576,128]{2,1,0:T(8,128)(2,1)S(1)}, u32[]{:S(2)}, u32[]{:S(2)}) collective-permute-start(bf16[2,576,128]{2,1,0:T(8,128)(2,1)S(1)} %get-tuple-element.14), channel_id=1, source_target_pairs={{0,4},{4,8},{8,12},{12,14},{14,10},{10,6},{6,2},{2,0},{1,5},{5,9},... | collective-permute-start | bytes 884744 | tf_op jit(solution)/shard_map/ppermute | solution.py:413
  75.5 6.8 %collective-permute-start.6 = (bf16[2,576,128]{2,1,0:T(8,128)(2,1)S(1)}, bf16[2,576,128]{2,1,0:T(8,128)(2,1)S(1)}, u32[]{:S(2)}, u32[]{:S(2)}) collective-permute-start(bf16[2,576,128]{2,1,0:T(8,128)(2,1)S(1)} %get-tuple-element.13), channel_id=1, source_target_pairs={{0,2},{4,0},{8,4},{12,8},{14,12},{10,14},{6,10},{2,6},{1,3},{5,1},... | collective-permute-start | bytes 884744 | tf_op jit(solution)/shard_map/ppermute | solution.py:414
  82.4 6.8 %collective-permute-start.3 = (bf16[2,576,128]{2,1,0:T(8,128)(2,1)S(1)}, bf16[2,576,128]{2,1,0:T(8,128)(2,1)S(1)}, u32[]{:S(2)}, u32[]{:S(2)}) collective-permute-start(bf16[2,576,128]{2,1,0:T(8,128)(2,1)S(1)} %get-tuple-element.12), channel_id=1, source_target_pairs={{0,4},{4,8},{8,12},{12,14},{14,10},{10,6},{6,2},{2,0},{1,5},{5,9},... | collective-permute-start | bytes 884744 | tf_op jit(solution)/shard_map/ppermute | solution.py:413
  83.9 6.7 %collective-permute-start.7 = (bf16[2,576,128]{2,1,0:T(8,128)(2,1)S(1)}, bf16[2,576,128]{2,1,0:T(8,128)(2,1)S(1)}, u32[]{:S(2)}, u32[]{:S(2)}) collective-permute-start(bf16[2,576,128]{2,1,0:T(8,128)(2,1)S(1)} %get-tuple-element.11), channel_id=1, source_target_pairs={{0,2},{4,0},{8,4},{12,8},{14,12},{10,14},{6,10},{2,6},{1,3},{5,1},... | collective-permute-start | bytes 884744 | tf_op jit(solution)/shard_map/ppermute | solution.py:414
  93.0 16.1 %all-to-all-start.1 = ((bf16[16,48,128]{2,1,0:T(8,128)(2,1)}), bf16[16,48,128]{2,1,0:T(8,128)(2,1)S(1)}, u32[]{:S(2)}, u32[]{:S(2)}) async-start(bf16[16,48,128]{2,1,0:T(8,128)(2,1)} %bitcast.30), calls=%async_computation.1 | async-start | bytes 393216 | tf_op jit(solution)/shard_map/all_to_all | solution.py:419
  99.5 2.2 %copy-start.8 = (bf16[1,1024,2048]{2,1,0:T(8,128)(2,1)S(1)}, bf16[1,1024,2048]{2,1,0:T(8,128)(2,1)}, u32[]{:S(2)}) copy-start(bf16[1,1024,2048]{2,1,0:T(8,128)(2,1)} %values.1) | copy-start | bytes 12582916

commit v2 on v1

--- a/solution.py
+++ b/solution.py
@@ -51,54 +51,129 @@
     return jnp.where(place < half, 2 * place, 2 * (count - 1 - place) + 1)
 
 
+def in_hbm(*arrays):
+    return [pltpu.with_memory_space_constraint(array, pltpu.HBM) for array in arrays]
+
+
+def weights(codes, scales, outer, column, block):
+    depth = codes.shape[0]
+    count = depth // QBLOCK
+    line = lax.broadcasted_iota(jnp.int32, outer.shape, 0)
+    line = jnp.sum(jnp.where(line == column, outer, 0.0), axis=0, keepdims=True)
+    rows = lax.broadcasted_iota(jnp.int32, (count, outer.shape[1]), 0) + block * count
+    lanes = lax.broadcasted_iota(jnp.int32, (count, outer.shape[1]), 1)
+    second = jnp.sum(jnp.where(rows == lanes, line, 0.0), axis=1, keepdims=True)
+    scale = (scales.astype(F32) + 1.0) / 256.0 * second
+    lane = lax.broadcasted_iota(jnp.int32, (8, 128), 1)
+    table = jnp.zeros((8, 128), F32)
+    for code, level in enumerate(NORMAL_FLOAT_LEVELS):
+        table = jnp.where(lane == code, level, table)
+    table = jnp.broadcast_to(table[None], (depth // 8, 8, 128)).reshape(depth, 128)
+    level = jnp.take_along_axis(table, codes, axis=1, mode="promise_in_bounds")
+    level = level.reshape(depth // QBLOCK, QBLOCK, HEAD_DIM) * scale[:, None, :]
+    return level.reshape(depth, HEAD_DIM).astype(BF16)
+
+
+def both_weights(key_codes, value_codes, key_scales, value_scales, outer, head, block):
+    half = outer.shape[0] // 2
+    column = head // (KV_HEADS // half)
+    count = key_codes.shape[0] // QBLOCK
+    rows = slice(None)
+    if count < outer.shape[1]:
+        rows = pl.ds(pl.multiple_of(block * count, count), count)
+    return jnp.concatenate(
+        [
+            weights(key_codes[...], key_scales[rows, :], outer[...], column, block),
+            weights(value_codes[...], value_scales[rows, :], outer[...], half + column, block),
+        ],
+        axis=1,
+    )
+
+
+def first_kernel(
+    owners, x, key_codes, value_codes, key_scales, value_scales, outer, gain,
+    key_out, value_out, scaled, total,
+):
+    block = pl.program_id(0)
+    groups, tokens, depth = x.shape
+    owner = owners[0]
+    both = both_weights(
+        key_codes, value_codes, key_scales, value_scales, outer, owner % KV_HEADS, block
+    )
+    for group in range(groups):
+        scaled[group] = (x[group].astype(F32) * gain[...]).astype(BF16)
+    product = jnp.dot(scaled[owner // KV_HEADS], both, preferred_element_type=F32)
+
+    @pl.when(block == 0)
+    def _():
+        total[...] = product
+
+    @pl.when(block != 0)
+    def _():
+        total[...] += product
+
+    @pl.when(block == pl.num_programs(0) - 1)
+    def _():
+        key_out[...] = total[:, :HEAD_DIM].astype(BF16)
+        value_out[...] = total[:, HEAD_DIM:].astype(BF16)
+
+
+def project_first(owners, x, codes, scales, outer, gain):
+    groups, tokens, features = x.shape
+    depth = min(512, features)
+    whole = lambda k, o: (0, 0)
+    x, codes, scales, outer, gain = in_hbm(x, codes, scales, outer, gain.reshape(1, features))
+    half_out = jax.ShapeDtypeStruct((tokens, HEAD_DIM), BF16)
+    return pl.pallas_call(
+        first_kernel,
+        grid_spec=pltpu.PrefetchScalarGridSpec(
+            num_scalar_prefetch=1,
+            grid=(features // depth,),
+            in_specs=[
+                pl.BlockSpec((groups, tokens, depth), lambda k, o: (0, 0, k)),
+                pl.BlockSpec((depth, HEAD_DIM), lambda k, o: (k, o[0] % KV_HEADS)),
+                pl.BlockSpec((depth, HEAD_DIM), lambda k, o: (k, KV_HEADS + o[0] % KV_HEADS)),
+                pl.BlockSpec((scales.shape[0], HEAD_DIM), lambda k, o: (0, o[0] % KV_HEADS)),
+                pl.BlockSpec(
+                    (scales.shape[0], HEAD_DIM), lambda k, o: (0, KV_HEADS + o[0] % KV_HEADS)
+                ),
+                pl.BlockSpec(outer.shape, whole),
+                pl.BlockSpec((1, depth), lambda k, o: (0, k)),
+            ],
+            out_specs=[
+                pl.BlockSpec((tokens, HEAD_DIM), whole),
+                pl.BlockSpec((tokens, HEAD_DIM), whole),
+                pl.BlockSpec((groups, tokens, depth), lambda k, o: (0, 0, k)),
+            ],
+            scratch_shapes=[pltpu.VMEM((tokens, 2 * HEAD_DIM), F32)],
+        ),
+        out_shape=[half_out, half_out, jax.ShapeDtypeStruct(x.shape, BF16)],
+        compiler_params=pltpu.CompilerParams(vmem_limit_bytes=24 * 1024 * 1024),
+        cost_estimate=pl.CostEstimate(
+            flops=4 * tokens * features * HEAD_DIM,
+            bytes_accessed=features * 2 * HEAD_DIM * 4 + 2 * x.size * 2,
+            transcendentals=0,
+        ),
+        name="project_first",
+    )(owners, x, codes, codes, scales, scales, outer, gain)
+
+
 def project_kernel(
-    heads, groups, x, key_codes, value_codes, key_scales, value_scales, outer, gain, levels,
-    out, table,
+    owners, x, key_codes, value_codes, key_scales, value_scales, outer, out
 ):
     item, block = pl.program_id(0), pl.program_id(1)
     depth = key_codes.shape[0]
-
-    @pl.when((item == 0) & (block == 0))
-    def _():
-        rows = lax.broadcasted_iota(jnp.int32, (128, 128), 0)
-        lanes = lax.broadcasted_iota(jnp.int32, (128, 128), 1)
-        for at in range(gain.shape[0]):
-            column = jnp.sum(
-                jnp.where(rows == lanes, gain[at : at + 1, :], 0.0), axis=1, keepdims=True
-            )
-            table[at * 128 : (at + 1) * 128, :] = column * levels[...]
-
+    owner = owners[item]
+    both = both_weights(
+        key_codes, value_codes, key_scales, value_scales, outer, owner % KV_HEADS, block
+    )
     begin = pl.multiple_of(block * depth, depth)
-    source = table[pl.ds(begin, depth), :]
-    scale_rows = depth // QBLOCK
-    if scale_rows == key_scales.shape[0]:
-        scale_at = slice(None)
-    else:
-        scale_at = pl.ds(pl.multiple_of(block * scale_rows, scale_rows), scale_rows)
-    head = heads[item]
-    outer_here = outer[scale_at, :]
-    lane = lax.broadcasted_iota(jnp.int32, outer_here.shape, 1)
-
-    def weight(codes, scales, column):
-        second = jnp.sum(jnp.where(lane == column, outer_here, 0.0), axis=1, keepdims=True)
-        scale = (scales[scale_at, :].astype(F32) + 1.0) / 256.0 * second
-        level = jnp.take_along_axis(source, codes[...], axis=1)
-        level = level.reshape(scale_rows, QBLOCK, HEAD_DIM) * scale[:, None, :]
-        return level.reshape(depth, HEAD_DIM).astype(BF16)
-
-    heads_per = KV_HEADS // (outer.shape[1] // 2)
-    both = jnp.concatenate(
-        [
-            weight(key_codes, key_scales, head // heads_per),
-            weight(value_codes, value_scales, outer.shape[1] // 2 + head // heads_per),
-        ],
-        axis=1,
-    )
-    product = jnp.dot(x[0, :, pl.ds(begin, depth)], both, preferred_element_type=F32)
+    lines = x[owner // KV_HEADS, :, pl.ds(begin, depth)]
+    product = jnp.dot(lines, both, preferred_element_type=F32)
 
     if x.shape[2] == depth:
-        out[0, 0] = product[:, :HEAD_DIM].astype(out.dtype)
-        out[0, 1] = product[:, HEAD_DIM:].astype(out.dtype)
+        out[0, 0] = product[:, :HEAD_DIM]
+        out[0, 1] = product[:, HEAD_DIM:]
     else:
 
         @pl.when(block == 0)
@@ -112,30 +187,28 @@
             out[0, 1] += product[:, HEAD_DIM:]
 
 
-def project(owners, x, codes, scales, outer, gain, levels):
+def project(owners, x, codes, scales, outer):
     count = owners.shape[0]
     tokens, features = x.shape[1:]
     depth = min(1024, features)
-    blocks = features // depth
-    heads = owners % KV_HEADS
-    groups = owners // KV_HEADS
+    whole = lambda i, k, o: (0, 0)
+    codes, scales, outer = in_hbm(codes, scales, outer)
     return pl.pallas_call(
         project_kernel,
         grid_spec=pltpu.PrefetchScalarGridSpec(
-            num_scalar_prefetch=2,
-            grid=(count, blocks),
+            num_scalar_prefetch=1,
+            grid=(count, features // depth),
             in_specs=[
-                pl.BlockSpec((1, tokens, features), lambda i, k, h, g: (g[i], 0, 0)),
-                pl.BlockSpec((depth, HEAD_DIM), lambda i, k, h, g: (k, h[i])),
-                pl.BlockSpec((depth, HEAD_DIM), lambda i, k, h, g: (k, KV_HEADS + h[i])),
-                pl.BlockSpec((scales.shape[0], HEAD_DIM), lambda i, k, h, g: (0, h[i])),
-                pl.BlockSpec((scales.shape[0], HEAD_DIM), lambda i, k, h, g: (0, KV_HEADS + h[i])),
-                pl.BlockSpec(outer.shape, lambda i, k, h, g: (0, 0)),
-                pl.BlockSpec(gain.shape, lambda i, k, h, g: (0, 0)),
-                pl.BlockSpec(levels.shape, lambda i, k, h, g: (0, 0)),
+                pl.BlockSpec(memory_space=pltpu.VMEM),
+                pl.BlockSpec((depth, HEAD_DIM), lambda i, k, o: (k, o[i] % KV_HEADS)),
+                pl.BlockSpec((depth, HEAD_DIM), lambda i, k, o: (k, KV_HEADS + o[i] % KV_HEADS)),
+                pl.BlockSpec((scales.shape[0], HEAD_DIM), lambda i, k, o: (0, o[i] % KV_HEADS)),
+                pl.BlockSpec(
+                    (scales.shape[0], HEAD_DIM), lambda i, k, o: (0, KV_HEADS + o[i] % KV_HEADS)
+                ),
+                pl.BlockSpec(outer.shape, whole),
             ],
-            out_specs=pl.BlockSpec((1, 2, tokens, HEAD_DIM), lambda i, k, h, g: (i, 0, 0, 0)),
-            scratch_shapes=[pltpu.VMEM((features, 128), F32)],
+            out_specs=pl.BlockSpec((1, 2, tokens, HEAD_DIM), lambda i, k, o: (i, 0, 0, 0)),
         ),
         out_shape=jax.ShapeDtypeStruct((count, 2, tokens, HEAD_DIM), F32),
         compiler_params=pltpu.CompilerParams(vmem_limit_bytes=24 * 1024 * 1024),
@@ -145,7 +218,27 @@
             transcendentals=0,
         ),
         name="project",
-    )(heads, groups, x, codes, codes, scales, scales, outer, gain, levels)
+    )(owners, x, codes, codes, scales, scales, outer)
+
+
+def merge_kernel(terms, right, left, to_right, to_left):
+    to_right[0] = (terms[0, 0] + right[...].astype(F32)).astype(BF16)
+    to_right[1] = terms[0, 1].astype(BF16)
+    to_left[0] = terms[1, 0].astype(BF16)
+    to_left[1] = (terms[1, 1] + left[...].astype(F32)).astype(BF16)
+
+
+def merge(terms, right, left):
+    vmem = pl.BlockSpec(memory_space=pltpu.VMEM)
+    shape = jax.ShapeDtypeStruct(terms.shape[1:], BF16)
+    return pl.pallas_call(
+        merge_kernel,
+        in_specs=[vmem] * 3,
+        out_specs=[vmem] * 2,
+        out_shape=[shape, shape],
+        compiler_params=pltpu.CompilerParams(vmem_limit_bytes=16 * 1024 * 1024),
+        name="merge",
+    )(terms, right, left)
 
 
 def pieces_tail(logs):
@@ -199,6 +292,7 @@
 
 def cache_attention(info, grouped, kv_cache, fresh):
     length = kv_cache.shape[1]
+    (kv_cache,) = in_hbm(kv_cache)
     return pl.pallas_call(
         cache_kernel,
         grid_spec=pltpu.PrefetchScalarGridSpec(
@@ -233,11 +327,12 @@
         for core in range(2):
             out[owner, core, :ROWS] = empty
             out[owner, core, ROWS:] = empty_tail
+    mine = own.shape[0] - 1
     for prompt in range(own.shape[2] // STRETCH):
         at = slice(prompt * STRETCH, (prompt + 1) * STRETCH)
         scale = inverse[at, :]
-        keys = own[0, 0, at] + right[0, at].astype(F32) + left[0, at].astype(F32)
-        values = own[0, 1, at] + right[1, at].astype(F32) + left[1, at].astype(F32)
+        keys = own[mine, 0, at] + right[0, at].astype(F32) + left[0, at].astype(F32)
+        values = own[mine, 1, at] + right[1, at].astype(F32) + left[1, at].astype(F32)
         keys = (keys * scale).astype(BF16).astype(F32)
         values = (values * scale).astype(BF16)
         keys = keys * cosine[at, :] + pltpu.roll(keys, HEAD_DIM // 2, 1) * sine[at, :]
@@ -332,26 +427,15 @@
     place = jnp.where(here % 2 == 0, here // 2, count - 1 - here // 2)
 
     x = stretch.transpose(1, 0, 2).reshape(groups, tokens, features)
-    gain = norm_gain.reshape(features // 128, 128)
-    levels = jnp.pad(jnp.array(NORMAL_FLOAT_LEVELS, F32), (0, 128 - 16)).reshape(1, 128)
+    outer = outer_scales.T
 
     def owners_at(distances):
         places = (place + jnp.array(distances, jnp.int32)) % count
         return ring_device(places, count).astype(jnp.int32)
 
-    def project_at(distances):
-        return project(
-            owners_at(distances), x, kv_codes, scale_codes, outer_scales, gain, levels
-        )
-
     ring = [ring_device(at, count) for at in range(count)]
     to_right = [(ring[at], ring[(at + 1) % count]) for at in range(count)]
     to_left = [(ring[at], ring[at - 1]) for at in range(count)]
-
-    half = count // 2
-    far = project_at([half])[0].astype(BF16)
-    right = lax.ppermute(far[0], "tp", to_right)
-    left = lax.ppermute(far[1], "tp", to_left)
 
     grouped = queries.reshape(STEPS, KV_HEADS, GROUP, HEAD_DIM).transpose(1, 0, 2, 3)
     grouped = grouped.reshape(KV_HEADS, ROWS, HEAD_DIM)
@@ -367,11 +451,6 @@
         ],
         axis=2,
     ).reshape(count, PART, HEAD_DIM)
-    incoming = lax.all_to_all(outgoing, "tp", split_axis=0, concat_axis=0, tiled=True)
-    squares = jnp.sum(incoming[:, ROWS : ROWS + 3 * width // 128].astype(F32), axis=0)
-    squares = jnp.sum(squares.reshape(3, width), axis=0)[:tokens]
-    inverse = lax.rsqrt(squares / D + EPSILON)[:, None]
-
     first = rep_here * per_rep + group_here * per_group
     targets = lax.dynamic_slice_in_dim(target_rows, first, per_group)
     lengths = lax.dynamic_slice_in_dim(prompt_lengths, first, per_group)
@@ -391,30 +470,47 @@
     )
     info = jnp.stack([span, rep_here]).astype(jnp.int32)
     fresh = jnp.pad(new_kv[0], ((0, 16 - STEPS), (0, 0)))
-    cached = cache_attention(info, grouped, kv_cache, fresh)
-    cached = lax.all_gather(cached, "rep")
+    half = count // 2
+    far_keys, far_values, x_scaled = project_first(
+        owners_at([half]), x, kv_codes, scale_codes, outer, norm_gain
+    )
+    right_in = lax.ppermute(far_keys, "tp", to_right)
+    left_in = lax.ppermute(far_values, "tp", to_left)
 
     distances = list(range(half - 1, 0, -1))
     size = max(1, -(-len(distances) // 3))
-    own = None
     for begin in range(0, len(distances), size):
         here_distances = distances[begin : begin + size]
         wanted = [sign * d for d in here_distances for sign in (1, -1)]
         if begin + size >= len(distances):
             wanted = wanted + [0]
-        terms = project_at(wanted)
+        owners = owners_at(wanted)
+        if begin > 0:
+            owners, right, left = lax.optimization_barrier((owners, right, left))
+        terms = project(owners, x_scaled, kv_codes, scale_codes, outer)
         for at, distance in enumerate(here_distances):
             if distance == half - 1:
-                right = jnp.stack([terms[2 * at, 0] + right.astype(F32), terms[2 * at, 1]])
-                left = jnp.stack([terms[2 * at + 1, 0], terms[2 * at + 1, 1] + left.astype(F32)])
+                right, left = merge(terms, right_in, left_in)
             else:
-                right = terms[2 * at] + right.astype(F32)
-                left = terms[2 * at + 1] + left.astype(F32)
-            right = lax.ppermute(right.astype(BF16), "tp", to_right)
-            left = lax.ppermute(left.astype(BF16), "tp", to_left)
-        own = terms[-1:]
-
-    handed = stretch_attention(targets, own, right, left, inverse, cosine, sine, incoming)
+                right = (terms[2 * at] + right_in.astype(F32)).astype(BF16)
+                left = (terms[2 * at + 1] + left_in.astype(F32)).astype(BF16)
+            if distance == half - 1:
+                outgoing, right, left = lax.optimization_barrier((outgoing, right, left))
+                incoming = lax.all_to_all(
+                    outgoing, "tp", split_axis=0, concat_axis=0, tiled=True
+                )
+            if distance == 1:
+                info, right, left = lax.optimization_barrier((info, right, left))
+            right_in = lax.ppermute(right, "tp", to_right)
+            left_in = lax.ppermute(left, "tp", to_left)
+
+    cached = lax.all_gather(cache_attention(info, grouped, kv_cache, fresh), "rep")
+    squares = jnp.sum(incoming[:, ROWS : ROWS + 3 * width // 128].astype(F32), axis=0)
+    squares = jnp.sum(squares.reshape(3, width), axis=0)[:tokens]
+    inverse = lax.rsqrt(squares / D + EPSILON)[:, None]
+    inverse, cached = lax.optimization_barrier((inverse, cached))
+
+    handed = stretch_attention(targets, terms, right_in, left_in, inverse, cosine, sine, incoming)
     handed = handed.reshape(2 * count, PART, HEAD_DIM)
     handed = lax.all_to_all(handed, ("tp", "rep"), split_axis=0, concat_axis=0, tiled=True)
     handed = handed.reshape(groups, KV_HEADS, 2, PART, HEAD_DIM)

time: 111 us -> 89.9 us (0.81)
  local copies, waits for them, and re-layouts: 36 us -> 5.26 us
  blocking collectives: 2 us -> 16.8 us
  waiting for transfers between devices: 11.4 us -> 0.25 us
  Pallas kernels: 33 us -> 40.3 us
  starting transfers between devices: 19.4 us -> 15.3 us
  other arithmetic: 5.88 us -> 9.2 us
    unnamed x52 -> x29, local copies, waits for them, and re-layouts: 32.3 us -> 2.14 us
    all_to_all x0 -> x1, blocking collectives: none -> 14.9 us  [per_device(): lax.all_to_all(handed, ('tp', 'rep'), split_axis=0, concat_axis=0, tiled=...]
    ppermute x8, waiting for transfers between devices: 11.4 us -> 0.25 us  [the longest x3 0.24 us: per_device(): left_in = lax.ppermute(left, 'tp', to_left)]
    pallas_call x0 -> x2, Pallas kernels: none -> 7.39 us  [the longest x1 6.33 us: project_first(): pl.pallas_call(first_kernel, grid_spec=pltpu.PrefetchScalarGridSpec(num_s...]
    all_to_all x1 -> x0, starting transfers between devices: 3.74 us -> none  [per_device(): lax.all_to_all(handed, ('tp', 'rep'), split_axis=0, concat_axis=0, tiled=...]
    convert_element_type x3 -> x2, other arithmetic: 0.3 us -> 2.98 us  [per_device(): left = (terms[2 * at + 1] + left_in.astype(F32)).astype(BF16)]
    pallas_call x1, Pallas kernels: 5.42 us -> 7.16 us  [cache_attention(): pl.pallas_call(cache_kernel, grid_spec=pltpu.PrefetchScalarGridSpec(num_s...]
    pallas_call x4 -> x3, Pallas kernels: 25 us -> 23.4 us  [project(): pl.pallas_call(project_kernel, grid_spec=pltpu.PrefetchScalarGridSpec(num...]
  transfers between devices with their start and end apart: 10 -> 9, of which waited for: 4 -> 1; matrix products, arithmetic and copies ran while one was open for 7% -> 13% of each run, Pallas kernels for 25% -> 34%
where the time goes in v2:
time: 89.9 us; the launch traced here: 89.3 us
  Pallas kernels  40.3 us (45%)
  blocking collectives  16.8 us (19%)
  starting transfers between devices  15.3 us (17%)
  other arithmetic  9.2 us (10%)
  local copies, waits for them, and re-layouts  5.26 us (6%)
  between operations  2.13 us (2%)
    pallas_call x3, Pallas kernels, project(): pl.pallas_call(project_kernel, grid_spec=pltpu.PrefetchScalarGridSpec(num...  23.4 us
    all_to_all x1, blocking collectives, per_device(): lax.all_to_all(handed, ('tp', 'rep'), split_axis=0, concat_axis=0, tiled=...  14.9 us
    pallas_call x1, Pallas kernels, cache_attention(): pl.pallas_call(cache_kernel, grid_spec=pltpu.PrefetchScalarGridSpec(num_s...  7.16 us
    pallas_call x1, Pallas kernels, project_first(): pl.pallas_call(first_kernel, grid_spec=pltpu.PrefetchScalarGridSpec(num_s...  6.33 us
    all_to_all x1, starting transfers between devices, per_device(): lax.all_to_all(outgoing, 'tp', split_axis=0, concat_axis=0, tiled=True)  6.04 us
    ppermute x3, starting transfers between devices, per_device(): right_in = lax.ppermute(right, 'tp', to_right)  5.89 us
    ppermute x1, starting transfers between devices, per_device(): right_in = lax.ppermute(far_keys, 'tp', to_right)  3.1 us
    convert_element_type x2, other arithmetic, per_device(): left = (terms[2 * at + 1] + left_in.astype(F32)).astype(BF16)  2.98 us
  transfers between devices with their start and end apart: 9, of which 1 were waited for; matrix products, arithmetic and copies ran while one was open for 13% of the time, Pallas kernels for 34%

profile of v2, /device:TPU:0, one launch (start us, length us, event | category | flops | bytes accessed | tf_op | source)
XLA Modules:
  0.0 89.3 jit_solution(9063262841996594014)
XLA Ops:
  0.0 6.3 %project_first.1 = (bf16[576,128]{1,0:T(8,128)(2,1)}, bf16[576,128]{1,0:T(8,128)(2,1)}, bf16[1,576,2048]{2,1,0:T(8,128)(2,1)S(1)}) custom-call(s32[1]{0:T(128)S(6)} %select_n.72.owners, bf16[1,576,2048]{2,1,0:T(8,128)(2,1)} %bitcast.63, s32[2048,2048]{1,0:T(8,128)} %value_codes.7, s32[2048,2048]{1,0:T(8,128)} %value_codes.7, s32[32,2048]{1,0:T(8,128)} %value_scales.7, ...), custom_call_target="tpu_custom_call" | custom-call | flops 603979776 | bytes 6815744 | tf_op jit(solution)/shard_map/project_first/pallas_call | solution.py:127
  6.3 0.0 copy-start.11
  6.3 0.0 copy-start.10
  6.4 3.1 %collective-permute-start = (bf16[576,128]{1,0:T(8,128)(2,1)}, bf16[576,128]{1,0:T(8,128)(2,1)}, u32[]{:S(2)}, u32[]{:S(2)}) collective-permute-start(bf16[576,128]{1,0:T(8,128)(2,1)} %get-tuple-element.21), channel_id=1, source_target_pairs={{0,4},{4,8},{8,12},{12,14},{14,10},{10,6},{6,2},{2,0},{1,5},{5,9},... | collective-permute-start | bytes 442376 | tf_op jit(solution)/shard_map/ppermute | solution.py:477
  9.5 0.0 collective-permute-start.1
  9.5 0.5 multiply_reduce_fusion
  10.0 0.5 multiply_power_fusion
  10.6 0.1 reduce_sum.39
  10.8 0.6 compare_reduce_fusion
  11.4 0.7 fusion.17
  12.7 0.1 dynamic-slice_add_fusion
  12.8 0.1 add_convert_fusion
  12.9 0.1 convert_element_type.74
  12.9 6.9 %project.3.terms = f32[2,2,576,128]{3,2,1,0:T(8,128)S(1)} custom-call(s32[2]{0:T(128)S(1)} %compare_select_fusion.8.owners, bf16[1,576,2048]{2,1,0:T(8,128)(2,1)S(1)} %get-tuple-element.20.x, s32[2048,2048]{1,0:T(8,128)} %value_codes.7, s32[2048,2048]{1,0:T(8,128)} %value_codes.7, s32[32,2048]{1,0:T(8,128)} %value_scales.7, s32[32,2048]{1,0:T(8,128)} %value_scales.7, ...), custom_call_target="tpu_custom_call" | custom-call | flops 1207959552 | bytes 6553600 | tf_op jit(solution)/shard_map/project/pallas_call | solution.py:196
  19.9 2.0 %fusion.8 = (f32[576,64]{1,0:T(8,128)}, f32[576,64]{1,0:T(8,128)}, f32[576,64]{1,0:T(8,128)}) fusion(f32[64]{0:T(128)S(1)} %copy-done.9, f32[576]{0:T(1024)S(1)} %convert_element_type.74), kind=kLoop, calls=%fused_computation.18 | loop fusion | flops 73728 | bytes 444928 | tf_op jit(solution)/shard_map/neg | solution.py:463
  23.1 0.1 pad_add_fusion.info
  23.1 0.7 dynamic_slice.6.targets
  23.9 0.8 copy.23
  24.7 0.0 copy-start.3
  24.8 1.4 %pad.14.fresh_keys.fresh_values = bf16[16,2048]{1,0:T(8,128)(2,1)} pad(bf16[2,2048]{1,0:T(2,128)(2,1)} %bitcast.70, bf16[]{:T(256)} %constant.112.clone.1), padding=0_14x0_0 | pad | bytes 73730 | tf_op jit(solution)/shard_map/jit(_pad)/pad | solution.py:472
  26.1 0.6 maximum_bitcast_fusion
  26.8 0.0 collective-permute-done.right
  26.8 0.0 collective-permute-done.1.left
  26.8 1.1 %merge.1 = (bf16[2,576,128]{2,1,0:T(8,128)(2,1)S(1)}, bf16[2,576,128]{2,1,0:T(8,128)(2,1)S(1)}) custom-call(f32[2,2,576,128]{3,2,1,0:T(8,128)S(1)} %project.3.terms, bf16[576,128]{1,0:T(8,128)(2,1)} %collective-permute-done.right, bf16[576,128]{1,0:T(8,128)(2,1)} %collective-permute-done.1.left), custom_call_target="tpu_custom_call" | custom-call | tf_op jit(solution)/shard_map/merge/pallas_call | solution.py:234
  27.8 2.1 %collective-permute-start.2 = (bf16[2,576,128]{2,1,0:T(8,128)(2,1)S(1)}, bf16[2,576,128]{2,1,0:T(8,128)(2,1)S(1)}, u32[]{:S(2)}, u32[]{:S(2)}) collective-permute-start(bf16[2,576,128]{2,1,0:T(8,128)(2,1)S(1)} %get-tuple-element.26), channel_id=1, source_target_pairs={{0,4},{4,8},{8,12},{12,14},{14,10},{10,6},{6,2},{2,0},{1,5},{5,9},... | collective-permute-start | bytes 884744 | tf_op jit(solution)/shard_map/ppermute | solution.py:504
  29.9 0.7 compare_select_fusion.7.owners
  30.6 7.0 %project.4 = f32[2,2,576,128]{3,2,1,0:T(8,128)S(1)} custom-call(s32[2]{0:T(128)S(1)} %compare_select_fusion.6.owners, bf16[1,576,2048]{2,1,0:T(8,128)(2,1)S(1)} %get-tuple-element.20.x, s32[2048,2048]{1,0:T(8,128)} %value_codes.7, s32[2048,2048]{1,0:T(8,128)} %value_codes.7, s32[32,2048]{1,0:T(8,128)} %value_scales.7, s32[32,2048]{1,0:T(8,128)} %value_scales.7, ...), custom_call_target="tpu_custom_call" | custom-call | flops 1207959552 | bytes 6553600 | tf_op jit(solution)/shard_map/project/pallas_call | solution.py:196
  37.6 0.2 collective-permute-done.3
  37.8 1.0 %fusion.5 = (bf16[2,576,128]{2,1,0:T(8,128)(2,1)}, bf16[2,576,128]{2,1,0:T(8,128)(2,1)}) fusion(f32[2,2,576,128]{3,2,1,0:T(8,128)S(1)} %project.4, bf16[2,576,128]{2,1,0:T(8,128)(2,1)S(1)} %collective-permute-done.3, bf16[2,576,128]{2,1,0:T(8,128)(2,1)S(1)} %collective-permute-done.2), kind=kLoop, calls=%fused_computation.9 | loop fusion | flops 884736 | bytes 2359296 | tf_op jit(solution)/shard_map/convert_element_type | solution.py:496
  38.8 1.8 %collective-permute-start.4 = (bf16[2,576,128]{2,1,0:T(8,128)(2,1)}, bf16[2,576,128]{2,1,0:T(8,128)(2,1)}, u32[]{:S(2)}, u32[]{:S(2)}) collective-permute-start(bf16[2,576,128]{2,1,0:T(8,128)(2,1)} %get-tuple-element.38), channel_id=1, source_target_pairs={{0,4},{4,8},{8,12},{12,14},{14,10},{10,6},{6,2},{2,0},{1,5},{5,9},... | collective-permute-start | bytes 884744 | tf_op jit(solution)/shard_map/ppermute | solution.py:504
  40.6 0.2 collective-permute-start.5
  40.8 0.2 pad_maximum_fusion
  41.0 6.0 %all-to-all-start = ((bf16[8,48,128]{2,1,0:T(8,128)(2,1)}), bf16[8,48,128]{2,1,0:T(8,128)(2,1)S(1)}, u32[]{:S(2)}, u32[]{:S(2)}) async-start(bf16[8,48,128]{2,1,0:T(8,128)(2,1)} %maximum_bitcast_fusion), calls=%async_computation | async-start | bytes 196608 | tf_op jit(solution)/shard_map/all_to_all | solution.py:499
  47.1 9.5 %project.5.own = f32[3,2,576,128]{3,2,1,0:T(8,128)S(1)} custom-call(s32[3]{0:T(128)S(1)} %compare_select_fusion.7.owners, bf16[1,576,2048]{2,1,0:T(8,128)(2,1)S(1)} %get-tuple-element.20.x, s32[2048,2048]{1,0:T(8,128)} %value_codes.7, s32[2048,2048]{1,0:T(8,128)} %value_codes.7, s32[32,2048]{1,0:T(8,128)} %value_scales.7, s32[32,2048]{1,0:T(8,128)} %value_scales.7, ...), custom_call_target="tpu_custom_call" | custom-call | flops 1811939328 | bytes 8650752 | tf_op jit(solution)/shard_map/project/pallas_call | solution.py:196
  56.6 0.0 copy-start.4
  56.6 0.0 collective-permute-done.4
  56.6 0.0 collective-permute-done.5
  56.6 2.0 %fusion.1 = (bf16[2,576,128]{2,1,0:T(8,128)(2,1)}, bf16[2,576,128]{2,1,0:T(8,128)(2,1)}) fusion(f32[3,2,576,128]{3,2,1,0:T(8,128)S(1)} %project.5.own, bf16[2,576,128]{2,1,0:T(8,128)(2,1)} %collective-permute-done.5, bf16[2,576,128]{2,1,0:T(8,128)(2,1)} %collective-permute-done.4), kind=kLoop, calls=%fused_computation.3 | loop fusion | flops 884736 | bytes 2359296 | tf_op jit(solution)/shard_map/convert_element_type | solution.py:496
  58.7 1.2 %copy-done = f32[3,2,576,128]{3,2,1,0:T(8,128)} copy-done((f32[3,2,576,128]{3,2,1,0:T(8,128)}, f32[3,2,576,128]{3,2,1,0:T(8,128)S(1)}, u32[]{:S(2)}) %copy-start) | copy-done | bytes 1769496
  59.9 2.0 %collective-permute-start.6 = (bf16[2,576,128]{2,1,0:T(8,128)(2,1)}, bf16[2,576,128]{2,1,0:T(8,128)(2,1)S(1)}, u32[]{:S(2)}, u32[]{:S(2)}) collective-permute-start(bf16[2,576,128]{2,1,0:T(8,128)(2,1)} %get-tuple-element.32), channel_id=1, source_target_pairs={{0,4},{4,8},{8,12},{12,14},{14,10},{10,6},{6,2},{2,0},{1,5},{5,9},... | collective-permute-start | bytes 884744 | tf_op jit(solution)/shard_map/ppermute | solution.py:504
  61.9 0.0 collective-permute-start.7
  62.0 7.2 %cache_attention.1 = bf16[8,48,128]{2,1,0:T(8,128)(2,1)S(1)} custom-call(s32[2]{0:T(128)S(1)} %pad_add_fusion.info, bf16[8,32,128]{2,1,0:T(8,128)(2,1)S(1)} %bitcast.62, bf16[1,1024,2048]{2,1,0:T(8,128)(2,1)} %values.1, bf16[1,1024,2048]{2,1,0:T(8,128)(2,1)} %values.1, bf16[16,2048]{1,0:T(8,128)(2,1)S(1)} %copy-done.2, bf16[16,2048]{1,0:T(8,128)(2,1)S(1)} %copy-done.2), custom_call_target="tpu_custom_call" | custom-call | flops 134217728 | bytes 4194304 | tf_op jit(solution)/shard_map/cache_attention/pallas_call | solution.py:296
  69.2 1.9 %all-gather = bf16[16,48,128]{2,1,0:T(8,128)(2,1)S(1)} all-gather(bf16[8,48,128]{2,1,0:T(8,128)(2,1)S(1)} %cache_attention.1), channel_id=2, replica_groups=mesh['grp'=2,'tp'=8,'rep'=2] {'rep'}, dimensions={0}, use_global_device_ids=true | all-gather | bytes 294912 | tf_op jit(solution)/shard_map/all_gather | solution.py:507
  71.2 0.2 copy.22.inverse
  71.4 2.1 %stretch_attention.1 = bf16[8,2,48,128]{3,2,1,0:T(8,128)(2,1)S(1)} custom-call(s32[3]{0:T(128)S(1)} %dynamic_slice.6.targets, f32[3,2,576,128]{3,2,1,0:T(8,128)S(1)} %copy-done.1, bf16[2,576,128]{2,1,0:T(8,128)(2,1)S(1)} %collective-permute-done.6.right, bf16[2,576,128]{2,1,0:T(8,128)(2,1)} %collective-permute-done.7.left, f32[576,1]{1,0:T(8,128)S(1)} %copy.22.inverse, ...), custom_call_target="tpu_custom_call" | custom-call | tf_op jit(solution)/shard_map/stretch_attention/pallas_call | solution.py:356
  73.4 14.9 %all_to_all.10 = bf16[16,48,128]{2,1,0:T(8,128)(2,1)S(1)} all-to-all(bf16[16,48,128]{2,1,0:T(8,128)(2,1)S(1)} %bitcast.60), channel_id=1, replica_groups=mesh['grp'=2,'tp'=8,'rep'=2] {'tp','rep'}, dimensions={0} | all-to-all | bytes 393216 | tf_op jit(solution)/shard_map/all_to_all | solution.py:515
  88.3 0.3 combine.1
  88.6 0.7 reshape.98
  (41 shorter events, 0.2 us)
Async XLA Ops:
  0.0 9.5 %copy-start.5 = (bf16[192,3,2048]{2,0,1:T(8,128)(2,1)S(1)}, bf16[192,3,2048]{2,0,1:T(8,128)(2,1)}, u32[]{:S(2)}) copy-start(bf16[192,3,2048]{2,0,1:T(8,128)(2,1)} %param.15) | copy-start | bytes 7077892
  6.3 4.2 %copy-start.13 = (s32[2]{0:T(128)S(1)}, s32[2]{0:T(128)}, u32[]{:S(2)}) copy-start(s32[2]{0:T(128)} %constant.137.clone) | copy-start | bytes 28
  6.3 4.4 %copy-start.12 = (s32[2]{0:T(128)S(1)}, s32[2]{0:T(128)}, u32[]{:S(2)}) copy-start(s32[2]{0:T(128)} %constant.138.clone) | copy-start | bytes 28
  6.3 4.4 %copy-start.11 = (s32[6]{0:T(128)S(1)}, s32[6]{0:T(128)}, u32[]{:S(2)}) copy-start(s32[6]{0:T(128)} %param.21) | copy-start | bytes 76
  6.3 5.0 %copy-start.10 = (s32[6]{0:T(128)S(1)}, s32[6]{0:T(128)}, u32[]{:S(2)}) copy-start(s32[6]{0:T(128)} %param.20) | copy-start | bytes 76
  6.4 20.4 %collective-permute-start = (bf16[576,128]{1,0:T(8,128)(2,1)}, bf16[576,128]{1,0:T(8,128)(2,1)}, u32[]{:S(2)}, u32[]{:S(2)}) collective-permute-start(bf16[576,128]{1,0:T(8,128)(2,1)} %get-tuple-element.21), channel_id=1, source_target_pairs={{0,4},{4,8},{8,12},{12,14},{14,10},{10,6},{6,2},{2,0},{1,5},{5,9},... | collective-permute-start | bytes 442376 | tf_op jit(solution)/shard_map/ppermute | solution.py:477
  9.5 17.3 %collective-permute-start.1 = (bf16[576,128]{1,0:T(8,128)(2,1)}, bf16[576,128]{1,0:T(8,128)(2,1)}, u32[]{:S(2)}, u32[]{:S(2)}) collective-permute-start(bf16[576,128]{1,0:T(8,128)(2,1)} %get-tuple-element.22), channel_id=1, source_target_pairs={{0,2},{4,0},{8,4},{12,8},{14,12},{10,14},{6,10},{2,6},{1,3},{5,1},... | collective-permute-start | bytes 442376 | tf_op jit(solution)/shard_map/ppermute | solution.py:478
  12.9 6.9 %copy-start.9 = (f32[64]{0:T(128)S(1)}, f32[64]{0:T(128)}, u32[]{:S(2)}) copy-start(f32[64]{0:T(128)} %multiply_power_fusion) | copy-start | bytes 772
  24.7 1.4 %copy-start.3 = (bf16[2,8,16,128]{3,2,0,1:T(8,128)(2,1)}, bf16[2,8,16,128]{3,2,0,1:T(8,128)(2,1)S(1)}, u32[]{:S(2)}) copy-start(bf16[2,8,16,128]{3,2,0,1:T(8,128)(2,1)S(1)} %copy.21) | copy-start | bytes 196612
  27.8 9.7 %collective-permute-start.2 = (bf16[2,576,128]{2,1,0:T(8,128)(2,1)S(1)}, bf16[2,576,128]{2,1,0:T(8,128)(2,1)S(1)}, u32[]{:S(2)}, u32[]{:S(2)}) collective-permute-start(bf16[2,576,128]{2,1,0:T(8,128)(2,1)S(1)} %get-tuple-element.26), channel_id=1, source_target_pairs={{0,4},{4,8},{8,12},{12,14},{14,10},{10,6},{6,2},{2,0},{1,5},{5,9},... | collective-permute-start | bytes 884744 | tf_op jit(solution)/shard_map/ppermute | solution.py:504
  29.9 7.9 %collective-permute-start.3 = (bf16[2,576,128]{2,1,0:T(8,128)(2,1)S(1)}, bf16[2,576,128]{2,1,0:T(8,128)(2,1)S(1)}, u32[]{:S(2)}, u32[]{:S(2)}) collective-permute-start(bf16[2,576,128]{2,1,0:T(8,128)(2,1)S(1)} %get-tuple-element.27), channel_id=1, source_target_pairs={{0,2},{4,0},{8,4},{12,8},{14,12},{10,14},{6,10},{2,6},{1,3},{5,1},... | collective-permute-start | bytes 884744 | tf_op jit(solution)/shard_map/ppermute | solution.py:505
  37.5 3.3 %copy-start.6 = (f32[576,64]{1,0:T(8,128)S(1)}, f32[576,64]{1,0:T(8,128)}, u32[]{:S(2)}) copy-start(f32[576,64]{1,0:T(8,128)} %get-tuple-element.39) | copy-start | bytes 442372
  37.6 3.3 %copy-start.7 = (f32[576,64]{1,0:T(8,128)S(1)}, f32[576,64]{1,0:T(8,128)}, u32[]{:S(2)}) copy-start(f32[576,64]{1,0:T(8,128)} %get-tuple-element.40) | copy-start | bytes 442372
  37.6 3.2 %copy-start.8 = (f32[576,64]{1,0:T(8,128)S(1)}, f32[576,64]{1,0:T(8,128)}, u32[]{:S(2)}) copy-start(f32[576,64]{1,0:T(8,128)} %get-tuple-element.41) | copy-start | bytes 442372
  38.8 17.8 %collective-permute-start.4 = (bf16[2,576,128]{2,1,0:T(8,128)(2,1)}, bf16[2,576,128]{2,1,0:T(8,128)(2,1)}, u32[]{:S(2)}, u32[]{:S(2)}) collective-permute-start(bf16[2,576,128]{2,1,0:T(8,128)(2,1)} %get-tuple-element.38), channel_id=1, source_target_pairs={{0,4},{4,8},{8,12},{12,14},{14,10},{10,6},{6,2},{2,0},{1,5},{5,9},... | collective-permute-start | bytes 884744 | tf_op jit(solution)/shard_map/ppermute | solution.py:504
  40.6 16.1 %collective-permute-start.5 = (bf16[2,576,128]{2,1,0:T(8,128)(2,1)}, bf16[2,576,128]{2,1,0:T(8,128)(2,1)}, u32[]{:S(2)}, u32[]{:S(2)}) collective-permute-start(bf16[2,576,128]{2,1,0:T(8,128)(2,1)} %get-tuple-element.37), channel_id=1, source_target_pairs={{0,2},{4,0},{8,4},{12,8},{14,12},{10,14},{6,10},{2,6},{1,3},{5,1},... | collective-permute-start | bytes 884744 | tf_op jit(solution)/shard_map/ppermute | solution.py:505
  41.0 20.9 %all-to-all-start = ((bf16[8,48,128]{2,1,0:T(8,128)(2,1)}), bf16[8,48,128]{2,1,0:T(8,128)(2,1)S(1)}, u32[]{:S(2)}, u32[]{:S(2)}) async-start(bf16[8,48,128]{2,1,0:T(8,128)(2,1)} %maximum_bitcast_fusion), calls=%async_computation | async-start | bytes 196608 | tf_op jit(solution)/shard_map/all_to_all | solution.py:499
  56.6 5.4 %copy-start.2 = (bf16[16,2048]{1,0:T(8,128)(2,1)S(1)}, bf16[16,2048]{1,0:T(8,128)(2,1)}, u32[]{:S(2)}) copy-start(bf16[16,2048]{1,0:T(8,128)(2,1)} %pad.14.fresh_keys.fresh_values) | copy-start | bytes 196612
  56.6 5.4 %copy-start.4 = (bf16[2,8,16,128]{3,2,0,1:T(8,128)(2,1)S(1)}, bf16[2,8,16,128]{3,2,0,1:T(8,128)(2,1)}, u32[]{:S(2)}) copy-start(bf16[2,8,16,128]{3,2,0,1:T(8,128)(2,1)} %copy-done.3) | copy-start | bytes 196612
  58.7 1.2 %copy-start = (f32[3,2,576,128]{3,2,1,0:T(8,128)}, f32[3,2,576,128]{3,2,1,0:T(8,128)S(1)}, u32[]{:S(2)}) copy-start(f32[3,2,576,128]{3,2,1,0:T(8,128)S(1)} %project.5.own) | copy-start | bytes 5308420
  59.9 11.4 %collective-permute-start.6 = (bf16[2,576,128]{2,1,0:T(8,128)(2,1)}, bf16[2,576,128]{2,1,0:T(8,128)(2,1)S(1)}, u32[]{:S(2)}, u32[]{:S(2)}) collective-permute-start(bf16[2,576,128]{2,1,0:T(8,128)(2,1)} %get-tuple-element.32), channel_id=1, source_target_pairs={{0,4},{4,8},{8,12},{12,14},{14,10},{10,6},{6,2},{2,0},{1,5},{5,9},... | collective-permute-start | bytes 884744 | tf_op jit(solution)/shard_map/ppermute | solution.py:504
  61.9 9.4 %collective-permute-start.7 = (bf16[2,576,128]{2,1,0:T(8,128)(2,1)}, bf16[2,576,128]{2,1,0:T(8,128)(2,1)}, u32[]{:S(2)}, u32[]{:S(2)}) collective-permute-start(bf16[2,576,128]{2,1,0:T(8,128)(2,1)} %get-tuple-element.33), channel_id=1, source_target_pairs={{0,2},{4,0},{8,4},{12,8},{14,12},{10,14},{6,10},{2,6},{1,3},{5,1},... | collective-permute-start | bytes 884744 | tf_op jit(solution)/shard_map/ppermute | solution.py:505
  62.0 9.3 %copy-start.1 = (f32[3,2,576,128]{3,2,1,0:T(8,128)S(1)}, f32[3,2,576,128]{3,2,1,0:T(8,128)}, u32[]{:S(2)}) copy-start(f32[3,2,576,128]{3,2,1,0:T(8,128)} %copy-done) | copy-start | bytes 5308420

commit v3 on v2

v3 whole, which is shorter than its diff:
```python
import functools
import math

import jax
import jax.numpy as jnp
import numpy as np
from jax import lax
from jax.experimental import pallas as pl
from jax.experimental.pallas import tpu as pltpu
from jax.sharding import PartitionSpec as P

D = 16384
HEADS = 128
KV_HEADS = 8
HEAD_DIM = 128
STRETCH = 192
STEPS = 2
QBLOCK = 64
GROUP = HEADS // KV_HEADS
ROWS = GROUP * STEPS
TAIL = 16
PART = ROWS + TAIL
NORMAL_FLOAT_LEVELS = [
    -1.0,
    -0.6961928009986877,
    -0.5250730514526367,
    -0.39491748809814453,
    -0.28444138169288635,
    -0.18477343022823334,
    -0.09105003625154495,
    0.0,
    0.07958029955625534,
    0.16093020141124725,
    0.24611230194568634,
    0.33791524171829224,
    0.44070982933044434,
    0.5626170039176941,
    0.7229568362236023,
    1.0,
]
ROTARY_BASE = 500000.0
EPSILON = 1e-05
NEGATIVE = -1e30
BF16 = jnp.bfloat16
F32 = jnp.float32
MIB = 1024 * 1024
VMEM = pl.BlockSpec(memory_space=pltpu.VMEM)
SMEM = pl.BlockSpec(memory_space=pltpu.SMEM)


def in_hbm(*arrays):
    return [pltpu.with_memory_space_constraint(array, pltpu.HBM) for array in arrays]


def ring_device(place, count):
    half = count // 2
    if isinstance(place, int):
        return 2 * place if place < half else 2 * (count - 1 - place) + 1
    return jnp.where(place < half, 2 * place, 2 * (count - 1 - place) + 1)


def owner_at(distance):
    count = lax.axis_size("tp")
    here = lax.axis_index("tp")
    place = jnp.where(here % 2 == 0, here // 2, count - 1 - here // 2)
    return ring_device((place + distance + count) % count, count)


def gathered_levels(codes):
    lane = lax.broadcasted_iota(jnp.int32, (8, 128), 1)
    table = jnp.zeros((8, 128), F32)
    for code, level in enumerate(NORMAL_FLOAT_LEVELS):
        table = jnp.where(lane == code, level, table)
    depth = codes.shape[0]
    table = jnp.broadcast_to(table[None], (depth // 8, 8, 128)).reshape(depth, 128)
    return jnp.take_along_axis(table, codes, axis=1, mode="promise_in_bounds")


def selected_levels(codes):
    values = [jnp.float32(level) for level in NORMAL_FLOAT_LEVELS]
    for bit in (1, 2, 4, 8):
        mask = (codes & bit) != 0 if bit < 8 else codes >= 8
        values = [
            jnp.where(mask, values[at + 1], values[at]) for at in range(0, len(values), 2)
        ]
    return values[0]


def weights(levels, scales, outer, column, block):
    depth = levels.shape[0]
    count = depth // QBLOCK
    line = lax.broadcasted_iota(jnp.int32, outer.shape, 0)
    line = jnp.sum(jnp.where(line == column, outer, 0.0), axis=0, keepdims=True)
    rows = lax.broadcasted_iota(jnp.int32, (count, outer.shape[1]), 0) + block * count
    lanes = lax.broadcasted_iota(jnp.int32, (count, outer.shape[1]), 1)
    second = jnp.sum(jnp.where(rows == lanes, line, 0.0), axis=1, keepdims=True)
    scale = (scales.astype(F32) + 1.0) / 256.0 * second
    levels = levels.reshape(count, QBLOCK, HEAD_DIM) * scale[:, None, :]
    return levels.reshape(depth, HEAD_DIM).astype(BF16)


def both_weights(key_codes, value_codes, key_scales, value_scales, outer, head, block):
    half = outer.shape[0] // 2
    column = head // (KV_HEADS // half)
    count = key_codes.shape[0] // QBLOCK
    rows = slice(None)
    if count < outer.shape[1]:
        rows = pl.ds(pl.multiple_of(block * count, count), count)
    keys = gathered_levels(key_codes[...])
    values = selected_levels(value_codes[...])
    return jnp.concatenate(
        [
            weights(keys, key_scales[rows, :], outer[...], column, block),
            weights(values, value_scales[rows, :], outer[...], half + column, block),
        ],
        axis=1,
    )


def first_kernel(
    x, key_codes, value_codes, key_scales, value_scales, outer, gain,
    key_out, value_out, scaled, total,
):
    block = pl.program_id(0)
    owner = owner_at(lax.axis_size("tp") // 2)
    both = both_weights(
        key_codes, value_codes, key_scales, value_scales, outer, owner % KV_HEADS, block
    )
    for group in range(x.shape[0]):
        scaled[group] = (x[group].astype(F32) * gain[...]).astype(BF16)
    product = jnp.dot(scaled[owner // KV_HEADS], both, preferred_element_type=F32)

    @pl.when(block == 0)
    def _():
        total[...] = product

    @pl.when(block != 0)
    def _():
        total[...] += product

    @pl.when(block == pl.num_programs(0) - 1)
    def _():
        key_out[...] = total[:, :HEAD_DIM].astype(BF16)
        value_out[...] = total[:, HEAD_DIM:].astype(BF16)


def project_first(x, codes, scales, outer, gain):
    groups, tokens, features = x.shape
    depth = min(512, features)
    head = lambda: owner_at(lax.axis_size("tp") // 2) % KV_HEADS
    whole = lambda k: (0, 0)
    scale_block = (scales.shape[0], HEAD_DIM)
    x, codes, scales, outer, gain = in_hbm(x, codes, scales, outer, gain.reshape(1, features))
    half_out = jax.ShapeDtypeStruct((tokens, HEAD_DIM), BF16)
    return pl.pallas_call(
        first_kernel,
        grid=(features // depth,),
        in_specs=[
            pl.BlockSpec((groups, tokens, depth), lambda k: (0, 0, k)),
            pl.BlockSpec((depth, HEAD_DIM), lambda k: (k, head())),
            pl.BlockSpec((depth, HEAD_DIM), lambda k: (k, KV_HEADS + head())),
            pl.BlockSpec(scale_block, lambda k: (0, head())),
            pl.BlockSpec(scale_block, lambda k: (0, KV_HEADS + head())),
            pl.BlockSpec(outer.shape, whole),
            pl.BlockSpec((1, depth), lambda k: (0, k)),
        ],
        out_specs=[
            pl.BlockSpec((tokens, HEAD_DIM), whole),
            pl.BlockSpec((tokens, HEAD_DIM), whole),
            pl.BlockSpec((groups, tokens, depth), lambda k: (0, 0, k)),
        ],
        scratch_shapes=[pltpu.VMEM((tokens, 2 * HEAD_DIM), F32)],
        out_shape=[half_out, half_out, jax.ShapeDtypeStruct(x.shape, BF16)],
        compiler_params=pltpu.CompilerParams(vmem_limit_bytes=24 * MIB),
        cost_estimate=pl.CostEstimate(
            flops=4 * tokens * features * HEAD_DIM,
            bytes_accessed=features * 2 * HEAD_DIM * 4 + 2 * x.size * 2,
            transcendentals=0,
        ),
        name="project_first",
    )(x, codes, codes, scales, scales, outer, gain)


def distance_at(farthest, item):
    return (farthest - item // 2) * (1 - 2 * (item % 2))


def project_kernel(
    farthest, x, key_codes, value_codes, key_scales, value_scales, outer, out
):
    item, block = pl.program_id(0), pl.program_id(1)
    depth = key_codes.shape[0]
    owner = owner_at(distance_at(farthest, item))
    both = both_weights(
        key_codes, value_codes, key_scales, value_scales, outer, owner % KV_HEADS, block
    )
    begin = pl.multiple_of(block * depth, depth)
    lines = x[owner // KV_HEADS, :, pl.ds(begin, depth)]
    product = jnp.dot(lines, both, preferred_element_type=F32)

    @pl.when(block == 0)
    def _():
        out[item, 0] = product[:, :HEAD_DIM]
        out[item, 1] = product[:, HEAD_DIM:]

    @pl.when(block != 0)
    def _():
        out[item, 0] += product[:, :HEAD_DIM]
        out[item, 1] += product[:, HEAD_DIM:]


def project(farthest, count, x, codes, scales, outer):
    tokens, features = x.shape[1:]
    depth = min(1024, features)
    head = lambda i: owner_at(distance_at(farthest, i)) % KV_HEADS
    scale_block = (scales.shape[0], HEAD_DIM)
    codes, scales, outer = in_hbm(codes, scales, outer)
    return pl.pallas_call(
        functools.partial(project_kernel, farthest),
        grid=(count, features // depth),
        in_specs=[
            VMEM,
            pl.BlockSpec((depth, HEAD_DIM), lambda i, k: (k, head(i))),
            pl.BlockSpec((depth, HEAD_DIM), lambda i, k: (k, KV_HEADS + head(i))),
            pl.BlockSpec(scale_block, lambda i, k: (0, head(i))),
            pl.BlockSpec(scale_block, lambda i, k: (0, KV_HEADS + head(i))),
            pl.BlockSpec(outer.shape, lambda i, k: (0, 0)),
        ],
        out_specs=VMEM,
        out_shape=jax.ShapeDtypeStruct((count, 2, tokens, HEAD_DIM), F32),
        compiler_params=pltpu.CompilerParams(vmem_limit_bytes=40 * MIB),
        cost_estimate=pl.CostEstimate(
            flops=count * 4 * tokens * features * HEAD_DIM,
            bytes_accessed=count * features * 2 * HEAD_DIM * 4 + x.shape[1] * features * 2,
            transcendentals=0,
        ),
        name="project",
    )(x, codes, codes, scales, scales, outer)


def send_kernel(item, halves, terms, right, left, to_right, to_left):
    if halves:
        to_right[0] = (terms[item, 0] + right[...].astype(F32)).astype(BF16)
        to_right[1] = terms[item, 1].astype(BF16)
        to_left[0] = terms[item + 1, 0].astype(BF16)
        to_left[1] = (terms[item + 1, 1] + left[...].astype(F32)).astype(BF16)
    else:
        to_right[...] = (terms[item] + right[...].astype(F32)).astype(BF16)
        to_left[...] = (terms[item + 1] + left[...].astype(F32)).astype(BF16)


def sends(item, halves, terms, right, left):
    shape = jax.ShapeDtypeStruct(terms.shape[1:], BF16)
    return pl.pallas_call(
        functools.partial(send_kernel, item, halves),
        in_specs=[VMEM] * 3,
        out_specs=[VMEM] * 2,
        out_shape=[shape, shape],
        compiler_params=pltpu.CompilerParams(vmem_limit_bytes=16 * MIB),
        name="sends",
    )(terms, right, left)


def direct(count):
    return count <= 8


def part_shapes(count, copies):
    if direct(count):
        return [jax.ShapeDtypeStruct((PART, HEAD_DIM), BF16)] * count
    return [jax.ShapeDtypeStruct((count, copies, PART, HEAD_DIM), BF16)]


def exchange(parts):
    count = lax.axis_size("tp")
    if not direct(count):
        swapped = lax.all_to_all(parts[0], "tp", split_axis=0, concat_axis=0, tiled=True)
        return [swapped]
    turn = lambda by: [(at, (at + by) % count) for at in range(count)]
    return [parts[0]] + [lax.ppermute(parts[by], "tp", turn(by)) for by in range(1, count)]


def exchange_to_both(parts):
    count = lax.axis_size("tp")
    if not direct(count):
        flat = parts[0].reshape(2 * count, PART, HEAD_DIM)
        flat = lax.all_to_all(flat, ("tp", "rep"), split_axis=0, concat_axis=0, tiled=True)
        return [flat.reshape(count, 2, PART, HEAD_DIM)]
    cross = lambda by: [
        (2 * at + rep, 2 * ((at + by) % count) + 1 - rep) for at in range(count) for rep in range(2)
    ]
    other = [lax.ppermute(parts[by], ("tp", "rep"), cross(by)) for by in range(count)]
    return exchange(parts) + other


def pack_kernel(queries, squares, grouped, *outs):
    count = lax.axis_size("tp")
    here = lax.axis_index("tp")
    per_group = squares.shape[0] // (count // KV_HEADS)
    for head in range(KV_HEADS):
        for member in range(GROUP):
            lanes = slice((head * GROUP + member) * HEAD_DIM, (head * GROUP + member + 1) * HEAD_DIM)
            grouped[head, member * STEPS : (member + 1) * STEPS] = queries[0, :, lanes]
    at = lax.broadcasted_iota(jnp.int32, (TAIL, 128), 0)
    tails = []
    for group in range(count // KV_HEADS):
        tail = jnp.zeros((TAIL, 128), F32)
        for prompt in range(per_group):
            line = squares[group * per_group + prompt : group * per_group + prompt + 1, :]
            ends = jnp.concatenate(
                [line[:, 128:], jnp.zeros((1, 256 - STRETCH), F32)], axis=1
            )
            for half, piece in enumerate((line[:, :128], ends)):
                high = piece.astype(BF16).astype(F32)
                tail = jnp.where(at == 2 * prompt + half, high, tail)
                tail = jnp.where(at == TAIL // 2 + 2 * prompt + half, piece - high, tail)
        tails.append(tail.astype(BF16))
    if direct(count):
        for by in range(count):
            outs[by][:ROWS] = grouped[(here + by) % KV_HEADS]
            outs[by][ROWS:] = tails[0]
    else:
        for owner in range(count):
            outs[0][owner, 0, :ROWS] = grouped[owner % KV_HEADS]
            outs[0][owner, 0, ROWS:] = tails[owner // KV_HEADS]


def pack(queries, squares, count):
    return pl.pallas_call(
        pack_kernel,
        in_specs=[VMEM] * 2,
        out_specs=[VMEM] * (1 + len(part_shapes(count, 1))),
        out_shape=[jax.ShapeDtypeStruct((KV_HEADS, ROWS, HEAD_DIM), BF16)] + part_shapes(count, 1),
        compiler_params=pltpu.CompilerParams(vmem_limit_bytes=16 * MIB),
        name="pack",
    )(queries, squares)


def turned(column):
    rows = lax.broadcasted_iota(jnp.int32, (column.shape[0], 128), 0)
    lanes = lax.broadcasted_iota(jnp.int32, (column.shape[0], 128), 1)
    return jnp.sum(jnp.where(rows == lanes, column, 0.0), axis=0, keepdims=True)


def stood(row, count):
    rows = lax.broadcasted_iota(jnp.int32, (count, 128), 0)
    lanes = lax.broadcasted_iota(jnp.int32, (count, 128), 1)
    return jnp.sum(jnp.where(rows == lanes, row, 0.0), axis=1, keepdims=True)


def pieces_tail(logs):
    row = turned(logs)
    high = row.astype(BF16).astype(F32)
    middle = (row - high).astype(BF16).astype(F32)
    low = row - high - middle
    at = lax.broadcasted_iota(jnp.int32, (TAIL, 128), 0)
    tail = jnp.where(at == 0, high, jnp.where(at == 1, middle, jnp.where(at == 2, low, 0.0)))
    return tail.astype(BF16)


def tail_pieces(tail):
    tail = tail.astype(F32)
    return stood(tail[0:1, :] + tail[1:2, :] + tail[2:3, :], ROWS)


CACHE_HEADS = 4


def cache_kernel(targets, lengths, stored, q, keys, values, fresh_keys, fresh_values, out):
    scaling = HEAD_DIM ** (-0.5)
    dims = (((1,), (1,)), ((), ()))
    here = lax.axis_index("tp")
    rep = lax.axis_index("rep")
    length = keys.shape[1]
    span = stored[0]
    for prompt in range(targets.shape[0]):
        span = jnp.where(targets[prompt] == here, lengths[prompt] - STRETCH, span)
    place = lax.broadcasted_iota(jnp.int32, (ROWS, length), 1)
    allowed = place < span - rep * length
    second_step = lax.broadcasted_iota(jnp.int32, (ROWS, 1), 0) % STEPS == 1
    for at in range(CACHE_HEADS):
        lanes = slice(at * HEAD_DIM, (at + 1) * HEAD_DIM)
        query = q[at]
        wide = query.astype(F32)
        scores = lax.dot_general(query, keys[0, :, lanes], dims, preferred_element_type=F32)
        scores = jnp.where(allowed, scores * scaling, NEGATIVE)
        highest = jnp.max(scores, axis=1, keepdims=True)
        fresh = []
        for step in range(STEPS):
            key = fresh_keys[0, step : step + 1, lanes].astype(F32)
            score = jnp.sum(wide * key, axis=1, keepdims=True) * scaling
            shown = rep == 0 if step == 0 else second_step & (rep == 0)
            score = jnp.where(shown, score, NEGATIVE)
            highest = jnp.maximum(highest, score)
            fresh.append(score)
        some = highest > 0.5 * NEGATIVE
        highest = jnp.where(some, highest, 0.0)
        weight = jnp.exp(scores - highest)
        totals = jnp.sum(weight, axis=1, keepdims=True)
        sums = jnp.dot(weight.astype(BF16), values[0, :, lanes], preferred_element_type=F32)
        for step in range(STEPS):
            share = jnp.exp(fresh[step] - highest)
            totals += share
            value = fresh_values[0, step : step + 1, lanes].astype(F32)
            sums += share.astype(BF16).astype(F32) * value
        totals = jnp.where(some, totals, 1.0)
        out[at, :ROWS] = (sums / totals).astype(BF16)
        out[at, ROWS:] = pieces_tail(jnp.where(some, highest + jnp.log(totals), NEGATIVE))


def cache_attention(targets, lengths, stored, grouped, kv_cache, new_kv):
    length = kv_cache.shape[1]
    (kv_cache,) = in_hbm(kv_cache)
    width = CACHE_HEADS * HEAD_DIM
    blocks = KV_HEADS // CACHE_HEADS
    return pl.pallas_call(
        cache_kernel,
        grid=(blocks,),
        in_specs=[
            SMEM,
            SMEM,
            SMEM,
            pl.BlockSpec((CACHE_HEADS, ROWS, HEAD_DIM), lambda h: (h, 0, 0)),
            pl.BlockSpec((1, length, width), lambda h: (0, 0, h)),
            pl.BlockSpec((1, length, width), lambda h: (0, 0, blocks + h)),
            pl.BlockSpec((1, STEPS, width), lambda h: (0, 0, h)),
            pl.BlockSpec((1, STEPS, width), lambda h: (0, 0, blocks + h)),
        ],
        out_specs=pl.BlockSpec((CACHE_HEADS, PART, HEAD_DIM), lambda h: (h, 0, 0)),
        out_shape=jax.ShapeDtypeStruct((KV_HEADS, PART, HEAD_DIM), BF16),
        compiler_params=pltpu.CompilerParams(vmem_limit_bytes=24 * MIB),
        cost_estimate=pl.CostEstimate(
            flops=4 * HEADS * STEPS * length * HEAD_DIM,
            bytes_accessed=length * 2 * KV_HEADS * HEAD_DIM * 2,
            transcendentals=HEADS * STEPS * length,
        ),
        name="cache_attention",
    )(targets, lengths, stored, grouped, kv_cache, kv_cache, new_kv, new_kv)


def stretch_kernel(
    target_rows, starts, turns, own, right, left, *refs
):
    count = lax.axis_size("tp")
    here = lax.axis_index("tp")
    received = refs[: len(part_shapes(count, 1))]
    outs = refs[len(received) : -1]
    rows = refs[-1]
    groups = count // KV_HEADS
    per_group = own.shape[2] // STRETCH
    first = (lax.axis_index("rep") * groups + here // KV_HEADS) * per_group
    scaling = HEAD_DIM ** (-0.5)
    dims = (((1,), (1,)), ((), ()))
    mine = own.shape[0] - 1

    squares = jnp.zeros((TAIL, 128), F32)
    for by in range(count):
        if direct(count):
            rows[(here - by + count) % count] = received[by][:ROWS]
            squares += received[by][ROWS:].astype(F32)
        else:
            rows[by] = received[0][by, 0, :ROWS]
            squares += received[0][by, 0, ROWS:].astype(F32)
    inverse = lax.rsqrt((squares[: TAIL // 2] + squares[TAIL // 2 :]) / D + EPSILON)

    results = []
    for prompt in range(per_group):
        at = slice(prompt * STRETCH, (prompt + 1) * STRETCH)
        scale = jnp.concatenate(
            [
                stood(inverse[2 * prompt : 2 * prompt + 1], 128),
                stood(inverse[2 * prompt + 1 : 2 * prompt + 2], STRETCH - 128),
            ],
            axis=0,
        )
        keys = own[mine, 0, at] + right[0, at].astype(F32) + left[0, at].astype(F32)
        values = own[mine, 1, at] + right[1, at].astype(F32) + left[1, at].astype(F32)
        keys = (keys * scale).astype(BF16).astype(F32)
        values = (values * scale).astype(BF16)
        start_cosine = starts[0, pl.ds(first + prompt, 1), :]
        start_sine = starts[1, pl.ds(first + prompt, 1), :]
        cosine = turns[0] * start_cosine - turns[1] * start_sine
        sine = turns[1] * start_cosine + turns[0] * start_sine
        lane = lax.broadcasted_iota(jnp.int32, sine.shape, 1)
        sine = jnp.where(lane < HEAD_DIM // 2, -sine, sine)
        keys = keys * cosine + pltpu.roll(keys, HEAD_DIM // 2, 1) * sine
        target = target_rows[first + prompt]
        scores = lax.dot_general(rows[target], keys.astype(BF16), dims, preferred_element_type=F32)
        scores = scores * scaling
        highest = jnp.max(scores, axis=1, keepdims=True)
        weight = jnp.exp(scores - highest)
        totals = jnp.sum(weight, axis=1, keepdims=True)
        sums = jnp.dot(weight.astype(BF16), values, preferred_element_type=F32)
        tail = pieces_tail(highest + jnp.log(totals))
        results.append((target, sums / totals, tail))

    empty_tail = pieces_tail(jnp.full((ROWS, 1), NEGATIVE, F32))
    for by in range(count):
        owner = (here + by) % count if direct(count) else by
        part = jnp.zeros((ROWS, HEAD_DIM), F32)
        tail = empty_tail.astype(F32)
        for target, result, result_tail in results:
            part = jnp.where(target == owner, result, part)
            tail = jnp.where(target == owner, result_tail.astype(F32), tail)
        if direct(count):
            outs[by][:ROWS] = part.astype(BF16)
            outs[by][ROWS:] = tail.astype(BF16)
        else:
            for core in range(2):
                outs[0][by, core, :ROWS] = part.astype(BF16)
                outs[0][by, core, ROWS:] = tail.astype(BF16)


def stretch_attention(target_rows, starts, turns, own, right, left, received):
    count = lax.axis_size("tp")
    shapes = part_shapes(count, 2)
    return pl.pallas_call(
        stretch_kernel,
        in_specs=[SMEM] + [VMEM] * (5 + len(received)),
        out_specs=[VMEM] * len(shapes),
        out_shape=shapes,
        scratch_shapes=[pltpu.VMEM((count, ROWS, HEAD_DIM), BF16)],
        compiler_params=pltpu.CompilerParams(vmem_limit_bytes=16 * MIB),
        name="stretch_attention",
    )(target_rows, starts, turns, own, right, left, *received)


def combine_kernel(cached, *refs):
    count = lax.axis_size("tp")
    here = lax.axis_index("tp")
    out = refs[-1]
    for at in range(KV_HEADS):
        if direct(count):
            head = (here - at + count) % count
            handed = [refs[at][...], refs[count + at][...]]
        else:
            head = at
            handed = [
                refs[0][owner, core] for owner in range(at, count, KV_HEADS) for core in range(2)
            ]
        parts = [cached[0, head], cached[1, head]] + handed
        logs = [tail_pieces(part[ROWS:]) for part in parts]
        highest = functools.reduce(jnp.maximum, logs)
        shares = [jnp.exp(log - highest) for log in logs]
        total = functools.reduce(jnp.add, shares)
        sums = functools.reduce(
            jnp.add, [share * part[:ROWS].astype(F32) for share, part in zip(shares, parts)]
        )
        result = (sums / total).astype(BF16)
        for member in range(GROUP):
            begin = pl.multiple_of((head * GROUP + member) * HEAD_DIM, HEAD_DIM)
            out[:, pl.ds(begin, HEAD_DIM)] = result[member * STEPS : (member + 1) * STEPS]


def combine(cached, handed):
    return pl.pallas_call(
        combine_kernel,
        in_specs=[VMEM] * (1 + len(handed)),
        out_specs=VMEM,
        out_shape=jax.ShapeDtypeStruct((STEPS, HEADS * HEAD_DIM), BF16),
        compiler_params=pltpu.CompilerParams(vmem_limit_bytes=16 * MIB),
        name="combine",
    )(cached, *handed)


def rotary_turns():
    half = np.arange(HEAD_DIM // 2, dtype=np.float64) / (HEAD_DIM // 2)
    frequency = ROTARY_BASE ** (-np.concatenate([half, half]))
    angles = np.arange(STRETCH, dtype=np.float64)[:, None] * frequency
    return frequency.astype(np.float32), np.stack([np.cos(angles), np.sin(angles)]).astype(np.float32)


def per_device(
    stretch,
    norm_gain,
    kv_codes,
    scale_codes,
    outer_scales,
    prompt_lengths,
    target_rows,
    cache_lengths,
    kv_cache,
    queries,
    new_kv,
):
    count = lax.axis_size("tp")
    per_rep, features = stretch.shape[1:]
    groups = count // KV_HEADS
    lines = stretch.transpose(1, 0, 2)
    x = lines.reshape(groups, per_rep // groups * STRETCH, features)
    outer = outer_scales.T

    ring = [ring_device(at, count) for at in range(count)]
    to_right = [(ring[at], ring[(at + 1) % count]) for at in range(count)]
    to_left = [(ring[at], ring[at - 1]) for at in range(count)]

    half = count // 2
    far_keys, far_values, x_scaled = project_first(x, kv_codes, scale_codes, outer, norm_gain)
    right_in = lax.ppermute(far_keys, "tp", to_right)
    left_in = lax.ppermute(far_values, "tp", to_left)

    squares = jnp.sum(jnp.square(lines.astype(F32)), axis=2)
    grouped, *parts = pack(queries, squares, count)
    frequency, turns = rotary_turns()
    start = (prompt_lengths - STRETCH).astype(F32)[:, None] * jnp.asarray(frequency)
    starts = jnp.stack([jnp.cos(start), jnp.sin(start)])

    calls = [(half - 1, 2), (half - 2, 2 * (half - 2) + 1)]
    terms, item = None, 0
    for distance in range(half - 1, 0, -1):
        for farthest, items in calls:
            if farthest == distance:
                if distance < half - 1:
                    outer, right, left = lax.optimization_barrier((outer, right, left))
                terms = project(farthest, items, x_scaled, kv_codes, scale_codes, outer)
                item = 0
        right, left = sends(item, distance == half - 1, terms, right_in, left_in)
        item += 2
        if distance == half - 1:
            right, left, *parts = lax.optimization_barrier((right, left, *parts))
            received = exchange(parts)
        if distance == max(1, half - 2):
            right, left, grouped = lax.optimization_barrier((right, left, grouped))
        right_in = lax.ppermute(right, "tp", to_right)
        left_in = lax.ppermute(left, "tp", to_left)

    cached = cache_attention(
        target_rows, prompt_lengths, cache_lengths, grouped, kv_cache, new_kv
    )
    cached = lax.all_gather(cached, "rep")
    starts, cached = lax.optimization_barrier((starts, cached))
    handed = stretch_attention(
        target_rows, starts, jnp.asarray(turns), terms, right_in, left_in, received
    )
    out = combine(cached, exchange_to_both(handed))
    return out.reshape(1, STEPS, HEADS * HEAD_DIM)


def solution(mesh):
    in_specs = (
        P(None, ("grp", "rep"), "tp"),
        P("tp"),
        P("tp", None),
        P("tp", None),
        P("tp", None),
        P("grp"),
        P("grp"),
        P(("grp", "tp")),
        P(("grp", "tp"), "rep", None),
        P(("grp", "tp"), None, None),
        P(("grp", "tp"), None, None),
    )
    out_specs = P(("grp", "tp"), None, None)
    return jax.shard_map(
        per_device, mesh=mesh, in_specs=in_specs, out_specs=out_specs, check_vma=False
    )
```

time: 89.9 us -> 90 us (level)
  starting transfers between devices: 15.3 us -> 42.4 us
  blocking collectives: 16.8 us -> 1.93 us
  waiting for transfers between devices: 0.25 us -> 11.5 us
  other arithmetic: 9.2 us -> 0.66 us
  Pallas kernels: 40.3 us -> 32.4 us
  local copies, waits for them, and re-layouts: 5.26 us -> 0.04 us
  between operations: 2.13 us -> 0.85 us
    ppermute x0 -> x22, starting transfers between devices: none -> 33 us  [the longest x14 22 us: exchange(): lax.ppermute(parts[by], 'tp', turn(by))]
    all_to_all x1 -> x0, blocking collectives: 14.9 us -> none  [per_device(): lax.all_to_all(handed, ('tp', 'rep'), split_axis=0, concat_axis=0, tiled=...]
    pallas_call x8 -> x10, Pallas kernels: 40.3 us -> 32.4 us  [the longest x2 19.2 us: project(): pl.pallas_call(functools.partial(project_kernel, farthest), grid=(count,...]
    all_to_all x1 -> x0, starting transfers between devices: 6.04 us -> none  [per_device(): lax.all_to_all(outgoing, 'tp', split_axis=0, concat_axis=0, tiled=True)]
    ppermute x3, waiting for transfers between devices: 0.01 us -> 5.89 us  [per_device(): right_in = lax.ppermute(right, 'tp', to_right)]
    ppermute x0 -> x22, waiting for transfers between devices: none -> 4.11 us  [the longest x14 2.71 us: exchange(): lax.ppermute(parts[by], 'tp', turn(by))]
    convert_element_type x3 -> x1, other arithmetic: 3.06 us -> 0.01 us  [per_device(): (prompt_lengths - STRETCH).astype(F32)[:, None] * jnp.asarray(frequency)]
    unnamed x29 -> x14, local copies, waits for them, and re-layouts: 2.14 us -> 0.04 us
  transfers between devices with their start and end apart: 9 -> 30, of which waited for: 1 -> 5; matrix products, arithmetic and copies ran while one was open for 13% -> 1% of each run, Pallas kernels for 34% -> 26%
where the time goes in v3:
time: 90 us; the launch traced here: 89.7 us
  starting transfers between devices  42.4 us (47%)
  Pallas kernels  32.4 us (36%)
  waiting for transfers between devices  11.5 us (13%)
  blocking collectives  1.93 us (2%)
    ppermute x14, starting transfers between devices, exchange(): lax.ppermute(parts[by], 'tp', turn(by))  22 us
    pallas_call x2, Pallas kernels, project(): pl.pallas_call(functools.partial(project_kernel, farthest), grid=(count,...  19.2 us
    ppermute x8, starting transfers between devices, exchange_to_both(): lax.ppermute(parts[by], ('tp', 'rep'), cross(by))  11.1 us
    ppermute x3, waiting for transfers between devices, per_device(): right_in = lax.ppermute(right, 'tp', to_right)  5.89 us
    ppermute x3, starting transfers between devices, per_device(): right_in = lax.ppermute(right, 'tp', to_right)  5.79 us
    pallas_call x1, Pallas kernels, project_first(): pl.pallas_call(first_kernel, grid=(features // depth,), in_specs=[pl.Bloc...  5.75 us
    pallas_call x1, Pallas kernels, cache_attention(): pl.pallas_call(cache_kernel, grid=(blocks,), in_specs=[SMEM, SMEM, SMEM,...  4.42 us
    ppermute x1, starting transfers between devices, per_device(): right_in = lax.ppermute(far_keys, 'tp', to_right)  3.08 us
  transfers between devices with their start and end apart: 30, of which 5 were waited for; matrix products, arithmetic and copies ran while one was open for 1% of the time, Pallas kernels for 26%

profile of v3, /device:TPU:0, one launch (start us, length us, event | category | flops | bytes accessed | tf_op | source)
XLA Modules:
  0.0 89.7 jit_solution(17071893104654790464)
XLA Ops:
  0.0 5.7 %project_first.1 = (bf16[576,128]{1,0:T(8,128)(2,1)S(1)}, bf16[576,128]{1,0:T(8,128)(2,1)S(1)}, bf16[1,576,2048]{2,1,0:T(8,128)(2,1)S(1)}) custom-call(bf16[1,576,2048]{2,1,0:T(8,128)(2,1)} %bitcast.9, s32[2048,2048]{1,0:T(8,128)} %value_codes.5, s32[2048,2048]{1,0:T(8,128)} %value_codes.5, s32[32,2048]{1,0:T(8,128)} %value_scales.5, ...), custom_call_target="tpu_custom_call" | custom-call | flops 603979776 | bytes 6815744 | tf_op jit(solution)/shard_map/project_first/pallas_call | solution.py:155
  5.8 3.1 %collective-permute-start = (bf16[576,128]{1,0:T(8,128)(2,1)S(1)}, bf16[576,128]{1,0:T(8,128)(2,1)S(1)}, u32[]{:S(2)}, u32[]{:S(2)}) collective-permute-start(bf16[576,128]{1,0:T(8,128)(2,1)S(1)} %get-tuple-element.48), channel_id=1, source_target_pairs={{0,4},{4,8},{8,12},{12,14},{14,10},{10,6},{6,2},{2,0},{1,5},{5,9},... | collective-permute-start | bytes 442376 | tf_op jit(solution)/shard_map/ppermute | solution.py:599
  8.8 0.5 multiply_reduce_fusion.squares
  9.4 0.1 pack.1
  9.5 6.0 %project.2.terms = f32[2,2,576,128]{3,2,1,0:T(8,128)S(1)} custom-call(bf16[1,576,2048]{2,1,0:T(8,128)(2,1)S(1)} %get-tuple-element.47.x, s32[2048,2048]{1,0:T(8,128)} %value_codes.5, s32[2048,2048]{1,0:T(8,128)} %value_codes.5, s32[32,2048]{1,0:T(8,128)} %value_scales.5, s32[32,2048]{1,0:T(8,128)} %value_scales.5, f32[8,32]{1,0:T(8,128)} %bitcast.11), custom_call_target="tpu_custom_call" | custom-call | flops 1207959552 | bytes 6553600 | tf_op jit(solution)/shard_map/project/pallas_call | solution.py:218
  15.5 0.1 sends.3
  15.6 2.1 %collective-permute-start.2 = (bf16[2,576,128]{2,1,0:T(8,128)(2,1)S(1)}, bf16[2,576,128]{2,1,0:T(8,128)(2,1)S(1)}, u32[]{:S(2)}, u32[]{:S(2)}) collective-permute-start(bf16[2,576,128]{2,1,0:T(8,128)(2,1)S(1)} %get-tuple-element.60), channel_id=1, source_target_pairs={{0,4},{4,8},{8,12},{12,14},{14,10},{10,6},{6,2},{2,0},{1,5},{5,9},... | collective-permute-start | bytes 884744 | tf_op jit(solution)/shard_map/ppermute | solution.py:624
  17.7 13.2 %project.3.terms.own = f32[5,2,576,128]{3,2,1,0:T(8,128)S(1)} custom-call(bf16[1,576,2048]{2,1,0:T(8,128)(2,1)S(1)} %get-tuple-element.47.x, s32[2048,2048]{1,0:T(8,128)} %value_codes.5, s32[2048,2048]{1,0:T(8,128)} %value_codes.5, s32[32,2048]{1,0:T(8,128)} %value_scales.5, s32[32,2048]{1,0:T(8,128)} %value_scales.5, f32[8,32]{1,0:T(8,128)} %bitcast.12), custom_call_target="tpu_custom_call" | custom-call | flops 3019898880 | bytes 12845056 | tf_op jit(solution)/shard_map/project/pallas_call | solution.py:218
  30.9 0.0 copy-start.4
  30.9 0.0 copy-start.6
  30.9 0.0 copy-start.2
  30.9 0.1 sends.4
  31.0 2.1 %collective-permute-start.4 = (bf16[2,576,128]{2,1,0:T(8,128)(2,1)S(1)}, bf16[2,576,128]{2,1,0:T(8,128)(2,1)S(1)}, u32[]{:S(2)}, u32[]{:S(2)}) collective-permute-start(bf16[2,576,128]{2,1,0:T(8,128)(2,1)S(1)} %get-tuple-element.69), channel_id=1, source_target_pairs={{0,4},{4,8},{8,12},{12,14},{14,10},{10,6},{6,2},{2,0},{1,5},{5,9},... | collective-permute-start | bytes 884744 | tf_op jit(solution)/shard_map/ppermute | solution.py:624
  33.1 5.9 %collective-permute-done.4.right = bf16[2,576,128]{2,1,0:T(8,128)(2,1)S(1)} collective-permute-done((bf16[2,576,128]{2,1,0:T(8,128)(2,1)S(1)}, bf16[2,576,128]{2,1,0:T(8,128)(2,1)S(1)}, u32[]{:S(2)}, u32[]{:S(2)}) %collective-permute-start.4) | collective-permute-done | bytes 294944 | tf_op jit(solution)/shard_map/ppermute | solution.py:624
  39.0 1.4 %collective-permute-done.5.left = bf16[2,576,128]{2,1,0:T(8,128)(2,1)S(1)} collective-permute-done((bf16[2,576,128]{2,1,0:T(8,128)(2,1)S(1)}, bf16[2,576,128]{2,1,0:T(8,128)(2,1)S(1)}, u32[]{:S(2)}, u32[]{:S(2)}) %collective-permute-start.5) | collective-permute-done | bytes 294944 | tf_op jit(solution)/shard_map/ppermute | solution.py:625
  40.4 0.1 sends.5
  40.5 1.6 %collective-permute-start.6 = (bf16[2,576,128]{2,1,0:T(8,128)(2,1)S(1)}, bf16[2,576,128]{2,1,0:T(8,128)(2,1)S(1)}, u32[]{:S(2)}, u32[]{:S(2)}) collective-permute-start(bf16[2,576,128]{2,1,0:T(8,128)(2,1)S(1)} %get-tuple-element.71), channel_id=1, source_target_pairs={{0,4},{4,8},{8,12},{12,14},{14,10},{10,6},{6,2},{2,0},{1,5},{5,9},... | collective-permute-start | bytes 884744 | tf_op jit(solution)/shard_map/ppermute | solution.py:624
  42.2 0.4 collective-permute-start.7
  42.6 0.1 multiply_cosine_fusion
  42.7 1.4 %collective-permute-start.10 = (bf16[48,128]{1,0:T(8,128)(2,1)S(1)}, bf16[48,128]{1,0:T(8,128)(2,1)S(1)}, u32[]{:S(2)}, u32[]{:S(2)}) collective-permute-start(bf16[48,128]{1,0:T(8,128)(2,1)S(1)} %get-tuple-element.76), channel_id=1, source_target_pairs={{0,6},{2,8},{4,10},{6,12},{8,14},{10,0},{12,2},{14,4},{1,7},{3,9},... | collective-permute-start | bytes 36872 | tf_op jit(solution)/shard_map/ppermute | solution.py:280
  44.8 0.0 copy-start
  44.9 2.6 %collective-permute-start.11 = (bf16[48,128]{1,0:T(8,128)(2,1)S(1)}, bf16[48,128]{1,0:T(8,128)(2,1)S(1)}, u32[]{:S(2)}, u32[]{:S(2)}) collective-permute-start(bf16[48,128]{1,0:T(8,128)(2,1)S(1)} %get-tuple-element.77), channel_id=1, source_target_pairs={{0,8},{2,10},{4,12},{6,14},{8,0},{10,2},{12,4},{14,6},{1,9},{3,11}... | collective-permute-start | bytes 36872 | tf_op jit(solution)/shard_map/ppermute | solution.py:280
  47.5 2.4 %collective-permute-start.12 = (bf16[48,128]{1,0:T(8,128)(2,1)S(1)}, bf16[48,128]{1,0:T(8,128)(2,1)S(1)}, u32[]{:S(2)}, u32[]{:S(2)}) collective-permute-start(bf16[48,128]{1,0:T(8,128)(2,1)S(1)} %get-tuple-element.78), channel_id=1, source_target_pairs={{0,10},{2,12},{4,14},{6,0},{8,2},{10,4},{12,6},{14,8},{1,11},{3,13... | collective-permute-start | bytes 36872 | tf_op jit(solution)/shard_map/ppermute | solution.py:280
  49.9 2.0 %collective-permute-start.13 = (bf16[48,128]{1,0:T(8,128)(2,1)S(1)}, bf16[48,128]{1,0:T(8,128)(2,1)S(1)}, u32[]{:S(2)}, u32[]{:S(2)}) collective-permute-start(bf16[48,128]{1,0:T(8,128)(2,1)S(1)} %get-tuple-element.79), channel_id=1, source_target_pairs={{0,12},{2,14},{4,0},{6,2},{8,4},{10,6},{12,8},{14,10},{1,13},{3,15... | collective-permute-start | bytes 36872 | tf_op jit(solution)/shard_map/ppermute | solution.py:280
  51.9 4.4 %cache_attention.1 = bf16[8,48,128]{2,1,0:T(8,128)(2,1)S(1)} custom-call(s32[6]{0:T(128)S(1)} %copy-done.3, s32[6]{0:T(128)S(1)} %copy-done.4, s32[1]{0:T(128)S(6)} %copy.14.stored, bf16[8,32,128]{2,1,0:T(8,128)(2,1)S(1)} %get-tuple-element.66.q, bf16[1,1024,2048]{2,1,0:T(8,128)(2,1)} %values.1, bf16[1,1024,2048]{2,1,0:T(8,128)(2,1)} %values.1, ...), custom_call_target="tpu_custom_call" | custom-call | flops 134217728 | bytes 4194304 | tf_op jit(solution)/shard_map/cache_attention/pallas_call | solution.py:416
  56.4 1.0 %collective-permute-start.14 = (bf16[48,128]{1,0:T(8,128)(2,1)S(1)}, bf16[48,128]{1,0:T(8,128)(2,1)S(1)}, u32[]{:S(2)}, u32[]{:S(2)}) collective-permute-start(bf16[48,128]{1,0:T(8,128)(2,1)S(1)} %get-tuple-element.80), channel_id=1, source_target_pairs={{0,14},{2,0},{4,2},{6,4},{8,6},{10,8},{12,10},{14,12},{1,15},{3,1}... | collective-permute-start | bytes 36872 | tf_op jit(solution)/shard_map/ppermute | solution.py:280
  57.3 1.1 %collective-permute-start.8 = (bf16[48,128]{1,0:T(8,128)(2,1)S(1)}, bf16[48,128]{1,0:T(8,128)(2,1)S(1)}, u32[]{:S(2)}, u32[]{:S(2)}) collective-permute-start(bf16[48,128]{1,0:T(8,128)(2,1)S(1)} %get-tuple-element.74), channel_id=1, source_target_pairs={{0,2},{2,4},{4,6},{6,8},{8,10},{10,12},{12,14},{14,0},{1,3},{3,5},... | collective-permute-start | bytes 36872 | tf_op jit(solution)/shard_map/ppermute | solution.py:280
  58.4 0.9 collective-permute-start.9
  59.3 1.9 %all-gather = bf16[16,48,128]{2,1,0:T(8,128)(2,1)S(1)} all-gather(bf16[8,48,128]{2,1,0:T(8,128)(2,1)S(1)} %cache_attention.1), channel_id=2, replica_groups=mesh['grp'=2,'tp'=8,'rep'=2] {'rep'}, dimensions={0}, use_global_device_ids=true | all-gather | bytes 294912 | tf_op jit(solution)/shard_map/all_gather | solution.py:630
  61.3 2.5 %collective-permute-done.8.refs_1_ = bf16[48,128]{1,0:T(8,128)(2,1)S(1)} collective-permute-done((bf16[48,128]{1,0:T(8,128)(2,1)S(1)}, bf16[48,128]{1,0:T(8,128)(2,1)S(1)}, u32[]{:S(2)}, u32[]{:S(2)}) %collective-permute-start.8) | collective-permute-done | bytes 12320 | tf_op jit(solution)/shard_map/ppermute | solution.py:280
  63.7 0.2 collective-permute-done.9.refs_2_
  63.9 1.8 %stretch_attention.1 = (bf16[48,128]{1,0:T(8,128)(2,1)S(1)}, bf16[48,128]{1,0:T(8,128)(2,1)S(1)}, bf16[48,128]{1,0:T(8,128)(2,1)S(1)}, bf16[48,128]{1,0:T(8,128)...) custom-call(s32[6]{0:T(128)S(1)} %copy-done.3, ...), custom_call_target="tpu_custom_call" | custom-call | tf_op jit(solution)/shard_map/stretch_attention/pallas_call | solution.py:517
  65.7 1.8 %collective-permute-start.15 = (bf16[48,128]{1,0:T(8,128)(2,1)S(1)}, bf16[48,128]{1,0:T(8,128)(2,1)S(1)}, u32[]{:S(2)}, u32[]{:S(2)}) collective-permute-start(bf16[48,128]{1,0:T(8,128)(2,1)S(1)} %get-tuple-element.82), channel_id=1, source_target_pairs={{0,2},{2,4},{4,6},{6,8},{8,10},{10,12},{12,14},{14,0},{1,3},{3,5},... | collective-permute-start | bytes 36872 | tf_op jit(solution)/shard_map/ppermute | solution.py:280
  67.5 0.2 collective-permute-start.16
  67.7 0.4 collective-permute-start.17
  68.1 3.3 %collective-permute-start.18 = (bf16[48,128]{1,0:T(8,128)(2,1)S(1)}, bf16[48,128]{1,0:T(8,128)(2,1)S(1)}, u32[]{:S(2)}, u32[]{:S(2)}) collective-permute-start(bf16[48,128]{1,0:T(8,128)(2,1)S(1)} %get-tuple-element.85), channel_id=1, source_target_pairs={{0,8},{2,10},{4,12},{6,14},{8,0},{10,2},{12,4},{14,6},{1,9},{3,11}... | collective-permute-start | bytes 36872 | tf_op jit(solution)/shard_map/ppermute | solution.py:280
  71.4 1.2 %collective-permute-start.19 = (bf16[48,128]{1,0:T(8,128)(2,1)S(1)}, bf16[48,128]{1,0:T(8,128)(2,1)S(1)}, u32[]{:S(2)}, u32[]{:S(2)}) collective-permute-start(bf16[48,128]{1,0:T(8,128)(2,1)S(1)} %get-tuple-element.86), channel_id=1, source_target_pairs={{0,10},{2,12},{4,14},{6,0},{8,2},{10,4},{12,6},{14,8},{1,11},{3,13... | collective-permute-start | bytes 36872 | tf_op jit(solution)/shard_map/ppermute | solution.py:280
  72.5 2.6 %collective-permute-start.20 = (bf16[48,128]{1,0:T(8,128)(2,1)S(1)}, bf16[48,128]{1,0:T(8,128)(2,1)S(1)}, u32[]{:S(2)}, u32[]{:S(2)}) collective-permute-start(bf16[48,128]{1,0:T(8,128)(2,1)S(1)} %get-tuple-element.87), channel_id=1, source_target_pairs={{0,12},{2,14},{4,0},{6,2},{8,4},{10,6},{12,8},{14,10},{1,13},{3,15... | collective-permute-start | bytes 36872 | tf_op jit(solution)/shard_map/ppermute | solution.py:280
  75.2 1.1 %collective-permute-start.21 = (bf16[48,128]{1,0:T(8,128)(2,1)S(1)}, bf16[48,128]{1,0:T(8,128)(2,1)S(1)}, u32[]{:S(2)}, u32[]{:S(2)}) collective-permute-start(bf16[48,128]{1,0:T(8,128)(2,1)S(1)} %get-tuple-element.88), channel_id=1, source_target_pairs={{0,14},{2,0},{4,2},{6,4},{8,6},{10,8},{12,10},{14,12},{1,15},{3,1}... | collective-permute-start | bytes 36872 | tf_op jit(solution)/shard_map/ppermute | solution.py:280
  76.3 1.0 %collective-permute-start.23 = (bf16[48,128]{1,0:T(8,128)(2,1)S(1)}, bf16[48,128]{1,0:T(8,128)(2,1)S(1)}, u32[]{:S(2)}, u32[]{:S(2)}) collective-permute-start(bf16[48,128]{1,0:T(8,128)(2,1)S(1)} %get-tuple-element.82), channel_id=1, source_target_pairs={{0,3},{1,2},{2,5},{3,4},{4,7},{5,6},{6,9},{7,8},{8,11},{9,10},{10,... | collective-permute-start | bytes 36872 | tf_op jit(solution)/shard_map/ppermute | solution.py:292
  77.3 0.4 collective-permute-start.24
  77.7 2.0 %collective-permute-start.25 = (bf16[48,128]{1,0:T(8,128)(2,1)S(1)}, bf16[48,128]{1,0:T(8,128)(2,1)S(1)}, u32[]{:S(2)}, u32[]{:S(2)}) collective-permute-start(bf16[48,128]{1,0:T(8,128)(2,1)S(1)} %get-tuple-element.84), channel_id=1, source_target_pairs={{0,7},{1,6},{2,9},{3,8},{4,11},{5,10},{6,13},{7,12},{8,15},{9,14},... | collective-permute-start | bytes 36872 | tf_op jit(solution)/shard_map/ppermute | solution.py:292
  79.7 2.3 %collective-permute-start.26 = (bf16[48,128]{1,0:T(8,128)(2,1)S(1)}, bf16[48,128]{1,0:T(8,128)(2,1)S(1)}, u32[]{:S(2)}, u32[]{:S(2)}) collective-permute-start(bf16[48,128]{1,0:T(8,128)(2,1)S(1)} %get-tuple-element.85), channel_id=1, source_target_pairs={{0,9},{1,8},{2,11},{3,10},{4,13},{5,12},{6,15},{7,14},{8,1},{9,0},... | collective-permute-start | bytes 36872 | tf_op jit(solution)/shard_map/ppermute | solution.py:292
  82.0 2.2 %collective-permute-start.27 = (bf16[48,128]{1,0:T(8,128)(2,1)S(1)}, bf16[48,128]{1,0:T(8,128)(2,1)S(1)}, u32[]{:S(2)}, u32[]{:S(2)}) collective-permute-start(bf16[48,128]{1,0:T(8,128)(2,1)S(1)} %get-tuple-element.86), channel_id=1, source_target_pairs={{0,11},{1,10},{2,13},{3,12},{4,15},{5,14},{6,1},{7,0},{8,3},{9,2},... | collective-permute-start | bytes 36872 | tf_op jit(solution)/shard_map/ppermute | solution.py:292
  84.2 1.0 %collective-permute-start.28 = (bf16[48,128]{1,0:T(8,128)(2,1)S(1)}, bf16[48,128]{1,0:T(8,128)(2,1)S(1)}, u32[]{:S(2)}, u32[]{:S(2)}) collective-permute-start(bf16[48,128]{1,0:T(8,128)(2,1)S(1)} %get-tuple-element.87), channel_id=1, source_target_pairs={{0,13},{1,12},{2,15},{3,14},{4,1},{5,0},{6,3},{7,2},{8,5},{9,4},{1... | collective-permute-start | bytes 36872 | tf_op jit(solution)/shard_map/ppermute | solution.py:292
  85.2 2.2 %collective-permute-start.29 = (bf16[48,128]{1,0:T(8,128)(2,1)S(1)}, bf16[48,128]{1,0:T(8,128)(2,1)S(1)}, u32[]{:S(2)}, u32[]{:S(2)}) collective-permute-start(bf16[48,128]{1,0:T(8,128)(2,1)S(1)} %get-tuple-element.88), channel_id=1, source_target_pairs={{0,15},{1,14},{2,1},{3,0},{4,3},{5,2},{6,5},{7,4},{8,7},{9,6},{10,... | collective-permute-start | bytes 36872 | tf_op jit(solution)/shard_map/ppermute | solution.py:292
  87.4 1.4 %collective-permute-done.29.refs_15_ = bf16[48,128]{1,0:T(8,128)(2,1)S(1)} collective-permute-done((bf16[48,128]{1,0:T(8,128)(2,1)S(1)}, bf16[48,128]{1,0:T(8,128)(2,1)S(1)}, u32[]{:S(2)}, u32[]{:S(2)}) %collective-permute-start.29) | collective-permute-done | bytes 12320 | tf_op jit(solution)/shard_map/ppermute | solution.py:292
  88.8 0.9 %combine.1 = bf16[2,16384]{1,0:T(2,128)(2,1)} custom-call(bf16[2,8,48,128]{3,2,1,0:T(8,128)(2,1)S(1)} %bitcast.8, bf16[48,128]{1,0:T(8,128)(2,1)S(1)} %get-tuple-element.81.refs_0_, bf16[48,128]{1,0:T(8,128)(2,1)S(1)} %collective-permute-done.15.refs_1_, bf16[48,128]{1,0:T(8,128)(2,1)S(1)} %collective-permute-done.16.refs_2_, ...), custom_call_target="tpu_custom_call" | custom-call | tf_op jit(solution)/shard_map/combine/pallas_call | solution.py:556
  (41 shorter events, 0.1 us)
Async XLA Ops:
  0.0 8.8 %copy-start.5 = (bf16[192,3,2048]{2,0,1:T(8,128)(2,1)S(1)}, bf16[192,3,2048]{2,0,1:T(8,128)(2,1)}, u32[]{:S(2)}) copy-start(bf16[192,3,2048]{2,0,1:T(8,128)(2,1)} %param.13) | copy-start | bytes 7077892
  0.0 9.4 %copy-start.1 = (bf16[1,2,16384]{2,1,0:T(2,128)(2,1)S(1)}, bf16[1,2,16384]{2,1,0:T(2,128)(2,1)}, u32[]{:S(2)}) copy-start(bf16[1,2,16384]{2,1,0:T(2,128)(2,1)} %queries.1) | copy-start | bytes 196612
  5.8 9.7 %collective-permute-start = (bf16[576,128]{1,0:T(8,128)(2,1)S(1)}, bf16[576,128]{1,0:T(8,128)(2,1)S(1)}, u32[]{:S(2)}, u32[]{:S(2)}) collective-permute-start(bf16[576,128]{1,0:T(8,128)(2,1)S(1)} %get-tuple-element.48), channel_id=1, source_target_pairs={{0,4},{4,8},{8,12},{12,14},{14,10},{10,6},{6,2},{2,0},{1,5},{5,9},... | collective-permute-start | bytes 442376 | tf_op jit(solution)/shard_map/ppermute | solution.py:599
  8.8 6.7 %collective-permute-start.1 = (bf16[576,128]{1,0:T(8,128)(2,1)S(1)}, bf16[576,128]{1,0:T(8,128)(2,1)S(1)}, u32[]{:S(2)}, u32[]{:S(2)}) collective-permute-start(bf16[576,128]{1,0:T(8,128)(2,1)S(1)} %get-tuple-element.49), channel_id=1, source_target_pairs={{0,2},{4,0},{8,4},{12,8},{14,12},{10,14},{6,10},{2,6},{1,3},{5,1},... | collective-permute-start | bytes 442376 | tf_op jit(solution)/shard_map/ppermute | solution.py:600
  15.6 15.3 %collective-permute-start.2 = (bf16[2,576,128]{2,1,0:T(8,128)(2,1)S(1)}, bf16[2,576,128]{2,1,0:T(8,128)(2,1)S(1)}, u32[]{:S(2)}, u32[]{:S(2)}) collective-permute-start(bf16[2,576,128]{2,1,0:T(8,128)(2,1)S(1)} %get-tuple-element.60), channel_id=1, source_target_pairs={{0,4},{4,8},{8,12},{12,14},{14,10},{10,6},{6,2},{2,0},{1,5},{5,9},... | collective-permute-start | bytes 884744 | tf_op jit(solution)/shard_map/ppermute | solution.py:624
  17.7 13.2 %collective-permute-start.3 = (bf16[2,576,128]{2,1,0:T(8,128)(2,1)S(1)}, bf16[2,576,128]{2,1,0:T(8,128)(2,1)S(1)}, u32[]{:S(2)}, u32[]{:S(2)}) collective-permute-start(bf16[2,576,128]{2,1,0:T(8,128)(2,1)S(1)} %get-tuple-element.61), channel_id=1, source_target_pairs={{0,2},{4,0},{8,4},{12,8},{14,12},{10,14},{6,10},{2,6},{1,3},{5,1},... | collective-permute-start | bytes 884744 | tf_op jit(solution)/shard_map/ppermute | solution.py:625
  30.9 2.3 %copy-start.4 = (s32[6]{0:T(128)S(1)}, s32[6]{0:T(128)}, u32[]{:S(2)}) copy-start(s32[6]{0:T(128)} %lengths.1) | copy-start | bytes 76
  30.9 11.8 %copy-start.6 = (f32[128]{0:T(128)S(1)}, f32[128]{0:T(128)}, u32[]{:S(2)}) copy-start(f32[128]{0:T(128)} %constant.9.clone) | copy-start | bytes 1540
  30.9 21.0 %copy-start.2 = (bf16[1,2,2048]{2,1,0:T(2,128)(2,1)S(1)}, bf16[1,2,2048]{2,1,0:T(2,128)(2,1)}, u32[]{:S(2)}) copy-start(bf16[1,2,2048]{2,1,0:T(2,128)(2,1)} %fresh_values.1) | copy-start | bytes 24580
  30.9 21.0 %copy-start.3 = (s32[6]{0:T(128)S(1)}, s32[6]{0:T(128)}, u32[]{:S(2)}) copy-start(s32[6]{0:T(128)} %target_rows.1) | copy-start | bytes 76
  31.0 8.0 %collective-permute-start.4 = (bf16[2,576,128]{2,1,0:T(8,128)(2,1)S(1)}, bf16[2,576,128]{2,1,0:T(8,128)(2,1)S(1)}, u32[]{:S(2)}, u32[]{:S(2)}) collective-permute-start(bf16[2,576,128]{2,1,0:T(8,128)(2,1)S(1)} %get-tuple-element.69), channel_id=1, source_target_pairs={{0,4},{4,8},{8,12},{12,14},{14,10},{10,6},{6,2},{2,0},{1,5},{5,9},... | collective-permute-start | bytes 884744 | tf_op jit(solution)/shard_map/ppermute | solution.py:624
  33.1 7.3 %collective-permute-start.5 = (bf16[2,576,128]{2,1,0:T(8,128)(2,1)S(1)}, bf16[2,576,128]{2,1,0:T(8,128)(2,1)S(1)}, u32[]{:S(2)}, u32[]{:S(2)}) collective-permute-start(bf16[2,576,128]{2,1,0:T(8,128)(2,1)S(1)} %get-tuple-element.70), channel_id=1, source_target_pairs={{0,2},{4,0},{8,4},{12,8},{14,12},{10,14},{6,10},{2,6},{1,3},{5,1},... | collective-permute-start | bytes 884744 | tf_op jit(solution)/shard_map/ppermute | solution.py:625
  40.5 23.4 %collective-permute-start.6 = (bf16[2,576,128]{2,1,0:T(8,128)(2,1)S(1)}, bf16[2,576,128]{2,1,0:T(8,128)(2,1)S(1)}, u32[]{:S(2)}, u32[]{:S(2)}) collective-permute-start(bf16[2,576,128]{2,1,0:T(8,128)(2,1)S(1)} %get-tuple-element.71), channel_id=1, source_target_pairs={{0,4},{4,8},{8,12},{12,14},{14,10},{10,6},{6,2},{2,0},{1,5},{5,9},... | collective-permute-start | bytes 884744 | tf_op jit(solution)/shard_map/ppermute | solution.py:624
  42.2 21.8 %collective-permute-start.7 = (bf16[2,576,128]{2,1,0:T(8,128)(2,1)S(1)}, bf16[2,576,128]{2,1,0:T(8,128)(2,1)S(1)}, u32[]{:S(2)}, u32[]{:S(2)}) collective-permute-start(bf16[2,576,128]{2,1,0:T(8,128)(2,1)S(1)} %get-tuple-element.72), channel_id=1, source_target_pairs={{0,2},{4,0},{8,4},{12,8},{14,12},{10,14},{6,10},{2,6},{1,3},{5,1},... | collective-permute-start | bytes 884744 | tf_op jit(solution)/shard_map/ppermute | solution.py:625
  42.7 7.2 %collective-permute-start.10 = (bf16[48,128]{1,0:T(8,128)(2,1)S(1)}, bf16[48,128]{1,0:T(8,128)(2,1)S(1)}, u32[]{:S(2)}, u32[]{:S(2)}) collective-permute-start(bf16[48,128]{1,0:T(8,128)(2,1)S(1)} %get-tuple-element.76), channel_id=1, source_target_pairs={{0,6},{2,8},{4,10},{6,12},{8,14},{10,0},{12,2},{14,4},{1,7},{3,9},... | collective-permute-start | bytes 36872 | tf_op jit(solution)/shard_map/ppermute | solution.py:280
  44.8 19.1 %copy-start = (f32[2,192,128]{2,1,0:T(8,128)S(1)}, f32[2,192,128]{2,1,0:T(8,128)}, u32[]{:S(2)}) copy-start(f32[2,192,128]{2,1,0:T(8,128)} %constant.10.clone.turns) | copy-start | bytes 589828
  44.9 11.5 %collective-permute-start.11 = (bf16[48,128]{1,0:T(8,128)(2,1)S(1)}, bf16[48,128]{1,0:T(8,128)(2,1)S(1)}, u32[]{:S(2)}, u32[]{:S(2)}) collective-permute-start(bf16[48,128]{1,0:T(8,128)(2,1)S(1)} %get-tuple-element.77), channel_id=1, source_target_pairs={{0,8},{2,10},{4,12},{6,14},{8,0},{10,2},{12,4},{14,6},{1,9},{3,11}... | collective-permute-start | bytes 36872 | tf_op jit(solution)/shard_map/ppermute | solution.py:280
  47.5 9.8 %collective-permute-start.12 = (bf16[48,128]{1,0:T(8,128)(2,1)S(1)}, bf16[48,128]{1,0:T(8,128)(2,1)S(1)}, u32[]{:S(2)}, u32[]{:S(2)}) collective-permute-start(bf16[48,128]{1,0:T(8,128)(2,1)S(1)} %get-tuple-element.78), channel_id=1, source_target_pairs={{0,10},{2,12},{4,14},{6,0},{8,2},{10,4},{12,6},{14,8},{1,11},{3,13... | collective-permute-start | bytes 36872 | tf_op jit(solution)/shard_map/ppermute | solution.py:280
  49.9 8.5 %collective-permute-start.13 = (bf16[48,128]{1,0:T(8,128)(2,1)S(1)}, bf16[48,128]{1,0:T(8,128)(2,1)S(1)}, u32[]{:S(2)}, u32[]{:S(2)}) collective-permute-start(bf16[48,128]{1,0:T(8,128)(2,1)S(1)} %get-tuple-element.79), channel_id=1, source_target_pairs={{0,12},{2,14},{4,0},{6,2},{8,4},{10,6},{12,8},{14,10},{1,13},{3,15... | collective-permute-start | bytes 36872 | tf_op jit(solution)/shard_map/ppermute | solution.py:280
  56.4 4.9 %collective-permute-start.14 = (bf16[48,128]{1,0:T(8,128)(2,1)S(1)}, bf16[48,128]{1,0:T(8,128)(2,1)S(1)}, u32[]{:S(2)}, u32[]{:S(2)}) collective-permute-start(bf16[48,128]{1,0:T(8,128)(2,1)S(1)} %get-tuple-element.80), channel_id=1, source_target_pairs={{0,14},{2,0},{4,2},{6,4},{8,6},{10,8},{12,10},{14,12},{1,15},{3,1}... | collective-permute-start | bytes 36872 | tf_op jit(solution)/shard_map/ppermute | solution.py:280
  57.3 6.4 %collective-permute-start.8 = (bf16[48,128]{1,0:T(8,128)(2,1)S(1)}, bf16[48,128]{1,0:T(8,128)(2,1)S(1)}, u32[]{:S(2)}, u32[]{:S(2)}) collective-permute-start(bf16[48,128]{1,0:T(8,128)(2,1)S(1)} %get-tuple-element.74), channel_id=1, source_target_pairs={{0,2},{2,4},{4,6},{6,8},{8,10},{10,12},{12,14},{14,0},{1,3},{3,5},... | collective-permute-start | bytes 36872 | tf_op jit(solution)/shard_map/ppermute | solution.py:280
  58.4 5.5 %collective-permute-start.9 = (bf16[48,128]{1,0:T(8,128)(2,1)S(1)}, bf16[48,128]{1,0:T(8,128)(2,1)S(1)}, u32[]{:S(2)}, u32[]{:S(2)}) collective-permute-start(bf16[48,128]{1,0:T(8,128)(2,1)S(1)} %get-tuple-element.75), channel_id=1, source_target_pairs={{0,4},{2,6},{4,8},{6,10},{8,12},{10,14},{12,0},{14,2},{1,5},{3,7},... | collective-permute-start | bytes 36872 | tf_op jit(solution)/shard_map/ppermute | solution.py:280
  65.7 6.8 %collective-permute-start.15 = (bf16[48,128]{1,0:T(8,128)(2,1)S(1)}, bf16[48,128]{1,0:T(8,128)(2,1)S(1)}, u32[]{:S(2)}, u32[]{:S(2)}) collective-permute-start(bf16[48,128]{1,0:T(8,128)(2,1)S(1)} %get-tuple-element.82), channel_id=1, source_target_pairs={{0,2},{2,4},{4,6},{6,8},{8,10},{10,12},{12,14},{14,0},{1,3},{3,5},... | collective-permute-start | bytes 36872 | tf_op jit(solution)/shard_map/ppermute | solution.py:280
  67.5 7.7 %collective-permute-start.16 = (bf16[48,128]{1,0:T(8,128)(2,1)S(1)}, bf16[48,128]{1,0:T(8,128)(2,1)S(1)}, u32[]{:S(2)}, u32[]{:S(2)}) collective-permute-start(bf16[48,128]{1,0:T(8,128)(2,1)S(1)} %get-tuple-element.83), channel_id=1, source_target_pairs={{0,4},{2,6},{4,8},{6,10},{8,12},{10,14},{12,0},{14,2},{1,5},{3,7},... | collective-permute-start | bytes 36872 | tf_op jit(solution)/shard_map/ppermute | solution.py:280
  67.7 8.6 %collective-permute-start.17 = (bf16[48,128]{1,0:T(8,128)(2,1)S(1)}, bf16[48,128]{1,0:T(8,128)(2,1)S(1)}, u32[]{:S(2)}, u32[]{:S(2)}) collective-permute-start(bf16[48,128]{1,0:T(8,128)(2,1)S(1)} %get-tuple-element.84), channel_id=1, source_target_pairs={{0,6},{2,8},{4,10},{6,12},{8,14},{10,0},{12,2},{14,4},{1,7},{3,9},... | collective-permute-start | bytes 36872 | tf_op jit(solution)/shard_map/ppermute | solution.py:280
  68.1 8.2 %collective-permute-start.18 = (bf16[48,128]{1,0:T(8,128)(2,1)S(1)}, bf16[48,128]{1,0:T(8,128)(2,1)S(1)}, u32[]{:S(2)}, u32[]{:S(2)}) collective-permute-start(bf16[48,128]{1,0:T(8,128)(2,1)S(1)} %get-tuple-element.85), channel_id=1, source_target_pairs={{0,8},{2,10},{4,12},{6,14},{8,0},{10,2},{12,4},{14,6},{1,9},{3,11}... | collective-permute-start | bytes 36872 | tf_op jit(solution)/shard_map/ppermute | solution.py:280
  71.4 5.9 %collective-permute-start.19 = (bf16[48,128]{1,0:T(8,128)(2,1)S(1)}, bf16[48,128]{1,0:T(8,128)(2,1)S(1)}, u32[]{:S(2)}, u32[]{:S(2)}) collective-permute-start(bf16[48,128]{1,0:T(8,128)(2,1)S(1)} %get-tuple-element.86), channel_id=1, source_target_pairs={{0,10},{2,12},{4,14},{6,0},{8,2},{10,4},{12,6},{14,8},{1,11},{3,13... | collective-permute-start | bytes 36872 | tf_op jit(solution)/shard_map/ppermute | solution.py:280
  72.5 5.1 %collective-permute-start.20 = (bf16[48,128]{1,0:T(8,128)(2,1)S(1)}, bf16[48,128]{1,0:T(8,128)(2,1)S(1)}, u32[]{:S(2)}, u32[]{:S(2)}) collective-permute-start(bf16[48,128]{1,0:T(8,128)(2,1)S(1)} %get-tuple-element.87), channel_id=1, source_target_pairs={{0,12},{2,14},{4,0},{6,2},{8,4},{10,6},{12,8},{14,10},{1,13},{3,15... | collective-permute-start | bytes 36872 | tf_op jit(solution)/shard_map/ppermute | solution.py:280
  75.2 4.5 %collective-permute-start.21 = (bf16[48,128]{1,0:T(8,128)(2,1)S(1)}, bf16[48,128]{1,0:T(8,128)(2,1)S(1)}, u32[]{:S(2)}, u32[]{:S(2)}) collective-permute-start(bf16[48,128]{1,0:T(8,128)(2,1)S(1)} %get-tuple-element.88), channel_id=1, source_target_pairs={{0,14},{2,0},{4,2},{6,4},{8,6},{10,8},{12,10},{14,12},{1,15},{3,1}... | collective-permute-start | bytes 36872 | tf_op jit(solution)/shard_map/ppermute | solution.py:280
  76.3 5.7 %collective-permute-start.22 = (bf16[48,128]{1,0:T(8,128)(2,1)S(1)}, bf16[48,128]{1,0:T(8,128)(2,1)S(1)}, u32[]{:S(2)}, u32[]{:S(2)}) collective-permute-start(bf16[48,128]{1,0:T(8,128)(2,1)S(1)} %get-tuple-element.81.refs_0_), channel_id=1, source_target_pairs={{0,1},{1,0},{2,3},{3,2},{4,5},{5,4},{6,7},{7,6},{8,9},{9,8},{10,11... | collective-permute-start | bytes 36872 | tf_op jit(solution)/shard_map/ppermute | solution.py:292
  76.3 7.9 %collective-permute-start.23 = (bf16[48,128]{1,0:T(8,128)(2,1)S(1)}, bf16[48,128]{1,0:T(8,128)(2,1)S(1)}, u32[]{:S(2)}, u32[]{:S(2)}) collective-permute-start(bf16[48,128]{1,0:T(8,128)(2,1)S(1)} %get-tuple-element.82), channel_id=1, source_target_pairs={{0,3},{1,2},{2,5},{3,4},{4,7},{5,6},{6,9},{7,8},{8,11},{9,10},{10,... | collective-permute-start | bytes 36872 | tf_op jit(solution)/shard_map/ppermute | solution.py:292
  77.3 7.9 %collective-permute-start.24 = (bf16[48,128]{1,0:T(8,128)(2,1)S(1)}, bf16[48,128]{1,0:T(8,128)(2,1)S(1)}, u32[]{:S(2)}, u32[]{:S(2)}) collective-permute-start(bf16[48,128]{1,0:T(8,128)(2,1)S(1)} %get-tuple-element.83), channel_id=1, source_target_pairs={{0,5},{1,4},{2,7},{3,6},{4,9},{5,8},{6,11},{7,10},{8,13},{9,12},{1... | collective-permute-start | bytes 36872 | tf_op jit(solution)/shard_map/ppermute | solution.py:292
  77.7 9.7 %collective-permute-start.25 = (bf16[48,128]{1,0:T(8,128)(2,1)S(1)}, bf16[48,128]{1,0:T(8,128)(2,1)S(1)}, u32[]{:S(2)}, u32[]{:S(2)}) collective-permute-start(bf16[48,128]{1,0:T(8,128)(2,1)S(1)} %get-tuple-element.84), channel_id=1, source_target_pairs={{0,7},{1,6},{2,9},{3,8},{4,11},{5,10},{6,13},{7,12},{8,15},{9,14},... | collective-permute-start | bytes 36872 | tf_op jit(solution)/shard_map/ppermute | solution.py:292
  79.7 7.7 %collective-permute-start.26 = (bf16[48,128]{1,0:T(8,128)(2,1)S(1)}, bf16[48,128]{1,0:T(8,128)(2,1)S(1)}, u32[]{:S(2)}, u32[]{:S(2)}) collective-permute-start(bf16[48,128]{1,0:T(8,128)(2,1)S(1)} %get-tuple-element.85), channel_id=1, source_target_pairs={{0,9},{1,8},{2,11},{3,10},{4,13},{5,12},{6,15},{7,14},{8,1},{9,0},... | collective-permute-start | bytes 36872 | tf_op jit(solution)/shard_map/ppermute | solution.py:292
  82.0 5.4 %collective-permute-start.27 = (bf16[48,128]{1,0:T(8,128)(2,1)S(1)}, bf16[48,128]{1,0:T(8,128)(2,1)S(1)}, u32[]{:S(2)}, u32[]{:S(2)}) collective-permute-start(bf16[48,128]{1,0:T(8,128)(2,1)S(1)} %get-tuple-element.86), channel_id=1, source_target_pairs={{0,11},{1,10},{2,13},{3,12},{4,15},{5,14},{6,1},{7,0},{8,3},{9,2},... | collective-permute-start | bytes 36872 | tf_op jit(solution)/shard_map/ppermute | solution.py:292
  84.2 3.2 %collective-permute-start.28 = (bf16[48,128]{1,0:T(8,128)(2,1)S(1)}, bf16[48,128]{1,0:T(8,128)(2,1)S(1)}, u32[]{:S(2)}, u32[]{:S(2)}) collective-permute-start(bf16[48,128]{1,0:T(8,128)(2,1)S(1)} %get-tuple-element.87), channel_id=1, source_target_pairs={{0,13},{1,12},{2,15},{3,14},{4,1},{5,0},{6,3},{7,2},{8,5},{9,4},{1... | collective-permute-start | bytes 36872 | tf_op jit(solution)/shard_map/ppermute | solution.py:292
  85.2 3.6 %collective-permute-start.29 = (bf16[48,128]{1,0:T(8,128)(2,1)S(1)}, bf16[48,128]{1,0:T(8,128)(2,1)S(1)}, u32[]{:S(2)}, u32[]{:S(2)}) collective-permute-start(bf16[48,128]{1,0:T(8,128)(2,1)S(1)} %get-tuple-element.88), channel_id=1, source_target_pairs={{0,15},{1,14},{2,1},{3,0},{4,3},{5,2},{6,5},{7,4},{8,7},{9,6},{10,... | collective-permute-start | bytes 36872 | tf_op jit(solution)/shard_map/ppermute | solution.py:292

commit v4 on v0

v4 whole, which is shorter than its diff:
```python
import functools
import math

import jax
import jax.numpy as jnp
import numpy as np
from jax import lax
from jax.experimental import pallas as pl
from jax.experimental.pallas import tpu as pltpu
from jax.sharding import PartitionSpec as P

D = 16384
HEADS = 128
KV_HEADS = 8
HEAD_DIM = 128
STRETCH = 192
STEPS = 2
QBLOCK = 64
GROUP = HEADS // KV_HEADS
ROWS = GROUP * STEPS
TAIL = 16
PART = ROWS + TAIL
CORE_HEADS = KV_HEADS // 2
NORMAL_FLOAT_LEVELS = [
    -1.0,
    -0.6961928009986877,
    -0.5250730514526367,
    -0.39491748809814453,
    -0.28444138169288635,
    -0.18477343022823334,
    -0.09105003625154495,
    0.0,
    0.07958029955625534,
    0.16093020141124725,
    0.24611230194568634,
    0.33791524171829224,
    0.44070982933044434,
    0.5626170039176941,
    0.7229568362236023,
    1.0,
]
ROTARY_BASE = 500000.0
EPSILON = 1e-05
NEGATIVE = -1e30
BF16 = jnp.bfloat16
F32 = jnp.float32
MIB = 1024 * 1024
VMEM = pl.BlockSpec(memory_space=pltpu.VMEM)
SMEM = pl.BlockSpec(memory_space=pltpu.SMEM)


def in_hbm(*arrays):
    return [pltpu.with_memory_space_constraint(array, pltpu.HBM) for array in arrays]


def ring_device(place, count):
    half = count // 2
    if isinstance(place, int):
        return 2 * place if place < half else 2 * (count - 1 - place) + 1
    return jnp.where(place < half, 2 * place, 2 * (count - 1 - place) + 1)


def owner_at(distance):
    count = lax.axis_size("tp")
    here = lax.axis_index("tp")
    place = jnp.where(here % 2 == 0, here // 2, count - 1 - here // 2)
    return ring_device((place + distance + count) % count, count)


def turned(column):
    rows = lax.broadcasted_iota(jnp.int32, (column.shape[0], 128), 0)
    lanes = lax.broadcasted_iota(jnp.int32, (column.shape[0], 128), 1)
    return jnp.sum(jnp.where(rows == lanes, column, 0.0), axis=0, keepdims=True)


def stood(row, count):
    rows = lax.broadcasted_iota(jnp.int32, (count, 128), 0)
    lanes = lax.broadcasted_iota(jnp.int32, (count, 128), 1)
    return jnp.sum(jnp.where(rows == lanes, row, 0.0), axis=1, keepdims=True)


def token_rows(column):
    at = lax.broadcasted_iota(jnp.int32, (8, 128), 0)
    ends = turned(column[128:])
    return jnp.where(at == 0, turned(column[:128]), jnp.where(at == 1, ends, 0.0))


def token_column(rows):
    return jnp.concatenate([stood(rows[0:1], 128), stood(rows[1:2], STRETCH - 128)], axis=0)


def two_pieces(rows):
    high = rows.astype(BF16).astype(F32)
    return jnp.concatenate([high, rows - high], axis=0).astype(BF16)


def one_piece(rows):
    rows = rows.astype(F32)
    return rows[:8] + rows[8:]


def pieces_tail(logs):
    row = turned(logs)
    high = row.astype(BF16).astype(F32)
    middle = (row - high).astype(BF16).astype(F32)
    low = row - high - middle
    at = lax.broadcasted_iota(jnp.int32, (TAIL, 128), 0)
    tail = jnp.where(at == 0, high, jnp.where(at == 1, middle, jnp.where(at == 2, low, 0.0)))
    return tail.astype(BF16)


def tail_pieces(tail):
    tail = tail.astype(F32)
    return stood(tail[0:1, :] + tail[1:2, :] + tail[2:3, :], ROWS)


def gathered_levels(table, codes):
    table = jnp.broadcast_to(table[None], (codes.shape[0] // 8, 8, 128)).reshape(codes.shape)
    return jnp.take_along_axis(table, codes, axis=1, mode="promise_in_bounds")


def selected_levels(codes):
    values = [jnp.float32(level) for level in NORMAL_FLOAT_LEVELS]
    for bit in (1, 2, 4, 8):
        mask = (codes & bit) != 0 if bit < 8 else codes >= 8
        values = [
            jnp.where(mask, values[at + 1], values[at]) for at in range(0, len(values), 2)
        ]
    return values[0]


def block_scales(scales, outer, column):
    count = scales.shape[0]
    line = lax.broadcasted_iota(jnp.int32, outer.shape, 0)
    line = jnp.sum(jnp.where(line == column, outer, 0.0), axis=0, keepdims=True)
    rows = lax.broadcasted_iota(jnp.int32, (count, count), 0)
    lanes = lax.broadcasted_iota(jnp.int32, (count, count), 1)
    second = jnp.sum(jnp.where(rows == lanes, line, 0.0), axis=1, keepdims=True)
    return (scales.astype(F32) + 1.0) / 256.0 * second


def scaled_block(x, gain, begin, out, squares):
    width = x.shape[2]
    for prompt in range(x.shape[0]):
        wide = x[prompt].astype(F32)
        out[prompt, :, pl.ds(begin, width)] = (wide * gain[...]).astype(BF16)
        squares[prompt] += token_rows(jnp.sum(wide * wide, axis=1, keepdims=True))


def weights_kernel(
    x, key_codes, value_codes, key_scales, value_scales, outer, gain,
    out, scaled, squares, scales,
):
    item = pl.program_id(0)
    features = key_codes.shape[0]
    head = lax.axis_index("rep") * CORE_HEADS + item
    half = outer.shape[0] // 2
    column = head // (KV_HEADS // half)
    scales[0] = block_scales(key_scales[...], outer[...], column)
    scales[1] = block_scales(value_scales[...], outer[...], half + column)
    lane = lax.broadcasted_iota(jnp.int32, (8, 128), 1)
    table = jnp.zeros((8, 128), F32)
    for code, level in enumerate(NORMAL_FLOAT_LEVELS):
        table = jnp.where(lane == code, level, table)

    def body(block, _):
        rows = pl.ds(pl.multiple_of(block * QBLOCK, QBLOCK), QBLOCK)
        keys = gathered_levels(table, key_codes[rows, :])
        values = selected_levels(value_codes[rows, :])
        keys *= scales[0, pl.ds(block, 1), :]
        values *= scales[1, pl.ds(block, 1), :]
        out[item, rows, :HEAD_DIM] = keys.astype(BF16)
        out[item, rows, HEAD_DIM:] = values.astype(BF16)
        return 0

    lax.fori_loop(0, features // QBLOCK, body, 0, unroll=4)

    @pl.when(item == 0)
    def _():
        squares[...] = jnp.zeros(squares.shape, F32)

    @pl.when(item < features // x.shape[2])
    def _():
        scaled_block(x, gain, pl.multiple_of(item * x.shape[2], 128), scaled, squares)


def feature_width(features):
    return max(128, features // CORE_HEADS)


def feature_shapes(x):
    return [
        jax.ShapeDtypeStruct(x.shape, BF16),
        jax.ShapeDtypeStruct((x.shape[0], 8, 128), F32),
    ]


def dequantize(x, codes, scales, outer, gain):
    per_rep, _, features = x.shape
    width = feature_width(features)
    head = lambda i: lax.axis_index("rep") * CORE_HEADS + i
    block = lambda i: jnp.minimum(i, features // width - 1)
    x, codes, scales, outer, gain = in_hbm(x, codes, scales, outer, gain)
    return pl.pallas_call(
        weights_kernel,
        grid=(CORE_HEADS,),
        in_specs=[
            pl.BlockSpec((per_rep, STRETCH, width), lambda i: (0, 0, block(i))),
            pl.BlockSpec((features, HEAD_DIM), lambda i: (0, head(i))),
            pl.BlockSpec((features, HEAD_DIM), lambda i: (0, KV_HEADS + head(i))),
            pl.BlockSpec((scales.shape[0], HEAD_DIM), lambda i: (0, head(i))),
            pl.BlockSpec((scales.shape[0], HEAD_DIM), lambda i: (0, KV_HEADS + head(i))),
            pl.BlockSpec(outer.shape, lambda i: (0, 0)),
            pl.BlockSpec((1, width), lambda i: (0, block(i))),
        ],
        out_specs=[VMEM] * 3,
        out_shape=[
            jax.ShapeDtypeStruct((CORE_HEADS, features, 2 * HEAD_DIM), BF16)
        ] + feature_shapes(x),
        scratch_shapes=[pltpu.VMEM((2, scales.shape[0], HEAD_DIM), F32)],
        compiler_params=pltpu.CompilerParams(vmem_limit_bytes=32 * MIB),
        cost_estimate=pl.CostEstimate(
            flops=64 * codes.size // 2, bytes_accessed=codes.size * 2, transcendentals=0
        ),
        name="dequantize",
    )(x, codes, codes, scales, scales, outer, gain)


def scale_kernel(x, gain, scaled, squares):
    item = pl.program_id(0)

    @pl.when(item == 0)
    def _():
        squares[...] = jnp.zeros(squares.shape, F32)

    scaled_block(x, gain, pl.multiple_of(item * x.shape[2], 128), scaled, squares)


def scale_features(x, gain):
    per_rep, _, features = x.shape
    width = feature_width(features)
    return pl.pallas_call(
        scale_kernel,
        grid=(features // width,),
        in_specs=[
            pl.BlockSpec((per_rep, STRETCH, width), lambda i: (0, 0, i)),
            pl.BlockSpec((1, width), lambda i: (0, i)),
        ],
        out_specs=[VMEM] * 2,
        out_shape=feature_shapes(x),
        compiler_params=pltpu.CompilerParams(vmem_limit_bytes=24 * MIB),
        name="scale_features",
    )(x, gain)


def prompt_of(targets, owner):
    prompt = jnp.int32(-1)
    for at in range(targets.shape[0]):
        prompt = jnp.where(targets[at] == owner, at, prompt)
    return prompt


def first_kernel(targets, own, squares, other, gain, weight, *refs):
    outs, (line, total) = refs[:4], refs[4:]
    per_rep = own.shape[0]
    prompt = prompt_of(targets, owner_at(lax.axis_size("tp") // 2))
    at = lax.rem(jnp.maximum(prompt, 0), per_rep)
    is_own = prompt // per_rep == lax.axis_index("rep")

    @pl.when((prompt >= 0) & is_own)
    def _():
        line[...] = own[at]
        total[...] = squares[at]

    @pl.when((prompt >= 0) & jnp.logical_not(is_own))
    def _():
        wide = other[at].astype(F32)
        line[...] = (wide * gain[...]).astype(BF16)
        total[...] = token_rows(jnp.sum(wide * wide, axis=1, keepdims=True))

    @pl.when(prompt < 0)
    def _():
        line[...] = jnp.zeros(line.shape, BF16)
        total[...] = jnp.zeros(total.shape, F32)

    for head in range(CORE_HEADS):
        right, left = outs[2 * (head // 2)], outs[2 * (head // 2) + 1]
        rows = slice(head % 2 * STRETCH, (head % 2 + 1) * STRETCH)
        product = jnp.dot(line[...], weight[head], preferred_element_type=F32)
        right[rows] = product[:, :HEAD_DIM].astype(BF16)
        left[rows] = product[:, HEAD_DIM:].astype(BF16)
    outs[0][2 * STRETCH :] = two_pieces(total[...])


def project_first(targets, own, squares, other, gain, weight):
    rows = 2 * STRETCH
    shapes = [
        jax.ShapeDtypeStruct((size, HEAD_DIM), BF16) for size in (rows + TAIL, rows, rows, rows)
    ]
    return pl.pallas_call(
        first_kernel,
        in_specs=[SMEM] + [VMEM] * 5,
        out_specs=[VMEM] * 4,
        out_shape=shapes,
        scratch_shapes=[pltpu.VMEM(own.shape[1:], BF16), pltpu.VMEM((8, 128), F32)],
        compiler_params=pltpu.CompilerParams(vmem_limit_bytes=24 * MIB),
        cost_estimate=pl.CostEstimate(
            flops=STRETCH * weight.size * 2, bytes_accessed=weight.size, transcendentals=0
        ),
        name="project_first",
    )(targets, own, squares, other, gain, weight)


def distance_at(farthest, item):
    return (farthest - item // 2) * (1 - 2 * (item % 2))


def project_kernel(farthest, targets, own, squares, other, other_squares, weight, out):
    item = pl.program_id(0)
    per_rep = own.shape[0]
    prompt = prompt_of(targets, owner_at(distance_at(farthest, item)))
    at = lax.rem(jnp.maximum(prompt, 0), per_rep)
    is_own = prompt // per_rep == lax.axis_index("rep")

    def products(lines, sums):
        for head in range(CORE_HEADS):
            product = jnp.dot(lines[at], weight[head], preferred_element_type=F32)
            begin = head % 2 * STRETCH
            out[item, head // 2, begin : begin + STRETCH] = product[:, :HEAD_DIM]
            begin += 2 * STRETCH
            out[item, head // 2, begin : begin + STRETCH] = product[:, HEAD_DIM:]
        for half in range(2):
            out[item, half, 4 * STRETCH :] = sums[at]

    @pl.when((prompt >= 0) & is_own)
    def _():
        products(own, squares)

    @pl.when((prompt >= 0) & jnp.logical_not(is_own))
    def _():
        products(other, other_squares)

    @pl.when(prompt < 0)
    def _():
        out[item] = jnp.zeros(out.shape[1:], F32)


def project(farthest, items, targets, own, squares, other, other_squares, weight):
    return pl.pallas_call(
        functools.partial(project_kernel, farthest),
        grid=(items,),
        in_specs=[SMEM] + [VMEM] * 5,
        out_specs=VMEM,
        out_shape=jax.ShapeDtypeStruct((items, 2, 4 * STRETCH + 8, HEAD_DIM), F32),
        compiler_params=pltpu.CompilerParams(vmem_limit_bytes=24 * MIB),
        cost_estimate=pl.CostEstimate(
            flops=items * STRETCH * weight.size * 2, bytes_accessed=weight.size, transcendentals=0
        ),
        name="project",
    )(targets, own, squares, other, other_squares, weight)


def send_kernel(half, first, terms, right, left, to_right, to_left):
    rows = 4 * STRETCH
    middle = 2 * STRETCH
    if first:
        to_right[:middle] = (terms[0, half, :middle] + right[:middle].astype(F32)).astype(BF16)
        to_right[middle:rows] = terms[0, half, middle:rows].astype(BF16)
        to_left[:middle] = terms[1, half, :middle].astype(BF16)
        to_left[middle:rows] = (terms[1, half, middle:rows] + left[...].astype(F32)).astype(BF16)
    else:
        to_right[:rows] = (terms[0, half, :rows] + right[:rows].astype(F32)).astype(BF16)
        to_left[:rows] = (terms[1, half, :rows] + left[:rows].astype(F32)).astype(BF16)
    if half == 0:
        right_sum, left_sum = terms[0, 0, rows:], terms[1, 0, rows:]
        right_sum += one_piece(right[middle if first else rows :])
        if not first:
            left_sum += one_piece(left[rows:])
        to_right[rows:] = two_pieces(right_sum)
        to_left[rows:] = two_pieces(left_sum)


def sends(half, first, terms, right, left):
    rows = 4 * STRETCH + (TAIL if half == 0 else 0)
    shape = jax.ShapeDtypeStruct((rows, HEAD_DIM), BF16)
    return pl.pallas_call(
        functools.partial(send_kernel, half, first),
        in_specs=[VMEM] * 3,
        out_specs=[VMEM] * 2,
        out_shape=[shape, shape],
        compiler_params=pltpu.CompilerParams(vmem_limit_bytes=16 * MIB),
        name="sends",
    )(terms, right, left)


def regroup_kernel(queries, grouped):
    for head in range(KV_HEADS):
        for member in range(GROUP):
            begin = (head * GROUP + member) * HEAD_DIM
            rows = slice(member * STEPS, (member + 1) * STEPS)
            grouped[head, rows] = queries[0, :, begin : begin + HEAD_DIM]


def regroup(queries):
    return pl.pallas_call(
        regroup_kernel,
        in_specs=[VMEM],
        out_specs=VMEM,
        out_shape=jax.ShapeDtypeStruct((KV_HEADS, ROWS, HEAD_DIM), BF16),
        name="regroup",
    )(queries)


CACHE_HEADS = 4


def cache_kernel(targets, lengths, stored, q, keys, values, fresh_keys, fresh_values, out):
    scaling = HEAD_DIM ** (-0.5)
    dims = (((1,), (1,)), ((), ()))
    here = lax.axis_index("tp")
    rep = lax.axis_index("rep")
    length = keys.shape[1]
    span = stored[0]
    for prompt in range(targets.shape[0]):
        span = jnp.where(targets[prompt] == here, lengths[prompt] - STRETCH, span)
    place = lax.broadcasted_iota(jnp.int32, (ROWS, length), 1)
    allowed = place < span - rep * length
    second_step = lax.broadcasted_iota(jnp.int32, (ROWS, 1), 0) % STEPS == 1
    for at in range(CACHE_HEADS):
        lanes = slice(at * HEAD_DIM, (at + 1) * HEAD_DIM)
        query = q[at]
        wide = query.astype(F32)
        scores = lax.dot_general(query, keys[0, :, lanes], dims, preferred_element_type=F32)
        scores = jnp.where(allowed, scores * scaling, NEGATIVE)
        highest = jnp.max(scores, axis=1, keepdims=True)
        fresh = []
        for step in range(STEPS):
            key = fresh_keys[0, step : step + 1, lanes].astype(F32)
            score = jnp.sum(wide * key, axis=1, keepdims=True) * scaling
            shown = rep == 0 if step == 0 else second_step & (rep == 0)
            score = jnp.where(shown, score, NEGATIVE)
            highest = jnp.maximum(highest, score)
            fresh.append(score)
        some = highest > 0.5 * NEGATIVE
        highest = jnp.where(some, highest, 0.0)
        weight = jnp.exp(scores - highest)
        totals = jnp.sum(weight, axis=1, keepdims=True)
        sums = jnp.dot(weight.astype(BF16), values[0, :, lanes], preferred_element_type=F32)
        for step in range(STEPS):
            share = jnp.exp(fresh[step] - highest)
            totals += share
            value = fresh_values[0, step : step + 1, lanes].astype(F32)
            sums += share.astype(BF16).astype(F32) * value
        totals = jnp.where(some, totals, 1.0)
        out[at, :ROWS] = (sums / totals).astype(BF16)
        out[at, ROWS:] = pieces_tail(jnp.where(some, highest + jnp.log(totals), NEGATIVE))


def cache_attention(part, targets, lengths, stored, grouped, kv_cache, new_kv):
    length = kv_cache.shape[1]
    (kv_cache,) = in_hbm(kv_cache)
    width = CACHE_HEADS * HEAD_DIM
    blocks = KV_HEADS // CACHE_HEADS
    return pl.pallas_call(
        cache_kernel,
        grid=(1,),
        in_specs=[
            SMEM,
            SMEM,
            SMEM,
            pl.BlockSpec((CACHE_HEADS, ROWS, HEAD_DIM), lambda h: (part, 0, 0)),
            pl.BlockSpec((1, length, width), lambda h: (0, 0, part)),
            pl.BlockSpec((1, length, width), lambda h: (0, 0, blocks + part)),
            pl.BlockSpec((1, STEPS, width), lambda h: (0, 0, part)),
            pl.BlockSpec((1, STEPS, width), lambda h: (0, 0, blocks + part)),
        ],
        out_specs=pl.BlockSpec((CACHE_HEADS, PART, HEAD_DIM), lambda h: (0, 0, 0)),
        out_shape=jax.ShapeDtypeStruct((CACHE_HEADS, PART, HEAD_DIM), BF16),
        compiler_params=pltpu.CompilerParams(vmem_limit_bytes=24 * MIB),
        cost_estimate=pl.CostEstimate(
            flops=4 * CACHE_HEADS * ROWS * length * HEAD_DIM,
            bytes_accessed=length * 2 * width * 2,
            transcendentals=CACHE_HEADS * ROWS * length,
        ),
        name="cache_attention",
    )(targets, lengths, stored, grouped, kv_cache, kv_cache, new_kv, new_kv)


def final_kernel(
    targets, starts, turns, own, right_a, left_a, right_b, left_b, grouped, cached, out
):
    scaling = HEAD_DIM ** (-0.5)
    dims = (((1,), (1,)), ((), ()))
    mine = own.shape[0] - 1
    first = lax.axis_index("rep") * CORE_HEADS
    prompt = prompt_of(targets, lax.axis_index("tp"))
    row = pl.ds(jnp.maximum(prompt, 0), 1)
    start_cosine, start_sine = starts[0, row, :], starts[1, row, :]
    cosine = turns[0] * start_cosine - turns[1] * start_sine
    sine = turns[1] * start_cosine + turns[0] * start_sine
    lane = lax.broadcasted_iota(jnp.int32, sine.shape, 1)
    sine = jnp.where(lane < HEAD_DIM // 2, -sine, sine)
    rows = 4 * STRETCH
    squares = own[mine, 0, rows:] + one_piece(right_a[rows:]) + one_piece(left_a[rows:])
    scale = token_column(lax.rsqrt(squares / D + EPSILON))
    for head in range(CORE_HEADS):
        right, left = ((right_a, left_a), (right_b, left_b))[head // 2]
        at = slice(head % 2 * STRETCH, (head % 2 + 1) * STRETCH)
        keys = own[mine, head // 2, at] + right[at].astype(F32) + left[at].astype(F32)
        at = slice((2 + head % 2) * STRETCH, (3 + head % 2) * STRETCH)
        values = own[mine, head // 2, at] + right[at].astype(F32) + left[at].astype(F32)
        keys = (keys * scale).astype(BF16).astype(F32)
        values = (values * scale).astype(BF16)
        keys = keys * cosine + pltpu.roll(keys, HEAD_DIM // 2, 1) * sine
        scores = lax.dot_general(
            grouped[first + head], keys.astype(BF16), dims, preferred_element_type=F32
        )
        scores = scores * scaling
        highest = jnp.max(scores, axis=1, keepdims=True)
        weight = jnp.exp(scores - highest)
        totals = jnp.sum(weight, axis=1, keepdims=True)
        sums = jnp.dot(weight.astype(BF16), values, preferred_element_type=F32) / totals
        logs = jnp.where(prompt >= 0, highest + jnp.log(totals), NEGATIVE)
        parts = [cached[0, first + head], cached[1, first + head]]
        logs = [tail_pieces(part[ROWS:]) for part in parts] + [logs]
        sums = [part[:ROWS].astype(F32) for part in parts] + [sums]
        highest = functools.reduce(jnp.maximum, logs)
        shares = [jnp.exp(log - highest) for log in logs]
        total = functools.reduce(jnp.add, shares)
        joined = functools.reduce(jnp.add, [share * part for share, part in zip(shares, sums)])
        result = (joined / total).astype(BF16)
        for member in range(GROUP):
            begin = (head * GROUP + member) * HEAD_DIM
            out[:, begin : begin + HEAD_DIM] = result[member * STEPS : (member + 1) * STEPS]


def finish(targets, starts, turns, own, arrived, grouped, cached):
    width = CORE_HEADS * GROUP * HEAD_DIM
    return pl.pallas_call(
        final_kernel,
        in_specs=[SMEM] + [VMEM] * 9,
        out_specs=VMEM,
        out_shape=jax.ShapeDtypeStruct((STEPS, width), BF16),
        compiler_params=pltpu.CompilerParams(vmem_limit_bytes=16 * MIB),
        name="finish",
    )(targets, starts, turns, own, *arrived, grouped, cached)


def rotary_turns():
    half = np.arange(HEAD_DIM // 2, dtype=np.float64) / (HEAD_DIM // 2)
    frequency = ROTARY_BASE ** (-np.concatenate([half, half]))
    angles = np.arange(STRETCH, dtype=np.float64)[:, None] * frequency
    return frequency.astype(np.float32), np.stack([np.cos(angles), np.sin(angles)]).astype(np.float32)


def per_device(
    stretch,
    norm_gain,
    kv_codes,
    scale_codes,
    outer_scales,
    prompt_lengths,
    target_rows,
    cache_lengths,
    kv_cache,
    queries,
    new_kv,
):
    count = lax.axis_size("tp")
    half = count // 2
    lines = stretch.transpose(1, 0, 2)
    gain = norm_gain.reshape(1, -1)
    ring = [ring_device(at, count) for at in range(count)]
    to_right = [(ring[at], ring[(at + 1) % count]) for at in range(count)]
    to_left = [(ring[at], ring[at - 1]) for at in range(count)]

    def pass_on(right, left):
        return lax.ppermute(right, "tp", to_right), lax.ppermute(left, "tp", to_left)

    other_lines = lax.ppermute(lines, "rep", [(0, 1), (1, 0)])
    weight, own, squares = dequantize(lines, kv_codes, scale_codes, outer_scales.T, gain)
    firsts = project_first(target_rows, own, squares, other_lines, gain, weight)
    arrived = [pass_on(*firsts[:2]), pass_on(*firsts[2:])]

    gain, queries, _ = lax.optimization_barrier((gain, queries, firsts[3]))
    other, other_squares = scale_features(other_lines, gain)
    grouped = regroup(queries)
    frequency, turns = rotary_turns()
    start = (prompt_lengths - STRETCH).astype(F32)[:, None] * jnp.asarray(frequency)
    starts = jnp.stack([jnp.cos(start), jnp.sin(start)])

    targets = target_rows
    cached = []
    for distance in range(half - 1, 0, -1):
        items = 3 if distance == 1 else 2
        terms = project(distance, items, targets, own, squares, other, other_squares, weight)
        for part in range(2):
            right, left = sends(part, distance == half - 1, terms, *arrived[part])
            targets, _ = lax.optimization_barrier((target_rows, right))
            arrived[part] = pass_on(right, left)
            if distance == 1:
                cached.append(
                    cache_attention(
                        part, targets, prompt_lengths, cache_lengths, grouped, kv_cache, new_kv
                    )
                )

    cached = lax.all_gather(jnp.concatenate(cached), "rep")
    out = finish(
        target_rows, starts, jnp.asarray(turns), terms, [*arrived[0], *arrived[1]], grouped, cached
    )
    return lax.all_gather(out, "rep", axis=1, tiled=True).reshape(1, STEPS, HEADS * HEAD_DIM)


def solution(mesh):
    in_specs = (
        P(None, ("grp", "rep"), "tp"),
        P("tp"),
        P("tp", None),
        P("tp", None),
        P("tp", None),
        P("grp"),
        P("grp"),
        P(("grp", "tp")),
        P(("grp", "tp"), "rep", None),
        P(("grp", "tp"), None, None),
        P(("grp", "tp"), None, None),
    )
    out_specs = P(("grp", "tp"), None, None)
    return jax.shard_map(
        per_device, mesh=mesh, in_specs=in_specs, out_specs=out_specs, check_vma=False
    )
```

time: 339 us -> 63.7 us (0.19)
  blocking collectives: 268 us -> 3.8 us
  Pallas kernels: 0 us -> 33.8 us
  other arithmetic: 30.3 us -> 0.13 us
  local copies, waits for them, and re-layouts: 19.6 us -> 1.5 us
  starting transfers between devices: 4.4 us -> 18 us
  matrix products: 11.1 us -> 0 us
    unnamed x1 -> x0, blocking collectives: 240 us -> none
    pallas_call x0 -> x16, Pallas kernels: none -> 33.8 us  [the longest x1 11.5 us: dequantize(): pl.pallas_call(weights_kernel, grid=(CORE_HEADS,), in_specs=[pl.BlockSpec...]
    psum x1 -> x0, blocking collectives: 23.1 us -> none  [per_device(): lax.psum(jnp.sum(jnp.square(stretch.astype(jnp.float32)), axis=2), 'tp')]
    convert_element_type x6 -> x1, other arithmetic: 20.9 us -> 0.01 us  [per_device(): (prompt_lengths - STRETCH).astype(F32)[:, None] * jnp.asarray(frequency)]
    ppermute x0 -> x17, starting transfers between devices: none -> 18 us  [the longest x8 10.9 us: pass_on(): lax.ppermute(left, 'tp', to_left)]
    dot_general x8 -> x0, matrix products: 11.1 us -> none  [the longest x1 5.09 us: per_device(): jnp.einsum('cpd,dn->cpn', (stretch.astype(jnp.float32) * inverse[..., Non...]
    dot_general x1 -> x0, local copies, waits for them, and re-layouts: 5.9 us -> none  [per_device(): jnp.einsum('cpd,dn->cpn', (stretch.astype(jnp.float32) * inverse[..., Non...]
    unnamed x21 -> x15, local copies, waits for them, and re-layouts: 7.06 us -> 1.5 us
  transfers between devices with their start and end apart: 1 -> 17, of which waited for: 1 -> 5; matrix products, arithmetic and copies ran while one was open for 4% -> 0% of each run, Pallas kernels for 0% -> 48%
where the time goes in v4:
time: 63.7 us; the launch traced here: 63.2 us
  Pallas kernels  33.8 us (53%)
  starting transfers between devices  18 us (28%)
  waiting for transfers between devices  5.12 us (8%)
  blocking collectives  3.8 us (6%)
  local copies, waits for them, and re-layouts  1.5 us (2%)
  between operations  0.87 us (1%)
    pallas_call x1, Pallas kernels, dequantize(): pl.pallas_call(weights_kernel, grid=(CORE_HEADS,), in_specs=[pl.BlockSpec...  11.5 us
    ppermute x8, starting transfers between devices, pass_on(): lax.ppermute(left, 'tp', to_left)  10.9 us
    pallas_call x3, Pallas kernels, project(): pl.pallas_call(functools.partial(project_kernel, farthest), grid=(items,)...  8.17 us
    ppermute x8, starting transfers between devices, pass_on(): lax.ppermute(right, 'tp', to_right)  6.61 us
    pallas_call x2, Pallas kernels, cache_attention(): pl.pallas_call(cache_kernel, grid=(1,), in_specs=[SMEM, SMEM, SMEM, pl.Bl...  5.95 us
    ppermute x8, waiting for transfers between devices, pass_on(): lax.ppermute(right, 'tp', to_right)  4.77 us
    pallas_call x1, Pallas kernels, finish(): pl.pallas_call(final_kernel, in_specs=[SMEM] + [VMEM] * 9, out_specs=VMEM...  1.98 us
    all_gather x1, blocking collectives, per_device(): cached = lax.all_gather(jnp.concatenate(cached), 'rep')  1.95 us
  transfers between devices with their start and end apart: 17, of which 5 were waited for; matrix products, arithmetic and copies ran while one was open for 0% of the time, Pallas kernels for 48%

profile of v4, /device:TPU:0, one launch (start us, length us, event | category | flops | bytes accessed | tf_op | source)
XLA Modules:
  0.0 63.2 jit_solution(1109548306431910592)
XLA Ops:
  0.0 0.5 collective-permute-start
  0.5 11.5 %dequantize.1 = (bf16[4,2048,256]{2,1,0:T(8,128)(2,1)S(1)}, bf16[3,192,2048]{2,1,0:T(8,128)(2,1)S(1)}, f32[3,8,128]{2,1,0:T(8,128)S(1)}) custom-call(bf16[3,192,2048]{2,1,0:T(8,128)(2,1)} %bitcast.10, s32[2048,2048]{1,0:T(8,128)} %value_codes.1, s32[2048,2048]{1,0:T(8,128)} %value_codes.1, s32[32,2048]{1,0:T(8,128)} %value_scales.1, ...), custom_call_target="tpu_custom_call" | custom-call | flops 134217728 | bytes 8388608 | tf_op jit(solution)/shard_map/dequantize/pallas_call | solution.py:204
  12.0 0.0 collective-permute-done.other.x
  12.0 1.7 %project_first.1 = (bf16[400,128]{1,0:T(8,128)(2,1)S(1)}, bf16[384,128]{1,0:T(8,128)(2,1)S(1)}, bf16[384,128]{1,0:T(8,128)(2,1)S(1)}, bf16[384,128]{1,0:T(8,128)(2,1)S(1)}) custom-call(s32[6]{0:T(128)S(1)} %copy-done.4, bf16[3,192,2048]{2,1,0:T(8,128)(2,1)S(1)} %get-tuple-element.32.own, f32[3,8,128]{2,1,0:T(8,128)S(1)} %get-tuple-element.33.squares, ...), custom_call_target="tpu_custom_call" | custom-call | flops 805306368 | bytes 2097152 | tf_op jit(solution)/shard_map/project_first/pallas_call | solution.py:300
  13.7 2.8 %collective-permute-start.2 = (bf16[384,128]{1,0:T(8,128)(2,1)S(1)}, bf16[384,128]{1,0:T(8,128)(2,1)S(1)}, u32[]{:S(2)}, u32[]{:S(2)}) collective-permute-start(bf16[384,128]{1,0:T(8,128)(2,1)S(1)} %get-tuple-element.35), channel_id=1, source_target_pairs={{0,2},{4,0},{8,4},{12,8},{14,12},{10,14},{6,10},{2,6},{1,3},{5,1},... | collective-permute-start | bytes 294920 | tf_op jit(solution)/shard_map/ppermute | solution.py:578
  16.5 2.0 %collective-permute-start.6 = (bf16[384,128]{1,0:T(8,128)(2,1)S(1)}, bf16[384,128]{1,0:T(8,128)(2,1)S(1)}, u32[]{:S(2)}, u32[]{:S(2)}) collective-permute-start(bf16[384,128]{1,0:T(8,128)(2,1)S(1)} %get-tuple-element.46), channel_id=1, source_target_pairs={{0,2},{4,0},{8,4},{12,8},{14,12},{10,14},{6,10},{2,6},{1,3},{5,1},... | collective-permute-start | bytes 294920 | tf_op jit(solution)/shard_map/ppermute | solution.py:578
  18.5 1.2 %scale_features.1 = (bf16[3,192,2048]{2,1,0:T(8,128)(2,1)S(1)}, f32[3,8,128]{2,1,0:T(8,128)S(1)}) custom-call(bf16[3,192,2048]{2,1,0:T(8,128)(2,1)S(1)} %collective-permute-done.other.x, f32[1,2048]{1,0:T(1,128)S(1)} %bitcast.8), custom_call_target="tpu_custom_call" | custom-call | tf_op jit(solution)/shard_map/scale_features/pallas_call | solution.py:242
  19.8 1.8 %project.3.terms = f32[2,2,776,128]{3,2,1,0:T(8,128)S(1)} custom-call(s32[6]{0:T(128)S(1)} %copy-done.4, bf16[3,192,2048]{2,1,0:T(8,128)(2,1)S(1)} %get-tuple-element.32.own, f32[3,8,128]{2,1,0:T(8,128)S(1)} %get-tuple-element.33.squares, bf16[3,192,2048]{2,1,0:T(8,128)(2,1)S(1)} %get-tuple-element.37.other, ...), custom_call_target="tpu_custom_call" | custom-call | flops 1610612736 | bytes 2097152 | tf_op jit(solution)/shard_map/project/pallas_call | solution.py:349
  21.6 0.0 copy-start.6
  21.6 0.0 collective-permute-done.2.left
  21.6 1.8 %collective-permute-done.1.right = bf16[384,128]{1,0:T(8,128)(2,1)S(1)} collective-permute-done((bf16[384,128]{1,0:T(8,128)(2,1)S(1)}, bf16[384,128]{1,0:T(8,128)(2,1)S(1)}, u32[]{:S(2)}, u32[]{:S(2)}) %collective-permute-start.1) | collective-permute-done | bytes 98336 | tf_op jit(solution)/shard_map/ppermute | solution.py:578
  23.3 0.1 sends.6
  23.4 0.4 collective-permute-start.3
  23.8 1.7 %collective-permute-start.4 = (bf16[768,128]{1,0:T(8,128)(2,1)S(1)}, bf16[768,128]{1,0:T(8,128)(2,1)S(1)}, u32[]{:S(2)}, u32[]{:S(2)}) collective-permute-start(bf16[768,128]{1,0:T(8,128)(2,1)S(1)} %get-tuple-element.42), channel_id=1, source_target_pairs={{0,2},{4,0},{8,4},{12,8},{14,12},{10,14},{6,10},{2,6},{1,3},{5,1},... | collective-permute-start | bytes 589832 | tf_op jit(solution)/shard_map/ppermute | solution.py:578
  25.5 0.0 collective-permute-done.6.left
  25.5 0.0 collective-permute-done.5.right
  25.5 0.1 sends.8
  25.5 0.4 collective-permute-start.7
  25.9 1.7 %collective-permute-start.8 = (bf16[784,128]{1,0:T(8,128)(2,1)S(1)}, bf16[784,128]{1,0:T(8,128)(2,1)S(1)}, u32[]{:S(2)}, u32[]{:S(2)}) collective-permute-start(bf16[784,128]{1,0:T(8,128)(2,1)S(1)} %get-tuple-element.48), channel_id=1, source_target_pairs={{0,2},{4,0},{8,4},{12,8},{14,12},{10,14},{6,10},{2,6},{1,3},{5,1},... | collective-permute-start | bytes 602120 | tf_op jit(solution)/shard_map/ppermute | solution.py:578
  27.6 0.1 multiply_cosine_fusion
  27.7 2.7 %project.4.terms = f32[2,2,776,128]{3,2,1,0:T(8,128)S(1)} custom-call(s32[6]{0:T(128)S(1)} %copy-done.4, bf16[3,192,2048]{2,1,0:T(8,128)(2,1)S(1)} %get-tuple-element.32.own, f32[3,8,128]{2,1,0:T(8,128)S(1)} %get-tuple-element.33.squares, bf16[3,192,2048]{2,1,0:T(8,128)(2,1)S(1)} %get-tuple-element.37.other, ...), custom_call_target="tpu_custom_call" | custom-call | flops 1610612736 | bytes 2097152 | tf_op jit(solution)/shard_map/project/pallas_call | solution.py:349
  30.4 0.8 %collective-permute-done.3.right = bf16[768,128]{1,0:T(8,128)(2,1)S(1)} collective-permute-done((bf16[768,128]{1,0:T(8,128)(2,1)S(1)}, bf16[768,128]{1,0:T(8,128)(2,1)S(1)}, u32[]{:S(2)}, u32[]{:S(2)}) %collective-permute-start.3) | collective-permute-done | bytes 196640 | tf_op jit(solution)/shard_map/ppermute | solution.py:578
  31.3 0.3 collective-permute-done.4.left
  31.6 0.1 sends.7
  31.7 1.9 %collective-permute-start.13 = (bf16[768,128]{1,0:T(8,128)(2,1)S(1)}, bf16[768,128]{1,0:T(8,128)(2,1)S(1)}, u32[]{:S(2)}, u32[]{:S(2)}) collective-permute-start(bf16[768,128]{1,0:T(8,128)(2,1)S(1)} %get-tuple-element.43), channel_id=1, source_target_pairs={{0,4},{4,8},{8,12},{12,14},{14,10},{10,6},{6,2},{2,0},{1,5},{5,9},... | collective-permute-start | bytes 589832 | tf_op jit(solution)/shard_map/ppermute | solution.py:578
  33.6 0.2 collective-permute-start.14
  33.8 1.8 %collective-permute-done.7.right = bf16[784,128]{1,0:T(8,128)(2,1)S(1)} collective-permute-done((bf16[784,128]{1,0:T(8,128)(2,1)S(1)}, bf16[784,128]{1,0:T(8,128)(2,1)S(1)}, u32[]{:S(2)}, u32[]{:S(2)}) %collective-permute-start.7) | collective-permute-done | bytes 200736 | tf_op jit(solution)/shard_map/ppermute | solution.py:578
  35.6 0.1 sends.9
  35.7 2.1 %collective-permute-start.10 = (bf16[784,128]{1,0:T(8,128)(2,1)S(1)}, bf16[784,128]{1,0:T(8,128)(2,1)S(1)}, u32[]{:S(2)}, u32[]{:S(2)}) collective-permute-start(bf16[784,128]{1,0:T(8,128)(2,1)S(1)} %get-tuple-element.50), channel_id=1, source_target_pairs={{0,2},{4,0},{8,4},{12,8},{14,12},{10,14},{6,10},{2,6},{1,3},{5,1},... | collective-permute-start | bytes 602120 | tf_op jit(solution)/shard_map/ppermute | solution.py:578
  37.8 0.2 collective-permute-start.9
  38.0 3.7 %project.5.terms.own = f32[3,2,776,128]{3,2,1,0:T(8,128)S(1)} custom-call(s32[6]{0:T(128)S(1)} %copy-done.4, bf16[3,192,2048]{2,1,0:T(8,128)(2,1)S(1)} %get-tuple-element.32.own, f32[3,8,128]{2,1,0:T(8,128)S(1)} %get-tuple-element.33.squares, bf16[3,192,2048]{2,1,0:T(8,128)(2,1)S(1)} %get-tuple-element.37.other, ...), custom_call_target="tpu_custom_call" | custom-call | flops 2415919104 | bytes 2097152 | tf_op jit(solution)/shard_map/project/pallas_call | solution.py:349
  41.7 0.0 copy-start.2
  41.7 0.8 %sends.11 = (bf16[768,128]{1,0:T(8,128)(2,1)}, bf16[768,128]{1,0:T(8,128)(2,1)}) custom-call(f32[3,2,776,128]{3,2,1,0:T(8,128)S(1)} %project.5.terms.own, bf16[768,128]{1,0:T(8,128)(2,1)S(1)} %collective-permute-done.13.right, bf16[768,128]{1,0:T(8,128)(2,1)S(1)} %collective-permute-done.14.left), custom_call_target="tpu_custom_call" | custom-call | tf_op jit(solution)/shard_map/sends/pallas_call | solution.py:386
  42.6 2.0 %collective-permute-start.15 = (bf16[768,128]{1,0:T(8,128)(2,1)}, bf16[768,128]{1,0:T(8,128)(2,1)S(1)}, u32[]{:S(2)}, u32[]{:S(2)}) collective-permute-start(bf16[768,128]{1,0:T(8,128)(2,1)} %get-tuple-element.54), channel_id=1, source_target_pairs={{0,4},{4,8},{8,12},{12,14},{14,10},{10,6},{6,2},{2,0},{1,5},{5,9},... | collective-permute-start | bytes 589832 | tf_op jit(solution)/shard_map/ppermute | solution.py:578
  44.6 0.0 collective-permute-start.16
  44.6 0.3 collective-permute-done.9.right
  44.9 0.7 %sends.10 = (bf16[784,128]{1,0:T(8,128)(2,1)}, bf16[784,128]{1,0:T(8,128)(2,1)S(1)}) custom-call(f32[3,2,776,128]{3,2,1,0:T(8,128)S(1)} %project.5.terms.own, bf16[784,128]{1,0:T(8,128)(2,1)S(1)} %collective-permute-done.9.right, bf16[784,128]{1,0:T(8,128)(2,1)S(1)} %collective-permute-done.10.left), custom_call_target="tpu_custom_call" | custom-call | tf_op jit(solution)/shard_map/sends/pallas_call | solution.py:386
  45.6 1.7 %collective-permute-start.11 = (bf16[784,128]{1,0:T(8,128)(2,1)}, bf16[784,128]{1,0:T(8,128)(2,1)S(1)}, u32[]{:S(2)}, u32[]{:S(2)}) collective-permute-start(bf16[784,128]{1,0:T(8,128)(2,1)} %get-tuple-element.51), channel_id=1, source_target_pairs={{0,4},{4,8},{8,12},{12,14},{14,10},{10,6},{6,2},{2,0},{1,5},{5,9},... | collective-permute-start | bytes 602120 | tf_op jit(solution)/shard_map/ppermute | solution.py:578
  47.3 0.4 collective-permute-start.12
  48.4 1.6 %regroup.1.q.grouped = bf16[8,32,128]{2,1,0:T(8,128)(2,1)} custom-call(bf16[1,2,16384]{2,1,0:T(2,128)(2,1)} %queries), custom_call_target="tpu_custom_call" | custom-call | tf_op jit(solution)/shard_map/regroup/pallas_call | solution.py:405
  49.9 0.8 %copy-done = bf16[8,32,128]{2,1,0:T(8,128)(2,1)S(1)} copy-done((bf16[8,32,128]{2,1,0:T(8,128)(2,1)S(1)}, bf16[8,32,128]{2,1,0:T(8,128)(2,1)}, u32[]{:S(2)}) %copy-start) | copy-done | bytes 65560
  50.8 3.0 %cache_attention.3 = bf16[4,48,128]{2,1,0:T(8,128)(2,1)S(1)} custom-call(s32[6]{0:T(128)S(1)} %copy-done.4, s32[6]{0:T(128)S(1)} %copy-done.5, s32[1]{0:T(128)S(6)} %copy.15.stored, bf16[8,32,128]{2,1,0:T(8,128)(2,1)S(1)} %copy-done, bf16[1,1024,2048]{2,1,0:T(8,128)(2,1)} %values.3, bf16[1,1024,2048]{2,1,0:T(8,128)(2,1)} %values.3, ...), custom_call_target="tpu_custom_call" | custom-call | flops 67108864 | bytes 2097152 | tf_op jit(solution)/shard_map/cache_attention/pallas_call | solution.py:464
  53.7 0.0 copy-start.1
  53.7 3.0 %cache_attention.2 = bf16[4,48,128]{2,1,0:T(8,128)(2,1)S(1)} custom-call(s32[6]{0:T(128)S(1)} %copy-done.4, s32[6]{0:T(128)S(1)} %copy-done.5, s32[1]{0:T(128)S(6)} %copy.15.stored, bf16[8,32,128]{2,1,0:T(8,128)(2,1)S(1)} %copy-done, bf16[1,1024,2048]{2,1,0:T(8,128)(2,1)} %values.3, bf16[1,1024,2048]{2,1,0:T(8,128)(2,1)} %values.3, ...), custom_call_target="tpu_custom_call" | custom-call | flops 67108864 | bytes 2097152 | tf_op jit(solution)/shard_map/cache_attention/pallas_call | solution.py:464
  56.8 1.9 %all-gather = bf16[16,48,128]{2,1,0:T(8,128)(2,1)S(1)} all-gather(bf16[8,48,128]{2,1,0:T(8,128)(2,1)S(1)} %pad_maximum_fusion), channel_id=2, replica_groups=mesh['grp'=2,'tp'=8,'rep'=2] {'rep'}, dimensions={0}, use_global_device_ids=true | all-gather | bytes 294912 | tf_op jit(solution)/shard_map/all_gather | solution.py:608
  58.8 2.0 %finish.1 = bf16[2,8192]{1,0:T(2,128)(2,1)S(1)} custom-call(s32[6]{0:T(128)S(1)} %copy-done.4, f32[2,6,128]{2,1,0:T(8,128)S(1)} %pad_maximum_fusion.1.starts, f32[2,192,128]{2,1,0:T(8,128)S(1)} %copy-done.1, f32[3,2,776,128]{3,2,1,0:T(8,128)S(1)} %project.5.terms.own, bf16[784,128]{1,0:T(8,128)(2,1)S(1)} %collective-permute-done.11.right_a, ...), custom_call_target="tpu_custom_call" | custom-call | tf_op jit(solution)/shard_map/finish/pallas_call | solution.py:539
  60.7 1.9 %all_gather.11 = bf16[2,16384]{1,0:T(2,128)(2,1)S(1)} all-gather(bf16[2,8192]{1,0:T(2,128)(2,1)S(1)} %finish.1), channel_id=1, replica_groups=mesh['grp'=2,'tp'=8,'rep'=2] {'rep'}, dimensions={1}, use_global_device_ids=true | all-gather | bytes 98304 | tf_op jit(solution)/shard_map/all_gather | solution.py:612
  62.6 0.6 copy.16
  (23 shorter events, 0.1 us)
Async XLA Ops:
  0.0 12.0 %collective-permute-start = (bf16[3,192,2048]{2,1,0:T(8,128)(2,1)}, bf16[3,192,2048]{2,1,0:T(8,128)(2,1)S(1)}, u32[]{:S(2)}, u32[]{:S(2)}) collective-permute-start(bf16[3,192,2048]{2,1,0:T(8,128)(2,1)} %bitcast.9), channel_id=1, source_target_pairs={{0,1},{1,0},{2,3},{3,2},{4,5},{5,4},{6,7},{7,6},{8,9},{9,8},{10,11... | collective-permute-start | bytes 7077896 | tf_op jit(solution)/shard_map/ppermute | solution.py:580
  0.5 11.5 %copy-start.5 = (s32[6]{0:T(128)S(1)}, s32[6]{0:T(128)}, u32[]{:S(2)}) copy-start(s32[6]{0:T(128)} %lengths.3) | copy-start | bytes 76
  0.5 11.5 %copy-start.3 = (f32[2048]{0:T(1024)S(1)}, f32[2048]{0:T(1024)}, u32[]{:S(2)}) copy-start(f32[2048]{0:T(1024)} %param.14) | copy-start | bytes 24580
  0.5 11.5 %copy-start.4 = (s32[6]{0:T(128)S(1)}, s32[6]{0:T(128)}, u32[]{:S(2)}) copy-start(s32[6]{0:T(128)} %targets.9) | copy-start | bytes 76
  13.7 7.9 %collective-permute-start.2 = (bf16[384,128]{1,0:T(8,128)(2,1)S(1)}, bf16[384,128]{1,0:T(8,128)(2,1)S(1)}, u32[]{:S(2)}, u32[]{:S(2)}) collective-permute-start(bf16[384,128]{1,0:T(8,128)(2,1)S(1)} %get-tuple-element.35), channel_id=1, source_target_pairs={{0,2},{4,0},{8,4},{12,8},{14,12},{10,14},{6,10},{2,6},{1,3},{5,1},... | collective-permute-start | bytes 294920 | tf_op jit(solution)/shard_map/ppermute | solution.py:578
  16.5 9.0 %collective-permute-start.5 = (bf16[400,128]{1,0:T(8,128)(2,1)S(1)}, bf16[400,128]{1,0:T(8,128)(2,1)S(1)}, u32[]{:S(2)}, u32[]{:S(2)}) collective-permute-start(bf16[400,128]{1,0:T(8,128)(2,1)S(1)} %get-tuple-element.45), channel_id=1, source_target_pairs={{0,4},{4,8},{8,12},{12,14},{14,10},{10,6},{6,2},{2,0},{1,5},{5,9},... | collective-permute-start | bytes 307208 | tf_op jit(solution)/shard_map/ppermute | solution.py:578
  16.5 9.0 %collective-permute-start.6 = (bf16[384,128]{1,0:T(8,128)(2,1)S(1)}, bf16[384,128]{1,0:T(8,128)(2,1)S(1)}, u32[]{:S(2)}, u32[]{:S(2)}) collective-permute-start(bf16[384,128]{1,0:T(8,128)(2,1)S(1)} %get-tuple-element.46), channel_id=1, source_target_pairs={{0,2},{4,0},{8,4},{12,8},{14,12},{10,14},{6,10},{2,6},{1,3},{5,1},... | collective-permute-start | bytes 294920 | tf_op jit(solution)/shard_map/ppermute | solution.py:578
  18.5 4.8 %collective-permute-start.1 = (bf16[384,128]{1,0:T(8,128)(2,1)S(1)}, bf16[384,128]{1,0:T(8,128)(2,1)S(1)}, u32[]{:S(2)}, u32[]{:S(2)}) collective-permute-start(bf16[384,128]{1,0:T(8,128)(2,1)S(1)} %get-tuple-element.39), channel_id=1, source_target_pairs={{0,4},{4,8},{8,12},{12,14},{14,10},{10,6},{6,2},{2,0},{1,5},{5,9},... | collective-permute-start | bytes 294920 | tf_op jit(solution)/shard_map/ppermute | solution.py:578
  21.6 6.1 %copy-start.6 = (f32[128]{0:T(128)S(1)}, f32[128]{0:T(128)}, u32[]{:S(2)}) copy-start(f32[128]{0:T(128)} %constant.7.clone) | copy-start | bytes 1540
  23.4 7.9 %collective-permute-start.3 = (bf16[768,128]{1,0:T(8,128)(2,1)S(1)}, bf16[768,128]{1,0:T(8,128)(2,1)S(1)}, u32[]{:S(2)}, u32[]{:S(2)}) collective-permute-start(bf16[768,128]{1,0:T(8,128)(2,1)S(1)} %get-tuple-element.40), channel_id=1, source_target_pairs={{0,4},{4,8},{8,12},{12,14},{14,10},{10,6},{6,2},{2,0},{1,5},{5,9},... | collective-permute-start | bytes 589832 | tf_op jit(solution)/shard_map/ppermute | solution.py:578
  23.8 7.8 %collective-permute-start.4 = (bf16[768,128]{1,0:T(8,128)(2,1)S(1)}, bf16[768,128]{1,0:T(8,128)(2,1)S(1)}, u32[]{:S(2)}, u32[]{:S(2)}) collective-permute-start(bf16[768,128]{1,0:T(8,128)(2,1)S(1)} %get-tuple-element.42), channel_id=1, source_target_pairs={{0,2},{4,0},{8,4},{12,8},{14,12},{10,14},{6,10},{2,6},{1,3},{5,1},... | collective-permute-start | bytes 589832 | tf_op jit(solution)/shard_map/ppermute | solution.py:578
  25.5 10.0 %collective-permute-start.7 = (bf16[784,128]{1,0:T(8,128)(2,1)S(1)}, bf16[784,128]{1,0:T(8,128)(2,1)S(1)}, u32[]{:S(2)}, u32[]{:S(2)}) collective-permute-start(bf16[784,128]{1,0:T(8,128)(2,1)S(1)} %get-tuple-element.47), channel_id=1, source_target_pairs={{0,4},{4,8},{8,12},{12,14},{14,10},{10,6},{6,2},{2,0},{1,5},{5,9},... | collective-permute-start | bytes 602120 | tf_op jit(solution)/shard_map/ppermute | solution.py:578
  25.9 9.7 %collective-permute-start.8 = (bf16[784,128]{1,0:T(8,128)(2,1)S(1)}, bf16[784,128]{1,0:T(8,128)(2,1)S(1)}, u32[]{:S(2)}, u32[]{:S(2)}) collective-permute-start(bf16[784,128]{1,0:T(8,128)(2,1)S(1)} %get-tuple-element.48), channel_id=1, source_target_pairs={{0,2},{4,0},{8,4},{12,8},{14,12},{10,14},{6,10},{2,6},{1,3},{5,1},... | collective-permute-start | bytes 602120 | tf_op jit(solution)/shard_map/ppermute | solution.py:578
  31.7 10.0 %collective-permute-start.13 = (bf16[768,128]{1,0:T(8,128)(2,1)S(1)}, bf16[768,128]{1,0:T(8,128)(2,1)S(1)}, u32[]{:S(2)}, u32[]{:S(2)}) collective-permute-start(bf16[768,128]{1,0:T(8,128)(2,1)S(1)} %get-tuple-element.43), channel_id=1, source_target_pairs={{0,4},{4,8},{8,12},{12,14},{14,10},{10,6},{6,2},{2,0},{1,5},{5,9},... | collective-permute-start | bytes 589832 | tf_op jit(solution)/shard_map/ppermute | solution.py:578
  33.6 8.1 %collective-permute-start.14 = (bf16[768,128]{1,0:T(8,128)(2,1)S(1)}, bf16[768,128]{1,0:T(8,128)(2,1)S(1)}, u32[]{:S(2)}, u32[]{:S(2)}) collective-permute-start(bf16[768,128]{1,0:T(8,128)(2,1)S(1)} %get-tuple-element.53), channel_id=1, source_target_pairs={{0,2},{4,0},{8,4},{12,8},{14,12},{10,14},{6,10},{2,6},{1,3},{5,1},... | collective-permute-start | bytes 589832 | tf_op jit(solution)/shard_map/ppermute | solution.py:578
  35.7 8.9 %collective-permute-start.10 = (bf16[784,128]{1,0:T(8,128)(2,1)S(1)}, bf16[784,128]{1,0:T(8,128)(2,1)S(1)}, u32[]{:S(2)}, u32[]{:S(2)}) collective-permute-start(bf16[784,128]{1,0:T(8,128)(2,1)S(1)} %get-tuple-element.50), channel_id=1, source_target_pairs={{0,2},{4,0},{8,4},{12,8},{14,12},{10,14},{6,10},{2,6},{1,3},{5,1},... | collective-permute-start | bytes 602120 | tf_op jit(solution)/shard_map/ppermute | solution.py:578
  37.8 7.2 %collective-permute-start.9 = (bf16[784,128]{1,0:T(8,128)(2,1)S(1)}, bf16[784,128]{1,0:T(8,128)(2,1)S(1)}, u32[]{:S(2)}, u32[]{:S(2)}) collective-permute-start(bf16[784,128]{1,0:T(8,128)(2,1)S(1)} %get-tuple-element.49), channel_id=1, source_target_pairs={{0,4},{4,8},{8,12},{12,14},{14,10},{10,6},{6,2},{2,0},{1,5},{5,9},... | collective-permute-start | bytes 602120 | tf_op jit(solution)/shard_map/ppermute | solution.py:578
  41.7 8.2 %copy-start.2 = (bf16[1,2,2048]{2,1,0:T(2,128)(2,1)S(1)}, bf16[1,2,2048]{2,1,0:T(2,128)(2,1)}, u32[]{:S(2)}) copy-start(bf16[1,2,2048]{2,1,0:T(2,128)(2,1)} %fresh_values.3) | copy-start | bytes 24580
  42.6 16.2 %collective-permute-start.15 = (bf16[768,128]{1,0:T(8,128)(2,1)}, bf16[768,128]{1,0:T(8,128)(2,1)S(1)}, u32[]{:S(2)}, u32[]{:S(2)}) collective-permute-start(bf16[768,128]{1,0:T(8,128)(2,1)} %get-tuple-element.54), channel_id=1, source_target_pairs={{0,4},{4,8},{8,12},{12,14},{14,10},{10,6},{6,2},{2,0},{1,5},{5,9},... | collective-permute-start | bytes 589832 | tf_op jit(solution)/shard_map/ppermute | solution.py:578
  44.6 14.1 %collective-permute-start.16 = (bf16[768,128]{1,0:T(8,128)(2,1)}, bf16[768,128]{1,0:T(8,128)(2,1)S(1)}, u32[]{:S(2)}, u32[]{:S(2)}) collective-permute-start(bf16[768,128]{1,0:T(8,128)(2,1)} %get-tuple-element.55), channel_id=1, source_target_pairs={{0,2},{4,0},{8,4},{12,8},{14,12},{10,14},{6,10},{2,6},{1,3},{5,1},... | collective-permute-start | bytes 589832 | tf_op jit(solution)/shard_map/ppermute | solution.py:578
  45.6 13.1 %collective-permute-start.11 = (bf16[784,128]{1,0:T(8,128)(2,1)}, bf16[784,128]{1,0:T(8,128)(2,1)S(1)}, u32[]{:S(2)}, u32[]{:S(2)}) collective-permute-start(bf16[784,128]{1,0:T(8,128)(2,1)} %get-tuple-element.51), channel_id=1, source_target_pairs={{0,4},{4,8},{8,12},{12,14},{14,10},{10,6},{6,2},{2,0},{1,5},{5,9},... | collective-permute-start | bytes 602120 | tf_op jit(solution)/shard_map/ppermute | solution.py:578
  47.3 11.4 %collective-permute-start.12 = (bf16[784,128]{1,0:T(8,128)(2,1)S(1)}, bf16[784,128]{1,0:T(8,128)(2,1)S(1)}, u32[]{:S(2)}, u32[]{:S(2)}) collective-permute-start(bf16[784,128]{1,0:T(8,128)(2,1)S(1)} %get-tuple-element.52), channel_id=1, source_target_pairs={{0,2},{4,0},{8,4},{12,8},{14,12},{10,14},{6,10},{2,6},{1,3},{5,1},... | collective-permute-start | bytes 602120 | tf_op jit(solution)/shard_map/ppermute | solution.py:578
  49.9 0.8 %copy-start = (bf16[8,32,128]{2,1,0:T(8,128)(2,1)S(1)}, bf16[8,32,128]{2,1,0:T(8,128)(2,1)}, u32[]{:S(2)}) copy-start(bf16[8,32,128]{2,1,0:T(8,128)(2,1)} %regroup.1.q.grouped) | copy-start | bytes 196612
  53.7 5.0 %copy-start.1 = (f32[2,192,128]{2,1,0:T(8,128)S(1)}, f32[2,192,128]{2,1,0:T(8,128)}, u32[]{:S(2)}) copy-start(f32[2,192,128]{2,1,0:T(8,128)} %constant.8.clone.turns) | copy-start | bytes 589828

commit v5 on v4

v5 whole, which is shorter than its diff:
```python
import functools
import math

import jax
import jax.numpy as jnp
import numpy as np
from jax import lax
from jax.experimental import pallas as pl
from jax.experimental.pallas import tpu as pltpu
from jax.sharding import PartitionSpec as P

D = 16384
HEADS = 128
KV_HEADS = 8
HEAD_DIM = 128
STRETCH = 192
STEPS = 2
QBLOCK = 64
GROUP = HEADS // KV_HEADS
ROWS = GROUP * STEPS
TAIL = 16
PART = ROWS + TAIL
CORE_HEADS = KV_HEADS // 2
NORMAL_FLOAT_LEVELS = [
    -1.0,
    -0.6961928009986877,
    -0.5250730514526367,
    -0.39491748809814453,
    -0.28444138169288635,
    -0.18477343022823334,
    -0.09105003625154495,
    0.0,
    0.07958029955625534,
    0.16093020141124725,
    0.24611230194568634,
    0.33791524171829224,
    0.44070982933044434,
    0.5626170039176941,
    0.7229568362236023,
    1.0,
]
ROTARY_BASE = 500000.0
EPSILON = 1e-05
NEGATIVE = -1e30
BF16 = jnp.bfloat16
F32 = jnp.float32
MIB = 1024 * 1024
VMEM = pl.BlockSpec(memory_space=pltpu.VMEM)
SMEM = pl.BlockSpec(memory_space=pltpu.SMEM)


def in_hbm(*arrays):
    return [pltpu.with_memory_space_constraint(array, pltpu.HBM) for array in arrays]


def ring_device(place, count):
    half = count // 2
    if isinstance(place, int):
        return 2 * place if place < half else 2 * (count - 1 - place) + 1
    return jnp.where(place < half, 2 * place, 2 * (count - 1 - place) + 1)


def owner_at(distance):
    count = lax.axis_size("tp")
    here = lax.axis_index("tp")
    place = jnp.where(here % 2 == 0, here // 2, count - 1 - here // 2)
    return ring_device((place + distance + count) % count, count)


def turned(column):
    rows = lax.broadcasted_iota(jnp.int32, (column.shape[0], 128), 0)
    lanes = lax.broadcasted_iota(jnp.int32, (column.shape[0], 128), 1)
    return jnp.sum(jnp.where(rows == lanes, column, 0.0), axis=0, keepdims=True)


def stood(row, count):
    rows = lax.broadcasted_iota(jnp.int32, (count, 128), 0)
    lanes = lax.broadcasted_iota(jnp.int32, (count, 128), 1)
    return jnp.sum(jnp.where(rows == lanes, row, 0.0), axis=1, keepdims=True)


def token_rows(column):
    at = lax.broadcasted_iota(jnp.int32, (8, 128), 0)
    ends = turned(column[128:])
    return jnp.where(at == 0, turned(column[:128]), jnp.where(at == 1, ends, 0.0))


def token_column(rows):
    return jnp.concatenate([stood(rows[0:1], 128), stood(rows[1:2], STRETCH - 128)], axis=0)


def two_pieces(rows):
    high = rows.astype(BF16).astype(F32)
    return jnp.concatenate([high, rows - high], axis=0).astype(BF16)


def one_piece(rows):
    rows = rows.astype(F32)
    return rows[:8] + rows[8:]


def pieces_tail(logs):
    row = turned(logs)
    high = row.astype(BF16).astype(F32)
    middle = (row - high).astype(BF16).astype(F32)
    low = row - high - middle
    at = lax.broadcasted_iota(jnp.int32, (TAIL, 128), 0)
    tail = jnp.where(at == 0, high, jnp.where(at == 1, middle, jnp.where(at == 2, low, 0.0)))
    return tail.astype(BF16)


def tail_pieces(tail):
    tail = tail.astype(F32)
    return stood(tail[0:1, :] + tail[1:2, :] + tail[2:3, :], ROWS)


def gathered_levels(table, codes):
    table = jnp.broadcast_to(table[None], (codes.shape[0] // 8, 8, 128)).reshape(codes.shape)
    return jnp.take_along_axis(table, codes, axis=1, mode="promise_in_bounds")


def selected_levels(codes):
    values = [jnp.float32(level) for level in NORMAL_FLOAT_LEVELS]
    for bit in (1, 2, 4, 8):
        mask = (codes & bit) != 0 if bit < 8 else codes >= 8
        values = [
            jnp.where(mask, values[at + 1], values[at]) for at in range(0, len(values), 2)
        ]
    return values[0]


def block_scales(scales, outer, column):
    count = scales.shape[0]
    line = lax.broadcasted_iota(jnp.int32, outer.shape, 0)
    line = jnp.sum(jnp.where(line == column, outer, 0.0), axis=0, keepdims=True)
    rows = lax.broadcasted_iota(jnp.int32, (count, count), 0)
    lanes = lax.broadcasted_iota(jnp.int32, (count, count), 1)
    second = jnp.sum(jnp.where(rows == lanes, line, 0.0), axis=1, keepdims=True)
    return (scales.astype(F32) + 1.0) / 256.0 * second


def weights_kernel(
    half, key_codes, value_codes, key_scales, value_scales, outer, *refs
):
    if half == 0:
        x, gain, out, scaled, squares, scales = refs
    else:
        out, scales = refs
    item, block = pl.program_id(0), pl.program_id(1)
    depth = key_codes.shape[0]
    head = lax.axis_index("rep") * CORE_HEADS + 2 * half + item
    columns = outer.shape[0] // 2
    column = head // (KV_HEADS // columns)

    @pl.when(block == 0)
    def _():
        scales[0] = block_scales(key_scales[...], outer[...], column)
        scales[1] = block_scales(value_scales[...], outer[...], columns + column)

    lane = lax.broadcasted_iota(jnp.int32, (8, 128), 1)
    table = jnp.zeros((8, 128), F32)
    for code, level in enumerate(NORMAL_FLOAT_LEVELS):
        table = jnp.where(lane == code, level, table)
    together = 4

    def body(step, _):
        begins = [
            pl.multiple_of((step * together + at) * QBLOCK, QBLOCK) for at in range(together)
        ]
        codes = [
            (key_codes[pl.ds(begin, QBLOCK), :], value_codes[pl.ds(begin, QBLOCK), :])
            for begin in begins
        ]
        results = []
        for at, (key, value) in enumerate(codes):
            row = pl.ds(block * (depth // QBLOCK) + step * together + at, 1)
            results.append(
                (
                    (gathered_levels(table, key) * scales[0, row, :]).astype(BF16),
                    (selected_levels(value) * scales[1, row, :]).astype(BF16),
                )
            )
        for begin, (key, value) in zip(begins, results):
            rows = pl.ds(pl.multiple_of(block * depth + begin, QBLOCK), QBLOCK)
            out[item, rows, :HEAD_DIM] = key
            out[item, rows, HEAD_DIM:] = value
        return 0

    lax.fori_loop(0, depth // (QBLOCK * together), body, 0)

    if half == 0:
        at = item * pl.num_programs(1) + block

        @pl.when(at == 0)
        def _():
            squares[...] = jnp.zeros(squares.shape, F32)

        width = x.shape[2]
        begin = pl.multiple_of(at * width, 128)
        for prompt in range(x.shape[0]):
            wide = x[prompt].astype(F32)
            scaled[prompt, :, pl.ds(begin, width)] = (wide * gain[...]).astype(BF16)
            squares[prompt] += token_rows(jnp.sum(wide * wide, axis=1, keepdims=True))


def dequantize(half, x, codes, scales, outer, gain):
    per_rep, _, features = x.shape
    depth = min(1024, features)
    blocks = features // depth
    width = features // (2 * blocks)
    head = lambda i: lax.axis_index("rep") * CORE_HEADS + 2 * half + i
    x, codes, scales, outer, gain = in_hbm(x, codes, scales, outer, gain)
    in_specs = [
        pl.BlockSpec((depth, HEAD_DIM), lambda i, k: (k, head(i))),
        pl.BlockSpec((depth, HEAD_DIM), lambda i, k: (k, KV_HEADS + head(i))),
        pl.BlockSpec((scales.shape[0], HEAD_DIM), lambda i, k: (0, head(i))),
        pl.BlockSpec((scales.shape[0], HEAD_DIM), lambda i, k: (0, KV_HEADS + head(i))),
        pl.BlockSpec(outer.shape, lambda i, k: (0, 0)),
    ]
    operands = [codes, codes, scales, scales, outer]
    shapes = [jax.ShapeDtypeStruct((2, features, 2 * HEAD_DIM), BF16)]
    if half == 0:
        in_specs += [
            pl.BlockSpec((per_rep, STRETCH, width), lambda i, k: (0, 0, i * blocks + k)),
            pl.BlockSpec((1, width), lambda i, k: (0, i * blocks + k)),
        ]
        operands += [x, gain]
        shapes += [
            jax.ShapeDtypeStruct(x.shape, BF16),
            jax.ShapeDtypeStruct((per_rep, 8, 128), F32),
        ]
    return pl.pallas_call(
        functools.partial(weights_kernel, half),
        grid=(2, blocks),
        in_specs=in_specs,
        out_specs=[VMEM] * len(shapes),
        out_shape=shapes,
        scratch_shapes=[pltpu.VMEM((2, scales.shape[0], HEAD_DIM), F32)],
        compiler_params=pltpu.CompilerParams(vmem_limit_bytes=32 * MIB),
        cost_estimate=pl.CostEstimate(
            flops=16 * codes.size, bytes_accessed=codes.size, transcendentals=0
        ),
        name="dequantize",
    )(*operands)


def prompt_of(targets, owner):
    prompt = jnp.int32(-1)
    for at in range(targets.shape[0]):
        prompt = jnp.where(targets[at] == owner, at, prompt)
    return prompt


def lines_of(targets, distance, own, squares, other, gain, line, total):
    per_rep = own.shape[0]
    prompt = prompt_of(targets, owner_at(distance))
    at = lax.rem(jnp.maximum(prompt, 0), per_rep)
    is_own = prompt // per_rep == lax.axis_index("rep")

    @pl.when((prompt >= 0) & is_own)
    def _():
        line[...] = own[at]
        total[...] = squares[at]

    @pl.when((prompt >= 0) & jnp.logical_not(is_own))
    def _():
        wide = other[at].astype(F32)
        line[...] = (wide * gain[...]).astype(BF16)
        total[...] = token_rows(jnp.sum(wide * wide, axis=1, keepdims=True))

    @pl.when(prompt < 0)
    def _():
        line[...] = jnp.zeros(line.shape, BF16)
        total[...] = jnp.zeros(total.shape, F32)


def line_specs(distances, x):
    return [
        jax.ShapeDtypeStruct((len(distances) * STRETCH, x.shape[2]), BF16),
        jax.ShapeDtypeStruct((len(distances), 8, 128), F32),
    ]


def first_kernel(distances, targets, own, squares, other, gain, weight, *refs):
    right, left, terms, lines, totals = refs
    for item, distance in enumerate(distances):
        line = lines.at[item * STRETCH : (item + 1) * STRETCH]
        lines_of(targets, distance, own, squares, other, gain, line, totals.at[item])
    products(distances, lines, totals, weight, right, left, terms)


def second_kernel(distances, lines, totals, weight, *refs):
    products(distances, lines, totals, weight, *refs)


def products(distances, lines, totals, weight, right, left, terms):
    for head in range(2):
        product = jnp.dot(lines[...], weight[head], preferred_element_type=F32)
        rows = slice(head * STRETCH, (head + 1) * STRETCH)
        right[rows] = product[:STRETCH, :HEAD_DIM].astype(BF16)
        left[rows] = product[:STRETCH, HEAD_DIM:].astype(BF16)
        for item in range(1, len(distances)):
            part = product[item * STRETCH : (item + 1) * STRETCH]
            begin = head * STRETCH
            terms[item - 1, begin : begin + STRETCH] = part[:, :HEAD_DIM]
            begin += 2 * STRETCH
            terms[item - 1, begin : begin + STRETCH] = part[:, HEAD_DIM:]
    for item in range(1, len(distances)):
        terms[item - 1, 4 * STRETCH :] = totals[item]
    right[2 * STRETCH :] = two_pieces(totals[0])


def first_shapes(distances):
    rows = 2 * STRETCH
    return [
        jax.ShapeDtypeStruct((rows + TAIL, HEAD_DIM), BF16),
        jax.ShapeDtypeStruct((rows, HEAD_DIM), BF16),
        jax.ShapeDtypeStruct((len(distances) - 1, 2 * rows + 8, HEAD_DIM), F32),
    ]


def project_cost(distances, weight):
    return pl.CostEstimate(
        flops=len(distances) * STRETCH * weight.size * 2,
        bytes_accessed=weight.size,
        transcendentals=0,
    )


def project_first(distances, targets, own, squares, other, gain, weight):
    return pl.pallas_call(
        functools.partial(first_kernel, distances),
        in_specs=[SMEM] + [VMEM] * 5,
        out_specs=[VMEM] * 5,
        out_shape=first_shapes(distances) + line_specs(distances, own),
        compiler_params=pltpu.CompilerParams(vmem_limit_bytes=24 * MIB),
        cost_estimate=project_cost(distances, weight),
        name="project_first",
    )(targets, own, squares, other, gain, weight)


def project_second(distances, lines, totals, weight):
    return pl.pallas_call(
        functools.partial(second_kernel, distances),
        in_specs=[VMEM] * 3,
        out_specs=[VMEM] * 3,
        out_shape=first_shapes(distances),
        compiler_params=pltpu.CompilerParams(vmem_limit_bytes=24 * MIB),
        cost_estimate=project_cost(distances, weight),
        name="project_second",
    )(lines, totals, weight)


def project_kernel(
    distances, targets, own, squares, other, gain, weight_a, weight_b, out_a, out_b, lines, totals
):
    for item, distance in enumerate(distances):
        line = lines.at[item * STRETCH : (item + 1) * STRETCH]
        lines_of(targets, distance, own, squares, other, gain, line, totals.at[item])
    for weight, out in ((weight_a, out_a), (weight_b, out_b)):
        for head in range(2):
            product = jnp.dot(lines[...], weight[head], preferred_element_type=F32)
            for item in range(len(distances)):
                part = product[item * STRETCH : (item + 1) * STRETCH]
                begin = head * STRETCH
                out[item, begin : begin + STRETCH] = part[:, :HEAD_DIM]
                begin += 2 * STRETCH
                out[item, begin : begin + STRETCH] = part[:, HEAD_DIM:]
        for item in range(len(distances)):
            out[item, 4 * STRETCH :] = totals[item]


def project(distances, targets, own, squares, other, gain, weights):
    shape = jax.ShapeDtypeStruct((len(distances), 4 * STRETCH + 8, HEAD_DIM), F32)
    line, total = line_specs(distances, own)
    return pl.pallas_call(
        functools.partial(project_kernel, distances),
        in_specs=[SMEM] + [VMEM] * 6,
        out_specs=[VMEM] * 2,
        out_shape=[shape, shape],
        scratch_shapes=[pltpu.VMEM(line.shape, BF16), pltpu.VMEM(total.shape, F32)],
        compiler_params=pltpu.CompilerParams(vmem_limit_bytes=24 * MIB),
        cost_estimate=project_cost(distances, weights[0]),
        name="project",
    )(targets, own, squares, other, gain, *weights)


def send_kernel(half, first, terms, right, left, to_right, to_left):
    rows = 4 * STRETCH
    middle = 2 * STRETCH
    if first:
        to_right[:middle] = (terms[0, :middle] + right[:middle].astype(F32)).astype(BF16)
        to_right[middle:rows] = terms[0, middle:rows].astype(BF16)
        to_left[:middle] = terms[1, :middle].astype(BF16)
        to_left[middle:rows] = (terms[1, middle:rows] + left[...].astype(F32)).astype(BF16)
    else:
        to_right[:rows] = (terms[0, :rows] + right[:rows].astype(F32)).astype(BF16)
        to_left[:rows] = (terms[1, :rows] + left[:rows].astype(F32)).astype(BF16)
    if half == 0:
        right_sum, left_sum = terms[0, rows:], terms[1, rows:]
        right_sum += one_piece(right[middle if first else rows :])
        if not first:
            left_sum += one_piece(left[rows:])
        to_right[rows:] = two_pieces(right_sum)
        to_left[rows:] = two_pieces(left_sum)


def sends(half, first, terms, right, left):
    rows = 4 * STRETCH + (TAIL if half == 0 else 0)
    shape = jax.ShapeDtypeStruct((rows, HEAD_DIM), BF16)
    return pl.pallas_call(
        functools.partial(send_kernel, half, first),
        in_specs=[VMEM] * 3,
        out_specs=[VMEM] * 2,
        out_shape=[shape, shape],
        compiler_params=pltpu.CompilerParams(vmem_limit_bytes=16 * MIB),
        name="sends",
    )(terms, right, left)


def prepare_kernel(targets, queries, starts, turns, grouped, rotary):
    for head in range(KV_HEADS):
        for member in range(GROUP):
            begin = (head * GROUP + member) * HEAD_DIM
            rows = slice(member * STEPS, (member + 1) * STEPS)
            grouped[head, rows] = queries[0, :, begin : begin + HEAD_DIM]
    row = pl.ds(jnp.maximum(prompt_of(targets, lax.axis_index("tp")), 0), 1)
    cosine, sine = starts[0, row, :], starts[1, row, :]
    lane = lax.broadcasted_iota(jnp.int32, turns.shape[1:], 1)
    rotary[0] = turns[0] * cosine - turns[1] * sine
    sine = turns[1] * cosine + turns[0] * sine
    rotary[1] = jnp.where(lane < HEAD_DIM // 2, -sine, sine)


def prepare(targets, queries, starts, turns):
    return pl.pallas_call(
        prepare_kernel,
        in_specs=[SMEM] + [VMEM] * 3,
        out_specs=[VMEM] * 2,
        out_shape=[
            jax.ShapeDtypeStruct((KV_HEADS, ROWS, HEAD_DIM), BF16),
            jax.ShapeDtypeStruct(turns.shape, F32),
        ],
        compiler_params=pltpu.CompilerParams(vmem_limit_bytes=16 * MIB),
        name="prepare",
    )(targets, queries, starts, turns)


CACHE_HEADS = 2


def cache_kernel(targets, lengths, stored, q, keys, values, fresh_keys, fresh_values, out):
    scaling = HEAD_DIM ** (-0.5)
    dims = (((1,), (1,)), ((), ()))
    here = lax.axis_index("tp")
    rep = lax.axis_index("rep")
    length = keys.shape[1]
    span = stored[0]
    for prompt in range(targets.shape[0]):
        span = jnp.where(targets[prompt] == here, lengths[prompt] - STRETCH, span)
    place = lax.broadcasted_iota(jnp.int32, (ROWS, length), 1)
    allowed = place < span - rep * length
    second_step = lax.broadcasted_iota(jnp.int32, (ROWS, 1), 0) % STEPS == 1
    for at in range(CACHE_HEADS):
        lanes = slice(at * HEAD_DIM, (at + 1) * HEAD_DIM)
        query = q[at]
        wide = query.astype(F32)
        scores = lax.dot_general(query, keys[0, :, lanes], dims, preferred_element_type=F32)
        scores = jnp.where(allowed, scores * scaling, NEGATIVE)
        highest = jnp.max(scores, axis=1, keepdims=True)
        fresh = []
        for step in range(STEPS):
            key = fresh_keys[0, step : step + 1, lanes].astype(F32)
            score = jnp.sum(wide * key, axis=1, keepdims=True) * scaling
            shown = rep == 0 if step == 0 else second_step & (rep == 0)
            score = jnp.where(shown, score, NEGATIVE)
            highest = jnp.maximum(highest, score)
            fresh.append(score)
        some = highest > 0.5 * NEGATIVE
        highest = jnp.where(some, highest, 0.0)
        weight = jnp.exp(scores - highest)
        totals = jnp.sum(weight, axis=1, keepdims=True)
        sums = jnp.dot(weight.astype(BF16), values[0, :, lanes], preferred_element_type=F32)
        for step in range(STEPS):
            share = jnp.exp(fresh[step] - highest)
            totals += share
            value = fresh_values[0, step : step + 1, lanes].astype(F32)
            sums += share.astype(BF16).astype(F32) * value
        totals = jnp.where(some, totals, 1.0)
        out[at, :ROWS] = (sums / totals).astype(BF16)
        out[at, ROWS:] = pieces_tail(jnp.where(some, highest + jnp.log(totals), NEGATIVE))


def cache_attention(part, targets, lengths, stored, grouped, kv_cache, new_kv):
    length = kv_cache.shape[1]
    (kv_cache,) = in_hbm(kv_cache)
    width = CACHE_HEADS * HEAD_DIM
    blocks = KV_HEADS // CACHE_HEADS
    return pl.pallas_call(
        cache_kernel,
        grid=(2,),
        in_specs=[
            SMEM,
            SMEM,
            SMEM,
            pl.BlockSpec((CACHE_HEADS, ROWS, HEAD_DIM), lambda h: (2 * part + h, 0, 0)),
            pl.BlockSpec((1, length, width), lambda h: (0, 0, 2 * part + h)),
            pl.BlockSpec((1, length, width), lambda h: (0, 0, blocks + 2 * part + h)),
            pl.BlockSpec((1, STEPS, width), lambda h: (0, 0, 2 * part + h)),
            pl.BlockSpec((1, STEPS, width), lambda h: (0, 0, blocks + 2 * part + h)),
        ],
        out_specs=pl.BlockSpec((CACHE_HEADS, PART, HEAD_DIM), lambda h: (h, 0, 0)),
        out_shape=jax.ShapeDtypeStruct((2 * CACHE_HEADS, PART, HEAD_DIM), BF16),
        compiler_params=pltpu.CompilerParams(vmem_limit_bytes=24 * MIB),
        cost_estimate=pl.CostEstimate(
            flops=8 * CACHE_HEADS * ROWS * length * HEAD_DIM,
            bytes_accessed=2 * length * 2 * width * 2,
            transcendentals=2 * CACHE_HEADS * ROWS * length,
        ),
        name="cache_attention",
    )(targets, lengths, stored, grouped, kv_cache, kv_cache, new_kv, new_kv)


def final_kernel(
    targets, rotary, own_a, own_b, right_a, left_a, right_b, left_b, grouped, *refs
):
    cached, out = refs
    scaling = HEAD_DIM ** (-0.5)
    dims = (((1,), (1,)), ((), ()))
    mine = own_a.shape[0] - 1
    rep = lax.axis_index("rep")
    first = rep * CORE_HEADS
    prompt = prompt_of(targets, lax.axis_index("tp"))
    cosine, sine = rotary[0], rotary[1]
    rows = 4 * STRETCH
    squares = own_a[mine, rows:] + one_piece(right_a[rows:]) + one_piece(left_a[rows:])
    scale = token_column(lax.rsqrt(squares / D + EPSILON))
    for head in range(CORE_HEADS):
        own, right, left = ((own_a, right_a, left_a), (own_b, right_b, left_b))[head // 2]
        at = slice(head % 2 * STRETCH, (head % 2 + 1) * STRETCH)
        keys = own[mine, at] + right[at].astype(F32) + left[at].astype(F32)
        at = slice((2 + head % 2) * STRETCH, (3 + head % 2) * STRETCH)
        values = own[mine, at] + right[at].astype(F32) + left[at].astype(F32)
        keys = (keys * scale).astype(BF16).astype(F32)
        values = (values * scale).astype(BF16)
        keys = keys * cosine + pltpu.roll(keys, HEAD_DIM // 2, 1) * sine
        scores = lax.dot_general(
            grouped[first + head], keys.astype(BF16), dims, preferred_element_type=F32
        )
        scores = scores * scaling
        highest = jnp.max(scores, axis=1, keepdims=True)
        weight = jnp.exp(scores - highest)
        totals = jnp.sum(weight, axis=1, keepdims=True)
        sums = jnp.dot(weight.astype(BF16), values, preferred_element_type=F32) / totals
        logs = jnp.where(prompt >= 0, highest + jnp.log(totals), NEGATIVE)
        parts = [cached[0, first + head], cached[1, first + head]]
        logs = [tail_pieces(part[ROWS:]) for part in parts] + [logs]
        sums = [part[:ROWS].astype(F32) for part in parts] + [sums]
        highest = functools.reduce(jnp.maximum, logs)
        shares = [jnp.exp(log - highest) for log in logs]
        total = functools.reduce(jnp.add, shares)
        joined = functools.reduce(jnp.add, [share * part for share, part in zip(shares, sums)])
        result = (joined / total).astype(BF16)
        for member in range(GROUP):
            begin = (head * GROUP + member) * HEAD_DIM
            out[0, :, begin : begin + HEAD_DIM] = result[member * STEPS : (member + 1) * STEPS]


def finish(targets, rotary, own, arrived, grouped, cached):
    width = CORE_HEADS * GROUP * HEAD_DIM
    return pl.pallas_call(
        final_kernel,
        in_specs=[SMEM] + [VMEM] * 9,
        out_specs=VMEM,
        out_shape=jax.ShapeDtypeStruct((1, STEPS, width), BF16),
        compiler_params=pltpu.CompilerParams(vmem_limit_bytes=16 * MIB),
        name="finish",
    )(targets, rotary, *own, *arrived, grouped, cached)


def rotary_turns():
    half = np.arange(HEAD_DIM // 2, dtype=np.float64) / (HEAD_DIM // 2)
    frequency = ROTARY_BASE ** (-np.concatenate([half, half]))
    angles = np.arange(STRETCH, dtype=np.float64)[:, None] * frequency
    return frequency.astype(np.float32), np.stack([np.cos(angles), np.sin(angles)]).astype(np.float32)


def per_device(
    stretch,
    norm_gain,
    kv_codes,
    scale_codes,
    outer_scales,
    prompt_lengths,
    target_rows,
    cache_lengths,
    kv_cache,
    queries,
    new_kv,
):
    count = lax.axis_size("tp")
    half = count // 2
    lines = stretch.transpose(1, 0, 2)
    gain = norm_gain.reshape(1, -1)
    ring = [ring_device(at, count) for at in range(count)]
    to_right = [(ring[at], ring[(at + 1) % count]) for at in range(count)]
    to_left = [(ring[at], ring[at - 1]) for at in range(count)]

    def pass_on(right, left):
        return lax.ppermute(right, "tp", to_right), lax.ppermute(left, "tp", to_left)

    other = lax.ppermute(lines, "rep", [(0, 1), (1, 0)])
    first_half, own, squares = dequantize(0, lines, kv_codes, scale_codes, outer_scales.T, gain)
    (second_half,) = dequantize(1, lines, kv_codes, scale_codes, outer_scales.T, gain)
    frequency, turns = rotary_turns()
    start = (prompt_lengths - STRETCH).astype(F32)[:, None] * jnp.asarray(frequency)
    starts = jnp.stack([jnp.cos(start), jnp.sin(start)])
    targets, second_half = lax.optimization_barrier((target_rows, second_half))
    grouped, rotary = prepare(targets, queries, starts, jnp.asarray(turns))

    gain, second_half, grouped, rotary = lax.optimization_barrier(
        (gain, second_half, grouped, rotary)
    )
    distances = [half, half - 1, 1 - half]
    right, left, terms_a, lines_here, totals = project_first(
        distances, target_rows, own, squares, other, gain, first_half
    )
    arrived = [pass_on(right, left), None]
    right, left, terms_b = project_second(distances, lines_here, totals, second_half)
    arrived[1] = pass_on(right, left)
    terms = [terms_a, terms_b]

    targets = target_rows
    cached = []
    for distance in range(half - 1, 0, -1):
        if distance < half - 1:
            distances = [distance, -distance] + ([0] if distance == 1 else [])
            terms = list(
                project(distances, targets, own, squares, other, gain, [first_half, second_half])
            )
        for part in range(2):
            right, left = sends(part, distance == half - 1, terms[part], *arrived[part])
            if part == 0:
                right, cached, terms[1] = lax.optimization_barrier((right, cached, terms[1]))
            targets, _ = lax.optimization_barrier((target_rows, right))
            arrived[part] = pass_on(right, left)
        if distance in (2, 3):
            cached.append(
                cache_attention(
                    3 - distance, targets, prompt_lengths, cache_lengths, grouped, kv_cache, new_kv
                )
            )

    cached, _ = lax.optimization_barrier((cached, right))
    cached = lax.all_gather(jnp.concatenate(cached), "rep")
    out = finish(target_rows, rotary, terms, [*arrived[0], *arrived[1]], grouped, cached)
    return lax.all_gather(out, "rep", axis=2, tiled=True)


def solution(mesh):
    in_specs = (
        P(None, ("grp", "rep"), "tp"),
        P("tp"),
        P("tp", None),
        P("tp", None),
        P("tp", None),
        P("grp"),
        P("grp"),
        P(("grp", "tp")),
        P(("grp", "tp"), "rep", None),
        P(("grp", "tp"), None, None),
        P(("grp", "tp"), None, None),
    )
    out_specs = P(("grp", "tp"), None, None)
    return jax.shard_map(
        per_device, mesh=mesh, in_specs=in_specs, out_specs=out_specs, check_vma=False
    )
```

time: 63.7 us -> 61.9 us (0.972)
  Pallas kernels: 33.8 us -> 32 us
  local copies, waits for them, and re-layouts: 1.5 us -> 0.66 us
  waiting for transfers between devices: 5.12 us -> 5.92 us
    ppermute x8, starting transfers between devices: 6.61 us -> 16.7 us  [pass_on(): lax.ppermute(right, 'tp', to_right)]
    ppermute x8, starting transfers between devices: 10.9 us -> 1.12 us  [pass_on(): lax.ppermute(left, 'tp', to_left)]
    ppermute x8, waiting for transfers between devices: 0.34 us -> 4.22 us  [pass_on(): lax.ppermute(left, 'tp', to_left)]
    ppermute x8, waiting for transfers between devices: 4.77 us -> 1.7 us  [pass_on(): lax.ppermute(right, 'tp', to_right)]
    pallas_call x6, Pallas kernels: 1.81 us -> 0.5 us  [sends(): pl.pallas_call(functools.partial(send_kernel, half, first), in_specs=[VME...]
    unnamed x15, local copies, waits for them, and re-layouts: 1.5 us -> 0.66 us
  transfers between devices with their start and end apart: 17 -> 17, of which waited for: 5 -> 4; matrix products, arithmetic and copies ran while one was open for 0% -> 0% of each run, Pallas kernels for 48% -> 45%
where the time goes in v5:
time: 61.9 us; the launch traced here: 61.7 us
  Pallas kernels  32 us (52%)
  starting transfers between devices  18.3 us (30%)
  waiting for transfers between devices  5.92 us (10%)
  blocking collectives  3.8 us (6%)
  between operations  0.89 us (1%)
  local copies, waits for them, and re-layouts  0.66 us (1%)
    ppermute x8, starting transfers between devices, pass_on(): lax.ppermute(right, 'tp', to_right)  16.7 us
    pallas_call x2, Pallas kernels, dequantize(): pl.pallas_call(functools.partial(weights_kernel, half), grid=(2, blocks),...  12.9 us
    pallas_call x2, Pallas kernels, project(): pl.pallas_call(functools.partial(project_kernel, distances), in_specs=[SM...  6.52 us
    pallas_call x2, Pallas kernels, cache_attention(): pl.pallas_call(cache_kernel, grid=(2,), in_specs=[SMEM, SMEM, SMEM, pl.Bl...  5.58 us
    ppermute x8, waiting for transfers between devices, pass_on(): lax.ppermute(left, 'tp', to_left)  4.22 us
    pallas_call x1, Pallas kernels, project_first(): pl.pallas_call(functools.partial(first_kernel, distances), in_specs=[SMEM...  2.49 us
    pallas_call x1, Pallas kernels, finish(): pl.pallas_call(final_kernel, in_specs=[SMEM] + [VMEM] * 9, out_specs=VMEM...  1.98 us
    all_gather x1, blocking collectives, per_device(): cached = lax.all_gather(jnp.concatenate(cached), 'rep')  1.95 us
  transfers between devices with their start and end apart: 17, of which 4 were waited for; matrix products, arithmetic and copies ran while one was open for 0% of the time, Pallas kernels for 45%

profile of v5, /device:TPU:0, one launch (start us, length us, event | category | flops | bytes accessed | tf_op | source)
XLA Modules:
  0.0 61.7 jit_solution(15587509060522919096)
XLA Ops:
  0.0 0.5 collective-permute-start
  0.5 5.7 %dequantize.2.weight.weight_b = bf16[2,2048,256]{2,1,0:T(8,128)(2,1)S(1)} custom-call(s32[2048,2048]{1,0:T(8,128)} %value_codes.3, s32[2048,2048]{1,0:T(8,128)} %value_codes.3, s32[32,2048]{1,0:T(8,128)} %value_scales.3, s32[32,2048]{1,0:T(8,128)} %value_scales.3, f32[8,32]{1,0:T(8,128)} %bitcast.11), custom_call_target="tpu_custom_call" | custom-call | flops 67108864 | bytes 4194304 | tf_op jit(solution)/shard_map/dequantize/pallas_call | solution.py:232
  6.2 0.1 multiply_cosine_fusion
  6.4 0.7 %prepare.1 = (bf16[8,32,128]{2,1,0:T(8,128)(2,1)S(1)}, f32[2,192,128]{2,1,0:T(8,128)S(1)}) custom-call(s32[6]{0:T(128)S(1)} %copy-done.4, bf16[1,2,16384]{2,1,0:T(2,128)(2,1)S(1)} %copy-done.3, f32[2,6,128]{2,1,0:T(8,128)S(1)} %pad_maximum_fusion.1.starts, f32[2,192,128]{2,1,0:T(8,128)S(1)} %copy-done), custom_call_target="tpu_custom_call" | custom-call | tf_op jit(solution)/shard_map/prepare/pallas_call | solution.py:436
  7.1 0.0 copy-start.2
  7.1 7.1 %dequantize.3 = (bf16[2,2048,256]{2,1,0:T(8,128)(2,1)S(1)}, bf16[3,192,2048]{2,1,0:T(8,128)(2,1)S(1)}, f32[3,8,128]{2,1,0:T(8,128)S(1)}) custom-call(s32[2048,2048]{1,0:T(8,128)} %value_codes.3, s32[2048,2048]{1,0:T(8,128)} %value_codes.3, s32[32,2048]{1,0:T(8,128)} %value_scales.3, s32[32,2048]{1,0:T(8,128)} %value_scales.3, f32[8,32]{1,0:T(8,128)} %bitcast.12, ...), custom_call_target="tpu_custom_call" | custom-call | flops 67108864 | bytes 4194304 | tf_op jit(solution)/shard_map/dequantize/pallas_call | solution.py:232
  14.2 0.0 collective-permute-done.other
  14.3 2.5 %project_first.1 = (bf16[400,128]{1,0:T(8,128)(2,1)S(1)}, bf16[384,128]{1,0:T(8,128)(2,1)S(1)}, f32[2,776,128]{2,1,0:T(8,128)S(1)}, bf16[576,2048]{1,0:T(8,128)(2,1)S(1)}, f32[3,8,128]{2,1,0:T(8,128)S(1)}) custom-call(s32[6]{0:T(128)S(1)} %copy-done.4, bf16[3,192,2048]{2,1,0:T(8,128)(2,1)S(1)} %get-tuple-element.58.own, ...), custom_call_target="tpu_custom_call" | custom-call | flops 1207959552 | bytes 1048576 | tf_op jit(solution)/shard_map/project_first/pallas_call | solution.py:331
  16.8 2.6 %collective-permute-start.1 = (bf16[400,128]{1,0:T(8,128)(2,1)S(1)}, bf16[400,128]{1,0:T(8,128)(2,1)S(1)}, u32[]{:S(2)}, u32[]{:S(2)}) collective-permute-start(bf16[400,128]{1,0:T(8,128)(2,1)S(1)} %get-tuple-element.63), channel_id=1, source_target_pairs={{0,4},{4,8},{8,12},{12,14},{14,10},{10,6},{6,2},{2,0},{1,5},{5,9},... | collective-permute-start | bytes 307208 | tf_op jit(solution)/shard_map/ppermute | solution.py:610
  19.4 0.0 collective-permute-start.2
  19.4 1.4 %project_second.1 = (bf16[400,128]{1,0:T(8,128)(2,1)S(1)}, bf16[384,128]{1,0:T(8,128)(2,1)S(1)}, f32[2,776,128]{2,1,0:T(8,128)S(1)}) custom-call(bf16[576,2048]{1,0:T(8,128)(2,1)S(1)} %get-tuple-element.66.lines, f32[3,8,128]{2,1,0:T(8,128)S(1)} %get-tuple-element.67.totals, bf16[2,2048,256]{2,1,0:T(8,128)(2,1)S(1)} %dequantize.2.weight.weight_b), custom_call_target="tpu_custom_call" | custom-call | flops 1207959552 | bytes 1048576 | tf_op jit(solution)/shard_map/project_second/pallas_call | solution.py:343
  20.8 2.1 %collective-permute-start.3 = (bf16[400,128]{1,0:T(8,128)(2,1)S(1)}, bf16[400,128]{1,0:T(8,128)(2,1)S(1)}, u32[]{:S(2)}, u32[]{:S(2)}) collective-permute-start(bf16[400,128]{1,0:T(8,128)(2,1)S(1)} %get-tuple-element.71), channel_id=1, source_target_pairs={{0,4},{4,8},{8,12},{12,14},{14,10},{10,6},{6,2},{2,0},{1,5},{5,9},... | collective-permute-start | bytes 307208 | tf_op jit(solution)/shard_map/ppermute | solution.py:610
  22.9 0.0 collective-permute-start.4
  22.9 1.5 %collective-permute-done.2.left = bf16[384,128]{1,0:T(8,128)(2,1)S(1)} collective-permute-done((bf16[384,128]{1,0:T(8,128)(2,1)S(1)}, bf16[384,128]{1,0:T(8,128)(2,1)S(1)}, u32[]{:S(2)}, u32[]{:S(2)}) %collective-permute-start.2) | collective-permute-done | bytes 98336 | tf_op jit(solution)/shard_map/ppermute | solution.py:610
  24.4 0.0 collective-permute-done.1.right
  24.4 0.1 sends.6
  24.4 1.6 %collective-permute-start.5 = (bf16[784,128]{1,0:T(8,128)(2,1)S(1)}, bf16[784,128]{1,0:T(8,128)(2,1)S(1)}, u32[]{:S(2)}, u32[]{:S(2)}) collective-permute-start(bf16[784,128]{1,0:T(8,128)(2,1)S(1)} %get-tuple-element.76), channel_id=1, source_target_pairs={{0,4},{4,8},{8,12},{12,14},{14,10},{10,6},{6,2},{2,0},{1,5},{5,9},... | collective-permute-start | bytes 602120 | tf_op jit(solution)/shard_map/ppermute | solution.py:610
  26.1 0.5 collective-permute-start.6
  26.5 1.0 %collective-permute-done.4.left = bf16[384,128]{1,0:T(8,128)(2,1)S(1)} collective-permute-done((bf16[384,128]{1,0:T(8,128)(2,1)S(1)}, bf16[384,128]{1,0:T(8,128)(2,1)S(1)}, u32[]{:S(2)}, u32[]{:S(2)}) %collective-permute-start.4) | collective-permute-done | bytes 98336 | tf_op jit(solution)/shard_map/ppermute | solution.py:610
  27.5 0.1 sends.7
  27.5 2.0 %collective-permute-start.7 = (bf16[768,128]{1,0:T(8,128)(2,1)S(1)}, bf16[768,128]{1,0:T(8,128)(2,1)S(1)}, u32[]{:S(2)}, u32[]{:S(2)}) collective-permute-start(bf16[768,128]{1,0:T(8,128)(2,1)S(1)} %get-tuple-element.73), channel_id=1, source_target_pairs={{0,4},{4,8},{8,12},{12,14},{14,10},{10,6},{6,2},{2,0},{1,5},{5,9},... | collective-permute-start | bytes 589832 | tf_op jit(solution)/shard_map/ppermute | solution.py:610
  29.5 0.1 collective-permute-start.8
  30.3 2.8 %cache_attention.2 = bf16[4,48,128]{2,1,0:T(8,128)(2,1)S(1)} custom-call(s32[6]{0:T(128)S(1)} %copy-done.4, s32[6]{0:T(128)S(1)} %copy-done.5, s32[1]{0:T(128)S(6)} %copy.15.stored, bf16[8,32,128]{2,1,0:T(8,128)(2,1)S(1)} %get-tuple-element.79.q.grouped, bf16[1,1024,2048]{2,1,0:T(8,128)(2,1)} %values.3, bf16[1,1024,2048]{2,1,0:T(8,128)(2,1)} %values.3, ...), custom_call_target="tpu_custom_call" | custom-call | flops 67108864 | bytes 2097152 | tf_op jit(solution)/shard_map/cache_attention/pallas_call | solution.py:499
  33.1 2.5 %project.2 = (f32[2,776,128]{2,1,0:T(8,128)S(1)}, f32[2,776,128]{2,1,0:T(8,128)S(1)}) custom-call(s32[6]{0:T(128)S(1)} %copy-done.4, bf16[3,192,2048]{2,1,0:T(8,128)(2,1)S(1)} %get-tuple-element.58.own, f32[3,8,128]{2,1,0:T(8,128)S(1)} %get-tuple-element.59.squares, bf16[3,192,2048]{2,1,0:T(8,128)(2,1)S(1)} %collective-permute-done.other, ...), custom_call_target="tpu_custom_call" | custom-call | flops 805306368 | bytes 1048576 | tf_op jit(solution)/shard_map/project/pallas_call | solution.py:376
  35.7 0.0 collective-permute-done.6.left
  35.7 0.1 sends.8
  35.8 2.5 %collective-permute-start.9 = (bf16[784,128]{1,0:T(8,128)(2,1)S(1)}, bf16[784,128]{1,0:T(8,128)(2,1)S(1)}, u32[]{:S(2)}, u32[]{:S(2)}) collective-permute-start(bf16[784,128]{1,0:T(8,128)(2,1)S(1)} %get-tuple-element.86), channel_id=1, source_target_pairs={{0,4},{4,8},{8,12},{12,14},{14,10},{10,6},{6,2},{2,0},{1,5},{5,9},... | collective-permute-start | bytes 602120 | tf_op jit(solution)/shard_map/ppermute | solution.py:610
  38.2 0.0 collective-permute-start.10
  38.3 0.1 sends.9
  38.4 2.3 %collective-permute-start.13 = (bf16[768,128]{1,0:T(8,128)(2,1)S(1)}, bf16[768,128]{1,0:T(8,128)(2,1)S(1)}, u32[]{:S(2)}, u32[]{:S(2)}) collective-permute-start(bf16[768,128]{1,0:T(8,128)(2,1)S(1)} %get-tuple-element.83), channel_id=1, source_target_pairs={{0,4},{4,8},{8,12},{12,14},{14,10},{10,6},{6,2},{2,0},{1,5},{5,9},... | collective-permute-start | bytes 589832 | tf_op jit(solution)/shard_map/ppermute | solution.py:610
  40.7 0.0 collective-permute-start.14
  40.7 2.8 %cache_attention.3 = bf16[4,48,128]{2,1,0:T(8,128)(2,1)S(1)} custom-call(s32[6]{0:T(128)S(1)} %copy-done.4, s32[6]{0:T(128)S(1)} %copy-done.5, s32[1]{0:T(128)S(6)} %copy.15.stored, bf16[8,32,128]{2,1,0:T(8,128)(2,1)S(1)} %get-tuple-element.79.q.grouped, bf16[1,1024,2048]{2,1,0:T(8,128)(2,1)} %values.3, bf16[1,1024,2048]{2,1,0:T(8,128)(2,1)} %values.3, ...), custom_call_target="tpu_custom_call" | custom-call | flops 67108864 | bytes 2097152 | tf_op jit(solution)/shard_map/cache_attention/pallas_call | solution.py:499
  43.5 4.0 %project.3 = (f32[3,776,128]{2,1,0:T(8,128)S(1)}, f32[3,776,128]{2,1,0:T(8,128)S(1)}) custom-call(s32[6]{0:T(128)S(1)} %copy-done.4, bf16[3,192,2048]{2,1,0:T(8,128)(2,1)S(1)} %get-tuple-element.58.own, f32[3,8,128]{2,1,0:T(8,128)S(1)} %get-tuple-element.59.squares, bf16[3,192,2048]{2,1,0:T(8,128)(2,1)S(1)} %collective-permute-done.other, ...), custom_call_target="tpu_custom_call" | custom-call | flops 1207959552 | bytes 1048576 | tf_op jit(solution)/shard_map/project/pallas_call | solution.py:376
  47.5 0.0 collective-permute-done.9.right
  47.5 0.1 sends.10
  47.6 1.8 %collective-permute-start.11 = (bf16[784,128]{1,0:T(8,128)(2,1)S(1)}, bf16[784,128]{1,0:T(8,128)(2,1)S(1)}, u32[]{:S(2)}, u32[]{:S(2)}) collective-permute-start(bf16[784,128]{1,0:T(8,128)(2,1)S(1)} %get-tuple-element.92), channel_id=1, source_target_pairs={{0,4},{4,8},{8,12},{12,14},{14,10},{10,6},{6,2},{2,0},{1,5},{5,9},... | collective-permute-start | bytes 602120 | tf_op jit(solution)/shard_map/ppermute | solution.py:610
  49.4 0.3 collective-permute-start.12
  49.7 0.1 sends.11
  49.8 1.8 %collective-permute-start.15 = (bf16[768,128]{1,0:T(8,128)(2,1)S(1)}, bf16[768,128]{1,0:T(8,128)(2,1)S(1)}, u32[]{:S(2)}, u32[]{:S(2)}) collective-permute-start(bf16[768,128]{1,0:T(8,128)(2,1)S(1)} %get-tuple-element.95), channel_id=1, source_target_pairs={{0,4},{4,8},{8,12},{12,14},{14,10},{10,6},{6,2},{2,0},{1,5},{5,9},... | collective-permute-start | bytes 589832 | tf_op jit(solution)/shard_map/ppermute | solution.py:610
  51.6 0.3 collective-permute-start.16
  51.9 1.9 %all-gather = bf16[16,48,128]{2,1,0:T(8,128)(2,1)S(1)} all-gather(bf16[8,48,128]{2,1,0:T(8,128)(2,1)S(1)} %pad_maximum_fusion), channel_id=2, replica_groups=mesh['grp'=2,'tp'=8,'rep'=2] {'rep'}, dimensions={0}, use_global_device_ids=true | all-gather | bytes 294912 | tf_op jit(solution)/shard_map/all_gather | solution.py:655
  53.8 1.7 %collective-permute-done.15.right_b = bf16[768,128]{1,0:T(8,128)(2,1)S(1)} collective-permute-done((bf16[768,128]{1,0:T(8,128)(2,1)S(1)}, bf16[768,128]{1,0:T(8,128)(2,1)S(1)}, u32[]{:S(2)}, u32[]{:S(2)}) %collective-permute-start.15) | collective-permute-done | bytes 196640 | tf_op jit(solution)/shard_map/ppermute | solution.py:610
  55.5 1.7 %collective-permute-done.16.left_b = bf16[768,128]{1,0:T(8,128)(2,1)S(1)} collective-permute-done((bf16[768,128]{1,0:T(8,128)(2,1)S(1)}, bf16[768,128]{1,0:T(8,128)(2,1)S(1)}, u32[]{:S(2)}, u32[]{:S(2)}) %collective-permute-start.16) | collective-permute-done | bytes 196640 | tf_op jit(solution)/shard_map/ppermute | solution.py:610
  57.2 0.0 collective-permute-done.11.right_a
  57.2 0.0 collective-permute-done.12.left_a
  57.2 2.0 %finish.1 = bf16[1,2,8192]{2,1,0:T(2,128)(2,1)S(1)} custom-call(s32[6]{0:T(128)S(1)} %copy-done.4, f32[2,192,128]{2,1,0:T(8,128)S(1)} %get-tuple-element.57.rotary, f32[3,776,128]{2,1,0:T(8,128)S(1)} %get-tuple-element.85.terms.own_a, f32[3,776,128]{2,1,0:T(8,128)S(1)} %get-tuple-element.91.terms.own_b, ...), custom_call_target="tpu_custom_call" | custom-call | tf_op jit(solution)/shard_map/finish/pallas_call | solution.py:571
  59.2 1.9 %all_gather.11 = bf16[1,2,16384]{2,1,0:T(2,128)(2,1)S(1)} all-gather(bf16[1,2,8192]{2,1,0:T(2,128)(2,1)S(1)} %finish.1), channel_id=1, replica_groups=mesh['grp'=2,'tp'=8,'rep'=2] {'rep'}, dimensions={2}, use_global_device_ids=true | all-gather | bytes 98304 | tf_op jit(solution)/shard_map/all_gather | solution.py:657
  61.1 0.6 %copy.16 = bf16[1,2,16384]{2,1,0:T(2,128)(2,1)} copy(bf16[1,2,16384]{2,1,0:T(2,128)(2,1)S(1)} %all_gather.11) | data formatting | bytes 131072
  (23 shorter events, 0.1 us)
Async XLA Ops:
  0.0 14.2 %collective-permute-start = (bf16[3,192,2048]{2,1,0:T(8,128)(2,1)}, bf16[3,192,2048]{2,1,0:T(8,128)(2,1)S(1)}, u32[]{:S(2)}, u32[]{:S(2)}) collective-permute-start(bf16[3,192,2048]{2,1,0:T(8,128)(2,1)} %bitcast.9), channel_id=1, source_target_pairs={{0,1},{1,0},{2,3},{3,2},{4,5},{5,4},{6,7},{7,6},{8,9},{9,8},{10,11... | collective-permute-start | bytes 7077896 | tf_op jit(solution)/shard_map/ppermute | solution.py:612
  0.5 5.8 %copy-start.5 = (s32[6]{0:T(128)S(1)}, s32[6]{0:T(128)}, u32[]{:S(2)}) copy-start(s32[6]{0:T(128)} %lengths.3) | copy-start | bytes 76
  0.5 5.8 %copy-start.6 = (f32[128]{0:T(128)S(1)}, f32[128]{0:T(128)}, u32[]{:S(2)}) copy-start(f32[128]{0:T(128)} %constant.7.clone) | copy-start | bytes 1540
  0.5 5.9 %copy-start = (f32[2,192,128]{2,1,0:T(8,128)S(1)}, f32[2,192,128]{2,1,0:T(8,128)}, u32[]{:S(2)}) copy-start(f32[2,192,128]{2,1,0:T(8,128)} %constant.8.clone.turns) | copy-start | bytes 589828
  0.5 5.9 %copy-start.3 = (bf16[1,2,16384]{2,1,0:T(2,128)(2,1)S(1)}, bf16[1,2,16384]{2,1,0:T(2,128)(2,1)}, u32[]{:S(2)}) copy-start(bf16[1,2,16384]{2,1,0:T(2,128)(2,1)} %queries.1) | copy-start | bytes 196612
  0.5 5.9 %copy-start.4 = (s32[6]{0:T(128)S(1)}, s32[6]{0:T(128)}, u32[]{:S(2)}) copy-start(s32[6]{0:T(128)} %targets.8) | copy-start | bytes 76
  7.1 7.2 %copy-start.2 = (f32[2048]{0:T(1024)S(1)}, f32[2048]{0:T(1024)}, u32[]{:S(2)}) copy-start(f32[2048]{0:T(1024)} %param.14) | copy-start | bytes 24580
  16.8 7.6 %collective-permute-start.1 = (bf16[400,128]{1,0:T(8,128)(2,1)S(1)}, bf16[400,128]{1,0:T(8,128)(2,1)S(1)}, u32[]{:S(2)}, u32[]{:S(2)}) collective-permute-start(bf16[400,128]{1,0:T(8,128)(2,1)S(1)} %get-tuple-element.63), channel_id=1, source_target_pairs={{0,4},{4,8},{8,12},{12,14},{14,10},{10,6},{6,2},{2,0},{1,5},{5,9},... | collective-permute-start | bytes 307208 | tf_op jit(solution)/shard_map/ppermute | solution.py:610
  19.4 5.0 %collective-permute-start.2 = (bf16[384,128]{1,0:T(8,128)(2,1)S(1)}, bf16[384,128]{1,0:T(8,128)(2,1)S(1)}, u32[]{:S(2)}, u32[]{:S(2)}) collective-permute-start(bf16[384,128]{1,0:T(8,128)(2,1)S(1)} %get-tuple-element.64), channel_id=1, source_target_pairs={{0,2},{4,0},{8,4},{12,8},{14,12},{10,14},{6,10},{2,6},{1,3},{5,1},... | collective-permute-start | bytes 294920 | tf_op jit(solution)/shard_map/ppermute | solution.py:610
  19.4 10.9 %copy-start.1 = (bf16[1,2,2048]{2,1,0:T(2,128)(2,1)S(1)}, bf16[1,2,2048]{2,1,0:T(2,128)(2,1)}, u32[]{:S(2)}) copy-start(bf16[1,2,2048]{2,1,0:T(2,128)(2,1)} %fresh_values.3) | copy-start | bytes 24580
  20.8 6.7 %collective-permute-start.3 = (bf16[400,128]{1,0:T(8,128)(2,1)S(1)}, bf16[400,128]{1,0:T(8,128)(2,1)S(1)}, u32[]{:S(2)}, u32[]{:S(2)}) collective-permute-start(bf16[400,128]{1,0:T(8,128)(2,1)S(1)} %get-tuple-element.71), channel_id=1, source_target_pairs={{0,4},{4,8},{8,12},{12,14},{14,10},{10,6},{6,2},{2,0},{1,5},{5,9},... | collective-permute-start | bytes 307208 | tf_op jit(solution)/shard_map/ppermute | solution.py:610
  22.9 4.6 %collective-permute-start.4 = (bf16[384,128]{1,0:T(8,128)(2,1)S(1)}, bf16[384,128]{1,0:T(8,128)(2,1)S(1)}, u32[]{:S(2)}, u32[]{:S(2)}) collective-permute-start(bf16[384,128]{1,0:T(8,128)(2,1)S(1)} %get-tuple-element.72), channel_id=1, source_target_pairs={{0,2},{4,0},{8,4},{12,8},{14,12},{10,14},{6,10},{2,6},{1,3},{5,1},... | collective-permute-start | bytes 294920 | tf_op jit(solution)/shard_map/ppermute | solution.py:610
  24.4 11.2 %collective-permute-start.5 = (bf16[784,128]{1,0:T(8,128)(2,1)S(1)}, bf16[784,128]{1,0:T(8,128)(2,1)S(1)}, u32[]{:S(2)}, u32[]{:S(2)}) collective-permute-start(bf16[784,128]{1,0:T(8,128)(2,1)S(1)} %get-tuple-element.76), channel_id=1, source_target_pairs={{0,4},{4,8},{8,12},{12,14},{14,10},{10,6},{6,2},{2,0},{1,5},{5,9},... | collective-permute-start | bytes 602120 | tf_op jit(solution)/shard_map/ppermute | solution.py:610
  26.1 9.6 %collective-permute-start.6 = (bf16[784,128]{1,0:T(8,128)(2,1)S(1)}, bf16[784,128]{1,0:T(8,128)(2,1)S(1)}, u32[]{:S(2)}, u32[]{:S(2)}) collective-permute-start(bf16[784,128]{1,0:T(8,128)(2,1)S(1)} %get-tuple-element.77), channel_id=1, source_target_pairs={{0,2},{4,0},{8,4},{12,8},{14,12},{10,14},{6,10},{2,6},{1,3},{5,1},... | collective-permute-start | bytes 602120 | tf_op jit(solution)/shard_map/ppermute | solution.py:610
  27.5 10.7 %collective-permute-start.7 = (bf16[768,128]{1,0:T(8,128)(2,1)S(1)}, bf16[768,128]{1,0:T(8,128)(2,1)S(1)}, u32[]{:S(2)}, u32[]{:S(2)}) collective-permute-start(bf16[768,128]{1,0:T(8,128)(2,1)S(1)} %get-tuple-element.73), channel_id=1, source_target_pairs={{0,4},{4,8},{8,12},{12,14},{14,10},{10,6},{6,2},{2,0},{1,5},{5,9},... | collective-permute-start | bytes 589832 | tf_op jit(solution)/shard_map/ppermute | solution.py:610
  29.5 8.7 %collective-permute-start.8 = (bf16[768,128]{1,0:T(8,128)(2,1)S(1)}, bf16[768,128]{1,0:T(8,128)(2,1)S(1)}, u32[]{:S(2)}, u32[]{:S(2)}) collective-permute-start(bf16[768,128]{1,0:T(8,128)(2,1)S(1)} %get-tuple-element.82), channel_id=1, source_target_pairs={{0,2},{4,0},{8,4},{12,8},{14,12},{10,14},{6,10},{2,6},{1,3},{5,1},... | collective-permute-start | bytes 589832 | tf_op jit(solution)/shard_map/ppermute | solution.py:610
  35.8 11.7 %collective-permute-start.9 = (bf16[784,128]{1,0:T(8,128)(2,1)S(1)}, bf16[784,128]{1,0:T(8,128)(2,1)S(1)}, u32[]{:S(2)}, u32[]{:S(2)}) collective-permute-start(bf16[784,128]{1,0:T(8,128)(2,1)S(1)} %get-tuple-element.86), channel_id=1, source_target_pairs={{0,4},{4,8},{8,12},{12,14},{14,10},{10,6},{6,2},{2,0},{1,5},{5,9},... | collective-permute-start | bytes 602120 | tf_op jit(solution)/shard_map/ppermute | solution.py:610
  38.2 9.2 %collective-permute-start.10 = (bf16[784,128]{1,0:T(8,128)(2,1)S(1)}, bf16[784,128]{1,0:T(8,128)(2,1)S(1)}, u32[]{:S(2)}, u32[]{:S(2)}) collective-permute-start(bf16[784,128]{1,0:T(8,128)(2,1)S(1)} %get-tuple-element.87), channel_id=1, source_target_pairs={{0,2},{4,0},{8,4},{12,8},{14,12},{10,14},{6,10},{2,6},{1,3},{5,1},... | collective-permute-start | bytes 602120 | tf_op jit(solution)/shard_map/ppermute | solution.py:610
  38.4 11.3 %collective-permute-start.13 = (bf16[768,128]{1,0:T(8,128)(2,1)S(1)}, bf16[768,128]{1,0:T(8,128)(2,1)S(1)}, u32[]{:S(2)}, u32[]{:S(2)}) collective-permute-start(bf16[768,128]{1,0:T(8,128)(2,1)S(1)} %get-tuple-element.83), channel_id=1, source_target_pairs={{0,4},{4,8},{8,12},{12,14},{14,10},{10,6},{6,2},{2,0},{1,5},{5,9},... | collective-permute-start | bytes 589832 | tf_op jit(solution)/shard_map/ppermute | solution.py:610
  40.7 9.0 %collective-permute-start.14 = (bf16[768,128]{1,0:T(8,128)(2,1)S(1)}, bf16[768,128]{1,0:T(8,128)(2,1)S(1)}, u32[]{:S(2)}, u32[]{:S(2)}) collective-permute-start(bf16[768,128]{1,0:T(8,128)(2,1)S(1)} %get-tuple-element.94), channel_id=1, source_target_pairs={{0,2},{4,0},{8,4},{12,8},{14,12},{10,14},{6,10},{2,6},{1,3},{5,1},... | collective-permute-start | bytes 589832 | tf_op jit(solution)/shard_map/ppermute | solution.py:610
  47.6 9.6 %collective-permute-start.11 = (bf16[784,128]{1,0:T(8,128)(2,1)S(1)}, bf16[784,128]{1,0:T(8,128)(2,1)S(1)}, u32[]{:S(2)}, u32[]{:S(2)}) collective-permute-start(bf16[784,128]{1,0:T(8,128)(2,1)S(1)} %get-tuple-element.92), channel_id=1, source_target_pairs={{0,4},{4,8},{8,12},{12,14},{14,10},{10,6},{6,2},{2,0},{1,5},{5,9},... | collective-permute-start | bytes 602120 | tf_op jit(solution)/shard_map/ppermute | solution.py:610
  49.4 7.8 %collective-permute-start.12 = (bf16[784,128]{1,0:T(8,128)(2,1)S(1)}, bf16[784,128]{1,0:T(8,128)(2,1)S(1)}, u32[]{:S(2)}, u32[]{:S(2)}) collective-permute-start(bf16[784,128]{1,0:T(8,128)(2,1)S(1)} %get-tuple-element.93), channel_id=1, source_target_pairs={{0,2},{4,0},{8,4},{12,8},{14,12},{10,14},{6,10},{2,6},{1,3},{5,1},... | collective-permute-start | bytes 602120 | tf_op jit(solution)/shard_map/ppermute | solution.py:610
  49.8 5.7 %collective-permute-start.15 = (bf16[768,128]{1,0:T(8,128)(2,1)S(1)}, bf16[768,128]{1,0:T(8,128)(2,1)S(1)}, u32[]{:S(2)}, u32[]{:S(2)}) collective-permute-start(bf16[768,128]{1,0:T(8,128)(2,1)S(1)} %get-tuple-element.95), channel_id=1, source_target_pairs={{0,4},{4,8},{8,12},{12,14},{14,10},{10,6},{6,2},{2,0},{1,5},{5,9},... | collective-permute-start | bytes 589832 | tf_op jit(solution)/shard_map/ppermute | solution.py:610
  51.6 5.7 %collective-permute-start.16 = (bf16[768,128]{1,0:T(8,128)(2,1)S(1)}, bf16[768,128]{1,0:T(8,128)(2,1)S(1)}, u32[]{:S(2)}, u32[]{:S(2)}) collective-permute-start(bf16[768,128]{1,0:T(8,128)(2,1)S(1)} %get-tuple-element.96), channel_id=1, source_target_pairs={{0,2},{4,0},{8,4},{12,8},{14,12},{10,14},{6,10},{2,6},{1,3},{5,1},... | collective-permute-start | bytes 589832 | tf_op jit(solution)/shard_map/ppermute | solution.py:610

commit v6 on v5

--- a/solution.py
+++ b/solution.py
@@ -140,108 +140,94 @@
 
 
 def weights_kernel(
-    half, key_codes, value_codes, key_scales, value_scales, outer, *refs
+    x, key_codes, value_codes, key_scales, value_scales, outer, gain,
+    out_a, out_b, scaled, squares, scales,
 ):
-    if half == 0:
-        x, gain, out, scaled, squares, scales = refs
-    else:
-        out, scales = refs
-    item, block = pl.program_id(0), pl.program_id(1)
+    block = pl.program_id(0)
     depth = key_codes.shape[0]
-    head = lax.axis_index("rep") * CORE_HEADS + 2 * half + item
     columns = outer.shape[0] // 2
-    column = head // (KV_HEADS // columns)
 
     @pl.when(block == 0)
     def _():
-        scales[0] = block_scales(key_scales[...], outer[...], column)
-        scales[1] = block_scales(value_scales[...], outer[...], columns + column)
+        squares[...] = jnp.zeros(squares.shape, F32)
+        for at in range(CORE_HEADS):
+            head = lax.axis_index("rep") * CORE_HEADS + at
+            column = head // (KV_HEADS // columns)
+            lanes = slice(at * HEAD_DIM, (at + 1) * HEAD_DIM)
+            scales[2 * at] = block_scales(key_scales[:, lanes], outer[...], column)
+            scales[2 * at + 1] = block_scales(value_scales[:, lanes], outer[...], columns + column)
 
     lane = lax.broadcasted_iota(jnp.int32, (8, 128), 1)
     table = jnp.zeros((8, 128), F32)
     for code, level in enumerate(NORMAL_FLOAT_LEVELS):
         table = jnp.where(lane == code, level, table)
-    together = 4
 
     def body(step, _):
-        begins = [
-            pl.multiple_of((step * together + at) * QBLOCK, QBLOCK) for at in range(together)
-        ]
-        codes = [
-            (key_codes[pl.ds(begin, QBLOCK), :], value_codes[pl.ds(begin, QBLOCK), :])
-            for begin in begins
-        ]
+        begin = pl.multiple_of(step * QBLOCK, QBLOCK)
+        codes = []
+        for at in range(CORE_HEADS):
+            lanes = slice(at * HEAD_DIM, (at + 1) * HEAD_DIM)
+            rows = pl.ds(begin, QBLOCK)
+            codes.append((key_codes[rows, lanes], value_codes[rows, lanes]))
+        row = pl.ds(block * (depth // QBLOCK) + step, 1)
         results = []
         for at, (key, value) in enumerate(codes):
-            row = pl.ds(block * (depth // QBLOCK) + step * together + at, 1)
             results.append(
                 (
-                    (gathered_levels(table, key) * scales[0, row, :]).astype(BF16),
-                    (selected_levels(value) * scales[1, row, :]).astype(BF16),
+                    (gathered_levels(table, key) * scales[2 * at, row, :]).astype(BF16),
+                    (selected_levels(value) * scales[2 * at + 1, row, :]).astype(BF16),
                 )
             )
-        for begin, (key, value) in zip(begins, results):
-            rows = pl.ds(pl.multiple_of(block * depth + begin, QBLOCK), QBLOCK)
-            out[item, rows, :HEAD_DIM] = key
-            out[item, rows, HEAD_DIM:] = value
+        rows = pl.ds(pl.multiple_of(block * depth + begin, QBLOCK), QBLOCK)
+        for at, (key, value) in enumerate(results):
+            out = (out_a, out_b)[at // 2]
+            out[at % 2, rows, :HEAD_DIM] = key
+            out[at % 2, rows, HEAD_DIM:] = value
         return 0
 
-    lax.fori_loop(0, depth // (QBLOCK * together), body, 0)
-
-    if half == 0:
-        at = item * pl.num_programs(1) + block
-
-        @pl.when(at == 0)
-        def _():
-            squares[...] = jnp.zeros(squares.shape, F32)
-
-        width = x.shape[2]
-        begin = pl.multiple_of(at * width, 128)
-        for prompt in range(x.shape[0]):
-            wide = x[prompt].astype(F32)
-            scaled[prompt, :, pl.ds(begin, width)] = (wide * gain[...]).astype(BF16)
-            squares[prompt] += token_rows(jnp.sum(wide * wide, axis=1, keepdims=True))
-
-
-def dequantize(half, x, codes, scales, outer, gain):
+    lax.fori_loop(0, depth // QBLOCK, body, 0)
+
+    width = x.shape[2]
+    begin = pl.multiple_of(block * width, 128)
+    for prompt in range(x.shape[0]):
+        wide = x[prompt].astype(F32)
+        scaled[prompt, :, pl.ds(begin, width)] = (wide * gain[...]).astype(BF16)
+        squares[prompt] += token_rows(jnp.sum(wide * wide, axis=1, keepdims=True))
+
+
+def dequantize(x, codes, scales, outer, gain):
     per_rep, _, features = x.shape
-    depth = min(1024, features)
-    blocks = features // depth
-    width = features // (2 * blocks)
-    head = lambda i: lax.axis_index("rep") * CORE_HEADS + 2 * half + i
+    depth = min(256, features)
+    width = CORE_HEADS * HEAD_DIM
+    rep = lambda: lax.axis_index("rep")
     x, codes, scales, outer, gain = in_hbm(x, codes, scales, outer, gain)
-    in_specs = [
-        pl.BlockSpec((depth, HEAD_DIM), lambda i, k: (k, head(i))),
-        pl.BlockSpec((depth, HEAD_DIM), lambda i, k: (k, KV_HEADS + head(i))),
-        pl.BlockSpec((scales.shape[0], HEAD_DIM), lambda i, k: (0, head(i))),
-        pl.BlockSpec((scales.shape[0], HEAD_DIM), lambda i, k: (0, KV_HEADS + head(i))),
-        pl.BlockSpec(outer.shape, lambda i, k: (0, 0)),
-    ]
-    operands = [codes, codes, scales, scales, outer]
-    shapes = [jax.ShapeDtypeStruct((2, features, 2 * HEAD_DIM), BF16)]
-    if half == 0:
-        in_specs += [
-            pl.BlockSpec((per_rep, STRETCH, width), lambda i, k: (0, 0, i * blocks + k)),
-            pl.BlockSpec((1, width), lambda i, k: (0, i * blocks + k)),
-        ]
-        operands += [x, gain]
-        shapes += [
+    weight = jax.ShapeDtypeStruct((2, features, 2 * HEAD_DIM), BF16)
+    return pl.pallas_call(
+        weights_kernel,
+        grid=(features // depth,),
+        in_specs=[
+            pl.BlockSpec((per_rep, STRETCH, depth), lambda k: (0, 0, k)),
+            pl.BlockSpec((depth, width), lambda k: (k, rep())),
+            pl.BlockSpec((depth, width), lambda k: (k, 2 + rep())),
+            pl.BlockSpec((scales.shape[0], width), lambda k: (0, rep())),
+            pl.BlockSpec((scales.shape[0], width), lambda k: (0, 2 + rep())),
+            pl.BlockSpec(outer.shape, lambda k: (0, 0)),
+            pl.BlockSpec((1, depth), lambda k: (0, k)),
+        ],
+        out_specs=[VMEM] * 4,
+        out_shape=[
+            weight,
+            weight,
             jax.ShapeDtypeStruct(x.shape, BF16),
             jax.ShapeDtypeStruct((per_rep, 8, 128), F32),
-        ]
-    return pl.pallas_call(
-        functools.partial(weights_kernel, half),
-        grid=(2, blocks),
-        in_specs=in_specs,
-        out_specs=[VMEM] * len(shapes),
-        out_shape=shapes,
-        scratch_shapes=[pltpu.VMEM((2, scales.shape[0], HEAD_DIM), F32)],
+        ],
+        scratch_shapes=[pltpu.VMEM((2 * CORE_HEADS, scales.shape[0], HEAD_DIM), F32)],
         compiler_params=pltpu.CompilerParams(vmem_limit_bytes=32 * MIB),
         cost_estimate=pl.CostEstimate(
-            flops=16 * codes.size, bytes_accessed=codes.size, transcendentals=0
+            flops=32 * codes.size, bytes_accessed=codes.size * 2, transcendentals=0
         ),
         name="dequantize",
-    )(*operands)
+    )(x, codes, codes, scales, scales, outer, gain)
 
 
 def prompt_of(targets, owner):
@@ -446,31 +432,29 @@
     )(targets, queries, starts, turns)
 
 
-CACHE_HEADS = 2
-
-
-def cache_kernel(targets, lengths, stored, q, keys, values, fresh_keys, fresh_values, out):
+def cache_kernel(part, targets, lengths, stored, q, cache, new, out):
     scaling = HEAD_DIM ** (-0.5)
     dims = (((1,), (1,)), ((), ()))
     here = lax.axis_index("tp")
     rep = lax.axis_index("rep")
-    length = keys.shape[1]
-    span = stored[0]
-    for prompt in range(targets.shape[0]):
-        span = jnp.where(targets[prompt] == here, lengths[prompt] - STRETCH, span)
-    place = lax.broadcasted_iota(jnp.int32, (ROWS, length), 1)
-    allowed = place < span - rep * length
+    length = cache.shape[1]
+    prompt = prompt_of(targets, here)
+    handed = lengths[jnp.maximum(prompt, 0)] - STRETCH
+    span = jnp.where(prompt >= 0, handed, stored[0]) - rep * length
+    allowed = lax.broadcasted_iota(jnp.int32, (ROWS, length), 1) < span
     second_step = lax.broadcasted_iota(jnp.int32, (ROWS, 1), 0) % STEPS == 1
-    for at in range(CACHE_HEADS):
-        lanes = slice(at * HEAD_DIM, (at + 1) * HEAD_DIM)
-        query = q[at]
+    for at in range(CORE_HEADS):
+        head = part * CORE_HEADS + at
+        key_lanes = slice(head * HEAD_DIM, (head + 1) * HEAD_DIM)
+        value_lanes = slice((KV_HEADS + head) * HEAD_DIM, (KV_HEADS + head + 1) * HEAD_DIM)
+        query = q[head]
         wide = query.astype(F32)
-        scores = lax.dot_general(query, keys[0, :, lanes], dims, preferred_element_type=F32)
+        scores = lax.dot_general(query, cache[0, :, key_lanes], dims, preferred_element_type=F32)
         scores = jnp.where(allowed, scores * scaling, NEGATIVE)
         highest = jnp.max(scores, axis=1, keepdims=True)
         fresh = []
         for step in range(STEPS):
-            key = fresh_keys[0, step : step + 1, lanes].astype(F32)
+            key = new[0, step : step + 1, key_lanes].astype(F32)
             score = jnp.sum(wide * key, axis=1, keepdims=True) * scaling
             shown = rep == 0 if step == 0 else second_step & (rep == 0)
             score = jnp.where(shown, score, NEGATIVE)
@@ -480,11 +464,11 @@
         highest = jnp.where(some, highest, 0.0)
         weight = jnp.exp(scores - highest)
         totals = jnp.sum(weight, axis=1, keepdims=True)
-        sums = jnp.dot(weight.astype(BF16), values[0, :, lanes], preferred_element_type=F32)
+        sums = jnp.dot(weight.astype(BF16), cache[0, :, value_lanes], preferred_element_type=F32)
         for step in range(STEPS):
             share = jnp.exp(fresh[step] - highest)
             totals += share
-            value = fresh_values[0, step : step + 1, lanes].astype(F32)
+            value = new[0, step : step + 1, value_lanes].astype(F32)
             sums += share.astype(BF16).astype(F32) * value
         totals = jnp.where(some, totals, 1.0)
         out[at, :ROWS] = (sums / totals).astype(BF16)
@@ -492,33 +476,19 @@
 
 
 def cache_attention(part, targets, lengths, stored, grouped, kv_cache, new_kv):
-    length = kv_cache.shape[1]
-    (kv_cache,) = in_hbm(kv_cache)
-    width = CACHE_HEADS * HEAD_DIM
-    blocks = KV_HEADS // CACHE_HEADS
-    return pl.pallas_call(
-        cache_kernel,
-        grid=(2,),
-        in_specs=[
-            SMEM,
-            SMEM,
-            SMEM,
-            pl.BlockSpec((CACHE_HEADS, ROWS, HEAD_DIM), lambda h: (2 * part + h, 0, 0)),
-            pl.BlockSpec((1, length, width), lambda h: (0, 0, 2 * part + h)),
-            pl.BlockSpec((1, length, width), lambda h: (0, 0, blocks + 2 * part + h)),
-            pl.BlockSpec((1, STEPS, width), lambda h: (0, 0, 2 * part + h)),
-            pl.BlockSpec((1, STEPS, width), lambda h: (0, 0, blocks + 2 * part + h)),
-        ],
-        out_specs=pl.BlockSpec((CACHE_HEADS, PART, HEAD_DIM), lambda h: (h, 0, 0)),
-        out_shape=jax.ShapeDtypeStruct((2 * CACHE_HEADS, PART, HEAD_DIM), BF16),
-        compiler_params=pltpu.CompilerParams(vmem_limit_bytes=24 * MIB),
+    return pl.pallas_call(
+        functools.partial(cache_kernel, part),
+        in_specs=[SMEM] * 3 + [VMEM] * 3,
+        out_specs=VMEM,
+        out_shape=jax.ShapeDtypeStruct((CORE_HEADS, PART, HEAD_DIM), BF16),
+        compiler_params=pltpu.CompilerParams(vmem_limit_bytes=16 * MIB),
         cost_estimate=pl.CostEstimate(
-            flops=8 * CACHE_HEADS * ROWS * length * HEAD_DIM,
-            bytes_accessed=2 * length * 2 * width * 2,
-            transcendentals=2 * CACHE_HEADS * ROWS * length,
+            flops=2 * grouped.size * kv_cache.shape[1],
+            bytes_accessed=kv_cache.size,
+            transcendentals=CORE_HEADS * ROWS * kv_cache.shape[1],
         ),
         name="cache_attention",
-    )(targets, lengths, stored, grouped, kv_cache, kv_cache, new_kv, new_kv)
+    )(targets, lengths, stored, grouped, kv_cache, new_kv)
 
 
 def final_kernel(
@@ -610,8 +580,9 @@
         return lax.ppermute(right, "tp", to_right), lax.ppermute(left, "tp", to_left)
 
     other = lax.ppermute(lines, "rep", [(0, 1), (1, 0)])
-    first_half, own, squares = dequantize(0, lines, kv_codes, scale_codes, outer_scales.T, gain)
-    (second_half,) = dequantize(1, lines, kv_codes, scale_codes, outer_scales.T, gain)
+    first_half, second_half, own, squares = dequantize(
+        lines, kv_codes, scale_codes, outer_scales.T, gain
+    )
     frequency, turns = rotary_turns()
     start = (prompt_lengths - STRETCH).astype(F32)[:, None] * jnp.asarray(frequency)
     starts = jnp.stack([jnp.cos(start), jnp.sin(start)])

time: 61.9 us -> 59 us (0.953)
  Pallas kernels: 32 us -> 29.1 us
  starting transfers between devices: 18.3 us -> 17.4 us
  waiting for transfers between devices: 5.92 us -> 6.79 us
    pallas_call x4 -> x3, Pallas kernels: 18.5 us -> 15.3 us  [the longest x1 11.4 us: dequantize(): pl.pallas_call(weights_kernel, grid=(features // depth,), in_specs=[pl.Bl...]
    ppermute x8, starting transfers between devices: 16.7 us -> 15.3 us  [pass_on(): lax.ppermute(right, 'tp', to_right)]
    ppermute x8, waiting for transfers between devices: 1.7 us -> 3.12 us  [pass_on(): lax.ppermute(right, 'tp', to_right)]
  transfers between devices with their start and end apart: 17 -> 17, of which waited for: 4 -> 4; matrix products, arithmetic and copies ran while one was open for 0% -> 0% of each run, Pallas kernels for 45% -> 41%
where the time goes in v6:
time: 59 us; the launch traced here: 58.7 us
  Pallas kernels  29.1 us (49%)
  starting transfers between devices  17.4 us (29%)
  waiting for transfers between devices  6.79 us (12%)
  blocking collectives  3.8 us (6%)
  between operations  0.89 us (2%)
  local copies, waits for them, and re-layouts  0.66 us (1%)
    ppermute x8, starting transfers between devices, pass_on(): lax.ppermute(right, 'tp', to_right)  15.3 us
    pallas_call x1, Pallas kernels, dequantize(): pl.pallas_call(weights_kernel, grid=(features // depth,), in_specs=[pl.Bl...  11.4 us
    pallas_call x2, Pallas kernels, project(): pl.pallas_call(functools.partial(project_kernel, distances), in_specs=[SM...  6.43 us
    pallas_call x2, Pallas kernels, cache_attention(): pl.pallas_call(functools.partial(cache_kernel, part), in_specs=[SMEM] * 3...  3.98 us
    ppermute x8, waiting for transfers between devices, pass_on(): lax.ppermute(left, 'tp', to_left)  3.67 us
    ppermute x8, waiting for transfers between devices, pass_on(): lax.ppermute(right, 'tp', to_right)  3.12 us
    pallas_call x1, Pallas kernels, project_first(): pl.pallas_call(functools.partial(first_kernel, distances), in_specs=[SMEM...  2.77 us
    pallas_call x1, Pallas kernels, finish(): pl.pallas_call(final_kernel, in_specs=[SMEM] + [VMEM] * 9, out_specs=VMEM...  1.98 us
  transfers between devices with their start and end apart: 17, of which 4 were waited for; matrix products, arithmetic and copies ran while one was open for 0% of the time, Pallas kernels for 41%

profile of v6, /device:TPU:0, one launch (start us, length us, event | category | flops | bytes accessed | tf_op | source)
XLA Modules:
  0.0 58.7 jit_solution(4355856693941609994)
XLA Ops:
  0.0 0.5 collective-permute-start
  0.5 11.4 %dequantize.1 = (bf16[2,2048,256]{2,1,0:T(8,128)(2,1)S(1)}, bf16[2,2048,256]{2,1,0:T(8,128)(2,1)S(1)}, bf16[3,192,2048]{2,1,0:T(8,128)(2,1)S(1)}, f32[3,8,128]{2,1,0:T(8,128)S(1)}) custom-call(bf16[3,192,2048]{2,1,0:T(8,128)(2,1)} %bitcast.10, s32[2048,2048]{1,0:T(8,128)} %value_codes.1, s32[2048,2048]{1,0:T(8,128)} %value_codes.1, s32[32,2048]{1,0:T(8,128)} %value_scales.1, ...), custom_call_target="tpu_custom_call" | custom-call | flops 134217728 | bytes 8388608 | tf_op jit(solution)/shard_map/dequantize/pallas_call | solution.py:205
  11.9 0.1 multiply_cosine_fusion
  12.0 0.7 %prepare.1 = (bf16[8,32,128]{2,1,0:T(8,128)(2,1)S(1)}, f32[2,192,128]{2,1,0:T(8,128)S(1)}) custom-call(s32[6]{0:T(128)S(1)} %copy-done.5, bf16[1,2,16384]{2,1,0:T(2,128)(2,1)S(1)} %copy-done.3, f32[2,6,128]{2,1,0:T(8,128)S(1)} %pad_maximum_fusion.1.starts, f32[2,192,128]{2,1,0:T(8,128)S(1)} %copy-done.1), custom_call_target="tpu_custom_call" | custom-call | tf_op jit(solution)/shard_map/prepare/pallas_call | solution.py:422
  12.7 2.8 %project_first.1 = (bf16[400,128]{1,0:T(8,128)(2,1)S(1)}, bf16[384,128]{1,0:T(8,128)(2,1)S(1)}, f32[2,776,128]{2,1,0:T(8,128)S(1)}, bf16[576,2048]{1,0:T(8,128)(2,1)S(1)}, f32[3,8,128]{2,1,0:T(8,128)S(1)}) custom-call(s32[6]{0:T(128)S(1)} %copy-done.5, bf16[3,192,2048]{2,1,0:T(8,128)(2,1)S(1)} %get-tuple-element.60.own, ...), custom_call_target="tpu_custom_call" | custom-call | flops 1207959552 | bytes 1048576 | tf_op jit(solution)/shard_map/project_first/pallas_call | solution.py:317
  15.5 2.4 %collective-permute-start.1 = (bf16[400,128]{1,0:T(8,128)(2,1)S(1)}, bf16[400,128]{1,0:T(8,128)(2,1)S(1)}, u32[]{:S(2)}, u32[]{:S(2)}) collective-permute-start(bf16[400,128]{1,0:T(8,128)(2,1)S(1)} %get-tuple-element.65), channel_id=1, source_target_pairs={{0,4},{4,8},{8,12},{12,14},{14,10},{10,6},{6,2},{2,0},{1,5},{5,9},... | collective-permute-start | bytes 307208 | tf_op jit(solution)/shard_map/ppermute | solution.py:580
  17.9 0.0 collective-permute-start.2
  17.9 1.4 %project_second.1 = (bf16[400,128]{1,0:T(8,128)(2,1)S(1)}, bf16[384,128]{1,0:T(8,128)(2,1)S(1)}, f32[2,776,128]{2,1,0:T(8,128)S(1)}) custom-call(bf16[576,2048]{1,0:T(8,128)(2,1)S(1)} %get-tuple-element.68.lines, f32[3,8,128]{2,1,0:T(8,128)S(1)} %get-tuple-element.69.totals, bf16[2,2048,256]{2,1,0:T(8,128)(2,1)S(1)} %get-tuple-element.70.weight.weight_b), custom_call_target="tpu_custom_call" | custom-call | flops 1207959552 | bytes 1048576 | tf_op jit(solution)/shard_map/project_second/pallas_call | solution.py:329
  19.3 2.1 %collective-permute-start.3 = (bf16[400,128]{1,0:T(8,128)(2,1)S(1)}, bf16[400,128]{1,0:T(8,128)(2,1)S(1)}, u32[]{:S(2)}, u32[]{:S(2)}) collective-permute-start(bf16[400,128]{1,0:T(8,128)(2,1)S(1)} %get-tuple-element.73), channel_id=1, source_target_pairs={{0,4},{4,8},{8,12},{12,14},{14,10},{10,6},{6,2},{2,0},{1,5},{5,9},... | collective-permute-start | bytes 307208 | tf_op jit(solution)/shard_map/ppermute | solution.py:580
  21.3 0.0 collective-permute-start.4
  21.3 1.4 %collective-permute-done.2.left = bf16[384,128]{1,0:T(8,128)(2,1)S(1)} collective-permute-done((bf16[384,128]{1,0:T(8,128)(2,1)S(1)}, bf16[384,128]{1,0:T(8,128)(2,1)S(1)}, u32[]{:S(2)}, u32[]{:S(2)}) %collective-permute-start.2) | collective-permute-done | bytes 98336 | tf_op jit(solution)/shard_map/ppermute | solution.py:580
  22.8 0.0 collective-permute-done.1.right
  22.8 0.1 sends.6
  22.8 1.7 %collective-permute-start.5 = (bf16[784,128]{1,0:T(8,128)(2,1)S(1)}, bf16[784,128]{1,0:T(8,128)(2,1)S(1)}, u32[]{:S(2)}, u32[]{:S(2)}) collective-permute-start(bf16[784,128]{1,0:T(8,128)(2,1)S(1)} %get-tuple-element.78), channel_id=1, source_target_pairs={{0,4},{4,8},{8,12},{12,14},{14,10},{10,6},{6,2},{2,0},{1,5},{5,9},... | collective-permute-start | bytes 602120 | tf_op jit(solution)/shard_map/ppermute | solution.py:580
  24.6 0.3 collective-permute-start.6
  24.9 1.0 %collective-permute-done.4.left = bf16[384,128]{1,0:T(8,128)(2,1)S(1)} collective-permute-done((bf16[384,128]{1,0:T(8,128)(2,1)S(1)}, bf16[384,128]{1,0:T(8,128)(2,1)S(1)}, u32[]{:S(2)}, u32[]{:S(2)}) %collective-permute-start.4) | collective-permute-done | bytes 98336 | tf_op jit(solution)/shard_map/ppermute | solution.py:580
  26.0 0.1 sends.7
  26.0 1.6 %collective-permute-start.7 = (bf16[768,128]{1,0:T(8,128)(2,1)S(1)}, bf16[768,128]{1,0:T(8,128)(2,1)S(1)}, u32[]{:S(2)}, u32[]{:S(2)}) collective-permute-start(bf16[768,128]{1,0:T(8,128)(2,1)S(1)} %get-tuple-element.75), channel_id=1, source_target_pairs={{0,4},{4,8},{8,12},{12,14},{14,10},{10,6},{6,2},{2,0},{1,5},{5,9},... | collective-permute-start | bytes 589832 | tf_op jit(solution)/shard_map/ppermute | solution.py:580
  27.7 0.4 collective-permute-start.8
  28.8 2.0 %cache_attention.2 = bf16[4,48,128]{2,1,0:T(8,128)(2,1)S(1)} custom-call(s32[6]{0:T(128)S(1)} %copy-done.5, s32[6]{0:T(128)S(1)} %copy-done.6, s32[1]{0:T(128)S(6)} %copy.15.stored, bf16[8,32,128]{2,1,0:T(8,128)(2,1)S(1)} %get-tuple-element.81.q.grouped, bf16[1,1024,2048]{2,1,0:T(8,128)(2,1)S(1)} %copy-done, bf16[1,2,2048]{2,1,0:T(2,128)(2,1)S(1)} %copy-done.4), custom_call_target="tpu_custom_call" | custom-call | flops 67108864 | bytes 2097152 | tf_op jit(solution)/shard_map/cache_attention/pallas_call | solution.py:479
  30.8 2.5 %project.2 = (f32[2,776,128]{2,1,0:T(8,128)S(1)}, f32[2,776,128]{2,1,0:T(8,128)S(1)}) custom-call(s32[6]{0:T(128)S(1)} %copy-done.5, bf16[3,192,2048]{2,1,0:T(8,128)(2,1)S(1)} %get-tuple-element.60.own, f32[3,8,128]{2,1,0:T(8,128)S(1)} %get-tuple-element.61.squares, bf16[3,192,2048]{2,1,0:T(8,128)(2,1)S(1)} %collective-permute-done.other, ...), custom_call_target="tpu_custom_call" | custom-call | flops 805306368 | bytes 1048576 | tf_op jit(solution)/shard_map/project/pallas_call | solution.py:362
  33.3 0.0 collective-permute-done.5.right
  33.3 0.0 collective-permute-done.6.left
  33.3 0.1 sends.8
  33.4 1.9 %collective-permute-start.9 = (bf16[784,128]{1,0:T(8,128)(2,1)S(1)}, bf16[784,128]{1,0:T(8,128)(2,1)S(1)}, u32[]{:S(2)}, u32[]{:S(2)}) collective-permute-start(bf16[784,128]{1,0:T(8,128)(2,1)S(1)} %get-tuple-element.88), channel_id=1, source_target_pairs={{0,4},{4,8},{8,12},{12,14},{14,10},{10,6},{6,2},{2,0},{1,5},{5,9},... | collective-permute-start | bytes 602120 | tf_op jit(solution)/shard_map/ppermute | solution.py:580
  35.3 0.2 collective-permute-start.10
  35.6 0.0 collective-permute-done.7.right
  35.6 0.0 collective-permute-done.8.left
  35.6 0.1 sends.9
  35.7 1.9 %collective-permute-start.13 = (bf16[768,128]{1,0:T(8,128)(2,1)S(1)}, bf16[768,128]{1,0:T(8,128)(2,1)S(1)}, u32[]{:S(2)}, u32[]{:S(2)}) collective-permute-start(bf16[768,128]{1,0:T(8,128)(2,1)S(1)} %get-tuple-element.85), channel_id=1, source_target_pairs={{0,4},{4,8},{8,12},{12,14},{14,10},{10,6},{6,2},{2,0},{1,5},{5,9},... | collective-permute-start | bytes 589832 | tf_op jit(solution)/shard_map/ppermute | solution.py:580
  37.5 0.2 collective-permute-start.14
  37.8 2.0 %cache_attention.3 = bf16[4,48,128]{2,1,0:T(8,128)(2,1)S(1)} custom-call(s32[6]{0:T(128)S(1)} %copy-done.5, s32[6]{0:T(128)S(1)} %copy-done.6, s32[1]{0:T(128)S(6)} %copy.15.stored, bf16[8,32,128]{2,1,0:T(8,128)(2,1)S(1)} %get-tuple-element.81.q.grouped, bf16[1,1024,2048]{2,1,0:T(8,128)(2,1)S(1)} %copy-done, bf16[1,2,2048]{2,1,0:T(2,128)(2,1)S(1)} %copy-done.4), custom_call_target="tpu_custom_call" | custom-call | flops 67108864 | bytes 2097152 | tf_op jit(solution)/shard_map/cache_attention/pallas_call | solution.py:479
  39.7 3.9 %project.3 = (f32[3,776,128]{2,1,0:T(8,128)S(1)}, f32[3,776,128]{2,1,0:T(8,128)S(1)}) custom-call(s32[6]{0:T(128)S(1)} %copy-done.5, bf16[3,192,2048]{2,1,0:T(8,128)(2,1)S(1)} %get-tuple-element.60.own, f32[3,8,128]{2,1,0:T(8,128)S(1)} %get-tuple-element.61.squares, bf16[3,192,2048]{2,1,0:T(8,128)(2,1)S(1)} %collective-permute-done.other, ...), custom_call_target="tpu_custom_call" | custom-call | flops 1207959552 | bytes 1048576 | tf_op jit(solution)/shard_map/project/pallas_call | solution.py:362
  43.7 0.1 sends.10
  43.7 1.9 %collective-permute-start.11 = (bf16[784,128]{1,0:T(8,128)(2,1)S(1)}, bf16[784,128]{1,0:T(8,128)(2,1)S(1)}, u32[]{:S(2)}, u32[]{:S(2)}) collective-permute-start(bf16[784,128]{1,0:T(8,128)(2,1)S(1)} %get-tuple-element.94), channel_id=1, source_target_pairs={{0,4},{4,8},{8,12},{12,14},{14,10},{10,6},{6,2},{2,0},{1,5},{5,9},... | collective-permute-start | bytes 602120 | tf_op jit(solution)/shard_map/ppermute | solution.py:580
  45.6 0.2 collective-permute-start.12
  45.8 0.0 collective-permute-done.13.right
  45.8 0.1 sends.11
  45.9 1.9 %collective-permute-start.15 = (bf16[768,128]{1,0:T(8,128)(2,1)S(1)}, bf16[768,128]{1,0:T(8,128)(2,1)S(1)}, u32[]{:S(2)}, u32[]{:S(2)}) collective-permute-start(bf16[768,128]{1,0:T(8,128)(2,1)S(1)} %get-tuple-element.97), channel_id=1, source_target_pairs={{0,4},{4,8},{8,12},{12,14},{14,10},{10,6},{6,2},{2,0},{1,5},{5,9},... | collective-permute-start | bytes 589832 | tf_op jit(solution)/shard_map/ppermute | solution.py:580
  47.8 0.2 collective-permute-start.16
  48.0 1.9 %all-gather = bf16[16,48,128]{2,1,0:T(8,128)(2,1)S(1)} all-gather(bf16[8,48,128]{2,1,0:T(8,128)(2,1)S(1)} %pad_maximum_fusion), channel_id=2, replica_groups=mesh['grp'=2,'tp'=8,'rep'=2] {'rep'}, dimensions={0}, use_global_device_ids=true | all-gather | bytes 294912 | tf_op jit(solution)/shard_map/all_gather | solution.py:626
  50.0 3.1 %collective-permute-done.15.right_b = bf16[768,128]{1,0:T(8,128)(2,1)S(1)} collective-permute-done((bf16[768,128]{1,0:T(8,128)(2,1)S(1)}, bf16[768,128]{1,0:T(8,128)(2,1)S(1)}, u32[]{:S(2)}, u32[]{:S(2)}) %collective-permute-start.15) | collective-permute-done | bytes 196640 | tf_op jit(solution)/shard_map/ppermute | solution.py:580
  53.1 1.2 %collective-permute-done.16.left_b = bf16[768,128]{1,0:T(8,128)(2,1)S(1)} collective-permute-done((bf16[768,128]{1,0:T(8,128)(2,1)S(1)}, bf16[768,128]{1,0:T(8,128)(2,1)S(1)}, u32[]{:S(2)}, u32[]{:S(2)}) %collective-permute-start.16) | collective-permute-done | bytes 196640 | tf_op jit(solution)/shard_map/ppermute | solution.py:580
  54.2 0.0 collective-permute-done.11.right_a
  54.2 0.0 collective-permute-done.12.left_a
  54.3 2.0 %finish.1 = bf16[1,2,8192]{2,1,0:T(2,128)(2,1)S(1)} custom-call(s32[6]{0:T(128)S(1)} %copy-done.5, f32[2,192,128]{2,1,0:T(8,128)S(1)} %get-tuple-element.59.rotary, f32[3,776,128]{2,1,0:T(8,128)S(1)} %get-tuple-element.87.terms.own_a, f32[3,776,128]{2,1,0:T(8,128)S(1)} %get-tuple-element.93.terms.own_b, ...), custom_call_target="tpu_custom_call" | custom-call | tf_op jit(solution)/shard_map/finish/pallas_call | solution.py:541
  56.2 1.9 %all_gather.11 = bf16[1,2,16384]{2,1,0:T(2,128)(2,1)S(1)} all-gather(bf16[1,2,8192]{2,1,0:T(2,128)(2,1)S(1)} %finish.1), channel_id=1, replica_groups=mesh['grp'=2,'tp'=8,'rep'=2] {'rep'}, dimensions={2}, use_global_device_ids=true | all-gather | bytes 98304 | tf_op jit(solution)/shard_map/all_gather | solution.py:628
  58.1 0.6 %copy.16 = bf16[1,2,16384]{2,1,0:T(2,128)(2,1)} copy(bf16[1,2,16384]{2,1,0:T(2,128)(2,1)S(1)} %all_gather.11) | data formatting | bytes 131072
  (24 shorter events, 0.1 us)
Async XLA Ops:
  0.0 12.7 %collective-permute-start = (bf16[3,192,2048]{2,1,0:T(8,128)(2,1)}, bf16[3,192,2048]{2,1,0:T(8,128)(2,1)S(1)}, u32[]{:S(2)}, u32[]{:S(2)}) collective-permute-start(bf16[3,192,2048]{2,1,0:T(8,128)(2,1)} %bitcast.9), channel_id=1, source_target_pairs={{0,1},{1,0},{2,3},{3,2},{4,5},{5,4},{6,7},{7,6},{8,9},{9,8},{10,11... | collective-permute-start | bytes 7077896 | tf_op jit(solution)/shard_map/ppermute | solution.py:582
  0.5 11.4 %copy-start.6 = (s32[6]{0:T(128)S(1)}, s32[6]{0:T(128)}, u32[]{:S(2)}) copy-start(s32[6]{0:T(128)} %lengths.3) | copy-start | bytes 76
  0.5 11.4 %copy-start.7 = (f32[128]{0:T(128)S(1)}, f32[128]{0:T(128)}, u32[]{:S(2)}) copy-start(f32[128]{0:T(128)} %constant.7.clone) | copy-start | bytes 1540
  0.5 11.5 %copy-start.1 = (f32[2,192,128]{2,1,0:T(8,128)S(1)}, f32[2,192,128]{2,1,0:T(8,128)}, u32[]{:S(2)}) copy-start(f32[2,192,128]{2,1,0:T(8,128)} %constant.8.clone.turns) | copy-start | bytes 589828
  0.5 11.6 %copy-start.3 = (bf16[1,2,16384]{2,1,0:T(2,128)(2,1)S(1)}, bf16[1,2,16384]{2,1,0:T(2,128)(2,1)}, u32[]{:S(2)}) copy-start(bf16[1,2,16384]{2,1,0:T(2,128)(2,1)} %queries.1) | copy-start | bytes 196612
  0.5 11.6 %copy-start.5 = (s32[6]{0:T(128)S(1)}, s32[6]{0:T(128)}, u32[]{:S(2)}) copy-start(s32[6]{0:T(128)} %targets.8) | copy-start | bytes 76
  0.5 12.2 %copy-start.2 = (f32[2048]{0:T(1024)S(1)}, f32[2048]{0:T(1024)}, u32[]{:S(2)}) copy-start(f32[2048]{0:T(1024)} %param.14) | copy-start | bytes 24580
  15.5 7.3 %collective-permute-start.1 = (bf16[400,128]{1,0:T(8,128)(2,1)S(1)}, bf16[400,128]{1,0:T(8,128)(2,1)S(1)}, u32[]{:S(2)}, u32[]{:S(2)}) collective-permute-start(bf16[400,128]{1,0:T(8,128)(2,1)S(1)} %get-tuple-element.65), channel_id=1, source_target_pairs={{0,4},{4,8},{8,12},{12,14},{14,10},{10,6},{6,2},{2,0},{1,5},{5,9},... | collective-permute-start | bytes 307208 | tf_op jit(solution)/shard_map/ppermute | solution.py:580
  17.9 4.9 %collective-permute-start.2 = (bf16[384,128]{1,0:T(8,128)(2,1)S(1)}, bf16[384,128]{1,0:T(8,128)(2,1)S(1)}, u32[]{:S(2)}, u32[]{:S(2)}) collective-permute-start(bf16[384,128]{1,0:T(8,128)(2,1)S(1)} %get-tuple-element.66), channel_id=1, source_target_pairs={{0,2},{4,0},{8,4},{12,8},{14,12},{10,14},{6,10},{2,6},{1,3},{5,1},... | collective-permute-start | bytes 294920 | tf_op jit(solution)/shard_map/ppermute | solution.py:580
  17.9 10.9 %copy-start = (bf16[1,1024,2048]{2,1,0:T(8,128)(2,1)S(1)}, bf16[1,1024,2048]{2,1,0:T(8,128)(2,1)}, u32[]{:S(2)}) copy-start(bf16[1,1024,2048]{2,1,0:T(8,128)(2,1)} %cache.3) | copy-start | bytes 12582916
  17.9 10.9 %copy-start.4 = (bf16[1,2,2048]{2,1,0:T(2,128)(2,1)S(1)}, bf16[1,2,2048]{2,1,0:T(2,128)(2,1)}, u32[]{:S(2)}) copy-start(bf16[1,2,2048]{2,1,0:T(2,128)(2,1)} %new.3) | copy-start | bytes 24580
  19.3 6.7 %collective-permute-start.3 = (bf16[400,128]{1,0:T(8,128)(2,1)S(1)}, bf16[400,128]{1,0:T(8,128)(2,1)S(1)}, u32[]{:S(2)}, u32[]{:S(2)}) collective-permute-start(bf16[400,128]{1,0:T(8,128)(2,1)S(1)} %get-tuple-element.73), channel_id=1, source_target_pairs={{0,4},{4,8},{8,12},{12,14},{14,10},{10,6},{6,2},{2,0},{1,5},{5,9},... | collective-permute-start | bytes 307208 | tf_op jit(solution)/shard_map/ppermute | solution.py:580
  21.3 4.6 %collective-permute-start.4 = (bf16[384,128]{1,0:T(8,128)(2,1)S(1)}, bf16[384,128]{1,0:T(8,128)(2,1)S(1)}, u32[]{:S(2)}, u32[]{:S(2)}) collective-permute-start(bf16[384,128]{1,0:T(8,128)(2,1)S(1)} %get-tuple-element.74), channel_id=1, source_target_pairs={{0,2},{4,0},{8,4},{12,8},{14,12},{10,14},{6,10},{2,6},{1,3},{5,1},... | collective-permute-start | bytes 294920 | tf_op jit(solution)/shard_map/ppermute | solution.py:580
  22.8 10.5 %collective-permute-start.5 = (bf16[784,128]{1,0:T(8,128)(2,1)S(1)}, bf16[784,128]{1,0:T(8,128)(2,1)S(1)}, u32[]{:S(2)}, u32[]{:S(2)}) collective-permute-start(bf16[784,128]{1,0:T(8,128)(2,1)S(1)} %get-tuple-element.78), channel_id=1, source_target_pairs={{0,4},{4,8},{8,12},{12,14},{14,10},{10,6},{6,2},{2,0},{1,5},{5,9},... | collective-permute-start | bytes 602120 | tf_op jit(solution)/shard_map/ppermute | solution.py:580
  24.6 8.8 %collective-permute-start.6 = (bf16[784,128]{1,0:T(8,128)(2,1)S(1)}, bf16[784,128]{1,0:T(8,128)(2,1)S(1)}, u32[]{:S(2)}, u32[]{:S(2)}) collective-permute-start(bf16[784,128]{1,0:T(8,128)(2,1)S(1)} %get-tuple-element.79), channel_id=1, source_target_pairs={{0,2},{4,0},{8,4},{12,8},{14,12},{10,14},{6,10},{2,6},{1,3},{5,1},... | collective-permute-start | bytes 602120 | tf_op jit(solution)/shard_map/ppermute | solution.py:580
  26.0 9.5 %collective-permute-start.7 = (bf16[768,128]{1,0:T(8,128)(2,1)S(1)}, bf16[768,128]{1,0:T(8,128)(2,1)S(1)}, u32[]{:S(2)}, u32[]{:S(2)}) collective-permute-start(bf16[768,128]{1,0:T(8,128)(2,1)S(1)} %get-tuple-element.75), channel_id=1, source_target_pairs={{0,4},{4,8},{8,12},{12,14},{14,10},{10,6},{6,2},{2,0},{1,5},{5,9},... | collective-permute-start | bytes 589832 | tf_op jit(solution)/shard_map/ppermute | solution.py:580
  27.7 7.9 %collective-permute-start.8 = (bf16[768,128]{1,0:T(8,128)(2,1)S(1)}, bf16[768,128]{1,0:T(8,128)(2,1)S(1)}, u32[]{:S(2)}, u32[]{:S(2)}) collective-permute-start(bf16[768,128]{1,0:T(8,128)(2,1)S(1)} %get-tuple-element.84), channel_id=1, source_target_pairs={{0,2},{4,0},{8,4},{12,8},{14,12},{10,14},{6,10},{2,6},{1,3},{5,1},... | collective-permute-start | bytes 589832 | tf_op jit(solution)/shard_map/ppermute | solution.py:580
  33.4 10.2 %collective-permute-start.9 = (bf16[784,128]{1,0:T(8,128)(2,1)S(1)}, bf16[784,128]{1,0:T(8,128)(2,1)S(1)}, u32[]{:S(2)}, u32[]{:S(2)}) collective-permute-start(bf16[784,128]{1,0:T(8,128)(2,1)S(1)} %get-tuple-element.88), channel_id=1, source_target_pairs={{0,4},{4,8},{8,12},{12,14},{14,10},{10,6},{6,2},{2,0},{1,5},{5,9},... | collective-permute-start | bytes 602120 | tf_op jit(solution)/shard_map/ppermute | solution.py:580
  35.3 8.3 %collective-permute-start.10 = (bf16[784,128]{1,0:T(8,128)(2,1)S(1)}, bf16[784,128]{1,0:T(8,128)(2,1)S(1)}, u32[]{:S(2)}, u32[]{:S(2)}) collective-permute-start(bf16[784,128]{1,0:T(8,128)(2,1)S(1)} %get-tuple-element.89), channel_id=1, source_target_pairs={{0,2},{4,0},{8,4},{12,8},{14,12},{10,14},{6,10},{2,6},{1,3},{5,1},... | collective-permute-start | bytes 602120 | tf_op jit(solution)/shard_map/ppermute | solution.py:580
  35.7 10.1 %collective-permute-start.13 = (bf16[768,128]{1,0:T(8,128)(2,1)S(1)}, bf16[768,128]{1,0:T(8,128)(2,1)S(1)}, u32[]{:S(2)}, u32[]{:S(2)}) collective-permute-start(bf16[768,128]{1,0:T(8,128)(2,1)S(1)} %get-tuple-element.85), channel_id=1, source_target_pairs={{0,4},{4,8},{8,12},{12,14},{14,10},{10,6},{6,2},{2,0},{1,5},{5,9},... | collective-permute-start | bytes 589832 | tf_op jit(solution)/shard_map/ppermute | solution.py:580
  37.5 8.3 %collective-permute-start.14 = (bf16[768,128]{1,0:T(8,128)(2,1)S(1)}, bf16[768,128]{1,0:T(8,128)(2,1)S(1)}, u32[]{:S(2)}, u32[]{:S(2)}) collective-permute-start(bf16[768,128]{1,0:T(8,128)(2,1)S(1)} %get-tuple-element.96), channel_id=1, source_target_pairs={{0,2},{4,0},{8,4},{12,8},{14,12},{10,14},{6,10},{2,6},{1,3},{5,1},... | collective-permute-start | bytes 589832 | tf_op jit(solution)/shard_map/ppermute | solution.py:580
  43.7 10.5 %collective-permute-start.11 = (bf16[784,128]{1,0:T(8,128)(2,1)S(1)}, bf16[784,128]{1,0:T(8,128)(2,1)S(1)}, u32[]{:S(2)}, u32[]{:S(2)}) collective-permute-start(bf16[784,128]{1,0:T(8,128)(2,1)S(1)} %get-tuple-element.94), channel_id=1, source_target_pairs={{0,4},{4,8},{8,12},{12,14},{14,10},{10,6},{6,2},{2,0},{1,5},{5,9},... | collective-permute-start | bytes 602120 | tf_op jit(solution)/shard_map/ppermute | solution.py:580
  45.6 8.6 %collective-permute-start.12 = (bf16[784,128]{1,0:T(8,128)(2,1)S(1)}, bf16[784,128]{1,0:T(8,128)(2,1)S(1)}, u32[]{:S(2)}, u32[]{:S(2)}) collective-permute-start(bf16[784,128]{1,0:T(8,128)(2,1)S(1)} %get-tuple-element.95), channel_id=1, source_target_pairs={{0,2},{4,0},{8,4},{12,8},{14,12},{10,14},{6,10},{2,6},{1,3},{5,1},... | collective-permute-start | bytes 602120 | tf_op jit(solution)/shard_map/ppermute | solution.py:580
  45.9 7.1 %collective-permute-start.15 = (bf16[768,128]{1,0:T(8,128)(2,1)S(1)}, bf16[768,128]{1,0:T(8,128)(2,1)S(1)}, u32[]{:S(2)}, u32[]{:S(2)}) collective-permute-start(bf16[768,128]{1,0:T(8,128)(2,1)S(1)} %get-tuple-element.97), channel_id=1, source_target_pairs={{0,4},{4,8},{8,12},{12,14},{14,10},{10,6},{6,2},{2,0},{1,5},{5,9},... | collective-permute-start | bytes 589832 | tf_op jit(solution)/shard_map/ppermute | solution.py:580
  47.8 6.5 %collective-permute-start.16 = (bf16[768,128]{1,0:T(8,128)(2,1)S(1)}, bf16[768,128]{1,0:T(8,128)(2,1)S(1)}, u32[]{:S(2)}, u32[]{:S(2)}) collective-permute-start(bf16[768,128]{1,0:T(8,128)(2,1)S(1)} %get-tuple-element.98), channel_id=1, source_target_pairs={{0,2},{4,0},{8,4},{12,8},{14,12},{10,14},{6,10},{2,6},{1,3},{5,1},... | collective-permute-start | bytes 589832 | tf_op jit(solution)/shard_map/ppermute | solution.py:580

commit v7 on v6

--- a/solution.py
+++ b/solution.py
@@ -115,18 +115,28 @@
 
 
 def gathered_levels(table, codes):
-    table = jnp.broadcast_to(table[None], (codes.shape[0] // 8, 8, 128)).reshape(codes.shape)
-    return jnp.take_along_axis(table, codes, axis=1, mode="promise_in_bounds")
+    numbers = lax.GatherDimensionNumbers(
+        offset_dims=(),
+        collapsed_slice_dims=(1,),
+        start_index_map=(1,),
+        operand_batching_dims=(0,),
+        start_indices_batching_dims=(0,),
+    )
+    return lax.gather(
+        table, codes[..., None], numbers, (1, 1), mode=lax.GatherScatterMode.PROMISE_IN_BOUNDS
+    )
 
 
 def selected_levels(codes):
-    values = [jnp.float32(level) for level in NORMAL_FLOAT_LEVELS]
-    for bit in (1, 2, 4, 8):
-        mask = (codes & bit) != 0 if bit < 8 else codes >= 8
-        values = [
-            jnp.where(mask, values[at + 1], values[at]) for at in range(0, len(values), 2)
-        ]
-    return values[0]
+    masks = [(codes & 1) != 0, (codes & 2) != 0, (codes & 4) != 0, codes >= 8]
+
+    def node(bit, base):
+        if bit < 0:
+            return jnp.float32(NORMAL_FLOAT_LEVELS[base])
+        low = node(bit - 1, base)
+        return jnp.where(masks[bit], node(bit - 1, base + (1 << bit)), low)
+
+    return node(3, 0)
 
 
 def block_scales(scales, outer, column):
@@ -164,25 +174,21 @@
 
     def body(step, _):
         begin = pl.multiple_of(step * QBLOCK, QBLOCK)
-        codes = []
+        row = pl.ds(block * (depth // QBLOCK) + step, 1)
         for at in range(CORE_HEADS):
             lanes = slice(at * HEAD_DIM, (at + 1) * HEAD_DIM)
-            rows = pl.ds(begin, QBLOCK)
-            codes.append((key_codes[rows, lanes], value_codes[rows, lanes]))
-        row = pl.ds(block * (depth // QBLOCK) + step, 1)
-        results = []
-        for at, (key, value) in enumerate(codes):
-            results.append(
-                (
-                    (gathered_levels(table, key) * scales[2 * at, row, :]).astype(BF16),
-                    (selected_levels(value) * scales[2 * at + 1, row, :]).astype(BF16),
-                )
-            )
-        rows = pl.ds(pl.multiple_of(block * depth + begin, QBLOCK), QBLOCK)
-        for at, (key, value) in enumerate(results):
             out = (out_a, out_b)[at // 2]
-            out[at % 2, rows, :HEAD_DIM] = key
-            out[at % 2, rows, HEAD_DIM:] = value
+            key_scale, value_scale = scales[2 * at, row, :], scales[2 * at + 1, row, :]
+            for tile in range(QBLOCK // 16):
+                rows = pl.ds(pl.multiple_of(begin + 16 * tile, 16), 16)
+                key, value = key_codes[rows, lanes], value_codes[rows, lanes]
+                keys = [gathered_levels(table, key[half : half + 8]) for half in (0, 8)]
+                values = [selected_levels(value[half : half + 8]) for half in (0, 8)]
+                rows = pl.ds(pl.multiple_of(block * depth + begin + 16 * tile, 16), 16)
+                keys = jnp.concatenate([level * key_scale for level in keys], axis=0)
+                values = jnp.concatenate([level * value_scale for level in values], axis=0)
+                out[at % 2, rows, :HEAD_DIM] = keys.astype(BF16)
+                out[at % 2, rows, HEAD_DIM:] = values.astype(BF16)
         return 0
 
     lax.fori_loop(0, depth // QBLOCK, body, 0)

time: 59 us -> 57.5 us (0.975)
  Pallas kernels: 29.1 us -> 27.9 us
  waiting for transfers between devices: 6.79 us -> 5.83 us
    pallas_call x1, Pallas kernels: 11.4 us -> 10.2 us  [dequantize(): pl.pallas_call(weights_kernel, grid=(features // depth,), in_specs=[pl.Bl...]
    ppermute x8, waiting for transfers between devices: 3.12 us -> 2 us  [pass_on(): lax.ppermute(right, 'tp', to_right)]
    ppermute x8, starting transfers between devices: 1.65 us -> 2.63 us  [pass_on(): lax.ppermute(left, 'tp', to_left)]
    ppermute x8, starting transfers between devices: 15.3 us -> 14.6 us  [pass_on(): lax.ppermute(right, 'tp', to_right)]
where the time goes in v7:
time: 57.5 us; the launch traced here: 56.9 us
  Pallas kernels  27.9 us (49%)
  starting transfers between devices  17.6 us (31%)
  waiting for transfers between devices  5.83 us (10%)
  blocking collectives  3.8 us (7%)
  between operations  0.89 us (2%)
  local copies, waits for them, and re-layouts  0.66 us (1%)
    ppermute x8, starting transfers between devices, pass_on(): lax.ppermute(right, 'tp', to_right)  14.6 us
    pallas_call x1, Pallas kernels, dequantize(): pl.pallas_call(weights_kernel, grid=(features // depth,), in_specs=[pl.Bl...  10.2 us
    pallas_call x2, Pallas kernels, project(): pl.pallas_call(functools.partial(project_kernel, distances), in_specs=[SM...  6.7 us
    pallas_call x2, Pallas kernels, cache_attention(): pl.pallas_call(functools.partial(cache_kernel, part), in_specs=[SMEM] * 3...  3.98 us
    ppermute x8, waiting for transfers between devices, pass_on(): lax.ppermute(left, 'tp', to_left)  3.83 us
    ppermute x8, starting transfers between devices, pass_on(): lax.ppermute(left, 'tp', to_left)  2.63 us
    pallas_call x1, Pallas kernels, project_first(): pl.pallas_call(functools.partial(first_kernel, distances), in_specs=[SMEM...  2.49 us
    ppermute x8, waiting for transfers between devices, pass_on(): lax.ppermute(right, 'tp', to_right)  2 us
  transfers between devices with their start and end apart: 17, of which 4 were waited for; matrix products, arithmetic and copies ran while one was open for 0% of the time, Pallas kernels for 41%

profile of v7, /device:TPU:0, one launch (start us, length us, event | category | flops | bytes accessed | tf_op | source)
XLA Modules:
  0.0 56.9 jit_solution(9642223461467345520)
XLA Ops:
  0.0 0.5 collective-permute-start
  0.5 10.2 %dequantize.1 = (bf16[2,2048,256]{2,1,0:T(8,128)(2,1)S(1)}, bf16[2,2048,256]{2,1,0:T(8,128)(2,1)S(1)}, bf16[3,192,2048]{2,1,0:T(8,128)(2,1)S(1)}, f32[3,8,128]{2,1,0:T(8,128)S(1)}) custom-call(bf16[3,192,2048]{2,1,0:T(8,128)(2,1)} %bitcast.10, s32[2048,2048]{1,0:T(8,128)} %value_codes.1, s32[2048,2048]{1,0:T(8,128)} %value_codes.1, s32[32,2048]{1,0:T(8,128)} %value_scales.1, ...), custom_call_target="tpu_custom_call" | custom-call | flops 134217728 | bytes 8388608 | tf_op jit(solution)/shard_map/dequantize/pallas_call | solution.py:211
  10.7 0.1 multiply_cosine_fusion
  10.9 0.7 %prepare.1 = (bf16[8,32,128]{2,1,0:T(8,128)(2,1)S(1)}, f32[2,192,128]{2,1,0:T(8,128)S(1)}) custom-call(s32[6]{0:T(128)S(1)} %copy-done.5, bf16[1,2,16384]{2,1,0:T(2,128)(2,1)S(1)} %copy-done.3, f32[2,6,128]{2,1,0:T(8,128)S(1)} %pad_maximum_fusion.1.starts, f32[2,192,128]{2,1,0:T(8,128)S(1)} %copy-done.1), custom_call_target="tpu_custom_call" | custom-call | tf_op jit(solution)/shard_map/prepare/pallas_call | solution.py:428
  11.5 0.0 collective-permute-done.other
  11.6 2.5 %project_first.1 = (bf16[400,128]{1,0:T(8,128)(2,1)S(1)}, bf16[384,128]{1,0:T(8,128)(2,1)S(1)}, f32[2,776,128]{2,1,0:T(8,128)S(1)}, bf16[576,2048]{1,0:T(8,128)(2,1)S(1)}, f32[3,8,128]{2,1,0:T(8,128)S(1)}) custom-call(s32[6]{0:T(128)S(1)} %copy-done.5, bf16[3,192,2048]{2,1,0:T(8,128)(2,1)S(1)} %get-tuple-element.60.own, ...), custom_call_target="tpu_custom_call" | custom-call | flops 1207959552 | bytes 1048576 | tf_op jit(solution)/shard_map/project_first/pallas_call | solution.py:323
  14.1 2.6 %collective-permute-start.1 = (bf16[400,128]{1,0:T(8,128)(2,1)S(1)}, bf16[400,128]{1,0:T(8,128)(2,1)S(1)}, u32[]{:S(2)}, u32[]{:S(2)}) collective-permute-start(bf16[400,128]{1,0:T(8,128)(2,1)S(1)} %get-tuple-element.65), channel_id=1, source_target_pairs={{0,4},{4,8},{8,12},{12,14},{14,10},{10,6},{6,2},{2,0},{1,5},{5,9},... | collective-permute-start | bytes 307208 | tf_op jit(solution)/shard_map/ppermute | solution.py:586
  16.7 0.0 collective-permute-start.2
  16.7 1.4 %project_second.1 = (bf16[400,128]{1,0:T(8,128)(2,1)S(1)}, bf16[384,128]{1,0:T(8,128)(2,1)S(1)}, f32[2,776,128]{2,1,0:T(8,128)S(1)}) custom-call(bf16[576,2048]{1,0:T(8,128)(2,1)S(1)} %get-tuple-element.68.lines, f32[3,8,128]{2,1,0:T(8,128)S(1)} %get-tuple-element.69.totals, bf16[2,2048,256]{2,1,0:T(8,128)(2,1)S(1)} %get-tuple-element.70.weight.weight_b), custom_call_target="tpu_custom_call" | custom-call | flops 1207959552 | bytes 1048576 | tf_op jit(solution)/shard_map/project_second/pallas_call | solution.py:335
  18.1 2.1 %collective-permute-start.3 = (bf16[400,128]{1,0:T(8,128)(2,1)S(1)}, bf16[400,128]{1,0:T(8,128)(2,1)S(1)}, u32[]{:S(2)}, u32[]{:S(2)}) collective-permute-start(bf16[400,128]{1,0:T(8,128)(2,1)S(1)} %get-tuple-element.73), channel_id=1, source_target_pairs={{0,4},{4,8},{8,12},{12,14},{14,10},{10,6},{6,2},{2,0},{1,5},{5,9},... | collective-permute-start | bytes 307208 | tf_op jit(solution)/shard_map/ppermute | solution.py:586
  20.2 0.0 collective-permute-start.4
  20.2 1.4 %collective-permute-done.2.left = bf16[384,128]{1,0:T(8,128)(2,1)S(1)} collective-permute-done((bf16[384,128]{1,0:T(8,128)(2,1)S(1)}, bf16[384,128]{1,0:T(8,128)(2,1)S(1)}, u32[]{:S(2)}, u32[]{:S(2)}) %collective-permute-start.2) | collective-permute-done | bytes 98336 | tf_op jit(solution)/shard_map/ppermute | solution.py:586
  21.6 0.1 sends.6
  21.7 1.6 %collective-permute-start.5 = (bf16[784,128]{1,0:T(8,128)(2,1)S(1)}, bf16[784,128]{1,0:T(8,128)(2,1)S(1)}, u32[]{:S(2)}, u32[]{:S(2)}) collective-permute-start(bf16[784,128]{1,0:T(8,128)(2,1)S(1)} %get-tuple-element.78), channel_id=1, source_target_pairs={{0,4},{4,8},{8,12},{12,14},{14,10},{10,6},{6,2},{2,0},{1,5},{5,9},... | collective-permute-start | bytes 602120 | tf_op jit(solution)/shard_map/ppermute | solution.py:586
  23.3 0.4 collective-permute-start.6
  23.8 1.0 %collective-permute-done.4.left = bf16[384,128]{1,0:T(8,128)(2,1)S(1)} collective-permute-done((bf16[384,128]{1,0:T(8,128)(2,1)S(1)}, bf16[384,128]{1,0:T(8,128)(2,1)S(1)}, u32[]{:S(2)}, u32[]{:S(2)}) %collective-permute-start.4) | collective-permute-done | bytes 98336 | tf_op jit(solution)/shard_map/ppermute | solution.py:586
  24.8 0.0 collective-permute-done.3.right
  24.8 0.1 sends.7
  24.9 1.6 %collective-permute-start.7 = (bf16[768,128]{1,0:T(8,128)(2,1)S(1)}, bf16[768,128]{1,0:T(8,128)(2,1)S(1)}, u32[]{:S(2)}, u32[]{:S(2)}) collective-permute-start(bf16[768,128]{1,0:T(8,128)(2,1)S(1)} %get-tuple-element.75), channel_id=1, source_target_pairs={{0,4},{4,8},{8,12},{12,14},{14,10},{10,6},{6,2},{2,0},{1,5},{5,9},... | collective-permute-start | bytes 589832 | tf_op jit(solution)/shard_map/ppermute | solution.py:586
  26.5 0.4 collective-permute-start.8
  27.6 2.0 %cache_attention.2 = bf16[4,48,128]{2,1,0:T(8,128)(2,1)S(1)} custom-call(s32[6]{0:T(128)S(1)} %copy-done.5, s32[6]{0:T(128)S(1)} %copy-done.6, s32[1]{0:T(128)S(6)} %copy.15.stored, bf16[8,32,128]{2,1,0:T(8,128)(2,1)S(1)} %get-tuple-element.81.q.grouped, bf16[1,1024,2048]{2,1,0:T(8,128)(2,1)S(1)} %copy-done, bf16[1,2,2048]{2,1,0:T(2,128)(2,1)S(1)} %copy-done.4), custom_call_target="tpu_custom_call" | custom-call | flops 67108864 | bytes 2097152 | tf_op jit(solution)/shard_map/cache_attention/pallas_call | solution.py:485
  29.6 2.8 %project.2 = (f32[2,776,128]{2,1,0:T(8,128)S(1)}, f32[2,776,128]{2,1,0:T(8,128)S(1)}) custom-call(s32[6]{0:T(128)S(1)} %copy-done.5, bf16[3,192,2048]{2,1,0:T(8,128)(2,1)S(1)} %get-tuple-element.60.own, f32[3,8,128]{2,1,0:T(8,128)S(1)} %get-tuple-element.61.squares, bf16[3,192,2048]{2,1,0:T(8,128)(2,1)S(1)} %collective-permute-done.other, ...), custom_call_target="tpu_custom_call" | custom-call | flops 805306368 | bytes 1048576 | tf_op jit(solution)/shard_map/project/pallas_call | solution.py:368
  32.5 0.0 collective-permute-done.5.right
  32.5 0.0 collective-permute-done.6.left
  32.5 0.1 sends.8
  32.6 1.6 %collective-permute-start.9 = (bf16[784,128]{1,0:T(8,128)(2,1)S(1)}, bf16[784,128]{1,0:T(8,128)(2,1)S(1)}, u32[]{:S(2)}, u32[]{:S(2)}) collective-permute-start(bf16[784,128]{1,0:T(8,128)(2,1)S(1)} %get-tuple-element.88), channel_id=1, source_target_pairs={{0,4},{4,8},{8,12},{12,14},{14,10},{10,6},{6,2},{2,0},{1,5},{5,9},... | collective-permute-start | bytes 602120 | tf_op jit(solution)/shard_map/ppermute | solution.py:586
  34.2 0.5 collective-permute-start.10
  34.7 0.1 sends.9
  34.8 1.6 %collective-permute-start.13 = (bf16[768,128]{1,0:T(8,128)(2,1)S(1)}, bf16[768,128]{1,0:T(8,128)(2,1)S(1)}, u32[]{:S(2)}, u32[]{:S(2)}) collective-permute-start(bf16[768,128]{1,0:T(8,128)(2,1)S(1)} %get-tuple-element.85), channel_id=1, source_target_pairs={{0,4},{4,8},{8,12},{12,14},{14,10},{10,6},{6,2},{2,0},{1,5},{5,9},... | collective-permute-start | bytes 589832 | tf_op jit(solution)/shard_map/ppermute | solution.py:586
  36.4 0.5 collective-permute-start.14
  36.8 2.0 %cache_attention.3 = bf16[4,48,128]{2,1,0:T(8,128)(2,1)S(1)} custom-call(s32[6]{0:T(128)S(1)} %copy-done.5, s32[6]{0:T(128)S(1)} %copy-done.6, s32[1]{0:T(128)S(6)} %copy.15.stored, bf16[8,32,128]{2,1,0:T(8,128)(2,1)S(1)} %get-tuple-element.81.q.grouped, bf16[1,1024,2048]{2,1,0:T(8,128)(2,1)S(1)} %copy-done, bf16[1,2,2048]{2,1,0:T(2,128)(2,1)S(1)} %copy-done.4), custom_call_target="tpu_custom_call" | custom-call | flops 67108864 | bytes 2097152 | tf_op jit(solution)/shard_map/cache_attention/pallas_call | solution.py:485
  38.8 3.9 %project.3 = (f32[3,776,128]{2,1,0:T(8,128)S(1)}, f32[3,776,128]{2,1,0:T(8,128)S(1)}) custom-call(s32[6]{0:T(128)S(1)} %copy-done.5, bf16[3,192,2048]{2,1,0:T(8,128)(2,1)S(1)} %get-tuple-element.60.own, f32[3,8,128]{2,1,0:T(8,128)S(1)} %get-tuple-element.61.squares, bf16[3,192,2048]{2,1,0:T(8,128)(2,1)S(1)} %collective-permute-done.other, ...), custom_call_target="tpu_custom_call" | custom-call | flops 1207959552 | bytes 1048576 | tf_op jit(solution)/shard_map/project/pallas_call | solution.py:368
  42.7 0.0 collective-permute-done.10.left
  42.7 0.1 sends.10
  42.8 1.6 %collective-permute-start.11 = (bf16[784,128]{1,0:T(8,128)(2,1)S(1)}, bf16[784,128]{1,0:T(8,128)(2,1)S(1)}, u32[]{:S(2)}, u32[]{:S(2)}) collective-permute-start(bf16[784,128]{1,0:T(8,128)(2,1)S(1)} %get-tuple-element.94), channel_id=1, source_target_pairs={{0,4},{4,8},{8,12},{12,14},{14,10},{10,6},{6,2},{2,0},{1,5},{5,9},... | collective-permute-start | bytes 602120 | tf_op jit(solution)/shard_map/ppermute | solution.py:586
  44.5 0.5 collective-permute-start.12
  44.9 0.0 collective-permute-done.13.right
  44.9 0.0 collective-permute-done.14.left
  44.9 0.1 sends.11
  45.0 1.7 %collective-permute-start.15 = (bf16[768,128]{1,0:T(8,128)(2,1)S(1)}, bf16[768,128]{1,0:T(8,128)(2,1)S(1)}, u32[]{:S(2)}, u32[]{:S(2)}) collective-permute-start(bf16[768,128]{1,0:T(8,128)(2,1)S(1)} %get-tuple-element.97), channel_id=1, source_target_pairs={{0,4},{4,8},{8,12},{12,14},{14,10},{10,6},{6,2},{2,0},{1,5},{5,9},... | collective-permute-start | bytes 589832 | tf_op jit(solution)/shard_map/ppermute | solution.py:586
  46.7 0.4 collective-permute-start.16
  47.1 1.9 %all-gather = bf16[16,48,128]{2,1,0:T(8,128)(2,1)S(1)} all-gather(bf16[8,48,128]{2,1,0:T(8,128)(2,1)S(1)} %pad_maximum_fusion), channel_id=2, replica_groups=mesh['grp'=2,'tp'=8,'rep'=2] {'rep'}, dimensions={0}, use_global_device_ids=true | all-gather | bytes 294912 | tf_op jit(solution)/shard_map/all_gather | solution.py:632
  49.0 2.0 %collective-permute-done.15.right_b = bf16[768,128]{1,0:T(8,128)(2,1)S(1)} collective-permute-done((bf16[768,128]{1,0:T(8,128)(2,1)S(1)}, bf16[768,128]{1,0:T(8,128)(2,1)S(1)}, u32[]{:S(2)}, u32[]{:S(2)}) %collective-permute-start.15) | collective-permute-done | bytes 196640 | tf_op jit(solution)/shard_map/ppermute | solution.py:586
  51.0 1.4 %collective-permute-done.16.left_b = bf16[768,128]{1,0:T(8,128)(2,1)S(1)} collective-permute-done((bf16[768,128]{1,0:T(8,128)(2,1)S(1)}, bf16[768,128]{1,0:T(8,128)(2,1)S(1)}, u32[]{:S(2)}, u32[]{:S(2)}) %collective-permute-start.16) | collective-permute-done | bytes 196640 | tf_op jit(solution)/shard_map/ppermute | solution.py:586
  52.4 0.0 collective-permute-done.11.right_a
  52.4 2.0 %finish.1 = bf16[1,2,8192]{2,1,0:T(2,128)(2,1)S(1)} custom-call(s32[6]{0:T(128)S(1)} %copy-done.5, f32[2,192,128]{2,1,0:T(8,128)S(1)} %get-tuple-element.59.rotary, f32[3,776,128]{2,1,0:T(8,128)S(1)} %get-tuple-element.87.terms.own_a, f32[3,776,128]{2,1,0:T(8,128)S(1)} %get-tuple-element.93.terms.own_b, ...), custom_call_target="tpu_custom_call" | custom-call | tf_op jit(solution)/shard_map/finish/pallas_call | solution.py:547
  54.4 1.9 %all_gather.11 = bf16[1,2,16384]{2,1,0:T(2,128)(2,1)S(1)} all-gather(bf16[1,2,8192]{2,1,0:T(2,128)(2,1)S(1)} %finish.1), channel_id=1, replica_groups=mesh['grp'=2,'tp'=8,'rep'=2] {'rep'}, dimensions={2}, use_global_device_ids=true | all-gather | bytes 98304 | tf_op jit(solution)/shard_map/all_gather | solution.py:634
  56.2 0.6 %copy.16 = bf16[1,2,16384]{2,1,0:T(2,128)(2,1)} copy(bf16[1,2,16384]{2,1,0:T(2,128)(2,1)S(1)} %all_gather.11) | data formatting | bytes 131072
  (24 shorter events, 0.1 us)
Async XLA Ops:
  0.0 11.5 %collective-permute-start = (bf16[3,192,2048]{2,1,0:T(8,128)(2,1)}, bf16[3,192,2048]{2,1,0:T(8,128)(2,1)S(1)}, u32[]{:S(2)}, u32[]{:S(2)}) collective-permute-start(bf16[3,192,2048]{2,1,0:T(8,128)(2,1)} %bitcast.9), channel_id=1, source_target_pairs={{0,1},{1,0},{2,3},{3,2},{4,5},{5,4},{6,7},{7,6},{8,9},{9,8},{10,11... | collective-permute-start | bytes 7077896 | tf_op jit(solution)/shard_map/ppermute | solution.py:588
  0.5 10.2 %copy-start.6 = (s32[6]{0:T(128)S(1)}, s32[6]{0:T(128)}, u32[]{:S(2)}) copy-start(s32[6]{0:T(128)} %lengths.3) | copy-start | bytes 76
  0.5 10.3 %copy-start.7 = (f32[128]{0:T(128)S(1)}, f32[128]{0:T(128)}, u32[]{:S(2)}) copy-start(f32[128]{0:T(128)} %constant.7.clone) | copy-start | bytes 1540
  0.5 10.4 %copy-start.1 = (f32[2,192,128]{2,1,0:T(8,128)S(1)}, f32[2,192,128]{2,1,0:T(8,128)}, u32[]{:S(2)}) copy-start(f32[2,192,128]{2,1,0:T(8,128)} %constant.8.clone.turns) | copy-start | bytes 589828
  0.5 10.4 %copy-start.3 = (bf16[1,2,16384]{2,1,0:T(2,128)(2,1)S(1)}, bf16[1,2,16384]{2,1,0:T(2,128)(2,1)}, u32[]{:S(2)}) copy-start(bf16[1,2,16384]{2,1,0:T(2,128)(2,1)} %queries.1) | copy-start | bytes 196612
  0.5 10.4 %copy-start.5 = (s32[6]{0:T(128)S(1)}, s32[6]{0:T(128)}, u32[]{:S(2)}) copy-start(s32[6]{0:T(128)} %targets.8) | copy-start | bytes 76
  0.5 11.1 %copy-start.2 = (f32[2048]{0:T(1024)S(1)}, f32[2048]{0:T(1024)}, u32[]{:S(2)}) copy-start(f32[2048]{0:T(1024)} %param.14) | copy-start | bytes 24580
  14.1 7.6 %collective-permute-start.1 = (bf16[400,128]{1,0:T(8,128)(2,1)S(1)}, bf16[400,128]{1,0:T(8,128)(2,1)S(1)}, u32[]{:S(2)}, u32[]{:S(2)}) collective-permute-start(bf16[400,128]{1,0:T(8,128)(2,1)S(1)} %get-tuple-element.65), channel_id=1, source_target_pairs={{0,4},{4,8},{8,12},{12,14},{14,10},{10,6},{6,2},{2,0},{1,5},{5,9},... | collective-permute-start | bytes 307208 | tf_op jit(solution)/shard_map/ppermute | solution.py:586
  16.7 4.9 %collective-permute-start.2 = (bf16[384,128]{1,0:T(8,128)(2,1)S(1)}, bf16[384,128]{1,0:T(8,128)(2,1)S(1)}, u32[]{:S(2)}, u32[]{:S(2)}) collective-permute-start(bf16[384,128]{1,0:T(8,128)(2,1)S(1)} %get-tuple-element.66), channel_id=1, source_target_pairs={{0,2},{4,0},{8,4},{12,8},{14,12},{10,14},{6,10},{2,6},{1,3},{5,1},... | collective-permute-start | bytes 294920 | tf_op jit(solution)/shard_map/ppermute | solution.py:586
  16.7 10.9 %copy-start = (bf16[1,1024,2048]{2,1,0:T(8,128)(2,1)S(1)}, bf16[1,1024,2048]{2,1,0:T(8,128)(2,1)}, u32[]{:S(2)}) copy-start(bf16[1,1024,2048]{2,1,0:T(8,128)(2,1)} %cache.3) | copy-start | bytes 12582916
  16.7 10.9 %copy-start.4 = (bf16[1,2,2048]{2,1,0:T(2,128)(2,1)S(1)}, bf16[1,2,2048]{2,1,0:T(2,128)(2,1)}, u32[]{:S(2)}) copy-start(bf16[1,2,2048]{2,1,0:T(2,128)(2,1)} %new.3) | copy-start | bytes 24580
  18.1 6.7 %collective-permute-start.3 = (bf16[400,128]{1,0:T(8,128)(2,1)S(1)}, bf16[400,128]{1,0:T(8,128)(2,1)S(1)}, u32[]{:S(2)}, u32[]{:S(2)}) collective-permute-start(bf16[400,128]{1,0:T(8,128)(2,1)S(1)} %get-tuple-element.73), channel_id=1, source_target_pairs={{0,4},{4,8},{8,12},{12,14},{14,10},{10,6},{6,2},{2,0},{1,5},{5,9},... | collective-permute-start | bytes 307208 | tf_op jit(solution)/shard_map/ppermute | solution.py:586
  20.2 4.6 %collective-permute-start.4 = (bf16[384,128]{1,0:T(8,128)(2,1)S(1)}, bf16[384,128]{1,0:T(8,128)(2,1)S(1)}, u32[]{:S(2)}, u32[]{:S(2)}) collective-permute-start(bf16[384,128]{1,0:T(8,128)(2,1)S(1)} %get-tuple-element.74), channel_id=1, source_target_pairs={{0,2},{4,0},{8,4},{12,8},{14,12},{10,14},{6,10},{2,6},{1,3},{5,1},... | collective-permute-start | bytes 294920 | tf_op jit(solution)/shard_map/ppermute | solution.py:586
  21.7 10.8 %collective-permute-start.5 = (bf16[784,128]{1,0:T(8,128)(2,1)S(1)}, bf16[784,128]{1,0:T(8,128)(2,1)S(1)}, u32[]{:S(2)}, u32[]{:S(2)}) collective-permute-start(bf16[784,128]{1,0:T(8,128)(2,1)S(1)} %get-tuple-element.78), channel_id=1, source_target_pairs={{0,4},{4,8},{8,12},{12,14},{14,10},{10,6},{6,2},{2,0},{1,5},{5,9},... | collective-permute-start | bytes 602120 | tf_op jit(solution)/shard_map/ppermute | solution.py:586
  23.3 9.1 %collective-permute-start.6 = (bf16[784,128]{1,0:T(8,128)(2,1)S(1)}, bf16[784,128]{1,0:T(8,128)(2,1)S(1)}, u32[]{:S(2)}, u32[]{:S(2)}) collective-permute-start(bf16[784,128]{1,0:T(8,128)(2,1)S(1)} %get-tuple-element.79), channel_id=1, source_target_pairs={{0,2},{4,0},{8,4},{12,8},{14,12},{10,14},{6,10},{2,6},{1,3},{5,1},... | collective-permute-start | bytes 602120 | tf_op jit(solution)/shard_map/ppermute | solution.py:586
  24.9 9.8 %collective-permute-start.7 = (bf16[768,128]{1,0:T(8,128)(2,1)S(1)}, bf16[768,128]{1,0:T(8,128)(2,1)S(1)}, u32[]{:S(2)}, u32[]{:S(2)}) collective-permute-start(bf16[768,128]{1,0:T(8,128)(2,1)S(1)} %get-tuple-element.75), channel_id=1, source_target_pairs={{0,4},{4,8},{8,12},{12,14},{14,10},{10,6},{6,2},{2,0},{1,5},{5,9},... | collective-permute-start | bytes 589832 | tf_op jit(solution)/shard_map/ppermute | solution.py:586
  26.5 8.1 %collective-permute-start.8 = (bf16[768,128]{1,0:T(8,128)(2,1)S(1)}, bf16[768,128]{1,0:T(8,128)(2,1)S(1)}, u32[]{:S(2)}, u32[]{:S(2)}) collective-permute-start(bf16[768,128]{1,0:T(8,128)(2,1)S(1)} %get-tuple-element.84), channel_id=1, source_target_pairs={{0,2},{4,0},{8,4},{12,8},{14,12},{10,14},{6,10},{2,6},{1,3},{5,1},... | collective-permute-start | bytes 589832 | tf_op jit(solution)/shard_map/ppermute | solution.py:586
  32.6 10.2 %collective-permute-start.9 = (bf16[784,128]{1,0:T(8,128)(2,1)S(1)}, bf16[784,128]{1,0:T(8,128)(2,1)S(1)}, u32[]{:S(2)}, u32[]{:S(2)}) collective-permute-start(bf16[784,128]{1,0:T(8,128)(2,1)S(1)} %get-tuple-element.88), channel_id=1, source_target_pairs={{0,4},{4,8},{8,12},{12,14},{14,10},{10,6},{6,2},{2,0},{1,5},{5,9},... | collective-permute-start | bytes 602120 | tf_op jit(solution)/shard_map/ppermute | solution.py:586
  34.2 8.5 %collective-permute-start.10 = (bf16[784,128]{1,0:T(8,128)(2,1)S(1)}, bf16[784,128]{1,0:T(8,128)(2,1)S(1)}, u32[]{:S(2)}, u32[]{:S(2)}) collective-permute-start(bf16[784,128]{1,0:T(8,128)(2,1)S(1)} %get-tuple-element.89), channel_id=1, source_target_pairs={{0,2},{4,0},{8,4},{12,8},{14,12},{10,14},{6,10},{2,6},{1,3},{5,1},... | collective-permute-start | bytes 602120 | tf_op jit(solution)/shard_map/ppermute | solution.py:586
  34.8 10.1 %collective-permute-start.13 = (bf16[768,128]{1,0:T(8,128)(2,1)S(1)}, bf16[768,128]{1,0:T(8,128)(2,1)S(1)}, u32[]{:S(2)}, u32[]{:S(2)}) collective-permute-start(bf16[768,128]{1,0:T(8,128)(2,1)S(1)} %get-tuple-element.85), channel_id=1, source_target_pairs={{0,4},{4,8},{8,12},{12,14},{14,10},{10,6},{6,2},{2,0},{1,5},{5,9},... | collective-permute-start | bytes 589832 | tf_op jit(solution)/shard_map/ppermute | solution.py:586
  36.4 8.5 %collective-permute-start.14 = (bf16[768,128]{1,0:T(8,128)(2,1)S(1)}, bf16[768,128]{1,0:T(8,128)(2,1)S(1)}, u32[]{:S(2)}, u32[]{:S(2)}) collective-permute-start(bf16[768,128]{1,0:T(8,128)(2,1)S(1)} %get-tuple-element.96), channel_id=1, source_target_pairs={{0,2},{4,0},{8,4},{12,8},{14,12},{10,14},{6,10},{2,6},{1,3},{5,1},... | collective-permute-start | bytes 589832 | tf_op jit(solution)/shard_map/ppermute | solution.py:586
  42.8 9.6 %collective-permute-start.11 = (bf16[784,128]{1,0:T(8,128)(2,1)S(1)}, bf16[784,128]{1,0:T(8,128)(2,1)S(1)}, u32[]{:S(2)}, u32[]{:S(2)}) collective-permute-start(bf16[784,128]{1,0:T(8,128)(2,1)S(1)} %get-tuple-element.94), channel_id=1, source_target_pairs={{0,4},{4,8},{8,12},{12,14},{14,10},{10,6},{6,2},{2,0},{1,5},{5,9},... | collective-permute-start | bytes 602120 | tf_op jit(solution)/shard_map/ppermute | solution.py:586
  44.5 7.9 %collective-permute-start.12 = (bf16[784,128]{1,0:T(8,128)(2,1)S(1)}, bf16[784,128]{1,0:T(8,128)(2,1)S(1)}, u32[]{:S(2)}, u32[]{:S(2)}) collective-permute-start(bf16[784,128]{1,0:T(8,128)(2,1)S(1)} %get-tuple-element.95), channel_id=1, source_target_pairs={{0,2},{4,0},{8,4},{12,8},{14,12},{10,14},{6,10},{2,6},{1,3},{5,1},... | collective-permute-start | bytes 602120 | tf_op jit(solution)/shard_map/ppermute | solution.py:586
  45.0 6.0 %collective-permute-start.15 = (bf16[768,128]{1,0:T(8,128)(2,1)S(1)}, bf16[768,128]{1,0:T(8,128)(2,1)S(1)}, u32[]{:S(2)}, u32[]{:S(2)}) collective-permute-start(bf16[768,128]{1,0:T(8,128)(2,1)S(1)} %get-tuple-element.97), channel_id=1, source_target_pairs={{0,4},{4,8},{8,12},{12,14},{14,10},{10,6},{6,2},{2,0},{1,5},{5,9},... | collective-permute-start | bytes 589832 | tf_op jit(solution)/shard_map/ppermute | solution.py:586
  46.7 5.7 %collective-permute-start.16 = (bf16[768,128]{1,0:T(8,128)(2,1)S(1)}, bf16[768,128]{1,0:T(8,128)(2,1)S(1)}, u32[]{:S(2)}, u32[]{:S(2)}) collective-permute-start(bf16[768,128]{1,0:T(8,128)(2,1)S(1)} %get-tuple-element.98), channel_id=1, source_target_pairs={{0,2},{4,0},{8,4},{12,8},{14,12},{10,14},{6,10},{2,6},{1,3},{5,1},... | collective-permute-start | bytes 589832 | tf_op jit(solution)/shard_map/ppermute | solution.py:586

commit v8 on v7

--- a/solution.py
+++ b/solution.py
@@ -149,76 +149,112 @@
     return (scales.astype(F32) + 1.0) / 256.0 * second
 
 
+def code_tiles(table, key_codes, value_codes, scales, out_a, out_b, step):
+    begin = pl.multiple_of(step * QBLOCK, QBLOCK)
+    row = pl.ds(step, 1)
+    for at in range(CORE_HEADS):
+        lanes = slice(at * HEAD_DIM, (at + 1) * HEAD_DIM)
+        out = (out_a, out_b)[at // 2]
+        key_scale, value_scale = scales[2 * at, row, :], scales[2 * at + 1, row, :]
+        for tile in range(QBLOCK // 16):
+            rows = pl.ds(pl.multiple_of(begin + 16 * tile, 16), 16)
+            key, value = key_codes[rows, lanes], value_codes[rows, lanes]
+            keys = [gathered_levels(table, key[half : half + 8]) for half in (0, 8)]
+            values = [selected_levels(value[half : half + 8]) for half in (0, 8)]
+            keys = jnp.concatenate([level * key_scale for level in keys], axis=0)
+            values = jnp.concatenate([level * value_scale for level in values], axis=0)
+            out[at % 2, rows, :HEAD_DIM] = keys.astype(BF16)
+            out[at % 2, rows, HEAD_DIM:] = values.astype(BF16)
+
+
+def scale_prompt(x, gain, scaled, column, squares, prompt):
+    def body(step, _):
+        rows = pl.ds(pl.multiple_of(step * 16, 16), 16)
+        wide = x[prompt, rows, :].astype(F32)
+        scaled[prompt, rows, :] = (wide * gain[...]).astype(BF16)
+        total = jnp.sum(wide * wide, axis=1, keepdims=True)
+        column[rows, :] = jnp.broadcast_to(total, (16, 128))
+        return 0
+
+    lax.fori_loop(0, STRETCH // 16, body, 0)
+    squares[prompt] = token_rows(column[:, :1])
+
+
 def weights_kernel(
-    x, key_codes, value_codes, key_scales, value_scales, outer, gain,
-    out_a, out_b, scaled, squares, scales,
+    x, codes, key_scales, value_scales, outer, gain,
+    out_a, out_b, scaled, squares, key_codes, value_codes, lines, column, scales, arrivals,
 ):
-    block = pl.program_id(0)
-    depth = key_codes.shape[0]
+    per_rep = x.shape[0]
+    features, width = key_codes.shape
+    depth = min(256, features)
+    blocks = features // depth
     columns = outer.shape[0] // 2
-
-    @pl.when(block == 0)
-    def _():
-        squares[...] = jnp.zeros(squares.shape, F32)
-        for at in range(CORE_HEADS):
-            head = lax.axis_index("rep") * CORE_HEADS + at
-            column = head // (KV_HEADS // columns)
-            lanes = slice(at * HEAD_DIM, (at + 1) * HEAD_DIM)
-            scales[2 * at] = block_scales(key_scales[:, lanes], outer[...], column)
-            scales[2 * at + 1] = block_scales(value_scales[:, lanes], outer[...], columns + column)
-
+    rep = lax.axis_index("rep")
+
+    def code_copies(block):
+        rows = pl.ds(block * depth, depth)
+        return [
+            pltpu.make_async_copy(
+                codes.at[rows, pl.ds(pl.multiple_of((2 * kind + rep) * width, width), width)],
+                buffer.at[rows],
+                arrivals.at[2 * block + kind],
+            )
+            for kind, buffer in enumerate((key_codes, value_codes))
+        ]
+
+    def line_copy(prompt):
+        return pltpu.make_async_copy(
+            x.at[prompt], lines.at[prompt], arrivals.at[2 * blocks + prompt]
+        )
+
+    shares = [range(per_rep * at // blocks, per_rep * (at + 1) // blocks) for at in range(blocks)]
+    for block in range(blocks):
+        for copy in code_copies(block):
+            copy.start()
+        for prompt in shares[block]:
+            line_copy(prompt).start()
+
+    for at in range(CORE_HEADS):
+        column_at = (rep * CORE_HEADS + at) // (KV_HEADS // columns)
+        lanes = slice(at * HEAD_DIM, (at + 1) * HEAD_DIM)
+        scales[2 * at] = block_scales(key_scales[:, lanes], outer[...], column_at)
+        scales[2 * at + 1] = block_scales(value_scales[:, lanes], outer[...], columns + column_at)
     lane = lax.broadcasted_iota(jnp.int32, (8, 128), 1)
     table = jnp.zeros((8, 128), F32)
     for code, level in enumerate(NORMAL_FLOAT_LEVELS):
         table = jnp.where(lane == code, level, table)
 
     def body(step, _):
-        begin = pl.multiple_of(step * QBLOCK, QBLOCK)
-        row = pl.ds(block * (depth // QBLOCK) + step, 1)
-        for at in range(CORE_HEADS):
-            lanes = slice(at * HEAD_DIM, (at + 1) * HEAD_DIM)
-            out = (out_a, out_b)[at // 2]
-            key_scale, value_scale = scales[2 * at, row, :], scales[2 * at + 1, row, :]
-            for tile in range(QBLOCK // 16):
-                rows = pl.ds(pl.multiple_of(begin + 16 * tile, 16), 16)
-                key, value = key_codes[rows, lanes], value_codes[rows, lanes]
-                keys = [gathered_levels(table, key[half : half + 8]) for half in (0, 8)]
-                values = [selected_levels(value[half : half + 8]) for half in (0, 8)]
-                rows = pl.ds(pl.multiple_of(block * depth + begin + 16 * tile, 16), 16)
-                keys = jnp.concatenate([level * key_scale for level in keys], axis=0)
-                values = jnp.concatenate([level * value_scale for level in values], axis=0)
-                out[at % 2, rows, :HEAD_DIM] = keys.astype(BF16)
-                out[at % 2, rows, HEAD_DIM:] = values.astype(BF16)
+        code_tiles(table, key_codes, value_codes, scales, out_a, out_b, step)
         return 0
 
-    lax.fori_loop(0, depth // QBLOCK, body, 0)
-
-    width = x.shape[2]
-    begin = pl.multiple_of(block * width, 128)
-    for prompt in range(x.shape[0]):
-        wide = x[prompt].astype(F32)
-        scaled[prompt, :, pl.ds(begin, width)] = (wide * gain[...]).astype(BF16)
-        squares[prompt] += token_rows(jnp.sum(wide * wide, axis=1, keepdims=True))
+    steps = depth // QBLOCK
+    for block in range(blocks):
+        for copy in code_copies(block):
+            copy.wait()
+        lax.fori_loop(block * steps, (block + 1) * steps, body, 0)
+        for prompt in shares[block]:
+            line_copy(prompt).wait()
+            scale_prompt(lines, gain, scaled, column, squares, prompt)
 
 
 def dequantize(x, codes, scales, outer, gain):
     per_rep, _, features = x.shape
-    depth = min(256, features)
     width = CORE_HEADS * HEAD_DIM
+    blocks = features // min(256, features)
     rep = lambda: lax.axis_index("rep")
     x, codes, scales, outer, gain = in_hbm(x, codes, scales, outer, gain)
     weight = jax.ShapeDtypeStruct((2, features, 2 * HEAD_DIM), BF16)
     return pl.pallas_call(
         weights_kernel,
-        grid=(features // depth,),
+        grid=(1,),
         in_specs=[
-            pl.BlockSpec((per_rep, STRETCH, depth), lambda k: (0, 0, k)),
-            pl.BlockSpec((depth, width), lambda k: (k, rep())),
-            pl.BlockSpec((depth, width), lambda k: (k, 2 + rep())),
+            pl.BlockSpec(memory_space=pltpu.HBM),
+            pl.BlockSpec(memory_space=pltpu.HBM),
             pl.BlockSpec((scales.shape[0], width), lambda k: (0, rep())),
             pl.BlockSpec((scales.shape[0], width), lambda k: (0, 2 + rep())),
             pl.BlockSpec(outer.shape, lambda k: (0, 0)),
-            pl.BlockSpec((1, depth), lambda k: (0, k)),
+            pl.BlockSpec(gain.shape, lambda k: (0, 0)),
         ],
         out_specs=[VMEM] * 4,
         out_shape=[
@@ -227,13 +263,20 @@
             jax.ShapeDtypeStruct(x.shape, BF16),
             jax.ShapeDtypeStruct((per_rep, 8, 128), F32),
         ],
-        scratch_shapes=[pltpu.VMEM((2 * CORE_HEADS, scales.shape[0], HEAD_DIM), F32)],
-        compiler_params=pltpu.CompilerParams(vmem_limit_bytes=32 * MIB),
+        scratch_shapes=[
+            pltpu.VMEM((features, width), jnp.int32),
+            pltpu.VMEM((features, width), jnp.int32),
+            pltpu.VMEM(x.shape, BF16),
+            pltpu.VMEM((STRETCH, 128), F32),
+            pltpu.VMEM((2 * CORE_HEADS, scales.shape[0], HEAD_DIM), F32),
+            pltpu.SemaphoreType.DMA((2 * blocks + per_rep,)),
+        ],
+        compiler_params=pltpu.CompilerParams(vmem_limit_bytes=36 * MIB),
         cost_estimate=pl.CostEstimate(
             flops=32 * codes.size, bytes_accessed=codes.size * 2, transcendentals=0
         ),
         name="dequantize",
-    )(x, codes, codes, scales, scales, outer, gain)
+    )(x, codes, scales, scales, outer, gain)
 
 
 def prompt_of(targets, owner):

time: 57.5 us -> 59.2 us (1.030)
  Pallas kernels: 27.9 us -> 29.4 us
    ppermute x8, starting transfers between devices: 14.6 us -> 16.4 us  [pass_on(): lax.ppermute(right, 'tp', to_right)]
    ppermute x8, starting transfers between devices: 2.63 us -> 1.03 us  [pass_on(): lax.ppermute(left, 'tp', to_left)]
    pallas_call x1, Pallas kernels: 10.2 us -> 11.7 us  [dequantize(): pl.pallas_call(weights_kernel, grid=(1,), in_specs=[pl.BlockSpec(memory_s...]
  transfers between devices with their start and end apart: 17 -> 17, of which waited for: 4 -> 4; matrix products, arithmetic and copies ran while one was open for 0% -> 0% of each run, Pallas kernels for 41% -> 42%
where the time goes in v8:
time: 59.2 us; the launch traced here: 58.7 us
  Pallas kernels  29.4 us (50%)
  starting transfers between devices  17.9 us (30%)
  waiting for transfers between devices  5.94 us (10%)
  blocking collectives  3.8 us (6%)
  between operations  0.89 us (2%)
  local copies, waits for them, and re-layouts  0.66 us (1%)
    ppermute x8, starting transfers between devices, pass_on(): lax.ppermute(right, 'tp', to_right)  16.4 us
    pallas_call x1, Pallas kernels, dequantize(): pl.pallas_call(weights_kernel, grid=(1,), in_specs=[pl.BlockSpec(memory_s...  11.7 us
    pallas_call x2, Pallas kernels, project(): pl.pallas_call(functools.partial(project_kernel, distances), in_specs=[SM...  6.64 us
    ppermute x8, waiting for transfers between devices, pass_on(): lax.ppermute(left, 'tp', to_left)  4.23 us
    pallas_call x2, Pallas kernels, cache_attention(): pl.pallas_call(functools.partial(cache_kernel, part), in_specs=[SMEM] * 3...  3.97 us
    pallas_call x1, Pallas kernels, project_first(): pl.pallas_call(functools.partial(first_kernel, distances), in_specs=[SMEM...  2.47 us
    pallas_call x1, Pallas kernels, finish(): pl.pallas_call(final_kernel, in_specs=[SMEM] + [VMEM] * 9, out_specs=VMEM...  1.98 us
    all_gather x1, blocking collectives, per_device(): cached = lax.all_gather(jnp.concatenate(cached), 'rep')  1.95 us
  transfers between devices with their start and end apart: 17, of which 4 were waited for; matrix products, arithmetic and copies ran while one was open for 0% of the time, Pallas kernels for 42%

profile of v8, /device:TPU:0, one launch (start us, length us, event | category | flops | bytes accessed | tf_op | source)
XLA Modules:
  0.0 58.7 jit_solution(9779229912414328363)
XLA Ops:
  0.0 0.5 collective-permute-start
  0.5 11.7 %dequantize.1 = (bf16[2,2048,256]{2,1,0:T(8,128)(2,1)S(1)}, bf16[2,2048,256]{2,1,0:T(8,128)(2,1)S(1)}, bf16[3,192,2048]{2,1,0:T(8,128)(2,1)S(1)}, f32[3,8,128]{2,1,0:T(8,128)S(1)}) custom-call(bf16[3,192,2048]{2,1,0:T(8,128)(2,1)} %bitcast.10, s32[2048,2048]{1,0:T(8,128)} %codes.1, s32[32,2048]{1,0:T(8,128)} %value_scales.1, s32[32,2048]{1,0:T(8,128)} %value_scales.1, ...), custom_call_target="tpu_custom_call" | custom-call | flops 134217728 | bytes 8388608 | tf_op jit(solution)/shard_map/dequantize/pallas_call | solution.py:248
  12.2 0.1 multiply_cosine_fusion
  12.4 0.7 %prepare.1 = (bf16[8,32,128]{2,1,0:T(8,128)(2,1)S(1)}, f32[2,192,128]{2,1,0:T(8,128)S(1)}) custom-call(s32[6]{0:T(128)S(1)} %copy-done.5, bf16[1,2,16384]{2,1,0:T(2,128)(2,1)S(1)} %copy-done.3, f32[2,6,128]{2,1,0:T(8,128)S(1)} %pad_maximum_fusion.1.starts, f32[2,192,128]{2,1,0:T(8,128)S(1)} %copy-done.1), custom_call_target="tpu_custom_call" | custom-call | tf_op jit(solution)/shard_map/prepare/pallas_call | solution.py:471
  13.1 0.0 collective-permute-done.other
  13.1 2.5 %project_first.1 = (bf16[400,128]{1,0:T(8,128)(2,1)S(1)}, bf16[384,128]{1,0:T(8,128)(2,1)S(1)}, f32[2,776,128]{2,1,0:T(8,128)S(1)}, bf16[576,2048]{1,0:T(8,128)(2,1)S(1)}, f32[3,8,128]{2,1,0:T(8,128)S(1)}) custom-call(s32[6]{0:T(128)S(1)} %copy-done.5, bf16[3,192,2048]{2,1,0:T(8,128)(2,1)S(1)} %get-tuple-element.60.own, ...), custom_call_target="tpu_custom_call" | custom-call | flops 1207959552 | bytes 1048576 | tf_op jit(solution)/shard_map/project_first/pallas_call | solution.py:366
  15.6 2.7 %collective-permute-start.1 = (bf16[400,128]{1,0:T(8,128)(2,1)S(1)}, bf16[400,128]{1,0:T(8,128)(2,1)S(1)}, u32[]{:S(2)}, u32[]{:S(2)}) collective-permute-start(bf16[400,128]{1,0:T(8,128)(2,1)S(1)} %get-tuple-element.65), channel_id=1, source_target_pairs={{0,4},{4,8},{8,12},{12,14},{14,10},{10,6},{6,2},{2,0},{1,5},{5,9},... | collective-permute-start | bytes 307208 | tf_op jit(solution)/shard_map/ppermute | solution.py:629
  18.2 0.0 collective-permute-start.2
  18.2 1.4 %project_second.1 = (bf16[400,128]{1,0:T(8,128)(2,1)S(1)}, bf16[384,128]{1,0:T(8,128)(2,1)S(1)}, f32[2,776,128]{2,1,0:T(8,128)S(1)}) custom-call(bf16[576,2048]{1,0:T(8,128)(2,1)S(1)} %get-tuple-element.68.lines, f32[3,8,128]{2,1,0:T(8,128)S(1)} %get-tuple-element.69.totals, bf16[2,2048,256]{2,1,0:T(8,128)(2,1)S(1)} %get-tuple-element.70.weight.weight_b), custom_call_target="tpu_custom_call" | custom-call | flops 1207959552 | bytes 1048576 | tf_op jit(solution)/shard_map/project_second/pallas_call | solution.py:378
  19.6 2.1 %collective-permute-start.3 = (bf16[400,128]{1,0:T(8,128)(2,1)S(1)}, bf16[400,128]{1,0:T(8,128)(2,1)S(1)}, u32[]{:S(2)}, u32[]{:S(2)}) collective-permute-start(bf16[400,128]{1,0:T(8,128)(2,1)S(1)} %get-tuple-element.73), channel_id=1, source_target_pairs={{0,4},{4,8},{8,12},{12,14},{14,10},{10,6},{6,2},{2,0},{1,5},{5,9},... | collective-permute-start | bytes 307208 | tf_op jit(solution)/shard_map/ppermute | solution.py:629
  21.7 0.0 collective-permute-start.4
  21.7 1.4 %collective-permute-done.2.left = bf16[384,128]{1,0:T(8,128)(2,1)S(1)} collective-permute-done((bf16[384,128]{1,0:T(8,128)(2,1)S(1)}, bf16[384,128]{1,0:T(8,128)(2,1)S(1)}, u32[]{:S(2)}, u32[]{:S(2)}) %collective-permute-start.2) | collective-permute-done | bytes 98336 | tf_op jit(solution)/shard_map/ppermute | solution.py:629
  23.1 0.0 collective-permute-done.1.right
  23.1 0.1 sends.6
  23.2 1.6 %collective-permute-start.5 = (bf16[784,128]{1,0:T(8,128)(2,1)S(1)}, bf16[784,128]{1,0:T(8,128)(2,1)S(1)}, u32[]{:S(2)}, u32[]{:S(2)}) collective-permute-start(bf16[784,128]{1,0:T(8,128)(2,1)S(1)} %get-tuple-element.78), channel_id=1, source_target_pairs={{0,4},{4,8},{8,12},{12,14},{14,10},{10,6},{6,2},{2,0},{1,5},{5,9},... | collective-permute-start | bytes 602120 | tf_op jit(solution)/shard_map/ppermute | solution.py:629
  24.8 0.4 collective-permute-start.6
  25.3 1.0 %collective-permute-done.4.left = bf16[384,128]{1,0:T(8,128)(2,1)S(1)} collective-permute-done((bf16[384,128]{1,0:T(8,128)(2,1)S(1)}, bf16[384,128]{1,0:T(8,128)(2,1)S(1)}, u32[]{:S(2)}, u32[]{:S(2)}) %collective-permute-start.4) | collective-permute-done | bytes 98336 | tf_op jit(solution)/shard_map/ppermute | solution.py:629
  26.3 0.1 sends.7
  26.4 2.1 %collective-permute-start.7 = (bf16[768,128]{1,0:T(8,128)(2,1)S(1)}, bf16[768,128]{1,0:T(8,128)(2,1)S(1)}, u32[]{:S(2)}, u32[]{:S(2)}) collective-permute-start(bf16[768,128]{1,0:T(8,128)(2,1)S(1)} %get-tuple-element.75), channel_id=1, source_target_pairs={{0,4},{4,8},{8,12},{12,14},{14,10},{10,6},{6,2},{2,0},{1,5},{5,9},... | collective-permute-start | bytes 589832 | tf_op jit(solution)/shard_map/ppermute | solution.py:629
  28.4 0.0 collective-permute-start.8
  29.1 2.0 %cache_attention.2 = bf16[4,48,128]{2,1,0:T(8,128)(2,1)S(1)} custom-call(s32[6]{0:T(128)S(1)} %copy-done.5, s32[6]{0:T(128)S(1)} %copy-done.6, s32[1]{0:T(128)S(6)} %copy.15.stored, bf16[8,32,128]{2,1,0:T(8,128)(2,1)S(1)} %get-tuple-element.81.q.grouped, bf16[1,1024,2048]{2,1,0:T(8,128)(2,1)S(1)} %copy-done, bf16[1,2,2048]{2,1,0:T(2,128)(2,1)S(1)} %copy-done.4), custom_call_target="tpu_custom_call" | custom-call | flops 67108864 | bytes 2097152 | tf_op jit(solution)/shard_map/cache_attention/pallas_call | solution.py:528
  31.1 2.5 %project.2 = (f32[2,776,128]{2,1,0:T(8,128)S(1)}, f32[2,776,128]{2,1,0:T(8,128)S(1)}) custom-call(s32[6]{0:T(128)S(1)} %copy-done.5, bf16[3,192,2048]{2,1,0:T(8,128)(2,1)S(1)} %get-tuple-element.60.own, f32[3,8,128]{2,1,0:T(8,128)S(1)} %get-tuple-element.61.squares, bf16[3,192,2048]{2,1,0:T(8,128)(2,1)S(1)} %collective-permute-done.other, ...), custom_call_target="tpu_custom_call" | custom-call | flops 805306368 | bytes 1048576 | tf_op jit(solution)/shard_map/project/pallas_call | solution.py:411
  33.6 0.0 collective-permute-done.5.right
  33.6 0.0 collective-permute-done.6.left
  33.7 0.1 sends.8
  33.8 2.3 %collective-permute-start.9 = (bf16[784,128]{1,0:T(8,128)(2,1)S(1)}, bf16[784,128]{1,0:T(8,128)(2,1)S(1)}, u32[]{:S(2)}, u32[]{:S(2)}) collective-permute-start(bf16[784,128]{1,0:T(8,128)(2,1)S(1)} %get-tuple-element.88), channel_id=1, source_target_pairs={{0,4},{4,8},{8,12},{12,14},{14,10},{10,6},{6,2},{2,0},{1,5},{5,9},... | collective-permute-start | bytes 602120 | tf_op jit(solution)/shard_map/ppermute | solution.py:629
  36.1 0.0 collective-permute-start.10
  36.1 0.0 collective-permute-done.7.right
  36.1 0.0 collective-permute-done.8.left
  36.1 0.1 sends.9
  36.2 2.1 %collective-permute-start.13 = (bf16[768,128]{1,0:T(8,128)(2,1)S(1)}, bf16[768,128]{1,0:T(8,128)(2,1)S(1)}, u32[]{:S(2)}, u32[]{:S(2)}) collective-permute-start(bf16[768,128]{1,0:T(8,128)(2,1)S(1)} %get-tuple-element.85), channel_id=1, source_target_pairs={{0,4},{4,8},{8,12},{12,14},{14,10},{10,6},{6,2},{2,0},{1,5},{5,9},... | collective-permute-start | bytes 589832 | tf_op jit(solution)/shard_map/ppermute | solution.py:629
  38.3 0.0 collective-permute-start.14
  38.3 2.0 %cache_attention.3 = bf16[4,48,128]{2,1,0:T(8,128)(2,1)S(1)} custom-call(s32[6]{0:T(128)S(1)} %copy-done.5, s32[6]{0:T(128)S(1)} %copy-done.6, s32[1]{0:T(128)S(6)} %copy.15.stored, bf16[8,32,128]{2,1,0:T(8,128)(2,1)S(1)} %get-tuple-element.81.q.grouped, bf16[1,1024,2048]{2,1,0:T(8,128)(2,1)S(1)} %copy-done, bf16[1,2,2048]{2,1,0:T(2,128)(2,1)S(1)} %copy-done.4), custom_call_target="tpu_custom_call" | custom-call | flops 67108864 | bytes 2097152 | tf_op jit(solution)/shard_map/cache_attention/pallas_call | solution.py:528
  40.3 4.1 %project.3 = (f32[3,776,128]{2,1,0:T(8,128)S(1)}, f32[3,776,128]{2,1,0:T(8,128)S(1)}) custom-call(s32[6]{0:T(128)S(1)} %copy-done.5, bf16[3,192,2048]{2,1,0:T(8,128)(2,1)S(1)} %get-tuple-element.60.own, f32[3,8,128]{2,1,0:T(8,128)S(1)} %get-tuple-element.61.squares, bf16[3,192,2048]{2,1,0:T(8,128)(2,1)S(1)} %collective-permute-done.other, ...), custom_call_target="tpu_custom_call" | custom-call | flops 1207959552 | bytes 1048576 | tf_op jit(solution)/shard_map/project/pallas_call | solution.py:411
  44.4 0.0 collective-permute-done.9.right
  44.4 0.0 collective-permute-done.10.left
  44.4 0.1 sends.10
  44.5 1.8 %collective-permute-start.11 = (bf16[784,128]{1,0:T(8,128)(2,1)S(1)}, bf16[784,128]{1,0:T(8,128)(2,1)S(1)}, u32[]{:S(2)}, u32[]{:S(2)}) collective-permute-start(bf16[784,128]{1,0:T(8,128)(2,1)S(1)} %get-tuple-element.94), channel_id=1, source_target_pairs={{0,4},{4,8},{8,12},{12,14},{14,10},{10,6},{6,2},{2,0},{1,5},{5,9},... | collective-permute-start | bytes 602120 | tf_op jit(solution)/shard_map/ppermute | solution.py:629
  46.4 0.3 collective-permute-start.12
  46.6 0.1 sends.11
  46.7 1.8 %collective-permute-start.15 = (bf16[768,128]{1,0:T(8,128)(2,1)S(1)}, bf16[768,128]{1,0:T(8,128)(2,1)S(1)}, u32[]{:S(2)}, u32[]{:S(2)}) collective-permute-start(bf16[768,128]{1,0:T(8,128)(2,1)S(1)} %get-tuple-element.97), channel_id=1, source_target_pairs={{0,4},{4,8},{8,12},{12,14},{14,10},{10,6},{6,2},{2,0},{1,5},{5,9},... | collective-permute-start | bytes 589832 | tf_op jit(solution)/shard_map/ppermute | solution.py:629
  48.5 0.3 collective-permute-start.16
  48.8 1.9 %all-gather = bf16[16,48,128]{2,1,0:T(8,128)(2,1)S(1)} all-gather(bf16[8,48,128]{2,1,0:T(8,128)(2,1)S(1)} %pad_maximum_fusion), channel_id=2, replica_groups=mesh['grp'=2,'tp'=8,'rep'=2] {'rep'}, dimensions={0}, use_global_device_ids=true | all-gather | bytes 294912 | tf_op jit(solution)/shard_map/all_gather | solution.py:675
  50.8 1.7 %collective-permute-done.15.right_b = bf16[768,128]{1,0:T(8,128)(2,1)S(1)} collective-permute-done((bf16[768,128]{1,0:T(8,128)(2,1)S(1)}, bf16[768,128]{1,0:T(8,128)(2,1)S(1)}, u32[]{:S(2)}, u32[]{:S(2)}) %collective-permute-start.15) | collective-permute-done | bytes 196640 | tf_op jit(solution)/shard_map/ppermute | solution.py:629
  52.5 1.8 %collective-permute-done.16.left_b = bf16[768,128]{1,0:T(8,128)(2,1)S(1)} collective-permute-done((bf16[768,128]{1,0:T(8,128)(2,1)S(1)}, bf16[768,128]{1,0:T(8,128)(2,1)S(1)}, u32[]{:S(2)}, u32[]{:S(2)}) %collective-permute-start.16) | collective-permute-done | bytes 196640 | tf_op jit(solution)/shard_map/ppermute | solution.py:629
  54.2 2.0 %finish.1 = bf16[1,2,8192]{2,1,0:T(2,128)(2,1)S(1)} custom-call(s32[6]{0:T(128)S(1)} %copy-done.5, f32[2,192,128]{2,1,0:T(8,128)S(1)} %get-tuple-element.59.rotary, f32[3,776,128]{2,1,0:T(8,128)S(1)} %get-tuple-element.87.terms.own_a, f32[3,776,128]{2,1,0:T(8,128)S(1)} %get-tuple-element.93.terms.own_b, ...), custom_call_target="tpu_custom_call" | custom-call | tf_op jit(solution)/shard_map/finish/pallas_call | solution.py:590
  56.2 1.9 %all_gather.11 = bf16[1,2,16384]{2,1,0:T(2,128)(2,1)S(1)} all-gather(bf16[1,2,8192]{2,1,0:T(2,128)(2,1)S(1)} %finish.1), channel_id=1, replica_groups=mesh['grp'=2,'tp'=8,'rep'=2] {'rep'}, dimensions={2}, use_global_device_ids=true | all-gather | bytes 98304 | tf_op jit(solution)/shard_map/all_gather | solution.py:677
  58.1 0.6 %copy.16 = bf16[1,2,16384]{2,1,0:T(2,128)(2,1)} copy(bf16[1,2,16384]{2,1,0:T(2,128)(2,1)S(1)} %all_gather.11) | data formatting | bytes 131072
  (24 shorter events, 0.1 us)
Async XLA Ops:
  0.0 13.1 %collective-permute-start = (bf16[3,192,2048]{2,1,0:T(8,128)(2,1)}, bf16[3,192,2048]{2,1,0:T(8,128)(2,1)S(1)}, u32[]{:S(2)}, u32[]{:S(2)}) collective-permute-start(bf16[3,192,2048]{2,1,0:T(8,128)(2,1)} %bitcast.9), channel_id=1, source_target_pairs={{0,1},{1,0},{2,3},{3,2},{4,5},{5,4},{6,7},{7,6},{8,9},{9,8},{10,11... | collective-permute-start | bytes 7077896 | tf_op jit(solution)/shard_map/ppermute | solution.py:631
  0.5 11.7 %copy-start.6 = (s32[6]{0:T(128)S(1)}, s32[6]{0:T(128)}, u32[]{:S(2)}) copy-start(s32[6]{0:T(128)} %lengths.3) | copy-start | bytes 76
  0.5 11.8 %copy-start.7 = (f32[128]{0:T(128)S(1)}, f32[128]{0:T(128)}, u32[]{:S(2)}) copy-start(f32[128]{0:T(128)} %constant.7.clone) | copy-start | bytes 1540
  0.5 11.9 %copy-start.1 = (f32[2,192,128]{2,1,0:T(8,128)S(1)}, f32[2,192,128]{2,1,0:T(8,128)}, u32[]{:S(2)}) copy-start(f32[2,192,128]{2,1,0:T(8,128)} %constant.8.clone.turns) | copy-start | bytes 589828
  0.5 11.9 %copy-start.3 = (bf16[1,2,16384]{2,1,0:T(2,128)(2,1)S(1)}, bf16[1,2,16384]{2,1,0:T(2,128)(2,1)}, u32[]{:S(2)}) copy-start(bf16[1,2,16384]{2,1,0:T(2,128)(2,1)} %queries.1) | copy-start | bytes 196612
  0.5 11.9 %copy-start.5 = (s32[6]{0:T(128)S(1)}, s32[6]{0:T(128)}, u32[]{:S(2)}) copy-start(s32[6]{0:T(128)} %targets.8) | copy-start | bytes 76
  0.5 12.6 %copy-start.2 = (f32[2048]{0:T(1024)S(1)}, f32[2048]{0:T(1024)}, u32[]{:S(2)}) copy-start(f32[2048]{0:T(1024)} %param.14) | copy-start | bytes 24580
  15.6 7.6 %collective-permute-start.1 = (bf16[400,128]{1,0:T(8,128)(2,1)S(1)}, bf16[400,128]{1,0:T(8,128)(2,1)S(1)}, u32[]{:S(2)}, u32[]{:S(2)}) collective-permute-start(bf16[400,128]{1,0:T(8,128)(2,1)S(1)} %get-tuple-element.65), channel_id=1, source_target_pairs={{0,4},{4,8},{8,12},{12,14},{14,10},{10,6},{6,2},{2,0},{1,5},{5,9},... | collective-permute-start | bytes 307208 | tf_op jit(solution)/shard_map/ppermute | solution.py:629
  18.2 4.9 %collective-permute-start.2 = (bf16[384,128]{1,0:T(8,128)(2,1)S(1)}, bf16[384,128]{1,0:T(8,128)(2,1)S(1)}, u32[]{:S(2)}, u32[]{:S(2)}) collective-permute-start(bf16[384,128]{1,0:T(8,128)(2,1)S(1)} %get-tuple-element.66), channel_id=1, source_target_pairs={{0,2},{4,0},{8,4},{12,8},{14,12},{10,14},{6,10},{2,6},{1,3},{5,1},... | collective-permute-start | bytes 294920 | tf_op jit(solution)/shard_map/ppermute | solution.py:629
  18.2 10.9 %copy-start = (bf16[1,1024,2048]{2,1,0:T(8,128)(2,1)S(1)}, bf16[1,1024,2048]{2,1,0:T(8,128)(2,1)}, u32[]{:S(2)}) copy-start(bf16[1,1024,2048]{2,1,0:T(8,128)(2,1)} %cache.3) | copy-start | bytes 12582916
  18.2 10.9 %copy-start.4 = (bf16[1,2,2048]{2,1,0:T(2,128)(2,1)S(1)}, bf16[1,2,2048]{2,1,0:T(2,128)(2,1)}, u32[]{:S(2)}) copy-start(bf16[1,2,2048]{2,1,0:T(2,128)(2,1)} %new.3) | copy-start | bytes 24580
  19.6 6.7 %collective-permute-start.3 = (bf16[400,128]{1,0:T(8,128)(2,1)S(1)}, bf16[400,128]{1,0:T(8,128)(2,1)S(1)}, u32[]{:S(2)}, u32[]{:S(2)}) collective-permute-start(bf16[400,128]{1,0:T(8,128)(2,1)S(1)} %get-tuple-element.73), channel_id=1, source_target_pairs={{0,4},{4,8},{8,12},{12,14},{14,10},{10,6},{6,2},{2,0},{1,5},{5,9},... | collective-permute-start | bytes 307208 | tf_op jit(solution)/shard_map/ppermute | solution.py:629
  21.7 4.6 %collective-permute-start.4 = (bf16[384,128]{1,0:T(8,128)(2,1)S(1)}, bf16[384,128]{1,0:T(8,128)(2,1)S(1)}, u32[]{:S(2)}, u32[]{:S(2)}) collective-permute-start(bf16[384,128]{1,0:T(8,128)(2,1)S(1)} %get-tuple-element.74), channel_id=1, source_target_pairs={{0,2},{4,0},{8,4},{12,8},{14,12},{10,14},{6,10},{2,6},{1,3},{5,1},... | collective-permute-start | bytes 294920 | tf_op jit(solution)/shard_map/ppermute | solution.py:629
  23.2 10.5 %collective-permute-start.5 = (bf16[784,128]{1,0:T(8,128)(2,1)S(1)}, bf16[784,128]{1,0:T(8,128)(2,1)S(1)}, u32[]{:S(2)}, u32[]{:S(2)}) collective-permute-start(bf16[784,128]{1,0:T(8,128)(2,1)S(1)} %get-tuple-element.78), channel_id=1, source_target_pairs={{0,4},{4,8},{8,12},{12,14},{14,10},{10,6},{6,2},{2,0},{1,5},{5,9},... | collective-permute-start | bytes 602120 | tf_op jit(solution)/shard_map/ppermute | solution.py:629
  24.8 8.8 %collective-permute-start.6 = (bf16[784,128]{1,0:T(8,128)(2,1)S(1)}, bf16[784,128]{1,0:T(8,128)(2,1)S(1)}, u32[]{:S(2)}, u32[]{:S(2)}) collective-permute-start(bf16[784,128]{1,0:T(8,128)(2,1)S(1)} %get-tuple-element.79), channel_id=1, source_target_pairs={{0,2},{4,0},{8,4},{12,8},{14,12},{10,14},{6,10},{2,6},{1,3},{5,1},... | collective-permute-start | bytes 602120 | tf_op jit(solution)/shard_map/ppermute | solution.py:629
  26.4 9.7 %collective-permute-start.7 = (bf16[768,128]{1,0:T(8,128)(2,1)S(1)}, bf16[768,128]{1,0:T(8,128)(2,1)S(1)}, u32[]{:S(2)}, u32[]{:S(2)}) collective-permute-start(bf16[768,128]{1,0:T(8,128)(2,1)S(1)} %get-tuple-element.75), channel_id=1, source_target_pairs={{0,4},{4,8},{8,12},{12,14},{14,10},{10,6},{6,2},{2,0},{1,5},{5,9},... | collective-permute-start | bytes 589832 | tf_op jit(solution)/shard_map/ppermute | solution.py:629
  28.4 7.7 %collective-permute-start.8 = (bf16[768,128]{1,0:T(8,128)(2,1)S(1)}, bf16[768,128]{1,0:T(8,128)(2,1)S(1)}, u32[]{:S(2)}, u32[]{:S(2)}) collective-permute-start(bf16[768,128]{1,0:T(8,128)(2,1)S(1)} %get-tuple-element.84), channel_id=1, source_target_pairs={{0,2},{4,0},{8,4},{12,8},{14,12},{10,14},{6,10},{2,6},{1,3},{5,1},... | collective-permute-start | bytes 589832 | tf_op jit(solution)/shard_map/ppermute | solution.py:629
  33.8 10.7 %collective-permute-start.9 = (bf16[784,128]{1,0:T(8,128)(2,1)S(1)}, bf16[784,128]{1,0:T(8,128)(2,1)S(1)}, u32[]{:S(2)}, u32[]{:S(2)}) collective-permute-start(bf16[784,128]{1,0:T(8,128)(2,1)S(1)} %get-tuple-element.88), channel_id=1, source_target_pairs={{0,4},{4,8},{8,12},{12,14},{14,10},{10,6},{6,2},{2,0},{1,5},{5,9},... | collective-permute-start | bytes 602120 | tf_op jit(solution)/shard_map/ppermute | solution.py:629
  36.1 8.3 %collective-permute-start.10 = (bf16[784,128]{1,0:T(8,128)(2,1)S(1)}, bf16[784,128]{1,0:T(8,128)(2,1)S(1)}, u32[]{:S(2)}, u32[]{:S(2)}) collective-permute-start(bf16[784,128]{1,0:T(8,128)(2,1)S(1)} %get-tuple-element.89), channel_id=1, source_target_pairs={{0,2},{4,0},{8,4},{12,8},{14,12},{10,14},{6,10},{2,6},{1,3},{5,1},... | collective-permute-start | bytes 602120 | tf_op jit(solution)/shard_map/ppermute | solution.py:629
  36.2 10.4 %collective-permute-start.13 = (bf16[768,128]{1,0:T(8,128)(2,1)S(1)}, bf16[768,128]{1,0:T(8,128)(2,1)S(1)}, u32[]{:S(2)}, u32[]{:S(2)}) collective-permute-start(bf16[768,128]{1,0:T(8,128)(2,1)S(1)} %get-tuple-element.85), channel_id=1, source_target_pairs={{0,4},{4,8},{8,12},{12,14},{14,10},{10,6},{6,2},{2,0},{1,5},{5,9},... | collective-permute-start | bytes 589832 | tf_op jit(solution)/shard_map/ppermute | solution.py:629
  38.3 8.4 %collective-permute-start.14 = (bf16[768,128]{1,0:T(8,128)(2,1)S(1)}, bf16[768,128]{1,0:T(8,128)(2,1)S(1)}, u32[]{:S(2)}, u32[]{:S(2)}) collective-permute-start(bf16[768,128]{1,0:T(8,128)(2,1)S(1)} %get-tuple-element.96), channel_id=1, source_target_pairs={{0,2},{4,0},{8,4},{12,8},{14,12},{10,14},{6,10},{2,6},{1,3},{5,1},... | collective-permute-start | bytes 589832 | tf_op jit(solution)/shard_map/ppermute | solution.py:629
  44.5 9.7 %collective-permute-start.11 = (bf16[784,128]{1,0:T(8,128)(2,1)S(1)}, bf16[784,128]{1,0:T(8,128)(2,1)S(1)}, u32[]{:S(2)}, u32[]{:S(2)}) collective-permute-start(bf16[784,128]{1,0:T(8,128)(2,1)S(1)} %get-tuple-element.94), channel_id=1, source_target_pairs={{0,4},{4,8},{8,12},{12,14},{14,10},{10,6},{6,2},{2,0},{1,5},{5,9},... | collective-permute-start | bytes 602120 | tf_op jit(solution)/shard_map/ppermute | solution.py:629
  46.4 7.9 %collective-permute-start.12 = (bf16[784,128]{1,0:T(8,128)(2,1)S(1)}, bf16[784,128]{1,0:T(8,128)(2,1)S(1)}, u32[]{:S(2)}, u32[]{:S(2)}) collective-permute-start(bf16[784,128]{1,0:T(8,128)(2,1)S(1)} %get-tuple-element.95), channel_id=1, source_target_pairs={{0,2},{4,0},{8,4},{12,8},{14,12},{10,14},{6,10},{2,6},{1,3},{5,1},... | collective-permute-start | bytes 602120 | tf_op jit(solution)/shard_map/ppermute | solution.py:629
  46.7 5.7 %collective-permute-start.15 = (bf16[768,128]{1,0:T(8,128)(2,1)S(1)}, bf16[768,128]{1,0:T(8,128)(2,1)S(1)}, u32[]{:S(2)}, u32[]{:S(2)}) collective-permute-start(bf16[768,128]{1,0:T(8,128)(2,1)S(1)} %get-tuple-element.97), channel_id=1, source_target_pairs={{0,4},{4,8},{8,12},{12,14},{14,10},{10,6},{6,2},{2,0},{1,5},{5,9},... | collective-permute-start | bytes 589832 | tf_op jit(solution)/shard_map/ppermute | solution.py:629
  48.5 5.7 %collective-permute-start.16 = (bf16[768,128]{1,0:T(8,128)(2,1)S(1)}, bf16[768,128]{1,0:T(8,128)(2,1)S(1)}, u32[]{:S(2)}, u32[]{:S(2)}) collective-permute-start(bf16[768,128]{1,0:T(8,128)(2,1)S(1)} %get-tuple-element.98), channel_id=1, source_target_pairs={{0,2},{4,0},{8,4},{12,8},{14,12},{10,14},{6,10},{2,6},{1,3},{5,1},... | collective-permute-start | bytes 589832 | tf_op jit(solution)/shard_map/ppermute | solution.py:629

commit v9 on v7

--- a/solution.py
+++ b/solution.py
@@ -53,20 +53,6 @@
     return [pltpu.with_memory_space_constraint(array, pltpu.HBM) for array in arrays]
 
 
-def ring_device(place, count):
-    half = count // 2
-    if isinstance(place, int):
-        return 2 * place if place < half else 2 * (count - 1 - place) + 1
-    return jnp.where(place < half, 2 * place, 2 * (count - 1 - place) + 1)
-
-
-def owner_at(distance):
-    count = lax.axis_size("tp")
-    here = lax.axis_index("tp")
-    place = jnp.where(here % 2 == 0, here // 2, count - 1 - here // 2)
-    return ring_device((place + distance + count) % count, count)
-
-
 def turned(column):
     rows = lax.broadcasted_iota(jnp.int32, (column.shape[0], 128), 0)
     lanes = lax.broadcasted_iota(jnp.int32, (column.shape[0], 128), 1)
@@ -87,16 +73,6 @@
 
 def token_column(rows):
     return jnp.concatenate([stood(rows[0:1], 128), stood(rows[1:2], STRETCH - 128)], axis=0)
-
-
-def two_pieces(rows):
-    high = rows.astype(BF16).astype(F32)
-    return jnp.concatenate([high, rows - high], axis=0).astype(BF16)
-
-
-def one_piece(rows):
-    rows = rows.astype(F32)
-    return rows[:8] + rows[8:]
 
 
 def pieces_tail(logs):
@@ -107,6 +83,16 @@
     at = lax.broadcasted_iota(jnp.int32, (TAIL, 128), 0)
     tail = jnp.where(at == 0, high, jnp.where(at == 1, middle, jnp.where(at == 2, low, 0.0)))
     return tail.astype(BF16)
+
+
+def two_pieces(rows):
+    high = rows.astype(BF16).astype(F32)
+    return jnp.concatenate([high, rows - high], axis=0).astype(BF16)
+
+
+def one_piece(rows):
+    rows = rows.astype(F32)
+    return rows[:8] + rows[8:]
 
 
 def tail_pieces(tail):
@@ -243,9 +229,9 @@
     return prompt
 
 
-def lines_of(targets, distance, own, squares, other, gain, line, total):
+def lines_of(targets, owner, own, squares, other, gain, line, total):
     per_rep = own.shape[0]
-    prompt = prompt_of(targets, owner_at(distance))
+    prompt = prompt_of(targets, owner)
     at = lax.rem(jnp.maximum(prompt, 0), per_rep)
     is_own = prompt // per_rep == lax.axis_index("rep")
 
@@ -273,141 +259,65 @@
     ]
 
 
-def first_kernel(distances, targets, own, squares, other, gain, weight, *refs):
-    right, left, terms, lines, totals = refs
-    for item, distance in enumerate(distances):
+def owners_kernel(targets, own, squares, other, gain, weight, out, lines, totals):
+    together = out.shape[0]
+    for item in range(together):
         line = lines.at[item * STRETCH : (item + 1) * STRETCH]
-        lines_of(targets, distance, own, squares, other, gain, line, totals.at[item])
-    products(distances, lines, totals, weight, right, left, terms)
-
-
-def second_kernel(distances, lines, totals, weight, *refs):
-    products(distances, lines, totals, weight, *refs)
-
-
-def products(distances, lines, totals, weight, right, left, terms):
+        owner = pl.program_id(0) * together + item
+        lines_of(targets, owner, own, squares, other, gain, line, totals.at[item])
+    products(lines, weight, out)
+
+
+def again_kernel(lines, weight, out):
+    products(lines, weight, out)
+
+
+def products(lines, weight, out):
     for head in range(2):
-        product = jnp.dot(lines[...], weight[head], preferred_element_type=F32)
-        rows = slice(head * STRETCH, (head + 1) * STRETCH)
-        right[rows] = product[:STRETCH, :HEAD_DIM].astype(BF16)
-        left[rows] = product[:STRETCH, HEAD_DIM:].astype(BF16)
-        for item in range(1, len(distances)):
+        product = jnp.dot(lines[...], weight[head], preferred_element_type=F32).astype(BF16)
+        for item in range(out.shape[0]):
             part = product[item * STRETCH : (item + 1) * STRETCH]
             begin = head * STRETCH
-            terms[item - 1, begin : begin + STRETCH] = part[:, :HEAD_DIM]
+            out[item, begin : begin + STRETCH] = part[:, :HEAD_DIM]
             begin += 2 * STRETCH
-            terms[item - 1, begin : begin + STRETCH] = part[:, HEAD_DIM:]
-    for item in range(1, len(distances)):
-        terms[item - 1, 4 * STRETCH :] = totals[item]
-    right[2 * STRETCH :] = two_pieces(totals[0])
-
-
-def first_shapes(distances):
-    rows = 2 * STRETCH
-    return [
-        jax.ShapeDtypeStruct((rows + TAIL, HEAD_DIM), BF16),
-        jax.ShapeDtypeStruct((rows, HEAD_DIM), BF16),
-        jax.ShapeDtypeStruct((len(distances) - 1, 2 * rows + 8, HEAD_DIM), F32),
-    ]
-
-
-def project_cost(distances, weight):
-    return pl.CostEstimate(
-        flops=len(distances) * STRETCH * weight.size * 2,
-        bytes_accessed=weight.size,
-        transcendentals=0,
-    )
-
-
-def project_first(distances, targets, own, squares, other, gain, weight):
+            out[item, begin : begin + STRETCH] = part[:, HEAD_DIM:]
+
+
+TOGETHER = 4
+
+
+def project_owners(count, targets, own, squares, other, gain, weight):
+    features = own.shape[2]
     return pl.pallas_call(
-        functools.partial(first_kernel, distances),
+        owners_kernel,
+        grid=(count // TOGETHER,),
         in_specs=[SMEM] + [VMEM] * 5,
-        out_specs=[VMEM] * 5,
-        out_shape=first_shapes(distances) + line_specs(distances, own),
-        compiler_params=pltpu.CompilerParams(vmem_limit_bytes=24 * MIB),
-        cost_estimate=project_cost(distances, weight),
-        name="project_first",
+        out_specs=[
+            pl.BlockSpec((TOGETHER, 4 * STRETCH, HEAD_DIM), lambda i: (i, 0, 0)),
+            pl.BlockSpec((TOGETHER * STRETCH, features), lambda i: (i, 0)),
+            pl.BlockSpec((TOGETHER, 8, 128), lambda i: (i, 0, 0)),
+        ],
+        out_shape=[
+            jax.ShapeDtypeStruct((count, 4 * STRETCH, HEAD_DIM), BF16),
+            jax.ShapeDtypeStruct((count * STRETCH, features), BF16),
+            jax.ShapeDtypeStruct((count, 8, 128), F32),
+        ],
+        compiler_params=pltpu.CompilerParams(vmem_limit_bytes=32 * MIB),
+        name="project_owners",
     )(targets, own, squares, other, gain, weight)
 
 
-def project_second(distances, lines, totals, weight):
+def project_again(count, lines, weight):
+    features = lines.shape[1]
     return pl.pallas_call(
-        functools.partial(second_kernel, distances),
-        in_specs=[VMEM] * 3,
-        out_specs=[VMEM] * 3,
-        out_shape=first_shapes(distances),
-        compiler_params=pltpu.CompilerParams(vmem_limit_bytes=24 * MIB),
-        cost_estimate=project_cost(distances, weight),
-        name="project_second",
-    )(lines, totals, weight)
-
-
-def project_kernel(
-    distances, targets, own, squares, other, gain, weight_a, weight_b, out_a, out_b, lines, totals
-):
-    for item, distance in enumerate(distances):
-        line = lines.at[item * STRETCH : (item + 1) * STRETCH]
-        lines_of(targets, distance, own, squares, other, gain, line, totals.at[item])
-    for weight, out in ((weight_a, out_a), (weight_b, out_b)):
-        for head in range(2):
-            product = jnp.dot(lines[...], weight[head], preferred_element_type=F32)
-            for item in range(len(distances)):
-                part = product[item * STRETCH : (item + 1) * STRETCH]
-                begin = head * STRETCH
-                out[item, begin : begin + STRETCH] = part[:, :HEAD_DIM]
-                begin += 2 * STRETCH
-                out[item, begin : begin + STRETCH] = part[:, HEAD_DIM:]
-        for item in range(len(distances)):
-            out[item, 4 * STRETCH :] = totals[item]
-
-
-def project(distances, targets, own, squares, other, gain, weights):
-    shape = jax.ShapeDtypeStruct((len(distances), 4 * STRETCH + 8, HEAD_DIM), F32)
-    line, total = line_specs(distances, own)
-    return pl.pallas_call(
-        functools.partial(project_kernel, distances),
-        in_specs=[SMEM] + [VMEM] * 6,
-        out_specs=[VMEM] * 2,
-        out_shape=[shape, shape],
-        scratch_shapes=[pltpu.VMEM(line.shape, BF16), pltpu.VMEM(total.shape, F32)],
-        compiler_params=pltpu.CompilerParams(vmem_limit_bytes=24 * MIB),
-        cost_estimate=project_cost(distances, weights[0]),
-        name="project",
-    )(targets, own, squares, other, gain, *weights)
-
-
-def send_kernel(half, first, terms, right, left, to_right, to_left):
-    rows = 4 * STRETCH
-    middle = 2 * STRETCH
-    if first:
-        to_right[:middle] = (terms[0, :middle] + right[:middle].astype(F32)).astype(BF16)
-        to_right[middle:rows] = terms[0, middle:rows].astype(BF16)
-        to_left[:middle] = terms[1, :middle].astype(BF16)
-        to_left[middle:rows] = (terms[1, middle:rows] + left[...].astype(F32)).astype(BF16)
-    else:
-        to_right[:rows] = (terms[0, :rows] + right[:rows].astype(F32)).astype(BF16)
-        to_left[:rows] = (terms[1, :rows] + left[:rows].astype(F32)).astype(BF16)
-    if half == 0:
-        right_sum, left_sum = terms[0, rows:], terms[1, rows:]
-        right_sum += one_piece(right[middle if first else rows :])
-        if not first:
-            left_sum += one_piece(left[rows:])
-        to_right[rows:] = two_pieces(right_sum)
-        to_left[rows:] = two_pieces(left_sum)
-
-
-def sends(half, first, terms, right, left):
-    rows = 4 * STRETCH + (TAIL if half == 0 else 0)
-    shape = jax.ShapeDtypeStruct((rows, HEAD_DIM), BF16)
-    return pl.pallas_call(
-        functools.partial(send_kernel, half, first),
-        in_specs=[VMEM] * 3,
-        out_specs=[VMEM] * 2,
-        out_shape=[shape, shape],
-        compiler_params=pltpu.CompilerParams(vmem_limit_bytes=16 * MIB),
-        name="sends",
-    )(terms, right, left)
+        again_kernel,
+        grid=(count // TOGETHER,),
+        in_specs=[pl.BlockSpec((TOGETHER * STRETCH, features), lambda i: (i, 0)), VMEM],
+        out_specs=pl.BlockSpec((TOGETHER, 4 * STRETCH, HEAD_DIM), lambda i: (i, 0, 0)),
+        out_shape=jax.ShapeDtypeStruct((count, 4 * STRETCH, HEAD_DIM), BF16),
+        compiler_params=pltpu.CompilerParams(vmem_limit_bytes=32 * MIB),
+        name="project_again",
+    )(lines, weight)
 
 
 def prepare_kernel(targets, queries, starts, turns, grouped, rotary):
@@ -497,26 +407,18 @@
     )(targets, lengths, stored, grouped, kv_cache, new_kv)
 
 
-def final_kernel(
-    targets, rotary, own_a, own_b, right_a, left_a, right_b, left_b, grouped, *refs
-):
-    cached, out = refs
+def final_kernel(targets, rotary, squares, summed_a, summed_b, grouped, cached, out):
     scaling = HEAD_DIM ** (-0.5)
     dims = (((1,), (1,)), ((), ()))
-    mine = own_a.shape[0] - 1
-    rep = lax.axis_index("rep")
-    first = rep * CORE_HEADS
+    first = lax.axis_index("rep") * CORE_HEADS
     prompt = prompt_of(targets, lax.axis_index("tp"))
     cosine, sine = rotary[0], rotary[1]
-    rows = 4 * STRETCH
-    squares = own_a[mine, rows:] + one_piece(right_a[rows:]) + one_piece(left_a[rows:])
+    squares = squares[lax.axis_index("tp")]
     scale = token_column(lax.rsqrt(squares / D + EPSILON))
     for head in range(CORE_HEADS):
-        own, right, left = ((own_a, right_a, left_a), (own_b, right_b, left_b))[head // 2]
-        at = slice(head % 2 * STRETCH, (head % 2 + 1) * STRETCH)
-        keys = own[mine, at] + right[at].astype(F32) + left[at].astype(F32)
-        at = slice((2 + head % 2) * STRETCH, (3 + head % 2) * STRETCH)
-        values = own[mine, at] + right[at].astype(F32) + left[at].astype(F32)
+        summed = (summed_a, summed_b)[head // 2]
+        keys = summed[head % 2 * STRETCH : (head % 2 + 1) * STRETCH].astype(F32)
+        values = summed[(2 + head % 2) * STRETCH : (3 + head % 2) * STRETCH].astype(F32)
         keys = (keys * scale).astype(BF16).astype(F32)
         values = (values * scale).astype(BF16)
         keys = keys * cosine + pltpu.roll(keys, HEAD_DIM // 2, 1) * sine
@@ -542,16 +444,16 @@
             out[0, :, begin : begin + HEAD_DIM] = result[member * STEPS : (member + 1) * STEPS]
 
 
-def finish(targets, rotary, own, arrived, grouped, cached):
+def finish(targets, rotary, squares, summed, grouped, cached):
     width = CORE_HEADS * GROUP * HEAD_DIM
     return pl.pallas_call(
         final_kernel,
-        in_specs=[SMEM] + [VMEM] * 9,
+        in_specs=[SMEM] + [VMEM] * 6,
         out_specs=VMEM,
         out_shape=jax.ShapeDtypeStruct((1, STEPS, width), BF16),
         compiler_params=pltpu.CompilerParams(vmem_limit_bytes=16 * MIB),
         name="finish",
-    )(targets, rotary, *own, *arrived, grouped, cached)
+    )(targets, rotary, squares, *summed, grouped, cached)
 
 
 def rotary_turns():
@@ -575,15 +477,12 @@
     new_kv,
 ):
     count = lax.axis_size("tp")
-    half = count // 2
     lines = stretch.transpose(1, 0, 2)
     gain = norm_gain.reshape(1, -1)
-    ring = [ring_device(at, count) for at in range(count)]
-    to_right = [(ring[at], ring[(at + 1) % count]) for at in range(count)]
-    to_left = [(ring[at], ring[at - 1]) for at in range(count)]
-
-    def pass_on(right, left):
-        return lax.ppermute(right, "tp", to_right), lax.ppermute(left, "tp", to_left)
+
+    def scatter(array):
+        flat = array.reshape(-1, array.shape[2])
+        return lax.psum_scatter(flat, "tp", scatter_dimension=0, tiled=True)
 
     other = lax.ppermute(lines, "rep", [(0, 1), (1, 0)])
     first_half, second_half, own, squares = dequantize(
@@ -595,42 +494,26 @@
     targets, second_half = lax.optimization_barrier((target_rows, second_half))
     grouped, rotary = prepare(targets, queries, starts, jnp.asarray(turns))
 
-    gain, second_half, grouped, rotary = lax.optimization_barrier(
-        (gain, second_half, grouped, rotary)
+    gain, grouped, rotary = lax.optimization_barrier((gain, grouped, rotary))
+    sums, lines, squares = project_owners(
+        count, target_rows, own, squares, other, gain, first_half
     )
-    distances = [half, half - 1, 1 - half]
-    right, left, terms_a, lines_here, totals = project_first(
-        distances, target_rows, own, squares, other, gain, first_half
-    )
-    arrived = [pass_on(right, left), None]
-    right, left, terms_b = project_second(distances, lines_here, totals, second_half)
-    arrived[1] = pass_on(right, left)
-    terms = [terms_a, terms_b]
-
-    targets = target_rows
-    cached = []
-    for distance in range(half - 1, 0, -1):
-        if distance < half - 1:
-            distances = [distance, -distance] + ([0] if distance == 1 else [])
-            terms = list(
-                project(distances, targets, own, squares, other, gain, [first_half, second_half])
-            )
-        for part in range(2):
-            right, left = sends(part, distance == half - 1, terms[part], *arrived[part])
-            if part == 0:
-                right, cached, terms[1] = lax.optimization_barrier((right, cached, terms[1]))
-            targets, _ = lax.optimization_barrier((target_rows, right))
-            arrived[part] = pass_on(right, left)
-        if distance in (2, 3):
-            cached.append(
-                cache_attention(
-                    3 - distance, targets, prompt_lengths, cache_lengths, grouped, kv_cache, new_kv
-                )
-            )
-
-    cached, _ = lax.optimization_barrier((cached, right))
+    summed = [scatter(sums)]
+    sums = project_again(count, lines, second_half)
+    sums, squares, targets = lax.optimization_barrier((sums, squares, target_rows))
+    summed.append(scatter(sums))
+    cached = [
+        cache_attention(
+            part, targets, prompt_lengths, cache_lengths, grouped, kv_cache, new_kv
+        )
+        for part in range(2)
+    ]
+    step = 1
+    while step < count:
+        squares += lax.ppermute(squares, "tp", [(at, at ^ step) for at in range(count)])
+        step *= 2
     cached = lax.all_gather(jnp.concatenate(cached), "rep")
-    out = finish(target_rows, rotary, terms, [*arrived[0], *arrived[1]], grouped, cached)
+    out = finish(target_rows, rotary, squares, summed, grouped, cached)
     return lax.all_gather(out, "rep", axis=2, tiled=True)
 
 

time: 57.5 us -> 179 us (3.11)
  waiting for transfers between devices: 5.83 us -> 121 us
  between operations: 0.89 us -> 14.2 us
  starting transfers between devices: 17.6 us -> 7.11 us
  local copies, waits for them, and re-layouts: 0.66 us -> 4.69 us
    reduce_scatter x0 -> x2, waiting for transfers between devices: none -> 115 us  [scatter(): return lax.psum_scatter(flat, 'tp', scatter_dimension=0, tiled=True)]
    ppermute x16 -> x3, starting transfers between devices: 17.2 us -> 6.61 us  [per_device(): lax.ppermute(squares, 'tp', [(at, at ^ step) for at in range(count)])]
    unnamed x17 -> x21, local copies, waits for them, and re-layouts: 0.66 us -> 4.69 us
    ppermute x16 -> x3, waiting for transfers between devices: 5.83 us -> 5.28 us  [per_device(): lax.ppermute(squares, 'tp', [(at, at ^ step) for at in range(count)])]
    pallas_call x11 -> x3, Pallas kernels: 13.1 us -> 13.1 us  [the longest x1 6.62 us: project_owners(): pl.pallas_call(owners_kernel, grid=(count // TOGETHER,), in_specs=[SMEM]...]
  transfers between devices with their start and end apart: 17 -> 6, of which waited for: 4 -> 4; matrix products, arithmetic and copies ran while one was open for 0% -> 0% of each run, Pallas kernels for 41% -> 8%
where the time goes in v9:
time: 179 us
  waiting for transfers between devices  121 us (68%)
  Pallas kernels  27.9 us (16%)
  between operations  14.2 us (8%)
  starting transfers between devices  7.11 us (4%)
  local copies, waits for them, and re-layouts  4.69 us (3%)
  blocking collectives  3.79 us (2%)
    reduce_scatter x2, waiting for transfers between devices, scatter(): return lax.psum_scatter(flat, 'tp', scatter_dimension=0, tiled=True)  115 us
    pallas_call x1, Pallas kernels, dequantize(): pl.pallas_call(weights_kernel, grid=(features // depth,), in_specs=[pl.Bl...  10.2 us
    pallas_call x1, Pallas kernels, project_owners(): pl.pallas_call(owners_kernel, grid=(count // TOGETHER,), in_specs=[SMEM]...  6.62 us
    ppermute x3, starting transfers between devices, per_device(): lax.ppermute(squares, 'tp', [(at, at ^ step) for at in range(count)])  6.61 us
    ppermute x3, waiting for transfers between devices, per_device(): lax.ppermute(squares, 'tp', [(at, at ^ step) for at in range(count)])  5.28 us
    unnamed x21, local copies, waits for them, and re-layouts  4.69 us
    pallas_call x1, Pallas kernels, project_again(): pl.pallas_call(again_kernel, grid=(count // TOGETHER,), in_specs=[pl.Bloc...  4.52 us
    pallas_call x2, Pallas kernels, cache_attention(): pl.pallas_call(functools.partial(cache_kernel, part), in_specs=[SMEM] * 3...  3.97 us
  transfers between devices with their start and end apart: 6, of which 4 were waited for; matrix products, arithmetic and copies ran while one was open for 0% of the time, Pallas kernels for 8%

profile of v9, /device:TPU:0, one launch (start us, length us, event | category | flops | bytes accessed | tf_op | source)
XLA Modules:
  0.0 178.5 jit_solution(12549015495313480351)
XLA Ops:
  6.5 0.0 reduce-scatter.5.cloned.1.call-start
  6.5 0.5 collective-permute-start
  7.0 0.0 copy-start.8
  7.0 0.0 copy-start.9
  7.0 0.0 copy-start.1
  7.0 0.0 copy-start.4
  7.0 0.0 copy-start.7
  7.0 0.0 copy-start.6
  7.0 10.2 %dequantize.1 = (bf16[2,2048,256]{2,1,0:T(8,128)(2,1)S(1)}, bf16[2,2048,256]{2,1,0:T(8,128)(2,1)S(1)}, bf16[3,192,2048]{2,1,0:T(8,128)(2,1)S(1)}, f32[3,8,128]{2,1,0:T(8,128)S(1)}) custom-call(bf16[3,192,2048]{2,1,0:T(8,128)(2,1)} %bitcast.10, s32[2048,2048]{1,0:T(8,128)} %value_codes.1, s32[2048,2048]{1,0:T(8,128)} %value_codes.1, s32[32,2048]{1,0:T(8,128)} %value_scales.1, ...), custom_call_target="tpu_custom_call" | custom-call | flops 134217728 | bytes 8388608 | tf_op jit(solution)/shard_map/dequantize/pallas_call | solution.py:197
  17.2 0.0 copy-done.8
  17.2 0.0 copy-done.9
  17.3 0.1 multiply_cosine_fusion
  17.4 0.0 copy-done.1
  17.4 0.0 copy-done.4
  17.4 0.0 copy-done.7
  17.4 0.7 prepare.1
  18.1 0.0 collective-permute-done.other
  18.1 0.0 copy-done.6
  18.1 6.6 %project_owners.1 = (bf16[8,768,128]{2,1,0:T(8,128)(2,1)}, bf16[1536,2048]{1,0:T(8,128)(2,1)S(1)}, f32[8,8,128]{2,1,0:T(8,128)S(1)}) custom-call(s32[6]{0:T(128)S(1)} %copy-done.7, bf16[3,192,2048]{2,1,0:T(8,128)(2,1)S(1)} %get-tuple-element.27.own, f32[3,8,128]{2,1,0:T(8,128)S(1)} %get-tuple-element.28.squares, ...), custom_call_target="tpu_custom_call" | custom-call | tf_op jit(solution)/shard_map/project_owners/pallas_call | solution.py:291
  24.7 4.5 %project_again.1 = bf16[8,768,128]{2,1,0:T(8,128)(2,1)} custom-call(bf16[1536,2048]{1,0:T(8,128)(2,1)S(1)} %get-tuple-element.31.lines, bf16[2,2048,256]{2,1,0:T(8,128)(2,1)S(1)} %get-tuple-element.32.weight), custom_call_target="tpu_custom_call" | custom-call | tf_op jit(solution)/shard_map/project_again/pallas_call | solution.py:312
  29.2 0.0 copy-start.5
  29.2 0.0 reduce-scatter.5.cloned.1.call-update
  29.3 0.0 reduce-scatter.3.cloned.1.call-start
  29.3 0.7 reduce-scatter.3.cloned.1.call-update
  30.0 2.6 %collective-permute-start.1 = (f32[8,8,128]{2,1,0:T(8,128)S(1)}, f32[8,8,128]{2,1,0:T(8,128)S(1)}, u32[]{:S(2)}, u32[]{:S(2)}) collective-permute-start(f32[8,8,128]{2,1,0:T(8,128)S(1)} %get-tuple-element.34), channel_id=1, source_target_pairs={{0,2},{2,0},{4,6},{6,4},{8,10},{10,8},{12,14},{14,12},{1,3},{3,1},... | collective-permute-start | bytes 98312 | tf_op jit(solution)/shard_map/ppermute | solution.py:513
  33.2 0.0 copy-done.5
  33.2 0.0 copy-start
  33.3 2.2 %copy-done = bf16[1,1024,2048]{2,1,0:T(8,128)(2,1)S(1)} copy-done((bf16[1,1024,2048]{2,1,0:T(8,128)(2,1)S(1)}, bf16[1,1024,2048]{2,1,0:T(8,128)(2,1)}, u32[]{:S(2)}) %copy-start) | copy-done | bytes 4194328
  35.4 2.0 %cache_attention.2 = bf16[4,48,128]{2,1,0:T(8,128)(2,1)S(1)} custom-call(s32[6]{0:T(128)S(1)} %copy-done.7, s32[6]{0:T(128)S(1)} %copy-done.8, s32[1]{0:T(128)S(6)} %copy.15.stored, bf16[8,32,128]{2,1,0:T(8,128)(2,1)S(1)} %get-tuple-element.37.q.grouped, bf16[1,1024,2048]{2,1,0:T(8,128)(2,1)S(1)} %copy-done, bf16[1,2,2048]{2,1,0:T(2,128)(2,1)S(1)} %copy-done.5), custom_call_target="tpu_custom_call" | custom-call | flops 67108864 | bytes 2097152 | tf_op jit(solution)/shard_map/cache_attention/pallas_call | solution.py:395
  37.4 2.0 %cache_attention.3 = bf16[4,48,128]{2,1,0:T(8,128)(2,1)S(1)} custom-call(s32[6]{0:T(128)S(1)} %copy-done.7, s32[6]{0:T(128)S(1)} %copy-done.8, s32[1]{0:T(128)S(6)} %copy.15.stored, bf16[8,32,128]{2,1,0:T(8,128)(2,1)S(1)} %get-tuple-element.37.q.grouped, bf16[1,1024,2048]{2,1,0:T(8,128)(2,1)S(1)} %copy-done, bf16[1,2,2048]{2,1,0:T(2,128)(2,1)S(1)} %copy-done.5), custom_call_target="tpu_custom_call" | custom-call | flops 67108864 | bytes 2097152 | tf_op jit(solution)/shard_map/cache_attention/pallas_call | solution.py:395
  39.4 0.0 collective-permute-done.1
  39.4 1.6 collective-permute-start.2
  41.1 2.7 %collective-permute-done.2 = f32[8,8,128]{2,1,0:T(8,128)S(1)} collective-permute-done((f32[8,8,128]{2,1,0:T(8,128)S(1)}, f32[8,8,128]{2,1,0:T(8,128)S(1)}, u32[]{:S(2)}, u32[]{:S(2)}) %collective-permute-start.2) | collective-permute-done | bytes 32800 | tf_op jit(solution)/shard_map/ppermute | solution.py:513
  43.8 2.4 %collective-permute-start.3 = (f32[8,8,128]{2,1,0:T(8,128)S(1)}, f32[8,8,128]{2,1,0:T(8,128)S(1)}, u32[]{:S(2)}, u32[]{:S(2)}) collective-permute-start(f32[8,8,128]{2,1,0:T(8,128)S(1)} %add.15), channel_id=1, source_target_pairs={{0,8},{2,10},{4,12},{6,14},{8,0},{10,2},{12,4},{14,6},{1,9},{3,11}... | collective-permute-start | bytes 98312 | tf_op jit(solution)/shard_map/ppermute | solution.py:513
  46.2 1.9 %all-gather = bf16[16,48,128]{2,1,0:T(8,128)(2,1)S(1)} all-gather(bf16[8,48,128]{2,1,0:T(8,128)(2,1)S(1)} %pad_maximum_fusion), channel_id=2, replica_groups=mesh['grp'=2,'tp'=8,'rep'=2] {'rep'}, dimensions={0}, use_global_device_ids=true | all-gather | bytes 294912 | tf_op jit(solution)/shard_map/all_gather | solution.py:515
  48.1 2.6 %collective-permute-done.3 = f32[8,8,128]{2,1,0:T(8,128)S(1)} collective-permute-done((f32[8,8,128]{2,1,0:T(8,128)S(1)}, f32[8,8,128]{2,1,0:T(8,128)S(1)}, u32[]{:S(2)}, u32[]{:S(2)}) %collective-permute-start.3) | collective-permute-done | bytes 32800 | tf_op jit(solution)/shard_map/ppermute | solution.py:513
  50.7 47.1 %reduce-scatter.5.cloned.1.call-done.summed_b = bf16[768,128]{1,0:T(8,128)(2,1)} async-done(((bf16[6144,128]{1,0:T(8,128)(2,1)}), bf16[768,128]{1,0:T(8,128)(2,1)}) %reduce-scatter.5.cloned.1.call-update) | async-done | bytes 196624 | tf_op jit(solution)/shard_map/reduce_scatter | solution.py:485
  97.8 67.5 %reduce-scatter.3.cloned.1.call-done.summed_a = bf16[768,128]{1,0:T(8,128)(2,1)} async-done(((bf16[6144,128]{1,0:T(8,128)(2,1)}), bf16[768,128]{1,0:T(8,128)(2,1)}) %reduce-scatter.3.cloned.1.call-update) | async-done | bytes 196624 | tf_op jit(solution)/shard_map/reduce_scatter | solution.py:485
  165.4 0.0 copy-start.2
  165.4 0.9 copy-done.2
  166.3 0.0 copy-start.3
  166.3 0.9 copy-done.3
  167.2 2.0 %finish.1 = bf16[1,2,8192]{2,1,0:T(2,128)(2,1)S(1)} custom-call(s32[6]{0:T(128)S(1)} %copy-done.7, f32[2,192,128]{2,1,0:T(8,128)S(1)} %get-tuple-element.26.rotary, f32[8,8,128]{2,1,0:T(8,128)S(1)} %add.16.squares, bf16[768,128]{1,0:T(8,128)(2,1)S(1)} %copy-done.3, bf16[768,128]{1,0:T(8,128)(2,1)S(1)} %copy-done.2, ...), custom_call_target="tpu_custom_call" | custom-call | tf_op jit(solution)/shard_map/finish/pallas_call | solution.py:449
  169.2 1.9 %all_gather.11 = bf16[1,2,16384]{2,1,0:T(2,128)(2,1)S(1)} all-gather(bf16[1,2,8192]{2,1,0:T(2,128)(2,1)S(1)} %finish.1), channel_id=1, replica_groups=mesh['grp'=2,'tp'=8,'rep'=2] {'rep'}, dimensions={2}, use_global_device_ids=true | all-gather | bytes 98304 | tf_op jit(solution)/shard_map/all_gather | solution.py:517
  171.0 0.6 copy.16
  (6 shorter events, 0.0 us)
Async XLA Ops:
  6.5 91.3 %reduce-scatter.5.cloned.1.call-start = ((), (), s32[]{:S(2)}) async-start(), calls=%async_computation.3 | async-start | bytes 1769472 | tf_op jit(solution)/shard_map/reduce_scatter | solution.py:485
  6.5 11.5 %collective-permute-start = (bf16[3,192,2048]{2,1,0:T(8,128)(2,1)}, bf16[3,192,2048]{2,1,0:T(8,128)(2,1)S(1)}, u32[]{:S(2)}, u32[]{:S(2)}) collective-permute-start(bf16[3,192,2048]{2,1,0:T(8,128)(2,1)} %bitcast.9), channel_id=1, source_target_pairs={{0,1},{1,0},{2,3},{3,2},{4,5},{5,4},{6,7},{7,6},{8,9},{9,8},{10,11... | collective-permute-start | bytes 7077896 | tf_op jit(solution)/shard_map/ppermute | solution.py:487
  7.0 10.2 %copy-start.8 = (s32[6]{0:T(128)S(1)}, s32[6]{0:T(128)}, u32[]{:S(2)}) copy-start(s32[6]{0:T(128)} %lengths.3) | copy-start | bytes 76
  7.0 10.3 %copy-start.9 = (f32[128]{0:T(128)S(1)}, f32[128]{0:T(128)}, u32[]{:S(2)}) copy-start(f32[128]{0:T(128)} %constant.7.clone) | copy-start | bytes 1540
  7.0 10.4 %copy-start.1 = (f32[2,192,128]{2,1,0:T(8,128)S(1)}, f32[2,192,128]{2,1,0:T(8,128)}, u32[]{:S(2)}) copy-start(f32[2,192,128]{2,1,0:T(8,128)} %constant.8.clone.turns) | copy-start | bytes 589828
  7.0 10.4 %copy-start.4 = (bf16[1,2,16384]{2,1,0:T(2,128)(2,1)S(1)}, bf16[1,2,16384]{2,1,0:T(2,128)(2,1)}, u32[]{:S(2)}) copy-start(bf16[1,2,16384]{2,1,0:T(2,128)(2,1)} %queries.1) | copy-start | bytes 196612
  7.0 10.4 %copy-start.7 = (s32[6]{0:T(128)S(1)}, s32[6]{0:T(128)}, u32[]{:S(2)}) copy-start(s32[6]{0:T(128)} %targets.6) | copy-start | bytes 76
  7.0 11.1 %copy-start.6 = (f32[2048]{0:T(1024)S(1)}, f32[2048]{0:T(1024)}, u32[]{:S(2)}) copy-start(f32[2048]{0:T(1024)} %param.14) | copy-start | bytes 24580
  29.2 4.0 %copy-start.5 = (bf16[1,2,2048]{2,1,0:T(2,128)(2,1)S(1)}, bf16[1,2,2048]{2,1,0:T(2,128)(2,1)}, u32[]{:S(2)}) copy-start(bf16[1,2,2048]{2,1,0:T(2,128)(2,1)} %new.3) | copy-start | bytes 24580
  29.3 136.1 %reduce-scatter.3.cloned.1.call-start = ((), (), s32[]{:S(2)}) async-start(), calls=%async_computation.2 | async-start | bytes 1769472 | tf_op jit(solution)/shard_map/reduce_scatter | solution.py:485
  30.0 9.4 %collective-permute-start.1 = (f32[8,8,128]{2,1,0:T(8,128)S(1)}, f32[8,8,128]{2,1,0:T(8,128)S(1)}, u32[]{:S(2)}, u32[]{:S(2)}) collective-permute-start(f32[8,8,128]{2,1,0:T(8,128)S(1)} %get-tuple-element.34), channel_id=1, source_target_pairs={{0,2},{2,0},{4,6},{6,4},{8,10},{10,8},{12,14},{14,12},{1,3},{3,1},... | collective-permute-start | bytes 98312 | tf_op jit(solution)/shard_map/ppermute | solution.py:513
  33.2 2.2 %copy-start = (bf16[1,1024,2048]{2,1,0:T(8,128)(2,1)S(1)}, bf16[1,1024,2048]{2,1,0:T(8,128)(2,1)}, u32[]{:S(2)}) copy-start(bf16[1,1024,2048]{2,1,0:T(8,128)(2,1)} %cache.3) | copy-start | bytes 12582916
  39.4 4.3 %collective-permute-start.2 = (f32[8,8,128]{2,1,0:T(8,128)S(1)}, f32[8,8,128]{2,1,0:T(8,128)S(1)}, u32[]{:S(2)}, u32[]{:S(2)}) collective-permute-start(f32[8,8,128]{2,1,0:T(8,128)S(1)} %add.14), channel_id=1, source_target_pairs={{0,4},{2,6},{4,0},{6,2},{8,12},{10,14},{12,8},{14,10},{1,5},{3,7},... | collective-permute-start | bytes 98312 | tf_op jit(solution)/shard_map/ppermute | solution.py:513
  43.8 6.9 %collective-permute-start.3 = (f32[8,8,128]{2,1,0:T(8,128)S(1)}, f32[8,8,128]{2,1,0:T(8,128)S(1)}, u32[]{:S(2)}, u32[]{:S(2)}) collective-permute-start(f32[8,8,128]{2,1,0:T(8,128)S(1)} %add.15), channel_id=1, source_target_pairs={{0,8},{2,10},{4,12},{6,14},{8,0},{10,2},{12,4},{14,6},{1,9},{3,11}... | collective-permute-start | bytes 98312 | tf_op jit(solution)/shard_map/ppermute | solution.py:513
  165.4 0.9 copy-start.2
  166.3 0.9 copy-start.3
Sparse Core Ops, SparseCore 0:
  29.4 68.3 reduce-scatter.4
  101.6 63.6 reduce-scatter.2

commit v10 on v7

--- a/solution.py
+++ b/solution.py
@@ -127,18 +127,6 @@
     )
 
 
-def selected_levels(codes):
-    masks = [(codes & 1) != 0, (codes & 2) != 0, (codes & 4) != 0, codes >= 8]
-
-    def node(bit, base):
-        if bit < 0:
-            return jnp.float32(NORMAL_FLOAT_LEVELS[base])
-        low = node(bit - 1, base)
-        return jnp.where(masks[bit], node(bit - 1, base + (1 << bit)), low)
-
-    return node(3, 0)
-
-
 def block_scales(scales, outer, column):
     count = scales.shape[0]
     line = lax.broadcasted_iota(jnp.int32, outer.shape, 0)
@@ -149,17 +137,13 @@
     return (scales.astype(F32) + 1.0) / 256.0 * second
 
 
-def weights_kernel(
-    x, key_codes, value_codes, key_scales, value_scales, outer, gain,
-    out_a, out_b, scaled, squares, scales,
-):
+def weights_kernel(key_codes, value_codes, key_scales, value_scales, outer, out, scales):
     block = pl.program_id(0)
     depth = key_codes.shape[0]
     columns = outer.shape[0] // 2
 
     @pl.when(block == 0)
     def _():
-        squares[...] = jnp.zeros(squares.shape, F32)
         for at in range(CORE_HEADS):
             head = lax.axis_index("rep") * CORE_HEADS + at
             column = head // (KV_HEADS // columns)
@@ -177,63 +161,83 @@
         row = pl.ds(block * (depth // QBLOCK) + step, 1)
         for at in range(CORE_HEADS):
             lanes = slice(at * HEAD_DIM, (at + 1) * HEAD_DIM)
-            out = (out_a, out_b)[at // 2]
             key_scale, value_scale = scales[2 * at, row, :], scales[2 * at + 1, row, :]
             for tile in range(QBLOCK // 16):
                 rows = pl.ds(pl.multiple_of(begin + 16 * tile, 16), 16)
                 key, value = key_codes[rows, lanes], value_codes[rows, lanes]
                 keys = [gathered_levels(table, key[half : half + 8]) for half in (0, 8)]
-                values = [selected_levels(value[half : half + 8]) for half in (0, 8)]
+                values = [gathered_levels(table, value[half : half + 8]) for half in (0, 8)]
                 rows = pl.ds(pl.multiple_of(block * depth + begin + 16 * tile, 16), 16)
                 keys = jnp.concatenate([level * key_scale for level in keys], axis=0)
                 values = jnp.concatenate([level * value_scale for level in values], axis=0)
-                out[at % 2, rows, :HEAD_DIM] = keys.astype(BF16)
-                out[at % 2, rows, HEAD_DIM:] = values.astype(BF16)
+                out[at, rows, :HEAD_DIM] = keys.astype(BF16)
+                out[at, rows, HEAD_DIM:] = values.astype(BF16)
         return 0
 
     lax.fori_loop(0, depth // QBLOCK, body, 0)
 
-    width = x.shape[2]
-    begin = pl.multiple_of(block * width, 128)
-    for prompt in range(x.shape[0]):
-        wide = x[prompt].astype(F32)
-        scaled[prompt, :, pl.ds(begin, width)] = (wide * gain[...]).astype(BF16)
-        squares[prompt] += token_rows(jnp.sum(wide * wide, axis=1, keepdims=True))
-
-
-def dequantize(x, codes, scales, outer, gain):
-    per_rep, _, features = x.shape
+
+def dequantize(codes, scales, outer):
+    features = codes.shape[0]
     depth = min(256, features)
     width = CORE_HEADS * HEAD_DIM
     rep = lambda: lax.axis_index("rep")
-    x, codes, scales, outer, gain = in_hbm(x, codes, scales, outer, gain)
-    weight = jax.ShapeDtypeStruct((2, features, 2 * HEAD_DIM), BF16)
+    codes, scales, outer = in_hbm(codes, scales, outer)
     return pl.pallas_call(
         weights_kernel,
         grid=(features // depth,),
         in_specs=[
-            pl.BlockSpec((per_rep, STRETCH, depth), lambda k: (0, 0, k)),
             pl.BlockSpec((depth, width), lambda k: (k, rep())),
             pl.BlockSpec((depth, width), lambda k: (k, 2 + rep())),
             pl.BlockSpec((scales.shape[0], width), lambda k: (0, rep())),
             pl.BlockSpec((scales.shape[0], width), lambda k: (0, 2 + rep())),
             pl.BlockSpec(outer.shape, lambda k: (0, 0)),
-            pl.BlockSpec((1, depth), lambda k: (0, k)),
         ],
-        out_specs=[VMEM] * 4,
-        out_shape=[
-            weight,
-            weight,
-            jax.ShapeDtypeStruct(x.shape, BF16),
-            jax.ShapeDtypeStruct((per_rep, 8, 128), F32),
-        ],
+        out_specs=VMEM,
+        out_shape=jax.ShapeDtypeStruct((CORE_HEADS, features, 2 * HEAD_DIM), BF16),
         scratch_shapes=[pltpu.VMEM((2 * CORE_HEADS, scales.shape[0], HEAD_DIM), F32)],
         compiler_params=pltpu.CompilerParams(vmem_limit_bytes=32 * MIB),
         cost_estimate=pl.CostEstimate(
             flops=32 * codes.size, bytes_accessed=codes.size * 2, transcendentals=0
         ),
         name="dequantize",
-    )(x, codes, codes, scales, scales, outer, gain)
+    )(codes, codes, scales, scales, outer)
+
+
+def scale_kernel(x, gain, scaled, squares):
+    item = pl.program_id(0)
+
+    @pl.when(item == 0)
+    def _():
+        squares[...] = jnp.zeros(squares.shape, F32)
+
+    width = x.shape[2]
+    begin = pl.multiple_of(item * width, 128)
+    for prompt in range(x.shape[0]):
+        wide = x[prompt].astype(F32)
+        scaled[prompt, :, pl.ds(begin, width)] = (wide * gain[...]).astype(BF16)
+        squares[prompt] += token_rows(jnp.sum(wide * wide, axis=1, keepdims=True))
+
+
+def scale_features(x, gain):
+    per_rep, _, features = x.shape
+    width = max(128, features // 4)
+    x, gain = in_hbm(x, gain)
+    return pl.pallas_call(
+        scale_kernel,
+        grid=(features // width,),
+        in_specs=[
+            pl.BlockSpec((per_rep, STRETCH, width), lambda i: (0, 0, i)),
+            pl.BlockSpec((1, width), lambda i: (0, i)),
+        ],
+        out_specs=[VMEM] * 2,
+        out_shape=[
+            jax.ShapeDtypeStruct(x.shape, BF16),
+            jax.ShapeDtypeStruct((per_rep, 8, 128), F32),
+        ],
+        compiler_params=pltpu.CompilerParams(vmem_limit_bytes=24 * MIB),
+        name="scale_features",
+    )(x, gain)
 
 
 def prompt_of(targets, owner):
@@ -243,154 +247,103 @@
     return prompt
 
 
-def lines_of(targets, distance, own, squares, other, gain, line, total):
+def with_lines(targets, distance, own, squares, other, other_squares, some, none):
     per_rep = own.shape[0]
     prompt = prompt_of(targets, owner_at(distance))
     at = lax.rem(jnp.maximum(prompt, 0), per_rep)
     is_own = prompt // per_rep == lax.axis_index("rep")
-
-    @pl.when((prompt >= 0) & is_own)
-    def _():
-        line[...] = own[at]
-        total[...] = squares[at]
-
-    @pl.when((prompt >= 0) & jnp.logical_not(is_own))
-    def _():
-        wide = other[at].astype(F32)
-        line[...] = (wide * gain[...]).astype(BF16)
-        total[...] = token_rows(jnp.sum(wide * wide, axis=1, keepdims=True))
-
-    @pl.when(prompt < 0)
-    def _():
-        line[...] = jnp.zeros(line.shape, BF16)
-        total[...] = jnp.zeros(total.shape, F32)
-
-
-def line_specs(distances, x):
-    return [
-        jax.ShapeDtypeStruct((len(distances) * STRETCH, x.shape[2]), BF16),
-        jax.ShapeDtypeStruct((len(distances), 8, 128), F32),
-    ]
-
-
-def first_kernel(distances, targets, own, squares, other, gain, weight, *refs):
-    right, left, terms, lines, totals = refs
+    pl.when((prompt >= 0) & is_own)(lambda: some(own.at[at], squares.at[at]))
+    pl.when((prompt >= 0) & jnp.logical_not(is_own))(
+        lambda: some(other.at[at], other_squares.at[at])
+    )
+    pl.when(prompt < 0)(none)
+
+
+def first_kernel(distance, targets, own, squares, other, other_squares, weight, right, left):
+    def some(lines, sums):
+        for head in range(CORE_HEADS):
+            product = jnp.dot(lines[...], weight[head], preferred_element_type=F32)
+            rows = slice(head * STRETCH, (head + 1) * STRETCH)
+            right[rows] = product[:, :HEAD_DIM].astype(BF16)
+            left[rows] = product[:, HEAD_DIM:].astype(BF16)
+        right[CORE_HEADS * STRETCH :] = two_pieces(sums[...])
+
+    def none():
+        right[...] = jnp.zeros(right.shape, BF16)
+        left[...] = jnp.zeros(left.shape, BF16)
+
+    with_lines(targets, distance, own, squares, other, other_squares, some, none)
+
+
+def project_first(distance, targets, own, squares, other, other_squares, weight):
+    rows = CORE_HEADS * STRETCH
+    return pl.pallas_call(
+        functools.partial(first_kernel, distance),
+        in_specs=[SMEM] + [VMEM] * 5,
+        out_specs=[VMEM] * 2,
+        out_shape=[
+            jax.ShapeDtypeStruct((rows + TAIL, HEAD_DIM), BF16),
+            jax.ShapeDtypeStruct((rows, HEAD_DIM), BF16),
+        ],
+        compiler_params=pltpu.CompilerParams(vmem_limit_bytes=24 * MIB),
+        cost_estimate=pl.CostEstimate(
+            flops=STRETCH * weight.size * 2, bytes_accessed=weight.size, transcendentals=0
+        ),
+        name="project_first",
+    )(targets, own, squares, other, other_squares, weight)
+
+
+def project_kernel(distances, targets, own, squares, other, other_squares, weight, out):
     for item, distance in enumerate(distances):
-        line = lines.at[item * STRETCH : (item + 1) * STRETCH]
-        lines_of(targets, distance, own, squares, other, gain, line, totals.at[item])
-    products(distances, lines, totals, weight, right, left, terms)
-
-
-def second_kernel(distances, lines, totals, weight, *refs):
-    products(distances, lines, totals, weight, *refs)
-
-
-def products(distances, lines, totals, weight, right, left, terms):
-    for head in range(2):
-        product = jnp.dot(lines[...], weight[head], preferred_element_type=F32)
-        rows = slice(head * STRETCH, (head + 1) * STRETCH)
-        right[rows] = product[:STRETCH, :HEAD_DIM].astype(BF16)
-        left[rows] = product[:STRETCH, HEAD_DIM:].astype(BF16)
-        for item in range(1, len(distances)):
-            part = product[item * STRETCH : (item + 1) * STRETCH]
-            begin = head * STRETCH
-            terms[item - 1, begin : begin + STRETCH] = part[:, :HEAD_DIM]
-            begin += 2 * STRETCH
-            terms[item - 1, begin : begin + STRETCH] = part[:, HEAD_DIM:]
-    for item in range(1, len(distances)):
-        terms[item - 1, 4 * STRETCH :] = totals[item]
-    right[2 * STRETCH :] = two_pieces(totals[0])
-
-
-def first_shapes(distances):
-    rows = 2 * STRETCH
-    return [
-        jax.ShapeDtypeStruct((rows + TAIL, HEAD_DIM), BF16),
-        jax.ShapeDtypeStruct((rows, HEAD_DIM), BF16),
-        jax.ShapeDtypeStruct((len(distances) - 1, 2 * rows + 8, HEAD_DIM), F32),
-    ]
-
-
-def project_cost(distances, weight):
-    return pl.CostEstimate(
-        flops=len(distances) * STRETCH * weight.size * 2,
-        bytes_accessed=weight.size,
-        transcendentals=0,
-    )
-
-
-def project_first(distances, targets, own, squares, other, gain, weight):
-    return pl.pallas_call(
-        functools.partial(first_kernel, distances),
+
+        def some(lines, sums, item=item):
+            for head in range(CORE_HEADS):
+                product = jnp.dot(lines[...], weight[head], preferred_element_type=F32)
+                begin = head % 2 * STRETCH
+                out[item, head // 2, begin : begin + STRETCH] = product[:, :HEAD_DIM]
+                begin += 2 * STRETCH
+                out[item, head // 2, begin : begin + STRETCH] = product[:, HEAD_DIM:]
+            for half in range(2):
+                out[item, half, 4 * STRETCH :] = sums[...]
+
+        def none(item=item):
+            out[item] = jnp.zeros(out.shape[1:], F32)
+
+        with_lines(targets, distance, own, squares, other, other_squares, some, none)
+
+
+def project(distances, targets, own, squares, other, other_squares, weight):
+    return pl.pallas_call(
+        functools.partial(project_kernel, distances),
         in_specs=[SMEM] + [VMEM] * 5,
-        out_specs=[VMEM] * 5,
-        out_shape=first_shapes(distances) + line_specs(distances, own),
+        out_specs=VMEM,
+        out_shape=jax.ShapeDtypeStruct((len(distances), 2, 4 * STRETCH + 8, HEAD_DIM), F32),
         compiler_params=pltpu.CompilerParams(vmem_limit_bytes=24 * MIB),
-        cost_estimate=project_cost(distances, weight),
-        name="project_first",
-    )(targets, own, squares, other, gain, weight)
-
-
-def project_second(distances, lines, totals, weight):
-    return pl.pallas_call(
-        functools.partial(second_kernel, distances),
-        in_specs=[VMEM] * 3,
-        out_specs=[VMEM] * 3,
-        out_shape=first_shapes(distances),
-        compiler_params=pltpu.CompilerParams(vmem_limit_bytes=24 * MIB),
-        cost_estimate=project_cost(distances, weight),
-        name="project_second",
-    )(lines, totals, weight)
-
-
-def project_kernel(
-    distances, targets, own, squares, other, gain, weight_a, weight_b, out_a, out_b, lines, totals
-):
-    for item, distance in enumerate(distances):
-        line = lines.at[item * STRETCH : (item + 1) * STRETCH]
-        lines_of(targets, distance, own, squares, other, gain, line, totals.at[item])
-    for weight, out in ((weight_a, out_a), (weight_b, out_b)):
-        for head in range(2):
-            product = jnp.dot(lines[...], weight[head], preferred_element_type=F32)
-            for item in range(len(distances)):
-                part = product[item * STRETCH : (item + 1) * STRETCH]
-                begin = head * STRETCH
-                out[item, begin : begin + STRETCH] = part[:, :HEAD_DIM]
-                begin += 2 * STRETCH
-                out[item, begin : begin + STRETCH] = part[:, HEAD_DIM:]
-        for item in range(len(distances)):
-            out[item, 4 * STRETCH :] = totals[item]
-
-
-def project(distances, targets, own, squares, other, gain, weights):
-    shape = jax.ShapeDtypeStruct((len(distances), 4 * STRETCH + 8, HEAD_DIM), F32)
-    line, total = line_specs(distances, own)
-    return pl.pallas_call(
-        functools.partial(project_kernel, distances),
-        in_specs=[SMEM] + [VMEM] * 6,
-        out_specs=[VMEM] * 2,
-        out_shape=[shape, shape],
-        scratch_shapes=[pltpu.VMEM(line.shape, BF16), pltpu.VMEM(total.shape, F32)],
-        compiler_params=pltpu.CompilerParams(vmem_limit_bytes=24 * MIB),
-        cost_estimate=project_cost(distances, weights[0]),
+        cost_estimate=pl.CostEstimate(
+            flops=len(distances) * STRETCH * weight.size * 2 // 2,
+            bytes_accessed=weight.size,
+            transcendentals=0,
+        ),
         name="project",
-    )(targets, own, squares, other, gain, *weights)
+    )(targets, own, squares, other, other_squares, weight)
 
 
 def send_kernel(half, first, terms, right, left, to_right, to_left):
     rows = 4 * STRETCH
     middle = 2 * STRETCH
     if first:
-        to_right[:middle] = (terms[0, :middle] + right[:middle].astype(F32)).astype(BF16)
-        to_right[middle:rows] = terms[0, middle:rows].astype(BF16)
-        to_left[:middle] = terms[1, :middle].astype(BF16)
-        to_left[middle:rows] = (terms[1, middle:rows] + left[...].astype(F32)).astype(BF16)
+        from_right = right[half * middle : (half + 1) * middle].astype(F32)
+        from_left = left[half * middle : (half + 1) * middle].astype(F32)
+        to_right[:middle] = (terms[0, half, :middle] + from_right).astype(BF16)
+        to_right[middle:rows] = terms[0, half, middle:rows].astype(BF16)
+        to_left[:middle] = terms[1, half, :middle].astype(BF16)
+        to_left[middle:rows] = (terms[1, half, middle:rows] + from_left).astype(BF16)
     else:
-        to_right[:rows] = (terms[0, :rows] + right[:rows].astype(F32)).astype(BF16)
-        to_left[:rows] = (terms[1, :rows] + left[:rows].astype(F32)).astype(BF16)
+        to_right[:rows] = (terms[0, half, :rows] + right[:rows].astype(F32)).astype(BF16)
+        to_left[:rows] = (terms[1, half, :rows] + left[:rows].astype(F32)).astype(BF16)
     if half == 0:
-        right_sum, left_sum = terms[0, rows:], terms[1, rows:]
-        right_sum += one_piece(right[middle if first else rows :])
+        right_sum = terms[0, 0, rows:] + one_piece(right[rows:])
+        left_sum = terms[1, 0, rows:]
         if not first:
             left_sum += one_piece(left[rows:])
         to_right[rows:] = two_pieces(right_sum)
@@ -450,9 +403,9 @@
     allowed = lax.broadcasted_iota(jnp.int32, (ROWS, length), 1) < span
     second_step = lax.broadcasted_iota(jnp.int32, (ROWS, 1), 0) % STEPS == 1
     for at in range(CORE_HEADS):
-        head = part * CORE_HEADS + at
-        key_lanes = slice(head * HEAD_DIM, (head + 1) * HEAD_DIM)
-        value_lanes = slice((KV_HEADS + head) * HEAD_DIM, (KV_HEADS + head + 1) * HEAD_DIM)
+        head = (rep if part == 1 else 1 - rep) * CORE_HEADS + at
+        key_lanes = pl.ds(pl.multiple_of(head * HEAD_DIM, HEAD_DIM), HEAD_DIM)
+        value_lanes = pl.ds(pl.multiple_of((KV_HEADS + head) * HEAD_DIM, HEAD_DIM), HEAD_DIM)
         query = q[head]
         wide = query.astype(F32)
         scores = lax.dot_general(query, cache[0, :, key_lanes], dims, preferred_element_type=F32)
@@ -498,25 +451,24 @@
 
 
 def final_kernel(
-    targets, rotary, own_a, own_b, right_a, left_a, right_b, left_b, grouped, *refs
+    targets, rotary, own, right_a, left_a, right_b, left_b, grouped, cached_there, cached_here, out
 ):
-    cached, out = refs
     scaling = HEAD_DIM ** (-0.5)
     dims = (((1,), (1,)), ((), ()))
-    mine = own_a.shape[0] - 1
+    mine = own.shape[0] - 1
     rep = lax.axis_index("rep")
     first = rep * CORE_HEADS
     prompt = prompt_of(targets, lax.axis_index("tp"))
     cosine, sine = rotary[0], rotary[1]
     rows = 4 * STRETCH
-    squares = own_a[mine, rows:] + one_piece(right_a[rows:]) + one_piece(left_a[rows:])
+    squares = own[mine, 0, rows:] + one_piece(right_a[rows:]) + one_piece(left_a[rows:])
     scale = token_column(lax.rsqrt(squares / D + EPSILON))
     for head in range(CORE_HEADS):
-        own, right, left = ((own_a, right_a, left_a), (own_b, right_b, left_b))[head // 2]
+        right, left = ((right_a, left_a), (right_b, left_b))[head // 2]
         at = slice(head % 2 * STRETCH, (head % 2 + 1) * STRETCH)
-        keys = own[mine, at] + right[at].astype(F32) + left[at].astype(F32)
+        keys = own[mine, head // 2, at] + right[at].astype(F32) + left[at].astype(F32)
         at = slice((2 + head % 2) * STRETCH, (3 + head % 2) * STRETCH)
-        values = own[mine, at] + right[at].astype(F32) + left[at].astype(F32)
+        values = own[mine, head // 2, at] + right[at].astype(F32) + left[at].astype(F32)
         keys = (keys * scale).astype(BF16).astype(F32)
         values = (values * scale).astype(BF16)
         keys = keys * cosine + pltpu.roll(keys, HEAD_DIM // 2, 1) * sine
@@ -529,7 +481,7 @@
         totals = jnp.sum(weight, axis=1, keepdims=True)
         sums = jnp.dot(weight.astype(BF16), values, preferred_element_type=F32) / totals
         logs = jnp.where(prompt >= 0, highest + jnp.log(totals), NEGATIVE)
-        parts = [cached[0, first + head], cached[1, first + head]]
+        parts = [cached_there[head], cached_here[head]]
         logs = [tail_pieces(part[ROWS:]) for part in parts] + [logs]
         sums = [part[:ROWS].astype(F32) for part in parts] + [sums]
         highest = functools.reduce(jnp.maximum, logs)
@@ -551,7 +503,7 @@
         out_shape=jax.ShapeDtypeStruct((1, STEPS, width), BF16),
         compiler_params=pltpu.CompilerParams(vmem_limit_bytes=16 * MIB),
         name="finish",
-    )(targets, rotary, *own, *arrived, grouped, cached)
+    )(targets, rotary, own, *arrived, grouped, *cached)
 
 
 def rotary_turns():
@@ -585,51 +537,42 @@
     def pass_on(right, left):
         return lax.ppermute(right, "tp", to_right), lax.ppermute(left, "tp", to_left)
 
-    other = lax.ppermute(lines, "rep", [(0, 1), (1, 0)])
-    first_half, second_half, own, squares = dequantize(
-        lines, kv_codes, scale_codes, outer_scales.T, gain
-    )
+    own, squares = scale_features(lines, gain)
+    swap = lambda array: lax.ppermute(array, "rep", [(0, 1), (1, 0)])
+    other, other_squares = swap(own), swap(squares)
+    weight = dequantize(kv_codes, scale_codes, outer_scales.T)
     frequency, turns = rotary_turns()
     start = (prompt_lengths - STRETCH).astype(F32)[:, None] * jnp.asarray(frequency)
     starts = jnp.stack([jnp.cos(start), jnp.sin(start)])
-    targets, second_half = lax.optimization_barrier((target_rows, second_half))
+    targets, weight = lax.optimization_barrier((target_rows, weight))
     grouped, rotary = prepare(targets, queries, starts, jnp.asarray(turns))
 
-    gain, second_half, grouped, rotary = lax.optimization_barrier(
-        (gain, second_half, grouped, rotary)
-    )
-    distances = [half, half - 1, 1 - half]
-    right, left, terms_a, lines_here, totals = project_first(
-        distances, target_rows, own, squares, other, gain, first_half
-    )
-    arrived = [pass_on(right, left), None]
-    right, left, terms_b = project_second(distances, lines_here, totals, second_half)
-    arrived[1] = pass_on(right, left)
-    terms = [terms_a, terms_b]
-
-    targets = target_rows
+    weight, grouped, rotary = lax.optimization_barrier((weight, grouped, rotary))
+    features = [own, squares, other, other_squares]
+    right, left = project_first(half, target_rows, *features, weight)
+    targets, _ = lax.optimization_barrier((target_rows, left))
+    arrived = [pass_on(right, left)] * 2
+
     cached = []
     for distance in range(half - 1, 0, -1):
-        if distance < half - 1:
-            distances = [distance, -distance] + ([0] if distance == 1 else [])
-            terms = list(
-                project(distances, targets, own, squares, other, gain, [first_half, second_half])
+        distances = [distance, -distance] + ([0] if distance == 1 else [])
+        if len(cached) < 2:
+            cached.append(
+                cache_attention(
+                    len(cached), targets, prompt_lengths, cache_lengths, grouped, kv_cache, new_kv
+                )
             )
+        if len(cached) == 1:
+            cached = [swap(cached[0])]
+        terms = project(distances, targets, *features, weight)
+        later = terms
         for part in range(2):
-            right, left = sends(part, distance == half - 1, terms[part], *arrived[part])
+            right, left = sends(part, distance == half - 1, (terms, later)[part], *arrived[part])
             if part == 0:
-                right, cached, terms[1] = lax.optimization_barrier((right, cached, terms[1]))
+                right, cached, later = lax.optimization_barrier((right, cached, terms))
             targets, _ = lax.optimization_barrier((target_rows, right))
             arrived[part] = pass_on(right, left)
-        if distance in (2, 3):
-            cached.append(
-                cache_attention(
-                    3 - distance, targets, prompt_lengths, cache_lengths, grouped, kv_cache, new_kv
-                )
-            )
-
-    cached, _ = lax.optimization_barrier((cached, right))
-    cached = lax.all_gather(jnp.concatenate(cached), "rep")
+
     out = finish(target_rows, rotary, terms, [*arrived[0], *arrived[1]], grouped, cached)
     return lax.all_gather(out, "rep", axis=2, tiled=True)
 

time: 57.5 us -> 60 us (1.043)
  waiting for transfers between devices: 5.83 us -> 11.1 us
  blocking collectives: 3.8 us -> 1.85 us
  starting transfers between devices: 17.6 us -> 16.2 us
  Pallas kernels: 27.9 us -> 29.1 us
    ppermute x8 -> x7, waiting for transfers between devices: 2 us -> 5.32 us  [pass_on(): lax.ppermute(right, 'tp', to_right)]
    ppermute x8 -> x7, starting transfers between devices: 14.6 us -> 12.6 us  [pass_on(): lax.ppermute(right, 'tp', to_right)]
    all_gather x1 -> x0, blocking collectives: 1.95 us -> none  [per_device(): cached = lax.all_gather(jnp.concatenate(cached), 'rep')]
    ppermute x8 -> x7, waiting for transfers between devices: 3.83 us -> 5.74 us  [pass_on(): lax.ppermute(left, 'tp', to_left)]
    pallas_call x2, Pallas kernels: 3.89 us -> 4.57 us  [the longest x1 2.99 us: scale_features(): pl.pallas_call(scale_kernel, grid=(features // width,), in_specs=[pl.Bloc...]
    pallas_call x2 -> x3, Pallas kernels: 6.7 us -> 7.08 us  [project(): pl.pallas_call(functools.partial(project_kernel, distances), in_specs=[SM...]
    ppermute x8 -> x7, starting transfers between devices: 2.63 us -> 2.92 us  [pass_on(): lax.ppermute(left, 'tp', to_left)]
  transfers between devices with their start and end apart: 17 -> 17, of which waited for: 4 -> 7; matrix products, arithmetic and copies ran while one was open for 0% -> 0% of each run, Pallas kernels for 41% -> 38%
where the time goes in v10:
time: 60 us; the launch traced here: 59.9 us
  Pallas kernels  29.1 us (48%)
  starting transfers between devices  16.2 us (27%)
  waiting for transfers between devices  11.1 us (18%)
  blocking collectives  1.85 us (3%)
  between operations  0.91 us (2%)
  local copies, waits for them, and re-layouts  0.67 us (1%)
    ppermute x7, starting transfers between devices, pass_on(): lax.ppermute(right, 'tp', to_right)  12.6 us
    pallas_call x1, Pallas kernels, dequantize(): pl.pallas_call(weights_kernel, grid=(features // depth,), in_specs=[pl.Bl...  10.3 us
    pallas_call x3, Pallas kernels, project(): pl.pallas_call(functools.partial(project_kernel, distances), in_specs=[SM...  7.08 us
    ppermute x7, waiting for transfers between devices, pass_on(): lax.ppermute(left, 'tp', to_left)  5.74 us
    ppermute x7, waiting for transfers between devices, pass_on(): lax.ppermute(right, 'tp', to_right)  5.32 us
    pallas_call x2, Pallas kernels, cache_attention(): pl.pallas_call(functools.partial(cache_kernel, part), in_specs=[SMEM] * 3...  3.99 us
    pallas_call x1, Pallas kernels, scale_features(): pl.pallas_call(scale_kernel, grid=(features // width,), in_specs=[pl.Bloc...  2.99 us
    ppermute x7, starting transfers between devices, pass_on(): lax.ppermute(left, 'tp', to_left)  2.92 us
  transfers between devices with their start and end apart: 17, of which 7 were waited for; matrix products, arithmetic and copies ran while one was open for 0% of the time, Pallas kernels for 38%

profile of v10, /device:TPU:0, one launch (start us, length us, event | category | flops | bytes accessed | tf_op | source)
XLA Modules:
  0.0 59.9 jit_solution(1284649360661385143)
XLA Ops:
  0.0 3.0 %scale_features.1 = (bf16[3,192,2048]{2,1,0:T(8,128)(2,1)S(1)}, f32[3,8,128]{2,1,0:T(8,128)S(1)}) custom-call(bf16[3,192,2048]{2,1,0:T(8,128)(2,1)} %bitcast.3, f32[1,2048]{1,0:T(1,128)} %bitcast.4), custom_call_target="tpu_custom_call" | custom-call | tf_op jit(solution)/shard_map/scale_features/pallas_call | solution.py:226
  3.0 0.5 collective-permute-start
  3.5 0.1 collective-permute-start.1
  3.6 0.1 multiply_cosine_fusion
  3.7 0.0 copy-start.1
  3.7 0.0 copy-start.2
  3.8 0.0 copy-start.4
  3.8 10.3 %dequantize.1.weight = bf16[4,2048,256]{2,1,0:T(8,128)(2,1)S(1)} custom-call(s32[2048,2048]{1,0:T(8,128)} %value_codes.1, s32[2048,2048]{1,0:T(8,128)} %value_codes.1, s32[32,2048]{1,0:T(8,128)} %value_scales.1, s32[32,2048]{1,0:T(8,128)} %value_scales.1, f32[8,32]{1,0:T(8,128)} %bitcast.5), custom_call_target="tpu_custom_call" | custom-call | flops 134217728 | bytes 8388608 | tf_op jit(solution)/shard_map/dequantize/pallas_call | solution.py:186
  14.1 0.7 %prepare.1 = (bf16[8,32,128]{2,1,0:T(8,128)(2,1)S(1)}, f32[2,192,128]{2,1,0:T(8,128)S(1)}) custom-call(s32[6]{0:T(128)S(1)} %copy-done.4, bf16[1,2,16384]{2,1,0:T(2,128)(2,1)S(1)} %copy-done.2, f32[2,6,128]{2,1,0:T(8,128)S(1)} %pad_maximum_fusion.starts, f32[2,192,128]{2,1,0:T(8,128)S(1)} %copy-done.1), custom_call_target="tpu_custom_call" | custom-call | tf_op jit(solution)/shard_map/prepare/pallas_call | solution.py:381
  14.8 0.0 copy-start
  14.8 0.0 copy-start.3
  14.8 1.6 %project_first.1 = (bf16[784,128]{1,0:T(8,128)(2,1)S(1)}, bf16[768,128]{1,0:T(8,128)(2,1)S(1)}) custom-call(s32[6]{0:T(128)S(1)} %copy-done.4, bf16[3,192,2048]{2,1,0:T(8,128)(2,1)S(1)} %get-tuple-element.47.own, f32[3,8,128]{2,1,0:T(8,128)S(1)} %get-tuple-element.48.squares, bf16[3,192,2048]{2,1,0:T(8,128)(2,1)S(1)} %collective-permute-done.other, ...), custom_call_target="tpu_custom_call" | custom-call | flops 805306368 | bytes 2097152 | tf_op jit(solution)/shard_map/project_first/pallas_call | solution.py:280
  16.4 2.1 %collective-permute-start.2 = (bf16[784,128]{1,0:T(8,128)(2,1)S(1)}, bf16[784,128]{1,0:T(8,128)(2,1)S(1)}, u32[]{:S(2)}, u32[]{:S(2)}) collective-permute-start(bf16[784,128]{1,0:T(8,128)(2,1)S(1)} %get-tuple-element.52), channel_id=1, source_target_pairs={{0,4},{4,8},{8,12},{12,14},{14,10},{10,6},{6,2},{2,0},{1,5},{5,9},... | collective-permute-start | bytes 602120 | tf_op jit(solution)/shard_map/ppermute | solution.py:538
  18.5 0.9 %collective-permute-start.3 = (bf16[768,128]{1,0:T(8,128)(2,1)S(1)}, bf16[768,128]{1,0:T(8,128)(2,1)S(1)}, u32[]{:S(2)}, u32[]{:S(2)}) collective-permute-start(bf16[768,128]{1,0:T(8,128)(2,1)S(1)} %get-tuple-element.50), channel_id=1, source_target_pairs={{0,2},{4,0},{8,4},{12,8},{14,12},{10,14},{6,10},{2,6},{1,3},{5,1},... | collective-permute-start | bytes 589832 | tf_op jit(solution)/shard_map/ppermute | solution.py:538
  20.1 2.0 %cache_attention.2 = bf16[4,48,128]{2,1,0:T(8,128)(2,1)S(1)} custom-call(s32[6]{0:T(128)S(1)} %copy-done.4, s32[6]{0:T(128)S(1)} %copy-done.5, s32[1]{0:T(128)S(6)} %copy.15.stored, bf16[8,32,128]{2,1,0:T(8,128)(2,1)S(1)} %get-tuple-element.54.q.grouped, bf16[1,1024,2048]{2,1,0:T(8,128)(2,1)S(1)} %copy-done, bf16[1,2,2048]{2,1,0:T(2,128)(2,1)S(1)} %copy-done.3), custom_call_target="tpu_custom_call" | custom-call | flops 67108864 | bytes 2097152 | tf_op jit(solution)/shard_map/cache_attention/pallas_call | solution.py:438
  22.1 0.1 collective-permute-start.4
  22.2 1.7 %project.3.terms = f32[2,2,776,128]{3,2,1,0:T(8,128)S(1)} custom-call(s32[6]{0:T(128)S(1)} %copy-done.4, bf16[3,192,2048]{2,1,0:T(8,128)(2,1)S(1)} %get-tuple-element.47.own, f32[3,8,128]{2,1,0:T(8,128)S(1)} %get-tuple-element.48.squares, bf16[3,192,2048]{2,1,0:T(8,128)(2,1)S(1)} %collective-permute-done.other, ...), custom_call_target="tpu_custom_call" | custom-call | flops 805306368 | bytes 2097152 | tf_op jit(solution)/shard_map/project/pallas_call | solution.py:316
  23.9 2.0 %collective-permute-done.3.left = bf16[768,128]{1,0:T(8,128)(2,1)S(1)} collective-permute-done((bf16[768,128]{1,0:T(8,128)(2,1)S(1)}, bf16[768,128]{1,0:T(8,128)(2,1)S(1)}, u32[]{:S(2)}, u32[]{:S(2)}) %collective-permute-start.3) | collective-permute-done | bytes 196640 | tf_op jit(solution)/shard_map/ppermute | solution.py:538
  25.9 0.1 sends.6
  26.0 1.8 %collective-permute-start.5 = (bf16[784,128]{1,0:T(8,128)(2,1)S(1)}, bf16[784,128]{1,0:T(8,128)(2,1)S(1)}, u32[]{:S(2)}, u32[]{:S(2)}) collective-permute-start(bf16[784,128]{1,0:T(8,128)(2,1)S(1)} %get-tuple-element.58), channel_id=1, source_target_pairs={{0,4},{4,8},{8,12},{12,14},{14,10},{10,6},{6,2},{2,0},{1,5},{5,9},... | collective-permute-start | bytes 602120 | tf_op jit(solution)/shard_map/ppermute | solution.py:538
  27.8 0.3 collective-permute-start.6
  28.1 0.1 sends.7
  28.1 0.5 collective-permute-start.8
  28.6 1.6 %collective-permute-start.7 = (bf16[768,128]{1,0:T(8,128)(2,1)S(1)}, bf16[768,128]{1,0:T(8,128)(2,1)S(1)}, u32[]{:S(2)}, u32[]{:S(2)}) collective-permute-start(bf16[768,128]{1,0:T(8,128)(2,1)S(1)} %get-tuple-element.56), channel_id=1, source_target_pairs={{0,4},{4,8},{8,12},{12,14},{14,10},{10,6},{6,2},{2,0},{1,5},{5,9},... | collective-permute-start | bytes 589832 | tf_op jit(solution)/shard_map/ppermute | solution.py:538
  30.2 2.0 %cache_attention.3.cached_here = bf16[4,48,128]{2,1,0:T(8,128)(2,1)S(1)} custom-call(s32[6]{0:T(128)S(1)} %copy-done.4, s32[6]{0:T(128)S(1)} %copy-done.5, s32[1]{0:T(128)S(6)} %copy.15.stored, bf16[8,32,128]{2,1,0:T(8,128)(2,1)S(1)} %get-tuple-element.54.q.grouped, bf16[1,1024,2048]{2,1,0:T(8,128)(2,1)S(1)} %copy-done, bf16[1,2,2048]{2,1,0:T(2,128)(2,1)S(1)} %copy-done.3), custom_call_target="tpu_custom_call" | custom-call | flops 67108864 | bytes 2097152 | tf_op jit(solution)/shard_map/cache_attention/pallas_call | solution.py:438
  32.2 1.7 %project.4.terms = f32[2,2,776,128]{3,2,1,0:T(8,128)S(1)} custom-call(s32[6]{0:T(128)S(1)} %copy-done.4, bf16[3,192,2048]{2,1,0:T(8,128)(2,1)S(1)} %get-tuple-element.47.own, f32[3,8,128]{2,1,0:T(8,128)S(1)} %get-tuple-element.48.squares, bf16[3,192,2048]{2,1,0:T(8,128)(2,1)S(1)} %collective-permute-done.other, ...), custom_call_target="tpu_custom_call" | custom-call | flops 805306368 | bytes 2097152 | tf_op jit(solution)/shard_map/project/pallas_call | solution.py:316
  33.9 1.8 %collective-permute-done.6.left = bf16[784,128]{1,0:T(8,128)(2,1)S(1)} collective-permute-done((bf16[784,128]{1,0:T(8,128)(2,1)S(1)}, bf16[784,128]{1,0:T(8,128)(2,1)S(1)}, u32[]{:S(2)}, u32[]{:S(2)}) %collective-permute-start.6) | collective-permute-done | bytes 200736 | tf_op jit(solution)/shard_map/ppermute | solution.py:538
  35.7 0.1 sends.8
  35.8 1.6 %collective-permute-start.9 = (bf16[784,128]{1,0:T(8,128)(2,1)S(1)}, bf16[784,128]{1,0:T(8,128)(2,1)S(1)}, u32[]{:S(2)}, u32[]{:S(2)}) collective-permute-start(bf16[784,128]{1,0:T(8,128)(2,1)S(1)} %get-tuple-element.66), channel_id=1, source_target_pairs={{0,4},{4,8},{8,12},{12,14},{14,10},{10,6},{6,2},{2,0},{1,5},{5,9},... | collective-permute-start | bytes 602120 | tf_op jit(solution)/shard_map/ppermute | solution.py:538
  37.5 0.5 collective-permute-start.10
  37.9 0.4 collective-permute-done.8.left
  38.3 0.1 sends.9
  38.4 0.3 collective-permute-start.14
  38.7 1.8 %collective-permute-start.13 = (bf16[768,128]{1,0:T(8,128)(2,1)S(1)}, bf16[768,128]{1,0:T(8,128)(2,1)S(1)}, u32[]{:S(2)}, u32[]{:S(2)}) collective-permute-start(bf16[768,128]{1,0:T(8,128)(2,1)S(1)} %get-tuple-element.64), channel_id=1, source_target_pairs={{0,4},{4,8},{8,12},{12,14},{14,10},{10,6},{6,2},{2,0},{1,5},{5,9},... | collective-permute-start | bytes 589832 | tf_op jit(solution)/shard_map/ppermute | solution.py:538
  40.5 3.8 %project.5.terms.own = f32[3,2,776,128]{3,2,1,0:T(8,128)S(1)} custom-call(s32[6]{0:T(128)S(1)} %copy-done.4, bf16[3,192,2048]{2,1,0:T(8,128)(2,1)S(1)} %get-tuple-element.47.own, f32[3,8,128]{2,1,0:T(8,128)S(1)} %get-tuple-element.48.squares, bf16[3,192,2048]{2,1,0:T(8,128)(2,1)S(1)} %collective-permute-done.other, ...), custom_call_target="tpu_custom_call" | custom-call | flops 1207959552 | bytes 2097152 | tf_op jit(solution)/shard_map/project/pallas_call | solution.py:316
  44.3 0.1 sends.10
  44.4 1.9 %collective-permute-start.11 = (bf16[784,128]{1,0:T(8,128)(2,1)S(1)}, bf16[784,128]{1,0:T(8,128)(2,1)S(1)}, u32[]{:S(2)}, u32[]{:S(2)}) collective-permute-start(bf16[784,128]{1,0:T(8,128)(2,1)S(1)} %get-tuple-element.71), channel_id=1, source_target_pairs={{0,4},{4,8},{8,12},{12,14},{14,10},{10,6},{6,2},{2,0},{1,5},{5,9},... | collective-permute-start | bytes 602120 | tf_op jit(solution)/shard_map/ppermute | solution.py:538
  46.3 0.2 collective-permute-start.12
  46.5 0.3 collective-permute-done.14.left
  46.8 0.2 collective-permute-done.13.right
  47.0 0.1 sends.11
  47.1 1.8 %collective-permute-start.15 = (bf16[768,128]{1,0:T(8,128)(2,1)S(1)}, bf16[768,128]{1,0:T(8,128)(2,1)S(1)}, u32[]{:S(2)}, u32[]{:S(2)}) collective-permute-start(bf16[768,128]{1,0:T(8,128)(2,1)S(1)} %get-tuple-element.75), channel_id=1, source_target_pairs={{0,4},{4,8},{8,12},{12,14},{14,10},{10,6},{6,2},{2,0},{1,5},{5,9},... | collective-permute-start | bytes 589832 | tf_op jit(solution)/shard_map/ppermute | solution.py:538
  49.0 0.3 collective-permute-start.16
  49.2 5.1 %collective-permute-done.15.right_b = bf16[768,128]{1,0:T(8,128)(2,1)S(1)} collective-permute-done((bf16[768,128]{1,0:T(8,128)(2,1)S(1)}, bf16[768,128]{1,0:T(8,128)(2,1)S(1)}, u32[]{:S(2)}, u32[]{:S(2)}) %collective-permute-start.15) | collective-permute-done | bytes 196640 | tf_op jit(solution)/shard_map/ppermute | solution.py:538
  54.3 1.1 %collective-permute-done.16.left_b = bf16[768,128]{1,0:T(8,128)(2,1)S(1)} collective-permute-done((bf16[768,128]{1,0:T(8,128)(2,1)S(1)}, bf16[768,128]{1,0:T(8,128)(2,1)S(1)}, u32[]{:S(2)}, u32[]{:S(2)}) %collective-permute-start.16) | collective-permute-done | bytes 196640 | tf_op jit(solution)/shard_map/ppermute | solution.py:538
  55.4 2.0 %finish.1 = bf16[1,2,8192]{2,1,0:T(2,128)(2,1)S(1)} custom-call(s32[6]{0:T(128)S(1)} %copy-done.4, f32[2,192,128]{2,1,0:T(8,128)S(1)} %get-tuple-element.46.rotary, f32[3,2,776,128]{3,2,1,0:T(8,128)S(1)} %project.5.terms.own, bf16[784,128]{1,0:T(8,128)(2,1)S(1)} %collective-permute-done.11.right_a, bf16[784,128]{1,0:T(8,128)(2,1)S(1)} %collective-permute-done.12.left_a, ...), custom_call_target="tpu_custom_call" | custom-call | tf_op jit(solution)/shard_map/finish/pallas_call | solution.py:499
  57.4 1.9 %all_gather.3 = bf16[1,2,16384]{2,1,0:T(2,128)(2,1)S(1)} all-gather(bf16[1,2,8192]{2,1,0:T(2,128)(2,1)S(1)} %finish.1), channel_id=1, replica_groups=mesh['grp'=2,'tp'=8,'rep'=2] {'rep'}, dimensions={2}, use_global_device_ids=true | all-gather | bytes 98304 | tf_op jit(solution)/shard_map/all_gather | solution.py:577
  59.3 0.6 %copy.16 = bf16[1,2,16384]{2,1,0:T(2,128)(2,1)} copy(bf16[1,2,16384]{2,1,0:T(2,128)(2,1)S(1)} %all_gather.3) | data formatting | bytes 131072
  (21 shorter events, 0.1 us)
Async XLA Ops:
  0.0 3.6 %copy-start.6 = (f32[128]{0:T(128)S(1)}, f32[128]{0:T(128)}, u32[]{:S(2)}) copy-start(f32[128]{0:T(128)} %constant.7.clone) | copy-start | bytes 1540
  0.0 3.6 %copy-start.5 = (s32[6]{0:T(128)S(1)}, s32[6]{0:T(128)}, u32[]{:S(2)}) copy-start(s32[6]{0:T(128)} %lengths.3) | copy-start | bytes 76
  3.0 11.8 %collective-permute-start = (bf16[3,192,2048]{2,1,0:T(8,128)(2,1)S(1)}, bf16[3,192,2048]{2,1,0:T(8,128)(2,1)S(1)}, u32[]{:S(2)}, u32[]{:S(2)}) collective-permute-start(bf16[3,192,2048]{2,1,0:T(8,128)(2,1)S(1)} %get-tuple-element.47.own), channel_id=1, source_target_pairs={{0,1},{1,0},{2,3},{3,2},{4,5},{5,4},{6,7},{7,6},{8,9},{9,8},{10,11... | collective-permute-start | bytes 7077896 | tf_op jit(solution)/shard_map/ppermute | solution.py:541
  3.5 11.3 %collective-permute-start.1 = (f32[3,8,128]{2,1,0:T(8,128)S(1)}, f32[3,8,128]{2,1,0:T(8,128)S(1)}, u32[]{:S(2)}, u32[]{:S(2)}) collective-permute-start(f32[3,8,128]{2,1,0:T(8,128)S(1)} %get-tuple-element.48.squares), channel_id=1, source_target_pairs={{0,1},{1,0},{2,3},{3,2},{4,5},{5,4},{6,7},{7,6},{8,9},{9,8},{10,11... | collective-permute-start | bytes 36872 | tf_op jit(solution)/shard_map/ppermute | solution.py:541
  3.7 10.3 %copy-start.1 = (f32[2,192,128]{2,1,0:T(8,128)S(1)}, f32[2,192,128]{2,1,0:T(8,128)}, u32[]{:S(2)}) copy-start(f32[2,192,128]{2,1,0:T(8,128)} %constant.8.clone.turns) | copy-start | bytes 589828
  3.7 10.3 %copy-start.2 = (bf16[1,2,16384]{2,1,0:T(2,128)(2,1)S(1)}, bf16[1,2,16384]{2,1,0:T(2,128)(2,1)}, u32[]{:S(2)}) copy-start(bf16[1,2,16384]{2,1,0:T(2,128)(2,1)} %queries.1) | copy-start | bytes 196612
  3.8 10.3 %copy-start.4 = (s32[6]{0:T(128)S(1)}, s32[6]{0:T(128)}, u32[]{:S(2)}) copy-start(s32[6]{0:T(128)} %targets.9) | copy-start | bytes 76
  14.8 5.3 %copy-start = (bf16[1,1024,2048]{2,1,0:T(8,128)(2,1)S(1)}, bf16[1,1024,2048]{2,1,0:T(8,128)(2,1)}, u32[]{:S(2)}) copy-start(bf16[1,1024,2048]{2,1,0:T(8,128)(2,1)} %cache.3) | copy-start | bytes 12582916
  14.8 5.3 %copy-start.3 = (bf16[1,2,2048]{2,1,0:T(2,128)(2,1)S(1)}, bf16[1,2,2048]{2,1,0:T(2,128)(2,1)}, u32[]{:S(2)}) copy-start(bf16[1,2,2048]{2,1,0:T(2,128)(2,1)} %new.3) | copy-start | bytes 24580
  16.4 9.5 %collective-permute-start.2 = (bf16[784,128]{1,0:T(8,128)(2,1)S(1)}, bf16[784,128]{1,0:T(8,128)(2,1)S(1)}, u32[]{:S(2)}, u32[]{:S(2)}) collective-permute-start(bf16[784,128]{1,0:T(8,128)(2,1)S(1)} %get-tuple-element.52), channel_id=1, source_target_pairs={{0,4},{4,8},{8,12},{12,14},{14,10},{10,6},{6,2},{2,0},{1,5},{5,9},... | collective-permute-start | bytes 602120 | tf_op jit(solution)/shard_map/ppermute | solution.py:538
  18.5 7.4 %collective-permute-start.3 = (bf16[768,128]{1,0:T(8,128)(2,1)S(1)}, bf16[768,128]{1,0:T(8,128)(2,1)S(1)}, u32[]{:S(2)}, u32[]{:S(2)}) collective-permute-start(bf16[768,128]{1,0:T(8,128)(2,1)S(1)} %get-tuple-element.50), channel_id=1, source_target_pairs={{0,2},{4,0},{8,4},{12,8},{14,12},{10,14},{6,10},{2,6},{1,3},{5,1},... | collective-permute-start | bytes 589832 | tf_op jit(solution)/shard_map/ppermute | solution.py:538
  22.1 3.9 %collective-permute-start.4 = (bf16[4,48,128]{2,1,0:T(8,128)(2,1)S(1)}, bf16[4,48,128]{2,1,0:T(8,128)(2,1)S(1)}, u32[]{:S(2)}, u32[]{:S(2)}) collective-permute-start(bf16[4,48,128]{2,1,0:T(8,128)(2,1)S(1)} %cache_attention.2), channel_id=1, source_target_pairs={{0,1},{1,0},{2,3},{3,2},{4,5},{5,4},{6,7},{7,6},{8,9},{9,8},{10,11... | collective-permute-start | bytes 147464 | tf_op jit(solution)/shard_map/ppermute | solution.py:541
  26.0 7.9 %collective-permute-start.5 = (bf16[784,128]{1,0:T(8,128)(2,1)S(1)}, bf16[784,128]{1,0:T(8,128)(2,1)S(1)}, u32[]{:S(2)}, u32[]{:S(2)}) collective-permute-start(bf16[784,128]{1,0:T(8,128)(2,1)S(1)} %get-tuple-element.58), channel_id=1, source_target_pairs={{0,4},{4,8},{8,12},{12,14},{14,10},{10,6},{6,2},{2,0},{1,5},{5,9},... | collective-permute-start | bytes 602120 | tf_op jit(solution)/shard_map/ppermute | solution.py:538
  27.8 7.9 %collective-permute-start.6 = (bf16[784,128]{1,0:T(8,128)(2,1)S(1)}, bf16[784,128]{1,0:T(8,128)(2,1)S(1)}, u32[]{:S(2)}, u32[]{:S(2)}) collective-permute-start(bf16[784,128]{1,0:T(8,128)(2,1)S(1)} %get-tuple-element.59), channel_id=1, source_target_pairs={{0,2},{4,0},{8,4},{12,8},{14,12},{10,14},{6,10},{2,6},{1,3},{5,1},... | collective-permute-start | bytes 602120 | tf_op jit(solution)/shard_map/ppermute | solution.py:538
  28.1 10.2 %collective-permute-start.8 = (bf16[768,128]{1,0:T(8,128)(2,1)S(1)}, bf16[768,128]{1,0:T(8,128)(2,1)S(1)}, u32[]{:S(2)}, u32[]{:S(2)}) collective-permute-start(bf16[768,128]{1,0:T(8,128)(2,1)S(1)} %get-tuple-element.63), channel_id=1, source_target_pairs={{0,2},{4,0},{8,4},{12,8},{14,12},{10,14},{6,10},{2,6},{1,3},{5,1},... | collective-permute-start | bytes 589832 | tf_op jit(solution)/shard_map/ppermute | solution.py:538
  28.6 9.7 %collective-permute-start.7 = (bf16[768,128]{1,0:T(8,128)(2,1)S(1)}, bf16[768,128]{1,0:T(8,128)(2,1)S(1)}, u32[]{:S(2)}, u32[]{:S(2)}) collective-permute-start(bf16[768,128]{1,0:T(8,128)(2,1)S(1)} %get-tuple-element.56), channel_id=1, source_target_pairs={{0,4},{4,8},{8,12},{12,14},{14,10},{10,6},{6,2},{2,0},{1,5},{5,9},... | collective-permute-start | bytes 589832 | tf_op jit(solution)/shard_map/ppermute | solution.py:538
  35.8 8.5 %collective-permute-start.9 = (bf16[784,128]{1,0:T(8,128)(2,1)S(1)}, bf16[784,128]{1,0:T(8,128)(2,1)S(1)}, u32[]{:S(2)}, u32[]{:S(2)}) collective-permute-start(bf16[784,128]{1,0:T(8,128)(2,1)S(1)} %get-tuple-element.66), channel_id=1, source_target_pairs={{0,4},{4,8},{8,12},{12,14},{14,10},{10,6},{6,2},{2,0},{1,5},{5,9},... | collective-permute-start | bytes 602120 | tf_op jit(solution)/shard_map/ppermute | solution.py:538
  37.5 6.8 %collective-permute-start.10 = (bf16[784,128]{1,0:T(8,128)(2,1)S(1)}, bf16[784,128]{1,0:T(8,128)(2,1)S(1)}, u32[]{:S(2)}, u32[]{:S(2)}) collective-permute-start(bf16[784,128]{1,0:T(8,128)(2,1)S(1)} %get-tuple-element.67), channel_id=1, source_target_pairs={{0,2},{4,0},{8,4},{12,8},{14,12},{10,14},{6,10},{2,6},{1,3},{5,1},... | collective-permute-start | bytes 602120 | tf_op jit(solution)/shard_map/ppermute | solution.py:538
  38.4 8.4 %collective-permute-start.14 = (bf16[768,128]{1,0:T(8,128)(2,1)S(1)}, bf16[768,128]{1,0:T(8,128)(2,1)S(1)}, u32[]{:S(2)}, u32[]{:S(2)}) collective-permute-start(bf16[768,128]{1,0:T(8,128)(2,1)S(1)} %get-tuple-element.74), channel_id=1, source_target_pairs={{0,2},{4,0},{8,4},{12,8},{14,12},{10,14},{6,10},{2,6},{1,3},{5,1},... | collective-permute-start | bytes 589832 | tf_op jit(solution)/shard_map/ppermute | solution.py:538
  38.7 8.3 %collective-permute-start.13 = (bf16[768,128]{1,0:T(8,128)(2,1)S(1)}, bf16[768,128]{1,0:T(8,128)(2,1)S(1)}, u32[]{:S(2)}, u32[]{:S(2)}) collective-permute-start(bf16[768,128]{1,0:T(8,128)(2,1)S(1)} %get-tuple-element.64), channel_id=1, source_target_pairs={{0,4},{4,8},{8,12},{12,14},{14,10},{10,6},{6,2},{2,0},{1,5},{5,9},... | collective-permute-start | bytes 589832 | tf_op jit(solution)/shard_map/ppermute | solution.py:538
  44.4 11.0 %collective-permute-start.11 = (bf16[784,128]{1,0:T(8,128)(2,1)S(1)}, bf16[784,128]{1,0:T(8,128)(2,1)S(1)}, u32[]{:S(2)}, u32[]{:S(2)}) collective-permute-start(bf16[784,128]{1,0:T(8,128)(2,1)S(1)} %get-tuple-element.71), channel_id=1, source_target_pairs={{0,4},{4,8},{8,12},{12,14},{14,10},{10,6},{6,2},{2,0},{1,5},{5,9},... | collective-permute-start | bytes 602120 | tf_op jit(solution)/shard_map/ppermute | solution.py:538
  46.3 9.1 %collective-permute-start.12 = (bf16[784,128]{1,0:T(8,128)(2,1)S(1)}, bf16[784,128]{1,0:T(8,128)(2,1)S(1)}, u32[]{:S(2)}, u32[]{:S(2)}) collective-permute-start(bf16[784,128]{1,0:T(8,128)(2,1)S(1)} %get-tuple-element.72), channel_id=1, source_target_pairs={{0,2},{4,0},{8,4},{12,8},{14,12},{10,14},{6,10},{2,6},{1,3},{5,1},... | collective-permute-start | bytes 602120 | tf_op jit(solution)/shard_map/ppermute | solution.py:538
  47.1 7.2 %collective-permute-start.15 = (bf16[768,128]{1,0:T(8,128)(2,1)S(1)}, bf16[768,128]{1,0:T(8,128)(2,1)S(1)}, u32[]{:S(2)}, u32[]{:S(2)}) collective-permute-start(bf16[768,128]{1,0:T(8,128)(2,1)S(1)} %get-tuple-element.75), channel_id=1, source_target_pairs={{0,4},{4,8},{8,12},{12,14},{14,10},{10,6},{6,2},{2,0},{1,5},{5,9},... | collective-permute-start | bytes 589832 | tf_op jit(solution)/shard_map/ppermute | solution.py:538
  49.0 6.5 %collective-permute-start.16 = (bf16[768,128]{1,0:T(8,128)(2,1)S(1)}, bf16[768,128]{1,0:T(8,128)(2,1)S(1)}, u32[]{:S(2)}, u32[]{:S(2)}) collective-permute-start(bf16[768,128]{1,0:T(8,128)(2,1)S(1)} %get-tuple-element.76), channel_id=1, source_target_pairs={{0,2},{4,0},{8,4},{12,8},{14,12},{10,14},{6,10},{2,6},{1,3},{5,1},... | collective-permute-start | bytes 589832 | tf_op jit(solution)/shard_map/ppermute | solution.py:538

commit v11 on v10

--- a/solution.py
+++ b/solution.py
@@ -114,17 +114,22 @@
     return stood(tail[0:1, :] + tail[1:2, :] + tail[2:3, :], ROWS)
 
 
-def gathered_levels(table, codes):
-    numbers = lax.GatherDimensionNumbers(
-        offset_dims=(),
-        collapsed_slice_dims=(1,),
-        start_index_map=(1,),
-        operand_batching_dims=(0,),
-        start_indices_batching_dims=(0,),
-    )
-    return lax.gather(
-        table, codes[..., None], numbers, (1, 1), mode=lax.GatherScatterMode.PROMISE_IN_BOUNDS
-    )
+def block_leaves(scale):
+    wide = jnp.broadcast_to(scale, (16, HEAD_DIM))
+    return [(wide * jnp.float32(level)).astype(BF16) for level in NORMAL_FLOAT_LEVELS]
+
+
+def selected(codes, leaves):
+    codes = codes.astype(jnp.int16)
+    masks = [(codes & (1 << bit)) != 0 for bit in range(4)]
+
+    def node(bit, base):
+        if bit < 0:
+            return leaves[base]
+        low = node(bit - 1, base)
+        return jnp.where(masks[bit], node(bit - 1, base + (1 << bit)), low)
+
+    return node(3, 0)
 
 
 def block_scales(scales, outer, column):
@@ -151,27 +156,19 @@
             scales[2 * at] = block_scales(key_scales[:, lanes], outer[...], column)
             scales[2 * at + 1] = block_scales(value_scales[:, lanes], outer[...], columns + column)
 
-    lane = lax.broadcasted_iota(jnp.int32, (8, 128), 1)
-    table = jnp.zeros((8, 128), F32)
-    for code, level in enumerate(NORMAL_FLOAT_LEVELS):
-        table = jnp.where(lane == code, level, table)
-
     def body(step, _):
         begin = pl.multiple_of(step * QBLOCK, QBLOCK)
         row = pl.ds(block * (depth // QBLOCK) + step, 1)
         for at in range(CORE_HEADS):
             lanes = slice(at * HEAD_DIM, (at + 1) * HEAD_DIM)
-            key_scale, value_scale = scales[2 * at, row, :], scales[2 * at + 1, row, :]
-            for tile in range(QBLOCK // 16):
-                rows = pl.ds(pl.multiple_of(begin + 16 * tile, 16), 16)
-                key, value = key_codes[rows, lanes], value_codes[rows, lanes]
-                keys = [gathered_levels(table, key[half : half + 8]) for half in (0, 8)]
-                values = [gathered_levels(table, value[half : half + 8]) for half in (0, 8)]
-                rows = pl.ds(pl.multiple_of(block * depth + begin + 16 * tile, 16), 16)
-                keys = jnp.concatenate([level * key_scale for level in keys], axis=0)
-                values = jnp.concatenate([level * value_scale for level in values], axis=0)
-                out[at, rows, :HEAD_DIM] = keys.astype(BF16)
-                out[at, rows, HEAD_DIM:] = values.astype(BF16)
+            for kind, codes in enumerate((key_codes, value_codes)):
+                leaves = block_leaves(scales[2 * at + kind, row, :])
+                columns = slice(kind * HEAD_DIM, (kind + 1) * HEAD_DIM)
+                for tile in range(QBLOCK // 16):
+                    rows = pl.ds(pl.multiple_of(begin + 16 * tile, 16), 16)
+                    weight = selected(codes[rows, lanes], leaves)
+                    rows = pl.ds(pl.multiple_of(block * depth + begin + 16 * tile, 16), 16)
+                    out[at, rows, columns] = weight
         return 0
 
     lax.fori_loop(0, depth // QBLOCK, body, 0)
@@ -204,36 +201,53 @@
     )(codes, codes, scales, scales, outer)
 
 
-def scale_kernel(x, gain, scaled, squares):
-    item = pl.program_id(0)
-
-    @pl.when(item == 0)
-    def _():
-        squares[...] = jnp.zeros(squares.shape, F32)
-
-    width = x.shape[2]
-    begin = pl.multiple_of(item * width, 128)
-    for prompt in range(x.shape[0]):
-        wide = x[prompt].astype(F32)
-        scaled[prompt, :, pl.ds(begin, width)] = (wide * gain[...]).astype(BF16)
-        squares[prompt] += token_rows(jnp.sum(wide * wide, axis=1, keepdims=True))
+def scale_kernel(x, gain, scaled, squares, lines, factors, column, arrivals):
+    half = STRETCH // 2
+    pieces = [(prompt, slice(at, at + half)) for prompt in range(x.shape[0]) for at in (0, half)]
+
+    def copy(item):
+        prompt, rows = pieces[item]
+        return pltpu.make_async_copy(
+            x.at[prompt, rows], lines.at[prompt, rows], arrivals.at[item]
+        )
+
+    gain_copy = pltpu.make_async_copy(gain, factors, arrivals.at[len(pieces)])
+    gain_copy.start()
+    for item in range(len(pieces)):
+        copy(item).start()
+    gain_copy.wait()
+    for item, (prompt, rows) in enumerate(pieces):
+        copy(item).wait()
+        begin = rows.start
+
+        def body(step, _, prompt=prompt, begin=begin):
+            rows = pl.ds(pl.multiple_of(begin + step * 16, 16), 16)
+            wide = lines[prompt, rows, :].astype(F32)
+            scaled[prompt, rows, :] = (wide * factors[...]).astype(BF16)
+            total = jnp.sum(wide * wide, axis=1, keepdims=True)
+            column[rows, :] = jnp.broadcast_to(total, (16, 128))
+            return 0
+
+        lax.fori_loop(0, half // 16, body, 0)
+        if begin > 0:
+            squares[prompt] = token_rows(column[:, :1])
 
 
 def scale_features(x, gain):
-    per_rep, _, features = x.shape
-    width = max(128, features // 4)
     x, gain = in_hbm(x, gain)
     return pl.pallas_call(
         scale_kernel,
-        grid=(features // width,),
-        in_specs=[
-            pl.BlockSpec((per_rep, STRETCH, width), lambda i: (0, 0, i)),
-            pl.BlockSpec((1, width), lambda i: (0, i)),
-        ],
+        in_specs=[pl.BlockSpec(memory_space=pltpu.HBM)] * 2,
         out_specs=[VMEM] * 2,
         out_shape=[
             jax.ShapeDtypeStruct(x.shape, BF16),
-            jax.ShapeDtypeStruct((per_rep, 8, 128), F32),
+            jax.ShapeDtypeStruct((x.shape[0], 8, 128), F32),
+        ],
+        scratch_shapes=[
+            pltpu.VMEM(x.shape, BF16),
+            pltpu.VMEM(gain.shape, F32),
+            pltpu.VMEM((STRETCH, 128), F32),
+            pltpu.SemaphoreType.DMA((2 * x.shape[0] + 1,)),
         ],
         compiler_params=pltpu.CompilerParams(vmem_limit_bytes=24 * MIB),
         name="scale_features",
@@ -544,14 +558,12 @@
     frequency, turns = rotary_turns()
     start = (prompt_lengths - STRETCH).astype(F32)[:, None] * jnp.asarray(frequency)
     starts = jnp.stack([jnp.cos(start), jnp.sin(start)])
-    targets, weight = lax.optimization_barrier((target_rows, weight))
-    grouped, rotary = prepare(targets, queries, starts, jnp.asarray(turns))
-
-    weight, grouped, rotary = lax.optimization_barrier((weight, grouped, rotary))
+
     features = [own, squares, other, other_squares]
     right, left = project_first(half, target_rows, *features, weight)
     targets, _ = lax.optimization_barrier((target_rows, left))
     arrived = [pass_on(right, left)] * 2
+    grouped, rotary = prepare(targets, queries, starts, jnp.asarray(turns))
 
     cached = []
     for distance in range(half - 1, 0, -1):

time: 60 us -> 60.8 us (1.013)
    ppermute x7, starting transfers between devices: 2.92 us -> 5.95 us  [pass_on(): lax.ppermute(left, 'tp', to_left)]
    ppermute x7, starting transfers between devices: 12.6 us -> 9.63 us  [pass_on(): lax.ppermute(right, 'tp', to_right)]
    pallas_call x1, Pallas kernels: 2.99 us -> 5.31 us  [scale_features(): pl.pallas_call(scale_kernel, in_specs=[pl.BlockSpec(memory_space=pltpu.HB...]
    pallas_call x1, Pallas kernels: 10.3 us -> 8.58 us  [dequantize(): pl.pallas_call(weights_kernel, grid=(features // depth,), in_specs=[pl.Bl...]
  transfers between devices with their start and end apart: 17 -> 17, of which waited for: 7 -> 7; matrix products, arithmetic and copies ran while one was open for 0% -> 0% of each run, Pallas kernels for 38% -> 34%
where the time goes in v11:
time: 60.8 us; the launch traced here: 60.6 us
  Pallas kernels  29.5 us (49%)
  starting transfers between devices  16.3 us (27%)
  waiting for transfers between devices  11.3 us (19%)
  blocking collectives  1.85 us (3%)
  between operations  0.91 us (1%)
  local copies, waits for them, and re-layouts  0.67 us (1%)
    ppermute x7, starting transfers between devices, pass_on(): lax.ppermute(right, 'tp', to_right)  9.63 us
    pallas_call x1, Pallas kernels, dequantize(): pl.pallas_call(weights_kernel, grid=(features // depth,), in_specs=[pl.Bl...  8.58 us
    pallas_call x3, Pallas kernels, project(): pl.pallas_call(functools.partial(project_kernel, distances), in_specs=[SM...  6.9 us
    ppermute x7, starting transfers between devices, pass_on(): lax.ppermute(left, 'tp', to_left)  5.95 us
    ppermute x7, waiting for transfers between devices, pass_on(): lax.ppermute(left, 'tp', to_left)  5.69 us
    ppermute x7, waiting for transfers between devices, pass_on(): lax.ppermute(right, 'tp', to_right)  5.61 us
    pallas_call x1, Pallas kernels, scale_features(): pl.pallas_call(scale_kernel, in_specs=[pl.BlockSpec(memory_space=pltpu.HB...  5.31 us
    pallas_call x2, Pallas kernels, cache_attention(): pl.pallas_call(functools.partial(cache_kernel, part), in_specs=[SMEM] * 3...  3.98 us
  transfers between devices with their start and end apart: 17, of which 7 were waited for; matrix products, arithmetic and copies ran while one was open for 0% of the time, Pallas kernels for 34%

profile of v11, /device:TPU:0, one launch (start us, length us, event | category | flops | bytes accessed | tf_op | source)
XLA Modules:
  0.0 60.6 jit_solution(7305000979139338882)
XLA Ops:
  0.0 5.3 %scale_features.1 = (bf16[3,192,2048]{2,1,0:T(8,128)(2,1)S(1)}, f32[3,8,128]{2,1,0:T(8,128)S(1)}) custom-call(bf16[3,192,2048]{2,1,0:T(8,128)(2,1)} %bitcast.3, f32[1,2048]{1,0:T(1,128)} %bitcast.4), custom_call_target="tpu_custom_call" | custom-call | tf_op jit(solution)/shard_map/scale_features/pallas_call | solution.py:238
  5.3 0.5 collective-permute-start
  5.8 0.1 collective-permute-start.1
  5.9 8.6 %dequantize.1.weight = bf16[4,2048,256]{2,1,0:T(8,128)(2,1)S(1)} custom-call(s32[2048,2048]{1,0:T(8,128)} %value_codes.1, s32[2048,2048]{1,0:T(8,128)} %value_codes.1, s32[32,2048]{1,0:T(8,128)} %value_scales.1, s32[32,2048]{1,0:T(8,128)} %value_scales.1, f32[8,32]{1,0:T(8,128)} %bitcast.5), custom_call_target="tpu_custom_call" | custom-call | flops 134217728 | bytes 8388608 | tf_op jit(solution)/shard_map/dequantize/pallas_call | solution.py:183
  14.5 0.0 copy-start.6
  14.5 0.0 copy-start.1
  14.5 0.0 copy-start.2
  14.6 0.0 copy-start.3
  14.6 0.0 copy-start
  14.6 1.6 %project_first.1 = (bf16[784,128]{1,0:T(8,128)(2,1)S(1)}, bf16[768,128]{1,0:T(8,128)(2,1)S(1)}) custom-call(s32[6]{0:T(128)S(1)} %copy-done.4, bf16[3,192,2048]{2,1,0:T(8,128)(2,1)S(1)} %get-tuple-element.37.own, f32[3,8,128]{2,1,0:T(8,128)S(1)} %get-tuple-element.38.squares, bf16[3,192,2048]{2,1,0:T(8,128)(2,1)S(1)} %collective-permute-done.other, ...), custom_call_target="tpu_custom_call" | custom-call | flops 805306368 | bytes 2097152 | tf_op jit(solution)/shard_map/project_first/pallas_call | solution.py:294
  16.2 2.0 %collective-permute-start.3 = (bf16[768,128]{1,0:T(8,128)(2,1)S(1)}, bf16[768,128]{1,0:T(8,128)(2,1)S(1)}, u32[]{:S(2)}, u32[]{:S(2)}) collective-permute-start(bf16[768,128]{1,0:T(8,128)(2,1)S(1)} %get-tuple-element.39), channel_id=1, source_target_pairs={{0,2},{4,0},{8,4},{12,8},{14,12},{10,14},{6,10},{2,6},{1,3},{5,1},... | collective-permute-start | bytes 589832 | tf_op jit(solution)/shard_map/ppermute | solution.py:552
  18.2 1.1 %collective-permute-start.2 = (bf16[784,128]{1,0:T(8,128)(2,1)S(1)}, bf16[784,128]{1,0:T(8,128)(2,1)S(1)}, u32[]{:S(2)}, u32[]{:S(2)}) collective-permute-start(bf16[784,128]{1,0:T(8,128)(2,1)S(1)} %get-tuple-element.42), channel_id=1, source_target_pairs={{0,4},{4,8},{8,12},{12,14},{14,10},{10,6},{6,2},{2,0},{1,5},{5,9},... | collective-permute-start | bytes 602120 | tf_op jit(solution)/shard_map/ppermute | solution.py:552
  19.3 0.1 multiply_cosine_fusion
  20.1 0.7 %prepare.1 = (bf16[8,32,128]{2,1,0:T(8,128)(2,1)S(1)}, f32[2,192,128]{2,1,0:T(8,128)S(1)}) custom-call(s32[6]{0:T(128)S(1)} %copy-done.4, bf16[1,2,16384]{2,1,0:T(2,128)(2,1)S(1)} %copy-done.2, f32[2,6,128]{2,1,0:T(8,128)S(1)} %pad_maximum_fusion.starts, f32[2,192,128]{2,1,0:T(8,128)S(1)} %copy-done.1), custom_call_target="tpu_custom_call" | custom-call | tf_op jit(solution)/shard_map/prepare/pallas_call | solution.py:395
  20.8 2.0 %cache_attention.2 = bf16[4,48,128]{2,1,0:T(8,128)(2,1)S(1)} custom-call(s32[6]{0:T(128)S(1)} %copy-done.4, s32[6]{0:T(128)S(1)} %copy-done.5, s32[1]{0:T(128)S(6)} %copy.15.stored, bf16[8,32,128]{2,1,0:T(8,128)(2,1)S(1)} %get-tuple-element.44.q.grouped, bf16[1,1024,2048]{2,1,0:T(8,128)(2,1)S(1)} %copy-done, bf16[1,2,2048]{2,1,0:T(2,128)(2,1)S(1)} %copy-done.3), custom_call_target="tpu_custom_call" | custom-call | flops 67108864 | bytes 2097152 | tf_op jit(solution)/shard_map/cache_attention/pallas_call | solution.py:452
  22.8 0.1 collective-permute-start.4
  22.9 1.7 %project.3.terms = f32[2,2,776,128]{3,2,1,0:T(8,128)S(1)} custom-call(s32[6]{0:T(128)S(1)} %copy-done.4, bf16[3,192,2048]{2,1,0:T(8,128)(2,1)S(1)} %get-tuple-element.37.own, f32[3,8,128]{2,1,0:T(8,128)S(1)} %get-tuple-element.38.squares, bf16[3,192,2048]{2,1,0:T(8,128)(2,1)S(1)} %collective-permute-done.other, ...), custom_call_target="tpu_custom_call" | custom-call | flops 805306368 | bytes 2097152 | tf_op jit(solution)/shard_map/project/pallas_call | solution.py:330
  24.6 1.1 %collective-permute-done.2.right = bf16[784,128]{1,0:T(8,128)(2,1)S(1)} collective-permute-done((bf16[784,128]{1,0:T(8,128)(2,1)S(1)}, bf16[784,128]{1,0:T(8,128)(2,1)S(1)}, u32[]{:S(2)}, u32[]{:S(2)}) %collective-permute-start.2) | collective-permute-done | bytes 200736 | tf_op jit(solution)/shard_map/ppermute | solution.py:552
  25.7 0.1 sends.6
  25.8 1.8 %collective-permute-start.5 = (bf16[784,128]{1,0:T(8,128)(2,1)S(1)}, bf16[784,128]{1,0:T(8,128)(2,1)S(1)}, u32[]{:S(2)}, u32[]{:S(2)}) collective-permute-start(bf16[784,128]{1,0:T(8,128)(2,1)S(1)} %get-tuple-element.48), channel_id=1, source_target_pairs={{0,4},{4,8},{8,12},{12,14},{14,10},{10,6},{6,2},{2,0},{1,5},{5,9},... | collective-permute-start | bytes 602120 | tf_op jit(solution)/shard_map/ppermute | solution.py:552
  27.6 0.3 collective-permute-start.6
  27.8 0.1 sends.7
  27.9 1.8 %collective-permute-start.8 = (bf16[768,128]{1,0:T(8,128)(2,1)S(1)}, bf16[768,128]{1,0:T(8,128)(2,1)S(1)}, u32[]{:S(2)}, u32[]{:S(2)}) collective-permute-start(bf16[768,128]{1,0:T(8,128)(2,1)S(1)} %get-tuple-element.53), channel_id=1, source_target_pairs={{0,2},{4,0},{8,4},{12,8},{14,12},{10,14},{6,10},{2,6},{1,3},{5,1},... | collective-permute-start | bytes 589832 | tf_op jit(solution)/shard_map/ppermute | solution.py:552
  29.7 0.3 collective-permute-start.7
  30.0 2.0 %cache_attention.3.cached_here = bf16[4,48,128]{2,1,0:T(8,128)(2,1)S(1)} custom-call(s32[6]{0:T(128)S(1)} %copy-done.4, s32[6]{0:T(128)S(1)} %copy-done.5, s32[1]{0:T(128)S(6)} %copy.15.stored, bf16[8,32,128]{2,1,0:T(8,128)(2,1)S(1)} %get-tuple-element.44.q.grouped, bf16[1,1024,2048]{2,1,0:T(8,128)(2,1)S(1)} %copy-done, bf16[1,2,2048]{2,1,0:T(2,128)(2,1)S(1)} %copy-done.3), custom_call_target="tpu_custom_call" | custom-call | flops 67108864 | bytes 2097152 | tf_op jit(solution)/shard_map/cache_attention/pallas_call | solution.py:452
  32.0 2.6 %project.4.terms = f32[2,2,776,128]{3,2,1,0:T(8,128)S(1)} custom-call(s32[6]{0:T(128)S(1)} %copy-done.4, bf16[3,192,2048]{2,1,0:T(8,128)(2,1)S(1)} %get-tuple-element.37.own, f32[3,8,128]{2,1,0:T(8,128)S(1)} %get-tuple-element.38.squares, bf16[3,192,2048]{2,1,0:T(8,128)(2,1)S(1)} %collective-permute-done.other, ...), custom_call_target="tpu_custom_call" | custom-call | flops 805306368 | bytes 2097152 | tf_op jit(solution)/shard_map/project/pallas_call | solution.py:330
  34.6 0.8 %collective-permute-done.6.left = bf16[784,128]{1,0:T(8,128)(2,1)S(1)} collective-permute-done((bf16[784,128]{1,0:T(8,128)(2,1)S(1)}, bf16[784,128]{1,0:T(8,128)(2,1)S(1)}, u32[]{:S(2)}, u32[]{:S(2)}) %collective-permute-start.6) | collective-permute-done | bytes 200736 | tf_op jit(solution)/shard_map/ppermute | solution.py:552
  35.4 0.1 sends.8
  35.5 1.6 %collective-permute-start.9 = (bf16[784,128]{1,0:T(8,128)(2,1)S(1)}, bf16[784,128]{1,0:T(8,128)(2,1)S(1)}, u32[]{:S(2)}, u32[]{:S(2)}) collective-permute-start(bf16[784,128]{1,0:T(8,128)(2,1)S(1)} %get-tuple-element.56), channel_id=1, source_target_pairs={{0,4},{4,8},{8,12},{12,14},{14,10},{10,6},{6,2},{2,0},{1,5},{5,9},... | collective-permute-start | bytes 602120 | tf_op jit(solution)/shard_map/ppermute | solution.py:552
  37.1 0.4 collective-permute-start.10
  37.6 2.0 %collective-permute-done.8.left = bf16[768,128]{1,0:T(8,128)(2,1)S(1)} collective-permute-done((bf16[768,128]{1,0:T(8,128)(2,1)S(1)}, bf16[768,128]{1,0:T(8,128)(2,1)S(1)}, u32[]{:S(2)}, u32[]{:S(2)}) %collective-permute-start.8) | collective-permute-done | bytes 196640 | tf_op jit(solution)/shard_map/ppermute | solution.py:552
  39.6 0.1 sends.9
  39.7 0.2 collective-permute-start.14
  39.9 1.9 %collective-permute-start.13 = (bf16[768,128]{1,0:T(8,128)(2,1)S(1)}, bf16[768,128]{1,0:T(8,128)(2,1)S(1)}, u32[]{:S(2)}, u32[]{:S(2)}) collective-permute-start(bf16[768,128]{1,0:T(8,128)(2,1)S(1)} %get-tuple-element.54), channel_id=1, source_target_pairs={{0,4},{4,8},{8,12},{12,14},{14,10},{10,6},{6,2},{2,0},{1,5},{5,9},... | collective-permute-start | bytes 589832 | tf_op jit(solution)/shard_map/ppermute | solution.py:552
  41.8 2.7 %project.5.terms.own = f32[3,2,776,128]{3,2,1,0:T(8,128)S(1)} custom-call(s32[6]{0:T(128)S(1)} %copy-done.4, bf16[3,192,2048]{2,1,0:T(8,128)(2,1)S(1)} %get-tuple-element.37.own, f32[3,8,128]{2,1,0:T(8,128)S(1)} %get-tuple-element.38.squares, bf16[3,192,2048]{2,1,0:T(8,128)(2,1)S(1)} %collective-permute-done.other, ...), custom_call_target="tpu_custom_call" | custom-call | flops 1207959552 | bytes 2097152 | tf_op jit(solution)/shard_map/project/pallas_call | solution.py:330
  44.5 0.6 %collective-permute-done.10.left = bf16[784,128]{1,0:T(8,128)(2,1)S(1)} collective-permute-done((bf16[784,128]{1,0:T(8,128)(2,1)S(1)}, bf16[784,128]{1,0:T(8,128)(2,1)S(1)}, u32[]{:S(2)}, u32[]{:S(2)}) %collective-permute-start.10) | collective-permute-done | bytes 200736 | tf_op jit(solution)/shard_map/ppermute | solution.py:552
  45.1 0.1 sends.10
  45.2 1.0 %collective-permute-start.11 = (bf16[784,128]{1,0:T(8,128)(2,1)S(1)}, bf16[784,128]{1,0:T(8,128)(2,1)S(1)}, u32[]{:S(2)}, u32[]{:S(2)}) collective-permute-start(bf16[784,128]{1,0:T(8,128)(2,1)S(1)} %get-tuple-element.61), channel_id=1, source_target_pairs={{0,4},{4,8},{8,12},{12,14},{14,10},{10,6},{6,2},{2,0},{1,5},{5,9},... | collective-permute-start | bytes 602120 | tf_op jit(solution)/shard_map/ppermute | solution.py:552
  46.2 1.0 %collective-permute-start.12 = (bf16[784,128]{1,0:T(8,128)(2,1)S(1)}, bf16[784,128]{1,0:T(8,128)(2,1)S(1)}, u32[]{:S(2)}, u32[]{:S(2)}) collective-permute-start(bf16[784,128]{1,0:T(8,128)(2,1)S(1)} %get-tuple-element.62), channel_id=1, source_target_pairs={{0,2},{4,0},{8,4},{12,8},{14,12},{10,14},{6,10},{2,6},{1,3},{5,1},... | collective-permute-start | bytes 602120 | tf_op jit(solution)/shard_map/ppermute | solution.py:552
  47.3 0.9 %collective-permute-done.14.left = bf16[768,128]{1,0:T(8,128)(2,1)S(1)} collective-permute-done((bf16[768,128]{1,0:T(8,128)(2,1)S(1)}, bf16[768,128]{1,0:T(8,128)(2,1)S(1)}, u32[]{:S(2)}, u32[]{:S(2)}) %collective-permute-start.14) | collective-permute-done | bytes 196640 | tf_op jit(solution)/shard_map/ppermute | solution.py:552
  48.1 0.1 sends.11
  48.2 1.9 %collective-permute-start.15 = (bf16[768,128]{1,0:T(8,128)(2,1)S(1)}, bf16[768,128]{1,0:T(8,128)(2,1)S(1)}, u32[]{:S(2)}, u32[]{:S(2)}) collective-permute-start(bf16[768,128]{1,0:T(8,128)(2,1)S(1)} %get-tuple-element.65), channel_id=1, source_target_pairs={{0,4},{4,8},{8,12},{12,14},{14,10},{10,6},{6,2},{2,0},{1,5},{5,9},... | collective-permute-start | bytes 589832 | tf_op jit(solution)/shard_map/ppermute | solution.py:552
  50.1 0.2 collective-permute-start.16
  50.3 4.5 %collective-permute-done.15.right_b = bf16[768,128]{1,0:T(8,128)(2,1)S(1)} collective-permute-done((bf16[768,128]{1,0:T(8,128)(2,1)S(1)}, bf16[768,128]{1,0:T(8,128)(2,1)S(1)}, u32[]{:S(2)}, u32[]{:S(2)}) %collective-permute-start.15) | collective-permute-done | bytes 196640 | tf_op jit(solution)/shard_map/ppermute | solution.py:552
  54.8 1.4 %collective-permute-done.16.left_b = bf16[768,128]{1,0:T(8,128)(2,1)S(1)} collective-permute-done((bf16[768,128]{1,0:T(8,128)(2,1)S(1)}, bf16[768,128]{1,0:T(8,128)(2,1)S(1)}, u32[]{:S(2)}, u32[]{:S(2)}) %collective-permute-start.16) | collective-permute-done | bytes 196640 | tf_op jit(solution)/shard_map/ppermute | solution.py:552
  56.1 2.0 %finish.1 = bf16[1,2,8192]{2,1,0:T(2,128)(2,1)S(1)} custom-call(s32[6]{0:T(128)S(1)} %copy-done.4, f32[2,192,128]{2,1,0:T(8,128)S(1)} %get-tuple-element.41.rotary, f32[3,2,776,128]{3,2,1,0:T(8,128)S(1)} %project.5.terms.own, bf16[784,128]{1,0:T(8,128)(2,1)S(1)} %collective-permute-done.11.right_a, bf16[784,128]{1,0:T(8,128)(2,1)S(1)} %collective-permute-done.12.left_a, ...), custom_call_target="tpu_custom_call" | custom-call | tf_op jit(solution)/shard_map/finish/pallas_call | solution.py:513
  58.1 1.9 %all_gather.3 = bf16[1,2,16384]{2,1,0:T(2,128)(2,1)S(1)} all-gather(bf16[1,2,8192]{2,1,0:T(2,128)(2,1)S(1)} %finish.1), channel_id=1, replica_groups=mesh['grp'=2,'tp'=8,'rep'=2] {'rep'}, dimensions={2}, use_global_device_ids=true | all-gather | bytes 98304 | tf_op jit(solution)/shard_map/all_gather | solution.py:589
  60.0 0.6 %copy.16 = bf16[1,2,16384]{2,1,0:T(2,128)(2,1)} copy(bf16[1,2,16384]{2,1,0:T(2,128)(2,1)S(1)} %all_gather.3) | data formatting | bytes 131072
  (21 shorter events, 0.1 us)
Async XLA Ops:
  0.0 5.9 %copy-start.5 = (s32[6]{0:T(128)S(1)}, s32[6]{0:T(128)}, u32[]{:S(2)}) copy-start(s32[6]{0:T(128)} %lengths.3) | copy-start | bytes 76
  5.3 9.3 %collective-permute-start = (bf16[3,192,2048]{2,1,0:T(8,128)(2,1)S(1)}, bf16[3,192,2048]{2,1,0:T(8,128)(2,1)S(1)}, u32[]{:S(2)}, u32[]{:S(2)}) collective-permute-start(bf16[3,192,2048]{2,1,0:T(8,128)(2,1)S(1)} %get-tuple-element.37.own), channel_id=1, source_target_pairs={{0,1},{1,0},{2,3},{3,2},{4,5},{5,4},{6,7},{7,6},{8,9},{9,8},{10,11... | collective-permute-start | bytes 7077896 | tf_op jit(solution)/shard_map/ppermute | solution.py:555
  5.8 8.7 %collective-permute-start.1 = (f32[3,8,128]{2,1,0:T(8,128)S(1)}, f32[3,8,128]{2,1,0:T(8,128)S(1)}, u32[]{:S(2)}, u32[]{:S(2)}) collective-permute-start(f32[3,8,128]{2,1,0:T(8,128)S(1)} %get-tuple-element.38.squares), channel_id=1, source_target_pairs={{0,1},{1,0},{2,3},{3,2},{4,5},{5,4},{6,7},{7,6},{8,9},{9,8},{10,11... | collective-permute-start | bytes 36872 | tf_op jit(solution)/shard_map/ppermute | solution.py:555
  5.9 8.7 %copy-start.4 = (s32[6]{0:T(128)S(1)}, s32[6]{0:T(128)}, u32[]{:S(2)}) copy-start(s32[6]{0:T(128)} %targets.9) | copy-start | bytes 76
  14.5 4.8 %copy-start.6 = (f32[128]{0:T(128)S(1)}, f32[128]{0:T(128)}, u32[]{:S(2)}) copy-start(f32[128]{0:T(128)} %constant.7.clone) | copy-start | bytes 1540
  14.5 5.6 %copy-start.1 = (f32[2,192,128]{2,1,0:T(8,128)S(1)}, f32[2,192,128]{2,1,0:T(8,128)}, u32[]{:S(2)}) copy-start(f32[2,192,128]{2,1,0:T(8,128)} %constant.8.clone.turns) | copy-start | bytes 589828
  14.5 5.6 %copy-start.2 = (bf16[1,2,16384]{2,1,0:T(2,128)(2,1)S(1)}, bf16[1,2,16384]{2,1,0:T(2,128)(2,1)}, u32[]{:S(2)}) copy-start(bf16[1,2,16384]{2,1,0:T(2,128)(2,1)} %queries.1) | copy-start | bytes 196612
  14.6 6.2 %copy-start.3 = (bf16[1,2,2048]{2,1,0:T(2,128)(2,1)S(1)}, bf16[1,2,2048]{2,1,0:T(2,128)(2,1)}, u32[]{:S(2)}) copy-start(bf16[1,2,2048]{2,1,0:T(2,128)(2,1)} %new.3) | copy-start | bytes 24580
  14.6 6.2 %copy-start = (bf16[1,1024,2048]{2,1,0:T(8,128)(2,1)S(1)}, bf16[1,1024,2048]{2,1,0:T(8,128)(2,1)}, u32[]{:S(2)}) copy-start(bf16[1,1024,2048]{2,1,0:T(8,128)(2,1)} %cache.3) | copy-start | bytes 12582916
  16.2 8.4 %collective-permute-start.3 = (bf16[768,128]{1,0:T(8,128)(2,1)S(1)}, bf16[768,128]{1,0:T(8,128)(2,1)S(1)}, u32[]{:S(2)}, u32[]{:S(2)}) collective-permute-start(bf16[768,128]{1,0:T(8,128)(2,1)S(1)} %get-tuple-element.39), channel_id=1, source_target_pairs={{0,2},{4,0},{8,4},{12,8},{14,12},{10,14},{6,10},{2,6},{1,3},{5,1},... | collective-permute-start | bytes 589832 | tf_op jit(solution)/shard_map/ppermute | solution.py:552
  18.2 7.5 %collective-permute-start.2 = (bf16[784,128]{1,0:T(8,128)(2,1)S(1)}, bf16[784,128]{1,0:T(8,128)(2,1)S(1)}, u32[]{:S(2)}, u32[]{:S(2)}) collective-permute-start(bf16[784,128]{1,0:T(8,128)(2,1)S(1)} %get-tuple-element.42), channel_id=1, source_target_pairs={{0,4},{4,8},{8,12},{12,14},{14,10},{10,6},{6,2},{2,0},{1,5},{5,9},... | collective-permute-start | bytes 602120 | tf_op jit(solution)/shard_map/ppermute | solution.py:552
  22.8 3.0 %collective-permute-start.4 = (bf16[4,48,128]{2,1,0:T(8,128)(2,1)S(1)}, bf16[4,48,128]{2,1,0:T(8,128)(2,1)S(1)}, u32[]{:S(2)}, u32[]{:S(2)}) collective-permute-start(bf16[4,48,128]{2,1,0:T(8,128)(2,1)S(1)} %cache_attention.2), channel_id=1, source_target_pairs={{0,1},{1,0},{2,3},{3,2},{4,5},{5,4},{6,7},{7,6},{8,9},{9,8},{10,11... | collective-permute-start | bytes 147464 | tf_op jit(solution)/shard_map/ppermute | solution.py:555
  25.8 8.8 %collective-permute-start.5 = (bf16[784,128]{1,0:T(8,128)(2,1)S(1)}, bf16[784,128]{1,0:T(8,128)(2,1)S(1)}, u32[]{:S(2)}, u32[]{:S(2)}) collective-permute-start(bf16[784,128]{1,0:T(8,128)(2,1)S(1)} %get-tuple-element.48), channel_id=1, source_target_pairs={{0,4},{4,8},{8,12},{12,14},{14,10},{10,6},{6,2},{2,0},{1,5},{5,9},... | collective-permute-start | bytes 602120 | tf_op jit(solution)/shard_map/ppermute | solution.py:552
  27.6 7.8 %collective-permute-start.6 = (bf16[784,128]{1,0:T(8,128)(2,1)S(1)}, bf16[784,128]{1,0:T(8,128)(2,1)S(1)}, u32[]{:S(2)}, u32[]{:S(2)}) collective-permute-start(bf16[784,128]{1,0:T(8,128)(2,1)S(1)} %get-tuple-element.49), channel_id=1, source_target_pairs={{0,2},{4,0},{8,4},{12,8},{14,12},{10,14},{6,10},{2,6},{1,3},{5,1},... | collective-permute-start | bytes 602120 | tf_op jit(solution)/shard_map/ppermute | solution.py:552
  27.9 11.7 %collective-permute-start.8 = (bf16[768,128]{1,0:T(8,128)(2,1)S(1)}, bf16[768,128]{1,0:T(8,128)(2,1)S(1)}, u32[]{:S(2)}, u32[]{:S(2)}) collective-permute-start(bf16[768,128]{1,0:T(8,128)(2,1)S(1)} %get-tuple-element.53), channel_id=1, source_target_pairs={{0,2},{4,0},{8,4},{12,8},{14,12},{10,14},{6,10},{2,6},{1,3},{5,1},... | collective-permute-start | bytes 589832 | tf_op jit(solution)/shard_map/ppermute | solution.py:552
  29.7 9.9 %collective-permute-start.7 = (bf16[768,128]{1,0:T(8,128)(2,1)S(1)}, bf16[768,128]{1,0:T(8,128)(2,1)S(1)}, u32[]{:S(2)}, u32[]{:S(2)}) collective-permute-start(bf16[768,128]{1,0:T(8,128)(2,1)S(1)} %get-tuple-element.46), channel_id=1, source_target_pairs={{0,4},{4,8},{8,12},{12,14},{14,10},{10,6},{6,2},{2,0},{1,5},{5,9},... | collective-permute-start | bytes 589832 | tf_op jit(solution)/shard_map/ppermute | solution.py:552
  35.5 8.9 %collective-permute-start.9 = (bf16[784,128]{1,0:T(8,128)(2,1)S(1)}, bf16[784,128]{1,0:T(8,128)(2,1)S(1)}, u32[]{:S(2)}, u32[]{:S(2)}) collective-permute-start(bf16[784,128]{1,0:T(8,128)(2,1)S(1)} %get-tuple-element.56), channel_id=1, source_target_pairs={{0,4},{4,8},{8,12},{12,14},{14,10},{10,6},{6,2},{2,0},{1,5},{5,9},... | collective-permute-start | bytes 602120 | tf_op jit(solution)/shard_map/ppermute | solution.py:552
  37.1 7.9 %collective-permute-start.10 = (bf16[784,128]{1,0:T(8,128)(2,1)S(1)}, bf16[784,128]{1,0:T(8,128)(2,1)S(1)}, u32[]{:S(2)}, u32[]{:S(2)}) collective-permute-start(bf16[784,128]{1,0:T(8,128)(2,1)S(1)} %get-tuple-element.57), channel_id=1, source_target_pairs={{0,2},{4,0},{8,4},{12,8},{14,12},{10,14},{6,10},{2,6},{1,3},{5,1},... | collective-permute-start | bytes 602120 | tf_op jit(solution)/shard_map/ppermute | solution.py:552
  39.7 8.4 %collective-permute-start.14 = (bf16[768,128]{1,0:T(8,128)(2,1)S(1)}, bf16[768,128]{1,0:T(8,128)(2,1)S(1)}, u32[]{:S(2)}, u32[]{:S(2)}) collective-permute-start(bf16[768,128]{1,0:T(8,128)(2,1)S(1)} %get-tuple-element.64), channel_id=1, source_target_pairs={{0,2},{4,0},{8,4},{12,8},{14,12},{10,14},{6,10},{2,6},{1,3},{5,1},... | collective-permute-start | bytes 589832 | tf_op jit(solution)/shard_map/ppermute | solution.py:552
  39.9 8.3 %collective-permute-start.13 = (bf16[768,128]{1,0:T(8,128)(2,1)S(1)}, bf16[768,128]{1,0:T(8,128)(2,1)S(1)}, u32[]{:S(2)}, u32[]{:S(2)}) collective-permute-start(bf16[768,128]{1,0:T(8,128)(2,1)S(1)} %get-tuple-element.54), channel_id=1, source_target_pairs={{0,4},{4,8},{8,12},{12,14},{14,10},{10,6},{6,2},{2,0},{1,5},{5,9},... | collective-permute-start | bytes 589832 | tf_op jit(solution)/shard_map/ppermute | solution.py:552
  45.2 11.0 %collective-permute-start.11 = (bf16[784,128]{1,0:T(8,128)(2,1)S(1)}, bf16[784,128]{1,0:T(8,128)(2,1)S(1)}, u32[]{:S(2)}, u32[]{:S(2)}) collective-permute-start(bf16[784,128]{1,0:T(8,128)(2,1)S(1)} %get-tuple-element.61), channel_id=1, source_target_pairs={{0,4},{4,8},{8,12},{12,14},{14,10},{10,6},{6,2},{2,0},{1,5},{5,9},... | collective-permute-start | bytes 602120 | tf_op jit(solution)/shard_map/ppermute | solution.py:552
  46.2 9.9 %collective-permute-start.12 = (bf16[784,128]{1,0:T(8,128)(2,1)S(1)}, bf16[784,128]{1,0:T(8,128)(2,1)S(1)}, u32[]{:S(2)}, u32[]{:S(2)}) collective-permute-start(bf16[784,128]{1,0:T(8,128)(2,1)S(1)} %get-tuple-element.62), channel_id=1, source_target_pairs={{0,2},{4,0},{8,4},{12,8},{14,12},{10,14},{6,10},{2,6},{1,3},{5,1},... | collective-permute-start | bytes 602120 | tf_op jit(solution)/shard_map/ppermute | solution.py:552
  48.2 6.5 %collective-permute-start.15 = (bf16[768,128]{1,0:T(8,128)(2,1)S(1)}, bf16[768,128]{1,0:T(8,128)(2,1)S(1)}, u32[]{:S(2)}, u32[]{:S(2)}) collective-permute-start(bf16[768,128]{1,0:T(8,128)(2,1)S(1)} %get-tuple-element.65), channel_id=1, source_target_pairs={{0,4},{4,8},{8,12},{12,14},{14,10},{10,6},{6,2},{2,0},{1,5},{5,9},... | collective-permute-start | bytes 589832 | tf_op jit(solution)/shard_map/ppermute | solution.py:552
  50.1 6.0 %collective-permute-start.16 = (bf16[768,128]{1,0:T(8,128)(2,1)S(1)}, bf16[768,128]{1,0:T(8,128)(2,1)S(1)}, u32[]{:S(2)}, u32[]{:S(2)}) collective-permute-start(bf16[768,128]{1,0:T(8,128)(2,1)S(1)} %get-tuple-element.66), channel_id=1, source_target_pairs={{0,2},{4,0},{8,4},{12,8},{14,12},{10,14},{6,10},{2,6},{1,3},{5,1},... | collective-permute-start | bytes 589832 | tf_op jit(solution)/shard_map/ppermute | solution.py:552

commit v12 on v11

--- a/solution.py
+++ b/solution.py
@@ -115,8 +115,9 @@
 
 
 def block_leaves(scale):
-    wide = jnp.broadcast_to(scale, (16, HEAD_DIM))
-    return [(wide * jnp.float32(level)).astype(BF16) for level in NORMAL_FLOAT_LEVELS]
+    wide = jnp.broadcast_to(scale, (8, HEAD_DIM))
+    leaves = [wide * jnp.float32(level) for level in NORMAL_FLOAT_LEVELS]
+    return [jnp.concatenate([leaf, leaf], axis=0).astype(BF16) for leaf in leaves]
 
 
 def selected(codes, leaves):
@@ -142,116 +143,114 @@
     return (scales.astype(F32) + 1.0) / 256.0 * second
 
 
-def weights_kernel(key_codes, value_codes, key_scales, value_scales, outer, out, scales):
-    block = pl.program_id(0)
-    depth = key_codes.shape[0]
+def weights_kernel(
+    x, codes, key_scales, value_scales, outer, gain,
+    out, scaled, squares, key_codes, value_codes, lines, scales, arrivals,
+):
+    per_rep = x.shape[0]
+    features, width = key_codes.shape
+    depth = min(256, features)
+    blocks = features // depth
     columns = outer.shape[0] // 2
-
-    @pl.when(block == 0)
-    def _():
-        for at in range(CORE_HEADS):
-            head = lax.axis_index("rep") * CORE_HEADS + at
-            column = head // (KV_HEADS // columns)
-            lanes = slice(at * HEAD_DIM, (at + 1) * HEAD_DIM)
-            scales[2 * at] = block_scales(key_scales[:, lanes], outer[...], column)
-            scales[2 * at + 1] = block_scales(value_scales[:, lanes], outer[...], columns + column)
+    rep = lax.axis_index("rep")
+
+    def code_copies(block):
+        rows = pl.ds(block * depth, depth)
+        return [
+            pltpu.make_async_copy(
+                codes.at[rows, pl.ds(pl.multiple_of((2 * kind + rep) * width, width), width)],
+                buffer.at[rows],
+                arrivals.at[2 * block + kind],
+            )
+            for kind, buffer in enumerate((key_codes, value_codes))
+        ]
+
+    def line_copy(prompt):
+        return pltpu.make_async_copy(
+            x.at[prompt], lines.at[prompt], arrivals.at[2 * blocks + prompt]
+        )
+
+    for block in range(blocks):
+        if block == blocks // 2:
+            for prompt in range(per_rep):
+                line_copy(prompt).start()
+        for copy in code_copies(block):
+            copy.start()
+    for at in range(CORE_HEADS):
+        column = (rep * CORE_HEADS + at) // (KV_HEADS // columns)
+        lanes = slice(at * HEAD_DIM, (at + 1) * HEAD_DIM)
+        scales[2 * at] = block_scales(key_scales[:, lanes], outer[...], column)
+        scales[2 * at + 1] = block_scales(value_scales[:, lanes], outer[...], columns + column)
+    squares[...] = jnp.zeros(squares.shape, F32)
 
     def body(step, _):
-        begin = pl.multiple_of(step * QBLOCK, QBLOCK)
-        row = pl.ds(block * (depth // QBLOCK) + step, 1)
+        row = pl.ds(step, 1)
         for at in range(CORE_HEADS):
             lanes = slice(at * HEAD_DIM, (at + 1) * HEAD_DIM)
-            for kind, codes in enumerate((key_codes, value_codes)):
+            for kind, buffer in enumerate((key_codes, value_codes)):
                 leaves = block_leaves(scales[2 * at + kind, row, :])
-                columns = slice(kind * HEAD_DIM, (kind + 1) * HEAD_DIM)
                 for tile in range(QBLOCK // 16):
-                    rows = pl.ds(pl.multiple_of(begin + 16 * tile, 16), 16)
-                    weight = selected(codes[rows, lanes], leaves)
-                    rows = pl.ds(pl.multiple_of(block * depth + begin + 16 * tile, 16), 16)
-                    out[at, rows, columns] = weight
+                    rows = pl.ds(pl.multiple_of(step * QBLOCK + 16 * tile, 16), 16)
+                    out[at, rows, kind * HEAD_DIM : (kind + 1) * HEAD_DIM] = selected(
+                        buffer[rows, lanes], leaves
+                    )
         return 0
 
-    lax.fori_loop(0, depth // QBLOCK, body, 0)
-
-
-def dequantize(codes, scales, outer):
-    features = codes.shape[0]
-    depth = min(256, features)
+    steps = depth // QBLOCK
+    late = blocks - blocks // 2
+    for block in range(blocks):
+        for copy in code_copies(block):
+            copy.wait()
+        lax.fori_loop(block * steps, (block + 1) * steps, body, 0)
+        if block == blocks // 2:
+            for prompt in range(per_rep):
+                line_copy(prompt).wait()
+        for chunk in range(blocks):
+            if blocks // 2 + chunk * late // blocks != block:
+                continue
+            lanes = slice(chunk * depth, (chunk + 1) * depth)
+            for prompt in range(per_rep):
+                wide = lines[prompt, :, lanes].astype(F32)
+                scaled[prompt, :, lanes] = (wide * gain[:, lanes]).astype(BF16)
+                squares[prompt] += token_rows(jnp.sum(wide * wide, axis=1, keepdims=True))
+
+
+def dequantize(x, codes, scales, outer, gain):
+    per_rep, _, features = x.shape
     width = CORE_HEADS * HEAD_DIM
+    blocks = features // min(256, features)
     rep = lambda: lax.axis_index("rep")
-    codes, scales, outer = in_hbm(codes, scales, outer)
+    x, codes, scales, outer, gain = in_hbm(x, codes, scales, outer, gain)
     return pl.pallas_call(
         weights_kernel,
-        grid=(features // depth,),
+        grid=(1,),
         in_specs=[
-            pl.BlockSpec((depth, width), lambda k: (k, rep())),
-            pl.BlockSpec((depth, width), lambda k: (k, 2 + rep())),
+            pl.BlockSpec(memory_space=pltpu.HBM),
+            pl.BlockSpec(memory_space=pltpu.HBM),
             pl.BlockSpec((scales.shape[0], width), lambda k: (0, rep())),
             pl.BlockSpec((scales.shape[0], width), lambda k: (0, 2 + rep())),
             pl.BlockSpec(outer.shape, lambda k: (0, 0)),
+            pl.BlockSpec(gain.shape, lambda k: (0, 0)),
         ],
-        out_specs=VMEM,
-        out_shape=jax.ShapeDtypeStruct((CORE_HEADS, features, 2 * HEAD_DIM), BF16),
-        scratch_shapes=[pltpu.VMEM((2 * CORE_HEADS, scales.shape[0], HEAD_DIM), F32)],
-        compiler_params=pltpu.CompilerParams(vmem_limit_bytes=32 * MIB),
+        out_specs=[VMEM] * 3,
+        out_shape=[
+            jax.ShapeDtypeStruct((CORE_HEADS, features, 2 * HEAD_DIM), BF16),
+            jax.ShapeDtypeStruct(x.shape, BF16),
+            jax.ShapeDtypeStruct((per_rep, 8, 128), F32),
+        ],
+        scratch_shapes=[
+            pltpu.VMEM((features, width), jnp.int32),
+            pltpu.VMEM((features, width), jnp.int32),
+            pltpu.VMEM(x.shape, BF16),
+            pltpu.VMEM((2 * CORE_HEADS, scales.shape[0], HEAD_DIM), F32),
+            pltpu.SemaphoreType.DMA((2 * blocks + per_rep,)),
+        ],
+        compiler_params=pltpu.CompilerParams(vmem_limit_bytes=36 * MIB),
         cost_estimate=pl.CostEstimate(
             flops=32 * codes.size, bytes_accessed=codes.size * 2, transcendentals=0
         ),
         name="dequantize",
-    )(codes, codes, scales, scales, outer)
-
-
-def scale_kernel(x, gain, scaled, squares, lines, factors, column, arrivals):
-    half = STRETCH // 2
-    pieces = [(prompt, slice(at, at + half)) for prompt in range(x.shape[0]) for at in (0, half)]
-
-    def copy(item):
-        prompt, rows = pieces[item]
-        return pltpu.make_async_copy(
-            x.at[prompt, rows], lines.at[prompt, rows], arrivals.at[item]
-        )
-
-    gain_copy = pltpu.make_async_copy(gain, factors, arrivals.at[len(pieces)])
-    gain_copy.start()
-    for item in range(len(pieces)):
-        copy(item).start()
-    gain_copy.wait()
-    for item, (prompt, rows) in enumerate(pieces):
-        copy(item).wait()
-        begin = rows.start
-
-        def body(step, _, prompt=prompt, begin=begin):
-            rows = pl.ds(pl.multiple_of(begin + step * 16, 16), 16)
-            wide = lines[prompt, rows, :].astype(F32)
-            scaled[prompt, rows, :] = (wide * factors[...]).astype(BF16)
-            total = jnp.sum(wide * wide, axis=1, keepdims=True)
-            column[rows, :] = jnp.broadcast_to(total, (16, 128))
-            return 0
-
-        lax.fori_loop(0, half // 16, body, 0)
-        if begin > 0:
-            squares[prompt] = token_rows(column[:, :1])
-
-
-def scale_features(x, gain):
-    x, gain = in_hbm(x, gain)
-    return pl.pallas_call(
-        scale_kernel,
-        in_specs=[pl.BlockSpec(memory_space=pltpu.HBM)] * 2,
-        out_specs=[VMEM] * 2,
-        out_shape=[
-            jax.ShapeDtypeStruct(x.shape, BF16),
-            jax.ShapeDtypeStruct((x.shape[0], 8, 128), F32),
-        ],
-        scratch_shapes=[
-            pltpu.VMEM(x.shape, BF16),
-            pltpu.VMEM(gain.shape, F32),
-            pltpu.VMEM((STRETCH, 128), F32),
-            pltpu.SemaphoreType.DMA((2 * x.shape[0] + 1,)),
-        ],
-        compiler_params=pltpu.CompilerParams(vmem_limit_bytes=24 * MIB),
-        name="scale_features",
-    )(x, gain)
+    )(x, codes, scales, scales, outer, gain)
 
 
 def prompt_of(targets, owner):
@@ -261,19 +260,35 @@
     return prompt
 
 
-def with_lines(targets, distance, own, squares, other, other_squares, some, none):
+def with_lines(targets, distance, own, squares, other, gain, line, total, some, none):
     per_rep = own.shape[0]
     prompt = prompt_of(targets, owner_at(distance))
     at = lax.rem(jnp.maximum(prompt, 0), per_rep)
     is_own = prompt // per_rep == lax.axis_index("rep")
-    pl.when((prompt >= 0) & is_own)(lambda: some(own.at[at], squares.at[at]))
-    pl.when((prompt >= 0) & jnp.logical_not(is_own))(
-        lambda: some(other.at[at], other_squares.at[at])
-    )
+
+    @pl.when((prompt >= 0) & is_own)
+    def _():
+        some(own.at[at], squares.at[at])
+
+    @pl.when((prompt >= 0) & jnp.logical_not(is_own))
+    def _():
+        width = min(512, line.shape[1])
+        total[...] = jnp.zeros(total.shape, F32)
+        for begin in range(0, line.shape[1], width):
+            lanes = slice(begin, begin + width)
+            wide = other[at, :, lanes].astype(F32)
+            line[:, lanes] = (wide * gain[:, lanes]).astype(BF16)
+            total[...] += token_rows(jnp.sum(wide * wide, axis=1, keepdims=True))
+        some(line, total)
+
     pl.when(prompt < 0)(none)
 
 
-def first_kernel(distance, targets, own, squares, other, other_squares, weight, right, left):
+def line_scratch(x):
+    return [pltpu.VMEM(x.shape[1:], BF16), pltpu.VMEM((8, 128), F32)]
+
+
+def first_kernel(distance, targets, own, squares, other, gain, weight, right, left, line, total):
     def some(lines, sums):
         for head in range(CORE_HEADS):
             product = jnp.dot(lines[...], weight[head], preferred_element_type=F32)
@@ -286,10 +301,10 @@
         right[...] = jnp.zeros(right.shape, BF16)
         left[...] = jnp.zeros(left.shape, BF16)
 
-    with_lines(targets, distance, own, squares, other, other_squares, some, none)
-
-
-def project_first(distance, targets, own, squares, other, other_squares, weight):
+    with_lines(targets, distance, own, squares, other, gain, line, total, some, none)
+
+
+def project_first(distance, targets, own, squares, other, gain, weight):
     rows = CORE_HEADS * STRETCH
     return pl.pallas_call(
         functools.partial(first_kernel, distance),
@@ -299,15 +314,16 @@
             jax.ShapeDtypeStruct((rows + TAIL, HEAD_DIM), BF16),
             jax.ShapeDtypeStruct((rows, HEAD_DIM), BF16),
         ],
+        scratch_shapes=line_scratch(own),
         compiler_params=pltpu.CompilerParams(vmem_limit_bytes=24 * MIB),
         cost_estimate=pl.CostEstimate(
             flops=STRETCH * weight.size * 2, bytes_accessed=weight.size, transcendentals=0
         ),
         name="project_first",
-    )(targets, own, squares, other, other_squares, weight)
-
-
-def project_kernel(distances, targets, own, squares, other, other_squares, weight, out):
+    )(targets, own, squares, other, gain, weight)
+
+
+def project_kernel(distances, targets, own, squares, other, gain, weight, out, line, total):
     for item, distance in enumerate(distances):
 
         def some(lines, sums, item=item):
@@ -323,23 +339,24 @@
         def none(item=item):
             out[item] = jnp.zeros(out.shape[1:], F32)
 
-        with_lines(targets, distance, own, squares, other, other_squares, some, none)
-
-
-def project(distances, targets, own, squares, other, other_squares, weight):
+        with_lines(targets, distance, own, squares, other, gain, line, total, some, none)
+
+
+def project(distances, targets, own, squares, other, gain, weight):
     return pl.pallas_call(
         functools.partial(project_kernel, distances),
         in_specs=[SMEM] + [VMEM] * 5,
         out_specs=VMEM,
         out_shape=jax.ShapeDtypeStruct((len(distances), 2, 4 * STRETCH + 8, HEAD_DIM), F32),
+        scratch_shapes=line_scratch(own),
         compiler_params=pltpu.CompilerParams(vmem_limit_bytes=24 * MIB),
         cost_estimate=pl.CostEstimate(
-            flops=len(distances) * STRETCH * weight.size * 2 // 2,
+            flops=len(distances) * STRETCH * weight.size,
             bytes_accessed=weight.size,
             transcendentals=0,
         ),
         name="project",
-    )(targets, own, squares, other, other_squares, weight)
+    )(targets, own, squares, other, gain, weight)
 
 
 def send_kernel(half, first, terms, right, left, to_right, to_left):
@@ -551,15 +568,14 @@
     def pass_on(right, left):
         return lax.ppermute(right, "tp", to_right), lax.ppermute(left, "tp", to_left)
 
-    own, squares = scale_features(lines, gain)
     swap = lambda array: lax.ppermute(array, "rep", [(0, 1), (1, 0)])
-    other, other_squares = swap(own), swap(squares)
-    weight = dequantize(kv_codes, scale_codes, outer_scales.T)
+    other = swap(lines)
+    weight, own, squares = dequantize(lines, kv_codes, scale_codes, outer_scales.T, gain)
     frequency, turns = rotary_turns()
     start = (prompt_lengths - STRETCH).astype(F32)[:, None] * jnp.asarray(frequency)
     starts = jnp.stack([jnp.cos(start), jnp.sin(start)])
 
-    features = [own, squares, other, other_squares]
+    features = [own, squares, other, gain]
     right, left = project_first(half, target_rows, *features, weight)
     targets, _ = lax.optimization_barrier((target_rows, left))
     arrived = [pass_on(right, left)] * 2

time: 60.8 us -> 54.7 us (0.90)
  Pallas kernels: 29.5 us -> 24.2 us
  waiting for transfers between devices: 11.3 us -> 8.22 us
  starting transfers between devices: 16.3 us -> 18.7 us
    pallas_call x2 -> x1, Pallas kernels: 13.9 us -> 8.38 us  [dequantize(): pl.pallas_call(weights_kernel, grid=(1,), in_specs=[pl.BlockSpec(memory_s...]
    ppermute x7, starting transfers between devices: 5.95 us -> 11.1 us  [pass_on(): lax.ppermute(left, 'tp', to_left)]
    ppermute x7, waiting for transfers between devices: 5.69 us -> 1.75 us  [pass_on(): lax.ppermute(left, 'tp', to_left)]
    ppermute x7, starting transfers between devices: 9.63 us -> 6.88 us  [pass_on(): lax.ppermute(right, 'tp', to_right)]
    pallas_call x3, Pallas kernels: 6.9 us -> 8.05 us  [project(): pl.pallas_call(functools.partial(project_kernel, distances), in_specs=[SM...]
    pallas_call x1, Pallas kernels: 1.58 us -> 0.65 us  [project_first(): pl.pallas_call(functools.partial(first_kernel, distance), in_specs=[SMEM]...]
    ppermute x7, waiting for transfers between devices: 5.61 us -> 6.47 us  [pass_on(): lax.ppermute(right, 'tp', to_right)]
  transfers between devices with their start and end apart: 17 -> 16, of which waited for: 7 -> 4; matrix products, arithmetic and copies ran while one was open for 0% -> 0% of each run, Pallas kernels for 34% -> 39%
where the time goes in v12:
time: 54.7 us
  Pallas kernels  24.2 us (44%)
  starting transfers between devices  18.7 us (34%)
  waiting for transfers between devices  8.22 us (15%)
  blocking collectives  1.85 us (3%)
  between operations  0.93 us (2%)
  local copies, waits for them, and re-layouts  0.67 us (1%)
    ppermute x7, starting transfers between devices, pass_on(): lax.ppermute(left, 'tp', to_left)  11.1 us
    pallas_call x1, Pallas kernels, dequantize(): pl.pallas_call(weights_kernel, grid=(1,), in_specs=[pl.BlockSpec(memory_s...  8.38 us
    pallas_call x3, Pallas kernels, project(): pl.pallas_call(functools.partial(project_kernel, distances), in_specs=[SM...  8.05 us
    ppermute x7, starting transfers between devices, pass_on(): lax.ppermute(right, 'tp', to_right)  6.88 us
    ppermute x7, waiting for transfers between devices, pass_on(): lax.ppermute(right, 'tp', to_right)  6.47 us
    pallas_call x2, Pallas kernels, cache_attention(): pl.pallas_call(functools.partial(cache_kernel, part), in_specs=[SMEM] * 3...  3.98 us
    pallas_call x1, Pallas kernels, finish(): pl.pallas_call(final_kernel, in_specs=[SMEM] + [VMEM] * 9, out_specs=VMEM...  1.99 us
    all_gather x1, blocking collectives, per_device(): return lax.all_gather(out, 'rep', axis=2, tiled=True)  1.85 us
  transfers between devices with their start and end apart: 16, of which 4 were waited for; matrix products, arithmetic and copies ran while one was open for 0% of the time, Pallas kernels for 39%

profile of v12, /device:TPU:0, one launch (start us, length us, event | category | flops | bytes accessed | tf_op | source)
XLA Modules:
  0.0 54.7 jit_solution(6826536046272156979)
XLA Ops:
  0.0 0.5 collective-permute-start
  0.5 8.4 %dequantize.1 = (bf16[4,2048,256]{2,1,0:T(8,128)(2,1)S(1)}, bf16[3,192,2048]{2,1,0:T(8,128)(2,1)S(1)}, f32[3,8,128]{2,1,0:T(8,128)S(1)}) custom-call(bf16[3,192,2048]{2,1,0:T(8,128)(2,1)} %bitcast.9, s32[2048,2048]{1,0:T(8,128)} %codes.1, s32[32,2048]{1,0:T(8,128)} %value_scales.1, s32[32,2048]{1,0:T(8,128)} %value_scales.1, f32[8,32]{1,0:T(8,128)} %bitcast.10, ...), custom_call_target="tpu_custom_call" | custom-call | flops 134217728 | bytes 8388608 | tf_op jit(solution)/shard_map/dequantize/pallas_call | solution.py:224
  8.9 0.0 copy-start.7
  8.9 0.0 copy-start.2
  8.9 0.0 copy-start.3
  8.9 0.0 copy-start
  8.9 0.0 copy-start.4
  9.0 0.6 %project_first.1 = (bf16[784,128]{1,0:T(8,128)(2,1)S(1)}, bf16[768,128]{1,0:T(8,128)(2,1)S(1)}) custom-call(s32[6]{0:T(128)S(1)} %copy-done.5, bf16[3,192,2048]{2,1,0:T(8,128)(2,1)S(1)} %get-tuple-element.38.own, f32[3,8,128]{2,1,0:T(8,128)S(1)} %get-tuple-element.39.squares, bf16[3,192,2048]{2,1,0:T(8,128)(2,1)S(1)} %collective-permute-done.other, ...), custom_call_target="tpu_custom_call" | custom-call | flops 805306368 | bytes 2097152 | tf_op jit(solution)/shard_map/project_first/pallas_call | solution.py:309
  9.6 3.5 %collective-permute-start.2 = (bf16[768,128]{1,0:T(8,128)(2,1)S(1)}, bf16[768,128]{1,0:T(8,128)(2,1)S(1)}, u32[]{:S(2)}, u32[]{:S(2)}) collective-permute-start(bf16[768,128]{1,0:T(8,128)(2,1)S(1)} %get-tuple-element.41), channel_id=1, source_target_pairs={{0,2},{4,0},{8,4},{12,8},{14,12},{10,14},{6,10},{2,6},{1,3},{5,1},... | collective-permute-start | bytes 589832 | tf_op jit(solution)/shard_map/ppermute | solution.py:569
  13.1 0.0 collective-permute-start.1
  13.1 0.1 multiply_cosine_fusion
  13.9 0.7 %prepare.1 = (bf16[8,32,128]{2,1,0:T(8,128)(2,1)S(1)}, f32[2,192,128]{2,1,0:T(8,128)S(1)}) custom-call(s32[6]{0:T(128)S(1)} %copy-done.5, bf16[1,2,16384]{2,1,0:T(2,128)(2,1)S(1)} %copy-done.3, f32[2,6,128]{2,1,0:T(8,128)S(1)} %pad_maximum_fusion.starts, f32[2,192,128]{2,1,0:T(8,128)S(1)} %copy-done.2), custom_call_target="tpu_custom_call" | custom-call | tf_op jit(solution)/shard_map/prepare/pallas_call | solution.py:412
  14.6 2.0 %cache_attention.2 = bf16[4,48,128]{2,1,0:T(8,128)(2,1)S(1)} custom-call(s32[6]{0:T(128)S(1)} %copy-done.5, s32[6]{0:T(128)S(1)} %copy-done.6, s32[1]{0:T(128)S(6)} %copy.15.stored, bf16[8,32,128]{2,1,0:T(8,128)(2,1)S(1)} %get-tuple-element.46.q.grouped, bf16[1,1024,2048]{2,1,0:T(8,128)(2,1)S(1)} %copy-done, bf16[1,2,2048]{2,1,0:T(2,128)(2,1)S(1)} %copy-done.4), custom_call_target="tpu_custom_call" | custom-call | flops 67108864 | bytes 2097152 | tf_op jit(solution)/shard_map/cache_attention/pallas_call | solution.py:469
  16.6 0.3 collective-permute-start.3
  16.9 1.7 %project.3.terms = f32[2,2,776,128]{3,2,1,0:T(8,128)S(1)} custom-call(s32[6]{0:T(128)S(1)} %copy-done.5, bf16[3,192,2048]{2,1,0:T(8,128)(2,1)S(1)} %get-tuple-element.38.own, f32[3,8,128]{2,1,0:T(8,128)S(1)} %get-tuple-element.39.squares, bf16[3,192,2048]{2,1,0:T(8,128)(2,1)S(1)} %collective-permute-done.other, f32[1,2048]{1,0:T(1,128)S(1)} %bitcast.5, ...), custom_call_target="tpu_custom_call" | custom-call | flops 805306368 | bytes 2097152 | tf_op jit(solution)/shard_map/project/pallas_call | solution.py:346
  18.5 0.0 collective-permute-done.2.left
  18.6 1.7 %collective-permute-done.1.right = bf16[784,128]{1,0:T(8,128)(2,1)S(1)} collective-permute-done((bf16[784,128]{1,0:T(8,128)(2,1)S(1)}, bf16[784,128]{1,0:T(8,128)(2,1)S(1)}, u32[]{:S(2)}, u32[]{:S(2)}) %collective-permute-start.1) | collective-permute-done | bytes 200736 | tf_op jit(solution)/shard_map/ppermute | solution.py:569
  20.2 0.1 sends.6
  20.3 0.0 collective-permute-done.3.cached_there
  20.3 0.3 collective-permute-start.4
  20.6 1.7 %collective-permute-start.5 = (bf16[784,128]{1,0:T(8,128)(2,1)S(1)}, bf16[784,128]{1,0:T(8,128)(2,1)S(1)}, u32[]{:S(2)}, u32[]{:S(2)}) collective-permute-start(bf16[784,128]{1,0:T(8,128)(2,1)S(1)} %get-tuple-element.51), channel_id=1, source_target_pairs={{0,2},{4,0},{8,4},{12,8},{14,12},{10,14},{6,10},{2,6},{1,3},{5,1},... | collective-permute-start | bytes 602120 | tf_op jit(solution)/shard_map/ppermute | solution.py:569
  22.4 0.1 sends.7
  22.4 1.6 %collective-permute-start.7 = (bf16[768,128]{1,0:T(8,128)(2,1)S(1)}, bf16[768,128]{1,0:T(8,128)(2,1)S(1)}, u32[]{:S(2)}, u32[]{:S(2)}) collective-permute-start(bf16[768,128]{1,0:T(8,128)(2,1)S(1)} %get-tuple-element.55), channel_id=1, source_target_pairs={{0,2},{4,0},{8,4},{12,8},{14,12},{10,14},{6,10},{2,6},{1,3},{5,1},... | collective-permute-start | bytes 589832 | tf_op jit(solution)/shard_map/ppermute | solution.py:569
  24.1 0.4 collective-permute-start.6
  24.5 2.0 %cache_attention.3.cached_here = bf16[4,48,128]{2,1,0:T(8,128)(2,1)S(1)} custom-call(s32[6]{0:T(128)S(1)} %copy-done.5, s32[6]{0:T(128)S(1)} %copy-done.6, s32[1]{0:T(128)S(6)} %copy.15.stored, bf16[8,32,128]{2,1,0:T(8,128)(2,1)S(1)} %get-tuple-element.46.q.grouped, bf16[1,1024,2048]{2,1,0:T(8,128)(2,1)S(1)} %copy-done, bf16[1,2,2048]{2,1,0:T(2,128)(2,1)S(1)} %copy-done.4), custom_call_target="tpu_custom_call" | custom-call | flops 67108864 | bytes 2097152 | tf_op jit(solution)/shard_map/cache_attention/pallas_call | solution.py:469
  26.5 2.8 %project.4.terms = f32[2,2,776,128]{3,2,1,0:T(8,128)S(1)} custom-call(s32[6]{0:T(128)S(1)} %copy-done.5, bf16[3,192,2048]{2,1,0:T(8,128)(2,1)S(1)} %get-tuple-element.38.own, f32[3,8,128]{2,1,0:T(8,128)S(1)} %get-tuple-element.39.squares, bf16[3,192,2048]{2,1,0:T(8,128)(2,1)S(1)} %collective-permute-done.other, f32[1,2048]{1,0:T(1,128)S(1)} %bitcast.6, ...), custom_call_target="tpu_custom_call" | custom-call | flops 805306368 | bytes 2097152 | tf_op jit(solution)/shard_map/project/pallas_call | solution.py:346
  29.3 0.0 collective-permute-done.4.right
  29.3 0.1 sends.8
  29.4 1.2 %collective-permute-start.8 = (bf16[784,128]{1,0:T(8,128)(2,1)S(1)}, bf16[784,128]{1,0:T(8,128)(2,1)S(1)}, u32[]{:S(2)}, u32[]{:S(2)}) collective-permute-start(bf16[784,128]{1,0:T(8,128)(2,1)S(1)} %get-tuple-element.58), channel_id=1, source_target_pairs={{0,4},{4,8},{8,12},{12,14},{14,10},{10,6},{6,2},{2,0},{1,5},{5,9},... | collective-permute-start | bytes 602120 | tf_op jit(solution)/shard_map/ppermute | solution.py:569
  30.6 0.9 %collective-permute-start.9 = (bf16[784,128]{1,0:T(8,128)(2,1)S(1)}, bf16[784,128]{1,0:T(8,128)(2,1)S(1)}, u32[]{:S(2)}, u32[]{:S(2)}) collective-permute-start(bf16[784,128]{1,0:T(8,128)(2,1)S(1)} %get-tuple-element.59), channel_id=1, source_target_pairs={{0,2},{4,0},{8,4},{12,8},{14,12},{10,14},{6,10},{2,6},{1,3},{5,1},... | collective-permute-start | bytes 602120 | tf_op jit(solution)/shard_map/ppermute | solution.py:569
  31.5 0.3 collective-permute-done.7.left
  31.8 0.1 sends.9
  31.8 2.3 %collective-permute-start.13 = (bf16[768,128]{1,0:T(8,128)(2,1)S(1)}, bf16[768,128]{1,0:T(8,128)(2,1)S(1)}, u32[]{:S(2)}, u32[]{:S(2)}) collective-permute-start(bf16[768,128]{1,0:T(8,128)(2,1)S(1)} %get-tuple-element.66), channel_id=1, source_target_pairs={{0,2},{4,0},{8,4},{12,8},{14,12},{10,14},{6,10},{2,6},{1,3},{5,1},... | collective-permute-start | bytes 589832 | tf_op jit(solution)/shard_map/ppermute | solution.py:569
  34.2 0.7 %collective-permute-start.12 = (bf16[768,128]{1,0:T(8,128)(2,1)S(1)}, bf16[768,128]{1,0:T(8,128)(2,1)S(1)}, u32[]{:S(2)}, u32[]{:S(2)}) collective-permute-start(bf16[768,128]{1,0:T(8,128)(2,1)S(1)} %get-tuple-element.56), channel_id=1, source_target_pairs={{0,4},{4,8},{8,12},{12,14},{14,10},{10,6},{6,2},{2,0},{1,5},{5,9},... | collective-permute-start | bytes 589832 | tf_op jit(solution)/shard_map/ppermute | solution.py:569
  34.9 3.6 %project.5.terms.own = f32[3,2,776,128]{3,2,1,0:T(8,128)S(1)} custom-call(s32[6]{0:T(128)S(1)} %copy-done.5, bf16[3,192,2048]{2,1,0:T(8,128)(2,1)S(1)} %get-tuple-element.38.own, f32[3,8,128]{2,1,0:T(8,128)S(1)} %get-tuple-element.39.squares, bf16[3,192,2048]{2,1,0:T(8,128)(2,1)S(1)} %collective-permute-done.other, f32[1,2048]{1,0:T(1,128)S(1)} %bitcast.7, ...), custom_call_target="tpu_custom_call" | custom-call | flops 1207959552 | bytes 2097152 | tf_op jit(solution)/shard_map/project/pallas_call | solution.py:346
  38.5 0.0 collective-permute-done.8.right
  38.5 0.1 sends.10
  38.6 2.1 %collective-permute-start.10 = (bf16[784,128]{1,0:T(8,128)(2,1)S(1)}, bf16[784,128]{1,0:T(8,128)(2,1)S(1)}, u32[]{:S(2)}, u32[]{:S(2)}) collective-permute-start(bf16[784,128]{1,0:T(8,128)(2,1)S(1)} %get-tuple-element.63), channel_id=1, source_target_pairs={{0,4},{4,8},{8,12},{12,14},{14,10},{10,6},{6,2},{2,0},{1,5},{5,9},... | collective-permute-start | bytes 602120 | tf_op jit(solution)/shard_map/ppermute | solution.py:569
  40.7 0.0 collective-permute-start.11
  40.7 0.0 collective-permute-done.13.left
  40.7 0.1 sends.11
  40.8 2.1 %collective-permute-start.14 = (bf16[768,128]{1,0:T(8,128)(2,1)S(1)}, bf16[768,128]{1,0:T(8,128)(2,1)S(1)}, u32[]{:S(2)}, u32[]{:S(2)}) collective-permute-start(bf16[768,128]{1,0:T(8,128)(2,1)S(1)} %get-tuple-element.67), channel_id=1, source_target_pairs={{0,4},{4,8},{8,12},{12,14},{14,10},{10,6},{6,2},{2,0},{1,5},{5,9},... | collective-permute-start | bytes 589832 | tf_op jit(solution)/shard_map/ppermute | solution.py:569
  42.9 1.1 %collective-permute-start.15 = (bf16[768,128]{1,0:T(8,128)(2,1)S(1)}, bf16[768,128]{1,0:T(8,128)(2,1)S(1)}, u32[]{:S(2)}, u32[]{:S(2)}) collective-permute-start(bf16[768,128]{1,0:T(8,128)(2,1)S(1)} %get-tuple-element.68), channel_id=1, source_target_pairs={{0,2},{4,0},{8,4},{12,8},{14,12},{10,14},{6,10},{2,6},{1,3},{5,1},... | collective-permute-start | bytes 589832 | tf_op jit(solution)/shard_map/ppermute | solution.py:569
  44.0 4.8 %collective-permute-done.14.right_b = bf16[768,128]{1,0:T(8,128)(2,1)S(1)} collective-permute-done((bf16[768,128]{1,0:T(8,128)(2,1)S(1)}, bf16[768,128]{1,0:T(8,128)(2,1)S(1)}, u32[]{:S(2)}, u32[]{:S(2)}) %collective-permute-start.14) | collective-permute-done | bytes 196640 | tf_op jit(solution)/shard_map/ppermute | solution.py:569
  48.8 1.4 %collective-permute-done.15.left_b = bf16[768,128]{1,0:T(8,128)(2,1)S(1)} collective-permute-done((bf16[768,128]{1,0:T(8,128)(2,1)S(1)}, bf16[768,128]{1,0:T(8,128)(2,1)S(1)}, u32[]{:S(2)}, u32[]{:S(2)}) %collective-permute-start.15) | collective-permute-done | bytes 196640 | tf_op jit(solution)/shard_map/ppermute | solution.py:569
  50.2 2.0 %finish.1 = bf16[1,2,8192]{2,1,0:T(2,128)(2,1)S(1)} custom-call(s32[6]{0:T(128)S(1)} %copy-done.5, f32[2,192,128]{2,1,0:T(8,128)S(1)} %get-tuple-element.43.rotary, f32[3,2,776,128]{3,2,1,0:T(8,128)S(1)} %project.5.terms.own, bf16[784,128]{1,0:T(8,128)(2,1)S(1)} %collective-permute-done.10.right_a, bf16[784,128]{1,0:T(8,128)(2,1)S(1)} %collective-permute-done.11.left_a, ...), custom_call_target="tpu_custom_call" | custom-call | tf_op jit(solution)/shard_map/finish/pallas_call | solution.py:530
  52.2 1.9 %all_gather.3 = bf16[1,2,16384]{2,1,0:T(2,128)(2,1)S(1)} all-gather(bf16[1,2,8192]{2,1,0:T(2,128)(2,1)S(1)} %finish.1), channel_id=1, replica_groups=mesh['grp'=2,'tp'=8,'rep'=2] {'rep'}, dimensions={2}, use_global_device_ids=true | all-gather | bytes 98304 | tf_op jit(solution)/shard_map/all_gather | solution.py:605
  54.1 0.6 %copy.16 = bf16[1,2,16384]{2,1,0:T(2,128)(2,1)} copy(bf16[1,2,16384]{2,1,0:T(2,128)(2,1)S(1)} %all_gather.3) | data formatting | bytes 131072
  (20 shorter events, 0.0 us)
Async XLA Ops:
  0.0 8.9 %collective-permute-start = (bf16[3,192,2048]{2,1,0:T(8,128)(2,1)}, bf16[3,192,2048]{2,1,0:T(8,128)(2,1)S(1)}, u32[]{:S(2)}, u32[]{:S(2)}) collective-permute-start(bf16[3,192,2048]{2,1,0:T(8,128)(2,1)} %bitcast.8), channel_id=1, source_target_pairs={{0,1},{1,0},{2,3},{3,2},{4,5},{5,4},{6,7},{7,6},{8,9},{9,8},{10,11... | collective-permute-start | bytes 7077896 | tf_op jit(solution)/shard_map/ppermute | solution.py:571
  0.5 8.4 %copy-start.6 = (s32[6]{0:T(128)S(1)}, s32[6]{0:T(128)}, u32[]{:S(2)}) copy-start(s32[6]{0:T(128)} %lengths.3) | copy-start | bytes 76
  0.5 8.4 %copy-start.1 = (f32[2048]{0:T(1024)S(1)}, f32[2048]{0:T(1024)}, u32[]{:S(2)}) copy-start(f32[2048]{0:T(1024)} %param.14) | copy-start | bytes 24580
  0.5 8.4 %copy-start.5 = (s32[6]{0:T(128)S(1)}, s32[6]{0:T(128)}, u32[]{:S(2)}) copy-start(s32[6]{0:T(128)} %targets.9) | copy-start | bytes 76
  8.9 4.2 %copy-start.7 = (f32[128]{0:T(128)S(1)}, f32[128]{0:T(128)}, u32[]{:S(2)}) copy-start(f32[128]{0:T(128)} %constant.7.clone) | copy-start | bytes 1540
  8.9 5.0 %copy-start.2 = (f32[2,192,128]{2,1,0:T(8,128)S(1)}, f32[2,192,128]{2,1,0:T(8,128)}, u32[]{:S(2)}) copy-start(f32[2,192,128]{2,1,0:T(8,128)} %constant.8.clone.turns) | copy-start | bytes 589828
  8.9 5.0 %copy-start.3 = (bf16[1,2,16384]{2,1,0:T(2,128)(2,1)S(1)}, bf16[1,2,16384]{2,1,0:T(2,128)(2,1)}, u32[]{:S(2)}) copy-start(bf16[1,2,16384]{2,1,0:T(2,128)(2,1)} %queries.1) | copy-start | bytes 196612
  8.9 5.7 %copy-start = (bf16[1,1024,2048]{2,1,0:T(8,128)(2,1)S(1)}, bf16[1,1024,2048]{2,1,0:T(8,128)(2,1)}, u32[]{:S(2)}) copy-start(bf16[1,1024,2048]{2,1,0:T(8,128)(2,1)} %cache.3) | copy-start | bytes 12582916
  8.9 5.7 %copy-start.4 = (bf16[1,2,2048]{2,1,0:T(2,128)(2,1)S(1)}, bf16[1,2,2048]{2,1,0:T(2,128)(2,1)}, u32[]{:S(2)}) copy-start(bf16[1,2,2048]{2,1,0:T(2,128)(2,1)} %new.3) | copy-start | bytes 24580
  9.6 8.9 %collective-permute-start.2 = (bf16[768,128]{1,0:T(8,128)(2,1)S(1)}, bf16[768,128]{1,0:T(8,128)(2,1)S(1)}, u32[]{:S(2)}, u32[]{:S(2)}) collective-permute-start(bf16[768,128]{1,0:T(8,128)(2,1)S(1)} %get-tuple-element.41), channel_id=1, source_target_pairs={{0,2},{4,0},{8,4},{12,8},{14,12},{10,14},{6,10},{2,6},{1,3},{5,1},... | collective-permute-start | bytes 589832 | tf_op jit(solution)/shard_map/ppermute | solution.py:569
  13.1 7.1 %collective-permute-start.1 = (bf16[784,128]{1,0:T(8,128)(2,1)S(1)}, bf16[784,128]{1,0:T(8,128)(2,1)S(1)}, u32[]{:S(2)}, u32[]{:S(2)}) collective-permute-start(bf16[784,128]{1,0:T(8,128)(2,1)S(1)} %get-tuple-element.44), channel_id=1, source_target_pairs={{0,4},{4,8},{8,12},{12,14},{14,10},{10,6},{6,2},{2,0},{1,5},{5,9},... | collective-permute-start | bytes 602120 | tf_op jit(solution)/shard_map/ppermute | solution.py:569
  16.6 3.7 %collective-permute-start.3 = (bf16[4,48,128]{2,1,0:T(8,128)(2,1)S(1)}, bf16[4,48,128]{2,1,0:T(8,128)(2,1)S(1)}, u32[]{:S(2)}, u32[]{:S(2)}) collective-permute-start(bf16[4,48,128]{2,1,0:T(8,128)(2,1)S(1)} %cache_attention.2), channel_id=1, source_target_pairs={{0,1},{1,0},{2,3},{3,2},{4,5},{5,4},{6,7},{7,6},{8,9},{9,8},{10,11... | collective-permute-start | bytes 147464 | tf_op jit(solution)/shard_map/ppermute | solution.py:571
  20.3 9.0 %collective-permute-start.4 = (bf16[784,128]{1,0:T(8,128)(2,1)S(1)}, bf16[784,128]{1,0:T(8,128)(2,1)S(1)}, u32[]{:S(2)}, u32[]{:S(2)}) collective-permute-start(bf16[784,128]{1,0:T(8,128)(2,1)S(1)} %get-tuple-element.50), channel_id=1, source_target_pairs={{0,4},{4,8},{8,12},{12,14},{14,10},{10,6},{6,2},{2,0},{1,5},{5,9},... | collective-permute-start | bytes 602120 | tf_op jit(solution)/shard_map/ppermute | solution.py:569
  20.6 8.7 %collective-permute-start.5 = (bf16[784,128]{1,0:T(8,128)(2,1)S(1)}, bf16[784,128]{1,0:T(8,128)(2,1)S(1)}, u32[]{:S(2)}, u32[]{:S(2)}) collective-permute-start(bf16[784,128]{1,0:T(8,128)(2,1)S(1)} %get-tuple-element.51), channel_id=1, source_target_pairs={{0,2},{4,0},{8,4},{12,8},{14,12},{10,14},{6,10},{2,6},{1,3},{5,1},... | collective-permute-start | bytes 602120 | tf_op jit(solution)/shard_map/ppermute | solution.py:569
  22.4 9.3 %collective-permute-start.7 = (bf16[768,128]{1,0:T(8,128)(2,1)S(1)}, bf16[768,128]{1,0:T(8,128)(2,1)S(1)}, u32[]{:S(2)}, u32[]{:S(2)}) collective-permute-start(bf16[768,128]{1,0:T(8,128)(2,1)S(1)} %get-tuple-element.55), channel_id=1, source_target_pairs={{0,2},{4,0},{8,4},{12,8},{14,12},{10,14},{6,10},{2,6},{1,3},{5,1},... | collective-permute-start | bytes 589832 | tf_op jit(solution)/shard_map/ppermute | solution.py:569
  24.1 7.7 %collective-permute-start.6 = (bf16[768,128]{1,0:T(8,128)(2,1)S(1)}, bf16[768,128]{1,0:T(8,128)(2,1)S(1)}, u32[]{:S(2)}, u32[]{:S(2)}) collective-permute-start(bf16[768,128]{1,0:T(8,128)(2,1)S(1)} %get-tuple-element.48), channel_id=1, source_target_pairs={{0,4},{4,8},{8,12},{12,14},{14,10},{10,6},{6,2},{2,0},{1,5},{5,9},... | collective-permute-start | bytes 589832 | tf_op jit(solution)/shard_map/ppermute | solution.py:569
  29.4 9.1 %collective-permute-start.8 = (bf16[784,128]{1,0:T(8,128)(2,1)S(1)}, bf16[784,128]{1,0:T(8,128)(2,1)S(1)}, u32[]{:S(2)}, u32[]{:S(2)}) collective-permute-start(bf16[784,128]{1,0:T(8,128)(2,1)S(1)} %get-tuple-element.58), channel_id=1, source_target_pairs={{0,4},{4,8},{8,12},{12,14},{14,10},{10,6},{6,2},{2,0},{1,5},{5,9},... | collective-permute-start | bytes 602120 | tf_op jit(solution)/shard_map/ppermute | solution.py:569
  30.6 7.9 %collective-permute-start.9 = (bf16[784,128]{1,0:T(8,128)(2,1)S(1)}, bf16[784,128]{1,0:T(8,128)(2,1)S(1)}, u32[]{:S(2)}, u32[]{:S(2)}) collective-permute-start(bf16[784,128]{1,0:T(8,128)(2,1)S(1)} %get-tuple-element.59), channel_id=1, source_target_pairs={{0,2},{4,0},{8,4},{12,8},{14,12},{10,14},{6,10},{2,6},{1,3},{5,1},... | collective-permute-start | bytes 602120 | tf_op jit(solution)/shard_map/ppermute | solution.py:569
  31.8 8.9 %collective-permute-start.13 = (bf16[768,128]{1,0:T(8,128)(2,1)S(1)}, bf16[768,128]{1,0:T(8,128)(2,1)S(1)}, u32[]{:S(2)}, u32[]{:S(2)}) collective-permute-start(bf16[768,128]{1,0:T(8,128)(2,1)S(1)} %get-tuple-element.66), channel_id=1, source_target_pairs={{0,2},{4,0},{8,4},{12,8},{14,12},{10,14},{6,10},{2,6},{1,3},{5,1},... | collective-permute-start | bytes 589832 | tf_op jit(solution)/shard_map/ppermute | solution.py:569
  34.2 6.6 %collective-permute-start.12 = (bf16[768,128]{1,0:T(8,128)(2,1)S(1)}, bf16[768,128]{1,0:T(8,128)(2,1)S(1)}, u32[]{:S(2)}, u32[]{:S(2)}) collective-permute-start(bf16[768,128]{1,0:T(8,128)(2,1)S(1)} %get-tuple-element.56), channel_id=1, source_target_pairs={{0,4},{4,8},{8,12},{12,14},{14,10},{10,6},{6,2},{2,0},{1,5},{5,9},... | collective-permute-start | bytes 589832 | tf_op jit(solution)/shard_map/ppermute | solution.py:569
  38.6 11.6 %collective-permute-start.10 = (bf16[784,128]{1,0:T(8,128)(2,1)S(1)}, bf16[784,128]{1,0:T(8,128)(2,1)S(1)}, u32[]{:S(2)}, u32[]{:S(2)}) collective-permute-start(bf16[784,128]{1,0:T(8,128)(2,1)S(1)} %get-tuple-element.63), channel_id=1, source_target_pairs={{0,4},{4,8},{8,12},{12,14},{14,10},{10,6},{6,2},{2,0},{1,5},{5,9},... | collective-permute-start | bytes 602120 | tf_op jit(solution)/shard_map/ppermute | solution.py:569
  40.7 9.5 %collective-permute-start.11 = (bf16[784,128]{1,0:T(8,128)(2,1)S(1)}, bf16[784,128]{1,0:T(8,128)(2,1)S(1)}, u32[]{:S(2)}, u32[]{:S(2)}) collective-permute-start(bf16[784,128]{1,0:T(8,128)(2,1)S(1)} %get-tuple-element.64), channel_id=1, source_target_pairs={{0,2},{4,0},{8,4},{12,8},{14,12},{10,14},{6,10},{2,6},{1,3},{5,1},... | collective-permute-start | bytes 602120 | tf_op jit(solution)/shard_map/ppermute | solution.py:569
  40.8 8.0 %collective-permute-start.14 = (bf16[768,128]{1,0:T(8,128)(2,1)S(1)}, bf16[768,128]{1,0:T(8,128)(2,1)S(1)}, u32[]{:S(2)}, u32[]{:S(2)}) collective-permute-start(bf16[768,128]{1,0:T(8,128)(2,1)S(1)} %get-tuple-element.67), channel_id=1, source_target_pairs={{0,4},{4,8},{8,12},{12,14},{14,10},{10,6},{6,2},{2,0},{1,5},{5,9},... | collective-permute-start | bytes 589832 | tf_op jit(solution)/shard_map/ppermute | solution.py:569
  42.9 7.3 %collective-permute-start.15 = (bf16[768,128]{1,0:T(8,128)(2,1)S(1)}, bf16[768,128]{1,0:T(8,128)(2,1)S(1)}, u32[]{:S(2)}, u32[]{:S(2)}) collective-permute-start(bf16[768,128]{1,0:T(8,128)(2,1)S(1)} %get-tuple-element.68), channel_id=1, source_target_pairs={{0,2},{4,0},{8,4},{12,8},{14,12},{10,14},{6,10},{2,6},{1,3},{5,1},... | collective-permute-start | bytes 589832 | tf_op jit(solution)/shard_map/ppermute | solution.py:569

commit v13 on v12

--- a/solution.py
+++ b/solution.py
@@ -329,12 +329,10 @@
         def some(lines, sums, item=item):
             for head in range(CORE_HEADS):
                 product = jnp.dot(lines[...], weight[head], preferred_element_type=F32)
-                begin = head % 2 * STRETCH
-                out[item, head // 2, begin : begin + STRETCH] = product[:, :HEAD_DIM]
-                begin += 2 * STRETCH
-                out[item, head // 2, begin : begin + STRETCH] = product[:, HEAD_DIM:]
-            for half in range(2):
-                out[item, half, 4 * STRETCH :] = sums[...]
+                rows = slice(head * STRETCH, (head + 1) * STRETCH)
+                out[item, 0, rows] = product[:, :HEAD_DIM]
+                out[item, 1, rows] = product[:, HEAD_DIM:]
+            out[item, 0, CORE_HEADS * STRETCH :] = sums[...]
 
         def none(item=item):
             out[item] = jnp.zeros(out.shape[1:], F32)
@@ -359,39 +357,36 @@
     )(targets, own, squares, other, gain, weight)
 
 
-def send_kernel(half, first, terms, right, left, to_right, to_left):
-    rows = 4 * STRETCH
-    middle = 2 * STRETCH
-    if first:
-        from_right = right[half * middle : (half + 1) * middle].astype(F32)
-        from_left = left[half * middle : (half + 1) * middle].astype(F32)
-        to_right[:middle] = (terms[0, half, :middle] + from_right).astype(BF16)
-        to_right[middle:rows] = terms[0, half, middle:rows].astype(BF16)
-        to_left[:middle] = terms[1, half, :middle].astype(BF16)
-        to_left[middle:rows] = (terms[1, half, middle:rows] + from_left).astype(BF16)
-    else:
-        to_right[:rows] = (terms[0, half, :rows] + right[:rows].astype(F32)).astype(BF16)
-        to_left[:rows] = (terms[1, half, :rows] + left[:rows].astype(F32)).astype(BF16)
-    if half == 0:
-        right_sum = terms[0, 0, rows:] + one_piece(right[rows:])
-        left_sum = terms[1, 0, rows:]
-        if not first:
-            left_sum += one_piece(left[rows:])
-        to_right[rows:] = two_pieces(right_sum)
-        to_left[rows:] = two_pieces(left_sum)
-
-
-def sends(half, first, terms, right, left):
-    rows = 4 * STRETCH + (TAIL if half == 0 else 0)
-    shape = jax.ShapeDtypeStruct((rows, HEAD_DIM), BF16)
+def send_kernel(half, terms, *refs):
+    *arrived, to_right, to_left = refs
+    rows = CORE_HEADS * STRETCH
+    for item, out in enumerate((to_right, to_left)):
+        kind = (half + item) % 2
+        total = terms[item, kind, :rows]
+        if arrived:
+            total += arrived[item][:rows].astype(F32)
+        out[:rows] = total.astype(BF16)
+        if kind == 0:
+            squares = terms[item, 0, rows:]
+            if arrived:
+                squares += one_piece(arrived[item][rows : rows + TAIL])
+            out[rows : rows + TAIL] = two_pieces(squares)
+        spare = rows + (TAIL if kind == 0 else 0)
+        if spare < out.shape[0]:
+            out[spare:] = jnp.zeros((out.shape[0] - spare, HEAD_DIM), BF16)
+
+
+def sends(half, terms, arrived):
+    rows = CORE_HEADS * STRETCH
+    shapes = [jax.ShapeDtypeStruct((rows + TAIL, HEAD_DIM), BF16)] * 2
     return pl.pallas_call(
-        functools.partial(send_kernel, half, first),
-        in_specs=[VMEM] * 3,
+        functools.partial(send_kernel, half),
+        in_specs=[VMEM] * (1 + len(arrived)),
         out_specs=[VMEM] * 2,
-        out_shape=[shape, shape],
+        out_shape=shapes,
         compiler_params=pltpu.CompilerParams(vmem_limit_bytes=16 * MIB),
         name="sends",
-    )(terms, right, left)
+    )(terms, *arrived)
 
 
 def prepare_kernel(targets, queries, starts, turns, grouped, rotary):
@@ -482,24 +477,22 @@
 
 
 def final_kernel(
-    targets, rotary, own, right_a, left_a, right_b, left_b, grouped, cached_there, cached_here, out
+    targets, rotary, own, right_keys, left_values, right_values, left_keys, grouped,
+    cached_there, cached_here, out,
 ):
     scaling = HEAD_DIM ** (-0.5)
     dims = (((1,), (1,)), ((), ()))
     mine = own.shape[0] - 1
-    rep = lax.axis_index("rep")
-    first = rep * CORE_HEADS
+    first = lax.axis_index("rep") * CORE_HEADS
     prompt = prompt_of(targets, lax.axis_index("tp"))
     cosine, sine = rotary[0], rotary[1]
-    rows = 4 * STRETCH
-    squares = own[mine, 0, rows:] + one_piece(right_a[rows:]) + one_piece(left_a[rows:])
+    rows = CORE_HEADS * STRETCH
+    squares = own[mine, 0, rows:] + one_piece(right_keys[rows : rows + TAIL]) + one_piece(left_keys[rows : rows + TAIL])
     scale = token_column(lax.rsqrt(squares / D + EPSILON))
     for head in range(CORE_HEADS):
-        right, left = ((right_a, left_a), (right_b, left_b))[head // 2]
-        at = slice(head % 2 * STRETCH, (head % 2 + 1) * STRETCH)
-        keys = own[mine, head // 2, at] + right[at].astype(F32) + left[at].astype(F32)
-        at = slice((2 + head % 2) * STRETCH, (3 + head % 2) * STRETCH)
-        values = own[mine, head // 2, at] + right[at].astype(F32) + left[at].astype(F32)
+        at = slice(head * STRETCH, (head + 1) * STRETCH)
+        keys = own[mine, 0, at] + right_keys[at].astype(F32) + left_keys[at].astype(F32)
+        values = own[mine, 1, at] + right_values[at].astype(F32) + left_values[at].astype(F32)
         keys = (keys * scale).astype(BF16).astype(F32)
         values = (values * scale).astype(BF16)
         keys = keys * cosine + pltpu.roll(keys, HEAD_DIM // 2, 1) * sine
@@ -578,29 +571,35 @@
     features = [own, squares, other, gain]
     right, left = project_first(half, target_rows, *features, weight)
     targets, _ = lax.optimization_barrier((target_rows, left))
-    arrived = [pass_on(right, left)] * 2
-    grouped, rotary = prepare(targets, queries, starts, jnp.asarray(turns))
+    arrived = [pass_on(right, left), []]
 
     cached = []
     for distance in range(half - 1, 0, -1):
         distances = [distance, -distance] + ([0] if distance == 1 else [])
-        if len(cached) < 2:
-            cached.append(
-                cache_attention(
-                    len(cached), targets, prompt_lengths, cache_lengths, grouped, kv_cache, new_kv
+        terms = project(distances, targets, *features, weight)
+        right, left = sends(1, terms, arrived[1])
+        if distance == half - 1:
+            targets, _ = lax.optimization_barrier((target_rows, right))
+        terms, right = lax.optimization_barrier((terms, right))
+        arrived[1] = pass_on(right, left)
+        if distance == half - 1:
+            grouped, rotary = prepare(targets, queries, starts, jnp.asarray(turns))
+            cached = [
+                swap(
+                    cache_attention(
+                        0, targets, prompt_lengths, cache_lengths, grouped, kv_cache, new_kv
+                    )
                 )
-            )
-        if len(cached) == 1:
-            cached = [swap(cached[0])]
-        terms = project(distances, targets, *features, weight)
-        later = terms
-        for part in range(2):
-            right, left = sends(part, distance == half - 1, (terms, later)[part], *arrived[part])
-            if part == 0:
-                right, cached, later = lax.optimization_barrier((right, cached, terms))
-            targets, _ = lax.optimization_barrier((target_rows, right))
-            arrived[part] = pass_on(right, left)
-
+            ]
+        right, left = sends(0, terms, arrived[0])
+        if distance == half - 2 or half == 2:
+            cached, right = lax.optimization_barrier((cached, right))
+        targets, _ = lax.optimization_barrier((target_rows, right))
+        arrived[0] = pass_on(right, left)
+
+    cached.append(
+        cache_attention(1, targets, prompt_lengths, cache_lengths, grouped, kv_cache, new_kv)
+    )
     out = finish(target_rows, rotary, terms, [*arrived[0], *arrived[1]], grouped, cached)
     return lax.all_gather(out, "rep", axis=2, tiled=True)
 

time: 54.7 us -> 54.5 us (level)
  starting transfers between devices: 18.7 us -> 15.7 us
  waiting for transfers between devices: 8.22 us -> 10.9 us
    ppermute x7, starting transfers between devices: 6.88 us -> 3.64 us  [pass_on(): lax.ppermute(right, 'tp', to_right)]
    ppermute x7, waiting for transfers between devices: 1.75 us -> 4.82 us  [pass_on(): lax.ppermute(left, 'tp', to_left)]
    pallas_call x1, Pallas kernels: 0.65 us -> 1.6 us  [project_first(): pl.pallas_call(functools.partial(first_kernel, distance), in_specs=[SMEM]...]
    pallas_call x3, Pallas kernels: 8.05 us -> 7.11 us  [project(): pl.pallas_call(functools.partial(project_kernel, distances), in_specs=[SM...]
  transfers between devices with their start and end apart: 16 -> 16, of which waited for: 4 -> 9; matrix products, arithmetic and copies ran while one was open for 0% -> 0% of each run, Pallas kernels for 39% -> 38%
where the time goes in v13:
time: 54.5 us; the launch traced here: 54.3 us
  Pallas kernels  24.2 us (44%)
  starting transfers between devices  15.7 us (29%)
  waiting for transfers between devices  10.9 us (20%)
  blocking collectives  1.85 us (3%)
  between operations  0.9 us (2%)
  local copies, waits for them, and re-layouts  0.67 us (1%)
    ppermute x7, starting transfers between devices, pass_on(): lax.ppermute(left, 'tp', to_left)  11.5 us
    pallas_call x1, Pallas kernels, dequantize(): pl.pallas_call(weights_kernel, grid=(1,), in_specs=[pl.BlockSpec(memory_s...  8.36 us
    pallas_call x3, Pallas kernels, project(): pl.pallas_call(functools.partial(project_kernel, distances), in_specs=[SM...  7.11 us
    ppermute x7, waiting for transfers between devices, pass_on(): lax.ppermute(right, 'tp', to_right)  6.05 us
    ppermute x7, waiting for transfers between devices, pass_on(): lax.ppermute(left, 'tp', to_left)  4.82 us
    pallas_call x2, Pallas kernels, cache_attention(): pl.pallas_call(functools.partial(cache_kernel, part), in_specs=[SMEM] * 3...  3.98 us
    ppermute x7, starting transfers between devices, pass_on(): lax.ppermute(right, 'tp', to_right)  3.64 us
    pallas_call x1, Pallas kernels, finish(): pl.pallas_call(final_kernel, in_specs=[SMEM] + [VMEM] * 9, out_specs=VMEM...  1.98 us
  transfers between devices with their start and end apart: 16, of which 9 were waited for; matrix products, arithmetic and copies ran while one was open for 0% of the time, Pallas kernels for 38%

profile of v13, /device:TPU:0, one launch (start us, length us, event | category | flops | bytes accessed | tf_op | source)
XLA Modules:
  0.0 54.3 jit_solution(10871906721135001746)
XLA Ops:
  0.0 0.5 collective-permute-start
  0.5 8.4 %dequantize.1 = (bf16[4,2048,256]{2,1,0:T(8,128)(2,1)S(1)}, bf16[3,192,2048]{2,1,0:T(8,128)(2,1)S(1)}, f32[3,8,128]{2,1,0:T(8,128)S(1)}) custom-call(bf16[3,192,2048]{2,1,0:T(8,128)(2,1)} %bitcast.9, s32[2048,2048]{1,0:T(8,128)} %codes.1, s32[32,2048]{1,0:T(8,128)} %value_scales.1, s32[32,2048]{1,0:T(8,128)} %value_scales.1, f32[8,32]{1,0:T(8,128)} %bitcast.10, ...), custom_call_target="tpu_custom_call" | custom-call | flops 134217728 | bytes 8388608 | tf_op jit(solution)/shard_map/dequantize/pallas_call | solution.py:224
  8.8 0.0 collective-permute-done.other
  8.9 0.0 copy-start.6
  8.9 1.6 %project_first.1 = (bf16[784,128]{1,0:T(8,128)(2,1)S(1)}, bf16[768,128]{1,0:T(8,128)(2,1)S(1)}) custom-call(s32[6]{0:T(128)S(1)} %copy-done.5, bf16[3,192,2048]{2,1,0:T(8,128)(2,1)S(1)} %get-tuple-element.37.own, f32[3,8,128]{2,1,0:T(8,128)S(1)} %get-tuple-element.38.squares, bf16[3,192,2048]{2,1,0:T(8,128)(2,1)S(1)} %collective-permute-done.other, ...), custom_call_target="tpu_custom_call" | custom-call | flops 805306368 | bytes 2097152 | tf_op jit(solution)/shard_map/project_first/pallas_call | solution.py:309
  10.5 2.5 %collective-permute-start.3 = (bf16[768,128]{1,0:T(8,128)(2,1)S(1)}, bf16[768,128]{1,0:T(8,128)(2,1)S(1)}, u32[]{:S(2)}, u32[]{:S(2)}) collective-permute-start(bf16[768,128]{1,0:T(8,128)(2,1)S(1)} %get-tuple-element.40), channel_id=1, source_target_pairs={{0,2},{4,0},{8,4},{12,8},{14,12},{10,14},{6,10},{2,6},{1,3},{5,1},... | collective-permute-start | bytes 589832 | tf_op jit(solution)/shard_map/ppermute | solution.py:562
  13.0 0.2 collective-permute-start.2
  13.2 2.6 %project.3.terms = f32[2,2,776,128]{3,2,1,0:T(8,128)S(1)} custom-call(s32[6]{0:T(128)S(1)} %copy-done.5, bf16[3,192,2048]{2,1,0:T(8,128)(2,1)S(1)} %get-tuple-element.37.own, f32[3,8,128]{2,1,0:T(8,128)S(1)} %get-tuple-element.38.squares, bf16[3,192,2048]{2,1,0:T(8,128)(2,1)S(1)} %collective-permute-done.other, f32[1,2048]{1,0:T(1,128)S(1)} %bitcast.5, ...), custom_call_target="tpu_custom_call" | custom-call | flops 805306368 | bytes 2097152 | tf_op jit(solution)/shard_map/project/pallas_call | solution.py:344
  15.7 0.0 copy-start.7
  15.8 0.0 copy-start.2
  15.8 0.0 copy-start.3
  15.8 0.0 copy-start.4
  15.8 2.0 %collective-permute-start.4 = (bf16[784,128]{1,0:T(8,128)(2,1)S(1)}, bf16[784,128]{1,0:T(8,128)(2,1)S(1)}, u32[]{:S(2)}, u32[]{:S(2)}) collective-permute-start(bf16[784,128]{1,0:T(8,128)(2,1)S(1)} %get-tuple-element.50), channel_id=1, source_target_pairs={{0,4},{4,8},{8,12},{12,14},{14,10},{10,6},{6,2},{2,0},{1,5},{5,9},... | collective-permute-start | bytes 602120 | tf_op jit(solution)/shard_map/ppermute | solution.py:562
  17.9 0.0 collective-permute-start.5
  17.9 0.8 %collective-permute-done.3.refs_1_ = bf16[768,128]{1,0:T(8,128)(2,1)S(1)} collective-permute-done((bf16[768,128]{1,0:T(8,128)(2,1)S(1)}, bf16[768,128]{1,0:T(8,128)(2,1)S(1)}, u32[]{:S(2)}, u32[]{:S(2)}) %collective-permute-start.3) | collective-permute-done | bytes 196640 | tf_op jit(solution)/shard_map/ppermute | solution.py:562
  18.7 2.1 %collective-permute-done.2.refs_0_ = bf16[784,128]{1,0:T(8,128)(2,1)S(1)} collective-permute-done((bf16[784,128]{1,0:T(8,128)(2,1)S(1)}, bf16[784,128]{1,0:T(8,128)(2,1)S(1)}, u32[]{:S(2)}, u32[]{:S(2)}) %collective-permute-start.2) | collective-permute-done | bytes 200736 | tf_op jit(solution)/shard_map/ppermute | solution.py:562
  20.8 0.1 sends.7
  20.9 1.6 %collective-permute-start.7 = (bf16[784,128]{1,0:T(8,128)(2,1)S(1)}, bf16[784,128]{1,0:T(8,128)(2,1)S(1)}, u32[]{:S(2)}, u32[]{:S(2)}) collective-permute-start(bf16[784,128]{1,0:T(8,128)(2,1)S(1)} %get-tuple-element.54), channel_id=1, source_target_pairs={{0,2},{4,0},{8,4},{12,8},{14,12},{10,14},{6,10},{2,6},{1,3},{5,1},... | collective-permute-start | bytes 602120 | tf_op jit(solution)/shard_map/ppermute | solution.py:562
  22.5 0.4 collective-permute-start.6
  23.0 0.1 multiply_cosine_fusion
  23.8 0.7 %prepare.1 = (bf16[8,32,128]{2,1,0:T(8,128)(2,1)S(1)}, f32[2,192,128]{2,1,0:T(8,128)S(1)}) custom-call(s32[6]{0:T(128)S(1)} %copy-done.5, bf16[1,2,16384]{2,1,0:T(2,128)(2,1)S(1)} %copy-done.3, f32[2,6,128]{2,1,0:T(8,128)S(1)} %pad_maximum_fusion.starts, f32[2,192,128]{2,1,0:T(8,128)S(1)} %copy-done.2), custom_call_target="tpu_custom_call" | custom-call | tf_op jit(solution)/shard_map/prepare/pallas_call | solution.py:407
  24.5 2.0 %cache_attention.2 = bf16[4,48,128]{2,1,0:T(8,128)(2,1)S(1)} custom-call(s32[6]{0:T(128)S(1)} %copy-done.5, s32[6]{0:T(128)S(1)} %copy-done.6, s32[1]{0:T(128)S(6)} %copy.15.stored, bf16[8,32,128]{2,1,0:T(8,128)(2,1)S(1)} %get-tuple-element.45.q.grouped, bf16[1,1024,2048]{2,1,0:T(8,128)(2,1)S(1)} %copy-done, bf16[1,2,2048]{2,1,0:T(2,128)(2,1)S(1)} %copy-done.4), custom_call_target="tpu_custom_call" | custom-call | flops 67108864 | bytes 2097152 | tf_op jit(solution)/shard_map/cache_attention/pallas_call | solution.py:464
  26.5 0.1 collective-permute-start.1
  26.6 2.8 %project.4.terms = f32[2,2,776,128]{3,2,1,0:T(8,128)S(1)} custom-call(s32[6]{0:T(128)S(1)} %copy-done.5, bf16[3,192,2048]{2,1,0:T(8,128)(2,1)S(1)} %get-tuple-element.37.own, f32[3,8,128]{2,1,0:T(8,128)S(1)} %get-tuple-element.38.squares, bf16[3,192,2048]{2,1,0:T(8,128)(2,1)S(1)} %collective-permute-done.other, f32[1,2048]{1,0:T(1,128)S(1)} %bitcast.6, ...), custom_call_target="tpu_custom_call" | custom-call | flops 805306368 | bytes 2097152 | tf_op jit(solution)/shard_map/project/pallas_call | solution.py:344
  29.4 0.1 sends.8
  29.5 0.1 collective-permute-start.8
  29.5 2.0 %collective-permute-start.9 = (bf16[784,128]{1,0:T(8,128)(2,1)S(1)}, bf16[784,128]{1,0:T(8,128)(2,1)S(1)}, u32[]{:S(2)}, u32[]{:S(2)}) collective-permute-start(bf16[784,128]{1,0:T(8,128)(2,1)S(1)} %get-tuple-element.59), channel_id=1, source_target_pairs={{0,2},{4,0},{8,4},{12,8},{14,12},{10,14},{6,10},{2,6},{1,3},{5,1},... | collective-permute-start | bytes 602120 | tf_op jit(solution)/shard_map/ppermute | solution.py:562
  31.6 0.1 sends.9
  31.7 0.1 collective-permute-start.10
  31.8 2.0 %collective-permute-start.11 = (bf16[784,128]{1,0:T(8,128)(2,1)S(1)}, bf16[784,128]{1,0:T(8,128)(2,1)S(1)}, u32[]{:S(2)}, u32[]{:S(2)}) collective-permute-start(bf16[784,128]{1,0:T(8,128)(2,1)S(1)} %get-tuple-element.62), channel_id=1, source_target_pairs={{0,2},{4,0},{8,4},{12,8},{14,12},{10,14},{6,10},{2,6},{1,3},{5,1},... | collective-permute-start | bytes 602120 | tf_op jit(solution)/shard_map/ppermute | solution.py:562
  33.7 1.7 %project.5.terms.own = f32[3,2,776,128]{3,2,1,0:T(8,128)S(1)} custom-call(s32[6]{0:T(128)S(1)} %copy-done.5, bf16[3,192,2048]{2,1,0:T(8,128)(2,1)S(1)} %get-tuple-element.37.own, f32[3,8,128]{2,1,0:T(8,128)S(1)} %get-tuple-element.38.squares, bf16[3,192,2048]{2,1,0:T(8,128)(2,1)S(1)} %collective-permute-done.other, f32[1,2048]{1,0:T(1,128)S(1)} %bitcast.7, ...), custom_call_target="tpu_custom_call" | custom-call | flops 1207959552 | bytes 2097152 | tf_op jit(solution)/shard_map/project/pallas_call | solution.py:344
  35.5 1.8 %collective-permute-done.8.refs_0_ = bf16[784,128]{1,0:T(8,128)(2,1)S(1)} collective-permute-done((bf16[784,128]{1,0:T(8,128)(2,1)S(1)}, bf16[784,128]{1,0:T(8,128)(2,1)S(1)}, u32[]{:S(2)}, u32[]{:S(2)}) %collective-permute-start.8) | collective-permute-done | bytes 200736 | tf_op jit(solution)/shard_map/ppermute | solution.py:562
  37.3 0.1 collective-permute-done.9.refs_1_
  37.4 0.1 sends.10
  37.5 0.8 %collective-permute-start.14 = (bf16[784,128]{1,0:T(8,128)(2,1)S(1)}, bf16[784,128]{1,0:T(8,128)(2,1)S(1)}, u32[]{:S(2)}, u32[]{:S(2)}) collective-permute-start(bf16[784,128]{1,0:T(8,128)(2,1)S(1)} %get-tuple-element.65), channel_id=1, source_target_pairs={{0,4},{4,8},{8,12},{12,14},{14,10},{10,6},{6,2},{2,0},{1,5},{5,9},... | collective-permute-start | bytes 602120 | tf_op jit(solution)/shard_map/ppermute | solution.py:562
  38.3 1.3 %collective-permute-start.15 = (bf16[784,128]{1,0:T(8,128)(2,1)S(1)}, bf16[784,128]{1,0:T(8,128)(2,1)S(1)}, u32[]{:S(2)}, u32[]{:S(2)}) collective-permute-start(bf16[784,128]{1,0:T(8,128)(2,1)S(1)} %get-tuple-element.66), channel_id=1, source_target_pairs={{0,2},{4,0},{8,4},{12,8},{14,12},{10,14},{6,10},{2,6},{1,3},{5,1},... | collective-permute-start | bytes 602120 | tf_op jit(solution)/shard_map/ppermute | solution.py:562
  39.6 2.0 %collective-permute-done.10.refs_0_ = bf16[784,128]{1,0:T(8,128)(2,1)S(1)} collective-permute-done((bf16[784,128]{1,0:T(8,128)(2,1)S(1)}, bf16[784,128]{1,0:T(8,128)(2,1)S(1)}, u32[]{:S(2)}, u32[]{:S(2)}) %collective-permute-start.10) | collective-permute-done | bytes 200736 | tf_op jit(solution)/shard_map/ppermute | solution.py:562
  41.6 0.1 collective-permute-done.11.refs_1_
  41.7 0.1 sends.11
  41.8 2.1 %collective-permute-start.13 = (bf16[784,128]{1,0:T(8,128)(2,1)S(1)}, bf16[784,128]{1,0:T(8,128)(2,1)S(1)}, u32[]{:S(2)}, u32[]{:S(2)}) collective-permute-start(bf16[784,128]{1,0:T(8,128)(2,1)S(1)} %get-tuple-element.64), channel_id=1, source_target_pairs={{0,2},{4,0},{8,4},{12,8},{14,12},{10,14},{6,10},{2,6},{1,3},{5,1},... | collective-permute-start | bytes 602120 | tf_op jit(solution)/shard_map/ppermute | solution.py:562
  43.8 0.0 collective-permute-start.12
  43.9 2.0 %cache_attention.3.cached_here = bf16[4,48,128]{2,1,0:T(8,128)(2,1)S(1)} custom-call(s32[6]{0:T(128)S(1)} %copy-done.5, s32[6]{0:T(128)S(1)} %copy-done.6, s32[1]{0:T(128)S(6)} %copy.15.stored, bf16[8,32,128]{2,1,0:T(8,128)(2,1)S(1)} %get-tuple-element.45.q.grouped, bf16[1,1024,2048]{2,1,0:T(8,128)(2,1)S(1)} %copy-done, bf16[1,2,2048]{2,1,0:T(2,128)(2,1)S(1)} %copy-done.4), custom_call_target="tpu_custom_call" | custom-call | flops 67108864 | bytes 2097152 | tf_op jit(solution)/shard_map/cache_attention/pallas_call | solution.py:464
  45.9 0.1 collective-permute-done.14.right_values
  45.9 0.7 %collective-permute-done.15.left_keys = bf16[784,128]{1,0:T(8,128)(2,1)S(1)} collective-permute-done((bf16[784,128]{1,0:T(8,128)(2,1)S(1)}, bf16[784,128]{1,0:T(8,128)(2,1)S(1)}, u32[]{:S(2)}, u32[]{:S(2)}) %collective-permute-start.15) | collective-permute-done | bytes 200736 | tf_op jit(solution)/shard_map/ppermute | solution.py:562
  46.6 3.2 %collective-permute-done.13.left_values = bf16[784,128]{1,0:T(8,128)(2,1)S(1)} collective-permute-done((bf16[784,128]{1,0:T(8,128)(2,1)S(1)}, bf16[784,128]{1,0:T(8,128)(2,1)S(1)}, u32[]{:S(2)}, u32[]{:S(2)}) %collective-permute-start.13) | collective-permute-done | bytes 200736 | tf_op jit(solution)/shard_map/ppermute | solution.py:562
  49.8 2.0 %finish.1 = bf16[1,2,8192]{2,1,0:T(2,128)(2,1)S(1)} custom-call(s32[6]{0:T(128)S(1)} %copy-done.5, f32[2,192,128]{2,1,0:T(8,128)S(1)} %get-tuple-element.44.rotary, f32[3,2,776,128]{3,2,1,0:T(8,128)S(1)} %project.5.terms.own, bf16[784,128]{1,0:T(8,128)(2,1)S(1)} %collective-permute-done.12.right_keys, ...), custom_call_target="tpu_custom_call" | custom-call | tf_op jit(solution)/shard_map/finish/pallas_call | solution.py:523
  51.8 1.9 %all_gather.3 = bf16[1,2,16384]{2,1,0:T(2,128)(2,1)S(1)} all-gather(bf16[1,2,8192]{2,1,0:T(2,128)(2,1)S(1)} %finish.1), channel_id=1, replica_groups=mesh['grp'=2,'tp'=8,'rep'=2] {'rep'}, dimensions={2}, use_global_device_ids=true | all-gather | bytes 98304 | tf_op jit(solution)/shard_map/all_gather | solution.py:604
  53.7 0.6 %copy.16 = bf16[1,2,16384]{2,1,0:T(2,128)(2,1)} copy(bf16[1,2,16384]{2,1,0:T(2,128)(2,1)S(1)} %all_gather.3) | data formatting | bytes 131072
  (20 shorter events, 0.1 us)
Async XLA Ops:
  0.0 8.8 %collective-permute-start = (bf16[3,192,2048]{2,1,0:T(8,128)(2,1)}, bf16[3,192,2048]{2,1,0:T(8,128)(2,1)S(1)}, u32[]{:S(2)}, u32[]{:S(2)}) collective-permute-start(bf16[3,192,2048]{2,1,0:T(8,128)(2,1)} %bitcast.8), channel_id=1, source_target_pairs={{0,1},{1,0},{2,3},{3,2},{4,5},{5,4},{6,7},{7,6},{8,9},{9,8},{10,11... | collective-permute-start | bytes 7077896 | tf_op jit(solution)/shard_map/ppermute | solution.py:564
  0.5 8.4 %copy-start.1 = (f32[2048]{0:T(1024)S(1)}, f32[2048]{0:T(1024)}, u32[]{:S(2)}) copy-start(f32[2048]{0:T(1024)} %param.14) | copy-start | bytes 24580
  0.5 8.4 %copy-start.5 = (s32[6]{0:T(128)S(1)}, s32[6]{0:T(128)}, u32[]{:S(2)}) copy-start(s32[6]{0:T(128)} %targets.9) | copy-start | bytes 76
  8.9 4.3 %copy-start.6 = (s32[6]{0:T(128)S(1)}, s32[6]{0:T(128)}, u32[]{:S(2)}) copy-start(s32[6]{0:T(128)} %lengths.3) | copy-start | bytes 76
  10.5 8.2 %collective-permute-start.3 = (bf16[768,128]{1,0:T(8,128)(2,1)S(1)}, bf16[768,128]{1,0:T(8,128)(2,1)S(1)}, u32[]{:S(2)}, u32[]{:S(2)}) collective-permute-start(bf16[768,128]{1,0:T(8,128)(2,1)S(1)} %get-tuple-element.40), channel_id=1, source_target_pairs={{0,2},{4,0},{8,4},{12,8},{14,12},{10,14},{6,10},{2,6},{1,3},{5,1},... | collective-permute-start | bytes 589832 | tf_op jit(solution)/shard_map/ppermute | solution.py:562
  13.0 7.8 %collective-permute-start.2 = (bf16[784,128]{1,0:T(8,128)(2,1)S(1)}, bf16[784,128]{1,0:T(8,128)(2,1)S(1)}, u32[]{:S(2)}, u32[]{:S(2)}) collective-permute-start(bf16[784,128]{1,0:T(8,128)(2,1)S(1)} %get-tuple-element.47), channel_id=1, source_target_pairs={{0,4},{4,8},{8,12},{12,14},{14,10},{10,6},{6,2},{2,0},{1,5},{5,9},... | collective-permute-start | bytes 602120 | tf_op jit(solution)/shard_map/ppermute | solution.py:562
  13.2 11.3 %copy-start = (bf16[1,1024,2048]{2,1,0:T(8,128)(2,1)S(1)}, bf16[1,1024,2048]{2,1,0:T(8,128)(2,1)}, u32[]{:S(2)}) copy-start(bf16[1,1024,2048]{2,1,0:T(8,128)(2,1)} %cache.3) | copy-start | bytes 12582916
  15.7 7.2 %copy-start.7 = (f32[128]{0:T(128)S(1)}, f32[128]{0:T(128)}, u32[]{:S(2)}) copy-start(f32[128]{0:T(128)} %constant.7.clone) | copy-start | bytes 1540
  15.8 8.0 %copy-start.2 = (f32[2,192,128]{2,1,0:T(8,128)S(1)}, f32[2,192,128]{2,1,0:T(8,128)}, u32[]{:S(2)}) copy-start(f32[2,192,128]{2,1,0:T(8,128)} %constant.8.clone.turns) | copy-start | bytes 589828
  15.8 8.0 %copy-start.3 = (bf16[1,2,16384]{2,1,0:T(2,128)(2,1)S(1)}, bf16[1,2,16384]{2,1,0:T(2,128)(2,1)}, u32[]{:S(2)}) copy-start(bf16[1,2,16384]{2,1,0:T(2,128)(2,1)} %queries.1) | copy-start | bytes 196612
  15.8 8.7 %copy-start.4 = (bf16[1,2,2048]{2,1,0:T(2,128)(2,1)S(1)}, bf16[1,2,2048]{2,1,0:T(2,128)(2,1)}, u32[]{:S(2)}) copy-start(bf16[1,2,2048]{2,1,0:T(2,128)(2,1)} %new.3) | copy-start | bytes 24580
  15.8 13.5 %collective-permute-start.4 = (bf16[784,128]{1,0:T(8,128)(2,1)S(1)}, bf16[784,128]{1,0:T(8,128)(2,1)S(1)}, u32[]{:S(2)}, u32[]{:S(2)}) collective-permute-start(bf16[784,128]{1,0:T(8,128)(2,1)S(1)} %get-tuple-element.50), channel_id=1, source_target_pairs={{0,4},{4,8},{8,12},{12,14},{14,10},{10,6},{6,2},{2,0},{1,5},{5,9},... | collective-permute-start | bytes 602120 | tf_op jit(solution)/shard_map/ppermute | solution.py:562
  17.9 11.5 %collective-permute-start.5 = (bf16[784,128]{1,0:T(8,128)(2,1)S(1)}, bf16[784,128]{1,0:T(8,128)(2,1)S(1)}, u32[]{:S(2)}, u32[]{:S(2)}) collective-permute-start(bf16[784,128]{1,0:T(8,128)(2,1)S(1)} %get-tuple-element.51), channel_id=1, source_target_pairs={{0,2},{4,0},{8,4},{12,8},{14,12},{10,14},{6,10},{2,6},{1,3},{5,1},... | collective-permute-start | bytes 602120 | tf_op jit(solution)/shard_map/ppermute | solution.py:562
  20.9 10.6 %collective-permute-start.7 = (bf16[784,128]{1,0:T(8,128)(2,1)S(1)}, bf16[784,128]{1,0:T(8,128)(2,1)S(1)}, u32[]{:S(2)}, u32[]{:S(2)}) collective-permute-start(bf16[784,128]{1,0:T(8,128)(2,1)S(1)} %get-tuple-element.54), channel_id=1, source_target_pairs={{0,2},{4,0},{8,4},{12,8},{14,12},{10,14},{6,10},{2,6},{1,3},{5,1},... | collective-permute-start | bytes 602120 | tf_op jit(solution)/shard_map/ppermute | solution.py:562
  22.5 9.0 %collective-permute-start.6 = (bf16[784,128]{1,0:T(8,128)(2,1)S(1)}, bf16[784,128]{1,0:T(8,128)(2,1)S(1)}, u32[]{:S(2)}, u32[]{:S(2)}) collective-permute-start(bf16[784,128]{1,0:T(8,128)(2,1)S(1)} %get-tuple-element.48), channel_id=1, source_target_pairs={{0,4},{4,8},{8,12},{12,14},{14,10},{10,6},{6,2},{2,0},{1,5},{5,9},... | collective-permute-start | bytes 602120 | tf_op jit(solution)/shard_map/ppermute | solution.py:562
  26.5 5.2 %collective-permute-start.1 = (bf16[4,48,128]{2,1,0:T(8,128)(2,1)S(1)}, bf16[4,48,128]{2,1,0:T(8,128)(2,1)S(1)}, u32[]{:S(2)}, u32[]{:S(2)}) collective-permute-start(bf16[4,48,128]{2,1,0:T(8,128)(2,1)S(1)} %cache_attention.2), channel_id=1, source_target_pairs={{0,1},{1,0},{2,3},{3,2},{4,5},{5,4},{6,7},{7,6},{8,9},{9,8},{10,11... | collective-permute-start | bytes 147464 | tf_op jit(solution)/shard_map/ppermute | solution.py:564
  29.5 7.8 %collective-permute-start.8 = (bf16[784,128]{1,0:T(8,128)(2,1)S(1)}, bf16[784,128]{1,0:T(8,128)(2,1)S(1)}, u32[]{:S(2)}, u32[]{:S(2)}) collective-permute-start(bf16[784,128]{1,0:T(8,128)(2,1)S(1)} %get-tuple-element.58), channel_id=1, source_target_pairs={{0,4},{4,8},{8,12},{12,14},{14,10},{10,6},{6,2},{2,0},{1,5},{5,9},... | collective-permute-start | bytes 602120 | tf_op jit(solution)/shard_map/ppermute | solution.py:562
  29.5 7.8 %collective-permute-start.9 = (bf16[784,128]{1,0:T(8,128)(2,1)S(1)}, bf16[784,128]{1,0:T(8,128)(2,1)S(1)}, u32[]{:S(2)}, u32[]{:S(2)}) collective-permute-start(bf16[784,128]{1,0:T(8,128)(2,1)S(1)} %get-tuple-element.59), channel_id=1, source_target_pairs={{0,2},{4,0},{8,4},{12,8},{14,12},{10,14},{6,10},{2,6},{1,3},{5,1},... | collective-permute-start | bytes 602120 | tf_op jit(solution)/shard_map/ppermute | solution.py:562
  31.7 10.0 %collective-permute-start.10 = (bf16[784,128]{1,0:T(8,128)(2,1)S(1)}, bf16[784,128]{1,0:T(8,128)(2,1)S(1)}, u32[]{:S(2)}, u32[]{:S(2)}) collective-permute-start(bf16[784,128]{1,0:T(8,128)(2,1)S(1)} %get-tuple-element.56), channel_id=1, source_target_pairs={{0,4},{4,8},{8,12},{12,14},{14,10},{10,6},{6,2},{2,0},{1,5},{5,9},... | collective-permute-start | bytes 602120 | tf_op jit(solution)/shard_map/ppermute | solution.py:562
  31.8 9.9 %collective-permute-start.11 = (bf16[784,128]{1,0:T(8,128)(2,1)S(1)}, bf16[784,128]{1,0:T(8,128)(2,1)S(1)}, u32[]{:S(2)}, u32[]{:S(2)}) collective-permute-start(bf16[784,128]{1,0:T(8,128)(2,1)S(1)} %get-tuple-element.62), channel_id=1, source_target_pairs={{0,2},{4,0},{8,4},{12,8},{14,12},{10,14},{6,10},{2,6},{1,3},{5,1},... | collective-permute-start | bytes 602120 | tf_op jit(solution)/shard_map/ppermute | solution.py:562
  37.5 8.4 %collective-permute-start.14 = (bf16[784,128]{1,0:T(8,128)(2,1)S(1)}, bf16[784,128]{1,0:T(8,128)(2,1)S(1)}, u32[]{:S(2)}, u32[]{:S(2)}) collective-permute-start(bf16[784,128]{1,0:T(8,128)(2,1)S(1)} %get-tuple-element.65), channel_id=1, source_target_pairs={{0,4},{4,8},{8,12},{12,14},{14,10},{10,6},{6,2},{2,0},{1,5},{5,9},... | collective-permute-start | bytes 602120 | tf_op jit(solution)/shard_map/ppermute | solution.py:562
  38.3 8.3 %collective-permute-start.15 = (bf16[784,128]{1,0:T(8,128)(2,1)S(1)}, bf16[784,128]{1,0:T(8,128)(2,1)S(1)}, u32[]{:S(2)}, u32[]{:S(2)}) collective-permute-start(bf16[784,128]{1,0:T(8,128)(2,1)S(1)} %get-tuple-element.66), channel_id=1, source_target_pairs={{0,2},{4,0},{8,4},{12,8},{14,12},{10,14},{6,10},{2,6},{1,3},{5,1},... | collective-permute-start | bytes 602120 | tf_op jit(solution)/shard_map/ppermute | solution.py:562
  41.8 8.1 %collective-permute-start.13 = (bf16[784,128]{1,0:T(8,128)(2,1)S(1)}, bf16[784,128]{1,0:T(8,128)(2,1)S(1)}, u32[]{:S(2)}, u32[]{:S(2)}) collective-permute-start(bf16[784,128]{1,0:T(8,128)(2,1)S(1)} %get-tuple-element.64), channel_id=1, source_target_pairs={{0,2},{4,0},{8,4},{12,8},{14,12},{10,14},{6,10},{2,6},{1,3},{5,1},... | collective-permute-start | bytes 602120 | tf_op jit(solution)/shard_map/ppermute | solution.py:562
  43.8 6.0 %collective-permute-start.12 = (bf16[784,128]{1,0:T(8,128)(2,1)S(1)}, bf16[784,128]{1,0:T(8,128)(2,1)S(1)}, u32[]{:S(2)}, u32[]{:S(2)}) collective-permute-start(bf16[784,128]{1,0:T(8,128)(2,1)S(1)} %get-tuple-element.63), channel_id=1, source_target_pairs={{0,4},{4,8},{8,12},{12,14},{14,10},{10,6},{6,2},{2,0},{1,5},{5,9},... | collective-permute-start | bytes 602120 | tf_op jit(solution)/shard_map/ppermute | solution.py:562

commit v14 on v13

--- a/solution.py
+++ b/solution.py
@@ -573,30 +573,26 @@
     targets, _ = lax.optimization_barrier((target_rows, left))
     arrived = [pass_on(right, left), []]
 
-    cached = []
     for distance in range(half - 1, 0, -1):
         distances = [distance, -distance] + ([0] if distance == 1 else [])
         terms = project(distances, targets, *features, weight)
         right, left = sends(1, terms, arrived[1])
-        if distance == half - 1:
+        terms, right = lax.optimization_barrier((terms, right))
+        if distance == 1:
             targets, _ = lax.optimization_barrier((target_rows, right))
-        terms, right = lax.optimization_barrier((terms, right))
         arrived[1] = pass_on(right, left)
-        if distance == half - 1:
+        if distance == 1:
             grouped, rotary = prepare(targets, queries, starts, jnp.asarray(turns))
-            cached = [
-                swap(
-                    cache_attention(
-                        0, targets, prompt_lengths, cache_lengths, grouped, kv_cache, new_kv
-                    )
-                )
-            ]
+            cached = cache_attention(
+                0, targets, prompt_lengths, cache_lengths, grouped, kv_cache, new_kv
+            )
         right, left = sends(0, terms, arrived[0])
-        if distance == half - 2 or half == 2:
+        if distance == 1:
             cached, right = lax.optimization_barrier((cached, right))
         targets, _ = lax.optimization_barrier((target_rows, right))
         arrived[0] = pass_on(right, left)
 
+    cached = [swap(cached)]
     cached.append(
         cache_attention(1, targets, prompt_lengths, cache_lengths, grouped, kv_cache, new_kv)
     )

time: 54.5 us -> 52.8 us (0.969)
  waiting for transfers between devices: 10.9 us -> 8.34 us
  starting transfers between devices: 15.7 us -> 16.8 us
    ppermute x7, starting transfers between devices: 3.64 us -> 10 us  [pass_on(): lax.ppermute(right, 'tp', to_right)]
    ppermute x7, starting transfers between devices: 11.5 us -> 6.27 us  [pass_on(): lax.ppermute(left, 'tp', to_left)]
    ppermute x7, waiting for transfers between devices: 6.05 us -> 3.58 us  [pass_on(): lax.ppermute(right, 'tp', to_right)]
  transfers between devices with their start and end apart: 16 -> 16, of which waited for: 9 -> 8; matrix products, arithmetic and copies ran while one was open for 0% -> 0% of each run, Pallas kernels for 38% -> 39%
where the time goes in v14:
time: 52.8 us; the launch traced here: 52.6 us
  Pallas kernels  24 us (45%)
  starting transfers between devices  16.8 us (32%)
  waiting for transfers between devices  8.34 us (16%)
  blocking collectives  1.85 us (4%)
  between operations  0.9 us (2%)
  local copies, waits for them, and re-layouts  0.67 us (1%)
    ppermute x7, starting transfers between devices, pass_on(): lax.ppermute(right, 'tp', to_right)  10 us
    pallas_call x1, Pallas kernels, dequantize(): pl.pallas_call(weights_kernel, grid=(1,), in_specs=[pl.BlockSpec(memory_s...  8.35 us
    pallas_call x3, Pallas kernels, project(): pl.pallas_call(functools.partial(project_kernel, distances), in_specs=[SM...  6.95 us
    ppermute x7, starting transfers between devices, pass_on(): lax.ppermute(left, 'tp', to_left)  6.27 us
    ppermute x7, waiting for transfers between devices, pass_on(): lax.ppermute(left, 'tp', to_left)  4.76 us
    pallas_call x2, Pallas kernels, cache_attention(): pl.pallas_call(functools.partial(cache_kernel, part), in_specs=[SMEM] * 3...  3.98 us
    ppermute x7, waiting for transfers between devices, pass_on(): lax.ppermute(right, 'tp', to_right)  3.58 us
    pallas_call x1, Pallas kernels, finish(): pl.pallas_call(final_kernel, in_specs=[SMEM] + [VMEM] * 9, out_specs=VMEM...  1.98 us
  transfers between devices with their start and end apart: 16, of which 8 were waited for; matrix products, arithmetic and copies ran while one was open for 0% of the time, Pallas kernels for 39%

profile of v14, /device:TPU:0, one launch (start us, length us, event | category | flops | bytes accessed | tf_op | source)
XLA Modules:
  0.0 52.6 jit_solution(13445652757633067854)
XLA Ops:
  0.0 0.5 collective-permute-start
  1.1 8.3 %dequantize.1 = (bf16[4,2048,256]{2,1,0:T(8,128)(2,1)S(1)}, bf16[3,192,2048]{2,1,0:T(8,128)(2,1)S(1)}, f32[3,8,128]{2,1,0:T(8,128)S(1)}) custom-call(bf16[3,192,2048]{2,1,0:T(8,128)(2,1)} %bitcast.9, s32[2048,2048]{1,0:T(8,128)} %codes.1, s32[32,2048]{1,0:T(8,128)} %value_scales.1, s32[32,2048]{1,0:T(8,128)} %value_scales.1, f32[8,32]{1,0:T(8,128)} %bitcast.10, ...), custom_call_target="tpu_custom_call" | custom-call | flops 134217728 | bytes 8388608 | tf_op jit(solution)/shard_map/dequantize/pallas_call | solution.py:224
  9.5 0.0 copy-start.6
  9.5 1.6 %project_first.1 = (bf16[784,128]{1,0:T(8,128)(2,1)S(1)}, bf16[768,128]{1,0:T(8,128)(2,1)S(1)}) custom-call(s32[6]{0:T(128)S(1)} %copy-done.5, bf16[3,192,2048]{2,1,0:T(8,128)(2,1)S(1)} %get-tuple-element.37.own, f32[3,8,128]{2,1,0:T(8,128)S(1)} %get-tuple-element.38.squares, bf16[3,192,2048]{2,1,0:T(8,128)(2,1)S(1)} %collective-permute-done.other, ...), custom_call_target="tpu_custom_call" | custom-call | flops 805306368 | bytes 2097152 | tf_op jit(solution)/shard_map/project_first/pallas_call | solution.py:309
  11.1 1.6 %collective-permute-start.2 = (bf16[768,128]{1,0:T(8,128)(2,1)S(1)}, bf16[768,128]{1,0:T(8,128)(2,1)S(1)}, u32[]{:S(2)}, u32[]{:S(2)}) collective-permute-start(bf16[768,128]{1,0:T(8,128)(2,1)S(1)} %get-tuple-element.40), channel_id=1, source_target_pairs={{0,2},{4,0},{8,4},{12,8},{14,12},{10,14},{6,10},{2,6},{1,3},{5,1},... | collective-permute-start | bytes 589832 | tf_op jit(solution)/shard_map/ppermute | solution.py:562
  12.7 1.1 %collective-permute-start.1 = (bf16[784,128]{1,0:T(8,128)(2,1)S(1)}, bf16[784,128]{1,0:T(8,128)(2,1)S(1)}, u32[]{:S(2)}, u32[]{:S(2)}) collective-permute-start(bf16[784,128]{1,0:T(8,128)(2,1)S(1)} %get-tuple-element.44), channel_id=1, source_target_pairs={{0,4},{4,8},{8,12},{12,14},{14,10},{10,6},{6,2},{2,0},{1,5},{5,9},... | collective-permute-start | bytes 602120 | tf_op jit(solution)/shard_map/ppermute | solution.py:562
  13.8 1.7 %project.3.terms = f32[2,2,776,128]{3,2,1,0:T(8,128)S(1)} custom-call(s32[6]{0:T(128)S(1)} %copy-done.5, bf16[3,192,2048]{2,1,0:T(8,128)(2,1)S(1)} %get-tuple-element.37.own, f32[3,8,128]{2,1,0:T(8,128)S(1)} %get-tuple-element.38.squares, bf16[3,192,2048]{2,1,0:T(8,128)(2,1)S(1)} %collective-permute-done.other, f32[1,2048]{1,0:T(1,128)S(1)} %bitcast.5, ...), custom_call_target="tpu_custom_call" | custom-call | flops 805306368 | bytes 2097152 | tf_op jit(solution)/shard_map/project/pallas_call | solution.py:344
  15.5 0.0 copy-start.7
  15.6 2.9 %collective-permute-start.3 = (bf16[784,128]{1,0:T(8,128)(2,1)S(1)}, bf16[784,128]{1,0:T(8,128)(2,1)S(1)}, u32[]{:S(2)}, u32[]{:S(2)}) collective-permute-start(bf16[784,128]{1,0:T(8,128)(2,1)S(1)} %get-tuple-element.47), channel_id=1, source_target_pairs={{0,4},{4,8},{8,12},{12,14},{14,10},{10,6},{6,2},{2,0},{1,5},{5,9},... | collective-permute-start | bytes 602120 | tf_op jit(solution)/shard_map/ppermute | solution.py:562
  18.5 0.0 collective-permute-start.4
  18.5 0.8 %collective-permute-done.2.refs_1_ = bf16[768,128]{1,0:T(8,128)(2,1)S(1)} collective-permute-done((bf16[768,128]{1,0:T(8,128)(2,1)S(1)}, bf16[768,128]{1,0:T(8,128)(2,1)S(1)}, u32[]{:S(2)}, u32[]{:S(2)}) %collective-permute-start.2) | collective-permute-done | bytes 196640 | tf_op jit(solution)/shard_map/ppermute | solution.py:562
  19.3 1.2 %collective-permute-done.1.refs_0_ = bf16[784,128]{1,0:T(8,128)(2,1)S(1)} collective-permute-done((bf16[784,128]{1,0:T(8,128)(2,1)S(1)}, bf16[784,128]{1,0:T(8,128)(2,1)S(1)}, u32[]{:S(2)}, u32[]{:S(2)}) %collective-permute-start.1) | collective-permute-done | bytes 200736 | tf_op jit(solution)/shard_map/ppermute | solution.py:562
  20.5 0.1 sends.7
  20.6 0.8 %collective-permute-start.5 = (bf16[784,128]{1,0:T(8,128)(2,1)S(1)}, bf16[784,128]{1,0:T(8,128)(2,1)S(1)}, u32[]{:S(2)}, u32[]{:S(2)}) collective-permute-start(bf16[784,128]{1,0:T(8,128)(2,1)S(1)} %get-tuple-element.45), channel_id=1, source_target_pairs={{0,4},{4,8},{8,12},{12,14},{14,10},{10,6},{6,2},{2,0},{1,5},{5,9},... | collective-permute-start | bytes 602120 | tf_op jit(solution)/shard_map/ppermute | solution.py:562
  21.4 1.4 %collective-permute-start.6 = (bf16[784,128]{1,0:T(8,128)(2,1)S(1)}, bf16[784,128]{1,0:T(8,128)(2,1)S(1)}, u32[]{:S(2)}, u32[]{:S(2)}) collective-permute-start(bf16[784,128]{1,0:T(8,128)(2,1)S(1)} %get-tuple-element.51), channel_id=1, source_target_pairs={{0,2},{4,0},{8,4},{12,8},{14,12},{10,14},{6,10},{2,6},{1,3},{5,1},... | collective-permute-start | bytes 602120 | tf_op jit(solution)/shard_map/ppermute | solution.py:562
  22.8 0.1 multiply_cosine_fusion
  22.9 1.7 %project.4.terms = f32[2,2,776,128]{3,2,1,0:T(8,128)S(1)} custom-call(s32[6]{0:T(128)S(1)} %copy-done.5, bf16[3,192,2048]{2,1,0:T(8,128)(2,1)S(1)} %get-tuple-element.37.own, f32[3,8,128]{2,1,0:T(8,128)S(1)} %get-tuple-element.38.squares, bf16[3,192,2048]{2,1,0:T(8,128)(2,1)S(1)} %collective-permute-done.other, f32[1,2048]{1,0:T(1,128)S(1)} %bitcast.6, ...), custom_call_target="tpu_custom_call" | custom-call | flops 805306368 | bytes 2097152 | tf_op jit(solution)/shard_map/project/pallas_call | solution.py:344
  24.6 0.3 collective-permute-done.3.refs_0_
  24.8 1.6 %collective-permute-done.4.refs_1_ = bf16[784,128]{1,0:T(8,128)(2,1)S(1)} collective-permute-done((bf16[784,128]{1,0:T(8,128)(2,1)S(1)}, bf16[784,128]{1,0:T(8,128)(2,1)S(1)}, u32[]{:S(2)}, u32[]{:S(2)}) %collective-permute-start.4) | collective-permute-done | bytes 200736 | tf_op jit(solution)/shard_map/ppermute | solution.py:562
  26.4 0.1 sends.8
  26.5 1.8 %collective-permute-start.7 = (bf16[784,128]{1,0:T(8,128)(2,1)S(1)}, bf16[784,128]{1,0:T(8,128)(2,1)S(1)}, u32[]{:S(2)}, u32[]{:S(2)}) collective-permute-start(bf16[784,128]{1,0:T(8,128)(2,1)S(1)} %get-tuple-element.54), channel_id=1, source_target_pairs={{0,4},{4,8},{8,12},{12,14},{14,10},{10,6},{6,2},{2,0},{1,5},{5,9},... | collective-permute-start | bytes 602120 | tf_op jit(solution)/shard_map/ppermute | solution.py:562
  28.3 0.5 collective-permute-start.8
  28.7 0.4 collective-permute-done.5.refs_0_
  29.1 1.4 %collective-permute-done.6.refs_1_ = bf16[784,128]{1,0:T(8,128)(2,1)S(1)} collective-permute-done((bf16[784,128]{1,0:T(8,128)(2,1)S(1)}, bf16[784,128]{1,0:T(8,128)(2,1)S(1)}, u32[]{:S(2)}, u32[]{:S(2)}) %collective-permute-start.6) | collective-permute-done | bytes 200736 | tf_op jit(solution)/shard_map/ppermute | solution.py:562
  30.6 0.1 sends.9
  30.7 0.7 %collective-permute-start.10 = (bf16[784,128]{1,0:T(8,128)(2,1)S(1)}, bf16[784,128]{1,0:T(8,128)(2,1)S(1)}, u32[]{:S(2)}, u32[]{:S(2)}) collective-permute-start(bf16[784,128]{1,0:T(8,128)(2,1)S(1)} %get-tuple-element.62), channel_id=1, source_target_pairs={{0,2},{4,0},{8,4},{12,8},{14,12},{10,14},{6,10},{2,6},{1,3},{5,1},... | collective-permute-start | bytes 602120 | tf_op jit(solution)/shard_map/ppermute | solution.py:562
  31.3 1.4 %collective-permute-start.9 = (bf16[784,128]{1,0:T(8,128)(2,1)S(1)}, bf16[784,128]{1,0:T(8,128)(2,1)S(1)}, u32[]{:S(2)}, u32[]{:S(2)}) collective-permute-start(bf16[784,128]{1,0:T(8,128)(2,1)S(1)} %get-tuple-element.52), channel_id=1, source_target_pairs={{0,4},{4,8},{8,12},{12,14},{14,10},{10,6},{6,2},{2,0},{1,5},{5,9},... | collective-permute-start | bytes 602120 | tf_op jit(solution)/shard_map/ppermute | solution.py:562
  32.8 3.6 %project.5.terms.own = f32[3,2,776,128]{3,2,1,0:T(8,128)S(1)} custom-call(s32[6]{0:T(128)S(1)} %copy-done.5, bf16[3,192,2048]{2,1,0:T(8,128)(2,1)S(1)} %get-tuple-element.37.own, f32[3,8,128]{2,1,0:T(8,128)S(1)} %get-tuple-element.38.squares, bf16[3,192,2048]{2,1,0:T(8,128)(2,1)S(1)} %collective-permute-done.other, f32[1,2048]{1,0:T(1,128)S(1)} %bitcast.7, ...), custom_call_target="tpu_custom_call" | custom-call | flops 1207959552 | bytes 2097152 | tf_op jit(solution)/shard_map/project/pallas_call | solution.py:344
  36.4 0.0 copy-start.2
  36.4 0.0 copy-start.3
  36.4 0.0 copy-start.4
  36.4 0.0 collective-permute-done.8.refs_1_
  36.5 0.1 sends.10
  36.5 1.0 %collective-permute-start.13 = (bf16[784,128]{1,0:T(8,128)(2,1)S(1)}, bf16[784,128]{1,0:T(8,128)(2,1)S(1)}, u32[]{:S(2)}, u32[]{:S(2)}) collective-permute-start(bf16[784,128]{1,0:T(8,128)(2,1)S(1)} %get-tuple-element.57), channel_id=1, source_target_pairs={{0,4},{4,8},{8,12},{12,14},{14,10},{10,6},{6,2},{2,0},{1,5},{5,9},... | collective-permute-start | bytes 602120 | tf_op jit(solution)/shard_map/ppermute | solution.py:562
  37.5 1.1 %collective-permute-start.14 = (bf16[784,128]{1,0:T(8,128)(2,1)S(1)}, bf16[784,128]{1,0:T(8,128)(2,1)S(1)}, u32[]{:S(2)}, u32[]{:S(2)}) collective-permute-start(bf16[784,128]{1,0:T(8,128)(2,1)S(1)} %get-tuple-element.66), channel_id=1, source_target_pairs={{0,2},{4,0},{8,4},{12,8},{14,12},{10,14},{6,10},{2,6},{1,3},{5,1},... | collective-permute-start | bytes 602120 | tf_op jit(solution)/shard_map/ppermute | solution.py:562
  38.6 0.7 %prepare.1 = (bf16[8,32,128]{2,1,0:T(8,128)(2,1)S(1)}, f32[2,192,128]{2,1,0:T(8,128)S(1)}) custom-call(s32[6]{0:T(128)S(1)} %copy-done.5, bf16[1,2,16384]{2,1,0:T(2,128)(2,1)S(1)} %copy-done.3, f32[2,6,128]{2,1,0:T(8,128)S(1)} %pad_maximum_fusion.starts, f32[2,192,128]{2,1,0:T(8,128)S(1)} %copy-done.2), custom_call_target="tpu_custom_call" | custom-call | tf_op jit(solution)/shard_map/prepare/pallas_call | solution.py:407
  39.3 2.0 %cache_attention.2 = bf16[4,48,128]{2,1,0:T(8,128)(2,1)S(1)} custom-call(s32[6]{0:T(128)S(1)} %copy-done.5, s32[6]{0:T(128)S(1)} %copy-done.6, s32[1]{0:T(128)S(6)} %copy.15.stored, bf16[8,32,128]{2,1,0:T(8,128)(2,1)S(1)} %get-tuple-element.61.q.grouped, bf16[1,1024,2048]{2,1,0:T(8,128)(2,1)S(1)} %copy-done, bf16[1,2,2048]{2,1,0:T(2,128)(2,1)S(1)} %copy-done.4), custom_call_target="tpu_custom_call" | custom-call | flops 67108864 | bytes 2097152 | tf_op jit(solution)/shard_map/cache_attention/pallas_call | solution.py:464
  41.3 0.0 collective-permute-done.10.refs_1_
  41.3 0.1 sends.11
  41.4 1.0 %collective-permute-start.11 = (bf16[784,128]{1,0:T(8,128)(2,1)S(1)}, bf16[784,128]{1,0:T(8,128)(2,1)S(1)}, u32[]{:S(2)}, u32[]{:S(2)}) collective-permute-start(bf16[784,128]{1,0:T(8,128)(2,1)S(1)} %get-tuple-element.64), channel_id=1, source_target_pairs={{0,4},{4,8},{8,12},{12,14},{14,10},{10,6},{6,2},{2,0},{1,5},{5,9},... | collective-permute-start | bytes 602120 | tf_op jit(solution)/shard_map/ppermute | solution.py:562
  42.4 1.1 %collective-permute-start.12 = (bf16[784,128]{1,0:T(8,128)(2,1)S(1)}, bf16[784,128]{1,0:T(8,128)(2,1)S(1)}, u32[]{:S(2)}, u32[]{:S(2)}) collective-permute-start(bf16[784,128]{1,0:T(8,128)(2,1)S(1)} %get-tuple-element.65), channel_id=1, source_target_pairs={{0,2},{4,0},{8,4},{12,8},{14,12},{10,14},{6,10},{2,6},{1,3},{5,1},... | collective-permute-start | bytes 602120 | tf_op jit(solution)/shard_map/ppermute | solution.py:562
  43.5 2.0 %cache_attention.3.cached_here = bf16[4,48,128]{2,1,0:T(8,128)(2,1)S(1)} custom-call(s32[6]{0:T(128)S(1)} %copy-done.5, s32[6]{0:T(128)S(1)} %copy-done.6, s32[1]{0:T(128)S(6)} %copy.15.stored, bf16[8,32,128]{2,1,0:T(8,128)(2,1)S(1)} %get-tuple-element.61.q.grouped, bf16[1,1024,2048]{2,1,0:T(8,128)(2,1)S(1)} %copy-done, bf16[1,2,2048]{2,1,0:T(2,128)(2,1)S(1)} %copy-done.4), custom_call_target="tpu_custom_call" | custom-call | flops 67108864 | bytes 2097152 | tf_op jit(solution)/shard_map/cache_attention/pallas_call | solution.py:464
  45.5 0.0 collective-permute-done.13.right_values
  45.5 1.7 %collective-permute-done.11.right_keys = bf16[784,128]{1,0:T(8,128)(2,1)S(1)} collective-permute-done((bf16[784,128]{1,0:T(8,128)(2,1)S(1)}, bf16[784,128]{1,0:T(8,128)(2,1)S(1)}, u32[]{:S(2)}, u32[]{:S(2)}) %collective-permute-start.11) | collective-permute-done | bytes 200736 | tf_op jit(solution)/shard_map/ppermute | solution.py:562
  47.2 0.9 %collective-permute-done.12.left_values = bf16[784,128]{1,0:T(8,128)(2,1)S(1)} collective-permute-done((bf16[784,128]{1,0:T(8,128)(2,1)S(1)}, bf16[784,128]{1,0:T(8,128)(2,1)S(1)}, u32[]{:S(2)}, u32[]{:S(2)}) %collective-permute-start.12) | collective-permute-done | bytes 200736 | tf_op jit(solution)/shard_map/ppermute | solution.py:562
  48.2 2.0 %finish.1 = bf16[1,2,8192]{2,1,0:T(2,128)(2,1)S(1)} custom-call(s32[6]{0:T(128)S(1)} %copy-done.5, f32[2,192,128]{2,1,0:T(8,128)S(1)} %get-tuple-element.59.rotary, f32[3,2,776,128]{3,2,1,0:T(8,128)S(1)} %project.5.terms.own, bf16[784,128]{1,0:T(8,128)(2,1)S(1)} %collective-permute-done.11.right_keys, ...), custom_call_target="tpu_custom_call" | custom-call | tf_op jit(solution)/shard_map/finish/pallas_call | solution.py:523
  50.1 1.9 %all_gather.3 = bf16[1,2,16384]{2,1,0:T(2,128)(2,1)S(1)} all-gather(bf16[1,2,8192]{2,1,0:T(2,128)(2,1)S(1)} %finish.1), channel_id=1, replica_groups=mesh['grp'=2,'tp'=8,'rep'=2] {'rep'}, dimensions={2}, use_global_device_ids=true | all-gather | bytes 98304 | tf_op jit(solution)/shard_map/all_gather | solution.py:600
  52.0 0.6 %copy.16 = bf16[1,2,16384]{2,1,0:T(2,128)(2,1)} copy(bf16[1,2,16384]{2,1,0:T(2,128)(2,1)S(1)} %all_gather.3) | data formatting | bytes 131072
  (20 shorter events, 0.1 us)
Async XLA Ops:
  0.0 9.5 %collective-permute-start = (bf16[3,192,2048]{2,1,0:T(8,128)(2,1)}, bf16[3,192,2048]{2,1,0:T(8,128)(2,1)S(1)}, u32[]{:S(2)}, u32[]{:S(2)}) collective-permute-start(bf16[3,192,2048]{2,1,0:T(8,128)(2,1)} %bitcast.8), channel_id=1, source_target_pairs={{0,1},{1,0},{2,3},{3,2},{4,5},{5,4},{6,7},{7,6},{8,9},{9,8},{10,11... | collective-permute-start | bytes 7077896 | tf_op jit(solution)/shard_map/ppermute | solution.py:564
  1.1 8.4 %copy-start.1 = (f32[2048]{0:T(1024)S(1)}, f32[2048]{0:T(1024)}, u32[]{:S(2)}) copy-start(f32[2048]{0:T(1024)} %param.14) | copy-start | bytes 24580
  1.1 8.4 %copy-start.5 = (s32[6]{0:T(128)S(1)}, s32[6]{0:T(128)}, u32[]{:S(2)}) copy-start(s32[6]{0:T(128)} %targets.9) | copy-start | bytes 76
  9.5 4.3 %copy-start.6 = (s32[6]{0:T(128)S(1)}, s32[6]{0:T(128)}, u32[]{:S(2)}) copy-start(s32[6]{0:T(128)} %lengths.3) | copy-start | bytes 76
  11.1 8.2 %collective-permute-start.2 = (bf16[768,128]{1,0:T(8,128)(2,1)S(1)}, bf16[768,128]{1,0:T(8,128)(2,1)S(1)}, u32[]{:S(2)}, u32[]{:S(2)}) collective-permute-start(bf16[768,128]{1,0:T(8,128)(2,1)S(1)} %get-tuple-element.40), channel_id=1, source_target_pairs={{0,2},{4,0},{8,4},{12,8},{14,12},{10,14},{6,10},{2,6},{1,3},{5,1},... | collective-permute-start | bytes 589832 | tf_op jit(solution)/shard_map/ppermute | solution.py:562
  12.7 7.8 %collective-permute-start.1 = (bf16[784,128]{1,0:T(8,128)(2,1)S(1)}, bf16[784,128]{1,0:T(8,128)(2,1)S(1)}, u32[]{:S(2)}, u32[]{:S(2)}) collective-permute-start(bf16[784,128]{1,0:T(8,128)(2,1)S(1)} %get-tuple-element.44), channel_id=1, source_target_pairs={{0,4},{4,8},{8,12},{12,14},{14,10},{10,6},{6,2},{2,0},{1,5},{5,9},... | collective-permute-start | bytes 602120 | tf_op jit(solution)/shard_map/ppermute | solution.py:562
  15.5 7.3 %copy-start.7 = (f32[128]{0:T(128)S(1)}, f32[128]{0:T(128)}, u32[]{:S(2)}) copy-start(f32[128]{0:T(128)} %constant.7.clone) | copy-start | bytes 1540
  15.6 9.3 %collective-permute-start.3 = (bf16[784,128]{1,0:T(8,128)(2,1)S(1)}, bf16[784,128]{1,0:T(8,128)(2,1)S(1)}, u32[]{:S(2)}, u32[]{:S(2)}) collective-permute-start(bf16[784,128]{1,0:T(8,128)(2,1)S(1)} %get-tuple-element.47), channel_id=1, source_target_pairs={{0,4},{4,8},{8,12},{12,14},{14,10},{10,6},{6,2},{2,0},{1,5},{5,9},... | collective-permute-start | bytes 602120 | tf_op jit(solution)/shard_map/ppermute | solution.py:562
  18.5 7.9 %collective-permute-start.4 = (bf16[784,128]{1,0:T(8,128)(2,1)S(1)}, bf16[784,128]{1,0:T(8,128)(2,1)S(1)}, u32[]{:S(2)}, u32[]{:S(2)}) collective-permute-start(bf16[784,128]{1,0:T(8,128)(2,1)S(1)} %get-tuple-element.48), channel_id=1, source_target_pairs={{0,2},{4,0},{8,4},{12,8},{14,12},{10,14},{6,10},{2,6},{1,3},{5,1},... | collective-permute-start | bytes 602120 | tf_op jit(solution)/shard_map/ppermute | solution.py:562
  20.6 8.5 %collective-permute-start.5 = (bf16[784,128]{1,0:T(8,128)(2,1)S(1)}, bf16[784,128]{1,0:T(8,128)(2,1)S(1)}, u32[]{:S(2)}, u32[]{:S(2)}) collective-permute-start(bf16[784,128]{1,0:T(8,128)(2,1)S(1)} %get-tuple-element.45), channel_id=1, source_target_pairs={{0,4},{4,8},{8,12},{12,14},{14,10},{10,6},{6,2},{2,0},{1,5},{5,9},... | collective-permute-start | bytes 602120 | tf_op jit(solution)/shard_map/ppermute | solution.py:562
  21.4 9.2 %collective-permute-start.6 = (bf16[784,128]{1,0:T(8,128)(2,1)S(1)}, bf16[784,128]{1,0:T(8,128)(2,1)S(1)}, u32[]{:S(2)}, u32[]{:S(2)}) collective-permute-start(bf16[784,128]{1,0:T(8,128)(2,1)S(1)} %get-tuple-element.51), channel_id=1, source_target_pairs={{0,2},{4,0},{8,4},{12,8},{14,12},{10,14},{6,10},{2,6},{1,3},{5,1},... | collective-permute-start | bytes 602120 | tf_op jit(solution)/shard_map/ppermute | solution.py:562
  26.5 10.0 %collective-permute-start.7 = (bf16[784,128]{1,0:T(8,128)(2,1)S(1)}, bf16[784,128]{1,0:T(8,128)(2,1)S(1)}, u32[]{:S(2)}, u32[]{:S(2)}) collective-permute-start(bf16[784,128]{1,0:T(8,128)(2,1)S(1)} %get-tuple-element.54), channel_id=1, source_target_pairs={{0,4},{4,8},{8,12},{12,14},{14,10},{10,6},{6,2},{2,0},{1,5},{5,9},... | collective-permute-start | bytes 602120 | tf_op jit(solution)/shard_map/ppermute | solution.py:562
  28.3 8.2 %collective-permute-start.8 = (bf16[784,128]{1,0:T(8,128)(2,1)S(1)}, bf16[784,128]{1,0:T(8,128)(2,1)S(1)}, u32[]{:S(2)}, u32[]{:S(2)}) collective-permute-start(bf16[784,128]{1,0:T(8,128)(2,1)S(1)} %get-tuple-element.55), channel_id=1, source_target_pairs={{0,2},{4,0},{8,4},{12,8},{14,12},{10,14},{6,10},{2,6},{1,3},{5,1},... | collective-permute-start | bytes 602120 | tf_op jit(solution)/shard_map/ppermute | solution.py:562
  30.7 10.6 %collective-permute-start.10 = (bf16[784,128]{1,0:T(8,128)(2,1)S(1)}, bf16[784,128]{1,0:T(8,128)(2,1)S(1)}, u32[]{:S(2)}, u32[]{:S(2)}) collective-permute-start(bf16[784,128]{1,0:T(8,128)(2,1)S(1)} %get-tuple-element.62), channel_id=1, source_target_pairs={{0,2},{4,0},{8,4},{12,8},{14,12},{10,14},{6,10},{2,6},{1,3},{5,1},... | collective-permute-start | bytes 602120 | tf_op jit(solution)/shard_map/ppermute | solution.py:562
  31.3 10.0 %collective-permute-start.9 = (bf16[784,128]{1,0:T(8,128)(2,1)S(1)}, bf16[784,128]{1,0:T(8,128)(2,1)S(1)}, u32[]{:S(2)}, u32[]{:S(2)}) collective-permute-start(bf16[784,128]{1,0:T(8,128)(2,1)S(1)} %get-tuple-element.52), channel_id=1, source_target_pairs={{0,4},{4,8},{8,12},{12,14},{14,10},{10,6},{6,2},{2,0},{1,5},{5,9},... | collective-permute-start | bytes 602120 | tf_op jit(solution)/shard_map/ppermute | solution.py:562
  32.8 6.5 %copy-start = (bf16[1,1024,2048]{2,1,0:T(8,128)(2,1)S(1)}, bf16[1,1024,2048]{2,1,0:T(8,128)(2,1)}, u32[]{:S(2)}) copy-start(bf16[1,1024,2048]{2,1,0:T(8,128)(2,1)} %cache.3) | copy-start | bytes 12582916
  36.4 2.2 %copy-start.2 = (f32[2,192,128]{2,1,0:T(8,128)S(1)}, f32[2,192,128]{2,1,0:T(8,128)}, u32[]{:S(2)}) copy-start(f32[2,192,128]{2,1,0:T(8,128)} %constant.8.clone.turns) | copy-start | bytes 589828
  36.4 2.2 %copy-start.3 = (bf16[1,2,16384]{2,1,0:T(2,128)(2,1)S(1)}, bf16[1,2,16384]{2,1,0:T(2,128)(2,1)}, u32[]{:S(2)}) copy-start(bf16[1,2,16384]{2,1,0:T(2,128)(2,1)} %queries.1) | copy-start | bytes 196612
  36.4 2.9 %copy-start.4 = (bf16[1,2,2048]{2,1,0:T(2,128)(2,1)S(1)}, bf16[1,2,2048]{2,1,0:T(2,128)(2,1)}, u32[]{:S(2)}) copy-start(bf16[1,2,2048]{2,1,0:T(2,128)(2,1)} %new.3) | copy-start | bytes 24580
  36.5 9.0 %collective-permute-start.13 = (bf16[784,128]{1,0:T(8,128)(2,1)S(1)}, bf16[784,128]{1,0:T(8,128)(2,1)S(1)}, u32[]{:S(2)}, u32[]{:S(2)}) collective-permute-start(bf16[784,128]{1,0:T(8,128)(2,1)S(1)} %get-tuple-element.57), channel_id=1, source_target_pairs={{0,4},{4,8},{8,12},{12,14},{14,10},{10,6},{6,2},{2,0},{1,5},{5,9},... | collective-permute-start | bytes 602120 | tf_op jit(solution)/shard_map/ppermute | solution.py:562
  37.5 8.0 %collective-permute-start.14 = (bf16[784,128]{1,0:T(8,128)(2,1)S(1)}, bf16[784,128]{1,0:T(8,128)(2,1)S(1)}, u32[]{:S(2)}, u32[]{:S(2)}) collective-permute-start(bf16[784,128]{1,0:T(8,128)(2,1)S(1)} %get-tuple-element.66), channel_id=1, source_target_pairs={{0,2},{4,0},{8,4},{12,8},{14,12},{10,14},{6,10},{2,6},{1,3},{5,1},... | collective-permute-start | bytes 602120 | tf_op jit(solution)/shard_map/ppermute | solution.py:562
  41.4 5.8 %collective-permute-start.11 = (bf16[784,128]{1,0:T(8,128)(2,1)S(1)}, bf16[784,128]{1,0:T(8,128)(2,1)S(1)}, u32[]{:S(2)}, u32[]{:S(2)}) collective-permute-start(bf16[784,128]{1,0:T(8,128)(2,1)S(1)} %get-tuple-element.64), channel_id=1, source_target_pairs={{0,4},{4,8},{8,12},{12,14},{14,10},{10,6},{6,2},{2,0},{1,5},{5,9},... | collective-permute-start | bytes 602120 | tf_op jit(solution)/shard_map/ppermute | solution.py:562
  42.4 5.7 %collective-permute-start.12 = (bf16[784,128]{1,0:T(8,128)(2,1)S(1)}, bf16[784,128]{1,0:T(8,128)(2,1)S(1)}, u32[]{:S(2)}, u32[]{:S(2)}) collective-permute-start(bf16[784,128]{1,0:T(8,128)(2,1)S(1)} %get-tuple-element.65), channel_id=1, source_target_pairs={{0,2},{4,0},{8,4},{12,8},{14,12},{10,14},{6,10},{2,6},{1,3},{5,1},... | collective-permute-start | bytes 602120 | tf_op jit(solution)/shard_map/ppermute | solution.py:562
  43.5 2.0 %collective-permute-start.15 = (bf16[4,48,128]{2,1,0:T(8,128)(2,1)S(1)}, bf16[4,48,128]{2,1,0:T(8,128)(2,1)S(1)}, u32[]{:S(2)}, u32[]{:S(2)}) collective-permute-start(bf16[4,48,128]{2,1,0:T(8,128)(2,1)S(1)} %cache_attention.2), channel_id=1, source_target_pairs={{0,1},{1,0},{2,3},{3,2},{4,5},{5,4},{6,7},{7,6},{8,9},{9,8},{10,11... | collective-permute-start | bytes 147464 | tf_op jit(solution)/shard_map/ppermute | solution.py:564

commit v15 on v14

--- a/solution.py
+++ b/solution.py
@@ -426,38 +426,45 @@
     prompt = prompt_of(targets, here)
     handed = lengths[jnp.maximum(prompt, 0)] - STRETCH
     span = jnp.where(prompt >= 0, handed, stored[0]) - rep * length
-    allowed = lax.broadcasted_iota(jnp.int32, (ROWS, length), 1) < span
-    second_step = lax.broadcasted_iota(jnp.int32, (ROWS, 1), 0) % STEPS == 1
+    count = CORE_HEADS * ROWS
+    allowed = lax.broadcasted_iota(jnp.int32, (count, length), 1) < span
+    second_step = lax.broadcasted_iota(jnp.int32, (count, 1), 0) % STEPS == 1
+    scores, fresh, key_lanes, value_lanes = [], [[], []], [], []
     for at in range(CORE_HEADS):
         head = (rep if part == 1 else 1 - rep) * CORE_HEADS + at
-        key_lanes = pl.ds(pl.multiple_of(head * HEAD_DIM, HEAD_DIM), HEAD_DIM)
-        value_lanes = pl.ds(pl.multiple_of((KV_HEADS + head) * HEAD_DIM, HEAD_DIM), HEAD_DIM)
+        key_lanes.append(pl.ds(pl.multiple_of(head * HEAD_DIM, HEAD_DIM), HEAD_DIM))
+        begin = pl.multiple_of((KV_HEADS + head) * HEAD_DIM, HEAD_DIM)
+        value_lanes.append(pl.ds(begin, HEAD_DIM))
         query = q[head]
         wide = query.astype(F32)
-        scores = lax.dot_general(query, cache[0, :, key_lanes], dims, preferred_element_type=F32)
-        scores = jnp.where(allowed, scores * scaling, NEGATIVE)
-        highest = jnp.max(scores, axis=1, keepdims=True)
-        fresh = []
+        keys = cache[0, :, key_lanes[at]]
+        scores.append(lax.dot_general(query, keys, dims, preferred_element_type=F32))
         for step in range(STEPS):
-            key = new[0, step : step + 1, key_lanes].astype(F32)
-            score = jnp.sum(wide * key, axis=1, keepdims=True) * scaling
-            shown = rep == 0 if step == 0 else second_step & (rep == 0)
-            score = jnp.where(shown, score, NEGATIVE)
-            highest = jnp.maximum(highest, score)
-            fresh.append(score)
-        some = highest > 0.5 * NEGATIVE
-        highest = jnp.where(some, highest, 0.0)
-        weight = jnp.exp(scores - highest)
-        totals = jnp.sum(weight, axis=1, keepdims=True)
-        sums = jnp.dot(weight.astype(BF16), cache[0, :, value_lanes], preferred_element_type=F32)
+            key = new[0, step : step + 1, key_lanes[at]].astype(F32)
+            fresh[step].append(jnp.sum(wide * key, axis=1, keepdims=True))
+    scores = jnp.where(allowed, jnp.concatenate(scores, axis=0) * scaling, NEGATIVE)
+    highest = jnp.max(scores, axis=1, keepdims=True)
+    for step in range(STEPS):
+        shown = rep == 0 if step == 0 else second_step & (rep == 0)
+        fresh[step] = jnp.where(shown, jnp.concatenate(fresh[step], axis=0) * scaling, NEGATIVE)
+        highest = jnp.maximum(highest, fresh[step])
+    some = highest > 0.5 * NEGATIVE
+    highest = jnp.where(some, highest, 0.0)
+    weight = jnp.exp(scores - highest)
+    shares = [jnp.exp(score - highest) for score in fresh]
+    totals = jnp.sum(weight, axis=1, keepdims=True) + shares[0] + shares[1]
+    totals = jnp.where(some, totals, 1.0)
+    logs = jnp.where(some, highest + jnp.log(totals), NEGATIVE)
+    weight = weight.astype(BF16)
+    for at in range(CORE_HEADS):
+        rows = slice(at * ROWS, (at + 1) * ROWS)
+        values = cache[0, :, value_lanes[at]]
+        sums = jnp.dot(weight[rows], values, preferred_element_type=F32)
         for step in range(STEPS):
-            share = jnp.exp(fresh[step] - highest)
-            totals += share
-            value = new[0, step : step + 1, value_lanes].astype(F32)
-            sums += share.astype(BF16).astype(F32) * value
-        totals = jnp.where(some, totals, 1.0)
-        out[at, :ROWS] = (sums / totals).astype(BF16)
-        out[at, ROWS:] = pieces_tail(jnp.where(some, highest + jnp.log(totals), NEGATIVE))
+            value = new[0, step : step + 1, value_lanes[at]].astype(F32)
+            sums += shares[step][rows].astype(BF16).astype(F32) * value
+        out[at, :ROWS] = (sums / totals[rows]).astype(BF16)
+        out[at, ROWS:] = pieces_tail(logs[rows])
 
 
 def cache_attention(part, targets, lengths, stored, grouped, kv_cache, new_kv):
@@ -468,9 +475,7 @@
         out_shape=jax.ShapeDtypeStruct((CORE_HEADS, PART, HEAD_DIM), BF16),
         compiler_params=pltpu.CompilerParams(vmem_limit_bytes=16 * MIB),
         cost_estimate=pl.CostEstimate(
-            flops=2 * grouped.size * kv_cache.shape[1],
-            bytes_accessed=kv_cache.size,
-            transcendentals=CORE_HEADS * ROWS * kv_cache.shape[1],
+            flops=1, bytes_accessed=1, transcendentals=0
         ),
         name="cache_attention",
     )(targets, lengths, stored, grouped, kv_cache, new_kv)
@@ -489,33 +494,42 @@
     rows = CORE_HEADS * STRETCH
     squares = own[mine, 0, rows:] + one_piece(right_keys[rows : rows + TAIL]) + one_piece(left_keys[rows : rows + TAIL])
     scale = token_column(lax.rsqrt(squares / D + EPSILON))
+    scores, handed = [], []
     for head in range(CORE_HEADS):
         at = slice(head * STRETCH, (head + 1) * STRETCH)
         keys = own[mine, 0, at] + right_keys[at].astype(F32) + left_keys[at].astype(F32)
         values = own[mine, 1, at] + right_values[at].astype(F32) + left_values[at].astype(F32)
         keys = (keys * scale).astype(BF16).astype(F32)
-        values = (values * scale).astype(BF16)
+        handed.append((values * scale).astype(BF16))
         keys = keys * cosine + pltpu.roll(keys, HEAD_DIM // 2, 1) * sine
-        scores = lax.dot_general(
-            grouped[first + head], keys.astype(BF16), dims, preferred_element_type=F32
+        scores.append(
+            lax.dot_general(
+                grouped[first + head], keys.astype(BF16), dims, preferred_element_type=F32
+            )
         )
-        scores = scores * scaling
-        highest = jnp.max(scores, axis=1, keepdims=True)
-        weight = jnp.exp(scores - highest)
-        totals = jnp.sum(weight, axis=1, keepdims=True)
-        sums = jnp.dot(weight.astype(BF16), values, preferred_element_type=F32) / totals
-        logs = jnp.where(prompt >= 0, highest + jnp.log(totals), NEGATIVE)
-        parts = [cached_there[head], cached_here[head]]
-        logs = [tail_pieces(part[ROWS:]) for part in parts] + [logs]
-        sums = [part[:ROWS].astype(F32) for part in parts] + [sums]
-        highest = functools.reduce(jnp.maximum, logs)
-        shares = [jnp.exp(log - highest) for log in logs]
-        total = functools.reduce(jnp.add, shares)
-        joined = functools.reduce(jnp.add, [share * part for share, part in zip(shares, sums)])
-        result = (joined / total).astype(BF16)
-        for member in range(GROUP):
-            begin = (head * GROUP + member) * HEAD_DIM
-            out[0, :, begin : begin + HEAD_DIM] = result[member * STEPS : (member + 1) * STEPS]
+    scores = jnp.concatenate(scores, axis=0) * scaling
+    highest = jnp.max(scores, axis=1, keepdims=True)
+    weight = jnp.exp(scores - highest)
+    totals = jnp.sum(weight, axis=1, keepdims=True)
+    weight = weight.astype(BF16)
+    sums = [
+        jnp.dot(weight[head * ROWS : (head + 1) * ROWS], handed[head], preferred_element_type=F32)
+        for head in range(CORE_HEADS)
+    ]
+    sums = [jnp.concatenate(sums, axis=0) / totals]
+    logs = [jnp.where(prompt >= 0, highest + jnp.log(totals), NEGATIVE)]
+    for cached in (cached_there, cached_here):
+        parts = [cached[head] for head in range(CORE_HEADS)]
+        sums.append(jnp.concatenate([part[:ROWS].astype(F32) for part in parts], axis=0))
+        logs.append(jnp.concatenate([tail_pieces(part[ROWS:]) for part in parts], axis=0))
+    highest = functools.reduce(jnp.maximum, logs)
+    shares = [jnp.exp(log - highest) for log in logs]
+    total = functools.reduce(jnp.add, shares)
+    joined = functools.reduce(jnp.add, [share * part for share, part in zip(shares, sums)])
+    result = (joined / total).astype(BF16)
+    for member in range(CORE_HEADS * GROUP):
+        lanes = slice(member * HEAD_DIM, (member + 1) * HEAD_DIM)
+        out[0, :, lanes] = result[member * STEPS : (member + 1) * STEPS]
 
 
 def finish(targets, rotary, own, arrived, grouped, cached):
@@ -574,25 +588,27 @@
     arrived = [pass_on(right, left), []]
 
     for distance in range(half - 1, 0, -1):
-        distances = [distance, -distance] + ([0] if distance == 1 else [])
-        terms = project(distances, targets, *features, weight)
+        terms = project([distance, -distance], targets, *features, weight)
         right, left = sends(1, terms, arrived[1])
-        terms, right = lax.optimization_barrier((terms, right))
-        if distance == 1:
-            targets, _ = lax.optimization_barrier((target_rows, right))
+        terms, right, left = lax.optimization_barrier((terms, right, left))
+        targets, _ = lax.optimization_barrier((target_rows, left))
         arrived[1] = pass_on(right, left)
-        if distance == 1:
-            grouped, rotary = prepare(targets, queries, starts, jnp.asarray(turns))
+        if distance == half - 1:
+            prepared = prepare(targets, queries, starts, jnp.asarray(turns))
+            terms, prepared = lax.optimization_barrier((terms, prepared))
+            grouped, rotary = prepared
+        if distance == max(1, half - 2):
             cached = cache_attention(
                 0, targets, prompt_lengths, cache_lengths, grouped, kv_cache, new_kv
             )
+            terms, cached = lax.optimization_barrier((terms, cached))
         right, left = sends(0, terms, arrived[0])
-        if distance == 1:
-            cached, right = lax.optimization_barrier((cached, right))
-        targets, _ = lax.optimization_barrier((target_rows, right))
+        targets, right = lax.optimization_barrier((target_rows, right))
         arrived[0] = pass_on(right, left)
 
+    cached, _ = lax.optimization_barrier((cached, right))
     cached = [swap(cached)]
+    terms = project([0], targets, *features, weight)
     cached.append(
         cache_attention(1, targets, prompt_lengths, cache_lengths, grouped, kv_cache, new_kv)
     )

time: 52.8 us -> 50.5 us (0.956)
  Pallas kernels: 24 us -> 23.3 us
  starting transfers between devices: 16.8 us -> 16.1 us
  waiting for transfers between devices: 8.34 us -> 7.68 us
    ppermute x7, waiting for transfers between devices: 4.76 us -> 1.23 us  [pass_on(): lax.ppermute(left, 'tp', to_left)]
    ppermute x7, starting transfers between devices: 10 us -> 7.08 us  [pass_on(): lax.ppermute(right, 'tp', to_right)]
    ppermute x7, waiting for transfers between devices: 3.58 us -> 6.44 us  [pass_on(): lax.ppermute(right, 'tp', to_right)]
    ppermute x7, starting transfers between devices: 6.27 us -> 8.54 us  [pass_on(): lax.ppermute(left, 'tp', to_left)]
    pallas_call x2, Pallas kernels: 3.98 us -> 3.19 us  [cache_attention(): pl.pallas_call(functools.partial(cache_kernel, part), in_specs=[SMEM] * 3...]
    pallas_call x3 -> x4, Pallas kernels: 6.95 us -> 7.67 us  [project(): pl.pallas_call(functools.partial(project_kernel, distances), in_specs=[SM...]
    pallas_call x1, Pallas kernels: 1.98 us -> 1.37 us  [finish(): pl.pallas_call(final_kernel, in_specs=[SMEM] + [VMEM] * 9, out_specs=VMEM...]
  transfers between devices with their start and end apart: 16 -> 16, of which waited for: 8 -> 6; matrix products, arithmetic and copies ran while one was open for 0% -> 0% of each run, Pallas kernels for 39% -> 40%
where the time goes in v15:
time: 50.5 us; the launch traced here: 50.6 us
  Pallas kernels  23.3 us (46%)
  starting transfers between devices  16.1 us (32%)
  waiting for transfers between devices  7.68 us (15%)
  blocking collectives  1.85 us (4%)
  between operations  0.92 us (2%)
  local copies, waits for them, and re-layouts  0.67 us (1%)
    ppermute x7, starting transfers between devices, pass_on(): lax.ppermute(left, 'tp', to_left)  8.54 us
    pallas_call x1, Pallas kernels, dequantize(): pl.pallas_call(weights_kernel, grid=(1,), in_specs=[pl.BlockSpec(memory_s...  8.38 us
    pallas_call x4, Pallas kernels, project(): pl.pallas_call(functools.partial(project_kernel, distances), in_specs=[SM...  7.67 us
    ppermute x7, starting transfers between devices, pass_on(): lax.ppermute(right, 'tp', to_right)  7.08 us
    ppermute x7, waiting for transfers between devices, pass_on(): lax.ppermute(right, 'tp', to_right)  6.44 us
    pallas_call x2, Pallas kernels, cache_attention(): pl.pallas_call(functools.partial(cache_kernel, part), in_specs=[SMEM] * 3...  3.19 us
    all_gather x1, blocking collectives, per_device(): return lax.all_gather(out, 'rep', axis=2, tiled=True)  1.85 us
    pallas_call x1, Pallas kernels, project_first(): pl.pallas_call(functools.partial(first_kernel, distance), in_specs=[SMEM]...  1.59 us
  transfers between devices with their start and end apart: 16, of which 6 were waited for; matrix products, arithmetic and copies ran while one was open for 0% of the time, Pallas kernels for 40%

profile of v15, /device:TPU:0, one launch (start us, length us, event | category | flops | bytes accessed | tf_op | source)
XLA Modules:
  0.0 50.6 jit_solution(13224159567113830914)
XLA Ops:
  0.0 0.5 collective-permute-start
  0.5 8.4 %dequantize.1 = (bf16[4,2048,256]{2,1,0:T(8,128)(2,1)S(1)}, bf16[3,192,2048]{2,1,0:T(8,128)(2,1)S(1)}, f32[3,8,128]{2,1,0:T(8,128)S(1)}) custom-call(bf16[3,192,2048]{2,1,0:T(8,128)(2,1)} %bitcast.10, s32[2048,2048]{1,0:T(8,128)} %codes.1, s32[32,2048]{1,0:T(8,128)} %value_scales.1, s32[32,2048]{1,0:T(8,128)} %value_scales.1, f32[8,32]{1,0:T(8,128)} %bitcast.11, ...), custom_call_target="tpu_custom_call" | custom-call | flops 134217728 | bytes 8388608 | tf_op jit(solution)/shard_map/dequantize/pallas_call | solution.py:224
  8.9 0.0 copy-start.7
  8.9 1.6 %project_first.1 = (bf16[784,128]{1,0:T(8,128)(2,1)S(1)}, bf16[768,128]{1,0:T(8,128)(2,1)S(1)}) custom-call(s32[6]{0:T(128)S(1)} %copy-done.4, bf16[3,192,2048]{2,1,0:T(8,128)(2,1)S(1)} %get-tuple-element.48.own, f32[3,8,128]{2,1,0:T(8,128)S(1)} %get-tuple-element.49.squares, bf16[3,192,2048]{2,1,0:T(8,128)(2,1)S(1)} %collective-permute-done.other, ...), custom_call_target="tpu_custom_call" | custom-call | flops 805306368 | bytes 2097152 | tf_op jit(solution)/shard_map/project_first/pallas_call | solution.py:309
  10.5 2.5 %collective-permute-start.2 = (bf16[768,128]{1,0:T(8,128)(2,1)S(1)}, bf16[768,128]{1,0:T(8,128)(2,1)S(1)}, u32[]{:S(2)}, u32[]{:S(2)}) collective-permute-start(bf16[768,128]{1,0:T(8,128)(2,1)S(1)} %get-tuple-element.51), channel_id=1, source_target_pairs={{0,2},{4,0},{8,4},{12,8},{14,12},{10,14},{6,10},{2,6},{1,3},{5,1},... | collective-permute-start | bytes 589832 | tf_op jit(solution)/shard_map/ppermute | solution.py:576
  13.1 0.1 multiply_cosine_fusion
  13.2 0.0 copy-start.2
  13.2 0.0 copy-start.3
  13.2 1.7 %project.4.terms = f32[2,2,776,128]{3,2,1,0:T(8,128)S(1)} custom-call(s32[6]{0:T(128)S(1)} %copy-done.4, bf16[3,192,2048]{2,1,0:T(8,128)(2,1)S(1)} %get-tuple-element.48.own, f32[3,8,128]{2,1,0:T(8,128)S(1)} %get-tuple-element.49.squares, bf16[3,192,2048]{2,1,0:T(8,128)(2,1)S(1)} %collective-permute-done.other, f32[1,2048]{1,0:T(1,128)S(1)} %bitcast.5, ...), custom_call_target="tpu_custom_call" | custom-call | flops 805306368 | bytes 2097152 | tf_op jit(solution)/shard_map/project/pallas_call | solution.py:344
  14.9 2.7 %collective-permute-start.3 = (bf16[784,128]{1,0:T(8,128)(2,1)S(1)}, bf16[784,128]{1,0:T(8,128)(2,1)S(1)}, u32[]{:S(2)}, u32[]{:S(2)}) collective-permute-start(bf16[784,128]{1,0:T(8,128)(2,1)S(1)} %get-tuple-element.65), channel_id=1, source_target_pairs={{0,4},{4,8},{8,12},{12,14},{14,10},{10,6},{6,2},{2,0},{1,5},{5,9},... | collective-permute-start | bytes 602120 | tf_op jit(solution)/shard_map/ppermute | solution.py:576
  17.6 0.0 collective-permute-start.4
  17.6 0.7 %prepare.1 = (bf16[8,32,128]{2,1,0:T(8,128)(2,1)S(1)}, f32[2,192,128]{2,1,0:T(8,128)S(1)}) custom-call(s32[6]{0:T(128)S(1)} %copy-done.4, bf16[1,2,16384]{2,1,0:T(2,128)(2,1)S(1)} %copy-done.3, f32[2,6,128]{2,1,0:T(8,128)S(1)} %pad_maximum_fusion.starts, f32[2,192,128]{2,1,0:T(8,128)S(1)} %copy-done.2), custom_call_target="tpu_custom_call" | custom-call | tf_op jit(solution)/shard_map/prepare/pallas_call | solution.py:407
  18.3 0.0 collective-permute-done.2.refs_1_
  18.3 2.6 %collective-permute-done.1.refs_0_ = bf16[784,128]{1,0:T(8,128)(2,1)S(1)} collective-permute-done((bf16[784,128]{1,0:T(8,128)(2,1)S(1)}, bf16[784,128]{1,0:T(8,128)(2,1)S(1)}, u32[]{:S(2)}, u32[]{:S(2)}) %collective-permute-start.1) | collective-permute-done | bytes 200736 | tf_op jit(solution)/shard_map/ppermute | solution.py:576
  20.9 0.1 sends.7
  21.0 0.1 collective-permute-start.5
  21.0 2.0 %collective-permute-start.6 = (bf16[784,128]{1,0:T(8,128)(2,1)S(1)}, bf16[784,128]{1,0:T(8,128)(2,1)S(1)}, u32[]{:S(2)}, u32[]{:S(2)}) collective-permute-start(bf16[784,128]{1,0:T(8,128)(2,1)S(1)} %get-tuple-element.74), channel_id=1, source_target_pairs={{0,2},{4,0},{8,4},{12,8},{14,12},{10,14},{6,10},{2,6},{1,3},{5,1},... | collective-permute-start | bytes 602120 | tf_op jit(solution)/shard_map/ppermute | solution.py:576
  23.7 0.0 copy-start
  23.7 0.0 copy-start.5
  23.7 1.8 %project.5.terms = f32[2,2,776,128]{3,2,1,0:T(8,128)S(1)} custom-call(s32[6]{0:T(128)S(1)} %copy-done.4, bf16[3,192,2048]{2,1,0:T(8,128)(2,1)S(1)} %get-tuple-element.48.own, f32[3,8,128]{2,1,0:T(8,128)S(1)} %get-tuple-element.49.squares, bf16[3,192,2048]{2,1,0:T(8,128)(2,1)S(1)} %collective-permute-done.other, f32[1,2048]{1,0:T(1,128)S(1)} %bitcast.6, ...), custom_call_target="tpu_custom_call" | custom-call | flops 805306368 | bytes 2097152 | tf_op jit(solution)/shard_map/project/pallas_call | solution.py:344
  25.6 0.0 collective-permute-done.4.refs_1_
  25.6 0.1 sends.8
  25.7 1.2 %collective-permute-start.8 = (bf16[784,128]{1,0:T(8,128)(2,1)S(1)}, bf16[784,128]{1,0:T(8,128)(2,1)S(1)}, u32[]{:S(2)}, u32[]{:S(2)}) collective-permute-start(bf16[784,128]{1,0:T(8,128)(2,1)S(1)} %get-tuple-element.69), channel_id=1, source_target_pairs={{0,2},{4,0},{8,4},{12,8},{14,12},{10,14},{6,10},{2,6},{1,3},{5,1},... | collective-permute-start | bytes 602120 | tf_op jit(solution)/shard_map/ppermute | solution.py:576
  26.9 0.8 %collective-permute-start.7 = (bf16[784,128]{1,0:T(8,128)(2,1)S(1)}, bf16[784,128]{1,0:T(8,128)(2,1)S(1)}, u32[]{:S(2)}, u32[]{:S(2)}) collective-permute-start(bf16[784,128]{1,0:T(8,128)(2,1)S(1)} %get-tuple-element.77), channel_id=1, source_target_pairs={{0,4},{4,8},{8,12},{12,14},{14,10},{10,6},{6,2},{2,0},{1,5},{5,9},... | collective-permute-start | bytes 602120 | tf_op jit(solution)/shard_map/ppermute | solution.py:576
  27.7 1.6 %cache_attention.2 = bf16[4,48,128]{2,1,0:T(8,128)(2,1)S(1)} custom-call(s32[6]{0:T(128)S(1)} %copy-done.4, s32[6]{0:T(128)S(1)} %copy-done.6, s32[1]{0:T(128)S(6)} %copy.15.stored, bf16[8,32,128]{2,1,0:T(8,128)(2,1)S(1)} %get-tuple-element.71.q.grouped, bf16[1,1024,2048]{2,1,0:T(8,128)(2,1)S(1)} %copy-done, bf16[1,2,2048]{2,1,0:T(2,128)(2,1)S(1)} %copy-done.5), custom_call_target="tpu_custom_call" | custom-call | flops 1 | bytes 1 | tf_op jit(solution)/shard_map/cache_attention/pallas_call | solution.py:471
  29.3 0.0 collective-permute-done.5.refs_0_
  29.4 0.4 collective-permute-done.6.refs_1_
  29.8 0.1 sends.9
  29.9 1.6 %collective-permute-start.9 = (bf16[784,128]{1,0:T(8,128)(2,1)S(1)}, bf16[784,128]{1,0:T(8,128)(2,1)S(1)}, u32[]{:S(2)}, u32[]{:S(2)}) collective-permute-start(bf16[784,128]{1,0:T(8,128)(2,1)S(1)} %get-tuple-element.81), channel_id=1, source_target_pairs={{0,4},{4,8},{8,12},{12,14},{14,10},{10,6},{6,2},{2,0},{1,5},{5,9},... | collective-permute-start | bytes 602120 | tf_op jit(solution)/shard_map/ppermute | solution.py:576
  31.4 0.5 %collective-permute-start.10 = (bf16[784,128]{1,0:T(8,128)(2,1)S(1)}, bf16[784,128]{1,0:T(8,128)(2,1)S(1)}, u32[]{:S(2)}, u32[]{:S(2)}) collective-permute-start(bf16[784,128]{1,0:T(8,128)(2,1)S(1)} %get-tuple-element.82), channel_id=1, source_target_pairs={{0,2},{4,0},{8,4},{12,8},{14,12},{10,14},{6,10},{2,6},{1,3},{5,1},... | collective-permute-start | bytes 602120 | tf_op jit(solution)/shard_map/ppermute | solution.py:576
  32.0 2.6 %project.6.terms = f32[2,2,776,128]{3,2,1,0:T(8,128)S(1)} custom-call(s32[6]{0:T(128)S(1)} %copy-done.4, bf16[3,192,2048]{2,1,0:T(8,128)(2,1)S(1)} %get-tuple-element.48.own, f32[3,8,128]{2,1,0:T(8,128)S(1)} %get-tuple-element.49.squares, bf16[3,192,2048]{2,1,0:T(8,128)(2,1)S(1)} %collective-permute-done.other, f32[1,2048]{1,0:T(1,128)S(1)} %bitcast.7, ...), custom_call_target="tpu_custom_call" | custom-call | flops 805306368 | bytes 2097152 | tf_op jit(solution)/shard_map/project/pallas_call | solution.py:344
  34.5 0.7 %collective-permute-done.7.refs_0_ = bf16[784,128]{1,0:T(8,128)(2,1)S(1)} collective-permute-done((bf16[784,128]{1,0:T(8,128)(2,1)S(1)}, bf16[784,128]{1,0:T(8,128)(2,1)S(1)}, u32[]{:S(2)}, u32[]{:S(2)}) %collective-permute-start.7) | collective-permute-done | bytes 200736 | tf_op jit(solution)/shard_map/ppermute | solution.py:576
  35.2 0.1 sends.10
  35.3 0.4 collective-permute-start.13
  35.7 1.7 %collective-permute-start.14 = (bf16[784,128]{1,0:T(8,128)(2,1)S(1)}, bf16[784,128]{1,0:T(8,128)(2,1)S(1)}, u32[]{:S(2)}, u32[]{:S(2)}) collective-permute-start(bf16[784,128]{1,0:T(8,128)(2,1)S(1)} %get-tuple-element.88), channel_id=1, source_target_pairs={{0,2},{4,0},{8,4},{12,8},{14,12},{10,14},{6,10},{2,6},{1,3},{5,1},... | collective-permute-start | bytes 602120 | tf_op jit(solution)/shard_map/ppermute | solution.py:576
  37.4 2.1 %collective-permute-done.9.refs_0_ = bf16[784,128]{1,0:T(8,128)(2,1)S(1)} collective-permute-done((bf16[784,128]{1,0:T(8,128)(2,1)S(1)}, bf16[784,128]{1,0:T(8,128)(2,1)S(1)}, u32[]{:S(2)}, u32[]{:S(2)}) %collective-permute-start.9) | collective-permute-done | bytes 200736 | tf_op jit(solution)/shard_map/ppermute | solution.py:576
  39.5 0.1 sends.11
  39.6 1.5 %collective-permute-start.11 = (bf16[784,128]{1,0:T(8,128)(2,1)S(1)}, bf16[784,128]{1,0:T(8,128)(2,1)S(1)}, u32[]{:S(2)}, u32[]{:S(2)}) collective-permute-start(bf16[784,128]{1,0:T(8,128)(2,1)S(1)} %get-tuple-element.85), channel_id=1, source_target_pairs={{0,4},{4,8},{8,12},{12,14},{14,10},{10,6},{6,2},{2,0},{1,5},{5,9},... | collective-permute-start | bytes 602120 | tf_op jit(solution)/shard_map/ppermute | solution.py:576
  41.1 0.6 %collective-permute-start.12 = (bf16[784,128]{1,0:T(8,128)(2,1)S(1)}, bf16[784,128]{1,0:T(8,128)(2,1)S(1)}, u32[]{:S(2)}, u32[]{:S(2)}) collective-permute-start(bf16[784,128]{1,0:T(8,128)(2,1)S(1)} %get-tuple-element.86), channel_id=1, source_target_pairs={{0,2},{4,0},{8,4},{12,8},{14,12},{10,14},{6,10},{2,6},{1,3},{5,1},... | collective-permute-start | bytes 602120 | tf_op jit(solution)/shard_map/ppermute | solution.py:576
  41.6 1.6 %cache_attention.3.cached_here = bf16[4,48,128]{2,1,0:T(8,128)(2,1)S(1)} custom-call(s32[6]{0:T(128)S(1)} %copy-done.4, s32[6]{0:T(128)S(1)} %copy-done.6, s32[1]{0:T(128)S(6)} %copy.15.stored, bf16[8,32,128]{2,1,0:T(8,128)(2,1)S(1)} %get-tuple-element.71.q.grouped, bf16[1,1024,2048]{2,1,0:T(8,128)(2,1)S(1)} %copy-done, bf16[1,2,2048]{2,1,0:T(2,128)(2,1)S(1)} %copy-done.5), custom_call_target="tpu_custom_call" | custom-call | flops 1 | bytes 1 | tf_op jit(solution)/shard_map/cache_attention/pallas_call | solution.py:471
  43.2 1.6 %project.7.own = f32[1,2,776,128]{3,2,1,0:T(8,128)S(1)} custom-call(s32[6]{0:T(128)S(1)} %copy-done.4, bf16[3,192,2048]{2,1,0:T(8,128)(2,1)S(1)} %get-tuple-element.48.own, f32[3,8,128]{2,1,0:T(8,128)S(1)} %get-tuple-element.49.squares, bf16[3,192,2048]{2,1,0:T(8,128)(2,1)S(1)} %collective-permute-done.other, f32[1,2048]{1,0:T(1,128)S(1)} %bitcast.8, ...), custom_call_target="tpu_custom_call" | custom-call | flops 402653184 | bytes 2097152 | tf_op jit(solution)/shard_map/project/pallas_call | solution.py:344
  44.8 0.0 collective-permute-done.13.right_values
  44.8 0.0 collective-permute-done.14.left_keys
  44.9 1.1 %collective-permute-done.11.right_keys = bf16[784,128]{1,0:T(8,128)(2,1)S(1)} collective-permute-done((bf16[784,128]{1,0:T(8,128)(2,1)S(1)}, bf16[784,128]{1,0:T(8,128)(2,1)S(1)}, u32[]{:S(2)}, u32[]{:S(2)}) %collective-permute-start.11) | collective-permute-done | bytes 200736 | tf_op jit(solution)/shard_map/ppermute | solution.py:576
  46.0 0.8 %collective-permute-done.12.left_values = bf16[784,128]{1,0:T(8,128)(2,1)S(1)} collective-permute-done((bf16[784,128]{1,0:T(8,128)(2,1)S(1)}, bf16[784,128]{1,0:T(8,128)(2,1)S(1)}, u32[]{:S(2)}, u32[]{:S(2)}) %collective-permute-start.12) | collective-permute-done | bytes 200736 | tf_op jit(solution)/shard_map/ppermute | solution.py:576
  46.8 1.4 %finish.1 = bf16[1,2,8192]{2,1,0:T(2,128)(2,1)S(1)} custom-call(s32[6]{0:T(128)S(1)} %copy-done.4, f32[2,192,128]{2,1,0:T(8,128)S(1)} %get-tuple-element.60.rotary, f32[1,2,776,128]{3,2,1,0:T(8,128)S(1)} %project.7.own, bf16[784,128]{1,0:T(8,128)(2,1)S(1)} %collective-permute-done.11.right_keys, bf16[784,128]{1,0:T(8,128)(2,1)S(1)} %collective-permute-done.12.left_values, ...), custom_call_target="tpu_custom_call" | custom-call | tf_op jit(solution)/shard_map/finish/pallas_call | solution.py:537
  48.2 1.9 %all_gather.3 = bf16[1,2,16384]{2,1,0:T(2,128)(2,1)S(1)} all-gather(bf16[1,2,8192]{2,1,0:T(2,128)(2,1)S(1)} %finish.1), channel_id=1, replica_groups=mesh['grp'=2,'tp'=8,'rep'=2] {'rep'}, dimensions={2}, use_global_device_ids=true | all-gather | bytes 98304 | tf_op jit(solution)/shard_map/all_gather | solution.py:616
  50.0 0.6 %copy.16 = bf16[1,2,16384]{2,1,0:T(2,128)(2,1)} copy(bf16[1,2,16384]{2,1,0:T(2,128)(2,1)S(1)} %all_gather.3) | data formatting | bytes 131072
  (21 shorter events, 0.1 us)
Async XLA Ops:
  0.0 8.9 %collective-permute-start = (bf16[3,192,2048]{2,1,0:T(8,128)(2,1)}, bf16[3,192,2048]{2,1,0:T(8,128)(2,1)S(1)}, u32[]{:S(2)}, u32[]{:S(2)}) collective-permute-start(bf16[3,192,2048]{2,1,0:T(8,128)(2,1)} %bitcast.9), channel_id=1, source_target_pairs={{0,1},{1,0},{2,3},{3,2},{4,5},{5,4},{6,7},{7,6},{8,9},{9,8},{10,11... | collective-permute-start | bytes 7077896 | tf_op jit(solution)/shard_map/ppermute | solution.py:578
  0.5 8.4 %copy-start.6 = (s32[6]{0:T(128)S(1)}, s32[6]{0:T(128)}, u32[]{:S(2)}) copy-start(s32[6]{0:T(128)} %lengths.3) | copy-start | bytes 76
  0.5 8.4 %copy-start.1 = (f32[2048]{0:T(1024)S(1)}, f32[2048]{0:T(1024)}, u32[]{:S(2)}) copy-start(f32[2048]{0:T(1024)} %param.14) | copy-start | bytes 24580
  0.5 8.4 %copy-start.4 = (s32[6]{0:T(128)S(1)}, s32[6]{0:T(128)}, u32[]{:S(2)}) copy-start(s32[6]{0:T(128)} %targets.10) | copy-start | bytes 76
  8.9 4.2 %copy-start.7 = (f32[128]{0:T(128)S(1)}, f32[128]{0:T(128)}, u32[]{:S(2)}) copy-start(f32[128]{0:T(128)} %constant.7.clone) | copy-start | bytes 1540
  10.5 7.8 %collective-permute-start.2 = (bf16[768,128]{1,0:T(8,128)(2,1)S(1)}, bf16[768,128]{1,0:T(8,128)(2,1)S(1)}, u32[]{:S(2)}, u32[]{:S(2)}) collective-permute-start(bf16[768,128]{1,0:T(8,128)(2,1)S(1)} %get-tuple-element.51), channel_id=1, source_target_pairs={{0,2},{4,0},{8,4},{12,8},{14,12},{10,14},{6,10},{2,6},{1,3},{5,1},... | collective-permute-start | bytes 589832 | tf_op jit(solution)/shard_map/ppermute | solution.py:576
  13.1 7.8 %collective-permute-start.1 = (bf16[784,128]{1,0:T(8,128)(2,1)S(1)}, bf16[784,128]{1,0:T(8,128)(2,1)S(1)}, u32[]{:S(2)}, u32[]{:S(2)}) collective-permute-start(bf16[784,128]{1,0:T(8,128)(2,1)S(1)} %get-tuple-element.62), channel_id=1, source_target_pairs={{0,4},{4,8},{8,12},{12,14},{14,10},{10,6},{6,2},{2,0},{1,5},{5,9},... | collective-permute-start | bytes 602120 | tf_op jit(solution)/shard_map/ppermute | solution.py:576
  13.2 4.4 %copy-start.2 = (f32[2,192,128]{2,1,0:T(8,128)S(1)}, f32[2,192,128]{2,1,0:T(8,128)}, u32[]{:S(2)}) copy-start(f32[2,192,128]{2,1,0:T(8,128)} %constant.8.clone.turns) | copy-start | bytes 589828
  13.2 4.4 %copy-start.3 = (bf16[1,2,16384]{2,1,0:T(2,128)(2,1)S(1)}, bf16[1,2,16384]{2,1,0:T(2,128)(2,1)}, u32[]{:S(2)}) copy-start(bf16[1,2,16384]{2,1,0:T(2,128)(2,1)} %queries.1) | copy-start | bytes 196612
  14.9 10.6 %collective-permute-start.3 = (bf16[784,128]{1,0:T(8,128)(2,1)S(1)}, bf16[784,128]{1,0:T(8,128)(2,1)S(1)}, u32[]{:S(2)}, u32[]{:S(2)}) collective-permute-start(bf16[784,128]{1,0:T(8,128)(2,1)S(1)} %get-tuple-element.65), channel_id=1, source_target_pairs={{0,4},{4,8},{8,12},{12,14},{14,10},{10,6},{6,2},{2,0},{1,5},{5,9},... | collective-permute-start | bytes 602120 | tf_op jit(solution)/shard_map/ppermute | solution.py:576
  17.6 8.0 %collective-permute-start.4 = (bf16[784,128]{1,0:T(8,128)(2,1)S(1)}, bf16[784,128]{1,0:T(8,128)(2,1)S(1)}, u32[]{:S(2)}, u32[]{:S(2)}) collective-permute-start(bf16[784,128]{1,0:T(8,128)(2,1)S(1)} %get-tuple-element.56), channel_id=1, source_target_pairs={{0,2},{4,0},{8,4},{12,8},{14,12},{10,14},{6,10},{2,6},{1,3},{5,1},... | collective-permute-start | bytes 602120 | tf_op jit(solution)/shard_map/ppermute | solution.py:576
  21.0 8.4 %collective-permute-start.5 = (bf16[784,128]{1,0:T(8,128)(2,1)S(1)}, bf16[784,128]{1,0:T(8,128)(2,1)S(1)}, u32[]{:S(2)}, u32[]{:S(2)}) collective-permute-start(bf16[784,128]{1,0:T(8,128)(2,1)S(1)} %get-tuple-element.73), channel_id=1, source_target_pairs={{0,4},{4,8},{8,12},{12,14},{14,10},{10,6},{6,2},{2,0},{1,5},{5,9},... | collective-permute-start | bytes 602120 | tf_op jit(solution)/shard_map/ppermute | solution.py:576
  21.0 8.8 %collective-permute-start.6 = (bf16[784,128]{1,0:T(8,128)(2,1)S(1)}, bf16[784,128]{1,0:T(8,128)(2,1)S(1)}, u32[]{:S(2)}, u32[]{:S(2)}) collective-permute-start(bf16[784,128]{1,0:T(8,128)(2,1)S(1)} %get-tuple-element.74), channel_id=1, source_target_pairs={{0,2},{4,0},{8,4},{12,8},{14,12},{10,14},{6,10},{2,6},{1,3},{5,1},... | collective-permute-start | bytes 602120 | tf_op jit(solution)/shard_map/ppermute | solution.py:576
  23.7 4.1 %copy-start = (bf16[1,1024,2048]{2,1,0:T(8,128)(2,1)S(1)}, bf16[1,1024,2048]{2,1,0:T(8,128)(2,1)}, u32[]{:S(2)}) copy-start(bf16[1,1024,2048]{2,1,0:T(8,128)(2,1)} %cache.3) | copy-start | bytes 12582916
  23.7 4.0 %copy-start.5 = (bf16[1,2,2048]{2,1,0:T(2,128)(2,1)S(1)}, bf16[1,2,2048]{2,1,0:T(2,128)(2,1)}, u32[]{:S(2)}) copy-start(bf16[1,2,2048]{2,1,0:T(2,128)(2,1)} %new.3) | copy-start | bytes 24580
  25.7 9.6 %collective-permute-start.8 = (bf16[784,128]{1,0:T(8,128)(2,1)S(1)}, bf16[784,128]{1,0:T(8,128)(2,1)S(1)}, u32[]{:S(2)}, u32[]{:S(2)}) collective-permute-start(bf16[784,128]{1,0:T(8,128)(2,1)S(1)} %get-tuple-element.69), channel_id=1, source_target_pairs={{0,2},{4,0},{8,4},{12,8},{14,12},{10,14},{6,10},{2,6},{1,3},{5,1},... | collective-permute-start | bytes 602120 | tf_op jit(solution)/shard_map/ppermute | solution.py:576
  26.9 8.3 %collective-permute-start.7 = (bf16[784,128]{1,0:T(8,128)(2,1)S(1)}, bf16[784,128]{1,0:T(8,128)(2,1)S(1)}, u32[]{:S(2)}, u32[]{:S(2)}) collective-permute-start(bf16[784,128]{1,0:T(8,128)(2,1)S(1)} %get-tuple-element.77), channel_id=1, source_target_pairs={{0,4},{4,8},{8,12},{12,14},{14,10},{10,6},{6,2},{2,0},{1,5},{5,9},... | collective-permute-start | bytes 602120 | tf_op jit(solution)/shard_map/ppermute | solution.py:576
  29.9 9.6 %collective-permute-start.9 = (bf16[784,128]{1,0:T(8,128)(2,1)S(1)}, bf16[784,128]{1,0:T(8,128)(2,1)S(1)}, u32[]{:S(2)}, u32[]{:S(2)}) collective-permute-start(bf16[784,128]{1,0:T(8,128)(2,1)S(1)} %get-tuple-element.81), channel_id=1, source_target_pairs={{0,4},{4,8},{8,12},{12,14},{14,10},{10,6},{6,2},{2,0},{1,5},{5,9},... | collective-permute-start | bytes 602120 | tf_op jit(solution)/shard_map/ppermute | solution.py:576
  31.4 8.0 %collective-permute-start.10 = (bf16[784,128]{1,0:T(8,128)(2,1)S(1)}, bf16[784,128]{1,0:T(8,128)(2,1)S(1)}, u32[]{:S(2)}, u32[]{:S(2)}) collective-permute-start(bf16[784,128]{1,0:T(8,128)(2,1)S(1)} %get-tuple-element.82), channel_id=1, source_target_pairs={{0,2},{4,0},{8,4},{12,8},{14,12},{10,14},{6,10},{2,6},{1,3},{5,1},... | collective-permute-start | bytes 602120 | tf_op jit(solution)/shard_map/ppermute | solution.py:576
  35.3 9.5 %collective-permute-start.13 = (bf16[784,128]{1,0:T(8,128)(2,1)S(1)}, bf16[784,128]{1,0:T(8,128)(2,1)S(1)}, u32[]{:S(2)}, u32[]{:S(2)}) collective-permute-start(bf16[784,128]{1,0:T(8,128)(2,1)S(1)} %get-tuple-element.87), channel_id=1, source_target_pairs={{0,4},{4,8},{8,12},{12,14},{14,10},{10,6},{6,2},{2,0},{1,5},{5,9},... | collective-permute-start | bytes 602120 | tf_op jit(solution)/shard_map/ppermute | solution.py:576
  35.7 9.1 %collective-permute-start.14 = (bf16[784,128]{1,0:T(8,128)(2,1)S(1)}, bf16[784,128]{1,0:T(8,128)(2,1)S(1)}, u32[]{:S(2)}, u32[]{:S(2)}) collective-permute-start(bf16[784,128]{1,0:T(8,128)(2,1)S(1)} %get-tuple-element.88), channel_id=1, source_target_pairs={{0,2},{4,0},{8,4},{12,8},{14,12},{10,14},{6,10},{2,6},{1,3},{5,1},... | collective-permute-start | bytes 602120 | tf_op jit(solution)/shard_map/ppermute | solution.py:576
  39.6 6.4 %collective-permute-start.11 = (bf16[784,128]{1,0:T(8,128)(2,1)S(1)}, bf16[784,128]{1,0:T(8,128)(2,1)S(1)}, u32[]{:S(2)}, u32[]{:S(2)}) collective-permute-start(bf16[784,128]{1,0:T(8,128)(2,1)S(1)} %get-tuple-element.85), channel_id=1, source_target_pairs={{0,4},{4,8},{8,12},{12,14},{14,10},{10,6},{6,2},{2,0},{1,5},{5,9},... | collective-permute-start | bytes 602120 | tf_op jit(solution)/shard_map/ppermute | solution.py:576
  41.1 5.7 %collective-permute-start.12 = (bf16[784,128]{1,0:T(8,128)(2,1)S(1)}, bf16[784,128]{1,0:T(8,128)(2,1)S(1)}, u32[]{:S(2)}, u32[]{:S(2)}) collective-permute-start(bf16[784,128]{1,0:T(8,128)(2,1)S(1)} %get-tuple-element.86), channel_id=1, source_target_pairs={{0,2},{4,0},{8,4},{12,8},{14,12},{10,14},{6,10},{2,6},{1,3},{5,1},... | collective-permute-start | bytes 602120 | tf_op jit(solution)/shard_map/ppermute | solution.py:576
  41.6 3.2 %collective-permute-start.15 = (bf16[4,48,128]{2,1,0:T(8,128)(2,1)S(1)}, bf16[4,48,128]{2,1,0:T(8,128)(2,1)S(1)}, u32[]{:S(2)}, u32[]{:S(2)}) collective-permute-start(bf16[4,48,128]{2,1,0:T(8,128)(2,1)S(1)} %cache_attention.2), channel_id=1, source_target_pairs={{0,1},{1,0},{2,3},{3,2},{4,5},{5,4},{6,7},{7,6},{8,9},{9,8},{10,11... | collective-permute-start | bytes 147464 | tf_op jit(solution)/shard_map/ppermute | solution.py:578

commit v16 on v15

--- a/solution.py
+++ b/solution.py
@@ -114,6 +114,9 @@
     return stood(tail[0:1, :] + tail[1:2, :] + tail[2:3, :], ROWS)
 
 
+CODE_ROWS = 128
+
+
 def block_leaves(scale):
     wide = jnp.broadcast_to(scale, (8, HEAD_DIM))
     leaves = [wide * jnp.float32(level) for level in NORMAL_FLOAT_LEVELS]
@@ -144,12 +147,10 @@
 
 
 def weights_kernel(
-    x, codes, key_scales, value_scales, outer, gain,
-    out, scaled, squares, key_codes, value_codes, lines, scales, arrivals,
+    codes, key_scales, value_scales, outer, out, key_codes, value_codes, scales, arrivals
 ):
-    per_rep = x.shape[0]
     features, width = key_codes.shape
-    depth = min(256, features)
+    depth = min(CODE_ROWS, features)
     blocks = features // depth
     columns = outer.shape[0] // 2
     rep = lax.axis_index("rep")
@@ -165,15 +166,7 @@
             for kind, buffer in enumerate((key_codes, value_codes))
         ]
 
-    def line_copy(prompt):
-        return pltpu.make_async_copy(
-            x.at[prompt], lines.at[prompt], arrivals.at[2 * blocks + prompt]
-        )
-
     for block in range(blocks):
-        if block == blocks // 2:
-            for prompt in range(per_rep):
-                line_copy(prompt).start()
         for copy in code_copies(block):
             copy.start()
     for at in range(CORE_HEADS):
@@ -181,7 +174,6 @@
         lanes = slice(at * HEAD_DIM, (at + 1) * HEAD_DIM)
         scales[2 * at] = block_scales(key_scales[:, lanes], outer[...], column)
         scales[2 * at + 1] = block_scales(value_scales[:, lanes], outer[...], columns + column)
-    squares[...] = jnp.zeros(squares.shape, F32)
 
     def body(step, _):
         row = pl.ds(step, 1)
@@ -197,60 +189,41 @@
         return 0
 
     steps = depth // QBLOCK
-    late = blocks - blocks // 2
     for block in range(blocks):
         for copy in code_copies(block):
             copy.wait()
         lax.fori_loop(block * steps, (block + 1) * steps, body, 0)
-        if block == blocks // 2:
-            for prompt in range(per_rep):
-                line_copy(prompt).wait()
-        for chunk in range(blocks):
-            if blocks // 2 + chunk * late // blocks != block:
-                continue
-            lanes = slice(chunk * depth, (chunk + 1) * depth)
-            for prompt in range(per_rep):
-                wide = lines[prompt, :, lanes].astype(F32)
-                scaled[prompt, :, lanes] = (wide * gain[:, lanes]).astype(BF16)
-                squares[prompt] += token_rows(jnp.sum(wide * wide, axis=1, keepdims=True))
-
-
-def dequantize(x, codes, scales, outer, gain):
-    per_rep, _, features = x.shape
+
+
+def dequantize(codes, scales, outer):
+    features = codes.shape[0]
     width = CORE_HEADS * HEAD_DIM
-    blocks = features // min(256, features)
+    blocks = features // min(CODE_ROWS, features)
     rep = lambda: lax.axis_index("rep")
-    x, codes, scales, outer, gain = in_hbm(x, codes, scales, outer, gain)
+    codes, scales, outer = in_hbm(codes, scales, outer)
     return pl.pallas_call(
         weights_kernel,
         grid=(1,),
         in_specs=[
             pl.BlockSpec(memory_space=pltpu.HBM),
-            pl.BlockSpec(memory_space=pltpu.HBM),
             pl.BlockSpec((scales.shape[0], width), lambda k: (0, rep())),
             pl.BlockSpec((scales.shape[0], width), lambda k: (0, 2 + rep())),
             pl.BlockSpec(outer.shape, lambda k: (0, 0)),
-            pl.BlockSpec(gain.shape, lambda k: (0, 0)),
         ],
-        out_specs=[VMEM] * 3,
-        out_shape=[
-            jax.ShapeDtypeStruct((CORE_HEADS, features, 2 * HEAD_DIM), BF16),
-            jax.ShapeDtypeStruct(x.shape, BF16),
-            jax.ShapeDtypeStruct((per_rep, 8, 128), F32),
-        ],
+        out_specs=VMEM,
+        out_shape=jax.ShapeDtypeStruct((CORE_HEADS, features, 2 * HEAD_DIM), BF16),
         scratch_shapes=[
             pltpu.VMEM((features, width), jnp.int32),
             pltpu.VMEM((features, width), jnp.int32),
-            pltpu.VMEM(x.shape, BF16),
             pltpu.VMEM((2 * CORE_HEADS, scales.shape[0], HEAD_DIM), F32),
-            pltpu.SemaphoreType.DMA((2 * blocks + per_rep,)),
+            pltpu.SemaphoreType.DMA((2 * blocks,)),
         ],
-        compiler_params=pltpu.CompilerParams(vmem_limit_bytes=36 * MIB),
+        compiler_params=pltpu.CompilerParams(vmem_limit_bytes=32 * MIB),
         cost_estimate=pl.CostEstimate(
             flops=32 * codes.size, bytes_accessed=codes.size * 2, transcendentals=0
         ),
         name="dequantize",
-    )(x, codes, scales, scales, outer, gain)
+    )(codes, scales, scales, outer)
 
 
 def prompt_of(targets, owner):
@@ -260,27 +233,24 @@
     return prompt
 
 
-def with_lines(targets, distance, own, squares, other, gain, line, total, some, none):
+def with_lines(targets, distance, own, other, gain, line, total, some, none):
     per_rep = own.shape[0]
     prompt = prompt_of(targets, owner_at(distance))
     at = lax.rem(jnp.maximum(prompt, 0), per_rep)
     is_own = prompt // per_rep == lax.axis_index("rep")
-
-    @pl.when((prompt >= 0) & is_own)
-    def _():
-        some(own.at[at], squares.at[at])
-
-    @pl.when((prompt >= 0) & jnp.logical_not(is_own))
-    def _():
-        width = min(512, line.shape[1])
+    width = min(512, line.shape[1])
+
+    def scale(x):
         total[...] = jnp.zeros(total.shape, F32)
         for begin in range(0, line.shape[1], width):
             lanes = slice(begin, begin + width)
-            wide = other[at, :, lanes].astype(F32)
+            wide = x[at, :, lanes].astype(F32)
             line[:, lanes] = (wide * gain[:, lanes]).astype(BF16)
             total[...] += token_rows(jnp.sum(wide * wide, axis=1, keepdims=True))
-        some(line, total)
-
+
+    pl.when((prompt >= 0) & is_own)(lambda: scale(own))
+    pl.when((prompt >= 0) & jnp.logical_not(is_own))(lambda: scale(other))
+    pl.when(prompt >= 0)(some)
     pl.when(prompt < 0)(none)
 
 
@@ -288,27 +258,27 @@
     return [pltpu.VMEM(x.shape[1:], BF16), pltpu.VMEM((8, 128), F32)]
 
 
-def first_kernel(distance, targets, own, squares, other, gain, weight, right, left, line, total):
-    def some(lines, sums):
+def first_kernel(distance, targets, own, other, gain, weight, right, left, line, total):
+    def some():
         for head in range(CORE_HEADS):
-            product = jnp.dot(lines[...], weight[head], preferred_element_type=F32)
+            product = jnp.dot(line[...], weight[head], preferred_element_type=F32)
             rows = slice(head * STRETCH, (head + 1) * STRETCH)
             right[rows] = product[:, :HEAD_DIM].astype(BF16)
             left[rows] = product[:, HEAD_DIM:].astype(BF16)
-        right[CORE_HEADS * STRETCH :] = two_pieces(sums[...])
+        right[CORE_HEADS * STRETCH :] = two_pieces(total[...])
 
     def none():
         right[...] = jnp.zeros(right.shape, BF16)
         left[...] = jnp.zeros(left.shape, BF16)
 
-    with_lines(targets, distance, own, squares, other, gain, line, total, some, none)
-
-
-def project_first(distance, targets, own, squares, other, gain, weight):
+    with_lines(targets, distance, own, other, gain, line, total, some, none)
+
+
+def project_first(distance, targets, own, other, gain, weight):
     rows = CORE_HEADS * STRETCH
     return pl.pallas_call(
         functools.partial(first_kernel, distance),
-        in_specs=[SMEM] + [VMEM] * 5,
+        in_specs=[SMEM] + [VMEM] * 4,
         out_specs=[VMEM] * 2,
         out_shape=[
             jax.ShapeDtypeStruct((rows + TAIL, HEAD_DIM), BF16),
@@ -320,30 +290,30 @@
             flops=STRETCH * weight.size * 2, bytes_accessed=weight.size, transcendentals=0
         ),
         name="project_first",
-    )(targets, own, squares, other, gain, weight)
-
-
-def project_kernel(distances, targets, own, squares, other, gain, weight, out, line, total):
+    )(targets, own, other, gain, weight)
+
+
+def project_kernel(distances, targets, own, other, gain, weight, out, line, total):
     for item, distance in enumerate(distances):
 
-        def some(lines, sums, item=item):
+        def some(item=item):
             for head in range(CORE_HEADS):
-                product = jnp.dot(lines[...], weight[head], preferred_element_type=F32)
+                product = jnp.dot(line[...], weight[head], preferred_element_type=F32)
                 rows = slice(head * STRETCH, (head + 1) * STRETCH)
                 out[item, 0, rows] = product[:, :HEAD_DIM]
                 out[item, 1, rows] = product[:, HEAD_DIM:]
-            out[item, 0, CORE_HEADS * STRETCH :] = sums[...]
+            out[item, 0, CORE_HEADS * STRETCH :] = total[...]
 
         def none(item=item):
             out[item] = jnp.zeros(out.shape[1:], F32)
 
-        with_lines(targets, distance, own, squares, other, gain, line, total, some, none)
-
-
-def project(distances, targets, own, squares, other, gain, weight):
+        with_lines(targets, distance, own, other, gain, line, total, some, none)
+
+
+def project(distances, targets, own, other, gain, weight):
     return pl.pallas_call(
         functools.partial(project_kernel, distances),
-        in_specs=[SMEM] + [VMEM] * 5,
+        in_specs=[SMEM] + [VMEM] * 4,
         out_specs=VMEM,
         out_shape=jax.ShapeDtypeStruct((len(distances), 2, 4 * STRETCH + 8, HEAD_DIM), F32),
         scratch_shapes=line_scratch(own),
@@ -354,7 +324,7 @@
             transcendentals=0,
         ),
         name="project",
-    )(targets, own, squares, other, gain, weight)
+    )(targets, own, other, gain, weight)
 
 
 def send_kernel(half, terms, *refs):
@@ -577,12 +547,12 @@
 
     swap = lambda array: lax.ppermute(array, "rep", [(0, 1), (1, 0)])
     other = swap(lines)
-    weight, own, squares = dequantize(lines, kv_codes, scale_codes, outer_scales.T, gain)
+    weight = dequantize(kv_codes, scale_codes, outer_scales.T)
     frequency, turns = rotary_turns()
     start = (prompt_lengths - STRETCH).astype(F32)[:, None] * jnp.asarray(frequency)
     starts = jnp.stack([jnp.cos(start), jnp.sin(start)])
 
-    features = [own, squares, other, gain]
+    features = [lines, other, gain]
     right, left = project_first(half, target_rows, *features, weight)
     targets, _ = lax.optimization_barrier((target_rows, left))
     arrived = [pass_on(right, left), []]

time: 50.5 us -> 50.7 us (level)
  waiting for transfers between devices: 7.68 us -> 5.83 us
  starting transfers between devices: 16.1 us -> 17.2 us
  Pallas kernels: 23.3 us -> 24.1 us
    ppermute x7, starting transfers between devices: 7.08 us -> 13 us  [pass_on(): lax.ppermute(right, 'tp', to_right)]
    ppermute x7, starting transfers between devices: 8.54 us -> 3.67 us  [pass_on(): lax.ppermute(left, 'tp', to_left)]
    ppermute x7, waiting for transfers between devices: 6.44 us -> 4.2 us  [pass_on(): lax.ppermute(right, 'tp', to_right)]
    pallas_call x4, Pallas kernels: 7.67 us -> 9.07 us  [project(): pl.pallas_call(functools.partial(project_kernel, distances), in_specs=[SM...]
    pallas_call x1, Pallas kernels: 8.38 us -> 7.42 us  [dequantize(): pl.pallas_call(weights_kernel, grid=(1,), in_specs=[pl.BlockSpec(memory_s...]
  transfers between devices with their start and end apart: 16 -> 16, of which waited for: 6 -> 6; matrix products, arithmetic and copies ran while one was open for 0% -> 0% of each run, Pallas kernels for 40% -> 41%
where the time goes in v16:
time: 50.7 us
  Pallas kernels  24.1 us (48%)
  starting transfers between devices  17.2 us (34%)
  waiting for transfers between devices  5.83 us (11%)
  blocking collectives  1.85 us (4%)
  between operations  0.92 us (2%)
  local copies, waits for them, and re-layouts  0.68 us (1%)
    ppermute x7, starting transfers between devices, pass_on(): lax.ppermute(right, 'tp', to_right)  13 us
    pallas_call x4, Pallas kernels, project(): pl.pallas_call(functools.partial(project_kernel, distances), in_specs=[SM...  9.07 us
    pallas_call x1, Pallas kernels, dequantize(): pl.pallas_call(weights_kernel, grid=(1,), in_specs=[pl.BlockSpec(memory_s...  7.42 us
    ppermute x7, waiting for transfers between devices, pass_on(): lax.ppermute(right, 'tp', to_right)  4.2 us
    ppermute x7, starting transfers between devices, pass_on(): lax.ppermute(left, 'tp', to_left)  3.67 us
    pallas_call x2, Pallas kernels, cache_attention(): pl.pallas_call(functools.partial(cache_kernel, part), in_specs=[SMEM] * 3...  3.18 us
    pallas_call x1, Pallas kernels, project_first(): pl.pallas_call(functools.partial(first_kernel, distance), in_specs=[SMEM]...  1.91 us
    all_gather x1, blocking collectives, per_device(): return lax.all_gather(out, 'rep', axis=2, tiled=True)  1.85 us
  transfers between devices with their start and end apart: 16, of which 6 were waited for; matrix products, arithmetic and copies ran while one was open for 0% of the time, Pallas kernels for 41%

profile of v16, /device:TPU:0, one launch (start us, length us, event | category | flops | bytes accessed | tf_op | source)
XLA Modules:
  0.0 50.7 jit_solution(5251174184130078174)
XLA Ops:
  0.0 0.5 collective-permute-start
  0.5 7.4 %dequantize.1.weight = bf16[4,2048,256]{2,1,0:T(8,128)(2,1)S(1)} custom-call(s32[2048,2048]{1,0:T(8,128)} %codes.1, s32[32,2048]{1,0:T(8,128)} %value_scales.1, s32[32,2048]{1,0:T(8,128)} %value_scales.1, f32[8,32]{1,0:T(8,128)} %bitcast.14), custom_call_target="tpu_custom_call" | custom-call | flops 134217728 | bytes 8388608 | tf_op jit(solution)/shard_map/dequantize/pallas_call | solution.py:204
  7.9 0.0 collective-permute-done.other
  8.0 0.0 copy-start.8
  8.0 1.9 %project_first.1 = (bf16[784,128]{1,0:T(8,128)(2,1)S(1)}, bf16[768,128]{1,0:T(8,128)(2,1)S(1)}) custom-call(s32[6]{0:T(128)S(1)} %copy-done.5, bf16[3,192,2048]{2,1,0:T(8,128)(2,1)S(1)} %bitcast.4, bf16[3,192,2048]{2,1,0:T(8,128)(2,1)S(1)} %collective-permute-done.other, f32[1,2048]{1,0:T(1,128)S(1)} %bitcast.9, bf16[4,2048,256]{2,1,0:T(8,128)(2,1)S(1)} %dequantize.1.weight), custom_call_target="tpu_custom_call" | custom-call | flops 805306368 | bytes 2097152 | tf_op jit(solution)/shard_map/project_first/pallas_call | solution.py:279
  9.9 1.3 %collective-permute-start.2 = (bf16[768,128]{1,0:T(8,128)(2,1)S(1)}, bf16[768,128]{1,0:T(8,128)(2,1)S(1)}, u32[]{:S(2)}, u32[]{:S(2)}) collective-permute-start(bf16[768,128]{1,0:T(8,128)(2,1)S(1)} %get-tuple-element.45), channel_id=1, source_target_pairs={{0,2},{4,0},{8,4},{12,8},{14,12},{10,14},{6,10},{2,6},{1,3},{5,1},... | collective-permute-start | bytes 589832 | tf_op jit(solution)/shard_map/ppermute | solution.py:546
  11.2 1.4 %collective-permute-start.1 = (bf16[784,128]{1,0:T(8,128)(2,1)S(1)}, bf16[784,128]{1,0:T(8,128)(2,1)S(1)}, u32[]{:S(2)}, u32[]{:S(2)}) collective-permute-start(bf16[784,128]{1,0:T(8,128)(2,1)S(1)} %get-tuple-element.56), channel_id=1, source_target_pairs={{0,4},{4,8},{8,12},{12,14},{14,10},{10,6},{6,2},{2,0},{1,5},{5,9},... | collective-permute-start | bytes 602120 | tf_op jit(solution)/shard_map/ppermute | solution.py:546
  12.6 0.1 multiply_cosine_fusion
  12.7 0.0 copy-start.3
  12.7 0.0 copy-start.4
  12.7 2.0 %project.4.terms = f32[2,2,776,128]{3,2,1,0:T(8,128)S(1)} custom-call(s32[6]{0:T(128)S(1)} %copy-done.5, bf16[3,192,2048]{2,1,0:T(8,128)(2,1)S(1)} %bitcast.5, bf16[3,192,2048]{2,1,0:T(8,128)(2,1)S(1)} %collective-permute-done.other, f32[1,2048]{1,0:T(1,128)S(1)} %bitcast.10, bf16[4,2048,256]{2,1,0:T(8,128)(2,1)S(1)} %dequantize.1.weight), custom_call_target="tpu_custom_call" | custom-call | flops 805306368 | bytes 2097152 | tf_op jit(solution)/shard_map/project/pallas_call | solution.py:314
  14.8 3.3 %collective-permute-start.3 = (bf16[784,128]{1,0:T(8,128)(2,1)S(1)}, bf16[784,128]{1,0:T(8,128)(2,1)S(1)}, u32[]{:S(2)}, u32[]{:S(2)}) collective-permute-start(bf16[784,128]{1,0:T(8,128)(2,1)S(1)} %get-tuple-element.59), channel_id=1, source_target_pairs={{0,4},{4,8},{8,12},{12,14},{14,10},{10,6},{6,2},{2,0},{1,5},{5,9},... | collective-permute-start | bytes 602120 | tf_op jit(solution)/shard_map/ppermute | solution.py:546
  18.0 0.0 collective-permute-start.4
  18.0 0.7 %prepare.1 = (bf16[8,32,128]{2,1,0:T(8,128)(2,1)S(1)}, f32[2,192,128]{2,1,0:T(8,128)S(1)}) custom-call(s32[6]{0:T(128)S(1)} %copy-done.5, bf16[1,2,16384]{2,1,0:T(2,128)(2,1)S(1)} %copy-done.4, f32[2,6,128]{2,1,0:T(8,128)S(1)} %pad_maximum_fusion.starts, f32[2,192,128]{2,1,0:T(8,128)S(1)} %copy-done.3), custom_call_target="tpu_custom_call" | custom-call | tf_op jit(solution)/shard_map/prepare/pallas_call | solution.py:377
  18.7 0.0 collective-permute-done.2.refs_1_
  18.7 1.0 %collective-permute-done.1.refs_0_ = bf16[784,128]{1,0:T(8,128)(2,1)S(1)} collective-permute-done((bf16[784,128]{1,0:T(8,128)(2,1)S(1)}, bf16[784,128]{1,0:T(8,128)(2,1)S(1)}, u32[]{:S(2)}, u32[]{:S(2)}) %collective-permute-start.1) | collective-permute-done | bytes 200736 | tf_op jit(solution)/shard_map/ppermute | solution.py:546
  19.8 0.1 sends.7
  19.9 1.0 %collective-permute-start.5 = (bf16[784,128]{1,0:T(8,128)(2,1)S(1)}, bf16[784,128]{1,0:T(8,128)(2,1)S(1)}, u32[]{:S(2)}, u32[]{:S(2)}) collective-permute-start(bf16[784,128]{1,0:T(8,128)(2,1)S(1)} %get-tuple-element.67), channel_id=1, source_target_pairs={{0,4},{4,8},{8,12},{12,14},{14,10},{10,6},{6,2},{2,0},{1,5},{5,9},... | collective-permute-start | bytes 602120 | tf_op jit(solution)/shard_map/ppermute | solution.py:546
  20.9 1.1 %collective-permute-start.6 = (bf16[784,128]{1,0:T(8,128)(2,1)S(1)}, bf16[784,128]{1,0:T(8,128)(2,1)S(1)}, u32[]{:S(2)}, u32[]{:S(2)}) collective-permute-start(bf16[784,128]{1,0:T(8,128)(2,1)S(1)} %get-tuple-element.68), channel_id=1, source_target_pairs={{0,2},{4,0},{8,4},{12,8},{14,12},{10,14},{6,10},{2,6},{1,3},{5,1},... | collective-permute-start | bytes 602120 | tf_op jit(solution)/shard_map/ppermute | solution.py:546
  22.7 0.0 copy-start.1
  22.7 0.0 copy-start.6
  22.7 3.2 %project.5.terms = f32[2,2,776,128]{3,2,1,0:T(8,128)S(1)} custom-call(s32[6]{0:T(128)S(1)} %copy-done.5, bf16[3,192,2048]{2,1,0:T(8,128)(2,1)S(1)} %bitcast.6, bf16[3,192,2048]{2,1,0:T(8,128)(2,1)S(1)} %collective-permute-done.other, f32[1,2048]{1,0:T(1,128)S(1)} %bitcast.11, bf16[4,2048,256]{2,1,0:T(8,128)(2,1)S(1)} %dequantize.1.weight), custom_call_target="tpu_custom_call" | custom-call | flops 805306368 | bytes 2097152 | tf_op jit(solution)/shard_map/project/pallas_call | solution.py:314
  26.0 0.0 collective-permute-done.3.refs_0_
  26.0 0.1 sends.8
  26.1 0.8 %collective-permute-start.8 = (bf16[784,128]{1,0:T(8,128)(2,1)S(1)}, bf16[784,128]{1,0:T(8,128)(2,1)S(1)}, u32[]{:S(2)}, u32[]{:S(2)}) collective-permute-start(bf16[784,128]{1,0:T(8,128)(2,1)S(1)} %get-tuple-element.63), channel_id=1, source_target_pairs={{0,2},{4,0},{8,4},{12,8},{14,12},{10,14},{6,10},{2,6},{1,3},{5,1},... | collective-permute-start | bytes 602120 | tf_op jit(solution)/shard_map/ppermute | solution.py:546
  26.8 1.3 %collective-permute-start.7 = (bf16[784,128]{1,0:T(8,128)(2,1)S(1)}, bf16[784,128]{1,0:T(8,128)(2,1)S(1)}, u32[]{:S(2)}, u32[]{:S(2)}) collective-permute-start(bf16[784,128]{1,0:T(8,128)(2,1)S(1)} %get-tuple-element.71), channel_id=1, source_target_pairs={{0,4},{4,8},{8,12},{12,14},{14,10},{10,6},{6,2},{2,0},{1,5},{5,9},... | collective-permute-start | bytes 602120 | tf_op jit(solution)/shard_map/ppermute | solution.py:546
  28.1 1.6 %cache_attention.2 = bf16[4,48,128]{2,1,0:T(8,128)(2,1)S(1)} custom-call(s32[6]{0:T(128)S(1)} %copy-done.5, s32[6]{0:T(128)S(1)} %copy-done.7, s32[1]{0:T(128)S(6)} %copy.15.stored, bf16[8,32,128]{2,1,0:T(8,128)(2,1)S(1)} %get-tuple-element.65.q.grouped, bf16[1,1024,2048]{2,1,0:T(8,128)(2,1)S(1)} %copy-done.1, bf16[1,2,2048]{2,1,0:T(2,128)(2,1)S(1)} %copy-done.6), custom_call_target="tpu_custom_call" | custom-call | flops 1 | bytes 1 | tf_op jit(solution)/shard_map/cache_attention/pallas_call | solution.py:441
  29.7 0.0 collective-permute-done.5.refs_0_
  29.8 0.5 collective-permute-done.6.refs_1_
  30.2 0.1 sends.9
  30.3 1.6 %collective-permute-start.9 = (bf16[784,128]{1,0:T(8,128)(2,1)S(1)}, bf16[784,128]{1,0:T(8,128)(2,1)S(1)}, u32[]{:S(2)}, u32[]{:S(2)}) collective-permute-start(bf16[784,128]{1,0:T(8,128)(2,1)S(1)} %get-tuple-element.75), channel_id=1, source_target_pairs={{0,4},{4,8},{8,12},{12,14},{14,10},{10,6},{6,2},{2,0},{1,5},{5,9},... | collective-permute-start | bytes 602120 | tf_op jit(solution)/shard_map/ppermute | solution.py:546
  32.0 0.5 collective-permute-start.10
  32.4 2.0 %project.6.terms = f32[2,2,776,128]{3,2,1,0:T(8,128)S(1)} custom-call(s32[6]{0:T(128)S(1)} %copy-done.5, bf16[3,192,2048]{2,1,0:T(8,128)(2,1)S(1)} %bitcast.7, bf16[3,192,2048]{2,1,0:T(8,128)(2,1)S(1)} %collective-permute-done.other, f32[1,2048]{1,0:T(1,128)S(1)} %bitcast.12, bf16[4,2048,256]{2,1,0:T(8,128)(2,1)S(1)} %dequantize.1.weight), custom_call_target="tpu_custom_call" | custom-call | flops 805306368 | bytes 2097152 | tf_op jit(solution)/shard_map/project/pallas_call | solution.py:314
  34.4 0.6 %collective-permute-done.7.refs_0_ = bf16[784,128]{1,0:T(8,128)(2,1)S(1)} collective-permute-done((bf16[784,128]{1,0:T(8,128)(2,1)S(1)}, bf16[784,128]{1,0:T(8,128)(2,1)S(1)}, u32[]{:S(2)}, u32[]{:S(2)}) %collective-permute-start.7) | collective-permute-done | bytes 200736 | tf_op jit(solution)/shard_map/ppermute | solution.py:546
  35.0 0.1 sends.10
  35.1 2.3 %collective-permute-start.13 = (bf16[784,128]{1,0:T(8,128)(2,1)S(1)}, bf16[784,128]{1,0:T(8,128)(2,1)S(1)}, u32[]{:S(2)}, u32[]{:S(2)}) collective-permute-start(bf16[784,128]{1,0:T(8,128)(2,1)S(1)} %get-tuple-element.81), channel_id=1, source_target_pairs={{0,4},{4,8},{8,12},{12,14},{14,10},{10,6},{6,2},{2,0},{1,5},{5,9},... | collective-permute-start | bytes 602120 | tf_op jit(solution)/shard_map/ppermute | solution.py:546
  37.4 1.5 %collective-permute-done.9.refs_0_ = bf16[784,128]{1,0:T(8,128)(2,1)S(1)} collective-permute-done((bf16[784,128]{1,0:T(8,128)(2,1)S(1)}, bf16[784,128]{1,0:T(8,128)(2,1)S(1)}, u32[]{:S(2)}, u32[]{:S(2)}) %collective-permute-start.9) | collective-permute-done | bytes 200736 | tf_op jit(solution)/shard_map/ppermute | solution.py:546
  38.9 0.1 sends.11
  39.0 2.1 %collective-permute-start.11 = (bf16[784,128]{1,0:T(8,128)(2,1)S(1)}, bf16[784,128]{1,0:T(8,128)(2,1)S(1)}, u32[]{:S(2)}, u32[]{:S(2)}) collective-permute-start(bf16[784,128]{1,0:T(8,128)(2,1)S(1)} %get-tuple-element.79), channel_id=1, source_target_pairs={{0,4},{4,8},{8,12},{12,14},{14,10},{10,6},{6,2},{2,0},{1,5},{5,9},... | collective-permute-start | bytes 602120 | tf_op jit(solution)/shard_map/ppermute | solution.py:546
  41.1 1.6 %cache_attention.3.cached_here = bf16[4,48,128]{2,1,0:T(8,128)(2,1)S(1)} custom-call(s32[6]{0:T(128)S(1)} %copy-done.5, s32[6]{0:T(128)S(1)} %copy-done.7, s32[1]{0:T(128)S(6)} %copy.15.stored, bf16[8,32,128]{2,1,0:T(8,128)(2,1)S(1)} %get-tuple-element.65.q.grouped, bf16[1,1024,2048]{2,1,0:T(8,128)(2,1)S(1)} %copy-done.1, bf16[1,2,2048]{2,1,0:T(2,128)(2,1)S(1)} %copy-done.6), custom_call_target="tpu_custom_call" | custom-call | flops 1 | bytes 1 | tf_op jit(solution)/shard_map/cache_attention/pallas_call | solution.py:441
  42.7 1.9 %project.7.own = f32[1,2,776,128]{3,2,1,0:T(8,128)S(1)} custom-call(s32[6]{0:T(128)S(1)} %copy-done.5, bf16[3,192,2048]{2,1,0:T(8,128)(2,1)S(1)} %bitcast.8, bf16[3,192,2048]{2,1,0:T(8,128)(2,1)S(1)} %collective-permute-done.other, f32[1,2048]{1,0:T(1,128)S(1)} %bitcast.13, bf16[4,2048,256]{2,1,0:T(8,128)(2,1)S(1)} %dequantize.1.weight), custom_call_target="tpu_custom_call" | custom-call | flops 402653184 | bytes 2097152 | tf_op jit(solution)/shard_map/project/pallas_call | solution.py:314
  44.6 0.0 collective-permute-done.13.right_values
  44.6 0.0 collective-permute-done.14.left_keys
  44.7 1.1 %collective-permute-done.11.right_keys = bf16[784,128]{1,0:T(8,128)(2,1)S(1)} collective-permute-done((bf16[784,128]{1,0:T(8,128)(2,1)S(1)}, bf16[784,128]{1,0:T(8,128)(2,1)S(1)}, u32[]{:S(2)}, u32[]{:S(2)}) %collective-permute-start.11) | collective-permute-done | bytes 200736 | tf_op jit(solution)/shard_map/ppermute | solution.py:546
  45.7 1.1 %collective-permute-done.12.left_values = bf16[784,128]{1,0:T(8,128)(2,1)S(1)} collective-permute-done((bf16[784,128]{1,0:T(8,128)(2,1)S(1)}, bf16[784,128]{1,0:T(8,128)(2,1)S(1)}, u32[]{:S(2)}, u32[]{:S(2)}) %collective-permute-start.12) | collective-permute-done | bytes 200736 | tf_op jit(solution)/shard_map/ppermute | solution.py:546
  46.8 1.4 %finish.1 = bf16[1,2,8192]{2,1,0:T(2,128)(2,1)S(1)} custom-call(s32[6]{0:T(128)S(1)} %copy-done.5, f32[2,192,128]{2,1,0:T(8,128)S(1)} %get-tuple-element.54.rotary, f32[1,2,776,128]{3,2,1,0:T(8,128)S(1)} %project.7.own, bf16[784,128]{1,0:T(8,128)(2,1)S(1)} %collective-permute-done.11.right_keys, bf16[784,128]{1,0:T(8,128)(2,1)S(1)} %collective-permute-done.12.left_values, ...), custom_call_target="tpu_custom_call" | custom-call | tf_op jit(solution)/shard_map/finish/pallas_call | solution.py:507
  48.2 1.9 %all_gather.3 = bf16[1,2,16384]{2,1,0:T(2,128)(2,1)S(1)} all-gather(bf16[1,2,8192]{2,1,0:T(2,128)(2,1)S(1)} %finish.1), channel_id=1, replica_groups=mesh['grp'=2,'tp'=8,'rep'=2] {'rep'}, dimensions={2}, use_global_device_ids=true | all-gather | bytes 98304 | tf_op jit(solution)/shard_map/all_gather | solution.py:586
  50.1 0.6 %copy.16 = bf16[1,2,16384]{2,1,0:T(2,128)(2,1)} copy(bf16[1,2,16384]{2,1,0:T(2,128)(2,1)S(1)} %all_gather.3) | data formatting | bytes 131072
  (23 shorter events, 0.1 us)
Async XLA Ops:
  0.0 7.9 %collective-permute-start = (bf16[3,192,2048]{2,1,0:T(8,128)(2,1)}, bf16[3,192,2048]{2,1,0:T(8,128)(2,1)S(1)}, u32[]{:S(2)}, u32[]{:S(2)}) collective-permute-start(bf16[3,192,2048]{2,1,0:T(8,128)(2,1)} %bitcast.3), channel_id=1, source_target_pairs={{0,1},{1,0},{2,3},{3,2},{4,5},{5,4},{6,7},{7,6},{8,9},{9,8},{10,11... | collective-permute-start | bytes 7077896 | tf_op jit(solution)/shard_map/ppermute | solution.py:548
  0.5 7.4 %copy-start.7 = (s32[6]{0:T(128)S(1)}, s32[6]{0:T(128)}, u32[]{:S(2)}) copy-start(s32[6]{0:T(128)} %lengths.3) | copy-start | bytes 76
  0.5 7.5 %copy-start = (bf16[192,3,2048]{2,0,1:T(8,128)(2,1)S(1)}, bf16[192,3,2048]{2,0,1:T(8,128)(2,1)}, u32[]{:S(2)}) copy-start(bf16[192,3,2048]{2,0,1:T(8,128)(2,1)} %param.13) | copy-start | bytes 7077892
  0.5 7.5 %copy-start.2 = (f32[2048]{0:T(1024)S(1)}, f32[2048]{0:T(1024)}, u32[]{:S(2)}) copy-start(f32[2048]{0:T(1024)} %param.14) | copy-start | bytes 24580
  0.5 7.5 %copy-start.5 = (s32[6]{0:T(128)S(1)}, s32[6]{0:T(128)}, u32[]{:S(2)}) copy-start(s32[6]{0:T(128)} %targets.10) | copy-start | bytes 76
  8.0 4.6 %copy-start.8 = (f32[128]{0:T(128)S(1)}, f32[128]{0:T(128)}, u32[]{:S(2)}) copy-start(f32[128]{0:T(128)} %constant.7.clone) | copy-start | bytes 1540
  9.9 8.8 %collective-permute-start.2 = (bf16[768,128]{1,0:T(8,128)(2,1)S(1)}, bf16[768,128]{1,0:T(8,128)(2,1)S(1)}, u32[]{:S(2)}, u32[]{:S(2)}) collective-permute-start(bf16[768,128]{1,0:T(8,128)(2,1)S(1)} %get-tuple-element.45), channel_id=1, source_target_pairs={{0,2},{4,0},{8,4},{12,8},{14,12},{10,14},{6,10},{2,6},{1,3},{5,1},... | collective-permute-start | bytes 589832 | tf_op jit(solution)/shard_map/ppermute | solution.py:546
  11.2 8.6 %collective-permute-start.1 = (bf16[784,128]{1,0:T(8,128)(2,1)S(1)}, bf16[784,128]{1,0:T(8,128)(2,1)S(1)}, u32[]{:S(2)}, u32[]{:S(2)}) collective-permute-start(bf16[784,128]{1,0:T(8,128)(2,1)S(1)} %get-tuple-element.56), channel_id=1, source_target_pairs={{0,4},{4,8},{8,12},{12,14},{14,10},{10,6},{6,2},{2,0},{1,5},{5,9},... | collective-permute-start | bytes 602120 | tf_op jit(solution)/shard_map/ppermute | solution.py:546
  12.7 5.3 %copy-start.3 = (f32[2,192,128]{2,1,0:T(8,128)S(1)}, f32[2,192,128]{2,1,0:T(8,128)}, u32[]{:S(2)}) copy-start(f32[2,192,128]{2,1,0:T(8,128)} %constant.8.clone.turns) | copy-start | bytes 589828
  12.7 5.3 %copy-start.4 = (bf16[1,2,16384]{2,1,0:T(2,128)(2,1)S(1)}, bf16[1,2,16384]{2,1,0:T(2,128)(2,1)}, u32[]{:S(2)}) copy-start(bf16[1,2,16384]{2,1,0:T(2,128)(2,1)} %queries.1) | copy-start | bytes 196612
  14.8 11.2 %collective-permute-start.3 = (bf16[784,128]{1,0:T(8,128)(2,1)S(1)}, bf16[784,128]{1,0:T(8,128)(2,1)S(1)}, u32[]{:S(2)}, u32[]{:S(2)}) collective-permute-start(bf16[784,128]{1,0:T(8,128)(2,1)S(1)} %get-tuple-element.59), channel_id=1, source_target_pairs={{0,4},{4,8},{8,12},{12,14},{14,10},{10,6},{6,2},{2,0},{1,5},{5,9},... | collective-permute-start | bytes 602120 | tf_op jit(solution)/shard_map/ppermute | solution.py:546
  18.0 7.9 %collective-permute-start.4 = (bf16[784,128]{1,0:T(8,128)(2,1)S(1)}, bf16[784,128]{1,0:T(8,128)(2,1)S(1)}, u32[]{:S(2)}, u32[]{:S(2)}) collective-permute-start(bf16[784,128]{1,0:T(8,128)(2,1)S(1)} %get-tuple-element.50), channel_id=1, source_target_pairs={{0,2},{4,0},{8,4},{12,8},{14,12},{10,14},{6,10},{2,6},{1,3},{5,1},... | collective-permute-start | bytes 602120 | tf_op jit(solution)/shard_map/ppermute | solution.py:546
  19.9 9.9 %collective-permute-start.5 = (bf16[784,128]{1,0:T(8,128)(2,1)S(1)}, bf16[784,128]{1,0:T(8,128)(2,1)S(1)}, u32[]{:S(2)}, u32[]{:S(2)}) collective-permute-start(bf16[784,128]{1,0:T(8,128)(2,1)S(1)} %get-tuple-element.67), channel_id=1, source_target_pairs={{0,4},{4,8},{8,12},{12,14},{14,10},{10,6},{6,2},{2,0},{1,5},{5,9},... | collective-permute-start | bytes 602120 | tf_op jit(solution)/shard_map/ppermute | solution.py:546
  20.9 9.3 %collective-permute-start.6 = (bf16[784,128]{1,0:T(8,128)(2,1)S(1)}, bf16[784,128]{1,0:T(8,128)(2,1)S(1)}, u32[]{:S(2)}, u32[]{:S(2)}) collective-permute-start(bf16[784,128]{1,0:T(8,128)(2,1)S(1)} %get-tuple-element.68), channel_id=1, source_target_pairs={{0,2},{4,0},{8,4},{12,8},{14,12},{10,14},{6,10},{2,6},{1,3},{5,1},... | collective-permute-start | bytes 602120 | tf_op jit(solution)/shard_map/ppermute | solution.py:546
  22.7 5.4 %copy-start.1 = (bf16[1,1024,2048]{2,1,0:T(8,128)(2,1)S(1)}, bf16[1,1024,2048]{2,1,0:T(8,128)(2,1)}, u32[]{:S(2)}) copy-start(bf16[1,1024,2048]{2,1,0:T(8,128)(2,1)} %cache.3) | copy-start | bytes 12582916
  22.7 5.4 %copy-start.6 = (bf16[1,2,2048]{2,1,0:T(2,128)(2,1)S(1)}, bf16[1,2,2048]{2,1,0:T(2,128)(2,1)}, u32[]{:S(2)}) copy-start(bf16[1,2,2048]{2,1,0:T(2,128)(2,1)} %new.3) | copy-start | bytes 24580
  26.1 8.9 %collective-permute-start.8 = (bf16[784,128]{1,0:T(8,128)(2,1)S(1)}, bf16[784,128]{1,0:T(8,128)(2,1)S(1)}, u32[]{:S(2)}, u32[]{:S(2)}) collective-permute-start(bf16[784,128]{1,0:T(8,128)(2,1)S(1)} %get-tuple-element.63), channel_id=1, source_target_pairs={{0,2},{4,0},{8,4},{12,8},{14,12},{10,14},{6,10},{2,6},{1,3},{5,1},... | collective-permute-start | bytes 602120 | tf_op jit(solution)/shard_map/ppermute | solution.py:546
  26.8 8.1 %collective-permute-start.7 = (bf16[784,128]{1,0:T(8,128)(2,1)S(1)}, bf16[784,128]{1,0:T(8,128)(2,1)S(1)}, u32[]{:S(2)}, u32[]{:S(2)}) collective-permute-start(bf16[784,128]{1,0:T(8,128)(2,1)S(1)} %get-tuple-element.71), channel_id=1, source_target_pairs={{0,4},{4,8},{8,12},{12,14},{14,10},{10,6},{6,2},{2,0},{1,5},{5,9},... | collective-permute-start | bytes 602120 | tf_op jit(solution)/shard_map/ppermute | solution.py:546
  30.3 8.6 %collective-permute-start.9 = (bf16[784,128]{1,0:T(8,128)(2,1)S(1)}, bf16[784,128]{1,0:T(8,128)(2,1)S(1)}, u32[]{:S(2)}, u32[]{:S(2)}) collective-permute-start(bf16[784,128]{1,0:T(8,128)(2,1)S(1)} %get-tuple-element.75), channel_id=1, source_target_pairs={{0,4},{4,8},{8,12},{12,14},{14,10},{10,6},{6,2},{2,0},{1,5},{5,9},... | collective-permute-start | bytes 602120 | tf_op jit(solution)/shard_map/ppermute | solution.py:546
  32.0 7.0 %collective-permute-start.10 = (bf16[784,128]{1,0:T(8,128)(2,1)S(1)}, bf16[784,128]{1,0:T(8,128)(2,1)S(1)}, u32[]{:S(2)}, u32[]{:S(2)}) collective-permute-start(bf16[784,128]{1,0:T(8,128)(2,1)S(1)} %get-tuple-element.76), channel_id=1, source_target_pairs={{0,2},{4,0},{8,4},{12,8},{14,12},{10,14},{6,10},{2,6},{1,3},{5,1},... | collective-permute-start | bytes 602120 | tf_op jit(solution)/shard_map/ppermute | solution.py:546
  35.1 9.6 %collective-permute-start.13 = (bf16[784,128]{1,0:T(8,128)(2,1)S(1)}, bf16[784,128]{1,0:T(8,128)(2,1)S(1)}, u32[]{:S(2)}, u32[]{:S(2)}) collective-permute-start(bf16[784,128]{1,0:T(8,128)(2,1)S(1)} %get-tuple-element.81), channel_id=1, source_target_pairs={{0,4},{4,8},{8,12},{12,14},{14,10},{10,6},{6,2},{2,0},{1,5},{5,9},... | collective-permute-start | bytes 602120 | tf_op jit(solution)/shard_map/ppermute | solution.py:546
  37.4 7.3 %collective-permute-start.14 = (bf16[784,128]{1,0:T(8,128)(2,1)S(1)}, bf16[784,128]{1,0:T(8,128)(2,1)S(1)}, u32[]{:S(2)}, u32[]{:S(2)}) collective-permute-start(bf16[784,128]{1,0:T(8,128)(2,1)S(1)} %get-tuple-element.82), channel_id=1, source_target_pairs={{0,2},{4,0},{8,4},{12,8},{14,12},{10,14},{6,10},{2,6},{1,3},{5,1},... | collective-permute-start | bytes 602120 | tf_op jit(solution)/shard_map/ppermute | solution.py:546
  39.0 6.7 %collective-permute-start.11 = (bf16[784,128]{1,0:T(8,128)(2,1)S(1)}, bf16[784,128]{1,0:T(8,128)(2,1)S(1)}, u32[]{:S(2)}, u32[]{:S(2)}) collective-permute-start(bf16[784,128]{1,0:T(8,128)(2,1)S(1)} %get-tuple-element.79), channel_id=1, source_target_pairs={{0,4},{4,8},{8,12},{12,14},{14,10},{10,6},{6,2},{2,0},{1,5},{5,9},... | collective-permute-start | bytes 602120 | tf_op jit(solution)/shard_map/ppermute | solution.py:546
  41.1 5.7 %collective-permute-start.12 = (bf16[784,128]{1,0:T(8,128)(2,1)S(1)}, bf16[784,128]{1,0:T(8,128)(2,1)S(1)}, u32[]{:S(2)}, u32[]{:S(2)}) collective-permute-start(bf16[784,128]{1,0:T(8,128)(2,1)S(1)} %get-tuple-element.80), channel_id=1, source_target_pairs={{0,2},{4,0},{8,4},{12,8},{14,12},{10,14},{6,10},{2,6},{1,3},{5,1},... | collective-permute-start | bytes 602120 | tf_op jit(solution)/shard_map/ppermute | solution.py:546
  41.1 3.5 %collective-permute-start.15 = (bf16[4,48,128]{2,1,0:T(8,128)(2,1)S(1)}, bf16[4,48,128]{2,1,0:T(8,128)(2,1)S(1)}, u32[]{:S(2)}, u32[]{:S(2)}) collective-permute-start(bf16[4,48,128]{2,1,0:T(8,128)(2,1)S(1)} %cache_attention.2), channel_id=1, source_target_pairs={{0,1},{1,0},{2,3},{3,2},{4,5},{5,4},{6,7},{7,6},{8,9},{9,8},{10,11... | collective-permute-start | bytes 147464 | tf_op jit(solution)/shard_map/ppermute | solution.py:548

commit v17 on v16

--- a/solution.py
+++ b/solution.py
@@ -183,9 +183,8 @@
                 leaves = block_leaves(scales[2 * at + kind, row, :])
                 for tile in range(QBLOCK // 16):
                     rows = pl.ds(pl.multiple_of(step * QBLOCK + 16 * tile, 16), 16)
-                    out[at, rows, kind * HEAD_DIM : (kind + 1) * HEAD_DIM] = selected(
-                        buffer[rows, lanes], leaves
-                    )
+                    half = slice(at % 2 * HEAD_DIM, (at % 2 + 1) * HEAD_DIM)
+                    out[2 * kind + at // 2, rows, half] = selected(buffer[rows, lanes], leaves)
         return 0
 
     steps = depth // QBLOCK
@@ -241,12 +240,13 @@
     width = min(512, line.shape[1])
 
     def scale(x):
-        total[...] = jnp.zeros(total.shape, F32)
+        sums = jnp.zeros((STRETCH, 1), F32)
         for begin in range(0, line.shape[1], width):
             lanes = slice(begin, begin + width)
             wide = x[at, :, lanes].astype(F32)
             line[:, lanes] = (wide * gain[:, lanes]).astype(BF16)
-            total[...] += token_rows(jnp.sum(wide * wide, axis=1, keepdims=True))
+            sums += jnp.sum(wide * wide, axis=1, keepdims=True)
+        total[...] = token_rows(sums)
 
     pl.when((prompt >= 0) & is_own)(lambda: scale(own))
     pl.when((prompt >= 0) & jnp.logical_not(is_own))(lambda: scale(other))
@@ -254,17 +254,23 @@
     pl.when(prompt < 0)(none)
 
 
+def products(line, weight, kind):
+    for pair in range(2):
+        product = jnp.dot(line[...], weight[2 * kind + pair], preferred_element_type=F32)
+        for at in range(2):
+            begin = (2 * pair + at) * STRETCH
+            yield slice(begin, begin + STRETCH), product[:, at * HEAD_DIM : (at + 1) * HEAD_DIM]
+
+
 def line_scratch(x):
     return [pltpu.VMEM(x.shape[1:], BF16), pltpu.VMEM((8, 128), F32)]
 
 
 def first_kernel(distance, targets, own, other, gain, weight, right, left, line, total):
     def some():
-        for head in range(CORE_HEADS):
-            product = jnp.dot(line[...], weight[head], preferred_element_type=F32)
-            rows = slice(head * STRETCH, (head + 1) * STRETCH)
-            right[rows] = product[:, :HEAD_DIM].astype(BF16)
-            left[rows] = product[:, HEAD_DIM:].astype(BF16)
+        for kind, out in enumerate((right, left)):
+            for rows, product in products(line, weight, kind):
+                out[rows] = product.astype(BF16)
         right[CORE_HEADS * STRETCH :] = two_pieces(total[...])
 
     def none():
@@ -297,11 +303,9 @@
     for item, distance in enumerate(distances):
 
         def some(item=item):
-            for head in range(CORE_HEADS):
-                product = jnp.dot(line[...], weight[head], preferred_element_type=F32)
-                rows = slice(head * STRETCH, (head + 1) * STRETCH)
-                out[item, 0, rows] = product[:, :HEAD_DIM]
-                out[item, 1, rows] = product[:, HEAD_DIM:]
+            for kind in range(2):
+                for rows, product in products(line, weight, kind):
+                    out[item, kind, rows] = product
             out[item, 0, CORE_HEADS * STRETCH :] = total[...]
 
         def none(item=item):
@@ -327,12 +331,70 @@
     )(targets, own, other, gain, weight)
 
 
+def early_kernel(distance, targets, own, other, gain, weight, out, lines, totals):
+    for item in range(2):
+        line, total, kind = lines.at[item], totals.at[item], 1 - item
+
+        def some(item=item, line=line, total=total, kind=kind):
+            for rows, product in products(line, weight, kind):
+                out[item, 0, rows] = product
+            if kind == 0:
+                out[item, 0, CORE_HEADS * STRETCH :] = total[...]
+
+        def none(item=item, line=line, total=total):
+            out[item] = jnp.zeros(out.shape[1:], F32)
+            line[...] = jnp.zeros(line.shape, BF16)
+            total[...] = jnp.zeros(total.shape, F32)
+
+        towards = distance * (1 - 2 * item)
+        with_lines(targets, towards, own, other, gain, line, total, some, none)
+
+
+def late_kernel(lines, totals, weight, out):
+    for item in range(2):
+        for rows, product in products(lines.at[item], weight, item):
+            out[item, 0, rows] = product
+    out[0, 0, CORE_HEADS * STRETCH :] = totals[0]
+
+
+def project_early(distance, targets, own, other, gain, weight):
+    return pl.pallas_call(
+        functools.partial(early_kernel, distance),
+        in_specs=[SMEM] + [VMEM] * 4,
+        out_specs=[VMEM] * 3,
+        out_shape=[
+            jax.ShapeDtypeStruct((2, 1, CORE_HEADS * STRETCH + 8, HEAD_DIM), F32),
+            jax.ShapeDtypeStruct((2,) + own.shape[1:], BF16),
+            jax.ShapeDtypeStruct((2, 8, 128), F32),
+        ],
+        compiler_params=pltpu.CompilerParams(vmem_limit_bytes=24 * MIB),
+        cost_estimate=pl.CostEstimate(
+            flops=STRETCH * weight.size, bytes_accessed=weight.size, transcendentals=0
+        ),
+        name="project_early",
+    )(targets, own, other, gain, weight)
+
+
+def project_late(lines, totals, weight):
+    return pl.pallas_call(
+        late_kernel,
+        in_specs=[VMEM] * 3,
+        out_specs=VMEM,
+        out_shape=jax.ShapeDtypeStruct((2, 1, CORE_HEADS * STRETCH + 8, HEAD_DIM), F32),
+        compiler_params=pltpu.CompilerParams(vmem_limit_bytes=24 * MIB),
+        cost_estimate=pl.CostEstimate(
+            flops=STRETCH * weight.size, bytes_accessed=weight.size, transcendentals=0
+        ),
+        name="project_late",
+    )(lines, totals, weight)
+
+
 def send_kernel(half, terms, *refs):
     *arrived, to_right, to_left = refs
     rows = CORE_HEADS * STRETCH
     for item, out in enumerate((to_right, to_left)):
         kind = (half + item) % 2
-        total = terms[item, kind, :rows]
+        total = terms[item, kind % terms.shape[1], :rows]
         if arrived:
             total += arrived[item][:rows].astype(F32)
         out[:rows] = total.astype(BF16)
@@ -558,13 +620,19 @@
     arrived = [pass_on(right, left), []]
 
     for distance in range(half - 1, 0, -1):
-        terms = project([distance, -distance], targets, *features, weight)
+        if distance == half - 1:
+            terms, *kept = project_early(distance, targets, *features, weight)
+        else:
+            terms = project([distance, -distance], targets, *features, weight)
+            kept = terms
         right, left = sends(1, terms, arrived[1])
-        terms, right, left = lax.optimization_barrier((terms, right, left))
+        kept, right, left = lax.optimization_barrier((kept, right, left))
         targets, _ = lax.optimization_barrier((target_rows, left))
         arrived[1] = pass_on(right, left)
+        terms = kept
         if distance == half - 1:
             prepared = prepare(targets, queries, starts, jnp.asarray(turns))
+            terms = project_late(*kept, weight)
             terms, prepared = lax.optimization_barrier((terms, prepared))
             grouped, rotary = prepared
         if distance == max(1, half - 2):

time: 50.7 us -> 49.9 us (0.984)
  waiting for transfers between devices: 5.83 us -> 4.74 us
  Pallas kernels: 24.1 us -> 24.8 us
    ppermute x7, waiting for transfers between devices: 4.2 us -> 1.29 us  [pass_on(): lax.ppermute(right, 'tp', to_right)]
    pallas_call x0 -> x2, Pallas kernels: none -> 2.63 us  [the longest x1 1.61 us: project_early(): pl.pallas_call(functools.partial(early_kernel, distance), in_specs=[SMEM]...]
    pallas_call x4 -> x3, Pallas kernels: 9.07 us -> 7.1 us  [project(): pl.pallas_call(functools.partial(project_kernel, distances), in_specs=[SM...]
    ppermute x7, waiting for transfers between devices: 1.63 us -> 3.44 us  [pass_on(): lax.ppermute(left, 'tp', to_left)]
  transfers between devices with their start and end apart: 16 -> 16, of which waited for: 6 -> 6; matrix products, arithmetic and copies ran while one was open for 0% -> 0% of each run, Pallas kernels for 41% -> 43%
where the time goes in v17:
time: 49.9 us; the launch traced here: 50.2 us
  Pallas kernels  24.8 us (50%)
  starting transfers between devices  17.1 us (34%)
  waiting for transfers between devices  4.74 us (9%)
  blocking collectives  1.85 us (4%)
  between operations  0.95 us (2%)
  local copies, waits for them, and re-layouts  0.68 us (1%)
    ppermute x7, starting transfers between devices, pass_on(): lax.ppermute(right, 'tp', to_right)  12.8 us
    pallas_call x1, Pallas kernels, dequantize(): pl.pallas_call(weights_kernel, grid=(1,), in_specs=[pl.BlockSpec(memory_s...  7.42 us
    pallas_call x3, Pallas kernels, project(): pl.pallas_call(functools.partial(project_kernel, distances), in_specs=[SM...  7.1 us
    ppermute x7, starting transfers between devices, pass_on(): lax.ppermute(left, 'tp', to_left)  3.8 us
    ppermute x7, waiting for transfers between devices, pass_on(): lax.ppermute(left, 'tp', to_left)  3.44 us
    pallas_call x2, Pallas kernels, cache_attention(): pl.pallas_call(functools.partial(cache_kernel, part), in_specs=[SMEM] * 3...  3.18 us
    pallas_call x1, Pallas kernels, project_first(): pl.pallas_call(functools.partial(first_kernel, distance), in_specs=[SMEM]...  1.9 us
    all_gather x1, blocking collectives, per_device(): return lax.all_gather(out, 'rep', axis=2, tiled=True)  1.85 us
  transfers between devices with their start and end apart: 16, of which 6 were waited for; matrix products, arithmetic and copies ran while one was open for 0% of the time, Pallas kernels for 43%

profile of v17, /device:TPU:0, one launch (start us, length us, event | category | flops | bytes accessed | tf_op | source)
XLA Modules:
  0.0 50.2 jit_solution(9222840649876589804)
XLA Ops:
  0.0 0.5 collective-permute-start
  0.5 7.4 %dequantize.1.weight = bf16[4,2048,256]{2,1,0:T(8,128)(2,1)S(1)} custom-call(s32[2048,2048]{1,0:T(8,128)} %codes.1, s32[32,2048]{1,0:T(8,128)} %value_scales.1, s32[32,2048]{1,0:T(8,128)} %value_scales.1, f32[8,32]{1,0:T(8,128)} %bitcast.14), custom_call_target="tpu_custom_call" | custom-call | flops 134217728 | bytes 8388608 | tf_op jit(solution)/shard_map/dequantize/pallas_call | solution.py:203
  7.9 0.0 collective-permute-done.other
  8.0 0.0 copy-start.8
  8.0 1.9 %project_first.1 = (bf16[784,128]{1,0:T(8,128)(2,1)S(1)}, bf16[768,128]{1,0:T(8,128)(2,1)S(1)}) custom-call(s32[6]{0:T(128)S(1)} %copy-done.5, bf16[3,192,2048]{2,1,0:T(8,128)(2,1)S(1)} %bitcast.4, bf16[3,192,2048]{2,1,0:T(8,128)(2,1)S(1)} %collective-permute-done.other, f32[1,2048]{1,0:T(1,128)S(1)} %bitcast.9, bf16[4,2048,256]{2,1,0:T(8,128)(2,1)S(1)} %dequantize.1.weight), custom_call_target="tpu_custom_call" | custom-call | flops 805306368 | bytes 2097152 | tf_op jit(solution)/shard_map/project_first/pallas_call | solution.py:285
  9.9 1.4 %collective-permute-start.1 = (bf16[784,128]{1,0:T(8,128)(2,1)S(1)}, bf16[784,128]{1,0:T(8,128)(2,1)S(1)}, u32[]{:S(2)}, u32[]{:S(2)}) collective-permute-start(bf16[784,128]{1,0:T(8,128)(2,1)S(1)} %get-tuple-element.64), channel_id=1, source_target_pairs={{0,4},{4,8},{8,12},{12,14},{14,10},{10,6},{6,2},{2,0},{1,5},{5,9},... | collective-permute-start | bytes 602120 | tf_op jit(solution)/shard_map/ppermute | solution.py:608
  11.3 1.2 %collective-permute-start.2 = (bf16[768,128]{1,0:T(8,128)(2,1)S(1)}, bf16[768,128]{1,0:T(8,128)(2,1)S(1)}, u32[]{:S(2)}, u32[]{:S(2)}) collective-permute-start(bf16[768,128]{1,0:T(8,128)(2,1)S(1)} %get-tuple-element.49), channel_id=1, source_target_pairs={{0,2},{4,0},{8,4},{12,8},{14,12},{10,14},{6,10},{2,6},{1,3},{5,1},... | collective-permute-start | bytes 589832 | tf_op jit(solution)/shard_map/ppermute | solution.py:608
  12.5 0.1 multiply_cosine_fusion
  12.6 1.6 %project_early.1 = (f32[2,1,776,128]{3,2,1,0:T(8,128)S(1)}, bf16[2,192,2048]{2,1,0:T(8,128)(2,1)S(1)}, f32[2,8,128]{2,1,0:T(8,128)S(1)}) custom-call(s32[6]{0:T(128)S(1)} %copy-done.5, bf16[3,192,2048]{2,1,0:T(8,128)(2,1)S(1)} %bitcast.5, bf16[3,192,2048]{2,1,0:T(8,128)(2,1)S(1)} %collective-permute-done.other, f32[1,2048]{1,0:T(1,128)S(1)} %bitcast.10, ...), custom_call_target="tpu_custom_call" | custom-call | flops 402653184 | bytes 2097152 | tf_op jit(solution)/shard_map/project_early/pallas_call | solution.py:361
  14.3 0.0 copy-start.3
  14.3 0.0 copy-start.4
  14.3 2.5 %collective-permute-start.3 = (bf16[784,128]{1,0:T(8,128)(2,1)S(1)}, bf16[784,128]{1,0:T(8,128)(2,1)S(1)}, u32[]{:S(2)}, u32[]{:S(2)}) collective-permute-start(bf16[784,128]{1,0:T(8,128)(2,1)S(1)} %get-tuple-element.67), channel_id=1, source_target_pairs={{0,4},{4,8},{8,12},{12,14},{14,10},{10,6},{6,2},{2,0},{1,5},{5,9},... | collective-permute-start | bytes 602120 | tf_op jit(solution)/shard_map/ppermute | solution.py:608
  16.8 0.4 collective-permute-start.4
  17.2 1.0 %project_late.1.terms = f32[2,1,776,128]{3,2,1,0:T(8,128)S(1)} custom-call(bf16[2,192,2048]{2,1,0:T(8,128)(2,1)S(1)} %get-tuple-element.56.lines, f32[2,8,128]{2,1,0:T(8,128)S(1)} %get-tuple-element.57.totals, bf16[4,2048,256]{2,1,0:T(8,128)(2,1)S(1)} %dequantize.1.weight), custom_call_target="tpu_custom_call" | custom-call | flops 402653184 | bytes 2097152 | tf_op jit(solution)/shard_map/project_late/pallas_call | solution.py:379
  18.3 0.7 %prepare.1 = (bf16[8,32,128]{2,1,0:T(8,128)(2,1)S(1)}, f32[2,192,128]{2,1,0:T(8,128)S(1)}) custom-call(s32[6]{0:T(128)S(1)} %copy-done.5, bf16[1,2,16384]{2,1,0:T(2,128)(2,1)S(1)} %copy-done.4, f32[2,6,128]{2,1,0:T(8,128)S(1)} %pad_maximum_fusion.starts, f32[2,192,128]{2,1,0:T(8,128)S(1)} %copy-done.3), custom_call_target="tpu_custom_call" | custom-call | tf_op jit(solution)/shard_map/prepare/pallas_call | solution.py:439
  18.9 0.4 collective-permute-done.2.refs_1_
  19.4 0.1 sends.7
  19.5 2.5 %collective-permute-start.5 = (bf16[784,128]{1,0:T(8,128)(2,1)S(1)}, bf16[784,128]{1,0:T(8,128)(2,1)S(1)}, u32[]{:S(2)}, u32[]{:S(2)}) collective-permute-start(bf16[784,128]{1,0:T(8,128)(2,1)S(1)} %get-tuple-element.75), channel_id=1, source_target_pairs={{0,4},{4,8},{8,12},{12,14},{14,10},{10,6},{6,2},{2,0},{1,5},{5,9},... | collective-permute-start | bytes 602120 | tf_op jit(solution)/shard_map/ppermute | solution.py:608
  22.0 0.0 collective-permute-start.6
  22.7 0.0 copy-start.1
  22.7 0.0 copy-start.6
  22.7 3.2 %project.3.terms = f32[2,2,776,128]{3,2,1,0:T(8,128)S(1)} custom-call(s32[6]{0:T(128)S(1)} %copy-done.5, bf16[3,192,2048]{2,1,0:T(8,128)(2,1)S(1)} %bitcast.6, bf16[3,192,2048]{2,1,0:T(8,128)(2,1)S(1)} %collective-permute-done.other, f32[1,2048]{1,0:T(1,128)S(1)} %bitcast.11, bf16[4,2048,256]{2,1,0:T(8,128)(2,1)S(1)} %dequantize.1.weight), custom_call_target="tpu_custom_call" | custom-call | flops 805306368 | bytes 2097152 | tf_op jit(solution)/shard_map/project/pallas_call | solution.py:318
  25.9 0.1 sends.8
  26.0 0.1 collective-permute-start.8
  26.1 2.3 %collective-permute-start.7 = (bf16[784,128]{1,0:T(8,128)(2,1)S(1)}, bf16[784,128]{1,0:T(8,128)(2,1)S(1)}, u32[]{:S(2)}, u32[]{:S(2)}) collective-permute-start(bf16[784,128]{1,0:T(8,128)(2,1)S(1)} %get-tuple-element.79), channel_id=1, source_target_pairs={{0,4},{4,8},{8,12},{12,14},{14,10},{10,6},{6,2},{2,0},{1,5},{5,9},... | collective-permute-start | bytes 602120 | tf_op jit(solution)/shard_map/ppermute | solution.py:608
  28.4 1.6 %cache_attention.2 = bf16[4,48,128]{2,1,0:T(8,128)(2,1)S(1)} custom-call(s32[6]{0:T(128)S(1)} %copy-done.5, s32[6]{0:T(128)S(1)} %copy-done.7, s32[1]{0:T(128)S(6)} %copy.15.stored, bf16[8,32,128]{2,1,0:T(8,128)(2,1)S(1)} %get-tuple-element.73.q.grouped, bf16[1,1024,2048]{2,1,0:T(8,128)(2,1)S(1)} %copy-done.1, bf16[1,2,2048]{2,1,0:T(2,128)(2,1)S(1)} %copy-done.6), custom_call_target="tpu_custom_call" | custom-call | flops 1 | bytes 1 | tf_op jit(solution)/shard_map/cache_attention/pallas_call | solution.py:503
  30.0 0.0 collective-permute-done.6.refs_1_
  30.0 0.1 sends.9
  30.1 1.8 %collective-permute-start.9 = (bf16[784,128]{1,0:T(8,128)(2,1)S(1)}, bf16[784,128]{1,0:T(8,128)(2,1)S(1)}, u32[]{:S(2)}, u32[]{:S(2)}) collective-permute-start(bf16[784,128]{1,0:T(8,128)(2,1)S(1)} %get-tuple-element.83), channel_id=1, source_target_pairs={{0,4},{4,8},{8,12},{12,14},{14,10},{10,6},{6,2},{2,0},{1,5},{5,9},... | collective-permute-start | bytes 602120 | tf_op jit(solution)/shard_map/ppermute | solution.py:608
  31.9 0.2 collective-permute-start.10
  32.1 3.2 %project.4.terms = f32[2,2,776,128]{3,2,1,0:T(8,128)S(1)} custom-call(s32[6]{0:T(128)S(1)} %copy-done.5, bf16[3,192,2048]{2,1,0:T(8,128)(2,1)S(1)} %bitcast.7, bf16[3,192,2048]{2,1,0:T(8,128)(2,1)S(1)} %collective-permute-done.other, f32[1,2048]{1,0:T(1,128)S(1)} %bitcast.12, bf16[4,2048,256]{2,1,0:T(8,128)(2,1)S(1)} %dequantize.1.weight), custom_call_target="tpu_custom_call" | custom-call | flops 805306368 | bytes 2097152 | tf_op jit(solution)/shard_map/project/pallas_call | solution.py:318
  35.4 0.0 collective-permute-done.7.refs_0_
  35.4 0.1 sends.10
  35.5 0.8 %collective-permute-start.13 = (bf16[784,128]{1,0:T(8,128)(2,1)S(1)}, bf16[784,128]{1,0:T(8,128)(2,1)S(1)}, u32[]{:S(2)}, u32[]{:S(2)}) collective-permute-start(bf16[784,128]{1,0:T(8,128)(2,1)S(1)} %get-tuple-element.89), channel_id=1, source_target_pairs={{0,4},{4,8},{8,12},{12,14},{14,10},{10,6},{6,2},{2,0},{1,5},{5,9},... | collective-permute-start | bytes 602120 | tf_op jit(solution)/shard_map/ppermute | solution.py:608
  36.3 1.3 %collective-permute-start.14 = (bf16[784,128]{1,0:T(8,128)(2,1)S(1)}, bf16[784,128]{1,0:T(8,128)(2,1)S(1)}, u32[]{:S(2)}, u32[]{:S(2)}) collective-permute-start(bf16[784,128]{1,0:T(8,128)(2,1)S(1)} %get-tuple-element.90), channel_id=1, source_target_pairs={{0,2},{4,0},{8,4},{12,8},{14,12},{10,14},{6,10},{2,6},{1,3},{5,1},... | collective-permute-start | bytes 602120 | tf_op jit(solution)/shard_map/ppermute | solution.py:608
  37.6 0.4 collective-permute-done.9.refs_0_
  38.0 1.0 %collective-permute-done.10.refs_1_ = bf16[784,128]{1,0:T(8,128)(2,1)S(1)} collective-permute-done((bf16[784,128]{1,0:T(8,128)(2,1)S(1)}, bf16[784,128]{1,0:T(8,128)(2,1)S(1)}, u32[]{:S(2)}, u32[]{:S(2)}) %collective-permute-start.10) | collective-permute-done | bytes 200736 | tf_op jit(solution)/shard_map/ppermute | solution.py:608
  39.0 0.1 sends.11
  39.1 1.5 %collective-permute-start.11 = (bf16[784,128]{1,0:T(8,128)(2,1)S(1)}, bf16[784,128]{1,0:T(8,128)(2,1)S(1)}, u32[]{:S(2)}, u32[]{:S(2)}) collective-permute-start(bf16[784,128]{1,0:T(8,128)(2,1)S(1)} %get-tuple-element.87), channel_id=1, source_target_pairs={{0,4},{4,8},{8,12},{12,14},{14,10},{10,6},{6,2},{2,0},{1,5},{5,9},... | collective-permute-start | bytes 602120 | tf_op jit(solution)/shard_map/ppermute | solution.py:608
  40.6 0.6 %collective-permute-start.12 = (bf16[784,128]{1,0:T(8,128)(2,1)S(1)}, bf16[784,128]{1,0:T(8,128)(2,1)S(1)}, u32[]{:S(2)}, u32[]{:S(2)}) collective-permute-start(bf16[784,128]{1,0:T(8,128)(2,1)S(1)} %get-tuple-element.88), channel_id=1, source_target_pairs={{0,2},{4,0},{8,4},{12,8},{14,12},{10,14},{6,10},{2,6},{1,3},{5,1},... | collective-permute-start | bytes 602120 | tf_op jit(solution)/shard_map/ppermute | solution.py:608
  41.2 1.6 %cache_attention.3.cached_here = bf16[4,48,128]{2,1,0:T(8,128)(2,1)S(1)} custom-call(s32[6]{0:T(128)S(1)} %copy-done.5, s32[6]{0:T(128)S(1)} %copy-done.7, s32[1]{0:T(128)S(6)} %copy.15.stored, bf16[8,32,128]{2,1,0:T(8,128)(2,1)S(1)} %get-tuple-element.73.q.grouped, bf16[1,1024,2048]{2,1,0:T(8,128)(2,1)S(1)} %copy-done.1, bf16[1,2,2048]{2,1,0:T(2,128)(2,1)S(1)} %copy-done.6), custom_call_target="tpu_custom_call" | custom-call | flops 1 | bytes 1 | tf_op jit(solution)/shard_map/cache_attention/pallas_call | solution.py:503
  42.8 0.6 %project.5.own = f32[1,2,776,128]{3,2,1,0:T(8,128)S(1)} custom-call(s32[6]{0:T(128)S(1)} %copy-done.5, bf16[3,192,2048]{2,1,0:T(8,128)(2,1)S(1)} %bitcast.8, bf16[3,192,2048]{2,1,0:T(8,128)(2,1)S(1)} %collective-permute-done.other, f32[1,2048]{1,0:T(1,128)S(1)} %bitcast.13, bf16[4,2048,256]{2,1,0:T(8,128)(2,1)S(1)} %dequantize.1.weight), custom_call_target="tpu_custom_call" | custom-call | flops 402653184 | bytes 2097152 | tf_op jit(solution)/shard_map/project/pallas_call | solution.py:318
  43.4 0.6 %collective-permute-done.14.left_keys = bf16[784,128]{1,0:T(8,128)(2,1)S(1)} collective-permute-done((bf16[784,128]{1,0:T(8,128)(2,1)S(1)}, bf16[784,128]{1,0:T(8,128)(2,1)S(1)}, u32[]{:S(2)}, u32[]{:S(2)}) %collective-permute-start.14) | collective-permute-done | bytes 200736 | tf_op jit(solution)/shard_map/ppermute | solution.py:608
  44.1 0.9 %collective-permute-done.11.right_keys = bf16[784,128]{1,0:T(8,128)(2,1)S(1)} collective-permute-done((bf16[784,128]{1,0:T(8,128)(2,1)S(1)}, bf16[784,128]{1,0:T(8,128)(2,1)S(1)}, u32[]{:S(2)}, u32[]{:S(2)}) %collective-permute-start.11) | collective-permute-done | bytes 200736 | tf_op jit(solution)/shard_map/ppermute | solution.py:608
  45.0 1.4 %collective-permute-done.12.left_values = bf16[784,128]{1,0:T(8,128)(2,1)S(1)} collective-permute-done((bf16[784,128]{1,0:T(8,128)(2,1)S(1)}, bf16[784,128]{1,0:T(8,128)(2,1)S(1)}, u32[]{:S(2)}, u32[]{:S(2)}) %collective-permute-start.12) | collective-permute-done | bytes 200736 | tf_op jit(solution)/shard_map/ppermute | solution.py:608
  46.3 1.4 %finish.1 = bf16[1,2,8192]{2,1,0:T(2,128)(2,1)S(1)} custom-call(s32[6]{0:T(128)S(1)} %copy-done.5, f32[2,192,128]{2,1,0:T(8,128)S(1)} %get-tuple-element.62.rotary, f32[1,2,776,128]{3,2,1,0:T(8,128)S(1)} %project.5.own, bf16[784,128]{1,0:T(8,128)(2,1)S(1)} %collective-permute-done.11.right_keys, bf16[784,128]{1,0:T(8,128)(2,1)S(1)} %collective-permute-done.12.left_values, ...), custom_call_target="tpu_custom_call" | custom-call | tf_op jit(solution)/shard_map/finish/pallas_call | solution.py:569
  47.7 1.9 %all_gather.3 = bf16[1,2,16384]{2,1,0:T(2,128)(2,1)S(1)} all-gather(bf16[1,2,8192]{2,1,0:T(2,128)(2,1)S(1)} %finish.1), channel_id=1, replica_groups=mesh['grp'=2,'tp'=8,'rep'=2] {'rep'}, dimensions={2}, use_global_device_ids=true | all-gather | bytes 98304 | tf_op jit(solution)/shard_map/all_gather | solution.py:654
  49.5 0.6 %copy.16 = bf16[1,2,16384]{2,1,0:T(2,128)(2,1)} copy(bf16[1,2,16384]{2,1,0:T(2,128)(2,1)S(1)} %all_gather.3) | data formatting | bytes 131072
  (24 shorter events, 0.1 us)
Async XLA Ops:
  0.0 7.9 %collective-permute-start = (bf16[3,192,2048]{2,1,0:T(8,128)(2,1)}, bf16[3,192,2048]{2,1,0:T(8,128)(2,1)S(1)}, u32[]{:S(2)}, u32[]{:S(2)}) collective-permute-start(bf16[3,192,2048]{2,1,0:T(8,128)(2,1)} %bitcast.3), channel_id=1, source_target_pairs={{0,1},{1,0},{2,3},{3,2},{4,5},{5,4},{6,7},{7,6},{8,9},{9,8},{10,11... | collective-permute-start | bytes 7077896 | tf_op jit(solution)/shard_map/ppermute | solution.py:610
  0.5 7.4 %copy-start.7 = (s32[6]{0:T(128)S(1)}, s32[6]{0:T(128)}, u32[]{:S(2)}) copy-start(s32[6]{0:T(128)} %lengths.3) | copy-start | bytes 76
  0.5 7.5 %copy-start = (bf16[192,3,2048]{2,0,1:T(8,128)(2,1)S(1)}, bf16[192,3,2048]{2,0,1:T(8,128)(2,1)}, u32[]{:S(2)}) copy-start(bf16[192,3,2048]{2,0,1:T(8,128)(2,1)} %param.13) | copy-start | bytes 7077892
  0.5 7.5 %copy-start.2 = (f32[2048]{0:T(1024)S(1)}, f32[2048]{0:T(1024)}, u32[]{:S(2)}) copy-start(f32[2048]{0:T(1024)} %param.14) | copy-start | bytes 24580
  0.5 7.5 %copy-start.5 = (s32[6]{0:T(128)S(1)}, s32[6]{0:T(128)}, u32[]{:S(2)}) copy-start(s32[6]{0:T(128)} %targets.10) | copy-start | bytes 76
  8.0 4.5 %copy-start.8 = (f32[128]{0:T(128)S(1)}, f32[128]{0:T(128)}, u32[]{:S(2)}) copy-start(f32[128]{0:T(128)} %constant.7.clone) | copy-start | bytes 1540
  9.9 9.5 %collective-permute-start.1 = (bf16[784,128]{1,0:T(8,128)(2,1)S(1)}, bf16[784,128]{1,0:T(8,128)(2,1)S(1)}, u32[]{:S(2)}, u32[]{:S(2)}) collective-permute-start(bf16[784,128]{1,0:T(8,128)(2,1)S(1)} %get-tuple-element.64), channel_id=1, source_target_pairs={{0,4},{4,8},{8,12},{12,14},{14,10},{10,6},{6,2},{2,0},{1,5},{5,9},... | collective-permute-start | bytes 602120 | tf_op jit(solution)/shard_map/ppermute | solution.py:608
  11.3 8.1 %collective-permute-start.2 = (bf16[768,128]{1,0:T(8,128)(2,1)S(1)}, bf16[768,128]{1,0:T(8,128)(2,1)S(1)}, u32[]{:S(2)}, u32[]{:S(2)}) collective-permute-start(bf16[768,128]{1,0:T(8,128)(2,1)S(1)} %get-tuple-element.49), channel_id=1, source_target_pairs={{0,2},{4,0},{8,4},{12,8},{14,12},{10,14},{6,10},{2,6},{1,3},{5,1},... | collective-permute-start | bytes 589832 | tf_op jit(solution)/shard_map/ppermute | solution.py:608
  14.3 4.0 %copy-start.3 = (f32[2,192,128]{2,1,0:T(8,128)S(1)}, f32[2,192,128]{2,1,0:T(8,128)}, u32[]{:S(2)}) copy-start(f32[2,192,128]{2,1,0:T(8,128)} %constant.8.clone.turns) | copy-start | bytes 589828
  14.3 4.0 %copy-start.4 = (bf16[1,2,16384]{2,1,0:T(2,128)(2,1)S(1)}, bf16[1,2,16384]{2,1,0:T(2,128)(2,1)}, u32[]{:S(2)}) copy-start(bf16[1,2,16384]{2,1,0:T(2,128)(2,1)} %queries.1) | copy-start | bytes 196612
  14.3 11.6 %collective-permute-start.3 = (bf16[784,128]{1,0:T(8,128)(2,1)S(1)}, bf16[784,128]{1,0:T(8,128)(2,1)S(1)}, u32[]{:S(2)}, u32[]{:S(2)}) collective-permute-start(bf16[784,128]{1,0:T(8,128)(2,1)S(1)} %get-tuple-element.67), channel_id=1, source_target_pairs={{0,4},{4,8},{8,12},{12,14},{14,10},{10,6},{6,2},{2,0},{1,5},{5,9},... | collective-permute-start | bytes 602120 | tf_op jit(solution)/shard_map/ppermute | solution.py:608
  16.8 9.1 %collective-permute-start.4 = (bf16[784,128]{1,0:T(8,128)(2,1)S(1)}, bf16[784,128]{1,0:T(8,128)(2,1)S(1)}, u32[]{:S(2)}, u32[]{:S(2)}) collective-permute-start(bf16[784,128]{1,0:T(8,128)(2,1)S(1)} %get-tuple-element.58), channel_id=1, source_target_pairs={{0,2},{4,0},{8,4},{12,8},{14,12},{10,14},{6,10},{2,6},{1,3},{5,1},... | collective-permute-start | bytes 602120 | tf_op jit(solution)/shard_map/ppermute | solution.py:608
  19.5 10.5 %collective-permute-start.5 = (bf16[784,128]{1,0:T(8,128)(2,1)S(1)}, bf16[784,128]{1,0:T(8,128)(2,1)S(1)}, u32[]{:S(2)}, u32[]{:S(2)}) collective-permute-start(bf16[784,128]{1,0:T(8,128)(2,1)S(1)} %get-tuple-element.75), channel_id=1, source_target_pairs={{0,4},{4,8},{8,12},{12,14},{14,10},{10,6},{6,2},{2,0},{1,5},{5,9},... | collective-permute-start | bytes 602120 | tf_op jit(solution)/shard_map/ppermute | solution.py:608
  22.0 8.0 %collective-permute-start.6 = (bf16[784,128]{1,0:T(8,128)(2,1)S(1)}, bf16[784,128]{1,0:T(8,128)(2,1)S(1)}, u32[]{:S(2)}, u32[]{:S(2)}) collective-permute-start(bf16[784,128]{1,0:T(8,128)(2,1)S(1)} %get-tuple-element.76), channel_id=1, source_target_pairs={{0,2},{4,0},{8,4},{12,8},{14,12},{10,14},{6,10},{2,6},{1,3},{5,1},... | collective-permute-start | bytes 602120 | tf_op jit(solution)/shard_map/ppermute | solution.py:608
  22.7 5.7 %copy-start.1 = (bf16[1,1024,2048]{2,1,0:T(8,128)(2,1)S(1)}, bf16[1,1024,2048]{2,1,0:T(8,128)(2,1)}, u32[]{:S(2)}) copy-start(bf16[1,1024,2048]{2,1,0:T(8,128)(2,1)} %cache.3) | copy-start | bytes 12582916
  22.7 5.7 %copy-start.6 = (bf16[1,2,2048]{2,1,0:T(2,128)(2,1)S(1)}, bf16[1,2,2048]{2,1,0:T(2,128)(2,1)}, u32[]{:S(2)}) copy-start(bf16[1,2,2048]{2,1,0:T(2,128)(2,1)} %new.3) | copy-start | bytes 24580
  26.0 9.4 %collective-permute-start.8 = (bf16[784,128]{1,0:T(8,128)(2,1)S(1)}, bf16[784,128]{1,0:T(8,128)(2,1)S(1)}, u32[]{:S(2)}, u32[]{:S(2)}) collective-permute-start(bf16[784,128]{1,0:T(8,128)(2,1)S(1)} %get-tuple-element.71), channel_id=1, source_target_pairs={{0,2},{4,0},{8,4},{12,8},{14,12},{10,14},{6,10},{2,6},{1,3},{5,1},... | collective-permute-start | bytes 602120 | tf_op jit(solution)/shard_map/ppermute | solution.py:608
  26.1 9.3 %collective-permute-start.7 = (bf16[784,128]{1,0:T(8,128)(2,1)S(1)}, bf16[784,128]{1,0:T(8,128)(2,1)S(1)}, u32[]{:S(2)}, u32[]{:S(2)}) collective-permute-start(bf16[784,128]{1,0:T(8,128)(2,1)S(1)} %get-tuple-element.79), channel_id=1, source_target_pairs={{0,4},{4,8},{8,12},{12,14},{14,10},{10,6},{6,2},{2,0},{1,5},{5,9},... | collective-permute-start | bytes 602120 | tf_op jit(solution)/shard_map/ppermute | solution.py:608
  30.1 7.9 %collective-permute-start.9 = (bf16[784,128]{1,0:T(8,128)(2,1)S(1)}, bf16[784,128]{1,0:T(8,128)(2,1)S(1)}, u32[]{:S(2)}, u32[]{:S(2)}) collective-permute-start(bf16[784,128]{1,0:T(8,128)(2,1)S(1)} %get-tuple-element.83), channel_id=1, source_target_pairs={{0,4},{4,8},{8,12},{12,14},{14,10},{10,6},{6,2},{2,0},{1,5},{5,9},... | collective-permute-start | bytes 602120 | tf_op jit(solution)/shard_map/ppermute | solution.py:608
  31.9 7.1 %collective-permute-start.10 = (bf16[784,128]{1,0:T(8,128)(2,1)S(1)}, bf16[784,128]{1,0:T(8,128)(2,1)S(1)}, u32[]{:S(2)}, u32[]{:S(2)}) collective-permute-start(bf16[784,128]{1,0:T(8,128)(2,1)S(1)} %get-tuple-element.84), channel_id=1, source_target_pairs={{0,2},{4,0},{8,4},{12,8},{14,12},{10,14},{6,10},{2,6},{1,3},{5,1},... | collective-permute-start | bytes 602120 | tf_op jit(solution)/shard_map/ppermute | solution.py:608
  35.5 7.9 %collective-permute-start.13 = (bf16[784,128]{1,0:T(8,128)(2,1)S(1)}, bf16[784,128]{1,0:T(8,128)(2,1)S(1)}, u32[]{:S(2)}, u32[]{:S(2)}) collective-permute-start(bf16[784,128]{1,0:T(8,128)(2,1)S(1)} %get-tuple-element.89), channel_id=1, source_target_pairs={{0,4},{4,8},{8,12},{12,14},{14,10},{10,6},{6,2},{2,0},{1,5},{5,9},... | collective-permute-start | bytes 602120 | tf_op jit(solution)/shard_map/ppermute | solution.py:608
  36.3 7.8 %collective-permute-start.14 = (bf16[784,128]{1,0:T(8,128)(2,1)S(1)}, bf16[784,128]{1,0:T(8,128)(2,1)S(1)}, u32[]{:S(2)}, u32[]{:S(2)}) collective-permute-start(bf16[784,128]{1,0:T(8,128)(2,1)S(1)} %get-tuple-element.90), channel_id=1, source_target_pairs={{0,2},{4,0},{8,4},{12,8},{14,12},{10,14},{6,10},{2,6},{1,3},{5,1},... | collective-permute-start | bytes 602120 | tf_op jit(solution)/shard_map/ppermute | solution.py:608
  39.1 5.9 %collective-permute-start.11 = (bf16[784,128]{1,0:T(8,128)(2,1)S(1)}, bf16[784,128]{1,0:T(8,128)(2,1)S(1)}, u32[]{:S(2)}, u32[]{:S(2)}) collective-permute-start(bf16[784,128]{1,0:T(8,128)(2,1)S(1)} %get-tuple-element.87), channel_id=1, source_target_pairs={{0,4},{4,8},{8,12},{12,14},{14,10},{10,6},{6,2},{2,0},{1,5},{5,9},... | collective-permute-start | bytes 602120 | tf_op jit(solution)/shard_map/ppermute | solution.py:608
  40.6 5.7 %collective-permute-start.12 = (bf16[784,128]{1,0:T(8,128)(2,1)S(1)}, bf16[784,128]{1,0:T(8,128)(2,1)S(1)}, u32[]{:S(2)}, u32[]{:S(2)}) collective-permute-start(bf16[784,128]{1,0:T(8,128)(2,1)S(1)} %get-tuple-element.88), channel_id=1, source_target_pairs={{0,2},{4,0},{8,4},{12,8},{14,12},{10,14},{6,10},{2,6},{1,3},{5,1},... | collective-permute-start | bytes 602120 | tf_op jit(solution)/shard_map/ppermute | solution.py:608
  41.2 2.9 %collective-permute-start.15 = (bf16[4,48,128]{2,1,0:T(8,128)(2,1)S(1)}, bf16[4,48,128]{2,1,0:T(8,128)(2,1)S(1)}, u32[]{:S(2)}, u32[]{:S(2)}) collective-permute-start(bf16[4,48,128]{2,1,0:T(8,128)(2,1)S(1)} %cache_attention.2), channel_id=1, source_target_pairs={{0,1},{1,0},{2,3},{3,2},{4,5},{5,4},{6,7},{7,6},{8,9},{9,8},{10,11... | collective-permute-start | bytes 147464 | tf_op jit(solution)/shard_map/ppermute | solution.py:610

commit v18 on v17

--- a/solution.py
+++ b/solution.py
@@ -457,7 +457,7 @@
     length = cache.shape[1]
     prompt = prompt_of(targets, here)
     handed = lengths[jnp.maximum(prompt, 0)] - STRETCH
-    span = jnp.where(prompt >= 0, handed, stored[0]) - rep * length
+    span = jnp.where(prompt >= 0, handed, stored[...]) - rep * length
     count = CORE_HEADS * ROWS
     allowed = lax.broadcasted_iota(jnp.int32, (count, length), 1) < span
     second_step = lax.broadcasted_iota(jnp.int32, (count, 1), 0) % STEPS == 1
@@ -502,7 +502,7 @@
 def cache_attention(part, targets, lengths, stored, grouped, kv_cache, new_kv):
     return pl.pallas_call(
         functools.partial(cache_kernel, part),
-        in_specs=[SMEM] * 3 + [VMEM] * 3,
+        in_specs=[SMEM] * 2 + [VMEM] * 4,
         out_specs=VMEM,
         out_shape=jax.ShapeDtypeStruct((CORE_HEADS, PART, HEAD_DIM), BF16),
         compiler_params=pltpu.CompilerParams(vmem_limit_bytes=16 * MIB),
@@ -510,7 +510,7 @@
             flops=1, bytes_accessed=1, transcendentals=0
         ),
         name="cache_attention",
-    )(targets, lengths, stored, grouped, kv_cache, new_kv)
+    )(targets, lengths, stored.reshape(1, 1), grouped, kv_cache, new_kv)
 
 
 def final_kernel(
@@ -620,22 +620,22 @@
     arrived = [pass_on(right, left), []]
 
     for distance in range(half - 1, 0, -1):
-        if distance == half - 1:
+        split = distance >= half - 2
+        if split:
             terms, *kept = project_early(distance, targets, *features, weight)
         else:
             terms = project([distance, -distance], targets, *features, weight)
             kept = terms
         right, left = sends(1, terms, arrived[1])
         kept, right, left = lax.optimization_barrier((kept, right, left))
-        targets, _ = lax.optimization_barrier((target_rows, left))
+        targets, _, _ = lax.optimization_barrier((target_rows, right, left))
         arrived[1] = pass_on(right, left)
-        terms = kept
+        terms = project_late(*kept, weight) if split else kept
         if distance == half - 1:
             prepared = prepare(targets, queries, starts, jnp.asarray(turns))
-            terms = project_late(*kept, weight)
             terms, prepared = lax.optimization_barrier((terms, prepared))
             grouped, rotary = prepared
-        if distance == max(1, half - 2):
+        if distance == 1:
             cached = cache_attention(
                 0, targets, prompt_lengths, cache_lengths, grouped, kv_cache, new_kv
             )

time: 49.9 us -> 50.6 us (1.014); the launches traced: 50.2 us -> 50.3 us
  starting transfers between devices: 17.1 us -> 15.6 us
  waiting for transfers between devices: 4.74 us -> 6.01 us
    pallas_call x3 -> x2, Pallas kernels: 7.1 us -> 4.05 us  [project(): pl.pallas_call(functools.partial(project_kernel, distances), in_specs=[SM...]
    ppermute x7, starting transfers between devices: 12.8 us -> 10.3 us  [pass_on(): lax.ppermute(right, 'tp', to_right)]
    pallas_call x1 -> x2, Pallas kernels: 1.61 us -> 4.05 us  [project_early(): pl.pallas_call(functools.partial(early_kernel, distance), in_specs=[SMEM]...]
    ppermute x7, waiting for transfers between devices: 3.44 us -> 4.92 us  [pass_on(): lax.ppermute(left, 'tp', to_left)]
    pallas_call x1 -> x2, Pallas kernels: 1.03 us -> 2.07 us  [project_late(): pl.pallas_call(late_kernel, in_specs=[VMEM] * 3, out_specs=VMEM, out_shap...]
    ppermute x7, starting transfers between devices: 3.8 us -> 4.76 us  [pass_on(): lax.ppermute(left, 'tp', to_left)]
where the time goes in v18:
time: 50.6 us; the launch traced here: 50.3 us
  Pallas kernels  25.2 us (50%)
  starting transfers between devices  15.6 us (31%)
  waiting for transfers between devices  6.01 us (12%)
  blocking collectives  1.85 us (4%)
  between operations  0.94 us (2%)
  local copies, waits for them, and re-layouts  0.68 us (1%)
    ppermute x7, starting transfers between devices, pass_on(): lax.ppermute(right, 'tp', to_right)  10.3 us
    pallas_call x1, Pallas kernels, dequantize(): pl.pallas_call(weights_kernel, grid=(1,), in_specs=[pl.BlockSpec(memory_s...  7.42 us
    ppermute x7, waiting for transfers between devices, pass_on(): lax.ppermute(left, 'tp', to_left)  4.92 us
    ppermute x7, starting transfers between devices, pass_on(): lax.ppermute(left, 'tp', to_left)  4.76 us
    pallas_call x2, Pallas kernels, project(): pl.pallas_call(functools.partial(project_kernel, distances), in_specs=[SM...  4.05 us
    pallas_call x2, Pallas kernels, project_early(): pl.pallas_call(functools.partial(early_kernel, distance), in_specs=[SMEM]...  4.05 us
    pallas_call x2, Pallas kernels, cache_attention(): pl.pallas_call(functools.partial(cache_kernel, part), in_specs=[SMEM] * 2...  3.13 us
    pallas_call x2, Pallas kernels, project_late(): pl.pallas_call(late_kernel, in_specs=[VMEM] * 3, out_specs=VMEM, out_shap...  2.07 us
  transfers between devices with their start and end apart: 16, of which 6 were waited for; matrix products, arithmetic and copies ran while one was open for 0% of the time, Pallas kernels for 43%

profile of v18, /device:TPU:0, one launch (start us, length us, event | category | flops | bytes accessed | tf_op | source)
XLA Modules:
  0.0 50.3 jit_solution(11076083632481591999)
XLA Ops:
  0.0 0.5 collective-permute-start
  0.5 7.4 %dequantize.1.weight = bf16[4,2048,256]{2,1,0:T(8,128)(2,1)S(1)} custom-call(s32[2048,2048]{1,0:T(8,128)} %codes.1, s32[32,2048]{1,0:T(8,128)} %value_scales.1, s32[32,2048]{1,0:T(8,128)} %value_scales.1, f32[8,32]{1,0:T(8,128)} %bitcast.17), custom_call_target="tpu_custom_call" | custom-call | flops 134217728 | bytes 8388608 | tf_op jit(solution)/shard_map/dequantize/pallas_call | solution.py:203
  7.9 0.0 collective-permute-done.other
  8.0 0.0 copy-start.8
  8.0 1.9 %project_first.1 = (bf16[784,128]{1,0:T(8,128)(2,1)S(1)}, bf16[768,128]{1,0:T(8,128)(2,1)S(1)}) custom-call(s32[6]{0:T(128)S(1)} %copy-done.5, bf16[3,192,2048]{2,1,0:T(8,128)(2,1)S(1)} %bitcast.7, bf16[3,192,2048]{2,1,0:T(8,128)(2,1)S(1)} %collective-permute-done.other, f32[1,2048]{1,0:T(1,128)S(1)} %bitcast.12, bf16[4,2048,256]{2,1,0:T(8,128)(2,1)S(1)} %dequantize.1.weight), custom_call_target="tpu_custom_call" | custom-call | flops 805306368 | bytes 2097152 | tf_op jit(solution)/shard_map/project_first/pallas_call | solution.py:285
  9.9 2.6 %collective-permute-start.1 = (bf16[784,128]{1,0:T(8,128)(2,1)S(1)}, bf16[784,128]{1,0:T(8,128)(2,1)S(1)}, u32[]{:S(2)}, u32[]{:S(2)}) collective-permute-start(bf16[784,128]{1,0:T(8,128)(2,1)S(1)} %get-tuple-element.69), channel_id=1, source_target_pairs={{0,4},{4,8},{8,12},{12,14},{14,10},{10,6},{6,2},{2,0},{1,5},{5,9},... | collective-permute-start | bytes 602120 | tf_op jit(solution)/shard_map/ppermute | solution.py:608
  12.5 0.1 multiply_cosine_fusion
  12.6 0.0 copy-start.3
  12.7 0.0 copy-start.4
  12.7 2.4 %project_early.2 = (f32[2,1,776,128]{3,2,1,0:T(8,128)S(1)}, bf16[2,192,2048]{2,1,0:T(8,128)(2,1)S(1)}, f32[2,8,128]{2,1,0:T(8,128)S(1)}) custom-call(s32[6]{0:T(128)S(1)} %copy-done.5, bf16[3,192,2048]{2,1,0:T(8,128)(2,1)S(1)} %bitcast.8, bf16[3,192,2048]{2,1,0:T(8,128)(2,1)S(1)} %collective-permute-done.other, f32[1,2048]{1,0:T(1,128)S(1)} %bitcast.13, ...), custom_call_target="tpu_custom_call" | custom-call | flops 402653184 | bytes 2097152 | tf_op jit(solution)/shard_map/project_early/pallas_call | solution.py:361
  15.2 2.1 %collective-permute-start.3 = (bf16[784,128]{1,0:T(8,128)(2,1)S(1)}, bf16[784,128]{1,0:T(8,128)(2,1)S(1)}, u32[]{:S(2)}, u32[]{:S(2)}) collective-permute-start(bf16[784,128]{1,0:T(8,128)(2,1)S(1)} %get-tuple-element.62), channel_id=1, source_target_pairs={{0,4},{4,8},{8,12},{12,14},{14,10},{10,6},{6,2},{2,0},{1,5},{5,9},... | collective-permute-start | bytes 602120 | tf_op jit(solution)/shard_map/ppermute | solution.py:608
  17.2 0.0 collective-permute-start.4
  17.2 0.7 %prepare.1 = (bf16[8,32,128]{2,1,0:T(8,128)(2,1)S(1)}, f32[2,192,128]{2,1,0:T(8,128)S(1)}) custom-call(s32[6]{0:T(128)S(1)} %copy-done.5, bf16[1,2,16384]{2,1,0:T(2,128)(2,1)S(1)} %copy-done.4, f32[2,6,128]{2,1,0:T(8,128)S(1)} %pad_maximum_fusion.starts, f32[2,192,128]{2,1,0:T(8,128)S(1)} %copy-done.3), custom_call_target="tpu_custom_call" | custom-call | tf_op jit(solution)/shard_map/prepare/pallas_call | solution.py:439
  17.9 1.0 %project_late.2.terms = f32[2,1,776,128]{3,2,1,0:T(8,128)S(1)} custom-call(bf16[2,192,2048]{2,1,0:T(8,128)(2,1)S(1)} %get-tuple-element.60.lines, f32[2,8,128]{2,1,0:T(8,128)S(1)} %get-tuple-element.61.totals, bf16[4,2048,256]{2,1,0:T(8,128)(2,1)S(1)} %dequantize.1.weight), custom_call_target="tpu_custom_call" | custom-call | flops 402653184 | bytes 2097152 | tf_op jit(solution)/shard_map/project_late/pallas_call | solution.py:379
  19.0 0.6 %collective-permute-done.2.refs_1_ = bf16[768,128]{1,0:T(8,128)(2,1)S(1)} collective-permute-done((bf16[768,128]{1,0:T(8,128)(2,1)S(1)}, bf16[768,128]{1,0:T(8,128)(2,1)S(1)}, u32[]{:S(2)}, u32[]{:S(2)}) %collective-permute-start.2) | collective-permute-done | bytes 196640 | tf_op jit(solution)/shard_map/ppermute | solution.py:608
  19.5 0.1 sends.7
  19.6 1.6 %collective-permute-start.5 = (bf16[784,128]{1,0:T(8,128)(2,1)S(1)}, bf16[784,128]{1,0:T(8,128)(2,1)S(1)}, u32[]{:S(2)}, u32[]{:S(2)}) collective-permute-start(bf16[784,128]{1,0:T(8,128)(2,1)S(1)} %get-tuple-element.79), channel_id=1, source_target_pairs={{0,4},{4,8},{8,12},{12,14},{14,10},{10,6},{6,2},{2,0},{1,5},{5,9},... | collective-permute-start | bytes 602120 | tf_op jit(solution)/shard_map/ppermute | solution.py:608
  21.3 0.5 collective-permute-start.6
  21.7 1.6 %project_early.3 = (f32[2,1,776,128]{3,2,1,0:T(8,128)S(1)}, bf16[2,192,2048]{2,1,0:T(8,128)(2,1)S(1)}, f32[2,8,128]{2,1,0:T(8,128)S(1)}) custom-call(s32[6]{0:T(128)S(1)} %copy-done.5, bf16[3,192,2048]{2,1,0:T(8,128)(2,1)S(1)} %bitcast.9, bf16[3,192,2048]{2,1,0:T(8,128)(2,1)S(1)} %collective-permute-done.other, f32[1,2048]{1,0:T(1,128)S(1)} %bitcast.14, ...), custom_call_target="tpu_custom_call" | custom-call | flops 402653184 | bytes 2097152 | tf_op jit(solution)/shard_map/project_early/pallas_call | solution.py:361
  23.4 1.3 %collective-permute-done.4.refs_1_ = bf16[784,128]{1,0:T(8,128)(2,1)S(1)} collective-permute-done((bf16[784,128]{1,0:T(8,128)(2,1)S(1)}, bf16[784,128]{1,0:T(8,128)(2,1)S(1)}, u32[]{:S(2)}, u32[]{:S(2)}) %collective-permute-start.4) | collective-permute-done | bytes 200736 | tf_op jit(solution)/shard_map/ppermute | solution.py:608
  24.7 0.1 sends.8
  24.8 1.6 %collective-permute-start.7 = (bf16[784,128]{1,0:T(8,128)(2,1)S(1)}, bf16[784,128]{1,0:T(8,128)(2,1)S(1)}, u32[]{:S(2)}, u32[]{:S(2)}) collective-permute-start(bf16[784,128]{1,0:T(8,128)(2,1)S(1)} %get-tuple-element.83), channel_id=1, source_target_pairs={{0,4},{4,8},{8,12},{12,14},{14,10},{10,6},{6,2},{2,0},{1,5},{5,9},... | collective-permute-start | bytes 602120 | tf_op jit(solution)/shard_map/ppermute | solution.py:608
  26.3 0.5 %collective-permute-start.8 = (bf16[784,128]{1,0:T(8,128)(2,1)S(1)}, bf16[784,128]{1,0:T(8,128)(2,1)S(1)}, u32[]{:S(2)}, u32[]{:S(2)}) collective-permute-start(bf16[784,128]{1,0:T(8,128)(2,1)S(1)} %get-tuple-element.84), channel_id=1, source_target_pairs={{0,2},{4,0},{8,4},{12,8},{14,12},{10,14},{6,10},{2,6},{1,3},{5,1},... | collective-permute-start | bytes 602120 | tf_op jit(solution)/shard_map/ppermute | solution.py:608
  26.8 1.0 %project_late.3.terms = f32[2,1,776,128]{3,2,1,0:T(8,128)S(1)} custom-call(bf16[2,192,2048]{2,1,0:T(8,128)(2,1)S(1)} %get-tuple-element.77.lines, f32[2,8,128]{2,1,0:T(8,128)S(1)} %get-tuple-element.78.totals, bf16[4,2048,256]{2,1,0:T(8,128)(2,1)S(1)} %dequantize.1.weight), custom_call_target="tpu_custom_call" | custom-call | flops 402653184 | bytes 2097152 | tf_op jit(solution)/shard_map/project_late/pallas_call | solution.py:379
  27.9 0.0 collective-permute-done.5.refs_0_
  27.9 1.2 %collective-permute-done.6.refs_1_ = bf16[784,128]{1,0:T(8,128)(2,1)S(1)} collective-permute-done((bf16[784,128]{1,0:T(8,128)(2,1)S(1)}, bf16[784,128]{1,0:T(8,128)(2,1)S(1)}, u32[]{:S(2)}, u32[]{:S(2)}) %collective-permute-start.6) | collective-permute-done | bytes 200736 | tf_op jit(solution)/shard_map/ppermute | solution.py:608
  29.1 0.1 sends.9
  29.2 1.4 %collective-permute-start.9 = (bf16[784,128]{1,0:T(8,128)(2,1)S(1)}, bf16[784,128]{1,0:T(8,128)(2,1)S(1)}, u32[]{:S(2)}, u32[]{:S(2)}) collective-permute-start(bf16[784,128]{1,0:T(8,128)(2,1)S(1)} %get-tuple-element.93), channel_id=1, source_target_pairs={{0,4},{4,8},{8,12},{12,14},{14,10},{10,6},{6,2},{2,0},{1,5},{5,9},... | collective-permute-start | bytes 602120 | tf_op jit(solution)/shard_map/ppermute | solution.py:608
  30.7 0.6 %collective-permute-start.10 = (bf16[784,128]{1,0:T(8,128)(2,1)S(1)}, bf16[784,128]{1,0:T(8,128)(2,1)S(1)}, u32[]{:S(2)}, u32[]{:S(2)}) collective-permute-start(bf16[784,128]{1,0:T(8,128)(2,1)S(1)} %get-tuple-element.94), channel_id=1, source_target_pairs={{0,2},{4,0},{8,4},{12,8},{14,12},{10,14},{6,10},{2,6},{1,3},{5,1},... | collective-permute-start | bytes 602120 | tf_op jit(solution)/shard_map/ppermute | solution.py:608
  31.9 0.0 copy-start.1
  32.0 0.0 copy-start.6
  32.0 3.4 %project.2.terms = f32[2,2,776,128]{3,2,1,0:T(8,128)S(1)} custom-call(s32[6]{0:T(128)S(1)} %copy-done.5, bf16[3,192,2048]{2,1,0:T(8,128)(2,1)S(1)} %bitcast.10, bf16[3,192,2048]{2,1,0:T(8,128)(2,1)S(1)} %collective-permute-done.other, f32[1,2048]{1,0:T(1,128)S(1)} %bitcast.15, bf16[4,2048,256]{2,1,0:T(8,128)(2,1)S(1)} %dequantize.1.weight), custom_call_target="tpu_custom_call" | custom-call | flops 805306368 | bytes 2097152 | tf_op jit(solution)/shard_map/project/pallas_call | solution.py:318
  35.4 0.0 collective-permute-done.7.refs_0_
  35.4 0.1 sends.10
  35.5 0.1 collective-permute-start.13
  35.6 2.0 %collective-permute-start.14 = (bf16[784,128]{1,0:T(8,128)(2,1)S(1)}, bf16[784,128]{1,0:T(8,128)(2,1)S(1)}, u32[]{:S(2)}, u32[]{:S(2)}) collective-permute-start(bf16[784,128]{1,0:T(8,128)(2,1)S(1)} %get-tuple-element.89), channel_id=1, source_target_pairs={{0,2},{4,0},{8,4},{12,8},{14,12},{10,14},{6,10},{2,6},{1,3},{5,1},... | collective-permute-start | bytes 602120 | tf_op jit(solution)/shard_map/ppermute | solution.py:608
  37.6 1.6 %cache_attention.2 = bf16[4,48,128]{2,1,0:T(8,128)(2,1)S(1)} custom-call(s32[6]{0:T(128)S(1)} %copy-done.5, s32[6]{0:T(128)S(1)} %copy-done.7, s32[1,1]{1,0:T(1,128)} %bitcast.4.stored, bf16[8,32,128]{2,1,0:T(8,128)(2,1)S(1)} %get-tuple-element.91.q.grouped, bf16[1,1024,2048]{2,1,0:T(8,128)(2,1)S(1)} %copy-done.1, bf16[1,2,2048]{2,1,0:T(2,128)(2,1)S(1)} %copy-done.6), custom_call_target="tpu_custom_call" | custom-call | flops 1 | bytes 1 | tf_op jit(solution)/shard_map/cache_attention/pallas_call | solution.py:503
  39.2 0.1 sends.11
  39.2 0.9 %collective-permute-start.11 = (bf16[784,128]{1,0:T(8,128)(2,1)S(1)}, bf16[784,128]{1,0:T(8,128)(2,1)S(1)}, u32[]{:S(2)}, u32[]{:S(2)}) collective-permute-start(bf16[784,128]{1,0:T(8,128)(2,1)S(1)} %get-tuple-element.97), channel_id=1, source_target_pairs={{0,4},{4,8},{8,12},{12,14},{14,10},{10,6},{6,2},{2,0},{1,5},{5,9},... | collective-permute-start | bytes 602120 | tf_op jit(solution)/shard_map/ppermute | solution.py:608
  40.2 1.1 %collective-permute-start.12 = (bf16[784,128]{1,0:T(8,128)(2,1)S(1)}, bf16[784,128]{1,0:T(8,128)(2,1)S(1)}, u32[]{:S(2)}, u32[]{:S(2)}) collective-permute-start(bf16[784,128]{1,0:T(8,128)(2,1)S(1)} %get-tuple-element.98), channel_id=1, source_target_pairs={{0,2},{4,0},{8,4},{12,8},{14,12},{10,14},{6,10},{2,6},{1,3},{5,1},... | collective-permute-start | bytes 602120 | tf_op jit(solution)/shard_map/ppermute | solution.py:608
  41.3 1.6 %cache_attention.3.cached_here = bf16[4,48,128]{2,1,0:T(8,128)(2,1)S(1)} custom-call(s32[6]{0:T(128)S(1)} %copy-done.5, s32[6]{0:T(128)S(1)} %copy-done.7, s32[1,1]{1,0:T(1,128)} %bitcast.5.stored, bf16[8,32,128]{2,1,0:T(8,128)(2,1)S(1)} %get-tuple-element.91.q.grouped, bf16[1,1024,2048]{2,1,0:T(8,128)(2,1)S(1)} %copy-done.1, bf16[1,2,2048]{2,1,0:T(2,128)(2,1)S(1)} %copy-done.6), custom_call_target="tpu_custom_call" | custom-call | flops 1 | bytes 1 | tf_op jit(solution)/shard_map/cache_attention/pallas_call | solution.py:503
  42.9 0.6 %project.3.own = f32[1,2,776,128]{3,2,1,0:T(8,128)S(1)} custom-call(s32[6]{0:T(128)S(1)} %copy-done.5, bf16[3,192,2048]{2,1,0:T(8,128)(2,1)S(1)} %bitcast.11, bf16[3,192,2048]{2,1,0:T(8,128)(2,1)S(1)} %collective-permute-done.other, f32[1,2048]{1,0:T(1,128)S(1)} %bitcast.16, bf16[4,2048,256]{2,1,0:T(8,128)(2,1)S(1)} %dequantize.1.weight), custom_call_target="tpu_custom_call" | custom-call | flops 402653184 | bytes 2097152 | tf_op jit(solution)/shard_map/project/pallas_call | solution.py:318
  43.6 0.4 collective-permute-done.14.left_keys
  44.0 1.1 %collective-permute-done.11.right_keys = bf16[784,128]{1,0:T(8,128)(2,1)S(1)} collective-permute-done((bf16[784,128]{1,0:T(8,128)(2,1)S(1)}, bf16[784,128]{1,0:T(8,128)(2,1)S(1)}, u32[]{:S(2)}, u32[]{:S(2)}) %collective-permute-start.11) | collective-permute-done | bytes 200736 | tf_op jit(solution)/shard_map/ppermute | solution.py:608
  45.1 1.4 %collective-permute-done.12.left_values = bf16[784,128]{1,0:T(8,128)(2,1)S(1)} collective-permute-done((bf16[784,128]{1,0:T(8,128)(2,1)S(1)}, bf16[784,128]{1,0:T(8,128)(2,1)S(1)}, u32[]{:S(2)}, u32[]{:S(2)}) %collective-permute-start.12) | collective-permute-done | bytes 200736 | tf_op jit(solution)/shard_map/ppermute | solution.py:608
  46.4 1.4 %finish.1 = bf16[1,2,8192]{2,1,0:T(2,128)(2,1)S(1)} custom-call(s32[6]{0:T(128)S(1)} %copy-done.5, f32[2,192,128]{2,1,0:T(8,128)S(1)} %get-tuple-element.67.rotary, f32[1,2,776,128]{3,2,1,0:T(8,128)S(1)} %project.3.own, bf16[784,128]{1,0:T(8,128)(2,1)S(1)} %collective-permute-done.11.right_keys, bf16[784,128]{1,0:T(8,128)(2,1)S(1)} %collective-permute-done.12.left_values, ...), custom_call_target="tpu_custom_call" | custom-call | tf_op jit(solution)/shard_map/finish/pallas_call | solution.py:569
  47.8 1.9 %all_gather.3 = bf16[1,2,16384]{2,1,0:T(2,128)(2,1)S(1)} all-gather(bf16[1,2,8192]{2,1,0:T(2,128)(2,1)S(1)} %finish.1), channel_id=1, replica_groups=mesh['grp'=2,'tp'=8,'rep'=2] {'rep'}, dimensions={2}, use_global_device_ids=true | all-gather | bytes 98304 | tf_op jit(solution)/shard_map/all_gather | solution.py:654
  49.7 0.6 %copy.16 = bf16[1,2,16384]{2,1,0:T(2,128)(2,1)} copy(bf16[1,2,16384]{2,1,0:T(2,128)(2,1)S(1)} %all_gather.3) | data formatting | bytes 131072
  (25 shorter events, 0.1 us)
Async XLA Ops:
  0.0 7.9 %collective-permute-start = (bf16[3,192,2048]{2,1,0:T(8,128)(2,1)}, bf16[3,192,2048]{2,1,0:T(8,128)(2,1)S(1)}, u32[]{:S(2)}, u32[]{:S(2)}) collective-permute-start(bf16[3,192,2048]{2,1,0:T(8,128)(2,1)} %bitcast.6), channel_id=1, source_target_pairs={{0,1},{1,0},{2,3},{3,2},{4,5},{5,4},{6,7},{7,6},{8,9},{9,8},{10,11... | collective-permute-start | bytes 7077896 | tf_op jit(solution)/shard_map/ppermute | solution.py:610
  0.5 7.4 %copy-start.7 = (s32[6]{0:T(128)S(1)}, s32[6]{0:T(128)}, u32[]{:S(2)}) copy-start(s32[6]{0:T(128)} %lengths.3) | copy-start | bytes 76
  0.5 7.5 %copy-start = (bf16[192,3,2048]{2,0,1:T(8,128)(2,1)S(1)}, bf16[192,3,2048]{2,0,1:T(8,128)(2,1)}, u32[]{:S(2)}) copy-start(bf16[192,3,2048]{2,0,1:T(8,128)(2,1)} %param.13) | copy-start | bytes 7077892
  0.5 7.5 %copy-start.2 = (f32[2048]{0:T(1024)S(1)}, f32[2048]{0:T(1024)}, u32[]{:S(2)}) copy-start(f32[2048]{0:T(1024)} %param.14) | copy-start | bytes 24580
  0.5 7.5 %copy-start.5 = (s32[6]{0:T(128)S(1)}, s32[6]{0:T(128)}, u32[]{:S(2)}) copy-start(s32[6]{0:T(128)} %targets.10) | copy-start | bytes 76
  8.0 4.6 %copy-start.8 = (f32[128]{0:T(128)S(1)}, f32[128]{0:T(128)}, u32[]{:S(2)}) copy-start(f32[128]{0:T(128)} %constant.7.clone) | copy-start | bytes 1540
  9.9 9.7 %collective-permute-start.1 = (bf16[784,128]{1,0:T(8,128)(2,1)S(1)}, bf16[784,128]{1,0:T(8,128)(2,1)S(1)}, u32[]{:S(2)}, u32[]{:S(2)}) collective-permute-start(bf16[784,128]{1,0:T(8,128)(2,1)S(1)} %get-tuple-element.69), channel_id=1, source_target_pairs={{0,4},{4,8},{8,12},{12,14},{14,10},{10,6},{6,2},{2,0},{1,5},{5,9},... | collective-permute-start | bytes 602120 | tf_op jit(solution)/shard_map/ppermute | solution.py:608
  12.5 7.0 %collective-permute-start.2 = (bf16[768,128]{1,0:T(8,128)(2,1)S(1)}, bf16[768,128]{1,0:T(8,128)(2,1)S(1)}, u32[]{:S(2)}, u32[]{:S(2)}) collective-permute-start(bf16[768,128]{1,0:T(8,128)(2,1)S(1)} %get-tuple-element.53), channel_id=1, source_target_pairs={{0,2},{4,0},{8,4},{12,8},{14,12},{10,14},{6,10},{2,6},{1,3},{5,1},... | collective-permute-start | bytes 589832 | tf_op jit(solution)/shard_map/ppermute | solution.py:608
  12.6 4.6 %copy-start.3 = (f32[2,192,128]{2,1,0:T(8,128)S(1)}, f32[2,192,128]{2,1,0:T(8,128)}, u32[]{:S(2)}) copy-start(f32[2,192,128]{2,1,0:T(8,128)} %constant.8.clone.turns) | copy-start | bytes 589828
  12.7 4.6 %copy-start.4 = (bf16[1,2,16384]{2,1,0:T(2,128)(2,1)S(1)}, bf16[1,2,16384]{2,1,0:T(2,128)(2,1)}, u32[]{:S(2)}) copy-start(bf16[1,2,16384]{2,1,0:T(2,128)(2,1)} %queries.1) | copy-start | bytes 196612
  15.2 8.2 %collective-permute-start.3 = (bf16[784,128]{1,0:T(8,128)(2,1)S(1)}, bf16[784,128]{1,0:T(8,128)(2,1)S(1)}, u32[]{:S(2)}, u32[]{:S(2)}) collective-permute-start(bf16[784,128]{1,0:T(8,128)(2,1)S(1)} %get-tuple-element.62), channel_id=1, source_target_pairs={{0,4},{4,8},{8,12},{12,14},{14,10},{10,6},{6,2},{2,0},{1,5},{5,9},... | collective-permute-start | bytes 602120 | tf_op jit(solution)/shard_map/ppermute | solution.py:608
  17.2 7.4 %collective-permute-start.4 = (bf16[784,128]{1,0:T(8,128)(2,1)S(1)}, bf16[784,128]{1,0:T(8,128)(2,1)S(1)}, u32[]{:S(2)}, u32[]{:S(2)}) collective-permute-start(bf16[784,128]{1,0:T(8,128)(2,1)S(1)} %get-tuple-element.63), channel_id=1, source_target_pairs={{0,2},{4,0},{8,4},{12,8},{14,12},{10,14},{6,10},{2,6},{1,3},{5,1},... | collective-permute-start | bytes 602120 | tf_op jit(solution)/shard_map/ppermute | solution.py:608
  19.6 8.2 %collective-permute-start.5 = (bf16[784,128]{1,0:T(8,128)(2,1)S(1)}, bf16[784,128]{1,0:T(8,128)(2,1)S(1)}, u32[]{:S(2)}, u32[]{:S(2)}) collective-permute-start(bf16[784,128]{1,0:T(8,128)(2,1)S(1)} %get-tuple-element.79), channel_id=1, source_target_pairs={{0,4},{4,8},{8,12},{12,14},{14,10},{10,6},{6,2},{2,0},{1,5},{5,9},... | collective-permute-start | bytes 602120 | tf_op jit(solution)/shard_map/ppermute | solution.py:608
  21.3 7.8 %collective-permute-start.6 = (bf16[784,128]{1,0:T(8,128)(2,1)S(1)}, bf16[784,128]{1,0:T(8,128)(2,1)S(1)}, u32[]{:S(2)}, u32[]{:S(2)}) collective-permute-start(bf16[784,128]{1,0:T(8,128)(2,1)S(1)} %get-tuple-element.80), channel_id=1, source_target_pairs={{0,2},{4,0},{8,4},{12,8},{14,12},{10,14},{6,10},{2,6},{1,3},{5,1},... | collective-permute-start | bytes 602120 | tf_op jit(solution)/shard_map/ppermute | solution.py:608
  24.8 10.6 %collective-permute-start.7 = (bf16[784,128]{1,0:T(8,128)(2,1)S(1)}, bf16[784,128]{1,0:T(8,128)(2,1)S(1)}, u32[]{:S(2)}, u32[]{:S(2)}) collective-permute-start(bf16[784,128]{1,0:T(8,128)(2,1)S(1)} %get-tuple-element.83), channel_id=1, source_target_pairs={{0,4},{4,8},{8,12},{12,14},{14,10},{10,6},{6,2},{2,0},{1,5},{5,9},... | collective-permute-start | bytes 602120 | tf_op jit(solution)/shard_map/ppermute | solution.py:608
  26.3 9.1 %collective-permute-start.8 = (bf16[784,128]{1,0:T(8,128)(2,1)S(1)}, bf16[784,128]{1,0:T(8,128)(2,1)S(1)}, u32[]{:S(2)}, u32[]{:S(2)}) collective-permute-start(bf16[784,128]{1,0:T(8,128)(2,1)S(1)} %get-tuple-element.84), channel_id=1, source_target_pairs={{0,2},{4,0},{8,4},{12,8},{14,12},{10,14},{6,10},{2,6},{1,3},{5,1},... | collective-permute-start | bytes 602120 | tf_op jit(solution)/shard_map/ppermute | solution.py:608
  29.2 9.9 %collective-permute-start.9 = (bf16[784,128]{1,0:T(8,128)(2,1)S(1)}, bf16[784,128]{1,0:T(8,128)(2,1)S(1)}, u32[]{:S(2)}, u32[]{:S(2)}) collective-permute-start(bf16[784,128]{1,0:T(8,128)(2,1)S(1)} %get-tuple-element.93), channel_id=1, source_target_pairs={{0,4},{4,8},{8,12},{12,14},{14,10},{10,6},{6,2},{2,0},{1,5},{5,9},... | collective-permute-start | bytes 602120 | tf_op jit(solution)/shard_map/ppermute | solution.py:608
  30.7 8.5 %collective-permute-start.10 = (bf16[784,128]{1,0:T(8,128)(2,1)S(1)}, bf16[784,128]{1,0:T(8,128)(2,1)S(1)}, u32[]{:S(2)}, u32[]{:S(2)}) collective-permute-start(bf16[784,128]{1,0:T(8,128)(2,1)S(1)} %get-tuple-element.94), channel_id=1, source_target_pairs={{0,2},{4,0},{8,4},{12,8},{14,12},{10,14},{6,10},{2,6},{1,3},{5,1},... | collective-permute-start | bytes 602120 | tf_op jit(solution)/shard_map/ppermute | solution.py:608
  31.9 5.6 %copy-start.1 = (bf16[1,1024,2048]{2,1,0:T(8,128)(2,1)S(1)}, bf16[1,1024,2048]{2,1,0:T(8,128)(2,1)}, u32[]{:S(2)}) copy-start(bf16[1,1024,2048]{2,1,0:T(8,128)(2,1)} %cache.3) | copy-start | bytes 12582916
  32.0 5.6 %copy-start.6 = (bf16[1,2,2048]{2,1,0:T(2,128)(2,1)S(1)}, bf16[1,2,2048]{2,1,0:T(2,128)(2,1)}, u32[]{:S(2)}) copy-start(bf16[1,2,2048]{2,1,0:T(2,128)(2,1)} %new.3) | copy-start | bytes 24580
  35.5 8.1 %collective-permute-start.13 = (bf16[784,128]{1,0:T(8,128)(2,1)S(1)}, bf16[784,128]{1,0:T(8,128)(2,1)S(1)}, u32[]{:S(2)}, u32[]{:S(2)}) collective-permute-start(bf16[784,128]{1,0:T(8,128)(2,1)S(1)} %get-tuple-element.88), channel_id=1, source_target_pairs={{0,4},{4,8},{8,12},{12,14},{14,10},{10,6},{6,2},{2,0},{1,5},{5,9},... | collective-permute-start | bytes 602120 | tf_op jit(solution)/shard_map/ppermute | solution.py:608
  35.6 8.4 %collective-permute-start.14 = (bf16[784,128]{1,0:T(8,128)(2,1)S(1)}, bf16[784,128]{1,0:T(8,128)(2,1)S(1)}, u32[]{:S(2)}, u32[]{:S(2)}) collective-permute-start(bf16[784,128]{1,0:T(8,128)(2,1)S(1)} %get-tuple-element.89), channel_id=1, source_target_pairs={{0,2},{4,0},{8,4},{12,8},{14,12},{10,14},{6,10},{2,6},{1,3},{5,1},... | collective-permute-start | bytes 602120 | tf_op jit(solution)/shard_map/ppermute | solution.py:608
  39.2 5.8 %collective-permute-start.11 = (bf16[784,128]{1,0:T(8,128)(2,1)S(1)}, bf16[784,128]{1,0:T(8,128)(2,1)S(1)}, u32[]{:S(2)}, u32[]{:S(2)}) collective-permute-start(bf16[784,128]{1,0:T(8,128)(2,1)S(1)} %get-tuple-element.97), channel_id=1, source_target_pairs={{0,4},{4,8},{8,12},{12,14},{14,10},{10,6},{6,2},{2,0},{1,5},{5,9},... | collective-permute-start | bytes 602120 | tf_op jit(solution)/shard_map/ppermute | solution.py:608
  40.2 6.3 %collective-permute-start.12 = (bf16[784,128]{1,0:T(8,128)(2,1)S(1)}, bf16[784,128]{1,0:T(8,128)(2,1)S(1)}, u32[]{:S(2)}, u32[]{:S(2)}) collective-permute-start(bf16[784,128]{1,0:T(8,128)(2,1)S(1)} %get-tuple-element.98), channel_id=1, source_target_pairs={{0,2},{4,0},{8,4},{12,8},{14,12},{10,14},{6,10},{2,6},{1,3},{5,1},... | collective-permute-start | bytes 602120 | tf_op jit(solution)/shard_map/ppermute | solution.py:608
  41.3 2.7 %collective-permute-start.15 = (bf16[4,48,128]{2,1,0:T(8,128)(2,1)S(1)}, bf16[4,48,128]{2,1,0:T(8,128)(2,1)S(1)}, u32[]{:S(2)}, u32[]{:S(2)}) collective-permute-start(bf16[4,48,128]{2,1,0:T(8,128)(2,1)S(1)} %cache_attention.2), channel_id=1, source_target_pairs={{0,1},{1,0},{2,3},{3,2},{4,5},{5,4},{6,7},{7,6},{8,9},{9,8},{10,11... | collective-permute-start | bytes 147464 | tf_op jit(solution)/shard_map/ppermute | solution.py:610

commit v19 on v17

--- a/solution.py
+++ b/solution.py
@@ -115,6 +115,7 @@
 
 
 CODE_ROWS = 128
+AHEAD = 4
 
 
 def block_leaves(scale):
@@ -166,7 +167,7 @@
             for kind, buffer in enumerate((key_codes, value_codes))
         ]
 
-    for block in range(blocks):
+    for block in range(min(AHEAD, blocks)):
         for copy in code_copies(block):
             copy.start()
     for at in range(CORE_HEADS):
@@ -191,6 +192,9 @@
     for block in range(blocks):
         for copy in code_copies(block):
             copy.wait()
+        if block + AHEAD < blocks:
+            for copy in code_copies(block + AHEAD):
+                copy.start()
         lax.fori_loop(block * steps, (block + 1) * steps, body, 0)
 
 

time: 49.9 us -> 49.9 us (level)
  waiting for transfers between devices: 4.74 us -> 5.54 us
  starting transfers between devices: 17.1 us -> 16.4 us
  Pallas kernels: 24.8 us -> 24.3 us
    ppermute x7, waiting for transfers between devices: 1.29 us -> 3.61 us  [pass_on(): lax.ppermute(right, 'tp', to_right)]
    ppermute x7, starting transfers between devices: 3.8 us -> 2.21 us  [pass_on(): lax.ppermute(left, 'tp', to_left)]
    ppermute x7, waiting for transfers between devices: 3.44 us -> 1.92 us  [pass_on(): lax.ppermute(left, 'tp', to_left)]
    pallas_call x3, Pallas kernels: 7.1 us -> 5.85 us  [project(): pl.pallas_call(functools.partial(project_kernel, distances), in_specs=[SM...]
    ppermute x7, starting transfers between devices: 12.8 us -> 13.7 us  [pass_on(): lax.ppermute(right, 'tp', to_right)]
    pallas_call x1, Pallas kernels: 1.61 us -> 2.43 us  [project_early(): pl.pallas_call(functools.partial(early_kernel, distance), in_specs=[SMEM]...]
  transfers between devices with their start and end apart: 16 -> 16, of which waited for: 6 -> 7; matrix products, arithmetic and copies ran while one was open for 0% -> 0% of each run, Pallas kernels for 43% -> 42%
where the time goes in v19:
time: 49.9 us; the launch traced here: 49.8 us
  Pallas kernels  24.3 us (49%)
  starting transfers between devices  16.4 us (33%)
  waiting for transfers between devices  5.54 us (11%)
  blocking collectives  1.85 us (4%)
  between operations  0.93 us (2%)
  local copies, waits for them, and re-layouts  0.68 us (1%)
    ppermute x7, starting transfers between devices, pass_on(): lax.ppermute(right, 'tp', to_right)  13.7 us
    pallas_call x1, Pallas kernels, dequantize(): pl.pallas_call(weights_kernel, grid=(1,), in_specs=[pl.BlockSpec(memory_s...  7.45 us
    pallas_call x3, Pallas kernels, project(): pl.pallas_call(functools.partial(project_kernel, distances), in_specs=[SM...  5.85 us
    ppermute x7, waiting for transfers between devices, pass_on(): lax.ppermute(right, 'tp', to_right)  3.61 us
    pallas_call x2, Pallas kernels, cache_attention(): pl.pallas_call(functools.partial(cache_kernel, part), in_specs=[SMEM] * 3...  3.18 us
    pallas_call x1, Pallas kernels, project_early(): pl.pallas_call(functools.partial(early_kernel, distance), in_specs=[SMEM]...  2.43 us
    ppermute x7, starting transfers between devices, pass_on(): lax.ppermute(left, 'tp', to_left)  2.21 us
    ppermute x7, waiting for transfers between devices, pass_on(): lax.ppermute(left, 'tp', to_left)  1.92 us
  transfers between devices with their start and end apart: 16, of which 7 were waited for; matrix products, arithmetic and copies ran while one was open for 0% of the time, Pallas kernels for 42%

profile of v19, /device:TPU:0, one launch (start us, length us, event | category | flops | bytes accessed | tf_op | source)
XLA Modules:
  0.0 49.8 jit_solution(16557651973795328160)
XLA Ops:
  0.0 0.5 collective-permute-start
  0.5 7.4 %dequantize.1.weight = bf16[4,2048,256]{2,1,0:T(8,128)(2,1)S(1)} custom-call(s32[2048,2048]{1,0:T(8,128)} %codes.1, s32[32,2048]{1,0:T(8,128)} %value_scales.1, s32[32,2048]{1,0:T(8,128)} %value_scales.1, f32[8,32]{1,0:T(8,128)} %bitcast.14), custom_call_target="tpu_custom_call" | custom-call | flops 134217728 | bytes 8388608 | tf_op jit(solution)/shard_map/dequantize/pallas_call | solution.py:207
  8.0 0.0 copy-start.8
  8.0 1.9 %project_first.1 = (bf16[784,128]{1,0:T(8,128)(2,1)S(1)}, bf16[768,128]{1,0:T(8,128)(2,1)S(1)}) custom-call(s32[6]{0:T(128)S(1)} %copy-done.5, bf16[3,192,2048]{2,1,0:T(8,128)(2,1)S(1)} %bitcast.4, bf16[3,192,2048]{2,1,0:T(8,128)(2,1)S(1)} %collective-permute-done.other, f32[1,2048]{1,0:T(1,128)S(1)} %bitcast.9, bf16[4,2048,256]{2,1,0:T(8,128)(2,1)S(1)} %dequantize.1.weight), custom_call_target="tpu_custom_call" | custom-call | flops 805306368 | bytes 2097152 | tf_op jit(solution)/shard_map/project_first/pallas_call | solution.py:289
  9.9 2.6 %collective-permute-start.1 = (bf16[784,128]{1,0:T(8,128)(2,1)S(1)}, bf16[784,128]{1,0:T(8,128)(2,1)S(1)}, u32[]{:S(2)}, u32[]{:S(2)}) collective-permute-start(bf16[784,128]{1,0:T(8,128)(2,1)S(1)} %get-tuple-element.64), channel_id=1, source_target_pairs={{0,4},{4,8},{8,12},{12,14},{14,10},{10,6},{6,2},{2,0},{1,5},{5,9},... | collective-permute-start | bytes 602120 | tf_op jit(solution)/shard_map/ppermute | solution.py:612
  12.6 0.1 multiply_cosine_fusion
  12.7 2.4 %project_early.1 = (f32[2,1,776,128]{3,2,1,0:T(8,128)S(1)}, bf16[2,192,2048]{2,1,0:T(8,128)(2,1)S(1)}, f32[2,8,128]{2,1,0:T(8,128)S(1)}) custom-call(s32[6]{0:T(128)S(1)} %copy-done.5, bf16[3,192,2048]{2,1,0:T(8,128)(2,1)S(1)} %bitcast.5, bf16[3,192,2048]{2,1,0:T(8,128)(2,1)S(1)} %collective-permute-done.other, f32[1,2048]{1,0:T(1,128)S(1)} %bitcast.10, ...), custom_call_target="tpu_custom_call" | custom-call | flops 402653184 | bytes 2097152 | tf_op jit(solution)/shard_map/project_early/pallas_call | solution.py:365
  15.2 0.0 copy-start.3
  15.2 0.0 copy-start.4
  15.2 2.1 %collective-permute-start.3 = (bf16[784,128]{1,0:T(8,128)(2,1)S(1)}, bf16[784,128]{1,0:T(8,128)(2,1)S(1)}, u32[]{:S(2)}, u32[]{:S(2)}) collective-permute-start(bf16[784,128]{1,0:T(8,128)(2,1)S(1)} %get-tuple-element.67), channel_id=1, source_target_pairs={{0,4},{4,8},{8,12},{12,14},{14,10},{10,6},{6,2},{2,0},{1,5},{5,9},... | collective-permute-start | bytes 602120 | tf_op jit(solution)/shard_map/ppermute | solution.py:612
  17.3 0.0 collective-permute-start.4
  17.3 1.0 %project_late.1.terms = f32[2,1,776,128]{3,2,1,0:T(8,128)S(1)} custom-call(bf16[2,192,2048]{2,1,0:T(8,128)(2,1)S(1)} %get-tuple-element.56.lines, f32[2,8,128]{2,1,0:T(8,128)S(1)} %get-tuple-element.57.totals, bf16[4,2048,256]{2,1,0:T(8,128)(2,1)S(1)} %dequantize.1.weight), custom_call_target="tpu_custom_call" | custom-call | flops 402653184 | bytes 2097152 | tf_op jit(solution)/shard_map/project_late/pallas_call | solution.py:383
  18.3 0.7 %prepare.1 = (bf16[8,32,128]{2,1,0:T(8,128)(2,1)S(1)}, f32[2,192,128]{2,1,0:T(8,128)S(1)}) custom-call(s32[6]{0:T(128)S(1)} %copy-done.5, bf16[1,2,16384]{2,1,0:T(2,128)(2,1)S(1)} %copy-done.4, f32[2,6,128]{2,1,0:T(8,128)S(1)} %pad_maximum_fusion.starts, f32[2,192,128]{2,1,0:T(8,128)S(1)} %copy-done.3), custom_call_target="tpu_custom_call" | custom-call | tf_op jit(solution)/shard_map/prepare/pallas_call | solution.py:443
  19.0 0.6 %collective-permute-done.2.refs_1_ = bf16[768,128]{1,0:T(8,128)(2,1)S(1)} collective-permute-done((bf16[768,128]{1,0:T(8,128)(2,1)S(1)}, bf16[768,128]{1,0:T(8,128)(2,1)S(1)}, u32[]{:S(2)}, u32[]{:S(2)}) %collective-permute-start.2) | collective-permute-done | bytes 196640 | tf_op jit(solution)/shard_map/ppermute | solution.py:612
  19.6 0.1 sends.7
  19.7 1.6 %collective-permute-start.5 = (bf16[784,128]{1,0:T(8,128)(2,1)S(1)}, bf16[784,128]{1,0:T(8,128)(2,1)S(1)}, u32[]{:S(2)}, u32[]{:S(2)}) collective-permute-start(bf16[784,128]{1,0:T(8,128)(2,1)S(1)} %get-tuple-element.75), channel_id=1, source_target_pairs={{0,4},{4,8},{8,12},{12,14},{14,10},{10,6},{6,2},{2,0},{1,5},{5,9},... | collective-permute-start | bytes 602120 | tf_op jit(solution)/shard_map/ppermute | solution.py:612
  21.3 0.5 collective-permute-start.6
  22.4 0.0 copy-start.1
  22.4 0.0 copy-start.6
  22.4 2.0 %project.3.terms = f32[2,2,776,128]{3,2,1,0:T(8,128)S(1)} custom-call(s32[6]{0:T(128)S(1)} %copy-done.5, bf16[3,192,2048]{2,1,0:T(8,128)(2,1)S(1)} %bitcast.6, bf16[3,192,2048]{2,1,0:T(8,128)(2,1)S(1)} %collective-permute-done.other, f32[1,2048]{1,0:T(1,128)S(1)} %bitcast.11, bf16[4,2048,256]{2,1,0:T(8,128)(2,1)S(1)} %dequantize.1.weight), custom_call_target="tpu_custom_call" | custom-call | flops 805306368 | bytes 2097152 | tf_op jit(solution)/shard_map/project/pallas_call | solution.py:322
  24.4 0.0 collective-permute-done.3.refs_0_
  24.4 0.3 collective-permute-done.4.refs_1_
  24.7 0.1 sends.8
  24.8 0.5 %collective-permute-start.8 = (bf16[784,128]{1,0:T(8,128)(2,1)S(1)}, bf16[784,128]{1,0:T(8,128)(2,1)S(1)}, u32[]{:S(2)}, u32[]{:S(2)}) collective-permute-start(bf16[784,128]{1,0:T(8,128)(2,1)S(1)} %get-tuple-element.71), channel_id=1, source_target_pairs={{0,2},{4,0},{8,4},{12,8},{14,12},{10,14},{6,10},{2,6},{1,3},{5,1},... | collective-permute-start | bytes 602120 | tf_op jit(solution)/shard_map/ppermute | solution.py:612
  25.3 2.4 %collective-permute-start.7 = (bf16[784,128]{1,0:T(8,128)(2,1)S(1)}, bf16[784,128]{1,0:T(8,128)(2,1)S(1)}, u32[]{:S(2)}, u32[]{:S(2)}) collective-permute-start(bf16[784,128]{1,0:T(8,128)(2,1)S(1)} %get-tuple-element.79), channel_id=1, source_target_pairs={{0,4},{4,8},{8,12},{12,14},{14,10},{10,6},{6,2},{2,0},{1,5},{5,9},... | collective-permute-start | bytes 602120 | tf_op jit(solution)/shard_map/ppermute | solution.py:612
  27.6 1.6 %cache_attention.2 = bf16[4,48,128]{2,1,0:T(8,128)(2,1)S(1)} custom-call(s32[6]{0:T(128)S(1)} %copy-done.5, s32[6]{0:T(128)S(1)} %copy-done.7, s32[1]{0:T(128)S(6)} %copy.15.stored, bf16[8,32,128]{2,1,0:T(8,128)(2,1)S(1)} %get-tuple-element.73.q.grouped, bf16[1,1024,2048]{2,1,0:T(8,128)(2,1)S(1)} %copy-done.1, bf16[1,2,2048]{2,1,0:T(2,128)(2,1)S(1)} %copy-done.6), custom_call_target="tpu_custom_call" | custom-call | flops 1 | bytes 1 | tf_op jit(solution)/shard_map/cache_attention/pallas_call | solution.py:507
  29.2 0.0 collective-permute-done.5.refs_0_
  29.3 0.1 sends.9
  29.3 1.8 %collective-permute-start.9 = (bf16[784,128]{1,0:T(8,128)(2,1)S(1)}, bf16[784,128]{1,0:T(8,128)(2,1)S(1)}, u32[]{:S(2)}, u32[]{:S(2)}) collective-permute-start(bf16[784,128]{1,0:T(8,128)(2,1)S(1)} %get-tuple-element.83), channel_id=1, source_target_pairs={{0,4},{4,8},{8,12},{12,14},{14,10},{10,6},{6,2},{2,0},{1,5},{5,9},... | collective-permute-start | bytes 602120 | tf_op jit(solution)/shard_map/ppermute | solution.py:612
  31.2 0.2 collective-permute-start.10
  31.4 2.0 %project.4.terms = f32[2,2,776,128]{3,2,1,0:T(8,128)S(1)} custom-call(s32[6]{0:T(128)S(1)} %copy-done.5, bf16[3,192,2048]{2,1,0:T(8,128)(2,1)S(1)} %bitcast.7, bf16[3,192,2048]{2,1,0:T(8,128)(2,1)S(1)} %collective-permute-done.other, f32[1,2048]{1,0:T(1,128)S(1)} %bitcast.12, bf16[4,2048,256]{2,1,0:T(8,128)(2,1)S(1)} %dequantize.1.weight), custom_call_target="tpu_custom_call" | custom-call | flops 805306368 | bytes 2097152 | tf_op jit(solution)/shard_map/project/pallas_call | solution.py:322
  33.4 0.5 collective-permute-done.7.refs_0_
  33.9 0.0 collective-permute-done.8.refs_1_
  33.9 0.1 sends.10
  34.0 1.4 %collective-permute-start.13 = (bf16[784,128]{1,0:T(8,128)(2,1)S(1)}, bf16[784,128]{1,0:T(8,128)(2,1)S(1)}, u32[]{:S(2)}, u32[]{:S(2)}) collective-permute-start(bf16[784,128]{1,0:T(8,128)(2,1)S(1)} %get-tuple-element.89), channel_id=1, source_target_pairs={{0,4},{4,8},{8,12},{12,14},{14,10},{10,6},{6,2},{2,0},{1,5},{5,9},... | collective-permute-start | bytes 602120 | tf_op jit(solution)/shard_map/ppermute | solution.py:612
  35.3 0.7 %collective-permute-start.14 = (bf16[784,128]{1,0:T(8,128)(2,1)S(1)}, bf16[784,128]{1,0:T(8,128)(2,1)S(1)}, u32[]{:S(2)}, u32[]{:S(2)}) collective-permute-start(bf16[784,128]{1,0:T(8,128)(2,1)S(1)} %get-tuple-element.90), channel_id=1, source_target_pairs={{0,2},{4,0},{8,4},{12,8},{14,12},{10,14},{6,10},{2,6},{1,3},{5,1},... | collective-permute-start | bytes 602120 | tf_op jit(solution)/shard_map/ppermute | solution.py:612
  36.0 2.1 %collective-permute-done.9.refs_0_ = bf16[784,128]{1,0:T(8,128)(2,1)S(1)} collective-permute-done((bf16[784,128]{1,0:T(8,128)(2,1)S(1)}, bf16[784,128]{1,0:T(8,128)(2,1)S(1)}, u32[]{:S(2)}, u32[]{:S(2)}) %collective-permute-start.9) | collective-permute-done | bytes 200736 | tf_op jit(solution)/shard_map/ppermute | solution.py:612
  38.2 0.2 collective-permute-done.10.refs_1_
  38.4 0.1 sends.11
  38.5 1.8 %collective-permute-start.11 = (bf16[784,128]{1,0:T(8,128)(2,1)S(1)}, bf16[784,128]{1,0:T(8,128)(2,1)S(1)}, u32[]{:S(2)}, u32[]{:S(2)}) collective-permute-start(bf16[784,128]{1,0:T(8,128)(2,1)S(1)} %get-tuple-element.87), channel_id=1, source_target_pairs={{0,4},{4,8},{8,12},{12,14},{14,10},{10,6},{6,2},{2,0},{1,5},{5,9},... | collective-permute-start | bytes 602120 | tf_op jit(solution)/shard_map/ppermute | solution.py:612
  40.3 0.3 collective-permute-start.12
  40.5 1.6 %cache_attention.3.cached_here = bf16[4,48,128]{2,1,0:T(8,128)(2,1)S(1)} custom-call(s32[6]{0:T(128)S(1)} %copy-done.5, s32[6]{0:T(128)S(1)} %copy-done.7, s32[1]{0:T(128)S(6)} %copy.15.stored, bf16[8,32,128]{2,1,0:T(8,128)(2,1)S(1)} %get-tuple-element.73.q.grouped, bf16[1,1024,2048]{2,1,0:T(8,128)(2,1)S(1)} %copy-done.1, bf16[1,2,2048]{2,1,0:T(2,128)(2,1)S(1)} %copy-done.6), custom_call_target="tpu_custom_call" | custom-call | flops 1 | bytes 1 | tf_op jit(solution)/shard_map/cache_attention/pallas_call | solution.py:507
  42.2 1.9 %project.5.own = f32[1,2,776,128]{3,2,1,0:T(8,128)S(1)} custom-call(s32[6]{0:T(128)S(1)} %copy-done.5, bf16[3,192,2048]{2,1,0:T(8,128)(2,1)S(1)} %bitcast.8, bf16[3,192,2048]{2,1,0:T(8,128)(2,1)S(1)} %collective-permute-done.other, f32[1,2048]{1,0:T(1,128)S(1)} %bitcast.13, bf16[4,2048,256]{2,1,0:T(8,128)(2,1)S(1)} %dequantize.1.weight), custom_call_target="tpu_custom_call" | custom-call | flops 402653184 | bytes 2097152 | tf_op jit(solution)/shard_map/project/pallas_call | solution.py:322
  44.1 1.0 %collective-permute-done.11.right_keys = bf16[784,128]{1,0:T(8,128)(2,1)S(1)} collective-permute-done((bf16[784,128]{1,0:T(8,128)(2,1)S(1)}, bf16[784,128]{1,0:T(8,128)(2,1)S(1)}, u32[]{:S(2)}, u32[]{:S(2)}) %collective-permute-start.11) | collective-permute-done | bytes 200736 | tf_op jit(solution)/shard_map/ppermute | solution.py:612
  45.1 0.9 %collective-permute-done.12.left_values = bf16[784,128]{1,0:T(8,128)(2,1)S(1)} collective-permute-done((bf16[784,128]{1,0:T(8,128)(2,1)S(1)}, bf16[784,128]{1,0:T(8,128)(2,1)S(1)}, u32[]{:S(2)}, u32[]{:S(2)}) %collective-permute-start.12) | collective-permute-done | bytes 200736 | tf_op jit(solution)/shard_map/ppermute | solution.py:612
  46.0 1.4 %finish.1 = bf16[1,2,8192]{2,1,0:T(2,128)(2,1)S(1)} custom-call(s32[6]{0:T(128)S(1)} %copy-done.5, f32[2,192,128]{2,1,0:T(8,128)S(1)} %get-tuple-element.62.rotary, f32[1,2,776,128]{3,2,1,0:T(8,128)S(1)} %project.5.own, bf16[784,128]{1,0:T(8,128)(2,1)S(1)} %collective-permute-done.11.right_keys, bf16[784,128]{1,0:T(8,128)(2,1)S(1)} %collective-permute-done.12.left_values, ...), custom_call_target="tpu_custom_call" | custom-call | tf_op jit(solution)/shard_map/finish/pallas_call | solution.py:573
  47.3 1.9 %all_gather.3 = bf16[1,2,16384]{2,1,0:T(2,128)(2,1)S(1)} all-gather(bf16[1,2,8192]{2,1,0:T(2,128)(2,1)S(1)} %finish.1), channel_id=1, replica_groups=mesh['grp'=2,'tp'=8,'rep'=2] {'rep'}, dimensions={2}, use_global_device_ids=true | all-gather | bytes 98304 | tf_op jit(solution)/shard_map/all_gather | solution.py:658
  49.2 0.6 %copy.16 = bf16[1,2,16384]{2,1,0:T(2,128)(2,1)} copy(bf16[1,2,16384]{2,1,0:T(2,128)(2,1)S(1)} %all_gather.3) | data formatting | bytes 131072
  (24 shorter events, 0.1 us)
Async XLA Ops:
  0.0 7.9 %collective-permute-start = (bf16[3,192,2048]{2,1,0:T(8,128)(2,1)}, bf16[3,192,2048]{2,1,0:T(8,128)(2,1)S(1)}, u32[]{:S(2)}, u32[]{:S(2)}) collective-permute-start(bf16[3,192,2048]{2,1,0:T(8,128)(2,1)} %bitcast.3), channel_id=1, source_target_pairs={{0,1},{1,0},{2,3},{3,2},{4,5},{5,4},{6,7},{7,6},{8,9},{9,8},{10,11... | collective-permute-start | bytes 7077896 | tf_op jit(solution)/shard_map/ppermute | solution.py:614
  0.5 7.5 %copy-start.7 = (s32[6]{0:T(128)S(1)}, s32[6]{0:T(128)}, u32[]{:S(2)}) copy-start(s32[6]{0:T(128)} %lengths.3) | copy-start | bytes 76
  0.5 7.5 %copy-start = (bf16[192,3,2048]{2,0,1:T(8,128)(2,1)S(1)}, bf16[192,3,2048]{2,0,1:T(8,128)(2,1)}, u32[]{:S(2)}) copy-start(bf16[192,3,2048]{2,0,1:T(8,128)(2,1)} %param.13) | copy-start | bytes 7077892
  0.5 7.5 %copy-start.2 = (f32[2048]{0:T(1024)S(1)}, f32[2048]{0:T(1024)}, u32[]{:S(2)}) copy-start(f32[2048]{0:T(1024)} %param.14) | copy-start | bytes 24580
  0.5 7.5 %copy-start.5 = (s32[6]{0:T(128)S(1)}, s32[6]{0:T(128)}, u32[]{:S(2)}) copy-start(s32[6]{0:T(128)} %targets.10) | copy-start | bytes 76
  8.0 4.6 %copy-start.8 = (f32[128]{0:T(128)S(1)}, f32[128]{0:T(128)}, u32[]{:S(2)}) copy-start(f32[128]{0:T(128)} %constant.7.clone) | copy-start | bytes 1540
  9.9 9.7 %collective-permute-start.1 = (bf16[784,128]{1,0:T(8,128)(2,1)S(1)}, bf16[784,128]{1,0:T(8,128)(2,1)S(1)}, u32[]{:S(2)}, u32[]{:S(2)}) collective-permute-start(bf16[784,128]{1,0:T(8,128)(2,1)S(1)} %get-tuple-element.64), channel_id=1, source_target_pairs={{0,4},{4,8},{8,12},{12,14},{14,10},{10,6},{6,2},{2,0},{1,5},{5,9},... | collective-permute-start | bytes 602120 | tf_op jit(solution)/shard_map/ppermute | solution.py:612
  12.5 7.0 %collective-permute-start.2 = (bf16[768,128]{1,0:T(8,128)(2,1)S(1)}, bf16[768,128]{1,0:T(8,128)(2,1)S(1)}, u32[]{:S(2)}, u32[]{:S(2)}) collective-permute-start(bf16[768,128]{1,0:T(8,128)(2,1)S(1)} %get-tuple-element.49), channel_id=1, source_target_pairs={{0,2},{4,0},{8,4},{12,8},{14,12},{10,14},{6,10},{2,6},{1,3},{5,1},... | collective-permute-start | bytes 589832 | tf_op jit(solution)/shard_map/ppermute | solution.py:612
  15.2 3.1 %copy-start.3 = (f32[2,192,128]{2,1,0:T(8,128)S(1)}, f32[2,192,128]{2,1,0:T(8,128)}, u32[]{:S(2)}) copy-start(f32[2,192,128]{2,1,0:T(8,128)} %constant.8.clone.turns) | copy-start | bytes 589828
  15.2 3.1 %copy-start.4 = (bf16[1,2,16384]{2,1,0:T(2,128)(2,1)S(1)}, bf16[1,2,16384]{2,1,0:T(2,128)(2,1)}, u32[]{:S(2)}) copy-start(bf16[1,2,16384]{2,1,0:T(2,128)(2,1)} %queries.1) | copy-start | bytes 196612
  15.2 9.2 %collective-permute-start.3 = (bf16[784,128]{1,0:T(8,128)(2,1)S(1)}, bf16[784,128]{1,0:T(8,128)(2,1)S(1)}, u32[]{:S(2)}, u32[]{:S(2)}) collective-permute-start(bf16[784,128]{1,0:T(8,128)(2,1)S(1)} %get-tuple-element.67), channel_id=1, source_target_pairs={{0,4},{4,8},{8,12},{12,14},{14,10},{10,6},{6,2},{2,0},{1,5},{5,9},... | collective-permute-start | bytes 602120 | tf_op jit(solution)/shard_map/ppermute | solution.py:612
  17.3 7.4 %collective-permute-start.4 = (bf16[784,128]{1,0:T(8,128)(2,1)S(1)}, bf16[784,128]{1,0:T(8,128)(2,1)S(1)}, u32[]{:S(2)}, u32[]{:S(2)}) collective-permute-start(bf16[784,128]{1,0:T(8,128)(2,1)S(1)} %get-tuple-element.58), channel_id=1, source_target_pairs={{0,2},{4,0},{8,4},{12,8},{14,12},{10,14},{6,10},{2,6},{1,3},{5,1},... | collective-permute-start | bytes 602120 | tf_op jit(solution)/shard_map/ppermute | solution.py:612
  19.7 9.6 %collective-permute-start.5 = (bf16[784,128]{1,0:T(8,128)(2,1)S(1)}, bf16[784,128]{1,0:T(8,128)(2,1)S(1)}, u32[]{:S(2)}, u32[]{:S(2)}) collective-permute-start(bf16[784,128]{1,0:T(8,128)(2,1)S(1)} %get-tuple-element.75), channel_id=1, source_target_pairs={{0,4},{4,8},{8,12},{12,14},{14,10},{10,6},{6,2},{2,0},{1,5},{5,9},... | collective-permute-start | bytes 602120 | tf_op jit(solution)/shard_map/ppermute | solution.py:612
  21.3 8.0 %collective-permute-start.6 = (bf16[784,128]{1,0:T(8,128)(2,1)S(1)}, bf16[784,128]{1,0:T(8,128)(2,1)S(1)}, u32[]{:S(2)}, u32[]{:S(2)}) collective-permute-start(bf16[784,128]{1,0:T(8,128)(2,1)S(1)} %get-tuple-element.76), channel_id=1, source_target_pairs={{0,2},{4,0},{8,4},{12,8},{14,12},{10,14},{6,10},{2,6},{1,3},{5,1},... | collective-permute-start | bytes 602120 | tf_op jit(solution)/shard_map/ppermute | solution.py:612
  22.4 5.2 %copy-start.1 = (bf16[1,1024,2048]{2,1,0:T(8,128)(2,1)S(1)}, bf16[1,1024,2048]{2,1,0:T(8,128)(2,1)}, u32[]{:S(2)}) copy-start(bf16[1,1024,2048]{2,1,0:T(8,128)(2,1)} %cache.3) | copy-start | bytes 12582916
  22.4 5.2 %copy-start.6 = (bf16[1,2,2048]{2,1,0:T(2,128)(2,1)S(1)}, bf16[1,2,2048]{2,1,0:T(2,128)(2,1)}, u32[]{:S(2)}) copy-start(bf16[1,2,2048]{2,1,0:T(2,128)(2,1)} %new.3) | copy-start | bytes 24580
  24.8 9.1 %collective-permute-start.8 = (bf16[784,128]{1,0:T(8,128)(2,1)S(1)}, bf16[784,128]{1,0:T(8,128)(2,1)S(1)}, u32[]{:S(2)}, u32[]{:S(2)}) collective-permute-start(bf16[784,128]{1,0:T(8,128)(2,1)S(1)} %get-tuple-element.71), channel_id=1, source_target_pairs={{0,2},{4,0},{8,4},{12,8},{14,12},{10,14},{6,10},{2,6},{1,3},{5,1},... | collective-permute-start | bytes 602120 | tf_op jit(solution)/shard_map/ppermute | solution.py:612
  25.3 8.6 %collective-permute-start.7 = (bf16[784,128]{1,0:T(8,128)(2,1)S(1)}, bf16[784,128]{1,0:T(8,128)(2,1)S(1)}, u32[]{:S(2)}, u32[]{:S(2)}) collective-permute-start(bf16[784,128]{1,0:T(8,128)(2,1)S(1)} %get-tuple-element.79), channel_id=1, source_target_pairs={{0,4},{4,8},{8,12},{12,14},{14,10},{10,6},{6,2},{2,0},{1,5},{5,9},... | collective-permute-start | bytes 602120 | tf_op jit(solution)/shard_map/ppermute | solution.py:612
  29.3 8.8 %collective-permute-start.9 = (bf16[784,128]{1,0:T(8,128)(2,1)S(1)}, bf16[784,128]{1,0:T(8,128)(2,1)S(1)}, u32[]{:S(2)}, u32[]{:S(2)}) collective-permute-start(bf16[784,128]{1,0:T(8,128)(2,1)S(1)} %get-tuple-element.83), channel_id=1, source_target_pairs={{0,4},{4,8},{8,12},{12,14},{14,10},{10,6},{6,2},{2,0},{1,5},{5,9},... | collective-permute-start | bytes 602120 | tf_op jit(solution)/shard_map/ppermute | solution.py:612
  31.2 7.2 %collective-permute-start.10 = (bf16[784,128]{1,0:T(8,128)(2,1)S(1)}, bf16[784,128]{1,0:T(8,128)(2,1)S(1)}, u32[]{:S(2)}, u32[]{:S(2)}) collective-permute-start(bf16[784,128]{1,0:T(8,128)(2,1)S(1)} %get-tuple-element.84), channel_id=1, source_target_pairs={{0,2},{4,0},{8,4},{12,8},{14,12},{10,14},{6,10},{2,6},{1,3},{5,1},... | collective-permute-start | bytes 602120 | tf_op jit(solution)/shard_map/ppermute | solution.py:612
  34.0 10.1 %collective-permute-start.13 = (bf16[784,128]{1,0:T(8,128)(2,1)S(1)}, bf16[784,128]{1,0:T(8,128)(2,1)S(1)}, u32[]{:S(2)}, u32[]{:S(2)}) collective-permute-start(bf16[784,128]{1,0:T(8,128)(2,1)S(1)} %get-tuple-element.89), channel_id=1, source_target_pairs={{0,4},{4,8},{8,12},{12,14},{14,10},{10,6},{6,2},{2,0},{1,5},{5,9},... | collective-permute-start | bytes 602120 | tf_op jit(solution)/shard_map/ppermute | solution.py:612
  35.3 8.7 %collective-permute-start.14 = (bf16[784,128]{1,0:T(8,128)(2,1)S(1)}, bf16[784,128]{1,0:T(8,128)(2,1)S(1)}, u32[]{:S(2)}, u32[]{:S(2)}) collective-permute-start(bf16[784,128]{1,0:T(8,128)(2,1)S(1)} %get-tuple-element.90), channel_id=1, source_target_pairs={{0,2},{4,0},{8,4},{12,8},{14,12},{10,14},{6,10},{2,6},{1,3},{5,1},... | collective-permute-start | bytes 602120 | tf_op jit(solution)/shard_map/ppermute | solution.py:612
  38.5 6.6 %collective-permute-start.11 = (bf16[784,128]{1,0:T(8,128)(2,1)S(1)}, bf16[784,128]{1,0:T(8,128)(2,1)S(1)}, u32[]{:S(2)}, u32[]{:S(2)}) collective-permute-start(bf16[784,128]{1,0:T(8,128)(2,1)S(1)} %get-tuple-element.87), channel_id=1, source_target_pairs={{0,4},{4,8},{8,12},{12,14},{14,10},{10,6},{6,2},{2,0},{1,5},{5,9},... | collective-permute-start | bytes 602120 | tf_op jit(solution)/shard_map/ppermute | solution.py:612
  40.3 5.7 %collective-permute-start.12 = (bf16[784,128]{1,0:T(8,128)(2,1)S(1)}, bf16[784,128]{1,0:T(8,128)(2,1)S(1)}, u32[]{:S(2)}, u32[]{:S(2)}) collective-permute-start(bf16[784,128]{1,0:T(8,128)(2,1)S(1)} %get-tuple-element.88), channel_id=1, source_target_pairs={{0,2},{4,0},{8,4},{12,8},{14,12},{10,14},{6,10},{2,6},{1,3},{5,1},... | collective-permute-start | bytes 602120 | tf_op jit(solution)/shard_map/ppermute | solution.py:612
  40.5 3.5 %collective-permute-start.15 = (bf16[4,48,128]{2,1,0:T(8,128)(2,1)S(1)}, bf16[4,48,128]{2,1,0:T(8,128)(2,1)S(1)}, u32[]{:S(2)}, u32[]{:S(2)}) collective-permute-start(bf16[4,48,128]{2,1,0:T(8,128)(2,1)S(1)} %cache_attention.2), channel_id=1, source_target_pairs={{0,1},{1,0},{2,3},{3,2},{4,5},{5,4},{6,7},{7,6},{8,9},{9,8},{10,11... | collective-permute-start | bytes 147464 | tf_op jit(solution)/shard_map/ppermute | solution.py:614

commit v20 on v17

--- a/solution.py
+++ b/solution.py
@@ -125,7 +125,7 @@
 
 def selected(codes, leaves):
     codes = codes.astype(jnp.int16)
-    masks = [(codes & (1 << bit)) != 0 for bit in range(4)]
+    masks = [(codes & (1 << bit)) != 0 for bit in range(3)] + [codes > 7]
 
     def node(bit, base):
         if bit < 0:
@@ -191,7 +191,7 @@
     for block in range(blocks):
         for copy in code_copies(block):
             copy.wait()
-        lax.fori_loop(block * steps, (block + 1) * steps, body, 0)
+        lax.fori_loop(block * steps, (block + 1) * steps, body, 0, unroll=2)
 
 
 def dequantize(codes, scales, outer):

time: 49.9 us -> 49.5 us (level); the launches traced: 50.2 us -> 49 us
  starting transfers between devices: 17.1 us -> 15.6 us
  waiting for transfers between devices: 4.74 us -> 5.88 us
  Pallas kernels: 24.8 us -> 24 us
    ppermute x7, starting transfers between devices: 12.8 us -> 7.26 us  [pass_on(): lax.ppermute(right, 'tp', to_right)]
    ppermute x7, starting transfers between devices: 3.8 us -> 7.86 us  [pass_on(): lax.ppermute(left, 'tp', to_left)]
    ppermute x7, waiting for transfers between devices: 1.29 us -> 4.58 us  [pass_on(): lax.ppermute(right, 'tp', to_right)]
    ppermute x7, waiting for transfers between devices: 3.44 us -> 1.29 us  [pass_on(): lax.ppermute(left, 'tp', to_left)]
    pallas_call x3, Pallas kernels: 7.1 us -> 6.03 us  [project(): pl.pallas_call(functools.partial(project_kernel, distances), in_specs=[SM...]
    pallas_call x1, Pallas kernels: 1.61 us -> 2.44 us  [project_early(): pl.pallas_call(functools.partial(early_kernel, distance), in_specs=[SMEM]...]
    pallas_call x1, Pallas kernels: 7.42 us -> 6.91 us  [dequantize(): pl.pallas_call(weights_kernel, grid=(1,), in_specs=[pl.BlockSpec(memory_s...]
  transfers between devices with their start and end apart: 16 -> 16, of which waited for: 6 -> 4; matrix products, arithmetic and copies ran while one was open for 0% -> 0% of each run, Pallas kernels for 43% -> 42%
where the time goes in v20:
time: 49.5 us; the launch traced here: 49 us
  Pallas kernels  24 us (48%)
  starting transfers between devices  15.6 us (32%)
  waiting for transfers between devices  5.88 us (12%)
  blocking collectives  1.85 us (4%)
  between operations  0.95 us (2%)
  local copies, waits for them, and re-layouts  0.68 us (1%)
    ppermute x7, starting transfers between devices, pass_on(): lax.ppermute(left, 'tp', to_left)  7.86 us
    ppermute x7, starting transfers between devices, pass_on(): lax.ppermute(right, 'tp', to_right)  7.26 us
    pallas_call x1, Pallas kernels, dequantize(): pl.pallas_call(weights_kernel, grid=(1,), in_specs=[pl.BlockSpec(memory_s...  6.91 us
    pallas_call x3, Pallas kernels, project(): pl.pallas_call(functools.partial(project_kernel, distances), in_specs=[SM...  6.03 us
    ppermute x7, waiting for transfers between devices, pass_on(): lax.ppermute(right, 'tp', to_right)  4.58 us
    pallas_call x2, Pallas kernels, cache_attention(): pl.pallas_call(functools.partial(cache_kernel, part), in_specs=[SMEM] * 3...  3.18 us
    pallas_call x1, Pallas kernels, project_early(): pl.pallas_call(functools.partial(early_kernel, distance), in_specs=[SMEM]...  2.44 us
    pallas_call x1, Pallas kernels, project_first(): pl.pallas_call(functools.partial(first_kernel, distance), in_specs=[SMEM]...  1.89 us
  transfers between devices with their start and end apart: 16, of which 4 were waited for; matrix products, arithmetic and copies ran while one was open for 0% of the time, Pallas kernels for 42%

profile of v20, /device:TPU:0, one launch (start us, length us, event | category | flops | bytes accessed | tf_op | source)
XLA Modules:
  0.0 49.0 jit_solution(13346997836474150715)
XLA Ops:
  0.0 0.5 collective-permute-start
  0.5 6.9 %dequantize.1.weight = bf16[4,2048,256]{2,1,0:T(8,128)(2,1)S(1)} custom-call(s32[2048,2048]{1,0:T(8,128)} %codes.1, s32[32,2048]{1,0:T(8,128)} %value_scales.1, s32[32,2048]{1,0:T(8,128)} %value_scales.1, f32[8,32]{1,0:T(8,128)} %bitcast.14), custom_call_target="tpu_custom_call" | custom-call | flops 134217728 | bytes 8388608 | tf_op jit(solution)/shard_map/dequantize/pallas_call | solution.py:203
  7.4 0.0 collective-permute-done.other
  7.4 0.0 copy-start.8
  7.5 1.9 %project_first.1 = (bf16[784,128]{1,0:T(8,128)(2,1)S(1)}, bf16[768,128]{1,0:T(8,128)(2,1)S(1)}) custom-call(s32[6]{0:T(128)S(1)} %copy-done.5, bf16[3,192,2048]{2,1,0:T(8,128)(2,1)S(1)} %bitcast.4, bf16[3,192,2048]{2,1,0:T(8,128)(2,1)S(1)} %collective-permute-done.other, f32[1,2048]{1,0:T(1,128)S(1)} %bitcast.9, bf16[4,2048,256]{2,1,0:T(8,128)(2,1)S(1)} %dequantize.1.weight), custom_call_target="tpu_custom_call" | custom-call | flops 805306368 | bytes 2097152 | tf_op jit(solution)/shard_map/project_first/pallas_call | solution.py:285
  9.4 2.6 %collective-permute-start.1 = (bf16[784,128]{1,0:T(8,128)(2,1)S(1)}, bf16[784,128]{1,0:T(8,128)(2,1)S(1)}, u32[]{:S(2)}, u32[]{:S(2)}) collective-permute-start(bf16[784,128]{1,0:T(8,128)(2,1)S(1)} %get-tuple-element.64), channel_id=1, source_target_pairs={{0,4},{4,8},{8,12},{12,14},{14,10},{10,6},{6,2},{2,0},{1,5},{5,9},... | collective-permute-start | bytes 602120 | tf_op jit(solution)/shard_map/ppermute | solution.py:608
  12.0 0.0 collective-permute-start.2
  12.0 0.1 multiply_cosine_fusion
  12.1 2.4 %project_early.1 = (f32[2,1,776,128]{3,2,1,0:T(8,128)S(1)}, bf16[2,192,2048]{2,1,0:T(8,128)(2,1)S(1)}, f32[2,8,128]{2,1,0:T(8,128)S(1)}) custom-call(s32[6]{0:T(128)S(1)} %copy-done.5, bf16[3,192,2048]{2,1,0:T(8,128)(2,1)S(1)} %bitcast.5, bf16[3,192,2048]{2,1,0:T(8,128)(2,1)S(1)} %collective-permute-done.other, f32[1,2048]{1,0:T(1,128)S(1)} %bitcast.10, ...), custom_call_target="tpu_custom_call" | custom-call | flops 402653184 | bytes 2097152 | tf_op jit(solution)/shard_map/project_early/pallas_call | solution.py:361
  14.6 0.0 copy-start.3
  14.7 0.0 copy-start.4
  14.7 1.2 %collective-permute-start.3 = (bf16[784,128]{1,0:T(8,128)(2,1)S(1)}, bf16[784,128]{1,0:T(8,128)(2,1)S(1)}, u32[]{:S(2)}, u32[]{:S(2)}) collective-permute-start(bf16[784,128]{1,0:T(8,128)(2,1)S(1)} %get-tuple-element.67), channel_id=1, source_target_pairs={{0,4},{4,8},{8,12},{12,14},{14,10},{10,6},{6,2},{2,0},{1,5},{5,9},... | collective-permute-start | bytes 602120 | tf_op jit(solution)/shard_map/ppermute | solution.py:608
  15.9 0.8 %collective-permute-start.4 = (bf16[784,128]{1,0:T(8,128)(2,1)S(1)}, bf16[784,128]{1,0:T(8,128)(2,1)S(1)}, u32[]{:S(2)}, u32[]{:S(2)}) collective-permute-start(bf16[784,128]{1,0:T(8,128)(2,1)S(1)} %get-tuple-element.58), channel_id=1, source_target_pairs={{0,2},{4,0},{8,4},{12,8},{14,12},{10,14},{6,10},{2,6},{1,3},{5,1},... | collective-permute-start | bytes 602120 | tf_op jit(solution)/shard_map/ppermute | solution.py:608
  16.7 1.0 %project_late.1.terms = f32[2,1,776,128]{3,2,1,0:T(8,128)S(1)} custom-call(bf16[2,192,2048]{2,1,0:T(8,128)(2,1)S(1)} %get-tuple-element.56.lines, f32[2,8,128]{2,1,0:T(8,128)S(1)} %get-tuple-element.57.totals, bf16[4,2048,256]{2,1,0:T(8,128)(2,1)S(1)} %dequantize.1.weight), custom_call_target="tpu_custom_call" | custom-call | flops 402653184 | bytes 2097152 | tf_op jit(solution)/shard_map/project_late/pallas_call | solution.py:379
  17.8 0.7 %prepare.1 = (bf16[8,32,128]{2,1,0:T(8,128)(2,1)S(1)}, f32[2,192,128]{2,1,0:T(8,128)S(1)}) custom-call(s32[6]{0:T(128)S(1)} %copy-done.5, bf16[1,2,16384]{2,1,0:T(2,128)(2,1)S(1)} %copy-done.4, f32[2,6,128]{2,1,0:T(8,128)S(1)} %pad_maximum_fusion.starts, f32[2,192,128]{2,1,0:T(8,128)S(1)} %copy-done.3), custom_call_target="tpu_custom_call" | custom-call | tf_op jit(solution)/shard_map/prepare/pallas_call | solution.py:439
  18.5 1.3 %collective-permute-done.2.refs_1_ = bf16[768,128]{1,0:T(8,128)(2,1)S(1)} collective-permute-done((bf16[768,128]{1,0:T(8,128)(2,1)S(1)}, bf16[768,128]{1,0:T(8,128)(2,1)S(1)}, u32[]{:S(2)}, u32[]{:S(2)}) %collective-permute-start.2) | collective-permute-done | bytes 196640 | tf_op jit(solution)/shard_map/ppermute | solution.py:608
  19.8 0.1 sends.7
  19.9 0.1 collective-permute-start.5
  19.9 2.0 %collective-permute-start.6 = (bf16[784,128]{1,0:T(8,128)(2,1)S(1)}, bf16[784,128]{1,0:T(8,128)(2,1)S(1)}, u32[]{:S(2)}, u32[]{:S(2)}) collective-permute-start(bf16[784,128]{1,0:T(8,128)(2,1)S(1)} %get-tuple-element.76), channel_id=1, source_target_pairs={{0,2},{4,0},{8,4},{12,8},{14,12},{10,14},{6,10},{2,6},{1,3},{5,1},... | collective-permute-start | bytes 602120 | tf_op jit(solution)/shard_map/ppermute | solution.py:608
  22.6 0.0 copy-start.1
  22.6 0.0 copy-start.6
  22.6 2.2 %project.3.terms = f32[2,2,776,128]{3,2,1,0:T(8,128)S(1)} custom-call(s32[6]{0:T(128)S(1)} %copy-done.5, bf16[3,192,2048]{2,1,0:T(8,128)(2,1)S(1)} %bitcast.6, bf16[3,192,2048]{2,1,0:T(8,128)(2,1)S(1)} %collective-permute-done.other, f32[1,2048]{1,0:T(1,128)S(1)} %bitcast.11, bf16[4,2048,256]{2,1,0:T(8,128)(2,1)S(1)} %dequantize.1.weight), custom_call_target="tpu_custom_call" | custom-call | flops 805306368 | bytes 2097152 | tf_op jit(solution)/shard_map/project/pallas_call | solution.py:318
  24.8 0.0 collective-permute-done.4.refs_1_
  24.8 0.1 sends.8
  24.9 2.0 %collective-permute-start.8 = (bf16[784,128]{1,0:T(8,128)(2,1)S(1)}, bf16[784,128]{1,0:T(8,128)(2,1)S(1)}, u32[]{:S(2)}, u32[]{:S(2)}) collective-permute-start(bf16[784,128]{1,0:T(8,128)(2,1)S(1)} %get-tuple-element.71), channel_id=1, source_target_pairs={{0,2},{4,0},{8,4},{12,8},{14,12},{10,14},{6,10},{2,6},{1,3},{5,1},... | collective-permute-start | bytes 602120 | tf_op jit(solution)/shard_map/ppermute | solution.py:608
  26.9 0.1 collective-permute-start.7
  27.0 1.6 %cache_attention.2 = bf16[4,48,128]{2,1,0:T(8,128)(2,1)S(1)} custom-call(s32[6]{0:T(128)S(1)} %copy-done.5, s32[6]{0:T(128)S(1)} %copy-done.7, s32[1]{0:T(128)S(6)} %copy.15.stored, bf16[8,32,128]{2,1,0:T(8,128)(2,1)S(1)} %get-tuple-element.73.q.grouped, bf16[1,1024,2048]{2,1,0:T(8,128)(2,1)S(1)} %copy-done.1, bf16[1,2,2048]{2,1,0:T(2,128)(2,1)S(1)} %copy-done.6), custom_call_target="tpu_custom_call" | custom-call | flops 1 | bytes 1 | tf_op jit(solution)/shard_map/cache_attention/pallas_call | solution.py:503
  28.6 0.0 collective-permute-done.5.refs_0_
  28.6 0.1 sends.9
  28.7 1.9 %collective-permute-start.9 = (bf16[784,128]{1,0:T(8,128)(2,1)S(1)}, bf16[784,128]{1,0:T(8,128)(2,1)S(1)}, u32[]{:S(2)}, u32[]{:S(2)}) collective-permute-start(bf16[784,128]{1,0:T(8,128)(2,1)S(1)} %get-tuple-element.83), channel_id=1, source_target_pairs={{0,4},{4,8},{8,12},{12,14},{14,10},{10,6},{6,2},{2,0},{1,5},{5,9},... | collective-permute-start | bytes 602120 | tf_op jit(solution)/shard_map/ppermute | solution.py:608
  30.6 0.1 collective-permute-start.10
  30.7 2.0 %project.4.terms = f32[2,2,776,128]{3,2,1,0:T(8,128)S(1)} custom-call(s32[6]{0:T(128)S(1)} %copy-done.5, bf16[3,192,2048]{2,1,0:T(8,128)(2,1)S(1)} %bitcast.7, bf16[3,192,2048]{2,1,0:T(8,128)(2,1)S(1)} %collective-permute-done.other, f32[1,2048]{1,0:T(1,128)S(1)} %bitcast.12, bf16[4,2048,256]{2,1,0:T(8,128)(2,1)S(1)} %dequantize.1.weight), custom_call_target="tpu_custom_call" | custom-call | flops 805306368 | bytes 2097152 | tf_op jit(solution)/shard_map/project/pallas_call | solution.py:318
  32.7 2.0 %collective-permute-done.7.refs_0_ = bf16[784,128]{1,0:T(8,128)(2,1)S(1)} collective-permute-done((bf16[784,128]{1,0:T(8,128)(2,1)S(1)}, bf16[784,128]{1,0:T(8,128)(2,1)S(1)}, u32[]{:S(2)}, u32[]{:S(2)}) %collective-permute-start.7) | collective-permute-done | bytes 200736 | tf_op jit(solution)/shard_map/ppermute | solution.py:608
  34.8 0.0 collective-permute-done.8.refs_1_
  34.8 0.1 sends.10
  34.9 1.2 %collective-permute-start.13 = (bf16[784,128]{1,0:T(8,128)(2,1)S(1)}, bf16[784,128]{1,0:T(8,128)(2,1)S(1)}, u32[]{:S(2)}, u32[]{:S(2)}) collective-permute-start(bf16[784,128]{1,0:T(8,128)(2,1)S(1)} %get-tuple-element.89), channel_id=1, source_target_pairs={{0,4},{4,8},{8,12},{12,14},{14,10},{10,6},{6,2},{2,0},{1,5},{5,9},... | collective-permute-start | bytes 602120 | tf_op jit(solution)/shard_map/ppermute | solution.py:608
  36.1 0.9 %collective-permute-start.14 = (bf16[784,128]{1,0:T(8,128)(2,1)S(1)}, bf16[784,128]{1,0:T(8,128)(2,1)S(1)}, u32[]{:S(2)}, u32[]{:S(2)}) collective-permute-start(bf16[784,128]{1,0:T(8,128)(2,1)S(1)} %get-tuple-element.90), channel_id=1, source_target_pairs={{0,2},{4,0},{8,4},{12,8},{14,12},{10,14},{6,10},{2,6},{1,3},{5,1},... | collective-permute-start | bytes 602120 | tf_op jit(solution)/shard_map/ppermute | solution.py:608
  37.0 2.1 %collective-permute-done.9.refs_0_ = bf16[784,128]{1,0:T(8,128)(2,1)S(1)} collective-permute-done((bf16[784,128]{1,0:T(8,128)(2,1)S(1)}, bf16[784,128]{1,0:T(8,128)(2,1)S(1)}, u32[]{:S(2)}, u32[]{:S(2)}) %collective-permute-start.9) | collective-permute-done | bytes 200736 | tf_op jit(solution)/shard_map/ppermute | solution.py:608
  39.1 0.1 sends.11
  39.2 0.1 collective-permute-start.11
  39.2 2.0 %collective-permute-start.12 = (bf16[784,128]{1,0:T(8,128)(2,1)S(1)}, bf16[784,128]{1,0:T(8,128)(2,1)S(1)}, u32[]{:S(2)}, u32[]{:S(2)}) collective-permute-start(bf16[784,128]{1,0:T(8,128)(2,1)S(1)} %get-tuple-element.88), channel_id=1, source_target_pairs={{0,2},{4,0},{8,4},{12,8},{14,12},{10,14},{6,10},{2,6},{1,3},{5,1},... | collective-permute-start | bytes 602120 | tf_op jit(solution)/shard_map/ppermute | solution.py:608
  41.3 0.0 collective-permute-start.15
  41.3 1.6 %cache_attention.3.cached_here = bf16[4,48,128]{2,1,0:T(8,128)(2,1)S(1)} custom-call(s32[6]{0:T(128)S(1)} %copy-done.5, s32[6]{0:T(128)S(1)} %copy-done.7, s32[1]{0:T(128)S(6)} %copy.15.stored, bf16[8,32,128]{2,1,0:T(8,128)(2,1)S(1)} %get-tuple-element.73.q.grouped, bf16[1,1024,2048]{2,1,0:T(8,128)(2,1)S(1)} %copy-done.1, bf16[1,2,2048]{2,1,0:T(2,128)(2,1)S(1)} %copy-done.6), custom_call_target="tpu_custom_call" | custom-call | flops 1 | bytes 1 | tf_op jit(solution)/shard_map/cache_attention/pallas_call | solution.py:503
  42.9 1.9 %project.5.own = f32[1,2,776,128]{3,2,1,0:T(8,128)S(1)} custom-call(s32[6]{0:T(128)S(1)} %copy-done.5, bf16[3,192,2048]{2,1,0:T(8,128)(2,1)S(1)} %bitcast.8, bf16[3,192,2048]{2,1,0:T(8,128)(2,1)S(1)} %collective-permute-done.other, f32[1,2048]{1,0:T(1,128)S(1)} %bitcast.13, bf16[4,2048,256]{2,1,0:T(8,128)(2,1)S(1)} %dequantize.1.weight), custom_call_target="tpu_custom_call" | custom-call | flops 402653184 | bytes 2097152 | tf_op jit(solution)/shard_map/project/pallas_call | solution.py:318
  44.8 0.4 collective-permute-done.11.right_keys
  45.2 1.4 %finish.1 = bf16[1,2,8192]{2,1,0:T(2,128)(2,1)S(1)} custom-call(s32[6]{0:T(128)S(1)} %copy-done.5, f32[2,192,128]{2,1,0:T(8,128)S(1)} %get-tuple-element.62.rotary, f32[1,2,776,128]{3,2,1,0:T(8,128)S(1)} %project.5.own, bf16[784,128]{1,0:T(8,128)(2,1)S(1)} %collective-permute-done.11.right_keys, bf16[784,128]{1,0:T(8,128)(2,1)S(1)} %collective-permute-done.12.left_values, ...), custom_call_target="tpu_custom_call" | custom-call | tf_op jit(solution)/shard_map/finish/pallas_call | solution.py:569
  46.6 1.9 %all_gather.3 = bf16[1,2,16384]{2,1,0:T(2,128)(2,1)S(1)} all-gather(bf16[1,2,8192]{2,1,0:T(2,128)(2,1)S(1)} %finish.1), channel_id=1, replica_groups=mesh['grp'=2,'tp'=8,'rep'=2] {'rep'}, dimensions={2}, use_global_device_ids=true | all-gather | bytes 98304 | tf_op jit(solution)/shard_map/all_gather | solution.py:654
  48.4 0.6 %copy.16 = bf16[1,2,16384]{2,1,0:T(2,128)(2,1)} copy(bf16[1,2,16384]{2,1,0:T(2,128)(2,1)S(1)} %all_gather.3) | data formatting | bytes 131072
  (24 shorter events, 0.1 us)
Async XLA Ops:
  0.0 7.4 %collective-permute-start = (bf16[3,192,2048]{2,1,0:T(8,128)(2,1)}, bf16[3,192,2048]{2,1,0:T(8,128)(2,1)S(1)}, u32[]{:S(2)}, u32[]{:S(2)}) collective-permute-start(bf16[3,192,2048]{2,1,0:T(8,128)(2,1)} %bitcast.3), channel_id=1, source_target_pairs={{0,1},{1,0},{2,3},{3,2},{4,5},{5,4},{6,7},{7,6},{8,9},{9,8},{10,11... | collective-permute-start | bytes 7077896 | tf_op jit(solution)/shard_map/ppermute | solution.py:610
  0.5 6.9 %copy-start.7 = (s32[6]{0:T(128)S(1)}, s32[6]{0:T(128)}, u32[]{:S(2)}) copy-start(s32[6]{0:T(128)} %lengths.3) | copy-start | bytes 76
  0.5 7.0 %copy-start = (bf16[192,3,2048]{2,0,1:T(8,128)(2,1)S(1)}, bf16[192,3,2048]{2,0,1:T(8,128)(2,1)}, u32[]{:S(2)}) copy-start(bf16[192,3,2048]{2,0,1:T(8,128)(2,1)} %param.13) | copy-start | bytes 7077892
  0.5 7.0 %copy-start.2 = (f32[2048]{0:T(1024)S(1)}, f32[2048]{0:T(1024)}, u32[]{:S(2)}) copy-start(f32[2048]{0:T(1024)} %param.14) | copy-start | bytes 24580
  0.5 7.0 %copy-start.5 = (s32[6]{0:T(128)S(1)}, s32[6]{0:T(128)}, u32[]{:S(2)}) copy-start(s32[6]{0:T(128)} %targets.10) | copy-start | bytes 76
  7.4 4.6 %copy-start.8 = (f32[128]{0:T(128)S(1)}, f32[128]{0:T(128)}, u32[]{:S(2)}) copy-start(f32[128]{0:T(128)} %constant.7.clone) | copy-start | bytes 1540
  9.4 10.4 %collective-permute-start.1 = (bf16[784,128]{1,0:T(8,128)(2,1)S(1)}, bf16[784,128]{1,0:T(8,128)(2,1)S(1)}, u32[]{:S(2)}, u32[]{:S(2)}) collective-permute-start(bf16[784,128]{1,0:T(8,128)(2,1)S(1)} %get-tuple-element.64), channel_id=1, source_target_pairs={{0,4},{4,8},{8,12},{12,14},{14,10},{10,6},{6,2},{2,0},{1,5},{5,9},... | collective-permute-start | bytes 602120 | tf_op jit(solution)/shard_map/ppermute | solution.py:608
  12.0 7.7 %collective-permute-start.2 = (bf16[768,128]{1,0:T(8,128)(2,1)S(1)}, bf16[768,128]{1,0:T(8,128)(2,1)S(1)}, u32[]{:S(2)}, u32[]{:S(2)}) collective-permute-start(bf16[768,128]{1,0:T(8,128)(2,1)S(1)} %get-tuple-element.49), channel_id=1, source_target_pairs={{0,2},{4,0},{8,4},{12,8},{14,12},{10,14},{6,10},{2,6},{1,3},{5,1},... | collective-permute-start | bytes 589832 | tf_op jit(solution)/shard_map/ppermute | solution.py:608
  14.6 3.1 %copy-start.3 = (f32[2,192,128]{2,1,0:T(8,128)S(1)}, f32[2,192,128]{2,1,0:T(8,128)}, u32[]{:S(2)}) copy-start(f32[2,192,128]{2,1,0:T(8,128)} %constant.8.clone.turns) | copy-start | bytes 589828
  14.7 3.1 %copy-start.4 = (bf16[1,2,16384]{2,1,0:T(2,128)(2,1)S(1)}, bf16[1,2,16384]{2,1,0:T(2,128)(2,1)}, u32[]{:S(2)}) copy-start(bf16[1,2,16384]{2,1,0:T(2,128)(2,1)} %queries.1) | copy-start | bytes 196612
  14.7 10.1 %collective-permute-start.3 = (bf16[784,128]{1,0:T(8,128)(2,1)S(1)}, bf16[784,128]{1,0:T(8,128)(2,1)S(1)}, u32[]{:S(2)}, u32[]{:S(2)}) collective-permute-start(bf16[784,128]{1,0:T(8,128)(2,1)S(1)} %get-tuple-element.67), channel_id=1, source_target_pairs={{0,4},{4,8},{8,12},{12,14},{14,10},{10,6},{6,2},{2,0},{1,5},{5,9},... | collective-permute-start | bytes 602120 | tf_op jit(solution)/shard_map/ppermute | solution.py:608
  15.9 8.9 %collective-permute-start.4 = (bf16[784,128]{1,0:T(8,128)(2,1)S(1)}, bf16[784,128]{1,0:T(8,128)(2,1)S(1)}, u32[]{:S(2)}, u32[]{:S(2)}) collective-permute-start(bf16[784,128]{1,0:T(8,128)(2,1)S(1)} %get-tuple-element.58), channel_id=1, source_target_pairs={{0,2},{4,0},{8,4},{12,8},{14,12},{10,14},{6,10},{2,6},{1,3},{5,1},... | collective-permute-start | bytes 602120 | tf_op jit(solution)/shard_map/ppermute | solution.py:608
  19.9 8.7 %collective-permute-start.5 = (bf16[784,128]{1,0:T(8,128)(2,1)S(1)}, bf16[784,128]{1,0:T(8,128)(2,1)S(1)}, u32[]{:S(2)}, u32[]{:S(2)}) collective-permute-start(bf16[784,128]{1,0:T(8,128)(2,1)S(1)} %get-tuple-element.75), channel_id=1, source_target_pairs={{0,4},{4,8},{8,12},{12,14},{14,10},{10,6},{6,2},{2,0},{1,5},{5,9},... | collective-permute-start | bytes 602120 | tf_op jit(solution)/shard_map/ppermute | solution.py:608
  19.9 8.6 %collective-permute-start.6 = (bf16[784,128]{1,0:T(8,128)(2,1)S(1)}, bf16[784,128]{1,0:T(8,128)(2,1)S(1)}, u32[]{:S(2)}, u32[]{:S(2)}) collective-permute-start(bf16[784,128]{1,0:T(8,128)(2,1)S(1)} %get-tuple-element.76), channel_id=1, source_target_pairs={{0,2},{4,0},{8,4},{12,8},{14,12},{10,14},{6,10},{2,6},{1,3},{5,1},... | collective-permute-start | bytes 602120 | tf_op jit(solution)/shard_map/ppermute | solution.py:608
  22.6 4.4 %copy-start.1 = (bf16[1,1024,2048]{2,1,0:T(8,128)(2,1)S(1)}, bf16[1,1024,2048]{2,1,0:T(8,128)(2,1)}, u32[]{:S(2)}) copy-start(bf16[1,1024,2048]{2,1,0:T(8,128)(2,1)} %cache.3) | copy-start | bytes 12582916
  22.6 4.4 %copy-start.6 = (bf16[1,2,2048]{2,1,0:T(2,128)(2,1)S(1)}, bf16[1,2,2048]{2,1,0:T(2,128)(2,1)}, u32[]{:S(2)}) copy-start(bf16[1,2,2048]{2,1,0:T(2,128)(2,1)} %new.3) | copy-start | bytes 24580
  24.9 9.9 %collective-permute-start.8 = (bf16[784,128]{1,0:T(8,128)(2,1)S(1)}, bf16[784,128]{1,0:T(8,128)(2,1)S(1)}, u32[]{:S(2)}, u32[]{:S(2)}) collective-permute-start(bf16[784,128]{1,0:T(8,128)(2,1)S(1)} %get-tuple-element.71), channel_id=1, source_target_pairs={{0,2},{4,0},{8,4},{12,8},{14,12},{10,14},{6,10},{2,6},{1,3},{5,1},... | collective-permute-start | bytes 602120 | tf_op jit(solution)/shard_map/ppermute | solution.py:608
  26.9 7.9 %collective-permute-start.7 = (bf16[784,128]{1,0:T(8,128)(2,1)S(1)}, bf16[784,128]{1,0:T(8,128)(2,1)S(1)}, u32[]{:S(2)}, u32[]{:S(2)}) collective-permute-start(bf16[784,128]{1,0:T(8,128)(2,1)S(1)} %get-tuple-element.79), channel_id=1, source_target_pairs={{0,4},{4,8},{8,12},{12,14},{14,10},{10,6},{6,2},{2,0},{1,5},{5,9},... | collective-permute-start | bytes 602120 | tf_op jit(solution)/shard_map/ppermute | solution.py:608
  28.7 10.4 %collective-permute-start.9 = (bf16[784,128]{1,0:T(8,128)(2,1)S(1)}, bf16[784,128]{1,0:T(8,128)(2,1)S(1)}, u32[]{:S(2)}, u32[]{:S(2)}) collective-permute-start(bf16[784,128]{1,0:T(8,128)(2,1)S(1)} %get-tuple-element.83), channel_id=1, source_target_pairs={{0,4},{4,8},{8,12},{12,14},{14,10},{10,6},{6,2},{2,0},{1,5},{5,9},... | collective-permute-start | bytes 602120 | tf_op jit(solution)/shard_map/ppermute | solution.py:608
  30.6 8.5 %collective-permute-start.10 = (bf16[784,128]{1,0:T(8,128)(2,1)S(1)}, bf16[784,128]{1,0:T(8,128)(2,1)S(1)}, u32[]{:S(2)}, u32[]{:S(2)}) collective-permute-start(bf16[784,128]{1,0:T(8,128)(2,1)S(1)} %get-tuple-element.84), channel_id=1, source_target_pairs={{0,2},{4,0},{8,4},{12,8},{14,12},{10,14},{6,10},{2,6},{1,3},{5,1},... | collective-permute-start | bytes 602120 | tf_op jit(solution)/shard_map/ppermute | solution.py:608
  34.9 9.9 %collective-permute-start.13 = (bf16[784,128]{1,0:T(8,128)(2,1)S(1)}, bf16[784,128]{1,0:T(8,128)(2,1)S(1)}, u32[]{:S(2)}, u32[]{:S(2)}) collective-permute-start(bf16[784,128]{1,0:T(8,128)(2,1)S(1)} %get-tuple-element.89), channel_id=1, source_target_pairs={{0,4},{4,8},{8,12},{12,14},{14,10},{10,6},{6,2},{2,0},{1,5},{5,9},... | collective-permute-start | bytes 602120 | tf_op jit(solution)/shard_map/ppermute | solution.py:608
  36.1 8.7 %collective-permute-start.14 = (bf16[784,128]{1,0:T(8,128)(2,1)S(1)}, bf16[784,128]{1,0:T(8,128)(2,1)S(1)}, u32[]{:S(2)}, u32[]{:S(2)}) collective-permute-start(bf16[784,128]{1,0:T(8,128)(2,1)S(1)} %get-tuple-element.90), channel_id=1, source_target_pairs={{0,2},{4,0},{8,4},{12,8},{14,12},{10,14},{6,10},{2,6},{1,3},{5,1},... | collective-permute-start | bytes 602120 | tf_op jit(solution)/shard_map/ppermute | solution.py:608
  39.2 6.0 %collective-permute-start.11 = (bf16[784,128]{1,0:T(8,128)(2,1)S(1)}, bf16[784,128]{1,0:T(8,128)(2,1)S(1)}, u32[]{:S(2)}, u32[]{:S(2)}) collective-permute-start(bf16[784,128]{1,0:T(8,128)(2,1)S(1)} %get-tuple-element.87), channel_id=1, source_target_pairs={{0,4},{4,8},{8,12},{12,14},{14,10},{10,6},{6,2},{2,0},{1,5},{5,9},... | collective-permute-start | bytes 602120 | tf_op jit(solution)/shard_map/ppermute | solution.py:608
  39.2 5.9 %collective-permute-start.12 = (bf16[784,128]{1,0:T(8,128)(2,1)S(1)}, bf16[784,128]{1,0:T(8,128)(2,1)S(1)}, u32[]{:S(2)}, u32[]{:S(2)}) collective-permute-start(bf16[784,128]{1,0:T(8,128)(2,1)S(1)} %get-tuple-element.88), channel_id=1, source_target_pairs={{0,2},{4,0},{8,4},{12,8},{14,12},{10,14},{6,10},{2,6},{1,3},{5,1},... | collective-permute-start | bytes 602120 | tf_op jit(solution)/shard_map/ppermute | solution.py:608
  41.3 3.5 %collective-permute-start.15 = (bf16[4,48,128]{2,1,0:T(8,128)(2,1)S(1)}, bf16[4,48,128]{2,1,0:T(8,128)(2,1)S(1)}, u32[]{:S(2)}, u32[]{:S(2)}) collective-permute-start(bf16[4,48,128]{2,1,0:T(8,128)(2,1)S(1)} %cache_attention.2), channel_id=1, source_target_pairs={{0,1},{1,0},{2,3},{3,2},{4,5},{5,4},{6,7},{7,6},{8,9},{9,8},{10,11... | collective-permute-start | bytes 147464 | tf_op jit(solution)/shard_map/ppermute | solution.py:610
